TPU v7x, 32 devices: a whole 2x2x4 slice. The times are simulated.
32 devices in a mesh: layer: 4 (over y, core), latent: 8 (over z, x).
Axes of the slice: x: 2, y: 2, z: 4, core: 2. Of those that a mesh axis runs over, the one named last changes fastest.
Arguments:
- resid: bfloat16 [2, 128, 3584], P(None, 'latent'), may hold values from -6 to 6
- target: bfloat16 [3, 128, 3584], P(None, 'latent'), may hold values from -6 to 6
- enc_weight: bfloat16 [4, 3584, 1024], P('layer', None, 'latent'), may hold values from -0.09375 to 0.09375
- enc_bias: float32 [4, 1024], P('layer', 'latent'), may hold values from -3 to 3
- dec_weight: bfloat16 [4, 2, 2, 1024, 1792], P('layer', None, None, 'latent'), may hold values from -0.125 to 0.125
- blocks: int32 [2, 1, 12], replicated, may hold values from 0 to 15, all different within a row
Outputs:
- errors: bfloat16 [4, 128, 1792], P('layer', 'latent')
- enc_grad: bfloat16 [4, 3584, 1024], P('layer', None, 'latent')
- bias_grad: float32 [4, 1024], P('layer', 'latent')
Inputs may be any that keep to these rules, and one draw needn't show every extreme that they name: Each row names 12 different blocks; every block is named in some row.
All inputs are finite; a program needn't handle non-finite values.
Results may differ from a plain program's by a relative error of at most 0.007.
Values may be sent and summed in bfloat16 or wider, within the bound.
No kernel may reach another device: no remote copies, remote signals or barrier semaphores. Data moves between devices by JAX's collectives and lax.ppermute only.
A program may use at most 64 MiB of HBM per device.

v0:
```python
import jax
import jax.numpy as jnp
from jax import lax
from jax.sharding import PartitionSpec as P


def swapped(shard, axis, stride):
    return lax.ppermute(shard, axis, [(i, i ^ 1 << stride) for i in range(lax.axis_size(axis))])


def from_behind(block, axis, distance):
    devices = range(lax.axis_size(axis))
    route = [(i - distance, i) for i in devices if i - distance in devices]
    return lax.ppermute(block, axis, route)


def contract_rows(left_rows, right_rows):
    return lax.dot_general(
        left_rows, right_rows, (((0,), (0,)), ((), ())), preferred_element_type=jnp.float32
    )


def contract_cols(left_rows, right_rows):
    return lax.dot_general(
        left_rows, right_rows, (((1,), (1,)), ((), ())), preferred_element_type=jnp.float32
    )


def on_device(resid, target, enc_weight, enc_bias, dec_weight, blocks):
    latent_devices = lax.axis_size("latent")
    layer_slot = lax.axis_index("layer")
    layer_row = layer_slot // 2
    which_half = layer_slot % 2
    column_pos = lax.axis_index("latent")
    rows_in = lax.dynamic_index_in_dim(resid, layer_row, 0, keepdims=False)
    local_rows = rows_in.shape[0]
    token_count = local_rows * latent_devices
    weight_in = enc_weight[0]
    block_width = weight_in.shape[1]
    decoder = dec_weight[0]
    column_width = decoder.shape[-1]
    dec_own = decoder[0].reshape(2 * block_width, column_width)
    dec_next = decoder[1].reshape(2 * block_width, column_width)
    listed = lax.dynamic_index_in_dim(blocks, layer_row, 0, keepdims=False)
    tile_len = token_count // listed.shape[0]
    flags = jnp.any(listed == which_half * latent_devices + column_pos, axis=1).astype(jnp.float32)
    gate_mask = jnp.repeat(flags, tile_len)[:, None]
    whole_in = lax.all_gather(rows_in, "latent", axis=0, tiled=True)
    preact = jnp.dot(whole_in, weight_in, preferred_element_type=jnp.float32)
    preact = preact + enc_bias[0][None, :]
    latents_on = (preact * gate_mask).astype(jnp.bfloat16)
    partner = swapped(latents_on, "layer", 0)
    lower_half = jnp.where(which_half == 0, latents_on, partner)
    upper_half = jnp.where(which_half == 0, partner, latents_on)
    pair_acts = jnp.concatenate([lower_half, upper_half], axis=1)
    totals = lax.psum_scatter(
        jnp.concatenate(
            [
                jnp.dot(pair_acts, dec_own, preferred_element_type=jnp.float32),
                jnp.dot(pair_acts, dec_next, preferred_element_type=jnp.float32),
            ],
            axis=1,
        ),
        "latent",
        scatter_dimension=0,
        tiled=True,
    )
    own_sum = totals[:, :column_width]
    ahead_part = totals[:, column_width:]
    targets = lax.dynamic_slice_in_dim(target, layer_row, 2, 0)
    targets = lax.dynamic_slice_in_dim(targets, which_half * column_width, column_width, 2).astype(
        jnp.float32
    )
    behind = from_behind(ahead_part, "layer", 2)
    err_own = (own_sum + behind - targets[0]).astype(jnp.bfloat16)
    next_own = from_behind(own_sum, "layer", -2)
    err_next = (next_own + ahead_part - targets[1]).astype(jnp.bfloat16)
    piece_pair = lax.all_gather((err_own, err_next), "latent", axis=0, tiled=True)
    grad_pair = contract_cols(piece_pair[0], dec_own) + contract_cols(piece_pair[1], dec_next)
    lower_grad = grad_pair[:, :block_width]
    upper_grad = grad_pair[:, block_width:]
    own_part = jnp.where(which_half == 0, lower_grad, upper_grad)
    their_part = jnp.where(which_half == 0, upper_grad, lower_grad)
    received = swapped(their_part, "layer", 0)
    grad_pre = (own_part + received) * gate_mask
    bias_grad = jnp.sum(grad_pre, axis=0)[None, :]
    grad_low = grad_pre.astype(jnp.bfloat16)
    grad_weight = contract_rows(whole_in, grad_low)
    return (err_own[None], grad_weight.astype(jnp.bfloat16)[None], bias_grad)


def solution(mesh):
    return jax.shard_map(
        on_device,
        mesh=mesh,
        in_specs=(
            P(None, "latent", None),
            P(None, "latent", None),
            P("layer", None, "latent"),
            P("layer", "latent"),
            P("layer", None, None, "latent", None),
            P(),
        ),
        out_specs=(P("layer", "latent", None), P("layer", None, "latent"), P("layer", "latent")),
        check_vma=False,
    )
```

profile of v0, /device:TPU:0, one launch (start us, length us, event | category | flops | bytes accessed | tf_op | source)
XLA Modules:
  0.0 202.8 jit_solution(8030014801883497726)
XLA Ops:
  7.2 0.0 copy-start
  7.2 0.0 reduce-scatter.2.cloned.1.call-start
  7.3 1.0 constant_dynamic-slice_fusion.1
  8.2 34.1 %all-gather = bf16[1,128,3584]{2,1,0:T(8,128)(2,1)S(1)} all-gather(bf16[1,16,3584]{2,1,0:T(8,128)(2,1)S(1)} %constant_dynamic-slice_fusion.1), channel_id=2, replica_groups=mesh['layer'=4,'latent'=8] {'latent'}, dimensions={1}, use_global_device_ids=true | all-gather | bytes 1032192 | tf_op jit(solution)/shard_map/all_gather | solution.py:48
  42.4 1.3 compare_reduce_fusion
  44.3 0.0 copy-start.3
  44.3 0.0 copy-done
  44.3 1.2 fusion.2
  45.6 0.1 collective-permute-start
  45.7 0.2 copy-done.3
  45.8 1.0 fusion.16
  46.9 0.0 copy-start.1
  46.9 0.0 collective-permute-done
  46.9 0.3 fusion.11
  47.2 0.8 copy-done.1
  48.1 0.3 fusion.10
  48.4 1.4 pad_maximum_fusion
  49.8 0.0 reduce-scatter.2.cloned.1.call-update
  49.8 67.2 %reduce-scatter.2.cloned.1.call-done = f32[16,3584]{1,0:T(8,128)} async-done(((f32[128,3584]{1,0:T(8,128)}), f32[16,3584]{1,0:T(8,128)}) %reduce-scatter.2.cloned.1.call-update) | async-done | bytes 229392 | tf_op jit(solution)/shard_map/reduce_scatter | solution.py:56
  117.0 0.0 copy-start.2
  117.0 1.1 fusion.17
  118.1 3.4 %collective-permute-start.1 = (f32[16,1792]{1,0:T(8,128)S(1)}, f32[16,1792]{1,0:T(8,128)S(1)}, u32[]{:S(2)}, u32[]{:S(2)}) collective-permute-start(f32[16,1792]{1,0:T(8,128)S(1)} %get-tuple-element.10), channel_id=1, source_target_pairs={{0,16},{8,24},{1,17},{9,25},{2,18},{10,26},{3,19},{11,27},{4,20},{... | collective-permute-start | bytes 344072 | tf_op jit(solution)/shard_map/ppermute | solution.py:14
  121.5 1.3 collective-permute-start.2
  122.8 1.0 dynamic-slice_convert_fusion
  123.8 0.0 collective-permute-done.1
  123.8 4.3 %collective-permute-done.2 = f32[16,1792]{1,0:T(8,128)S(1)} collective-permute-done((f32[16,1792]{1,0:T(8,128)S(1)}, f32[16,1792]{1,0:T(8,128)S(1)}, u32[]{:S(2)}, u32[]{:S(2)}) %collective-permute-start.2) | collective-permute-done | bytes 114720 | tf_op jit(solution)/shard_map/ppermute | solution.py:14
  128.2 1.0 fusion.7
  129.2 0.0 copy-start.4
  129.2 31.5 %all_gather.11 = bf16[128,1792]{1,0:T(8,128)(2,1)S(1)} all-gather(bf16[16,1792]{1,0:T(8,128)(2,1)S(1)} %get-tuple-element.7), channel_id=1, replica_groups=mesh['layer'=4,'latent'=8] {'latent'}, dimensions={0}, use_global_device_ids=true | all-gather | bytes 516096 | tf_op jit(solution)/shard_map/all_gather | solution.py:78
  160.7 0.0 copy-done.2
  160.7 0.4 fusion.18
  161.1 31.1 %all_gather.10 = bf16[128,1792]{1,0:T(8,128)(2,1)S(1)} all-gather(bf16[16,1792]{1,0:T(8,128)(2,1)S(1)} %get-tuple-element.8), channel_id=1, replica_groups=mesh['layer'=4,'latent'=8] {'latent'}, dimensions={0}, use_global_device_ids=true | all-gather | bytes 516096 | tf_op jit(solution)/shard_map/all_gather | solution.py:78
  192.2 0.4 convolution_add_fusion
  192.6 0.0 copy-done.4
  192.7 0.1 collective-permute-start.3
  192.7 1.2 collective-permute-done.3
  194.0 0.6 fusion.15
  194.6 1.4 fusion
  (2 shorter events, 0.0 us)
Async XLA Ops:
  7.2 37.2 %copy-start = (bf16[1,3584,128]{2,1,0:T(8,128)(2,1)S(1)}, bf16[1,3584,128]{2,1,0:T(8,128)(2,1)}, u32[]{:S(2)}) copy-start(bf16[1,3584,128]{2,1,0:T(8,128)(2,1)} %param.8) | copy-start | bytes 2752516
  7.2 109.9 %reduce-scatter.2.cloned.1.call-start = ((), (), s32[]{:S(2)}) async-start(), calls=%async_computation.1 | async-start | bytes 2064384 | tf_op jit(solution)/shard_map/reduce_scatter | solution.py:56
  44.3 1.5 copy-start.3
  45.6 1.3 collective-permute-start
  46.9 1.2 copy-start.1
  117.0 43.6 %copy-start.2 = (bf16[1,1,2,128,1792]{4,3,2,1,0:T(8,128)(2,1)S(1)}, bf16[1,1,2,128,1792]{4,3,2,1,0:T(8,128)(2,1)}, u32[]{:S(2)}) copy-start(bf16[1,1,2,128,1792]{4,3,2,1,0:T(8,128)(2,1)} %get-tuple-element.6) | copy-start | bytes 2752516
  118.1 5.7 %collective-permute-start.1 = (f32[16,1792]{1,0:T(8,128)S(1)}, f32[16,1792]{1,0:T(8,128)S(1)}, u32[]{:S(2)}, u32[]{:S(2)}) collective-permute-start(f32[16,1792]{1,0:T(8,128)S(1)} %get-tuple-element.10), channel_id=1, source_target_pairs={{0,16},{8,24},{1,17},{9,25},{2,18},{10,26},{3,19},{11,27},{4,20},{... | collective-permute-start | bytes 344072 | tf_op jit(solution)/shard_map/ppermute | solution.py:14
  121.5 6.7 %collective-permute-start.2 = (f32[16,1792]{1,0:T(8,128)S(1)}, f32[16,1792]{1,0:T(8,128)S(1)}, u32[]{:S(2)}, u32[]{:S(2)}) collective-permute-start(f32[16,1792]{1,0:T(8,128)S(1)} %get-tuple-element.9), channel_id=1, source_target_pairs={{16,0},{24,8},{17,1},{25,9},{18,2},{26,10},{19,3},{27,11},{20,4},{... | collective-permute-start | bytes 344072 | tf_op jit(solution)/shard_map/ppermute | solution.py:14
  129.2 63.5 %copy-start.4 = (bf16[16,1792]{1,0:T(8,128)(2,1)}, bf16[16,1792]{1,0:T(8,128)(2,1)S(1)}, u32[]{:S(2)}) copy-start(bf16[16,1792]{1,0:T(8,128)(2,1)S(1)} %get-tuple-element.8) | copy-start | bytes 172036
  192.7 1.3 collective-permute-start.3
Sparse Core Ops, SparseCore 0:
  49.9 67.0 reduce-scatter.1
where the time goes:
time: 203 us
  blocking collectives  96.8 us (48%)
  waiting for transfers between devices  72.8 us (36%)
  between operations  14.9 us (7%)
  other arithmetic  5.37 us (3%)
  starting transfers between devices  4.84 us (2%)
  local copies, waits for them, and re-layouts  4.12 us (2%)
  matrix products  4.02 us (2%)
    reduce_scatter x1, waiting for transfers between devices, on_device(): lax.psum_scatter(jnp.concatenate([jnp.dot(pair_acts, dec_own, preferred_e...  67.2 us
    all_gather x2, blocking collectives, on_device(): lax.all_gather((err_own, err_next), 'latent', axis=0, tiled=True)  62.6 us
    all_gather x1, blocking collectives, on_device(): whole_in = lax.all_gather(rows_in, 'latent', axis=0, tiled=True)  34.1 us
    ppermute x2, starting transfers between devices, from_behind(): return lax.ppermute(block, axis, route)  4.66 us
    ppermute x2, waiting for transfers between devices, from_behind(): return lax.ppermute(block, axis, route)  4.37 us
  transfers between devices with their start and end apart: 5, of which 3 were waited for; matrix products, arithmetic and copies ran while one was open for 1% of the time, Pallas kernels for 0%

commit v1 on v0

v1 whole, which is shorter than its diff:
```python
import jax
import jax.numpy as jnp
from jax import lax
from jax.sharding import PartitionSpec as P

BLOCK = 128


def halves_swapped(block):
    count = lax.axis_size("layer")
    return lax.ppermute(block, "layer", [(i, i ^ 1) for i in range(count)])


def shifted(block, distance):
    count = lax.axis_size("layer")
    route = [(i, i + distance) for i in range(count) if 0 <= i + distance < count]
    return lax.ppermute(block, "layer", route)


def neighbours_sums(own_sum, ahead_part):
    count = lax.axis_size("layer")
    if count == 4:
        first = lax.axis_index("layer") < 2
        sent = jnp.where(first, ahead_part, own_sum)
        got = lax.ppermute(sent, "layer", [(i, i ^ 2) for i in range(count)])
        nothing = jnp.zeros_like(got)
        return jnp.where(first, nothing, got), jnp.where(first, got, nothing)
    return shifted(ahead_part, 2), shifted(own_sum, -2)


def to_all(block):
    count = lax.axis_size("latent")
    copies = jnp.broadcast_to(block[None], (count,) + block.shape)
    return lax.all_to_all(copies, "latent", 0, 0).reshape((count * block.shape[0],) + block.shape[1:])


def on_device(resid, target, enc_weight, enc_bias, dec_weight, blocks):
    f32, bf16 = jnp.float32, jnp.bfloat16
    slots = lax.axis_size("latent")
    layer_slot = lax.axis_index("layer")
    layer, half = layer_slot // 2, layer_slot % 2
    slot = lax.axis_index("latent")
    _, rows, width = resid.shape
    tokens = rows * slots
    cols = width // 2
    weight = enc_weight[0]
    latents = weight.shape[1]
    decoder = dec_weight[0]
    dec_own = decoder[0].reshape(2 * latents, cols)
    dec_next = decoder[1].reshape(2 * latents, cols)

    mine = lax.dynamic_slice(resid, (layer, 0, half * cols), (1, rows, cols))[0]
    resid_half = to_all(mine)
    weight_mine = lax.dynamic_slice_in_dim(weight, half * cols, cols, 0)
    weight_other = halves_swapped(lax.dynamic_slice_in_dim(weight, (1 - half) * cols, cols, 0))
    bias_other = halves_swapped(enc_bias[0])
    weight_pair = jnp.concatenate(
        [
            jnp.where(half == 0, weight_mine, weight_other),
            jnp.where(half == 0, weight_other, weight_mine),
        ],
        axis=1,
    )
    bias_pair = jnp.concatenate(
        [jnp.where(half == 0, enc_bias[0], bias_other), jnp.where(half == 0, bias_other, enc_bias[0])]
    )
    listed = lax.dynamic_index_in_dim(blocks, layer, 0, keepdims=False)
    tile = tokens // listed.shape[0]
    per_device = latents // BLOCK
    firing = []
    for side in range(2):
        first = (side * slots + slot) * per_device
        names = first + jnp.arange(per_device)
        flags = jnp.any(listed[:, :, None] == names, axis=1).astype(f32)
        firing.append(jnp.repeat(jnp.repeat(flags, tile, axis=0), BLOCK, axis=1))
    gate_pair = jnp.concatenate(firing, axis=1)
    gate = jnp.where(half == 0, firing[0], firing[1])

    part = jnp.dot(resid_half, weight_pair, preferred_element_type=f32)
    preact = part + halves_swapped(part) + bias_pair
    acts = (preact * gate_pair).astype(bf16)
    resid_other = halves_swapped(resid_half)

    sums = jnp.concatenate(
        [
            jnp.dot(acts, dec_own, preferred_element_type=f32).astype(bf16),
            jnp.dot(acts, dec_next, preferred_element_type=f32).astype(bf16),
        ],
        axis=1,
    )
    pieces = lax.all_to_all(sums.reshape(slots, rows, width), "latent", 0, 0)
    totals = jnp.sum(pieces.astype(f32), axis=0)
    own_sum, ahead_part = totals[:, :cols], totals[:, cols:]
    behind, next_own = neighbours_sums(own_sum, ahead_part)
    wanted = lax.dynamic_slice(target, (layer, 0, half * cols), (2, rows, cols)).astype(f32)
    err_own = (own_sum + behind - wanted[0]).astype(bf16)
    err_next = (ahead_part + next_own - wanted[1]).astype(bf16)

    errs = to_all(jnp.concatenate([err_own, err_next], axis=1))
    across = (((1,), (1,)), ((), ()))
    grad_pair = lax.dot_general(errs[:, :cols], dec_own, across, preferred_element_type=f32)
    grad_pair = grad_pair + lax.dot_general(errs[:, cols:], dec_next, across, preferred_element_type=f32)
    lower, upper = grad_pair[:, :latents], grad_pair[:, latents:]
    kept = jnp.where(half == 0, lower, upper)
    sent = jnp.where(half == 0, upper, lower)
    grad_pre = (kept + halves_swapped(sent)) * gate
    bias_grad = jnp.sum(grad_pre, axis=0)[None, :]
    grad_low = grad_pre.astype(bf16)
    whole = jnp.concatenate(
        [jnp.where(half == 0, resid_half, resid_other), jnp.where(half == 0, resid_other, resid_half)], axis=1
    )
    enc_grad = lax.dot_general(whole, grad_low, (((0,), (0,)), ((), ())), preferred_element_type=f32)
    return err_own[None], enc_grad.astype(bf16)[None], bias_grad


def solution(mesh):
    return jax.shard_map(
        on_device,
        mesh=mesh,
        in_specs=(
            P(None, "latent", None),
            P(None, "latent", None),
            P("layer", None, "latent"),
            P("layer", "latent"),
            P("layer", None, None, "latent", None),
            P(),
        ),
        out_specs=(P("layer", "latent", None), P("layer", None, "latent"), P("layer", "latent")),
        check_vma=False,
    )
```

time: 203 us -> 92 us (0.45)
  blocking collectives: 96.8 us -> 0 us
  waiting for transfers between devices: 72.8 us -> 58.3 us
  between operations: 14.9 us -> 2.16 us
  starting transfers between devices: 4.84 us -> 16.8 us
    all_gather x3 -> x0, blocking collectives: 96.8 us -> none  [the longest x2 62.6 us: on_device(): lax.all_gather((err_own, err_next), 'latent', axis=0, tiled=True)]
    reduce_scatter x1 -> x0, waiting for transfers between devices: 67.2 us -> none  [on_device(): lax.psum_scatter(jnp.concatenate([jnp.dot(pair_acts, dec_own, preferred_e...]
    all_to_all x0 -> x3, waiting for transfers between devices: none -> 54.5 us  [the longest x2 31.1 us: to_all(): lax.all_to_all(copies, 'latent', 0, 0)]
    all_to_all x0 -> x3, starting transfers between devices: none -> 14.3 us  [the longest x2 10.7 us: to_all(): lax.all_to_all(copies, 'latent', 0, 0)]
    ppermute x4 -> x6, starting transfers between devices: 4.81 us -> 2.47 us  [the longest x1 1.58 us: neighbours_sums(): got = lax.ppermute(sent, 'layer', [(i, i ^ 2) for i in range(count)])]
    select_n x2 -> x5, other arithmetic: 0.02 us -> 2.31 us  [the longest x1 1.2 us: on_device(): jnp.where(half == 0, weight_mine, weight_other)]
    ppermute x4 -> x6, waiting for transfers between devices: 5.61 us -> 3.8 us  [the longest x1 2.36 us: neighbours_sums(): got = lax.ppermute(sent, 'layer', [(i, i ^ 2) for i in range(count)])]
  transfers between devices with their start and end apart: 5 -> 9, of which waited for: 3 -> 6; matrix products, arithmetic and copies ran while one was open for 1% -> 8% of each run, Pallas kernels for 0% -> 0%
where the time goes in v1:
time: 92 us; the launch traced here: 91.5 us
  waiting for transfers between devices  58.3 us (63%)
  starting transfers between devices  16.8 us (18%)
  other arithmetic  5.62 us (6%)
  local copies, waits for them, and re-layouts  5.45 us (6%)
  matrix products  3.16 us (3%)
  between operations  2.16 us (2%)
    all_to_all x2, waiting for transfers between devices, to_all(): lax.all_to_all(copies, 'latent', 0, 0)  31.1 us
    all_to_all x1, waiting for transfers between devices, on_device(): pieces = lax.all_to_all(sums.reshape(slots, rows, width), 'latent', 0, 0)  23.4 us
    all_to_all x2, starting transfers between devices, to_all(): lax.all_to_all(copies, 'latent', 0, 0)  10.7 us
    all_to_all x1, starting transfers between devices, on_device(): pieces = lax.all_to_all(sums.reshape(slots, rows, width), 'latent', 0, 0)  3.64 us
    ppermute x1, waiting for transfers between devices, neighbours_sums(): got = lax.ppermute(sent, 'layer', [(i, i ^ 2) for i in range(count)])  2.36 us
    dynamic_slice x1, local copies, waits for them, and re-layouts, on_device(): lax.dynamic_slice_in_dim(weight, (1 - half) * cols, cols, 0)  1.92 us
  transfers between devices with their start and end apart: 9, of which 6 were waited for; matrix products, arithmetic and copies ran while one was open for 8% of the time, Pallas kernels for 0%

profile of v1, /device:TPU:0, one launch (start us, length us, event | category | flops | bytes accessed | tf_op | source)
XLA Modules:
  0.0 91.5 jit_solution(6629060545960339551)
XLA Ops:
  0.6 0.0 copy-start
  0.6 0.0 copy-start.3
  0.7 0.0 copy-start.4
  0.7 1.9 %dynamic-slice_bitcast_fusion = bf16[1792,128]{1,0:T(8,128)(2,1)} fusion(bf16[1,3584,128]{2,1,0:T(8,128)(2,1)} %param.8, s32[]{:T(128)S(6)} %select_n.103), kind=kLoop, calls=%fused_computation.19 | loop fusion | bytes 917508 | tf_op jit(solution)/shard_map/dynamic_slice | solution.py:55
  2.6 0.5 collective-permute-start
  3.1 0.0 copy-done
  3.1 0.8 broadcast_in_dim.15
  3.9 6.8 %all-to-all-start = ((bf16[8,16,1792]{2,1,0:T(8,128)(2,1)}), bf16[8,16,1792]{2,1,0:T(8,128)(2,1)S(1)}, u32[]{:S(2)}, u32[]{:S(2)}) async-start(bf16[8,16,1792]{2,1,0:T(8,128)(2,1)} %broadcast_in_dim.15), calls=%async_computation | async-start | bytes 917504 | tf_op jit(solution)/shard_map/all_to_all | solution.py:34
  10.7 0.0 copy-done.3
  10.7 0.3 collective-permute-start.2
  11.0 0.0 copy-done.4
  11.0 0.6 compare_reduce_fusion
  12.9 0.0 copy-start.1
  13.0 1.7 %fusion.19 = (bf16[1,1,2,128,1792]{4,3,2,1,0:T(8,128)(2,1)S(1)}, bf16[1,1,2,128,1792]{4,3,2,1,0:T(8,128)(2,1)S(1)}) fusion(bf16[1,2,2,128,1792]{4,3,2,1,0:T(8,128)(2,1)} %param.10), kind=kLoop, calls=%fused_computation.45 | loop fusion | bytes 3670016 | tf_op jit(solution)/shard_map/slice | solution.py:49
  14.6 0.0 collective-permute-done
  14.6 0.0 copy-done.1
  14.7 1.2 %bitcast_select_fusion.1 = (bf16[1792,128]{1,0:T(8,128)(2,1)S(1)}, bf16[1792,128]{1,0:T(8,128)(2,1)S(1)}) fusion(bf16[1792,128]{1,0:T(8,128)(2,1)} %collective-permute-done, pred[]{:T(512)S(6)} %eq.47, bf16[1,3584,128]{2,1,0:T(8,128)(2,1)S(1)} %copy-done.1, s32[]{:T(128)S(6)} %select_n.101), kind=kLoop, calls=%fused_computation.18 | loop fusion | flops 458752 | bytes 1835013 | tf_op jit(solution)/shard_map/jit(_where)/select_n | solution.py:59
  15.9 8.6 %all-to-all-done = bf16[8,16,1792]{2,1,0:T(8,128)(2,1)S(1)} async-done(((bf16[8,16,1792]{2,1,0:T(8,128)(2,1)}), bf16[8,16,1792]{2,1,0:T(8,128)(2,1)S(1)}, u32[]{:S(2)}, u32[]{:S(2)}) %all-to-all-start) | async-done | bytes 458784 | tf_op jit(solution)/shard_map/all_to_all | solution.py:34
  24.4 0.3 fusion.1
  24.7 0.1 collective-permute-start.1
  24.8 0.0 collective-permute-done.2
  24.8 1.3 %collective-permute-done.1 = f32[128,256]{1,0:T(8,128)S(1)} collective-permute-done((f32[128,256]{1,0:T(8,128)S(1)}, f32[128,256]{1,0:T(8,128)S(1)}, u32[]{:S(2)}, u32[]{:S(2)}) %collective-permute-start.1) | collective-permute-done | bytes 131104 | tf_op jit(solution)/shard_map/ppermute | solution.py:11
  26.2 0.3 convolution_convert_fusion.1
  26.5 0.3 convolution_convert_fusion.2
  26.8 1.0 %pad_maximum_fusion = bf16[128,3584]{1,0:T(8,128)(2,1)} fusion(bf16[128,1792]{1,0:T(8,128)(2,1)S(1)} %convolution_convert_fusion.1, bf16[128,1792]{1,0:T(8,128)(2,1)S(1)} %convolution_convert_fusion.2), kind=kLoop, calls=%fused_computation.10 | loop fusion | flops 1835008 | bytes 1835008 | tf_op jit(solution)/shard_map/concatenate | solution.py:84
  27.8 3.6 %all-to-all-start.1 = ((bf16[8,16,3584]{2,1,0:T(8,128)(2,1)}), bf16[8,16,3584]{2,1,0:T(8,128)(2,1)S(1)}, u32[]{:S(2)}, u32[]{:S(2)}) async-start(bf16[8,16,3584]{2,1,0:T(8,128)(2,1)} %bitcast.7), calls=%async_computation.1 | async-start | bytes 1835008 | tf_op jit(solution)/shard_map/all_to_all | solution.py:91
  31.4 23.4 %all-to-all-done.1 = bf16[8,16,3584]{2,1,0:T(8,128)(2,1)S(1)} async-done(((bf16[8,16,3584]{2,1,0:T(8,128)(2,1)}), bf16[8,16,3584]{2,1,0:T(8,128)(2,1)S(1)}, u32[]{:S(2)}, u32[]{:S(2)}) %all-to-all-start.1) | async-done | bytes 917536 | tf_op jit(solution)/shard_map/all_to_all | solution.py:91
  54.8 0.1 convert_reduce_fusion
  55.0 1.6 %collective-permute-start.3 = (f32[16,1792]{1,0:T(8,128)S(1)}, f32[16,1792]{1,0:T(8,128)S(1)}, u32[]{:S(2)}, u32[]{:S(2)}) collective-permute-start(f32[16,1792]{1,0:T(8,128)S(1)} %slice_select_fusion), channel_id=1, source_target_pairs={{0,16},{8,24},{16,0},{24,8},{1,17},{9,25},{17,1},{25,9},{2,18},{10... | collective-permute-start | bytes 344072 | tf_op jit(solution)/shard_map/ppermute | solution.py:25
  56.5 0.9 dynamic-slice_convert_fusion
  57.5 2.4 %collective-permute-done.3 = f32[16,1792]{1,0:T(8,128)S(1)} collective-permute-done((f32[16,1792]{1,0:T(8,128)S(1)}, f32[16,1792]{1,0:T(8,128)S(1)}, u32[]{:S(2)}, u32[]{:S(2)}) %collective-permute-start.3) | collective-permute-done | bytes 114720 | tf_op jit(solution)/shard_map/ppermute | solution.py:25
  59.9 0.0 copy-start.2
  59.9 1.0 %broadcast_in_dim.36 = bf16[8,16,3584]{2,1,0:T(8,128)(2,1)} broadcast(bf16[16,3584]{1,0:T(8,128)(2,1)S(1)} %pad_maximum_fusion.1), dimensions={1,2} | broadcast | bytes 1032192 | tf_op jit(solution)/shard_map/broadcast_in_dim | solution.py:33
  60.9 3.9 %all-to-all-start.2 = ((bf16[8,16,3584]{2,1,0:T(8,128)(2,1)}), bf16[8,16,3584]{2,1,0:T(8,128)(2,1)S(1)}, u32[]{:S(2)}, u32[]{:S(2)}) async-start(bf16[8,16,3584]{2,1,0:T(8,128)(2,1)} %broadcast_in_dim.36), calls=%async_computation.2 | async-start | bytes 1835008 | tf_op jit(solution)/shard_map/all_to_all | solution.py:34
  64.8 0.0 collective-permute-start.4
  64.8 22.5 %all-to-all-done.2 = bf16[8,16,3584]{2,1,0:T(8,128)(2,1)S(1)} async-done(((bf16[8,16,3584]{2,1,0:T(8,128)(2,1)}), bf16[8,16,3584]{2,1,0:T(8,128)(2,1)S(1)}, u32[]{:S(2)}, u32[]{:S(2)}) %all-to-all-start.2) | async-done | bytes 917536 | tf_op jit(solution)/shard_map/all_to_all | solution.py:34
  87.3 0.5 fusion.9
  87.8 0.0 copy-done.2
  87.8 0.5 convolution_add_fusion
  88.2 0.1 collective-permute-start.5
  88.3 0.0 collective-permute-done.4
  88.3 1.1 %broadcast_select_fusion.1 = (bf16[128,1792]{1,0:T(8,128)(2,1)S(1)}, bf16[128,1792]{1,0:T(8,128)(2,1)S(1)}) fusion(bf16[128,1792]{1,0:T(8,128)(2,1)} %collective-permute-done.4, pred[]{:T(512)S(6)} %eq.47, bf16[8,16,1792]{2,1,0:T(8,128)(2,1)S(1)} %all-to-all-done), kind=kLoop, calls=%fused_computation.21 | loop fusion | flops 458752 | bytes 1835009 | tf_op jit(solution)/shard_map/jit(_where)/select_n | solution.py:110
  89.4 0.1 collective-permute-done.5
  89.6 0.5 fusion.18
  90.1 1.4 %fusion = bf16[1,3584,128]{2,1,0:T(8,128)(2,1)} fusion(bf16[128,1792]{1,0:T(8,128)(2,1)S(1)} %get-tuple-element.12, bf16[128,1792]{1,0:T(8,128)(2,1)S(1)} %get-tuple-element.11, bf16[128,128]{1,0:T(8,128)(2,1)S(1)} %get-tuple-element.6), kind=kOutput, calls=%fused_computation.1 | convolution fusion | flops 119734272 | bytes 1867776 | tf_op jit(solution)/shard_map/dot_general | solution.py:112
  (10 shorter events, 0.1 us)
Async XLA Ops:
  0.6 2.4 %copy-start = (bf16[2,16,3584]{2,1,0:T(8,128)(2,1)S(1)}, bf16[2,16,3584]{2,1,0:T(8,128)(2,1)}, u32[]{:S(2)}) copy-start(bf16[2,16,3584]{2,1,0:T(8,128)(2,1)} %param.6) | copy-start | bytes 688132
  0.6 10.0 %copy-start.3 = (f32[1,128]{1,0:T(1,128)S(1)}, f32[1,128]{1,0:T(1,128)}, u32[]{:S(2)}) copy-start(f32[1,128]{1,0:T(1,128)} %param.9) | copy-start | bytes 1540
  0.7 10.3 %copy-start.4 = (s32[2,1,12]{2,1,0:T(1,128)S(1)}, s32[2,1,12]{2,1,0:T(1,128)}, u32[]{:S(2)}) copy-start(s32[2,1,12]{2,1,0:T(1,128)} %param.11) | copy-start | bytes 292
  2.6 12.0 %collective-permute-start = (bf16[1792,128]{1,0:T(8,128)(2,1)}, bf16[1792,128]{1,0:T(8,128)(2,1)}, u32[]{:S(2)}, u32[]{:S(2)}) collective-permute-start(bf16[1792,128]{1,0:T(8,128)(2,1)} %dynamic-slice_bitcast_fusion), channel_id=1, source_target_pairs={{0,8},{8,0},{16,24},{24,16},{1,9},{9,1},{17,25},{25,17},{2,10},{10... | collective-permute-start | bytes 1376264 | tf_op jit(solution)/shard_map/ppermute | solution.py:11
  3.9 20.6 %all-to-all-start = ((bf16[8,16,1792]{2,1,0:T(8,128)(2,1)}), bf16[8,16,1792]{2,1,0:T(8,128)(2,1)S(1)}, u32[]{:S(2)}, u32[]{:S(2)}) async-start(bf16[8,16,1792]{2,1,0:T(8,128)(2,1)} %broadcast_in_dim.15), calls=%async_computation | async-start | bytes 917504 | tf_op jit(solution)/shard_map/all_to_all | solution.py:34
  10.7 14.1 %collective-permute-start.2 = (f32[128]{0:T(128)S(1)}, f32[128]{0:T(128)S(1)}, u32[]{:S(2)}, u32[]{:S(2)}) collective-permute-start(f32[128]{0:T(128)S(1)} %bitcast.51), channel_id=1, source_target_pairs={{0,8},{8,0},{16,24},{24,16},{1,9},{9,1},{17,25},{25,17},{2,10},{10... | collective-permute-start | bytes 1544 | tf_op jit(solution)/shard_map/ppermute | solution.py:11
  12.9 1.7 %copy-start.1 = (bf16[1,3584,128]{2,1,0:T(8,128)(2,1)S(1)}, bf16[1,3584,128]{2,1,0:T(8,128)(2,1)}, u32[]{:S(2)}) copy-start(bf16[1,3584,128]{2,1,0:T(8,128)(2,1)} %param.8) | copy-start | bytes 2752516
  24.7 1.4 %collective-permute-start.1 = (f32[128,256]{1,0:T(8,128)S(1)}, f32[128,256]{1,0:T(8,128)S(1)}, u32[]{:S(2)}, u32[]{:S(2)}) collective-permute-start(f32[128,256]{1,0:T(8,128)S(1)} %fusion.1), channel_id=1, source_target_pairs={{0,8},{8,0},{16,24},{24,16},{1,9},{9,1},{17,25},{25,17},{2,10},{10... | collective-permute-start | bytes 393224 | tf_op jit(solution)/shard_map/ppermute | solution.py:11
  27.8 27.0 %all-to-all-start.1 = ((bf16[8,16,3584]{2,1,0:T(8,128)(2,1)}), bf16[8,16,3584]{2,1,0:T(8,128)(2,1)S(1)}, u32[]{:S(2)}, u32[]{:S(2)}) async-start(bf16[8,16,3584]{2,1,0:T(8,128)(2,1)} %bitcast.7), calls=%async_computation.1 | async-start | bytes 1835008 | tf_op jit(solution)/shard_map/all_to_all | solution.py:91
  55.0 4.9 %collective-permute-start.3 = (f32[16,1792]{1,0:T(8,128)S(1)}, f32[16,1792]{1,0:T(8,128)S(1)}, u32[]{:S(2)}, u32[]{:S(2)}) collective-permute-start(f32[16,1792]{1,0:T(8,128)S(1)} %slice_select_fusion), channel_id=1, source_target_pairs={{0,16},{8,24},{16,0},{24,8},{1,17},{9,25},{17,1},{25,9},{2,18},{10... | collective-permute-start | bytes 344072 | tf_op jit(solution)/shard_map/ppermute | solution.py:25
  59.9 27.9 %copy-start.2 = (bf16[16,1792]{1,0:T(8,128)(2,1)}, bf16[16,1792]{1,0:T(8,128)(2,1)S(1)}, u32[]{:S(2)}) copy-start(bf16[16,1792]{1,0:T(8,128)(2,1)S(1)} %get-tuple-element.14) | copy-start | bytes 172036
  60.9 26.4 %all-to-all-start.2 = ((bf16[8,16,3584]{2,1,0:T(8,128)(2,1)}), bf16[8,16,3584]{2,1,0:T(8,128)(2,1)S(1)}, u32[]{:S(2)}, u32[]{:S(2)}) async-start(bf16[8,16,3584]{2,1,0:T(8,128)(2,1)} %broadcast_in_dim.36), calls=%async_computation.2 | async-start | bytes 1835008 | tf_op jit(solution)/shard_map/all_to_all | solution.py:34
  64.8 23.5 %collective-permute-start.4 = (bf16[128,1792]{1,0:T(8,128)(2,1)S(1)}, bf16[128,1792]{1,0:T(8,128)(2,1)}, u32[]{:S(2)}, u32[]{:S(2)}) collective-permute-start(bf16[128,1792]{1,0:T(8,128)(2,1)S(1)} %bitcast.48), channel_id=1, source_target_pairs={{0,8},{8,0},{16,24},{24,16},{1,9},{9,1},{17,25},{25,17},{2,10},{10... | collective-permute-start | bytes 1376264 | tf_op jit(solution)/shard_map/ppermute | solution.py:11
  88.2 1.3 %collective-permute-start.5 = (f32[128,128]{1,0:T(8,128)S(1)}, f32[128,128]{1,0:T(8,128)S(1)}, u32[]{:S(2)}, u32[]{:S(2)}) collective-permute-start(f32[128,128]{1,0:T(8,128)S(1)} %slice_select_fusion.1), channel_id=1, source_target_pairs={{0,8},{8,0},{16,24},{24,16},{1,9},{9,1},{17,25},{25,17},{2,10},{10... | collective-permute-start | bytes 196616 | tf_op jit(solution)/shard_map/ppermute | solution.py:11

commit v2 on v0

v2 whole, which is shorter than its diff:
```python
import jax
import jax.numpy as jnp
from jax import lax
from jax.sharding import PartitionSpec as P

BLOCK = 128
F32, BF16 = jnp.float32, jnp.bfloat16


def crossed(block, axis, mask):
    return lax.ppermute(block, axis, [(i, i ^ mask) for i in range(lax.axis_size(axis))])


def times(left, right):
    return jnp.dot(left, right, preferred_element_type=F32)


def times_transposed(left, right):
    return lax.dot_general(left, right, (((1,), (1,)), ((), ())), preferred_element_type=F32)


def both_halves(half, mine, other, axis):
    return jnp.concatenate([jnp.where(half == 0, mine, other), jnp.where(half == 0, other, mine)], axis=axis)


def gates(blocks, layer, slot, slots, latents, tokens):
    listed = lax.dynamic_index_in_dim(blocks, layer, 0, keepdims=False)
    tile = tokens // listed.shape[0]
    here = latents // BLOCK
    out = []
    for side in range(2):
        names = (side * slots + slot) * here + jnp.arange(here)
        flags = jnp.any(listed[:, :, None] == names, axis=1).astype(F32)
        out.append(jnp.repeat(jnp.repeat(flags, tile, axis=0), BLOCK, axis=1))
    return out


def paired_encoder(weight, bias, half, cols):
    other = crossed(lax.dynamic_slice_in_dim(weight, (1 - half) * cols, cols, 0), "layer", 1)
    mine = lax.dynamic_slice_in_dim(weight, half * cols, cols, 0)
    return both_halves(half, mine, other, 1), both_halves(half, bias, crossed(bias, "layer", 1), 0)


def encoder_gradient(resid_half, resid_other, grad_low, half):
    whole = both_halves(half, resid_half, resid_other, 1)
    grad = lax.dot_general(whole, grad_low, (((0,), (0,)), ((), ())), preferred_element_type=F32)
    return grad.astype(BF16)


def two_layers(resid, target, enc_weight, enc_bias, dec_weight, blocks):
    slots = lax.axis_size("latent")
    far = slots // 2
    layer, half = lax.axis_index("layer") // 2, lax.axis_index("layer") % 2
    slot = lax.axis_index("latent")
    _, rows, width = resid.shape
    tokens, cols, part = rows * slots, width // 2, width // 4
    latents = enc_weight.shape[2]
    near_rows = tokens // 2
    decoder = dec_weight[0].reshape(2, 2 * latents, cols)

    mine = lax.dynamic_slice(resid, (layer, 0, half * cols), (1, rows, cols))[0]
    along = [mine] + [crossed(mine, "latent", 2 * k) for k in range(1, far)]
    beside = [crossed(block, "latent", 1) for block in along]
    resid_half = jnp.concatenate(along + beside, axis=0)

    shared = lax.dynamic_index_in_dim(decoder, 1 - layer, 0, keepdims=False)
    dec_given = crossed(lax.dynamic_slice_in_dim(shared, (1 - layer) * part, part, 1), "layer", 2)
    dec_kept = lax.dynamic_slice_in_dim(shared, layer * part, part, 1)
    dec_own = lax.dynamic_index_in_dim(decoder, layer, 0, keepdims=False)
    weight_pair, bias_pair = paired_encoder(enc_weight[0], enc_bias[0], half, cols)
    firing = gates(blocks, layer, slot, slots, latents, tokens)
    gate = jnp.where(half == 0, firing[0], firing[1])

    partial = times(resid_half, weight_pair)
    preact = partial + crossed(partial, "layer", 1) + bias_pair
    acts = (preact * jnp.concatenate(firing, axis=1)).astype(BF16)
    acts_other = crossed(acts, "layer", 2)
    resid_other = crossed(resid_half, "layer", 1)

    def scattered(product):
        leaving = product(slice(near_rows, tokens)).astype(BF16)
        near = product(slice(0, near_rows)) + crossed(leaving, "latent", 1).astype(F32)
        total = near[:rows]
        for k in range(1, far):
            total = total + crossed(near[k * rows:(k + 1) * rows].astype(BF16), "latent", 2 * k).astype(F32)
        return total

    def gathered(block):
        along = [block] + [crossed(block, "latent", 2 * k) for k in range(1, far)]
        near = jnp.concatenate(along, axis=0)
        return jnp.concatenate([near, crossed(near, "latent", 1)], axis=0)

    sum_own = scattered(lambda at: times(acts[at], dec_own))
    sum_shared = scattered(lambda at: times(acts[at], dec_kept) + times(acts_other[at], dec_given))
    wanted_own = lax.dynamic_slice(target, (2 * layer, 0, half * cols), (1, rows, cols))[0]
    wanted_shared = lax.dynamic_slice(target, (1, 0, half * cols + layer * part), (1, rows, part))[0]
    err_own = (sum_own - wanted_own.astype(F32)).astype(BF16)
    err_shared = (sum_shared - wanted_shared.astype(F32)).astype(BF16)
    err_across = crossed(err_shared, "layer", 2)
    errors = jnp.where(layer == 0, err_own, jnp.concatenate([err_across, err_shared], axis=1))

    errs_own, errs_shared = gathered(err_own), gathered(err_shared)
    back = times_transposed(errs_shared, dec_given).astype(BF16)
    here = times_transposed(errs_own, dec_own) + times_transposed(errs_shared, dec_kept)

    def of_half(pair, which):
        return jnp.where(which == 0, pair[:, :latents], pair[:, latents:])

    grad = of_half(here, half) + crossed(of_half(here, 1 - half), "layer", 1)
    grad = grad + crossed(of_half(back, half), "layer", 2).astype(F32)
    grad = grad + crossed(of_half(back, 1 - half), "layer", 3).astype(F32)
    grad_pre = grad * gate
    bias_grad = jnp.sum(grad_pre, axis=0)[None, :]
    enc_grad = encoder_gradient(resid_half, resid_other, grad_pre.astype(BF16), half)
    return errors[None], enc_grad[None], bias_grad


def any_layers(resid, target, enc_weight, enc_bias, dec_weight, blocks):
    slots = lax.axis_size("latent")
    count = lax.axis_size("layer")
    layer, half = lax.axis_index("layer") // 2, lax.axis_index("layer") % 2
    slot = lax.axis_index("latent")
    _, rows, width = resid.shape
    tokens, cols = rows * slots, width // 2
    latents = enc_weight.shape[2]
    decoder = dec_weight[0].reshape(2, 2 * latents, cols)

    def to_all(block):
        copies = jnp.broadcast_to(block[None], (slots,) + block.shape)
        return lax.all_to_all(copies, "latent", 0, 0).reshape(tokens, block.shape[1])

    def shifted(block, distance):
        route = [(i, i + distance) for i in range(count) if 0 <= i + distance < count]
        return lax.ppermute(block, "layer", route)

    resid_half = to_all(lax.dynamic_slice(resid, (layer, 0, half * cols), (1, rows, cols))[0])
    weight_pair, bias_pair = paired_encoder(enc_weight[0], enc_bias[0], half, cols)
    firing = gates(blocks, layer, slot, slots, latents, tokens)
    gate = jnp.where(half == 0, firing[0], firing[1])
    partial = times(resid_half, weight_pair)
    preact = partial + crossed(partial, "layer", 1) + bias_pair
    acts = (preact * jnp.concatenate(firing, axis=1)).astype(BF16)
    resid_other = crossed(resid_half, "layer", 1)

    sums = jnp.concatenate([times(acts, decoder[t]).astype(BF16) for t in range(2)], axis=1)
    pieces = lax.all_to_all(sums.reshape(slots, rows, width), "latent", 0, 0)
    totals = jnp.sum(pieces.astype(F32), axis=0)
    own_sum, ahead_part = totals[:, :cols], totals[:, cols:]
    wanted = lax.dynamic_slice(target, (layer, 0, half * cols), (2, rows, cols)).astype(F32)
    err_own = (own_sum + shifted(ahead_part, 2) - wanted[0]).astype(BF16)
    err_next = (ahead_part + shifted(own_sum, -2) - wanted[1]).astype(BF16)
    errs = to_all(jnp.concatenate([err_own, err_next], axis=1))
    here = times_transposed(errs[:, :cols], decoder[0]) + times_transposed(errs[:, cols:], decoder[1])
    lower, upper = here[:, :latents], here[:, latents:]
    grad = jnp.where(half == 0, lower, upper) + crossed(jnp.where(half == 0, upper, lower), "layer", 1)
    grad_pre = grad * gate
    bias_grad = jnp.sum(grad_pre, axis=0)[None, :]
    enc_grad = encoder_gradient(resid_half, resid_other, grad_pre.astype(BF16), half)
    return err_own[None], enc_grad[None], bias_grad


def solution(mesh):
    small = mesh.shape["layer"] == 4 and mesh.shape["latent"] == 8
    return jax.shard_map(
        two_layers if small else any_layers,
        mesh=mesh,
        in_specs=(
            P(None, "latent", None),
            P(None, "latent", None),
            P("layer", None, "latent"),
            P("layer", "latent"),
            P("layer", None, None, "latent", None),
            P(),
        ),
        out_specs=(P("layer", "latent", None), P("layer", None, "latent"), P("layer", "latent")),
        check_vma=False,
    )
```

time: 203 us -> 79.8 us (0.39)
  blocking collectives: 96.8 us -> 0 us
  waiting for transfers between devices: 72.8 us -> 27.7 us
  starting transfers between devices: 4.84 us -> 36.7 us
  between operations: 14.9 us -> 2.3 us
    all_gather x3 -> x0, blocking collectives: 96.8 us -> none  [the longest x2 62.6 us: on_device(): lax.all_gather((err_own, err_next), 'latent', axis=0, tiled=True)]
    reduce_scatter x1 -> x0, waiting for transfers between devices: 67.2 us -> none  [on_device(): lax.psum_scatter(jnp.concatenate([jnp.dot(pair_acts, dec_own, preferred_e...]
    ppermute x4 -> x33, starting transfers between devices: 4.81 us -> 36.7 us  [crossed(): lax.ppermute(block, axis, [(i, i ^ mask) for i in range(lax.axis_size(axi...]
    ppermute x4 -> x33, waiting for transfers between devices: 5.61 us -> 27.7 us  [crossed(): lax.ppermute(block, axis, [(i, i ^ mask) for i in range(lax.axis_size(axi...]
    slice x2, local copies, waits for them, and re-layouts: 2.09 us -> 0.02 us  [scattered(): near[k * rows:(k + 1) * rows].astype(BF16)]
    dot_general x6 -> x11, matrix products: 4.02 us -> 4.42 us  [the longest x7 1.95 us: times(): return jnp.dot(left, right, preferred_element_type=F32)]
  transfers between devices with their start and end apart: 5 -> 33, of which waited for: 3 -> 15; matrix products, arithmetic and copies ran while one was open for 1% -> 12% of each run, Pallas kernels for 0% -> 0%
where the time goes in v2:
time: 79.8 us; the launch traced here: 79.5 us
  starting transfers between devices  36.7 us (46%)
  waiting for transfers between devices  27.7 us (35%)
  other arithmetic  4.46 us (6%)
  matrix products  4.42 us (6%)
  local copies, waits for them, and re-layouts  3.95 us (5%)
  between operations  2.3 us (3%)
    ppermute x33, starting transfers between devices, crossed(): lax.ppermute(block, axis, [(i, i ^ mask) for i in range(lax.axis_size(axi...  36.7 us
    ppermute x33, waiting for transfers between devices, crossed(): lax.ppermute(block, axis, [(i, i ^ mask) for i in range(lax.axis_size(axi...  27.7 us
    dot_general x7, matrix products, times(): return jnp.dot(left, right, preferred_element_type=F32)  1.95 us
    dynamic_slice x1, local copies, waits for them, and re-layouts, paired_encoder(): lax.dynamic_slice_in_dim(weight, (1 - half) * cols, cols, 0)  1.81 us
    unnamed x2, other arithmetic  1.63 us
  transfers between devices with their start and end apart: 33, of which 15 were waited for; matrix products, arithmetic and copies ran while one was open for 12% of the time, Pallas kernels for 0%

profile of v2, /device:TPU:0, one launch (start us, length us, event | category | flops | bytes accessed | tf_op | source)
XLA Modules:
  0.0 79.5 jit_solution(693602927255144230)
XLA Ops:
  0.7 1.0 %constant_dynamic-update-slice_fusion.7 = (bf16[128,1792]{1,0:T(8,128)(2,1)S(1)}, bf16[16,1792]{1,0:T(8,128)(2,1)S(1)}) fusion(bf16[2,16,3584]{2,1,0:T(8,128)(2,1)} %param.6, s32[]{:T(128)S(6)} %select_n.124, s32[]{:T(128)S(6)} %select_n.126), kind=kLoop, calls=%fused_computation.64 | loop fusion | bytes 172040
  1.7 3.0 %collective-permute-start = (bf16[16,1792]{1,0:T(8,128)(2,1)S(1)}, bf16[16,1792]{1,0:T(8,128)(2,1)S(1)}, u32[]{:S(2)}, u32[]{:S(2)}) collective-permute-start(bf16[16,1792]{1,0:T(8,128)(2,1)S(1)} %get-tuple-element.12), channel_id=1, source_target_pairs={{0,2},{1,3},{2,0},{3,1},{4,6},{5,7},{6,4},{7,5},{8,10},{9,11},{10,... | collective-permute-start | bytes 172040 | tf_op jit(solution)/shard_map/ppermute | solution.py:11
  4.7 2.6 %collective-permute-start.1 = (bf16[16,1792]{1,0:T(8,128)(2,1)S(1)}, bf16[16,1792]{1,0:T(8,128)(2,1)S(1)}, u32[]{:S(2)}, u32[]{:S(2)}) collective-permute-start(bf16[16,1792]{1,0:T(8,128)(2,1)S(1)} %get-tuple-element.12), channel_id=1, source_target_pairs={{0,4},{1,5},{2,6},{3,7},{4,0},{5,1},{6,2},{7,3},{8,12},{9,13},{10,... | collective-permute-start | bytes 172040 | tf_op jit(solution)/shard_map/ppermute | solution.py:11
  7.3 1.7 %collective-permute-start.3 = (bf16[16,1792]{1,0:T(8,128)(2,1)S(1)}, bf16[16,1792]{1,0:T(8,128)(2,1)S(1)}, u32[]{:S(2)}, u32[]{:S(2)}) collective-permute-start(bf16[16,1792]{1,0:T(8,128)(2,1)S(1)} %get-tuple-element.12), channel_id=1, source_target_pairs={{0,1},{1,0},{2,3},{3,2},{4,5},{5,4},{6,7},{7,6},{8,9},{9,8},{10,11... | collective-permute-start | bytes 172040 | tf_op jit(solution)/shard_map/ppermute | solution.py:11
  9.0 1.8 %dynamic-slice_bitcast_fusion.1 = bf16[1792,128]{1,0:T(8,128)(2,1)} fusion(bf16[1,3584,128]{2,1,0:T(8,128)(2,1)} %param.8, s32[]{:T(128)S(6)} %select_n.128), kind=kLoop, calls=%fused_computation.33 | loop fusion | bytes 917508 | tf_op jit(solution)/shard_map/dynamic_slice | solution.py:39
  10.8 1.3 %compare_reduce_fusion = (pred[]{:T(512)}, pred[]{:T(512)}) fusion(s32[]{:T(128)S(6)} %add_shard_map.3, s32[2,1,12]{2,1,0:T(1,128)} %param.11, s32[]{:T(128)S(6)} %select_n.124, s32[]{:T(128)S(6)} %axis_index.29), kind=kLoop, calls=%fused_computation.91 | loop fusion | flops 46 | bytes 62 | tf_op jit(solution)/shard_map/reduce_or | solution.py:33
  12.1 1.0 %dynamic-slice_bitcast_fusion = bf16[256,896]{1,0:T(8,128)(2,1)} fusion(bf16[2,256,1792]{2,1,0:T(8,128)(2,1)S(1)} %bitcast.55, s32[]{:T(128)S(6)} %select_n.136, s32[]{:T(128)S(6)} %select_n.140), kind=kLoop, calls=%fused_computation.31 | loop fusion | bytes 917512 | tf_op jit(solution)/shard_map/dynamic_slice | solution.py:67
  14.5 0.6 collective-permute-start.7
  15.1 1.6 %collective-permute-start.15 = (bf16[256,896]{1,0:T(8,128)(2,1)}, bf16[256,896]{1,0:T(8,128)(2,1)S(1)}, u32[]{:S(2)}, u32[]{:S(2)}) collective-permute-start(bf16[256,896]{1,0:T(8,128)(2,1)} %dynamic-slice_bitcast_fusion), channel_id=1, source_target_pairs={{0,16},{8,24},{16,0},{24,8},{1,17},{9,25},{17,1},{25,9},{2,18},{10... | collective-permute-start | bytes 1376264 | tf_op jit(solution)/shard_map/ppermute | solution.py:11
  16.7 0.6 collective-permute-start.4
  17.3 1.6 %collective-permute-start.5 = (bf16[16,1792]{1,0:T(8,128)(2,1)S(1)}, bf16[16,1792]{1,0:T(8,128)(2,1)S(1)}, u32[]{:S(2)}, u32[]{:S(2)}) collective-permute-start(bf16[16,1792]{1,0:T(8,128)(2,1)S(1)} %collective-permute-done.1), channel_id=1, source_target_pairs={{0,1},{1,0},{2,3},{3,2},{4,5},{5,4},{6,7},{7,6},{8,9},{9,8},{10,11... | collective-permute-start | bytes 172040 | tf_op jit(solution)/shard_map/ppermute | solution.py:11
  18.9 0.6 collective-permute-start.6
  19.5 1.8 %collective-permute-done.4 = bf16[16,1792]{1,0:T(8,128)(2,1)S(1)} collective-permute-done((bf16[16,1792]{1,0:T(8,128)(2,1)S(1)}, bf16[16,1792]{1,0:T(8,128)(2,1)S(1)}, u32[]{:S(2)}, u32[]{:S(2)}) %collective-permute-start.4) | collective-permute-done | bytes 57376 | tf_op jit(solution)/shard_map/ppermute | solution.py:11
  21.2 0.9 %collective-permute-done.5 = bf16[16,1792]{1,0:T(8,128)(2,1)S(1)} collective-permute-done((bf16[16,1792]{1,0:T(8,128)(2,1)S(1)}, bf16[16,1792]{1,0:T(8,128)(2,1)S(1)}, u32[]{:S(2)}, u32[]{:S(2)}) %collective-permute-start.5) | collective-permute-done | bytes 57376 | tf_op jit(solution)/shard_map/ppermute | solution.py:11
  22.2 0.9 %collective-permute-done.6 = bf16[16,1792]{1,0:T(8,128)(2,1)S(1)} collective-permute-done((bf16[16,1792]{1,0:T(8,128)(2,1)S(1)}, bf16[16,1792]{1,0:T(8,128)(2,1)S(1)}, u32[]{:S(2)}, u32[]{:S(2)}) %collective-permute-start.6) | collective-permute-done | bytes 57376 | tf_op jit(solution)/shard_map/ppermute | solution.py:11
  23.1 0.2 bitcast_select_fusion.1
  23.3 0.3 fusion.3
  23.6 0.5 collective-permute-start.8
  24.2 0.7 collective-permute-done.21
  25.0 0.2 collective-permute-done.8
  25.2 0.6 collective-permute-start.14
  25.8 0.3 fusion.19
  26.1 1.7 %collective-permute-done.15 = bf16[256,896]{1,0:T(8,128)(2,1)S(1)} collective-permute-done((bf16[256,896]{1,0:T(8,128)(2,1)}, bf16[256,896]{1,0:T(8,128)(2,1)S(1)}, u32[]{:S(2)}, u32[]{:S(2)}) %collective-permute-start.15) | collective-permute-done | bytes 458784 | tf_op jit(solution)/shard_map/ppermute | solution.py:11
  27.8 1.8 %collective-permute-done.14 = bf16[128,256]{1,0:T(8,128)(2,1)S(1)} collective-permute-done((bf16[128,256]{1,0:T(8,128)(2,1)S(1)}, bf16[128,256]{1,0:T(8,128)(2,1)S(1)}, u32[]{:S(2)}, u32[]{:S(2)}) %collective-permute-start.14) | collective-permute-done | bytes 65568 | tf_op jit(solution)/shard_map/ppermute | solution.py:11
  29.6 0.2 fusion.2
  29.8 0.9 %collective-permute-start.16 = (bf16[64,896]{1,0:T(8,128)(2,1)S(1)}, bf16[64,896]{1,0:T(8,128)(2,1)S(1)}, u32[]{:S(2)}, u32[]{:S(2)}) collective-permute-start(bf16[64,896]{1,0:T(8,128)(2,1)S(1)} %fusion.2), channel_id=1, source_target_pairs={{0,1},{1,0},{2,3},{3,2},{4,5},{5,4},{6,7},{7,6},{8,9},{9,8},{10,11... | collective-permute-start | bytes 344072 | tf_op jit(solution)/shard_map/ppermute | solution.py:11
  30.7 0.3 fusion.21
  31.0 3.6 %collective-permute-done.16 = bf16[64,896]{1,0:T(8,128)(2,1)S(1)} collective-permute-done((bf16[64,896]{1,0:T(8,128)(2,1)S(1)}, bf16[64,896]{1,0:T(8,128)(2,1)S(1)}, u32[]{:S(2)}, u32[]{:S(2)}) %collective-permute-start.16) | collective-permute-done | bytes 114720 | tf_op jit(solution)/shard_map/ppermute | solution.py:11
  34.7 0.2 fusion.60
  34.9 0.7 collective-permute-start.17
  35.7 3.5 %collective-permute-start.18 = (bf16[16,896]{1,0:T(8,128)(2,1)S(1)}, bf16[16,896]{1,0:T(8,128)(2,1)S(1)}, u32[]{:S(2)}, u32[]{:S(2)}) collective-permute-start(bf16[16,896]{1,0:T(8,128)(2,1)S(1)} %get-tuple-element.22), channel_id=1, source_target_pairs={{0,4},{1,5},{2,6},{3,7},{4,0},{5,1},{6,2},{7,3},{8,12},{9,13},{10,... | collective-permute-start | bytes 86024 | tf_op jit(solution)/shard_map/ppermute | solution.py:11
  39.2 0.2 collective-permute-start.19
  39.4 0.3 convolution_convert_fusion.1
  39.7 0.9 %collective-permute-start.10 = (bf16[64,1792]{1,0:T(8,128)(2,1)S(1)}, bf16[64,1792]{1,0:T(8,128)(2,1)S(1)}, u32[]{:S(2)}, u32[]{:S(2)}) collective-permute-start(bf16[64,1792]{1,0:T(8,128)(2,1)S(1)} %convolution_convert_fusion.1), channel_id=1, source_target_pairs={{0,1},{1,0},{2,3},{3,2},{4,5},{5,4},{6,7},{7,6},{8,9},{9,8},{10,11... | collective-permute-start | bytes 688136 | tf_op jit(solution)/shard_map/ppermute | solution.py:11
  40.5 0.5 collective-permute-done.18
  41.0 3.8 %collective-permute-done.19 = bf16[16,896]{1,0:T(8,128)(2,1)S(1)} collective-permute-done((bf16[16,896]{1,0:T(8,128)(2,1)S(1)}, bf16[16,896]{1,0:T(8,128)(2,1)S(1)}, u32[]{:S(2)}, u32[]{:S(2)}) %collective-permute-start.19) | collective-permute-done | bytes 28704 | tf_op jit(solution)/shard_map/ppermute | solution.py:11
  44.8 0.8 constant_dynamic-update-slice_fusion.17
  45.6 0.1 collective-permute-start.26
  45.7 0.9 %collective-permute-start.27 = (bf16[16,896]{1,0:T(8,128)(2,1)S(1)}, bf16[16,896]{1,0:T(8,128)(2,1)S(1)}, u32[]{:S(2)}, u32[]{:S(2)}) collective-permute-start(bf16[16,896]{1,0:T(8,128)(2,1)S(1)} %get-tuple-element.10), channel_id=1, source_target_pairs={{0,4},{1,5},{2,6},{3,7},{4,0},{5,1},{6,2},{7,3},{8,12},{9,13},{10,... | collective-permute-start | bytes 86024 | tf_op jit(solution)/shard_map/ppermute | solution.py:11
  46.5 3.5 %collective-permute-start.28 = (bf16[16,896]{1,0:T(8,128)(2,1)S(1)}, bf16[16,896]{1,0:T(8,128)(2,1)S(1)}, u32[]{:S(2)}, u32[]{:S(2)}) collective-permute-start(bf16[16,896]{1,0:T(8,128)(2,1)S(1)} %get-tuple-element.10), channel_id=1, source_target_pairs={{0,6},{1,7},{2,4},{3,5},{4,2},{5,3},{6,0},{7,1},{8,14},{9,15},{10,... | collective-permute-start | bytes 86024 | tf_op jit(solution)/shard_map/ppermute | solution.py:11
  50.1 1.1 %collective-permute-start.20 = (bf16[16,896]{1,0:T(8,128)(2,1)S(1)}, bf16[16,896]{1,0:T(8,128)(2,1)S(1)}, u32[]{:S(2)}, u32[]{:S(2)}) collective-permute-start(bf16[16,896]{1,0:T(8,128)(2,1)S(1)} %get-tuple-element.10), channel_id=1, source_target_pairs={{0,16},{8,24},{16,0},{24,8},{1,17},{9,25},{17,1},{25,9},{2,18},{10... | collective-permute-start | bytes 86024 | tf_op jit(solution)/shard_map/ppermute | solution.py:11
  51.2 0.3 fusion.59
  51.5 0.1 collective-permute-start.11
  51.6 0.9 %collective-permute-start.12 = (bf16[16,1792]{1,0:T(8,128)(2,1)S(1)}, bf16[16,1792]{1,0:T(8,128)(2,1)S(1)}, u32[]{:S(2)}, u32[]{:S(2)}) collective-permute-start(bf16[16,1792]{1,0:T(8,128)(2,1)S(1)} %get-tuple-element.19), channel_id=1, source_target_pairs={{0,4},{1,5},{2,6},{3,7},{4,0},{5,1},{6,2},{7,3},{8,12},{9,13},{10,... | collective-permute-start | bytes 172040 | tf_op jit(solution)/shard_map/ppermute | solution.py:11
  52.4 3.5 %collective-permute-start.13 = (bf16[16,1792]{1,0:T(8,128)(2,1)S(1)}, bf16[16,1792]{1,0:T(8,128)(2,1)S(1)}, u32[]{:S(2)}, u32[]{:S(2)}) collective-permute-start(bf16[16,1792]{1,0:T(8,128)(2,1)S(1)} %get-tuple-element.18), channel_id=1, source_target_pairs={{0,6},{1,7},{2,4},{3,5},{4,2},{5,3},{6,0},{7,1},{8,14},{9,15},{10,... | collective-permute-start | bytes 172040 | tf_op jit(solution)/shard_map/ppermute | solution.py:11
  56.0 0.8 %collective-permute-start.29 = (bf16[64,896]{1,0:T(8,128)(2,1)S(1)}, bf16[64,896]{1,0:T(8,128)(2,1)S(1)}, u32[]{:S(2)}, u32[]{:S(2)}) collective-permute-start(bf16[64,896]{1,0:T(8,128)(2,1)S(1)} %pad_maximum_fusion.1), channel_id=1, source_target_pairs={{0,1},{1,0},{2,3},{3,2},{4,5},{5,4},{6,7},{7,6},{8,9},{9,8},{10,11... | collective-permute-start | bytes 344072 | tf_op jit(solution)/shard_map/ppermute | solution.py:11
  56.8 2.8 %collective-permute-done.13 = bf16[16,1792]{1,0:T(8,128)(2,1)S(1)} collective-permute-done((bf16[16,1792]{1,0:T(8,128)(2,1)S(1)}, bf16[16,1792]{1,0:T(8,128)(2,1)S(1)}, u32[]{:S(2)}, u32[]{:S(2)}) %collective-permute-start.13) | collective-permute-done | bytes 57376 | tf_op jit(solution)/shard_map/ppermute | solution.py:11
  59.6 0.9 %constant_dynamic-update-slice_fusion.12 = (bf16[128,1792]{1,0:T(8,128)(2,1)S(1)}, bf16[16,1792]{1,0:T(8,128)(2,1)S(1)}) fusion(bf16[3,16,3584]{2,1,0:T(8,128)(2,1)} %param.7, s32[]{:T(128)S(6)} %select_n.134, s32[]{:T(128)S(6)} %select_n.126, bf16[16,1792]{1,0:T(8,128)(2,1)S(1)} %collective-permute-done.13, ...), kind=kLoop, calls=%fused_computation.69 | loop fusion | flops 258047 | bytes 458760
  60.5 0.1 collective-permute-start.22
  60.6 3.2 %collective-permute-start.23 = (bf16[16,1792]{1,0:T(8,128)(2,1)S(1)}, bf16[16,1792]{1,0:T(8,128)(2,1)S(1)}, u32[]{:S(2)}, u32[]{:S(2)}) collective-permute-start(bf16[16,1792]{1,0:T(8,128)(2,1)S(1)} %get-tuple-element.8), channel_id=1, source_target_pairs={{0,4},{1,5},{2,6},{3,7},{4,0},{5,1},{6,2},{7,3},{8,12},{9,13},{10,... | collective-permute-start | bytes 172040 | tf_op jit(solution)/shard_map/ppermute | solution.py:11
  63.7 1.2 %collective-permute-start.24 = (bf16[16,1792]{1,0:T(8,128)(2,1)S(1)}, bf16[16,1792]{1,0:T(8,128)(2,1)S(1)}, u32[]{:S(2)}, u32[]{:S(2)}) collective-permute-start(bf16[16,1792]{1,0:T(8,128)(2,1)S(1)} %get-tuple-element.8), channel_id=1, source_target_pairs={{0,6},{1,7},{2,4},{3,5},{4,2},{5,3},{6,0},{7,1},{8,14},{9,15},{10,... | collective-permute-start | bytes 172040 | tf_op jit(solution)/shard_map/ppermute | solution.py:11
  64.9 0.9 %collective-permute-done.23 = bf16[16,1792]{1,0:T(8,128)(2,1)S(1)} collective-permute-done((bf16[16,1792]{1,0:T(8,128)(2,1)S(1)}, bf16[16,1792]{1,0:T(8,128)(2,1)S(1)}, u32[]{:S(2)}, u32[]{:S(2)}) %collective-permute-start.23) | collective-permute-done | bytes 57376 | tf_op jit(solution)/shard_map/ppermute | solution.py:11
  65.9 3.8 %collective-permute-done.24 = bf16[16,1792]{1,0:T(8,128)(2,1)S(1)} collective-permute-done((bf16[16,1792]{1,0:T(8,128)(2,1)S(1)}, bf16[16,1792]{1,0:T(8,128)(2,1)S(1)}, u32[]{:S(2)}, u32[]{:S(2)}) %collective-permute-start.24) | collective-permute-done | bytes 57376 | tf_op jit(solution)/shard_map/ppermute | solution.py:11
  69.7 0.7 collective-permute-start.25
  70.5 0.3 convolution_convert_fusion.2
  70.8 1.0 %collective-permute-start.31 = (bf16[128,128]{1,0:T(8,128)(2,1)S(1)}, bf16[128,128]{1,0:T(8,128)(2,1)S(1)}, u32[]{:S(2)}, u32[]{:S(2)}) collective-permute-start(bf16[128,128]{1,0:T(8,128)(2,1)S(1)} %get-tuple-element.23), channel_id=1, source_target_pairs={{0,16},{8,24},{16,0},{24,8},{1,17},{9,25},{17,1},{25,9},{2,18},{10... | collective-permute-start | bytes 98312 | tf_op jit(solution)/shard_map/ppermute | solution.py:11
  71.8 0.4 fusion.17
  72.2 3.6 %collective-permute-done.25 = bf16[64,1792]{1,0:T(8,128)(2,1)S(1)} collective-permute-done((bf16[64,1792]{1,0:T(8,128)(2,1)S(1)}, bf16[64,1792]{1,0:T(8,128)(2,1)S(1)}, u32[]{:S(2)}, u32[]{:S(2)}) %collective-permute-start.25) | collective-permute-done | bytes 229408 | tf_op jit(solution)/shard_map/ppermute | solution.py:11
  75.8 0.5 convolution_add_fusion.2
  76.3 0.1 collective-permute-start.30
  76.4 0.6 fusion.34
  77.0 0.6 collective-permute-done.30
  77.6 0.5 fusion.54
  78.2 1.4 %fusion = bf16[1,3584,128]{2,1,0:T(8,128)(2,1)} fusion(bf16[128,1792]{1,0:T(8,128)(2,1)S(1)} %get-tuple-element.16, bf16[128,1792]{1,0:T(8,128)(2,1)S(1)} %get-tuple-element.15, bf16[128,128]{1,0:T(8,128)(2,1)S(1)} %get-tuple-element.6), kind=kOutput, calls=%fused_computation.1 | convolution fusion | flops 119734272 | bytes 1867776 | tf_op jit(solution)/shard_map/dot_general | solution.py:46
  (55 shorter events, 0.4 us)
Async XLA Ops:
  0.6 11.5 %copy-start = (bf16[1,2,2,128,1792]{4,3,2,1,0:T(8,128)(2,1)S(1)}, bf16[1,2,2,128,1792]{4,3,2,1,0:T(8,128)(2,1)}, u32[]{:S(2)}) copy-start(bf16[1,2,2,128,1792]{4,3,2,1,0:T(8,128)(2,1)} %param.10) | copy-start | bytes 5505028
  0.6 14.4 %copy-start.2 = (f32[1,128]{1,0:T(1,128)S(1)}, f32[1,128]{1,0:T(1,128)}, u32[]{:S(2)}) copy-start(f32[1,128]{1,0:T(1,128)} %param.9) | copy-start | bytes 1540
  0.7 22.5 %copy-start.1 = (bf16[1,3584,128]{2,1,0:T(8,128)(2,1)S(1)}, bf16[1,3584,128]{2,1,0:T(8,128)(2,1)}, u32[]{:S(2)}) copy-start(bf16[1,3584,128]{2,1,0:T(8,128)(2,1)} %param.8) | copy-start | bytes 2752516
  1.7 13.4 %collective-permute-start = (bf16[16,1792]{1,0:T(8,128)(2,1)S(1)}, bf16[16,1792]{1,0:T(8,128)(2,1)S(1)}, u32[]{:S(2)}, u32[]{:S(2)}) collective-permute-start(bf16[16,1792]{1,0:T(8,128)(2,1)S(1)} %get-tuple-element.12), channel_id=1, source_target_pairs={{0,2},{1,3},{2,0},{3,1},{4,6},{5,7},{6,4},{7,5},{8,10},{9,11},{10,... | collective-permute-start | bytes 172040 | tf_op jit(solution)/shard_map/ppermute | solution.py:11
  4.7 12.0 %collective-permute-start.1 = (bf16[16,1792]{1,0:T(8,128)(2,1)S(1)}, bf16[16,1792]{1,0:T(8,128)(2,1)S(1)}, u32[]{:S(2)}, u32[]{:S(2)}) collective-permute-start(bf16[16,1792]{1,0:T(8,128)(2,1)S(1)} %get-tuple-element.12), channel_id=1, source_target_pairs={{0,4},{1,5},{2,6},{3,7},{4,0},{5,1},{6,2},{7,3},{8,12},{9,13},{10,... | collective-permute-start | bytes 172040 | tf_op jit(solution)/shard_map/ppermute | solution.py:11
  7.3 10.0 %collective-permute-start.2 = (bf16[16,1792]{1,0:T(8,128)(2,1)S(1)}, bf16[16,1792]{1,0:T(8,128)(2,1)S(1)}, u32[]{:S(2)}, u32[]{:S(2)}) collective-permute-start(bf16[16,1792]{1,0:T(8,128)(2,1)S(1)} %get-tuple-element.12), channel_id=1, source_target_pairs={{0,6},{1,7},{2,4},{3,5},{4,2},{5,3},{6,0},{7,1},{8,14},{9,15},{10,... | collective-permute-start | bytes 172040 | tf_op jit(solution)/shard_map/ppermute | solution.py:11
  7.3 11.6 %collective-permute-start.3 = (bf16[16,1792]{1,0:T(8,128)(2,1)S(1)}, bf16[16,1792]{1,0:T(8,128)(2,1)S(1)}, u32[]{:S(2)}, u32[]{:S(2)}) collective-permute-start(bf16[16,1792]{1,0:T(8,128)(2,1)S(1)} %get-tuple-element.12), channel_id=1, source_target_pairs={{0,1},{1,0},{2,3},{3,2},{4,5},{5,4},{6,7},{7,6},{8,9},{9,8},{10,11... | collective-permute-start | bytes 172040 | tf_op jit(solution)/shard_map/ppermute | solution.py:11
  9.0 5.5 %collective-permute-start.9 = (f32[128]{0:T(128)}, f32[128]{0:T(128)S(1)}, u32[]{:S(2)}, u32[]{:S(2)}) collective-permute-start(f32[128]{0:T(128)} %bitcast.61), channel_id=1, source_target_pairs={{0,8},{8,0},{16,24},{24,16},{1,9},{9,1},{17,25},{25,17},{2,10},{10... | collective-permute-start | bytes 1544 | tf_op jit(solution)/shard_map/ppermute | solution.py:11
  14.5 8.6 %collective-permute-start.7 = (bf16[1792,128]{1,0:T(8,128)(2,1)}, bf16[1792,128]{1,0:T(8,128)(2,1)S(1)}, u32[]{:S(2)}, u32[]{:S(2)}) collective-permute-start(bf16[1792,128]{1,0:T(8,128)(2,1)} %dynamic-slice_bitcast_fusion.1), channel_id=1, source_target_pairs={{0,8},{8,0},{16,24},{24,16},{1,9},{9,1},{17,25},{25,17},{2,10},{10... | collective-permute-start | bytes 1376264 | tf_op jit(solution)/shard_map/ppermute | solution.py:11
  15.1 12.7 %collective-permute-start.15 = (bf16[256,896]{1,0:T(8,128)(2,1)}, bf16[256,896]{1,0:T(8,128)(2,1)S(1)}, u32[]{:S(2)}, u32[]{:S(2)}) collective-permute-start(bf16[256,896]{1,0:T(8,128)(2,1)} %dynamic-slice_bitcast_fusion), channel_id=1, source_target_pairs={{0,16},{8,24},{16,0},{24,8},{1,17},{9,25},{17,1},{25,9},{2,18},{10... | collective-permute-start | bytes 1376264 | tf_op jit(solution)/shard_map/ppermute | solution.py:11
  16.7 4.6 %collective-permute-start.4 = (bf16[16,1792]{1,0:T(8,128)(2,1)S(1)}, bf16[16,1792]{1,0:T(8,128)(2,1)S(1)}, u32[]{:S(2)}, u32[]{:S(2)}) collective-permute-start(bf16[16,1792]{1,0:T(8,128)(2,1)S(1)} %collective-permute-done), channel_id=1, source_target_pairs={{0,1},{1,0},{2,3},{3,2},{4,5},{5,4},{6,7},{7,6},{8,9},{9,8},{10,11... | collective-permute-start | bytes 172040 | tf_op jit(solution)/shard_map/ppermute | solution.py:11
  17.3 4.9 %collective-permute-start.5 = (bf16[16,1792]{1,0:T(8,128)(2,1)S(1)}, bf16[16,1792]{1,0:T(8,128)(2,1)S(1)}, u32[]{:S(2)}, u32[]{:S(2)}) collective-permute-start(bf16[16,1792]{1,0:T(8,128)(2,1)S(1)} %collective-permute-done.1), channel_id=1, source_target_pairs={{0,1},{1,0},{2,3},{3,2},{4,5},{5,4},{6,7},{7,6},{8,9},{9,8},{10,11... | collective-permute-start | bytes 172040 | tf_op jit(solution)/shard_map/ppermute | solution.py:11
  18.9 4.2 %collective-permute-start.6 = (bf16[16,1792]{1,0:T(8,128)(2,1)S(1)}, bf16[16,1792]{1,0:T(8,128)(2,1)S(1)}, u32[]{:S(2)}, u32[]{:S(2)}) collective-permute-start(bf16[16,1792]{1,0:T(8,128)(2,1)S(1)} %collective-permute-done.2), channel_id=1, source_target_pairs={{0,1},{1,0},{2,3},{3,2},{4,5},{5,4},{6,7},{7,6},{8,9},{9,8},{10,11... | collective-permute-start | bytes 172040 | tf_op jit(solution)/shard_map/ppermute | solution.py:11
  23.1 1.8 %collective-permute-start.21 = (bf16[128,1792]{1,0:T(8,128)(2,1)S(1)}, bf16[128,1792]{1,0:T(8,128)(2,1)S(1)}, u32[]{:S(2)}, u32[]{:S(2)}) collective-permute-start(bf16[128,1792]{1,0:T(8,128)(2,1)S(1)} %constant_dynamic-update-slice_fusion), channel_id=1, source_target_pairs={{0,8},{8,0},{16,24},{24,16},{1,9},{9,1},{17,25},{25,17},{2,10},{10... | collective-permute-start | bytes 1376264 | tf_op jit(solution)/shard_map/ppermute | solution.py:11
  23.6 1.5 %collective-permute-start.8 = (f32[128,256]{1,0:T(8,128)S(1)}, f32[128,256]{1,0:T(8,128)S(1)}, u32[]{:S(2)}, u32[]{:S(2)}) collective-permute-start(f32[128,256]{1,0:T(8,128)S(1)} %fusion.3), channel_id=1, source_target_pairs={{0,8},{8,0},{16,24},{24,16},{1,9},{9,1},{17,25},{25,17},{2,10},{10... | collective-permute-start | bytes 393224 | tf_op jit(solution)/shard_map/ppermute | solution.py:11
  25.2 4.4 %collective-permute-start.14 = (bf16[128,256]{1,0:T(8,128)(2,1)S(1)}, bf16[128,256]{1,0:T(8,128)(2,1)S(1)}, u32[]{:S(2)}, u32[]{:S(2)}) collective-permute-start(bf16[128,256]{1,0:T(8,128)(2,1)S(1)} %multiply_convert_fusion), channel_id=1, source_target_pairs={{0,16},{8,24},{16,0},{24,8},{1,17},{9,25},{17,1},{25,9},{2,18},{10... | collective-permute-start | bytes 196616 | tf_op jit(solution)/shard_map/ppermute | solution.py:11
  29.8 4.9 %collective-permute-start.16 = (bf16[64,896]{1,0:T(8,128)(2,1)S(1)}, bf16[64,896]{1,0:T(8,128)(2,1)S(1)}, u32[]{:S(2)}, u32[]{:S(2)}) collective-permute-start(bf16[64,896]{1,0:T(8,128)(2,1)S(1)} %fusion.2), channel_id=1, source_target_pairs={{0,1},{1,0},{2,3},{3,2},{4,5},{5,4},{6,7},{7,6},{8,9},{9,8},{10,11... | collective-permute-start | bytes 344072 | tf_op jit(solution)/shard_map/ppermute | solution.py:11
  34.9 5.6 %collective-permute-start.17 = (bf16[16,896]{1,0:T(8,128)(2,1)S(1)}, bf16[16,896]{1,0:T(8,128)(2,1)S(1)}, u32[]{:S(2)}, u32[]{:S(2)}) collective-permute-start(bf16[16,896]{1,0:T(8,128)(2,1)S(1)} %get-tuple-element.20), channel_id=1, source_target_pairs={{0,2},{1,3},{2,0},{3,1},{4,6},{5,7},{6,4},{7,5},{8,10},{9,11},{10,... | collective-permute-start | bytes 86024 | tf_op jit(solution)/shard_map/ppermute | solution.py:11
  35.7 5.3 %collective-permute-start.18 = (bf16[16,896]{1,0:T(8,128)(2,1)S(1)}, bf16[16,896]{1,0:T(8,128)(2,1)S(1)}, u32[]{:S(2)}, u32[]{:S(2)}) collective-permute-start(bf16[16,896]{1,0:T(8,128)(2,1)S(1)} %get-tuple-element.22), channel_id=1, source_target_pairs={{0,4},{1,5},{2,6},{3,7},{4,0},{5,1},{6,2},{7,3},{8,12},{9,13},{10,... | collective-permute-start | bytes 86024 | tf_op jit(solution)/shard_map/ppermute | solution.py:11
  39.2 5.7 %collective-permute-start.19 = (bf16[16,896]{1,0:T(8,128)(2,1)S(1)}, bf16[16,896]{1,0:T(8,128)(2,1)S(1)}, u32[]{:S(2)}, u32[]{:S(2)}) collective-permute-start(bf16[16,896]{1,0:T(8,128)(2,1)S(1)} %get-tuple-element.21), channel_id=1, source_target_pairs={{0,6},{1,7},{2,4},{3,5},{4,2},{5,3},{6,0},{7,1},{8,14},{9,15},{10,... | collective-permute-start | bytes 86024 | tf_op jit(solution)/shard_map/ppermute | solution.py:11
  39.7 11.5 %collective-permute-start.10 = (bf16[64,1792]{1,0:T(8,128)(2,1)S(1)}, bf16[64,1792]{1,0:T(8,128)(2,1)S(1)}, u32[]{:S(2)}, u32[]{:S(2)}) collective-permute-start(bf16[64,1792]{1,0:T(8,128)(2,1)S(1)} %convolution_convert_fusion.1), channel_id=1, source_target_pairs={{0,1},{1,0},{2,3},{3,2},{4,5},{5,4},{6,7},{7,6},{8,9},{9,8},{10,11... | collective-permute-start | bytes 688136 | tf_op jit(solution)/shard_map/ppermute | solution.py:11
  45.6 6.0 %collective-permute-start.26 = (bf16[16,896]{1,0:T(8,128)(2,1)S(1)}, bf16[16,896]{1,0:T(8,128)(2,1)S(1)}, u32[]{:S(2)}, u32[]{:S(2)}) collective-permute-start(bf16[16,896]{1,0:T(8,128)(2,1)S(1)} %get-tuple-element.10), channel_id=1, source_target_pairs={{0,2},{1,3},{2,0},{3,1},{4,6},{5,7},{6,4},{7,5},{8,10},{9,11},{10,... | collective-permute-start | bytes 86024 | tf_op jit(solution)/shard_map/ppermute | solution.py:11
  45.7 6.8 %collective-permute-start.27 = (bf16[16,896]{1,0:T(8,128)(2,1)S(1)}, bf16[16,896]{1,0:T(8,128)(2,1)S(1)}, u32[]{:S(2)}, u32[]{:S(2)}) collective-permute-start(bf16[16,896]{1,0:T(8,128)(2,1)S(1)} %get-tuple-element.10), channel_id=1, source_target_pairs={{0,4},{1,5},{2,6},{3,7},{4,0},{5,1},{6,2},{7,3},{8,12},{9,13},{10,... | collective-permute-start | bytes 86024 | tf_op jit(solution)/shard_map/ppermute | solution.py:11
  46.5 9.4 %collective-permute-start.28 = (bf16[16,896]{1,0:T(8,128)(2,1)S(1)}, bf16[16,896]{1,0:T(8,128)(2,1)S(1)}, u32[]{:S(2)}, u32[]{:S(2)}) collective-permute-start(bf16[16,896]{1,0:T(8,128)(2,1)S(1)} %get-tuple-element.10), channel_id=1, source_target_pairs={{0,6},{1,7},{2,4},{3,5},{4,2},{5,3},{6,0},{7,1},{8,14},{9,15},{10,... | collective-permute-start | bytes 86024 | tf_op jit(solution)/shard_map/ppermute | solution.py:11
  50.1 26.3 %collective-permute-start.20 = (bf16[16,896]{1,0:T(8,128)(2,1)S(1)}, bf16[16,896]{1,0:T(8,128)(2,1)S(1)}, u32[]{:S(2)}, u32[]{:S(2)}) collective-permute-start(bf16[16,896]{1,0:T(8,128)(2,1)S(1)} %get-tuple-element.10), channel_id=1, source_target_pairs={{0,16},{8,24},{16,0},{24,8},{1,17},{9,25},{17,1},{25,9},{2,18},{10... | collective-permute-start | bytes 86024 | tf_op jit(solution)/shard_map/ppermute | solution.py:11
  51.5 5.3 %collective-permute-start.11 = (bf16[16,1792]{1,0:T(8,128)(2,1)S(1)}, bf16[16,1792]{1,0:T(8,128)(2,1)S(1)}, u32[]{:S(2)}, u32[]{:S(2)}) collective-permute-start(bf16[16,1792]{1,0:T(8,128)(2,1)S(1)} %get-tuple-element.17), channel_id=1, source_target_pairs={{0,2},{1,3},{2,0},{3,1},{4,6},{5,7},{6,4},{7,5},{8,10},{9,11},{10,... | collective-permute-start | bytes 172040 | tf_op jit(solution)/shard_map/ppermute | solution.py:11
  51.6 5.2 %collective-permute-start.12 = (bf16[16,1792]{1,0:T(8,128)(2,1)S(1)}, bf16[16,1792]{1,0:T(8,128)(2,1)S(1)}, u32[]{:S(2)}, u32[]{:S(2)}) collective-permute-start(bf16[16,1792]{1,0:T(8,128)(2,1)S(1)} %get-tuple-element.19), channel_id=1, source_target_pairs={{0,4},{1,5},{2,6},{3,7},{4,0},{5,1},{6,2},{7,3},{8,12},{9,13},{10,... | collective-permute-start | bytes 172040 | tf_op jit(solution)/shard_map/ppermute | solution.py:11
  52.4 7.2 %collective-permute-start.13 = (bf16[16,1792]{1,0:T(8,128)(2,1)S(1)}, bf16[16,1792]{1,0:T(8,128)(2,1)S(1)}, u32[]{:S(2)}, u32[]{:S(2)}) collective-permute-start(bf16[16,1792]{1,0:T(8,128)(2,1)S(1)} %get-tuple-element.18), channel_id=1, source_target_pairs={{0,6},{1,7},{2,4},{3,5},{4,2},{5,3},{6,0},{7,1},{8,14},{9,15},{10,... | collective-permute-start | bytes 172040 | tf_op jit(solution)/shard_map/ppermute | solution.py:11
  56.0 14.5 %collective-permute-start.29 = (bf16[64,896]{1,0:T(8,128)(2,1)S(1)}, bf16[64,896]{1,0:T(8,128)(2,1)S(1)}, u32[]{:S(2)}, u32[]{:S(2)}) collective-permute-start(bf16[64,896]{1,0:T(8,128)(2,1)S(1)} %pad_maximum_fusion.1), channel_id=1, source_target_pairs={{0,1},{1,0},{2,3},{3,2},{4,5},{5,4},{6,7},{7,6},{8,9},{9,8},{10,11... | collective-permute-start | bytes 344072 | tf_op jit(solution)/shard_map/ppermute | solution.py:11
  60.5 4.5 %collective-permute-start.22 = (bf16[16,1792]{1,0:T(8,128)(2,1)S(1)}, bf16[16,1792]{1,0:T(8,128)(2,1)S(1)}, u32[]{:S(2)}, u32[]{:S(2)}) collective-permute-start(bf16[16,1792]{1,0:T(8,128)(2,1)S(1)} %get-tuple-element.8), channel_id=1, source_target_pairs={{0,2},{1,3},{2,0},{3,1},{4,6},{5,7},{6,4},{7,5},{8,10},{9,11},{10,... | collective-permute-start | bytes 172040 | tf_op jit(solution)/shard_map/ppermute | solution.py:11
  60.6 5.3 %collective-permute-start.23 = (bf16[16,1792]{1,0:T(8,128)(2,1)S(1)}, bf16[16,1792]{1,0:T(8,128)(2,1)S(1)}, u32[]{:S(2)}, u32[]{:S(2)}) collective-permute-start(bf16[16,1792]{1,0:T(8,128)(2,1)S(1)} %get-tuple-element.8), channel_id=1, source_target_pairs={{0,4},{1,5},{2,6},{3,7},{4,0},{5,1},{6,2},{7,3},{8,12},{9,13},{10,... | collective-permute-start | bytes 172040 | tf_op jit(solution)/shard_map/ppermute | solution.py:11
  63.7 6.0 %collective-permute-start.24 = (bf16[16,1792]{1,0:T(8,128)(2,1)S(1)}, bf16[16,1792]{1,0:T(8,128)(2,1)S(1)}, u32[]{:S(2)}, u32[]{:S(2)}) collective-permute-start(bf16[16,1792]{1,0:T(8,128)(2,1)S(1)} %get-tuple-element.8), channel_id=1, source_target_pairs={{0,6},{1,7},{2,4},{3,5},{4,2},{5,3},{6,0},{7,1},{8,14},{9,15},{10,... | collective-permute-start | bytes 172040 | tf_op jit(solution)/shard_map/ppermute | solution.py:11
  69.7 6.1 %collective-permute-start.25 = (bf16[64,1792]{1,0:T(8,128)(2,1)S(1)}, bf16[64,1792]{1,0:T(8,128)(2,1)S(1)}, u32[]{:S(2)}, u32[]{:S(2)}) collective-permute-start(bf16[64,1792]{1,0:T(8,128)(2,1)S(1)} %pad_maximum_fusion), channel_id=1, source_target_pairs={{0,1},{1,0},{2,3},{3,2},{4,5},{5,4},{6,7},{7,6},{8,9},{9,8},{10,11... | collective-permute-start | bytes 688136 | tf_op jit(solution)/shard_map/ppermute | solution.py:11
  70.8 6.2 %collective-permute-start.31 = (bf16[128,128]{1,0:T(8,128)(2,1)S(1)}, bf16[128,128]{1,0:T(8,128)(2,1)S(1)}, u32[]{:S(2)}, u32[]{:S(2)}) collective-permute-start(bf16[128,128]{1,0:T(8,128)(2,1)S(1)} %get-tuple-element.23), channel_id=1, source_target_pairs={{0,16},{8,24},{16,0},{24,8},{1,17},{9,25},{17,1},{25,9},{2,18},{10... | collective-permute-start | bytes 98312 | tf_op jit(solution)/shard_map/ppermute | solution.py:11
  71.8 5.2 %collective-permute-start.32 = (bf16[128,128]{1,0:T(8,128)(2,1)S(1)}, bf16[128,128]{1,0:T(8,128)(2,1)S(1)}, u32[]{:S(2)}, u32[]{:S(2)}) collective-permute-start(bf16[128,128]{1,0:T(8,128)(2,1)S(1)} %get-tuple-element.24), channel_id=1, source_target_pairs={{0,24},{8,16},{16,8},{24,0},{1,25},{9,17},{17,9},{25,1},{2,26},{10... | collective-permute-start | bytes 98312 | tf_op jit(solution)/shard_map/ppermute | solution.py:11
  76.3 1.3 %collective-permute-start.30 = (f32[128,128]{1,0:T(8,128)S(1)}, f32[128,128]{1,0:T(8,128)S(1)}, u32[]{:S(2)}, u32[]{:S(2)}) collective-permute-start(f32[128,128]{1,0:T(8,128)S(1)} %slice_select_fusion), channel_id=1, source_target_pairs={{0,8},{8,0},{16,24},{24,16},{1,9},{9,1},{17,25},{25,17},{2,10},{10... | collective-permute-start | bytes 196616 | tf_op jit(solution)/shard_map/ppermute | solution.py:11

commit v3 on v2

--- a/solution.py
+++ b/solution.py
@@ -35,10 +35,12 @@
     return out
 
 
-def paired_encoder(weight, bias, half, cols):
-    other = crossed(lax.dynamic_slice_in_dim(weight, (1 - half) * cols, cols, 0), "layer", 1)
+def half_preacts(resid_half, weight, weight_other, bias, half):
+    cols = resid_half.shape[1]
     mine = lax.dynamic_slice_in_dim(weight, half * cols, cols, 0)
-    return both_halves(half, mine, other, 1), both_halves(half, bias, crossed(bias, "layer", 1), 0)
+    other = lax.dynamic_slice_in_dim(weight_other, half * cols, cols, 0)
+    nothing = jnp.zeros_like(bias)
+    return times(resid_half, both_halves(half, mine, other, 1)) + both_halves(half, bias, nothing, 0)
 
 
 def encoder_gradient(resid_half, resid_other, grad_low, half):
@@ -58,50 +60,67 @@
     near_rows = tokens // 2
     decoder = dec_weight[0].reshape(2, 2 * latents, cols)
 
+    weight = enc_weight[0]
     mine = lax.dynamic_slice(resid, (layer, 0, half * cols), (1, rows, cols))[0]
-    along = [mine] + [crossed(mine, "latent", 2 * k) for k in range(1, far)]
-    beside = [crossed(block, "latent", 1) for block in along]
-    resid_half = jnp.concatenate(along + beside, axis=0)
+    along = [mine] + [None] * (far - 1)
+    for k in range(far - 1, 0, -1):
+        along[k] = crossed(mine, "latent", 2 * k)
+    beside = [crossed(mine, "latent", 1)]
 
     shared = lax.dynamic_index_in_dim(decoder, 1 - layer, 0, keepdims=False)
-    dec_given = crossed(lax.dynamic_slice_in_dim(shared, (1 - layer) * part, part, 1), "layer", 2)
+    given = lax.dynamic_slice_in_dim(shared, (1 - layer) * part, part, 1)
+    dec_given = crossed(given, "layer", 2)
+    wanted = [
+        lax.dynamic_slice(target, (2 * layer, 0, half * cols + i * part), (1, rows, part))[0] for i in range(2)
+    ]
+    wanted.append(lax.dynamic_slice(target, (1, 0, half * cols + layer * part), (1, rows, part))[0])
+    decoder, blocks, weight, *along = lax.optimization_barrier((decoder, blocks, weight, *along))
+    weight_other = crossed(weight, "layer", 1)
+    beside += [crossed(block, "latent", 1) for block in along[1:]]
+    shared = lax.dynamic_index_in_dim(decoder, 1 - layer, 0, keepdims=False)
     dec_kept = lax.dynamic_slice_in_dim(shared, layer * part, part, 1)
     dec_own = lax.dynamic_index_in_dim(decoder, layer, 0, keepdims=False)
-    weight_pair, bias_pair = paired_encoder(enc_weight[0], enc_bias[0], half, cols)
     firing = gates(blocks, layer, slot, slots, latents, tokens)
     gate = jnp.where(half == 0, firing[0], firing[1])
+    resid_half = jnp.concatenate(along + beside, axis=0)
+    resid_half, dec_given, *wanted = lax.optimization_barrier((resid_half, dec_given, *wanted))
 
-    partial = times(resid_half, weight_pair)
-    preact = partial + crossed(partial, "layer", 1) + bias_pair
-    acts = (preact * jnp.concatenate(firing, axis=1)).astype(BF16)
+    partial = half_preacts(resid_half, weight, weight_other, enc_bias[0], half)
+    acts = ((partial + crossed(partial, "layer", 1)) * jnp.concatenate(firing, axis=1)).astype(BF16)
     acts_other = crossed(acts, "layer", 2)
     resid_other = crossed(resid_half, "layer", 1)
 
-    def scattered(product):
-        leaving = product(slice(near_rows, tokens)).astype(BF16)
-        near = product(slice(0, near_rows)) + crossed(leaving, "latent", 1).astype(F32)
-        total = near[:rows]
-        for k in range(1, far):
-            total = total + crossed(near[k * rows:(k + 1) * rows].astype(BF16), "latent", 2 * k).astype(F32)
-        return total
+    near, away = slice(0, near_rows), slice(near_rows, tokens)
+    parts = [slice(0, part), slice(part, cols)]
+    products = {at: [times(acts[at], dec_own[:, p]) for p in parts] for at in (near, away)}
+    crossing = [crossed(product.astype(BF16), "latent", 1) for product in products[away]]
+    for at in (away, near):
+        products[at].append(times(acts[at], dec_kept) + times(acts_other[at], dec_given))
+    crossing.append(crossed(products[away][2].astype(BF16), "latent", 1))
+    sums = []
+    for product, came in zip(products[near], crossing):
+        total = product + came.astype(F32)
+        pieces = [total[:rows]]
+        for k in range(far - 1, 0, -1):
+            pieces.append(crossed(total[k * rows:(k + 1) * rows].astype(BF16), "latent", 2 * k).astype(F32))
+        sums.append(sum(pieces))
+    errs = [(total - aim.astype(F32)).astype(BF16) for total, aim in zip(sums, wanted)]
+    everywhere = []
+    for err in errs:
+        along = [err] + [None] * (far - 1)
+        for k in range(far - 1, 0, -1):
+            along[k] = crossed(err, "latent", 2 * k)
+        block = jnp.concatenate(along, axis=0)
+        everywhere.append(jnp.concatenate([block, crossed(block, "latent", 1)], axis=0))
+    err_across = crossed(errs[2], "layer", 2)
+    errors = jnp.concatenate(
+        [jnp.where(layer == 0, errs[0], err_across), jnp.where(layer == 0, errs[1], errs[2])], axis=1
+    )
 
-    def gathered(block):
-        along = [block] + [crossed(block, "latent", 2 * k) for k in range(1, far)]
-        near = jnp.concatenate(along, axis=0)
-        return jnp.concatenate([near, crossed(near, "latent", 1)], axis=0)
-
-    sum_own = scattered(lambda at: times(acts[at], dec_own))
-    sum_shared = scattered(lambda at: times(acts[at], dec_kept) + times(acts_other[at], dec_given))
-    wanted_own = lax.dynamic_slice(target, (2 * layer, 0, half * cols), (1, rows, cols))[0]
-    wanted_shared = lax.dynamic_slice(target, (1, 0, half * cols + layer * part), (1, rows, part))[0]
-    err_own = (sum_own - wanted_own.astype(F32)).astype(BF16)
-    err_shared = (sum_shared - wanted_shared.astype(F32)).astype(BF16)
-    err_across = crossed(err_shared, "layer", 2)
-    errors = jnp.where(layer == 0, err_own, jnp.concatenate([err_across, err_shared], axis=1))
-
-    errs_own, errs_shared = gathered(err_own), gathered(err_shared)
-    back = times_transposed(errs_shared, dec_given).astype(BF16)
-    here = times_transposed(errs_own, dec_own) + times_transposed(errs_shared, dec_kept)
+    back = times_transposed(everywhere[2], dec_given).astype(BF16)
+    here = times_transposed(everywhere[0], dec_own[:, parts[0]])
+    here = here + times_transposed(everywhere[1], dec_own[:, parts[1]])
+    here = here + times_transposed(everywhere[2], dec_kept)
 
     def of_half(pair, which):
         return jnp.where(which == 0, pair[:, :latents], pair[:, latents:])
@@ -134,11 +153,11 @@
         return lax.ppermute(block, "layer", route)
 
     resid_half = to_all(lax.dynamic_slice(resid, (layer, 0, half * cols), (1, rows, cols))[0])
-    weight_pair, bias_pair = paired_encoder(enc_weight[0], enc_bias[0], half, cols)
     firing = gates(blocks, layer, slot, slots, latents, tokens)
     gate = jnp.where(half == 0, firing[0], firing[1])
-    partial = times(resid_half, weight_pair)
-    preact = partial + crossed(partial, "layer", 1) + bias_pair
+    weight_other = crossed(enc_weight[0], "layer", 1)
+    partial = half_preacts(resid_half, enc_weight[0], weight_other, enc_bias[0], half)
+    preact = partial + crossed(partial, "layer", 1)
     acts = (preact * jnp.concatenate(firing, axis=1)).astype(BF16)
     resid_other = crossed(resid_half, "layer", 1)
 

time: 79.8 us -> 91.2 us (1.14)
  starting transfers between devices: 36.7 us -> 48.6 us
  waiting for transfers between devices: 27.7 us -> 18.4 us
  local copies, waits for them, and re-layouts: 3.95 us -> 10.4 us
  matrix products: 4.42 us -> 5.85 us
    ppermute x33 -> x40, starting transfers between devices: 36.7 us -> 48.6 us  [crossed(): lax.ppermute(block, axis, [(i, i ^ mask) for i in range(lax.axis_size(axi...]
    ppermute x33 -> x40, waiting for transfers between devices: 27.7 us -> 18.4 us  [crossed(): lax.ppermute(block, axis, [(i, i ^ mask) for i in range(lax.axis_size(axi...]
    unnamed x19 -> x20, local copies, waits for them, and re-layouts: 1.08 us -> 6.95 us
    select_n x3, other arithmetic: 0.26 us -> 3.08 us  [both_halves(): jnp.where(half == 0, mine, other)]
    dynamic_slice x2 -> x1, local copies, waits for them, and re-layouts: 2.8 us -> 0.97 us  [two_layers(): given = lax.dynamic_slice_in_dim(shared, (1 - layer) * part, part, 1)]
    squeeze x0 -> x3, local copies, waits for them, and re-layouts: none -> 1.8 us  [the longest x1 0.95 us: two_layers(): mine = lax.dynamic_slice(resid, (layer, 0, half * cols), (1, rows, cols))[0]]
    unnamed x2 -> x3, other arithmetic: 1.63 us -> 0.07 us
    dot_general x7 -> x9, matrix products: 1.95 us -> 3.24 us  [times(): return jnp.dot(left, right, preferred_element_type=F32)]
  transfers between devices with their start and end apart: 33 -> 40, of which waited for: 15 -> 13; matrix products, arithmetic and copies ran while one was open for 12% -> 19% of each run, Pallas kernels for 0% -> 0%
where the time goes in v3:
time: 91.2 us; the launch traced here: 90.7 us
  starting transfers between devices  48.6 us (53%)
  waiting for transfers between devices  18.4 us (20%)
  local copies, waits for them, and re-layouts  10.4 us (11%)
  matrix products  5.85 us (6%)
  other arithmetic  5.07 us (6%)
  between operations  2.32 us (3%)
    ppermute x40, starting transfers between devices, crossed(): lax.ppermute(block, axis, [(i, i ^ mask) for i in range(lax.axis_size(axi...  48.6 us
    ppermute x40, waiting for transfers between devices, crossed(): lax.ppermute(block, axis, [(i, i ^ mask) for i in range(lax.axis_size(axi...  18.4 us
    unnamed x20, local copies, waits for them, and re-layouts  6.95 us
    dot_general x9, matrix products, times(): return jnp.dot(left, right, preferred_element_type=F32)  3.24 us
    select_n x3, other arithmetic, both_halves(): jnp.where(half == 0, mine, other)  3.08 us
  transfers between devices with their start and end apart: 40, of which 13 were waited for; matrix products, arithmetic and copies ran while one was open for 19% of the time, Pallas kernels for 0%

profile of v3, /device:TPU:0, one launch (start us, length us, event | category | flops | bytes accessed | tf_op | source)
XLA Modules:
  0.0 90.7 jit_solution(4430979286755566072)
XLA Ops:
  0.7 1.0 %dynamic-slice_bitcast_fusion.2 = bf16[16,1792]{1,0:T(8,128)(2,1)S(1)} fusion(bf16[2,16,3584]{2,1,0:T(8,128)(2,1)} %param.6, s32[]{:T(128)S(6)} %select_n.137, s32[]{:T(128)S(6)} %select_n.139), kind=kLoop, calls=%fused_computation.62 | loop fusion | bytes 114696 | tf_op jit(solution)/shard_map/squeeze | solution.py:64
  1.6 3.0 %collective-permute-start = (bf16[16,1792]{1,0:T(8,128)(2,1)S(1)}, bf16[16,1792]{1,0:T(8,128)(2,1)S(1)}, u32[]{:S(2)}, u32[]{:S(2)}) collective-permute-start(bf16[16,1792]{1,0:T(8,128)(2,1)S(1)} %dynamic-slice_bitcast_fusion.2), channel_id=1, source_target_pairs={{0,2},{1,3},{2,0},{3,1},{4,6},{5,7},{6,4},{7,5},{8,10},{9,11},{10,... | collective-permute-start | bytes 172040 | tf_op jit(solution)/shard_map/ppermute | solution.py:11
  4.7 2.6 %collective-permute-start.1 = (bf16[16,1792]{1,0:T(8,128)(2,1)S(1)}, bf16[16,1792]{1,0:T(8,128)(2,1)S(1)}, u32[]{:S(2)}, u32[]{:S(2)}) collective-permute-start(bf16[16,1792]{1,0:T(8,128)(2,1)S(1)} %dynamic-slice_bitcast_fusion.2), channel_id=1, source_target_pairs={{0,4},{1,5},{2,6},{3,7},{4,0},{5,1},{6,2},{7,3},{8,12},{9,13},{10,... | collective-permute-start | bytes 172040 | tf_op jit(solution)/shard_map/ppermute | solution.py:11
  7.3 1.7 %collective-permute-start.3 = (bf16[16,1792]{1,0:T(8,128)(2,1)S(1)}, bf16[16,1792]{1,0:T(8,128)(2,1)}, u32[]{:S(2)}, u32[]{:S(2)}) collective-permute-start(bf16[16,1792]{1,0:T(8,128)(2,1)S(1)} %dynamic-slice_bitcast_fusion.2), channel_id=1, source_target_pairs={{0,1},{1,0},{2,3},{3,2},{4,5},{5,4},{6,7},{7,6},{8,9},{9,8},{10,11... | collective-permute-start | bytes 172040 | tf_op jit(solution)/shard_map/ppermute | solution.py:11
  9.0 1.0 %dynamic-slice_bitcast_fusion.1 = bf16[256,896]{1,0:T(8,128)(2,1)} fusion(bf16[2,256,1792]{2,1,0:T(8,128)(2,1)S(1)} %bitcast.42, s32[]{:T(128)S(6)} %select_n.141, s32[]{:T(128)S(6)} %select_n.143), kind=kLoop, calls=%fused_computation.25 | loop fusion | bytes 917512 | tf_op jit(solution)/shard_map/dynamic_slice | solution.py:71
  9.9 1.5 %collective-permute-start.7 = (bf16[256,896]{1,0:T(8,128)(2,1)}, bf16[256,896]{1,0:T(8,128)(2,1)S(1)}, u32[]{:S(2)}, u32[]{:S(2)}) collective-permute-start(bf16[256,896]{1,0:T(8,128)(2,1)} %dynamic-slice_bitcast_fusion.1), channel_id=1, source_target_pairs={{0,16},{8,24},{16,0},{24,8},{1,17},{9,25},{17,1},{25,9},{2,18},{10... | collective-permute-start | bytes 1376264 | tf_op jit(solution)/shard_map/ppermute | solution.py:11
  11.5 0.7 fusion.50
  12.1 0.8 dynamic-slice_bitcast_fusion.3
  13.2 0.6 constant_dynamic-update-slice_fusion.7
  13.9 1.5 %collective-permute-start.4 = (bf16[16,1792]{1,0:T(8,128)(2,1)S(1)}, bf16[16,1792]{1,0:T(8,128)(2,1)}, u32[]{:S(2)}, u32[]{:S(2)}) collective-permute-start(bf16[16,1792]{1,0:T(8,128)(2,1)S(1)} %collective-permute-done), channel_id=1, source_target_pairs={{0,1},{1,0},{2,3},{3,2},{4,5},{5,4},{6,7},{7,6},{8,9},{9,8},{10,11... | collective-permute-start | bytes 172040 | tf_op jit(solution)/shard_map/ppermute | solution.py:11
  15.4 0.6 constant_dynamic-update-slice_fusion.6
  16.0 0.5 collective-permute-start.5
  16.5 0.6 constant_dynamic-update-slice_fusion.5
  17.2 0.6 constant_dynamic-update-slice_fusion.4
  17.8 1.5 %collective-permute-start.6 = (bf16[16,1792]{1,0:T(8,128)(2,1)S(1)}, bf16[16,1792]{1,0:T(8,128)(2,1)S(1)}, u32[]{:S(2)}, u32[]{:S(2)}) collective-permute-start(bf16[16,1792]{1,0:T(8,128)(2,1)S(1)} %collective-permute-done.2), channel_id=1, source_target_pairs={{0,1},{1,0},{2,3},{3,2},{4,5},{5,4},{6,7},{7,6},{8,9},{9,8},{10,11... | collective-permute-start | bytes 172040 | tf_op jit(solution)/shard_map/ppermute | solution.py:11
  19.3 1.4 %constant_dynamic-update-slice_fusion.3 = bf16[128,1792]{1,0:T(8,128)(2,1)} fusion(bf16[128,1792]{1,0:T(8,128)(2,1)} %constant_dynamic-update-slice_fusion.4, bf16[16,1792]{1,0:T(8,128)(2,1)} %collective-permute-done.3), kind=kLoop, calls=%fused_computation.66 | loop fusion | bytes 114688
  20.8 0.6 compare_reduce_fusion
  22.8 1.4 %constant_dynamic-update-slice_fusion.2 = bf16[128,1792]{1,0:T(8,128)(2,1)} fusion(bf16[128,1792]{1,0:T(8,128)(2,1)} %constant_dynamic-update-slice_fusion.3, bf16[16,1792]{1,0:T(8,128)(2,1)} %collective-permute-done.4), kind=kLoop, calls=%fused_computation.65 | loop fusion | bytes 114688
  24.2 1.4 %constant_dynamic-update-slice_fusion.1 = bf16[128,1792]{1,0:T(8,128)(2,1)} fusion(bf16[128,1792]{1,0:T(8,128)(2,1)} %constant_dynamic-update-slice_fusion.2, bf16[16,1792]{1,0:T(8,128)(2,1)} %collective-permute-done.5), kind=kLoop, calls=%fused_computation.64 | loop fusion | bytes 114688
  25.7 0.6 constant_dynamic-update-slice_fusion
  26.5 1.3 %broadcast_select_fusion.3 = (bf16[1792,128]{1,0:T(8,128)(2,1)S(1)}, bf16[1792,128]{1,0:T(8,128)(2,1)S(1)}) fusion(pred[]{:T(512)S(6)} %eq.56, bf16[3584,128]{1,0:T(8,128)(2,1)} %collective-permute-done.8, s32[]{:T(128)S(6)} %select_n.139, bf16[3584,128]{1,0:T(8,128)(2,1)} %bitcast.47), kind=kLoop, calls=%fused_computation.29 | loop fusion | flops 458752 | bytes 1835013 | tf_op jit(solution)/shard_map/jit(_where)/select_n | solution.py:23
  27.9 1.3 %convolution_add_fusion.5 = f32[128,256]{1,0:T(8,128)S(1)} fusion(bf16[128,1792]{1,0:T(8,128)(2,1)} %constant_dynamic-update-slice_fusion, bf16[1792,128]{1,0:T(8,128)(2,1)S(1)} %get-tuple-element.38, bf16[1792,128]{1,0:T(8,128)(2,1)S(1)} %get-tuple-element.37, f32[256]{0:T(256)S(1)} %pad_maximum_fusion.3), kind=kOutput, calls=%fused_computation.12 | convolution fusion | flops 119308288 | bytes 1508352 | tf_op jit(solution)/shard_map/dot_general | solution.py:15
  29.2 0.3 collective-permute-start.9
  29.5 1.1 %broadcast_select_fusion.1 = (bf16[128,1792]{1,0:T(8,128)(2,1)S(1)}, bf16[128,1792]{1,0:T(8,128)(2,1)S(1)}) fusion(bf16[128,1792]{1,0:T(8,128)(2,1)} %constant_dynamic-update-slice_fusion, bf16[128,1792]{1,0:T(8,128)(2,1)S(1)} %collective-permute-done.24, pred[]{:T(512)S(6)} %eq.56), kind=kLoop, calls=%fused_computation.27 | loop fusion | flops 458752 | bytes 1835009 | tf_op jit(solution)/shard_map/jit(_where)/select_n | solution.py:23
  30.7 1.6 %collective-permute-start.14 = (bf16[128,256]{1,0:T(8,128)(2,1)S(1)}, bf16[128,256]{1,0:T(8,128)(2,1)S(1)}, u32[]{:S(2)}, u32[]{:S(2)}) collective-permute-start(bf16[128,256]{1,0:T(8,128)(2,1)S(1)} %multiply_convert_fusion), channel_id=1, source_target_pairs={{0,16},{8,24},{16,0},{24,8},{1,17},{9,25},{17,1},{25,9},{2,18},{10... | collective-permute-start | bytes 196616 | tf_op jit(solution)/shard_map/ppermute | solution.py:11
  32.7 0.6 collective-permute-start.10
  33.3 1.5 %collective-permute-start.20 = (bf16[64,896]{1,0:T(8,128)(2,1)S(1)}, bf16[64,896]{1,0:T(8,128)(2,1)S(1)}, u32[]{:S(2)}, u32[]{:S(2)}) collective-permute-start(bf16[64,896]{1,0:T(8,128)(2,1)S(1)} %convolution_convert_fusion.1), channel_id=1, source_target_pairs={{0,1},{1,0},{2,3},{3,2},{4,5},{5,4},{6,7},{7,6},{8,9},{9,8},{10,11... | collective-permute-start | bytes 344072 | tf_op jit(solution)/shard_map/ppermute | solution.py:11
  35.2 0.3 fusion.2
  35.6 0.6 collective-permute-start.15
  36.4 2.4 %collective-permute-done.10 = bf16[64,896]{1,0:T(8,128)(2,1)S(1)} collective-permute-done((bf16[64,896]{1,0:T(8,128)(2,1)S(1)}, bf16[64,896]{1,0:T(8,128)(2,1)S(1)}, u32[]{:S(2)}, u32[]{:S(2)}) %collective-permute-start.10) | collective-permute-done | bytes 114720 | tf_op jit(solution)/shard_map/ppermute | solution.py:11
  39.0 1.5 %collective-permute-start.11 = (bf16[16,896]{1,0:T(8,128)(2,1)S(1)}, bf16[16,896]{1,0:T(8,128)(2,1)S(1)}, u32[]{:S(2)}, u32[]{:S(2)}) collective-permute-start(bf16[16,896]{1,0:T(8,128)(2,1)S(1)} %get-tuple-element.44), channel_id=1, source_target_pairs={{0,6},{1,7},{2,4},{3,5},{4,2},{5,3},{6,0},{7,1},{8,14},{9,15},{10,... | collective-permute-start | bytes 86024 | tf_op jit(solution)/shard_map/ppermute | solution.py:11
  40.4 3.0 %collective-permute-start.13 = (bf16[16,896]{1,0:T(8,128)(2,1)S(1)}, bf16[16,896]{1,0:T(8,128)(2,1)S(1)}, u32[]{:S(2)}, u32[]{:S(2)}) collective-permute-start(bf16[16,896]{1,0:T(8,128)(2,1)S(1)} %get-tuple-element.45), channel_id=1, source_target_pairs={{0,2},{1,3},{2,0},{3,1},{4,6},{5,7},{6,4},{7,5},{8,10},{9,11},{10,... | collective-permute-start | bytes 86024 | tf_op jit(solution)/shard_map/ppermute | solution.py:11
  43.7 1.5 %collective-permute-start.21 = (bf16[16,896]{1,0:T(8,128)(2,1)S(1)}, bf16[16,896]{1,0:T(8,128)(2,1)S(1)}, u32[]{:S(2)}, u32[]{:S(2)}) collective-permute-start(bf16[16,896]{1,0:T(8,128)(2,1)S(1)} %get-tuple-element.50), channel_id=1, source_target_pairs={{0,6},{1,7},{2,4},{3,5},{4,2},{5,3},{6,0},{7,1},{8,14},{9,15},{10,... | collective-permute-start | bytes 86024 | tf_op jit(solution)/shard_map/ppermute | solution.py:11
  45.4 2.7 %collective-permute-start.23 = (bf16[16,896]{1,0:T(8,128)(2,1)S(1)}, bf16[16,896]{1,0:T(8,128)(2,1)S(1)}, u32[]{:S(2)}, u32[]{:S(2)}) collective-permute-start(bf16[16,896]{1,0:T(8,128)(2,1)S(1)} %get-tuple-element.51), channel_id=1, source_target_pairs={{0,2},{1,3},{2,0},{3,1},{4,6},{5,7},{6,4},{7,5},{8,10},{9,11},{10,... | collective-permute-start | bytes 86024 | tf_op jit(solution)/shard_map/ppermute | solution.py:11
  48.3 1.3 %collective-permute-done.21 = bf16[16,896]{1,0:T(8,128)(2,1)S(1)} collective-permute-done((bf16[16,896]{1,0:T(8,128)(2,1)S(1)}, bf16[16,896]{1,0:T(8,128)(2,1)S(1)}, u32[]{:S(2)}, u32[]{:S(2)}) %collective-permute-start.21) | collective-permute-done | bytes 28704 | tf_op jit(solution)/shard_map/ppermute | solution.py:11
  49.6 0.6 collective-permute-start.26
  50.2 0.6 collective-permute-done.22
  50.8 1.9 %collective-permute-start.27 = (bf16[16,896]{1,0:T(8,128)(2,1)S(1)}, bf16[16,896]{1,0:T(8,128)(2,1)S(1)}, u32[]{:S(2)}, u32[]{:S(2)}) collective-permute-start(bf16[16,896]{1,0:T(8,128)(2,1)S(1)} %get-tuple-element.32), channel_id=1, source_target_pairs={{0,6},{1,7},{2,4},{3,5},{4,2},{5,3},{6,0},{7,1},{8,14},{9,15},{10,... | collective-permute-start | bytes 86024 | tf_op jit(solution)/shard_map/ppermute | solution.py:11
  52.7 0.5 collective-permute-start.29
  53.2 2.1 %collective-permute-start.30 = (bf16[16,896]{1,0:T(8,128)(2,1)S(1)}, bf16[16,896]{1,0:T(8,128)(2,1)S(1)}, u32[]{:S(2)}, u32[]{:S(2)}) collective-permute-start(bf16[16,896]{1,0:T(8,128)(2,1)S(1)} %get-tuple-element.34), channel_id=1, source_target_pairs={{0,4},{1,5},{2,6},{3,7},{4,0},{5,1},{6,2},{7,3},{8,12},{9,13},{10,... | collective-permute-start | bytes 86024 | tf_op jit(solution)/shard_map/ppermute | solution.py:11
  55.2 1.9 %collective-permute-start.31 = (bf16[16,896]{1,0:T(8,128)(2,1)S(1)}, bf16[16,896]{1,0:T(8,128)(2,1)S(1)}, u32[]{:S(2)}, u32[]{:S(2)}) collective-permute-start(bf16[16,896]{1,0:T(8,128)(2,1)S(1)} %get-tuple-element.34), channel_id=1, source_target_pairs={{0,6},{1,7},{2,4},{3,5},{4,2},{5,3},{6,0},{7,1},{8,14},{9,15},{10,... | collective-permute-start | bytes 86024 | tf_op jit(solution)/shard_map/ppermute | solution.py:11
  57.1 1.4 %collective-permute-start.28 = (bf16[64,896]{1,0:T(8,128)(2,1)S(1)}, bf16[64,896]{1,0:T(8,128)(2,1)S(1)}, u32[]{:S(2)}, u32[]{:S(2)}) collective-permute-start(bf16[64,896]{1,0:T(8,128)(2,1)S(1)} %pad_maximum_fusion), channel_id=1, source_target_pairs={{0,1},{1,0},{2,3},{3,2},{4,5},{5,4},{6,7},{7,6},{8,9},{9,8},{10,11... | collective-permute-start | bytes 344072 | tf_op jit(solution)/shard_map/ppermute | solution.py:11
  58.5 2.7 %collective-permute-done.31 = bf16[16,896]{1,0:T(8,128)(2,1)S(1)} collective-permute-done((bf16[16,896]{1,0:T(8,128)(2,1)S(1)}, bf16[16,896]{1,0:T(8,128)(2,1)S(1)}, u32[]{:S(2)}, u32[]{:S(2)}) %collective-permute-start.31) | collective-permute-done | bytes 28704 | tf_op jit(solution)/shard_map/ppermute | solution.py:11
  61.2 0.7 collective-permute-start.32
  62.0 0.3 fusion.62
  62.4 2.5 %collective-permute-start.16 = (bf16[16,896]{1,0:T(8,128)(2,1)S(1)}, bf16[16,896]{1,0:T(8,128)(2,1)S(1)}, u32[]{:S(2)}, u32[]{:S(2)}) collective-permute-start(bf16[16,896]{1,0:T(8,128)(2,1)S(1)} %get-tuple-element.47), channel_id=1, source_target_pairs={{0,6},{1,7},{2,4},{3,5},{4,2},{5,3},{6,0},{7,1},{8,14},{9,15},{10,... | collective-permute-start | bytes 86024 | tf_op jit(solution)/shard_map/ppermute | solution.py:11
  64.9 2.0 %collective-permute-start.18 = (bf16[16,896]{1,0:T(8,128)(2,1)S(1)}, bf16[16,896]{1,0:T(8,128)(2,1)S(1)}, u32[]{:S(2)}, u32[]{:S(2)}) collective-permute-start(bf16[16,896]{1,0:T(8,128)(2,1)S(1)} %get-tuple-element.48), channel_id=1, source_target_pairs={{0,2},{1,3},{2,0},{3,1},{4,6},{5,7},{6,4},{7,5},{8,10},{9,11},{10,... | collective-permute-start | bytes 86024 | tf_op jit(solution)/shard_map/ppermute | solution.py:11
  66.8 1.3 %collective-permute-done.16 = bf16[16,896]{1,0:T(8,128)(2,1)S(1)} collective-permute-done((bf16[16,896]{1,0:T(8,128)(2,1)S(1)}, bf16[16,896]{1,0:T(8,128)(2,1)S(1)}, u32[]{:S(2)}, u32[]{:S(2)}) %collective-permute-start.16) | collective-permute-done | bytes 28704 | tf_op jit(solution)/shard_map/ppermute | solution.py:11
  68.2 1.5 %collective-permute-done.17 = bf16[16,896]{1,0:T(8,128)(2,1)S(1)} collective-permute-done((bf16[16,896]{1,0:T(8,128)(2,1)S(1)}, bf16[16,896]{1,0:T(8,128)(2,1)S(1)}, u32[]{:S(2)}, u32[]{:S(2)}) %collective-permute-start.17) | collective-permute-done | bytes 28704 | tf_op jit(solution)/shard_map/ppermute | solution.py:11
  69.7 1.1 %collective-permute-start.33 = (bf16[16,896]{1,0:T(8,128)(2,1)S(1)}, bf16[16,896]{1,0:T(8,128)(2,1)S(1)}, u32[]{:S(2)}, u32[]{:S(2)}) collective-permute-start(bf16[16,896]{1,0:T(8,128)(2,1)S(1)} %get-tuple-element.36), channel_id=1, source_target_pairs={{0,2},{1,3},{2,0},{3,1},{4,6},{5,7},{6,4},{7,5},{8,10},{9,11},{10,... | collective-permute-start | bytes 86024 | tf_op jit(solution)/shard_map/ppermute | solution.py:11
  70.8 1.3 %collective-permute-start.34 = (bf16[16,896]{1,0:T(8,128)(2,1)S(1)}, bf16[16,896]{1,0:T(8,128)(2,1)S(1)}, u32[]{:S(2)}, u32[]{:S(2)}) collective-permute-start(bf16[16,896]{1,0:T(8,128)(2,1)S(1)} %get-tuple-element.36), channel_id=1, source_target_pairs={{0,4},{1,5},{2,6},{3,7},{4,0},{5,1},{6,2},{7,3},{8,12},{9,13},{10,... | collective-permute-start | bytes 86024 | tf_op jit(solution)/shard_map/ppermute | solution.py:11
  72.1 2.1 %collective-permute-start.35 = (bf16[16,896]{1,0:T(8,128)(2,1)S(1)}, bf16[16,896]{1,0:T(8,128)(2,1)S(1)}, u32[]{:S(2)}, u32[]{:S(2)}) collective-permute-start(bf16[16,896]{1,0:T(8,128)(2,1)S(1)} %get-tuple-element.36), channel_id=1, source_target_pairs={{0,6},{1,7},{2,4},{3,5},{4,2},{5,3},{6,0},{7,1},{8,14},{9,15},{10,... | collective-permute-start | bytes 86024 | tf_op jit(solution)/shard_map/ppermute | solution.py:11
  74.2 1.6 %collective-permute-start.19 = (bf16[16,896]{1,0:T(8,128)(2,1)S(1)}, bf16[16,896]{1,0:T(8,128)(2,1)S(1)}, u32[]{:S(2)}, u32[]{:S(2)}) collective-permute-start(bf16[16,896]{1,0:T(8,128)(2,1)S(1)} %get-tuple-element.36), channel_id=1, source_target_pairs={{0,16},{8,24},{16,0},{24,8},{1,17},{9,25},{17,1},{25,9},{2,18},{10... | collective-permute-start | bytes 86024 | tf_op jit(solution)/shard_map/ppermute | solution.py:11
  75.8 2.0 %collective-permute-done.35 = bf16[16,896]{1,0:T(8,128)(2,1)S(1)} collective-permute-done((bf16[16,896]{1,0:T(8,128)(2,1)S(1)}, bf16[16,896]{1,0:T(8,128)(2,1)S(1)}, u32[]{:S(2)}, u32[]{:S(2)}) %collective-permute-start.35) | collective-permute-done | bytes 28704 | tf_op jit(solution)/shard_map/ppermute | solution.py:11
  77.8 1.1 %collective-permute-start.36 = (bf16[64,896]{1,0:T(8,128)(2,1)S(1)}, bf16[64,896]{1,0:T(8,128)(2,1)S(1)}, u32[]{:S(2)}, u32[]{:S(2)}) collective-permute-start(bf16[64,896]{1,0:T(8,128)(2,1)S(1)} %pad_maximum_fusion.2), channel_id=1, source_target_pairs={{0,1},{1,0},{2,3},{3,2},{4,5},{5,4},{6,7},{7,6},{8,9},{9,8},{10,11... | collective-permute-start | bytes 344072 | tf_op jit(solution)/shard_map/ppermute | solution.py:11
  79.2 3.4 %collective-permute-done.36 = bf16[64,896]{1,0:T(8,128)(2,1)S(1)} collective-permute-done((bf16[64,896]{1,0:T(8,128)(2,1)S(1)}, bf16[64,896]{1,0:T(8,128)(2,1)S(1)}, u32[]{:S(2)}, u32[]{:S(2)}) %collective-permute-start.36) | collective-permute-done | bytes 114720 | tf_op jit(solution)/shard_map/ppermute | solution.py:11
  82.6 0.4 fusion.10
  83.3 0.3 fusion.3
  83.7 1.7 %collective-permute-start.38 = (bf16[128,128]{1,0:T(8,128)(2,1)S(1)}, bf16[128,128]{1,0:T(8,128)(2,1)S(1)}, u32[]{:S(2)}, u32[]{:S(2)}) collective-permute-start(bf16[128,128]{1,0:T(8,128)(2,1)S(1)} %get-tuple-element.53), channel_id=1, source_target_pairs={{0,16},{8,24},{16,0},{24,8},{1,17},{9,25},{17,1},{25,9},{2,18},{10... | collective-permute-start | bytes 98312 | tf_op jit(solution)/shard_map/ppermute | solution.py:11
  85.6 0.6 maximum_bitcast_fusion
  86.3 1.4 %collective-permute-done.38 = bf16[128,128]{1,0:T(8,128)(2,1)S(1)} collective-permute-done((bf16[128,128]{1,0:T(8,128)(2,1)S(1)}, bf16[128,128]{1,0:T(8,128)(2,1)S(1)}, u32[]{:S(2)}, u32[]{:S(2)}) %collective-permute-start.38) | collective-permute-done | bytes 32800 | tf_op jit(solution)/shard_map/ppermute | solution.py:11
  87.7 1.1 %collective-permute-done.39 = bf16[128,128]{1,0:T(8,128)(2,1)S(1)} collective-permute-done((bf16[128,128]{1,0:T(8,128)(2,1)S(1)}, bf16[128,128]{1,0:T(8,128)(2,1)S(1)}, u32[]{:S(2)}, u32[]{:S(2)}) %collective-permute-start.39) | collective-permute-done | bytes 32800 | tf_op jit(solution)/shard_map/ppermute | solution.py:11
  88.8 0.6 fusion.54
  89.3 1.4 %fusion = bf16[1,3584,128]{2,1,0:T(8,128)(2,1)} fusion(bf16[128,1792]{1,0:T(8,128)(2,1)S(1)} %get-tuple-element.40, bf16[128,1792]{1,0:T(8,128)(2,1)S(1)} %get-tuple-element.39, bf16[128,128]{1,0:T(8,128)(2,1)S(1)} %get-tuple-element.30), kind=kOutput, calls=%fused_computation.1 | convolution fusion | flops 119734272 | bytes 1867776 | tf_op jit(solution)/shard_map/dot_general | solution.py:48
  (81 shorter events, 3.7 us)
Async XLA Ops:
  0.6 8.3 %copy-start = (bf16[1,2,2,128,1792]{4,3,2,1,0:T(8,128)(2,1)S(1)}, bf16[1,2,2,128,1792]{4,3,2,1,0:T(8,128)(2,1)}, u32[]{:S(2)}) copy-start(bf16[1,2,2,128,1792]{4,3,2,1,0:T(8,128)(2,1)} %param.10) | copy-start | bytes 5505028
  0.7 20.1 %copy-start.1 = (s32[2,1,12]{2,1,0:T(1,128)S(1)}, s32[2,1,12]{2,1,0:T(1,128)}, u32[]{:S(2)}) copy-start(s32[2,1,12]{2,1,0:T(1,128)} %param.11) | copy-start | bytes 292
  1.6 11.3 %collective-permute-start = (bf16[16,1792]{1,0:T(8,128)(2,1)S(1)}, bf16[16,1792]{1,0:T(8,128)(2,1)S(1)}, u32[]{:S(2)}, u32[]{:S(2)}) collective-permute-start(bf16[16,1792]{1,0:T(8,128)(2,1)S(1)} %dynamic-slice_bitcast_fusion.2), channel_id=1, source_target_pairs={{0,2},{1,3},{2,0},{3,1},{4,6},{5,7},{6,4},{7,5},{8,10},{9,11},{10,... | collective-permute-start | bytes 172040 | tf_op jit(solution)/shard_map/ppermute | solution.py:11
  4.7 8.3 %collective-permute-start.1 = (bf16[16,1792]{1,0:T(8,128)(2,1)S(1)}, bf16[16,1792]{1,0:T(8,128)(2,1)S(1)}, u32[]{:S(2)}, u32[]{:S(2)}) collective-permute-start(bf16[16,1792]{1,0:T(8,128)(2,1)S(1)} %dynamic-slice_bitcast_fusion.2), channel_id=1, source_target_pairs={{0,4},{1,5},{2,6},{3,7},{4,0},{5,1},{6,2},{7,3},{8,12},{9,13},{10,... | collective-permute-start | bytes 172040 | tf_op jit(solution)/shard_map/ppermute | solution.py:11
  7.3 6.0 %collective-permute-start.2 = (bf16[16,1792]{1,0:T(8,128)(2,1)S(1)}, bf16[16,1792]{1,0:T(8,128)(2,1)S(1)}, u32[]{:S(2)}, u32[]{:S(2)}) collective-permute-start(bf16[16,1792]{1,0:T(8,128)(2,1)S(1)} %dynamic-slice_bitcast_fusion.2), channel_id=1, source_target_pairs={{0,6},{1,7},{2,4},{3,5},{4,2},{5,3},{6,0},{7,1},{8,14},{9,15},{10,... | collective-permute-start | bytes 172040 | tf_op jit(solution)/shard_map/ppermute | solution.py:11
  7.3 10.6 %collective-permute-start.3 = (bf16[16,1792]{1,0:T(8,128)(2,1)S(1)}, bf16[16,1792]{1,0:T(8,128)(2,1)}, u32[]{:S(2)}, u32[]{:S(2)}) collective-permute-start(bf16[16,1792]{1,0:T(8,128)(2,1)S(1)} %dynamic-slice_bitcast_fusion.2), channel_id=1, source_target_pairs={{0,1},{1,0},{2,3},{3,2},{4,5},{5,4},{6,7},{7,6},{8,9},{9,8},{10,11... | collective-permute-start | bytes 172040 | tf_op jit(solution)/shard_map/ppermute | solution.py:11
  9.9 16.3 %collective-permute-start.7 = (bf16[256,896]{1,0:T(8,128)(2,1)}, bf16[256,896]{1,0:T(8,128)(2,1)S(1)}, u32[]{:S(2)}, u32[]{:S(2)}) collective-permute-start(bf16[256,896]{1,0:T(8,128)(2,1)} %dynamic-slice_bitcast_fusion.1), channel_id=1, source_target_pairs={{0,16},{8,24},{16,0},{24,8},{1,17},{9,25},{17,1},{25,9},{2,18},{10... | collective-permute-start | bytes 1376264 | tf_op jit(solution)/shard_map/ppermute | solution.py:11
  13.9 8.9 %collective-permute-start.4 = (bf16[16,1792]{1,0:T(8,128)(2,1)S(1)}, bf16[16,1792]{1,0:T(8,128)(2,1)}, u32[]{:S(2)}, u32[]{:S(2)}) collective-permute-start(bf16[16,1792]{1,0:T(8,128)(2,1)S(1)} %collective-permute-done), channel_id=1, source_target_pairs={{0,1},{1,0},{2,3},{3,2},{4,5},{5,4},{6,7},{7,6},{8,9},{9,8},{10,11... | collective-permute-start | bytes 172040 | tf_op jit(solution)/shard_map/ppermute | solution.py:11
  16.0 8.2 %collective-permute-start.5 = (bf16[16,1792]{1,0:T(8,128)(2,1)S(1)}, bf16[16,1792]{1,0:T(8,128)(2,1)}, u32[]{:S(2)}, u32[]{:S(2)}) collective-permute-start(bf16[16,1792]{1,0:T(8,128)(2,1)S(1)} %collective-permute-done.1), channel_id=1, source_target_pairs={{0,1},{1,0},{2,3},{3,2},{4,5},{5,4},{6,7},{7,6},{8,9},{9,8},{10,11... | collective-permute-start | bytes 172040 | tf_op jit(solution)/shard_map/ppermute | solution.py:11
  17.1 9.4 %collective-permute-start.8 = (bf16[3584,128]{1,0:T(8,128)(2,1)}, bf16[3584,128]{1,0:T(8,128)(2,1)}, u32[]{:S(2)}, u32[]{:S(2)}) collective-permute-start(bf16[3584,128]{1,0:T(8,128)(2,1)} %bitcast.46), channel_id=1, source_target_pairs={{0,8},{8,0},{16,24},{24,16},{1,9},{9,1},{17,25},{25,17},{2,10},{10... | collective-permute-start | bytes 2752520 | tf_op jit(solution)/shard_map/ppermute | solution.py:11
  17.8 7.8 %collective-permute-start.6 = (bf16[16,1792]{1,0:T(8,128)(2,1)S(1)}, bf16[16,1792]{1,0:T(8,128)(2,1)S(1)}, u32[]{:S(2)}, u32[]{:S(2)}) collective-permute-start(bf16[16,1792]{1,0:T(8,128)(2,1)S(1)} %collective-permute-done.2), channel_id=1, source_target_pairs={{0,1},{1,0},{2,3},{3,2},{4,5},{5,4},{6,7},{7,6},{8,9},{9,8},{10,11... | collective-permute-start | bytes 172040 | tf_op jit(solution)/shard_map/ppermute | solution.py:11
  26.3 3.2 %collective-permute-start.24 = (bf16[128,1792]{1,0:T(8,128)(2,1)}, bf16[128,1792]{1,0:T(8,128)(2,1)S(1)}, u32[]{:S(2)}, u32[]{:S(2)}) collective-permute-start(bf16[128,1792]{1,0:T(8,128)(2,1)} %constant_dynamic-update-slice_fusion), channel_id=1, source_target_pairs={{0,8},{8,0},{16,24},{24,16},{1,9},{9,1},{17,25},{25,17},{2,10},{10... | collective-permute-start | bytes 1376264 | tf_op jit(solution)/shard_map/ppermute | solution.py:11
  29.2 1.4 %collective-permute-start.9 = (f32[128,256]{1,0:T(8,128)S(1)}, f32[128,256]{1,0:T(8,128)S(1)}, u32[]{:S(2)}, u32[]{:S(2)}) collective-permute-start(f32[128,256]{1,0:T(8,128)S(1)} %convolution_add_fusion.5), channel_id=1, source_target_pairs={{0,8},{8,0},{16,24},{24,16},{1,9},{9,1},{17,25},{25,17},{2,10},{10... | collective-permute-start | bytes 393224 | tf_op jit(solution)/shard_map/ppermute | solution.py:11
  30.7 4.3 %collective-permute-start.14 = (bf16[128,256]{1,0:T(8,128)(2,1)S(1)}, bf16[128,256]{1,0:T(8,128)(2,1)S(1)}, u32[]{:S(2)}, u32[]{:S(2)}) collective-permute-start(bf16[128,256]{1,0:T(8,128)(2,1)S(1)} %multiply_convert_fusion), channel_id=1, source_target_pairs={{0,16},{8,24},{16,0},{24,8},{1,17},{9,25},{17,1},{25,9},{2,18},{10... | collective-permute-start | bytes 196616 | tf_op jit(solution)/shard_map/ppermute | solution.py:11
  32.7 6.1 %collective-permute-start.10 = (bf16[64,896]{1,0:T(8,128)(2,1)S(1)}, bf16[64,896]{1,0:T(8,128)(2,1)S(1)}, u32[]{:S(2)}, u32[]{:S(2)}) collective-permute-start(bf16[64,896]{1,0:T(8,128)(2,1)S(1)} %convolution_convert_fusion.2), channel_id=1, source_target_pairs={{0,1},{1,0},{2,3},{3,2},{4,5},{5,4},{6,7},{7,6},{8,9},{9,8},{10,11... | collective-permute-start | bytes 344072 | tf_op jit(solution)/shard_map/ppermute | solution.py:11
  33.3 10.2 %collective-permute-start.20 = (bf16[64,896]{1,0:T(8,128)(2,1)S(1)}, bf16[64,896]{1,0:T(8,128)(2,1)S(1)}, u32[]{:S(2)}, u32[]{:S(2)}) collective-permute-start(bf16[64,896]{1,0:T(8,128)(2,1)S(1)} %convolution_convert_fusion.1), channel_id=1, source_target_pairs={{0,1},{1,0},{2,3},{3,2},{4,5},{5,4},{6,7},{7,6},{8,9},{9,8},{10,11... | collective-permute-start | bytes 344072 | tf_op jit(solution)/shard_map/ppermute | solution.py:11
  35.6 26.5 %collective-permute-start.15 = (bf16[64,896]{1,0:T(8,128)(2,1)S(1)}, bf16[64,896]{1,0:T(8,128)(2,1)S(1)}, u32[]{:S(2)}, u32[]{:S(2)}) collective-permute-start(bf16[64,896]{1,0:T(8,128)(2,1)S(1)} %fusion.2), channel_id=1, source_target_pairs={{0,1},{1,0},{2,3},{3,2},{4,5},{5,4},{6,7},{7,6},{8,9},{9,8},{10,11... | collective-permute-start | bytes 344072 | tf_op jit(solution)/shard_map/ppermute | solution.py:11
  39.0 6.1 %collective-permute-start.11 = (bf16[16,896]{1,0:T(8,128)(2,1)S(1)}, bf16[16,896]{1,0:T(8,128)(2,1)S(1)}, u32[]{:S(2)}, u32[]{:S(2)}) collective-permute-start(bf16[16,896]{1,0:T(8,128)(2,1)S(1)} %get-tuple-element.44), channel_id=1, source_target_pairs={{0,6},{1,7},{2,4},{3,5},{4,2},{5,3},{6,0},{7,1},{8,14},{9,15},{10,... | collective-permute-start | bytes 86024 | tf_op jit(solution)/shard_map/ppermute | solution.py:11
  40.4 5.0 %collective-permute-start.12 = (bf16[16,896]{1,0:T(8,128)(2,1)S(1)}, bf16[16,896]{1,0:T(8,128)(2,1)S(1)}, u32[]{:S(2)}, u32[]{:S(2)}) collective-permute-start(bf16[16,896]{1,0:T(8,128)(2,1)S(1)} %get-tuple-element.46), channel_id=1, source_target_pairs={{0,4},{1,5},{2,6},{3,7},{4,0},{5,1},{6,2},{7,3},{8,12},{9,13},{10,... | collective-permute-start | bytes 86024 | tf_op jit(solution)/shard_map/ppermute | solution.py:11
  40.4 7.7 %collective-permute-start.13 = (bf16[16,896]{1,0:T(8,128)(2,1)S(1)}, bf16[16,896]{1,0:T(8,128)(2,1)S(1)}, u32[]{:S(2)}, u32[]{:S(2)}) collective-permute-start(bf16[16,896]{1,0:T(8,128)(2,1)S(1)} %get-tuple-element.45), channel_id=1, source_target_pairs={{0,2},{1,3},{2,0},{3,1},{4,6},{5,7},{6,4},{7,5},{8,10},{9,11},{10,... | collective-permute-start | bytes 86024 | tf_op jit(solution)/shard_map/ppermute | solution.py:11
  43.7 5.9 %collective-permute-start.21 = (bf16[16,896]{1,0:T(8,128)(2,1)S(1)}, bf16[16,896]{1,0:T(8,128)(2,1)S(1)}, u32[]{:S(2)}, u32[]{:S(2)}) collective-permute-start(bf16[16,896]{1,0:T(8,128)(2,1)S(1)} %get-tuple-element.50), channel_id=1, source_target_pairs={{0,6},{1,7},{2,4},{3,5},{4,2},{5,3},{6,0},{7,1},{8,14},{9,15},{10,... | collective-permute-start | bytes 86024 | tf_op jit(solution)/shard_map/ppermute | solution.py:11
  45.1 5.6 %collective-permute-start.22 = (bf16[16,896]{1,0:T(8,128)(2,1)S(1)}, bf16[16,896]{1,0:T(8,128)(2,1)S(1)}, u32[]{:S(2)}, u32[]{:S(2)}) collective-permute-start(bf16[16,896]{1,0:T(8,128)(2,1)S(1)} %get-tuple-element.52), channel_id=1, source_target_pairs={{0,4},{1,5},{2,6},{3,7},{4,0},{5,1},{6,2},{7,3},{8,12},{9,13},{10,... | collective-permute-start | bytes 86024 | tf_op jit(solution)/shard_map/ppermute | solution.py:11
  45.4 7.2 %collective-permute-start.23 = (bf16[16,896]{1,0:T(8,128)(2,1)S(1)}, bf16[16,896]{1,0:T(8,128)(2,1)S(1)}, u32[]{:S(2)}, u32[]{:S(2)}) collective-permute-start(bf16[16,896]{1,0:T(8,128)(2,1)S(1)} %get-tuple-element.51), channel_id=1, source_target_pairs={{0,2},{1,3},{2,0},{3,1},{4,6},{5,7},{6,4},{7,5},{8,10},{9,11},{10,... | collective-permute-start | bytes 86024 | tf_op jit(solution)/shard_map/ppermute | solution.py:11
  48.2 5.0 %collective-permute-start.25 = (bf16[16,896]{1,0:T(8,128)(2,1)S(1)}, bf16[16,896]{1,0:T(8,128)(2,1)S(1)}, u32[]{:S(2)}, u32[]{:S(2)}) collective-permute-start(bf16[16,896]{1,0:T(8,128)(2,1)S(1)} %get-tuple-element.32), channel_id=1, source_target_pairs={{0,2},{1,3},{2,0},{3,1},{4,6},{5,7},{6,4},{7,5},{8,10},{9,11},{10,... | collective-permute-start | bytes 86024 | tf_op jit(solution)/shard_map/ppermute | solution.py:11
  49.6 5.7 %collective-permute-start.26 = (bf16[16,896]{1,0:T(8,128)(2,1)S(1)}, bf16[16,896]{1,0:T(8,128)(2,1)S(1)}, u32[]{:S(2)}, u32[]{:S(2)}) collective-permute-start(bf16[16,896]{1,0:T(8,128)(2,1)S(1)} %get-tuple-element.32), channel_id=1, source_target_pairs={{0,4},{1,5},{2,6},{3,7},{4,0},{5,1},{6,2},{7,3},{8,12},{9,13},{10,... | collective-permute-start | bytes 86024 | tf_op jit(solution)/shard_map/ppermute | solution.py:11
  50.8 6.4 %collective-permute-start.27 = (bf16[16,896]{1,0:T(8,128)(2,1)S(1)}, bf16[16,896]{1,0:T(8,128)(2,1)S(1)}, u32[]{:S(2)}, u32[]{:S(2)}) collective-permute-start(bf16[16,896]{1,0:T(8,128)(2,1)S(1)} %get-tuple-element.32), channel_id=1, source_target_pairs={{0,6},{1,7},{2,4},{3,5},{4,2},{5,3},{6,0},{7,1},{8,14},{9,15},{10,... | collective-permute-start | bytes 86024 | tf_op jit(solution)/shard_map/ppermute | solution.py:11
  52.7 5.8 %collective-permute-start.29 = (bf16[16,896]{1,0:T(8,128)(2,1)S(1)}, bf16[16,896]{1,0:T(8,128)(2,1)S(1)}, u32[]{:S(2)}, u32[]{:S(2)}) collective-permute-start(bf16[16,896]{1,0:T(8,128)(2,1)S(1)} %get-tuple-element.34), channel_id=1, source_target_pairs={{0,2},{1,3},{2,0},{3,1},{4,6},{5,7},{6,4},{7,5},{8,10},{9,11},{10,... | collective-permute-start | bytes 86024 | tf_op jit(solution)/shard_map/ppermute | solution.py:11
  53.2 5.3 %collective-permute-start.30 = (bf16[16,896]{1,0:T(8,128)(2,1)S(1)}, bf16[16,896]{1,0:T(8,128)(2,1)S(1)}, u32[]{:S(2)}, u32[]{:S(2)}) collective-permute-start(bf16[16,896]{1,0:T(8,128)(2,1)S(1)} %get-tuple-element.34), channel_id=1, source_target_pairs={{0,4},{1,5},{2,6},{3,7},{4,0},{5,1},{6,2},{7,3},{8,12},{9,13},{10,... | collective-permute-start | bytes 86024 | tf_op jit(solution)/shard_map/ppermute | solution.py:11
  55.2 6.0 %collective-permute-start.31 = (bf16[16,896]{1,0:T(8,128)(2,1)S(1)}, bf16[16,896]{1,0:T(8,128)(2,1)S(1)}, u32[]{:S(2)}, u32[]{:S(2)}) collective-permute-start(bf16[16,896]{1,0:T(8,128)(2,1)S(1)} %get-tuple-element.34), channel_id=1, source_target_pairs={{0,6},{1,7},{2,4},{3,5},{4,2},{5,3},{6,0},{7,1},{8,14},{9,15},{10,... | collective-permute-start | bytes 86024 | tf_op jit(solution)/shard_map/ppermute | solution.py:11
  57.1 22.1 %collective-permute-start.28 = (bf16[64,896]{1,0:T(8,128)(2,1)S(1)}, bf16[64,896]{1,0:T(8,128)(2,1)S(1)}, u32[]{:S(2)}, u32[]{:S(2)}) collective-permute-start(bf16[64,896]{1,0:T(8,128)(2,1)S(1)} %pad_maximum_fusion), channel_id=1, source_target_pairs={{0,1},{1,0},{2,3},{3,2},{4,5},{5,4},{6,7},{7,6},{8,9},{9,8},{10,11... | collective-permute-start | bytes 344072 | tf_op jit(solution)/shard_map/ppermute | solution.py:11
  61.2 17.7 %collective-permute-start.32 = (bf16[64,896]{1,0:T(8,128)(2,1)S(1)}, bf16[64,896]{1,0:T(8,128)(2,1)S(1)}, u32[]{:S(2)}, u32[]{:S(2)}) collective-permute-start(bf16[64,896]{1,0:T(8,128)(2,1)S(1)} %pad_maximum_fusion.1), channel_id=1, source_target_pairs={{0,1},{1,0},{2,3},{3,2},{4,5},{5,4},{6,7},{7,6},{8,9},{9,8},{10,11... | collective-permute-start | bytes 344072 | tf_op jit(solution)/shard_map/ppermute | solution.py:11
  62.4 5.8 %collective-permute-start.16 = (bf16[16,896]{1,0:T(8,128)(2,1)S(1)}, bf16[16,896]{1,0:T(8,128)(2,1)S(1)}, u32[]{:S(2)}, u32[]{:S(2)}) collective-permute-start(bf16[16,896]{1,0:T(8,128)(2,1)S(1)} %get-tuple-element.47), channel_id=1, source_target_pairs={{0,6},{1,7},{2,4},{3,5},{4,2},{5,3},{6,0},{7,1},{8,14},{9,15},{10,... | collective-permute-start | bytes 86024 | tf_op jit(solution)/shard_map/ppermute | solution.py:11
  64.9 4.8 %collective-permute-start.17 = (bf16[16,896]{1,0:T(8,128)(2,1)S(1)}, bf16[16,896]{1,0:T(8,128)(2,1)S(1)}, u32[]{:S(2)}, u32[]{:S(2)}) collective-permute-start(bf16[16,896]{1,0:T(8,128)(2,1)S(1)} %get-tuple-element.49), channel_id=1, source_target_pairs={{0,4},{1,5},{2,6},{3,7},{4,0},{5,1},{6,2},{7,3},{8,12},{9,13},{10,... | collective-permute-start | bytes 86024 | tf_op jit(solution)/shard_map/ppermute | solution.py:11
  64.9 4.8 %collective-permute-start.18 = (bf16[16,896]{1,0:T(8,128)(2,1)S(1)}, bf16[16,896]{1,0:T(8,128)(2,1)S(1)}, u32[]{:S(2)}, u32[]{:S(2)}) collective-permute-start(bf16[16,896]{1,0:T(8,128)(2,1)S(1)} %get-tuple-element.48), channel_id=1, source_target_pairs={{0,2},{1,3},{2,0},{3,1},{4,6},{5,7},{6,4},{7,5},{8,10},{9,11},{10,... | collective-permute-start | bytes 86024 | tf_op jit(solution)/shard_map/ppermute | solution.py:11
  69.7 4.5 %collective-permute-start.33 = (bf16[16,896]{1,0:T(8,128)(2,1)S(1)}, bf16[16,896]{1,0:T(8,128)(2,1)S(1)}, u32[]{:S(2)}, u32[]{:S(2)}) collective-permute-start(bf16[16,896]{1,0:T(8,128)(2,1)S(1)} %get-tuple-element.36), channel_id=1, source_target_pairs={{0,2},{1,3},{2,0},{3,1},{4,6},{5,7},{6,4},{7,5},{8,10},{9,11},{10,... | collective-permute-start | bytes 86024 | tf_op jit(solution)/shard_map/ppermute | solution.py:11
  70.8 5.0 %collective-permute-start.34 = (bf16[16,896]{1,0:T(8,128)(2,1)S(1)}, bf16[16,896]{1,0:T(8,128)(2,1)S(1)}, u32[]{:S(2)}, u32[]{:S(2)}) collective-permute-start(bf16[16,896]{1,0:T(8,128)(2,1)S(1)} %get-tuple-element.36), channel_id=1, source_target_pairs={{0,4},{1,5},{2,6},{3,7},{4,0},{5,1},{6,2},{7,3},{8,12},{9,13},{10,... | collective-permute-start | bytes 86024 | tf_op jit(solution)/shard_map/ppermute | solution.py:11
  72.1 5.7 %collective-permute-start.35 = (bf16[16,896]{1,0:T(8,128)(2,1)S(1)}, bf16[16,896]{1,0:T(8,128)(2,1)S(1)}, u32[]{:S(2)}, u32[]{:S(2)}) collective-permute-start(bf16[16,896]{1,0:T(8,128)(2,1)S(1)} %get-tuple-element.36), channel_id=1, source_target_pairs={{0,6},{1,7},{2,4},{3,5},{4,2},{5,3},{6,0},{7,1},{8,14},{9,15},{10,... | collective-permute-start | bytes 86024 | tf_op jit(solution)/shard_map/ppermute | solution.py:11
  74.2 4.7 %collective-permute-start.19 = (bf16[16,896]{1,0:T(8,128)(2,1)S(1)}, bf16[16,896]{1,0:T(8,128)(2,1)S(1)}, u32[]{:S(2)}, u32[]{:S(2)}) collective-permute-start(bf16[16,896]{1,0:T(8,128)(2,1)S(1)} %get-tuple-element.36), channel_id=1, source_target_pairs={{0,16},{8,24},{16,0},{24,8},{1,17},{9,25},{17,1},{25,9},{2,18},{10... | collective-permute-start | bytes 86024 | tf_op jit(solution)/shard_map/ppermute | solution.py:11
  77.8 4.9 %collective-permute-start.36 = (bf16[64,896]{1,0:T(8,128)(2,1)S(1)}, bf16[64,896]{1,0:T(8,128)(2,1)S(1)}, u32[]{:S(2)}, u32[]{:S(2)}) collective-permute-start(bf16[64,896]{1,0:T(8,128)(2,1)S(1)} %pad_maximum_fusion.2), channel_id=1, source_target_pairs={{0,1},{1,0},{2,3},{3,2},{4,5},{5,4},{6,7},{7,6},{8,9},{9,8},{10,11... | collective-permute-start | bytes 344072 | tf_op jit(solution)/shard_map/ppermute | solution.py:11
  83.6 5.1 %collective-permute-start.37 = (f32[128,128]{1,0:T(8,128)S(1)}, f32[128,128]{1,0:T(8,128)S(1)}, u32[]{:S(2)}, u32[]{:S(2)}) collective-permute-start(f32[128,128]{1,0:T(8,128)S(1)} %slice_select_fusion), channel_id=1, source_target_pairs={{0,8},{8,0},{16,24},{24,16},{1,9},{9,1},{17,25},{25,17},{2,10},{10... | collective-permute-start | bytes 196616 | tf_op jit(solution)/shard_map/ppermute | solution.py:11
  83.7 4.0 %collective-permute-start.38 = (bf16[128,128]{1,0:T(8,128)(2,1)S(1)}, bf16[128,128]{1,0:T(8,128)(2,1)S(1)}, u32[]{:S(2)}, u32[]{:S(2)}) collective-permute-start(bf16[128,128]{1,0:T(8,128)(2,1)S(1)} %get-tuple-element.53), channel_id=1, source_target_pairs={{0,16},{8,24},{16,0},{24,8},{1,17},{9,25},{17,1},{25,9},{2,18},{10... | collective-permute-start | bytes 98312 | tf_op jit(solution)/shard_map/ppermute | solution.py:11
  85.4 3.3 %collective-permute-start.39 = (bf16[128,128]{1,0:T(8,128)(2,1)S(1)}, bf16[128,128]{1,0:T(8,128)(2,1)S(1)}, u32[]{:S(2)}, u32[]{:S(2)}) collective-permute-start(bf16[128,128]{1,0:T(8,128)(2,1)S(1)} %get-tuple-element.54), channel_id=1, source_target_pairs={{0,24},{8,16},{16,8},{24,0},{1,25},{9,17},{17,9},{25,1},{2,26},{10... | collective-permute-start | bytes 98312 | tf_op jit(solution)/shard_map/ppermute | solution.py:11

commit v4 on v2

--- a/solution.py
+++ b/solution.py
@@ -35,10 +35,12 @@
     return out
 
 
-def paired_encoder(weight, bias, half, cols):
-    other = crossed(lax.dynamic_slice_in_dim(weight, (1 - half) * cols, cols, 0), "layer", 1)
+def half_preacts(resid_half, weight, weight_other, bias, half):
+    cols = resid_half.shape[1]
     mine = lax.dynamic_slice_in_dim(weight, half * cols, cols, 0)
-    return both_halves(half, mine, other, 1), both_halves(half, bias, crossed(bias, "layer", 1), 0)
+    other = lax.dynamic_slice_in_dim(weight_other, half * cols, cols, 0)
+    nothing = jnp.zeros_like(bias)
+    return times(resid_half, both_halves(half, mine, other, 1)) + both_halves(half, bias, nothing, 0)
 
 
 def encoder_gradient(resid_half, resid_other, grad_low, half):
@@ -52,63 +54,107 @@
     far = slots // 2
     layer, half = lax.axis_index("layer") // 2, lax.axis_index("layer") % 2
     slot = lax.axis_index("latent")
+    side = slot % 2
     _, rows, width = resid.shape
     tokens, cols, part = rows * slots, width // 2, width // 4
     latents = enc_weight.shape[2]
-    near_rows = tokens // 2
     decoder = dec_weight[0].reshape(2, 2 * latents, cols)
 
+    def over_x(block):
+        return crossed(block, "latent", 1)
+
+    def along_z(block):
+        out = [block] + [None] * (far - 1)
+        for k in range(far - 1, 0, -1):
+            out[k] = crossed(block, "latent", 2 * k)
+        return out
+
+    def decoder_part(decoder, which, where):
+        return lax.dynamic_slice(decoder, (which, 0, where * part), (1, 2 * latents, part))[0]
+
+    def turned(array):
+        return array.reshape(far, 2, rows, array.shape[1])[:, ::-1].reshape(array.shape)
+
+    weight_other = crossed(enc_weight[0], "layer", 1)
     mine = lax.dynamic_slice(resid, (layer, 0, half * cols), (1, rows, cols))[0]
-    along = [mine] + [crossed(mine, "latent", 2 * k) for k in range(1, far)]
-    beside = [crossed(block, "latent", 1) for block in along]
-    resid_half = jnp.concatenate(along + beside, axis=0)
-
-    shared = lax.dynamic_index_in_dim(decoder, 1 - layer, 0, keepdims=False)
-    dec_given = crossed(lax.dynamic_slice_in_dim(shared, (1 - layer) * part, part, 1), "layer", 2)
-    dec_kept = lax.dynamic_slice_in_dim(shared, layer * part, part, 1)
-    dec_own = lax.dynamic_index_in_dim(decoder, layer, 0, keepdims=False)
-    weight_pair, bias_pair = paired_encoder(enc_weight[0], enc_bias[0], half, cols)
+    pair = jnp.concatenate([mine, over_x(mine)], axis=0)
+    pair, weight_other, later = lax.optimization_barrier((pair, weight_other, decoder))
+    column = along_z(pair)
+
+    shared_other = over_x(decoder_part(decoder, 1 - layer, 1 - side))
+    own_other = over_x(decoder_part(later, layer, 1 - side))
+    decoder, target, blocks, *column = lax.optimization_barrier((decoder, target, blocks, *column))
+    shared_mine, own_mine = decoder_part(decoder, 1 - layer, side), decoder_part(decoder, layer, side)
+    resid_half = jnp.concatenate(column, axis=0)
     firing = gates(blocks, layer, slot, slots, latents, tokens)
     gate = jnp.where(half == 0, firing[0], firing[1])
 
-    partial = times(resid_half, weight_pair)
-    preact = partial + crossed(partial, "layer", 1) + bias_pair
-    acts = (preact * jnp.concatenate(firing, axis=1)).astype(BF16)
-    acts_other = crossed(acts, "layer", 2)
+    def aims_for(where):
+        start = half * cols + where * part
+        own = lax.dynamic_slice(target, (2 * layer, 0, start), (1, rows, part))
+        return jnp.concatenate([own, lax.dynamic_slice(target, (1, 0, start), (1, rows, part))], axis=0)
+
+    aims, aims_other = aims_for(side), over_x(aims_for(1 - side))
+    aim_own = jnp.concatenate([aims[0], aims_other[0]], axis=0).astype(F32)
+    aim_shared = jnp.where(layer == 0, aims[1], aims_other[1]).astype(F32)
+
+    partial = half_preacts(resid_half, enc_weight[0], weight_other, enc_bias[0], half)
+    acts = ((partial + crossed(partial, "layer", 1)) * jnp.concatenate(firing, axis=1)).astype(BF16)
+    acts_other = turned(over_x(acts))
     resid_other = crossed(resid_half, "layer", 1)
 
-    def scattered(product):
-        leaving = product(slice(near_rows, tokens)).astype(BF16)
-        near = product(slice(0, near_rows)) + crossed(leaving, "latent", 1).astype(F32)
-        total = near[:rows]
-        for k in range(1, far):
-            total = total + crossed(near[k * rows:(k + 1) * rows].astype(BF16), "latent", 2 * k).astype(F32)
-        return total
-
-    def gathered(block):
-        along = [block] + [crossed(block, "latent", 2 * k) for k in range(1, far)]
-        near = jnp.concatenate(along, axis=0)
-        return jnp.concatenate([near, crossed(near, "latent", 1)], axis=0)
-
-    sum_own = scattered(lambda at: times(acts[at], dec_own))
-    sum_shared = scattered(lambda at: times(acts[at], dec_kept) + times(acts_other[at], dec_given))
-    wanted_own = lax.dynamic_slice(target, (2 * layer, 0, half * cols), (1, rows, cols))[0]
-    wanted_shared = lax.dynamic_slice(target, (1, 0, half * cols + layer * part), (1, rows, part))[0]
-    err_own = (sum_own - wanted_own.astype(F32)).astype(BF16)
-    err_shared = (sum_shared - wanted_shared.astype(F32)).astype(BF16)
-    err_across = crossed(err_shared, "layer", 2)
-    errors = jnp.where(layer == 0, err_own, jnp.concatenate([err_across, err_shared], axis=1))
-
-    errs_own, errs_shared = gathered(err_own), gathered(err_shared)
-    back = times_transposed(errs_shared, dec_given).astype(BF16)
-    here = times_transposed(errs_own, dec_own) + times_transposed(errs_shared, dec_kept)
+    def rows_of(array, which):
+        split = array.reshape(far, 2, rows, array.shape[1])
+        return jnp.where(which == 0, split[:, 0], split[:, 1]).reshape(tokens // 2, array.shape[1])
+
+    def kept(array):
+        return rows_of(array, layer)
+
+    def left(array):
+        return rows_of(array, 1 - layer)
+
+    leaving = times(left(acts), shared_mine) + times(left(acts_other), shared_other)
+    staying = times(kept(acts), shared_mine) + times(kept(acts_other), shared_other)
+    staying = staying + crossed(leaving.astype(BF16), "layer", 2).astype(F32)
+    sum_shared = staying[:rows]
+    for k in range(far - 1, 0, -1):
+        piece = staying[k * rows:(k + 1) * rows].astype(BF16)
+        sum_shared = sum_shared + crossed(piece, "latent", 2 * k).astype(F32)
+    err_shared = (sum_shared - aim_shared).astype(BF16)
+
+    acts, acts_other, staying = lax.optimization_barrier((acts, acts_other, staying))
+    product = times(acts, own_mine) + times(acts_other, own_other)
+    sum_own = product[:2 * rows]
+    for k in range(far - 1, 0, -1):
+        piece = product[2 * k * rows:2 * (k + 1) * rows].astype(BF16)
+        sum_own = sum_own + crossed(piece, "latent", 2 * k).astype(F32)
+    err_own = (sum_own - aim_own).astype(BF16)
+
+    shared_near = jnp.concatenate(along_z(err_shared), axis=0)
+    shared_far = crossed(shared_near, "layer", 2)
+    halves = [block.reshape(far, 1, rows, part) for block in (shared_near, shared_far)]
+    errs_shared = jnp.where(
+        layer == 0, jnp.concatenate(halves, axis=1), jnp.concatenate(halves[::-1], axis=1)
+    ).reshape(tokens, part)
+    errs_own = jnp.concatenate(along_z(err_own), axis=0)
+
+    here = jnp.where(layer == 0, err_own[:rows], shared_far[:rows])
+    there = over_x(jnp.where(layer == 0, err_own[rows:], err_shared))
+    errors = jnp.concatenate([jnp.where(side == 0, here, there), jnp.where(side == 0, there, here)], axis=1)
+
+    to_mine = times_transposed(errs_shared, shared_mine) + times_transposed(errs_own, own_mine)
+    to_other = times_transposed(errs_shared, shared_other) + times_transposed(errs_own, own_other)
+    to_other = turned(to_other.astype(BF16))
 
     def of_half(pair, which):
         return jnp.where(which == 0, pair[:, :latents], pair[:, latents:])
 
-    grad = of_half(here, half) + crossed(of_half(here, 1 - half), "layer", 1)
-    grad = grad + crossed(of_half(back, half), "layer", 2).astype(F32)
-    grad = grad + crossed(of_half(back, 1 - half), "layer", 3).astype(F32)
+    diagonal = of_half(to_other, 1 - half)
+    count = lax.axis_size("layer")
+    route = [(i * slots + j, (i ^ 1) * slots + (j ^ 1)) for i in range(count) for j in range(slots)]
+    grad = of_half(to_mine, half) + crossed(of_half(to_mine, 1 - half), "layer", 1)
+    grad = grad + over_x(of_half(to_other, half)).astype(F32)
+    grad = grad + lax.ppermute(diagonal, ("layer", "latent"), route).astype(F32)
     grad_pre = grad * gate
     bias_grad = jnp.sum(grad_pre, axis=0)[None, :]
     enc_grad = encoder_gradient(resid_half, resid_other, grad_pre.astype(BF16), half)
@@ -134,11 +180,11 @@
         return lax.ppermute(block, "layer", route)
 
     resid_half = to_all(lax.dynamic_slice(resid, (layer, 0, half * cols), (1, rows, cols))[0])
-    weight_pair, bias_pair = paired_encoder(enc_weight[0], enc_bias[0], half, cols)
     firing = gates(blocks, layer, slot, slots, latents, tokens)
     gate = jnp.where(half == 0, firing[0], firing[1])
-    partial = times(resid_half, weight_pair)
-    preact = partial + crossed(partial, "layer", 1) + bias_pair
+    weight_other = crossed(enc_weight[0], "layer", 1)
+    partial = half_preacts(resid_half, enc_weight[0], weight_other, enc_bias[0], half)
+    preact = partial + crossed(partial, "layer", 1)
     acts = (preact * jnp.concatenate(firing, axis=1)).astype(BF16)
     resid_other = crossed(resid_half, "layer", 1)
 

time: 79.8 us -> 79.7 us (level)
  waiting for transfers between devices: 27.7 us -> 19.3 us
  other arithmetic: 4.46 us -> 8.81 us
  local copies, waits for them, and re-layouts: 3.95 us -> 6.08 us
  matrix products: 4.42 us -> 5.72 us
    ppermute x33 -> x28, waiting for transfers between devices: 27.7 us -> 18.4 us  [crossed(): lax.ppermute(block, axis, [(i, i ^ mask) for i in range(lax.axis_size(axi...]
    squeeze x0 -> x5, local copies, waits for them, and re-layouts: none -> 4.48 us  [the longest x2 2.01 us: two_layers(): aim_own = jnp.concatenate([aims[0], aims_other[0]], axis=0).astype(F32)]
    select_n x3, other arithmetic: 0.26 us -> 3.13 us  [both_halves(): jnp.where(half == 0, mine, other)]
    dynamic_slice x2 -> x0, local copies, waits for them, and re-layouts: 2.8 us -> none  [the longest x1 1.81 us: paired_encoder(): lax.dynamic_slice_in_dim(weight, (1 - half) * cols, cols, 0)]
    select_n x0 -> x5, other arithmetic: none -> 2.22 us  [the longest x1 1.39 us: two_layers(): there = over_x(jnp.where(layer == 0, err_own[rows:], err_shared))]
    unnamed x2 -> x0, other arithmetic: 1.63 us -> none
    rev x0 -> x2, local copies, waits for them, and re-layouts: none -> 1.47 us  [turned(): array.reshape(far, 2, rows, array.shape[1])[:, ::-1].reshape(array.shape)]
    dot_general x7, matrix products: 1.95 us -> 3.16 us  [times(): return jnp.dot(left, right, preferred_element_type=F32)]
  transfers between devices with their start and end apart: 33 -> 29, of which waited for: 15 -> 12; matrix products, arithmetic and copies ran while one was open for 12% -> 22% of each run, Pallas kernels for 0% -> 0%
where the time goes in v4:
time: 79.7 us; the launch traced here: 79.2 us
  starting transfers between devices  37 us (46%)
  waiting for transfers between devices  19.3 us (24%)
  other arithmetic  8.81 us (11%)
  local copies, waits for them, and re-layouts  6.08 us (8%)
  matrix products  5.72 us (7%)
  between operations  2.26 us (3%)
    ppermute x28, starting transfers between devices, crossed(): lax.ppermute(block, axis, [(i, i ^ mask) for i in range(lax.axis_size(axi...  36.6 us
    ppermute x28, waiting for transfers between devices, crossed(): lax.ppermute(block, axis, [(i, i ^ mask) for i in range(lax.axis_size(axi...  18.4 us
    dot_general x7, matrix products, times(): return jnp.dot(left, right, preferred_element_type=F32)  3.16 us
    select_n x3, other arithmetic, both_halves(): jnp.where(half == 0, mine, other)  3.13 us
    squeeze x2, local copies, waits for them, and re-layouts, two_layers(): aim_own = jnp.concatenate([aims[0], aims_other[0]], axis=0).astype(F32)  2.01 us
    squeeze x2, local copies, waits for them, and re-layouts, decoder_part(): lax.dynamic_slice(decoder, (which, 0, where * part), (1, 2 * latents, part))  1.62 us
  transfers between devices with their start and end apart: 29, of which 12 were waited for; matrix products, arithmetic and copies ran while one was open for 22% of the time, Pallas kernels for 0%

profile of v4, /device:TPU:0, one launch (start us, length us, event | category | flops | bytes accessed | tf_op | source)
XLA Modules:
  0.0 79.2 jit_solution(5927305162639736817)
XLA Ops:
  0.6 0.5 collective-permute-start.1
  1.2 0.9 %dynamic-slice_bitcast_fusion.2 = bf16[16,1792]{1,0:T(8,128)(2,1)S(1)} fusion(bf16[2,16,3584]{2,1,0:T(8,128)(2,1)} %param.6, s32[]{:T(128)S(6)} %select_n.214, s32[]{:T(128)S(6)} %select_n.216), kind=kLoop, calls=%fused_computation.56 | loop fusion | bytes 114696 | tf_op jit(solution)/shard_map/squeeze | solution.py:79
  2.0 2.6 %collective-permute-start = (bf16[16,1792]{1,0:T(8,128)(2,1)S(1)}, bf16[16,1792]{1,0:T(8,128)(2,1)S(1)}, u32[]{:S(2)}, u32[]{:S(2)}) collective-permute-start(bf16[16,1792]{1,0:T(8,128)(2,1)S(1)} %dynamic-slice_bitcast_fusion.2), channel_id=1, source_target_pairs={{0,1},{1,0},{2,3},{3,2},{4,5},{5,4},{6,7},{7,6},{8,9},{9,8},{10,11... | collective-permute-start | bytes 172040 | tf_op jit(solution)/shard_map/ppermute | solution.py:11
  4.6 0.8 %dynamic-slice_bitcast_fusion.1 = bf16[256,896]{1,0:T(8,128)(2,1)} fusion(bf16[2,256,1792]{2,1,0:T(8,128)(2,1)S(1)} %bitcast.77, s32[]{:T(128)S(6)} %select_n.228, s32[]{:T(128)S(6)} %select_n.232), kind=kLoop, calls=%fused_computation.29 | loop fusion | bytes 917512 | tf_op jit(solution)/shard_map/squeeze | solution.py:73
  5.4 0.5 collective-permute-start.7
  5.9 0.7 fusion.40
  6.6 0.5 collective-permute-done
  7.1 1.9 %collective-permute-start.2 = (bf16[32,1792]{1,0:T(8,128)(2,1)S(1)}, bf16[32,1792]{1,0:T(8,128)(2,1)S(1)}, u32[]{:S(2)}, u32[]{:S(2)}) collective-permute-start(bf16[32,1792]{1,0:T(8,128)(2,1)S(1)} %pad_maximum_fusion.1), channel_id=1, source_target_pairs={{0,2},{1,3},{2,0},{3,1},{4,6},{5,7},{6,4},{7,5},{8,10},{9,11},{10,... | collective-permute-start | bytes 344072 | tf_op jit(solution)/shard_map/ppermute | solution.py:11
  9.0 2.6 %collective-permute-start.3 = (bf16[32,1792]{1,0:T(8,128)(2,1)S(1)}, bf16[32,1792]{1,0:T(8,128)(2,1)S(1)}, u32[]{:S(2)}, u32[]{:S(2)}) collective-permute-start(bf16[32,1792]{1,0:T(8,128)(2,1)S(1)} %pad_maximum_fusion.1), channel_id=1, source_target_pairs={{0,4},{1,5},{2,6},{3,7},{4,0},{5,1},{6,2},{7,3},{8,12},{9,13},{10,... | collective-permute-start | bytes 344072 | tf_op jit(solution)/shard_map/ppermute | solution.py:11
  11.6 1.2 %bitcast_select_fusion.1 = (bf16[1792,128]{1,0:T(8,128)(2,1)S(1)}, bf16[1792,128]{1,0:T(8,128)(2,1)S(1)}) fusion(pred[]{:T(512)S(6)} %eq.70, bf16[3584,128]{1,0:T(8,128)(2,1)S(1)} %collective-permute-done.1, s32[]{:T(128)S(6)} %select_n.216, bf16[1,3584,128]{2,1,0:T(8,128)(2,1)} %param.8), kind=kLoop, calls=%fused_computation.27 | loop fusion | flops 458752 | bytes 1835013 | tf_op jit(solution)/shard_map/jit(_where)/select_n | solution.py:23
  12.8 0.8 %dynamic-slice_bitcast_fusion = bf16[256,896]{1,0:T(8,128)(2,1)} fusion(bf16[2,256,1792]{2,1,0:T(8,128)(2,1)S(1)} %bitcast.75, s32[]{:T(128)S(6)} %select_n.214, s32[]{:T(128)S(6)} %select_n.232), kind=kLoop, calls=%fused_computation.28 | loop fusion | bytes 917512 | tf_op jit(solution)/shard_map/squeeze | solution.py:73
  13.6 2.0 %collective-permute-start.9 = (bf16[256,896]{1,0:T(8,128)(2,1)}, bf16[256,896]{1,0:T(8,128)(2,1)S(1)}, u32[]{:S(2)}, u32[]{:S(2)}) collective-permute-start(bf16[256,896]{1,0:T(8,128)(2,1)} %dynamic-slice_bitcast_fusion), channel_id=1, source_target_pairs={{0,1},{1,0},{2,3},{3,2},{4,5},{5,4},{6,7},{7,6},{8,9},{9,8},{10,11... | collective-permute-start | bytes 1376264 | tf_op jit(solution)/shard_map/ppermute | solution.py:11
  15.6 4.4 %collective-permute-done.3 = bf16[32,1792]{1,0:T(8,128)(2,1)S(1)} collective-permute-done((bf16[32,1792]{1,0:T(8,128)(2,1)S(1)}, bf16[32,1792]{1,0:T(8,128)(2,1)S(1)}, u32[]{:S(2)}, u32[]{:S(2)}) %collective-permute-start.3) | collective-permute-done | bytes 114720 | tf_op jit(solution)/shard_map/ppermute | solution.py:11
  20.1 1.4 %dynamic-slice_bitcast_fusion.3 = (bf16[16,896]{1,0:T(8,128)(2,1)}, bf16[1,16,896]{2,1,0:T(8,128)(2,1)S(1)}, bf16[1,16,896]{2,1,0:T(8,128)(2,1)S(1)}) fusion(bf16[3,16,3584]{2,1,0:T(8,128)(2,1)} %param.7, s32[]{:T(128)S(6)} %select_n.238, s32[]{:T(128)S(6)} %select_n.239, s32[]{:T(128)S(6)} %select_n.240), kind=kLoop, calls=%fused_computation.70 | loop fusion | bytes 172044 | tf_op jit(solution)/shard_map/squeeze | solution.py:98
  21.5 0.6 pad_maximum_fusion.3
  22.1 1.5 %collective-permute-start.13 = (bf16[2,16,896]{2,1,0:T(8,128)(2,1)}, bf16[2,16,896]{2,1,0:T(8,128)(2,1)S(1)}, u32[]{:S(2)}, u32[]{:S(2)}) collective-permute-start(bf16[2,16,896]{2,1,0:T(8,128)(2,1)} %pad_maximum_fusion.3), channel_id=1, source_target_pairs={{0,1},{1,0},{2,3},{3,2},{4,5},{5,4},{6,7},{7,6},{8,9},{9,8},{10,11... | collective-permute-start | bytes 172040 | tf_op jit(solution)/shard_map/ppermute | solution.py:11
  23.6 0.1 collective-permute-start.22
  23.7 0.3 convolution_add_fusion.5
  24.0 0.6 collective-permute-start.5
  24.6 0.7 compare_reduce_fusion
  26.6 2.6 %collective-permute-done.13 = bf16[2,16,896]{2,1,0:T(8,128)(2,1)S(1)} collective-permute-done((bf16[2,16,896]{2,1,0:T(8,128)(2,1)}, bf16[2,16,896]{2,1,0:T(8,128)(2,1)S(1)}, u32[]{:S(2)}, u32[]{:S(2)}) %collective-permute-start.13) | collective-permute-done | bytes 57376 | tf_op jit(solution)/shard_map/ppermute | solution.py:11
  29.2 0.6 slice_bitcast_fusion
  29.9 0.6 collective-permute-start.6
  30.4 0.2 fusion.15
  30.7 3.5 %collective-permute-done.6 = bf16[128,256]{1,0:T(8,128)(2,1)S(1)} collective-permute-done((bf16[128,256]{1,0:T(8,128)(2,1)S(1)}, bf16[128,256]{1,0:T(8,128)(2,1)S(1)}, u32[]{:S(2)}, u32[]{:S(2)}) %collective-permute-start.6) | collective-permute-done | bytes 65568 | tf_op jit(solution)/shard_map/ppermute | solution.py:11
  34.2 0.9 %fusion.2 = bf16[64,896]{1,0:T(8,128)(2,1)} fusion(f32[64,896]{1,0:T(8,128)S(1)} %fusion.15, bf16[64,256]{1,0:T(8,128)(2,1)S(1)} %bitcast.95, bf16[256,896]{1,0:T(8,128)(2,1)S(1)} %collective-permute-done.7), kind=kOutput, calls=%fused_computation.6 | convolution fusion | flops 29474816 | bytes 835584 | tf_op jit(solution)/shard_map/dot_general | solution.py:15
  35.1 1.5 %collective-permute-start.8 = (bf16[64,896]{1,0:T(8,128)(2,1)}, bf16[64,896]{1,0:T(8,128)(2,1)}, u32[]{:S(2)}, u32[]{:S(2)}) collective-permute-start(bf16[64,896]{1,0:T(8,128)(2,1)} %fusion.2), channel_id=1, source_target_pairs={{0,16},{8,24},{16,0},{24,8},{1,17},{9,25},{17,1},{25,9},{2,18},{10... | collective-permute-start | bytes 344072 | tf_op jit(solution)/shard_map/ppermute | solution.py:11
  36.6 0.2 fusion.17
  36.8 1.5 %rev.6 = bf16[4,2,16,256]{3,2,1,0:T(8,128)(2,1)} reverse(bf16[4,2,16,256]{3,2,1,0:T(8,128)(2,1)} %bitcast.89), dimensions={1} | reverse | bytes 131072 | tf_op jit(solution)/shard_map/rev | solution.py:76
  38.3 1.9 %collective-permute-done.8 = bf16[64,896]{1,0:T(8,128)(2,1)} collective-permute-done((bf16[64,896]{1,0:T(8,128)(2,1)}, bf16[64,896]{1,0:T(8,128)(2,1)}, u32[]{:S(2)}, u32[]{:S(2)}) %collective-permute-start.8) | collective-permute-done | bytes 114720 | tf_op jit(solution)/shard_map/ppermute | solution.py:11
  40.2 1.1 %fusion.51 = (bf16[64,896]{1,0:T(8,128)(2,1)S(1)}, f32[64,896]{1,0:T(8,128)S(1)}) fusion(bf16[64,896]{1,0:T(8,128)(2,1)} %collective-permute-done.8, f32[64,896]{1,0:T(8,128)S(1)} %fusion.17, bf16[64,256]{1,0:T(8,128)(2,1)S(1)} %bitcast.93, bf16[256,896]{1,0:T(8,128)(2,1)S(1)} %collective-permute-done.7), kind=kOutput, calls=%fused_computation.100 | convolution fusion | flops 29589504 | bytes 1179648 | tf_op jit(solution)/shard_map/dot_general | solution.py:15
  41.3 0.2 fusion.11
  41.6 0.2 fusion.50
  41.9 3.7 %collective-permute-start.10 = (bf16[32,896]{1,0:T(8,128)(2,1)S(1)}, bf16[32,896]{1,0:T(8,128)(2,1)S(1)}, u32[]{:S(2)}, u32[]{:S(2)}) collective-permute-start(bf16[32,896]{1,0:T(8,128)(2,1)S(1)} %get-tuple-element.40), channel_id=1, source_target_pairs={{0,6},{1,7},{2,4},{3,5},{4,2},{5,3},{6,0},{7,1},{8,14},{9,15},{10,... | collective-permute-start | bytes 172040 | tf_op jit(solution)/shard_map/ppermute | solution.py:11
  45.5 0.8 collective-permute-start.12
  46.3 3.7 %collective-permute-start.14 = (bf16[16,896]{1,0:T(8,128)(2,1)S(1)}, bf16[16,896]{1,0:T(8,128)(2,1)S(1)}, u32[]{:S(2)}, u32[]{:S(2)}) collective-permute-start(bf16[16,896]{1,0:T(8,128)(2,1)S(1)} %get-tuple-element.45), channel_id=1, source_target_pairs={{0,6},{1,7},{2,4},{3,5},{4,2},{5,3},{6,0},{7,1},{8,14},{9,15},{10,... | collective-permute-start | bytes 86024 | tf_op jit(solution)/shard_map/ppermute | solution.py:11
  50.0 0.6 collective-permute-done.11
  50.6 1.8 %collective-permute-start.16 = (bf16[16,896]{1,0:T(8,128)(2,1)S(1)}, bf16[16,896]{1,0:T(8,128)(2,1)S(1)}, u32[]{:S(2)}, u32[]{:S(2)}) collective-permute-start(bf16[16,896]{1,0:T(8,128)(2,1)S(1)} %get-tuple-element.46), channel_id=1, source_target_pairs={{0,2},{1,3},{2,0},{3,1},{4,6},{5,7},{6,4},{7,5},{8,10},{9,11},{10,... | collective-permute-start | bytes 86024 | tf_op jit(solution)/shard_map/ppermute | solution.py:11
  52.5 2.3 %collective-permute-done.15 = bf16[16,896]{1,0:T(8,128)(2,1)S(1)} collective-permute-done((bf16[16,896]{1,0:T(8,128)(2,1)S(1)}, bf16[16,896]{1,0:T(8,128)(2,1)S(1)}, u32[]{:S(2)}, u32[]{:S(2)}) %collective-permute-start.15) | collective-permute-done | bytes 28704 | tf_op jit(solution)/shard_map/ppermute | solution.py:11
  54.8 1.4 %slice_select_fusion.1 = (bf16[16,896]{1,0:T(8,128)(2,1)}, bf16[16,896]{1,0:T(8,128)(2,1)S(1)}) fusion(bf16[32,896]{1,0:T(8,128)(2,1)S(1)} %fusion.27, pred[]{:T(512)S(6)} %eq.69, bf16[2,16,896]{2,1,0:T(8,128)(2,1)S(1)} %copy-done.10, bf16[3,16,3584]{2,1,0:T(8,128)(2,1)} %param.7, s32[]{:T(128)S(6)} %select_n.239, ...), kind=kLoop, calls=%fused_computation.65 | loop fusion | flops 157696 | bytes 288256 | tf_op jit(solution)/shard_map/jit(_where)/select_n | solution.py:142
  56.2 1.5 %collective-permute-start.17 = (bf16[16,896]{1,0:T(8,128)(2,1)S(1)}, bf16[16,896]{1,0:T(8,128)(2,1)S(1)}, u32[]{:S(2)}, u32[]{:S(2)}) collective-permute-start(bf16[16,896]{1,0:T(8,128)(2,1)S(1)} %get-tuple-element.32), channel_id=1, source_target_pairs={{0,2},{1,3},{2,0},{3,1},{4,6},{5,7},{6,4},{7,5},{8,10},{9,11},{10,... | collective-permute-start | bytes 86024 | tf_op jit(solution)/shard_map/ppermute | solution.py:11
  57.7 1.2 %collective-permute-start.18 = (bf16[16,896]{1,0:T(8,128)(2,1)S(1)}, bf16[16,896]{1,0:T(8,128)(2,1)S(1)}, u32[]{:S(2)}, u32[]{:S(2)}) collective-permute-start(bf16[16,896]{1,0:T(8,128)(2,1)S(1)} %get-tuple-element.32), channel_id=1, source_target_pairs={{0,4},{1,5},{2,6},{3,7},{4,0},{5,1},{6,2},{7,3},{8,12},{9,13},{10,... | collective-permute-start | bytes 86024 | tf_op jit(solution)/shard_map/ppermute | solution.py:11
  58.9 1.7 %collective-permute-start.19 = (bf16[16,896]{1,0:T(8,128)(2,1)S(1)}, bf16[16,896]{1,0:T(8,128)(2,1)S(1)}, u32[]{:S(2)}, u32[]{:S(2)}) collective-permute-start(bf16[16,896]{1,0:T(8,128)(2,1)S(1)} %get-tuple-element.32), channel_id=1, source_target_pairs={{0,6},{1,7},{2,4},{3,5},{4,2},{5,3},{6,0},{7,1},{8,14},{9,15},{10,... | collective-permute-start | bytes 86024 | tf_op jit(solution)/shard_map/ppermute | solution.py:11
  60.6 0.6 collective-permute-start.23
  61.2 2.1 %collective-permute-start.24 = (bf16[32,896]{1,0:T(8,128)(2,1)S(1)}, bf16[32,896]{1,0:T(8,128)(2,1)S(1)}, u32[]{:S(2)}, u32[]{:S(2)}) collective-permute-start(bf16[32,896]{1,0:T(8,128)(2,1)S(1)} %fusion.27), channel_id=1, source_target_pairs={{0,4},{1,5},{2,6},{3,7},{4,0},{5,1},{6,2},{7,3},{8,12},{9,13},{10,... | collective-permute-start | bytes 172040 | tf_op jit(solution)/shard_map/ppermute | solution.py:11
  63.3 0.1 collective-permute-done.18
  63.4 1.6 %collective-permute-start.25 = (bf16[32,896]{1,0:T(8,128)(2,1)S(1)}, bf16[32,896]{1,0:T(8,128)(2,1)S(1)}, u32[]{:S(2)}, u32[]{:S(2)}) collective-permute-start(bf16[32,896]{1,0:T(8,128)(2,1)S(1)} %fusion.27), channel_id=1, source_target_pairs={{0,6},{1,7},{2,4},{3,5},{4,2},{5,3},{6,0},{7,1},{8,14},{9,15},{10,... | collective-permute-start | bytes 172040 | tf_op jit(solution)/shard_map/ppermute | solution.py:11
  65.0 0.5 collective-permute-start.21
  65.6 1.6 %collective-permute-start.20 = (bf16[64,896]{1,0:T(8,128)(2,1)S(1)}, bf16[64,896]{1,0:T(8,128)(2,1)S(1)}, u32[]{:S(2)}, u32[]{:S(2)}) collective-permute-start(bf16[64,896]{1,0:T(8,128)(2,1)S(1)} %pad_maximum_fusion.2), channel_id=1, source_target_pairs={{0,16},{8,24},{16,0},{24,8},{1,17},{9,25},{17,1},{25,9},{2,18},{10... | collective-permute-start | bytes 344072 | tf_op jit(solution)/shard_map/ppermute | solution.py:11
  67.2 1.3 %broadcast_select_fusion.1 = (bf16[128,1792]{1,0:T(8,128)(2,1)S(1)}, bf16[128,1792]{1,0:T(8,128)(2,1)S(1)}) fusion(bf16[128,1792]{1,0:T(8,128)(2,1)} %copy-done.1, bf16[128,1792]{1,0:T(8,128)(2,1)} %collective-permute-done.22, pred[]{:T(512)S(6)} %eq.70), kind=kLoop, calls=%fused_computation.31 | loop fusion | flops 458752 | bytes 1835009 | tf_op jit(solution)/shard_map/jit(_where)/select_n | solution.py:23
  68.5 0.9 %collective-permute-done.25 = bf16[32,896]{1,0:T(8,128)(2,1)S(1)} collective-permute-done((bf16[32,896]{1,0:T(8,128)(2,1)S(1)}, bf16[32,896]{1,0:T(8,128)(2,1)S(1)}, u32[]{:S(2)}, u32[]{:S(2)}) %collective-permute-start.25) | collective-permute-done | bytes 57376 | tf_op jit(solution)/shard_map/ppermute | solution.py:11
  69.3 0.3 fusion.32
  69.6 0.8 collective-permute-done.20
  70.5 0.3 fusion.13
  70.8 0.3 convolution_add_fusion.4
  71.2 0.3 fusion.3
  71.5 1.6 %collective-permute-start.27 = (bf16[128,128]{1,0:T(8,128)(2,1)S(1)}, bf16[128,128]{1,0:T(8,128)(2,1)S(1)}, u32[]{:S(2)}, u32[]{:S(2)}) collective-permute-start(bf16[128,128]{1,0:T(8,128)(2,1)S(1)} %get-tuple-element.48), channel_id=1, source_target_pairs={{0,1},{1,0},{2,3},{3,2},{4,5},{5,4},{6,7},{7,6},{8,9},{9,8},{10,11... | collective-permute-start | bytes 98312 | tf_op jit(solution)/shard_map/ppermute | solution.py:11
  73.1 0.4 collective-permute-start.28
  73.5 0.8 broadcast_select_fusion.9
  74.2 0.6 maximum_bitcast_fusion
  74.9 0.7 collective-permute-done.27
  75.5 0.9 %collective-permute-done.28 = bf16[128,128]{1,0:T(8,128)(2,1)S(1)} collective-permute-done((bf16[128,128]{1,0:T(8,128)(2,1)S(1)}, bf16[128,128]{1,0:T(8,128)(2,1)S(1)}, u32[]{:S(2)}, u32[]{:S(2)}) %collective-permute-start.28) | collective-permute-done | bytes 32800 | tf_op jit(solution)/shard_map/ppermute | solution.py:157
  76.4 1.4 %fusion.46 = (f32[128]{0:T(128)}, bf16[128,128]{1,0:T(8,128)(2,1)S(1)}) fusion(f32[]{:T(128)S(6)} %select_n.259, bf16[128,128]{1,0:T(8,128)(2,1)S(1)} %collective-permute-done.28, bf16[128,128]{1,0:T(8,128)(2,1)S(1)} %collective-permute-done.27, f32[128,128]{1,0:T(8,128)} %collective-permute-done.26, f32[128,256]{1,0:T(8,128)S(1)} %convolution_add_fusion.4, ...), kind=kLoop, calls=%fused_computation.96 | loop fusion | flops 147328 | bytes 295429 | tf_op jit(solution)/shard_map/reduce_sum | solution.py:159
  77.8 1.4 %fusion = bf16[1,3584,128]{2,1,0:T(8,128)(2,1)} fusion(bf16[128,1792]{1,0:T(8,128)(2,1)S(1)} %get-tuple-element.36, bf16[128,1792]{1,0:T(8,128)(2,1)S(1)} %get-tuple-element.35, bf16[128,128]{1,0:T(8,128)(2,1)S(1)} %get-tuple-element.30), kind=kOutput, calls=%fused_computation.1 | convolution fusion | flops 119734272 | bytes 1867776 | tf_op jit(solution)/shard_map/dot_general | solution.py:48
  (64 shorter events, 0.4 us)
Async XLA Ops:
  0.6 4.0 %copy-start = (bf16[1,2,2,128,1792]{4,3,2,1,0:T(8,128)(2,1)S(1)}, bf16[1,2,2,128,1792]{4,3,2,1,0:T(8,128)(2,1)}, u32[]{:S(2)}) copy-start(bf16[1,2,2,128,1792]{4,3,2,1,0:T(8,128)(2,1)} %param.10) | copy-start | bytes 5505028
  0.6 6.4 %collective-permute-start.1 = (bf16[3584,128]{1,0:T(8,128)(2,1)}, bf16[3584,128]{1,0:T(8,128)(2,1)S(1)}, u32[]{:S(2)}, u32[]{:S(2)}) collective-permute-start(bf16[3584,128]{1,0:T(8,128)(2,1)} %bitcast.91), channel_id=1, source_target_pairs={{0,8},{8,0},{16,24},{24,16},{1,9},{9,1},{17,25},{25,17},{2,10},{10... | collective-permute-start | bytes 2752520 | tf_op jit(solution)/shard_map/ppermute | solution.py:11
  2.0 5.0 %collective-permute-start = (bf16[16,1792]{1,0:T(8,128)(2,1)S(1)}, bf16[16,1792]{1,0:T(8,128)(2,1)S(1)}, u32[]{:S(2)}, u32[]{:S(2)}) collective-permute-start(bf16[16,1792]{1,0:T(8,128)(2,1)S(1)} %dynamic-slice_bitcast_fusion.2), channel_id=1, source_target_pairs={{0,1},{1,0},{2,3},{3,2},{4,5},{5,4},{6,7},{7,6},{8,9},{9,8},{10,11... | collective-permute-start | bytes 172040 | tf_op jit(solution)/shard_map/ppermute | solution.py:11
  5.4 28.8 %collective-permute-start.7 = (bf16[256,896]{1,0:T(8,128)(2,1)}, bf16[256,896]{1,0:T(8,128)(2,1)S(1)}, u32[]{:S(2)}, u32[]{:S(2)}) collective-permute-start(bf16[256,896]{1,0:T(8,128)(2,1)} %dynamic-slice_bitcast_fusion.1), channel_id=1, source_target_pairs={{0,1},{1,0},{2,3},{3,2},{4,5},{5,4},{6,7},{7,6},{8,9},{9,8},{10,11... | collective-permute-start | bytes 1376264 | tf_op jit(solution)/shard_map/ppermute | solution.py:11
  7.1 8.5 %collective-permute-start.2 = (bf16[32,1792]{1,0:T(8,128)(2,1)S(1)}, bf16[32,1792]{1,0:T(8,128)(2,1)S(1)}, u32[]{:S(2)}, u32[]{:S(2)}) collective-permute-start(bf16[32,1792]{1,0:T(8,128)(2,1)S(1)} %pad_maximum_fusion.1), channel_id=1, source_target_pairs={{0,2},{1,3},{2,0},{3,1},{4,6},{5,7},{6,4},{7,5},{8,10},{9,11},{10,... | collective-permute-start | bytes 344072 | tf_op jit(solution)/shard_map/ppermute | solution.py:11
  9.0 11.1 %collective-permute-start.3 = (bf16[32,1792]{1,0:T(8,128)(2,1)S(1)}, bf16[32,1792]{1,0:T(8,128)(2,1)S(1)}, u32[]{:S(2)}, u32[]{:S(2)}) collective-permute-start(bf16[32,1792]{1,0:T(8,128)(2,1)S(1)} %pad_maximum_fusion.1), channel_id=1, source_target_pairs={{0,4},{1,5},{2,6},{3,7},{4,0},{5,1},{6,2},{7,3},{8,12},{9,13},{10,... | collective-permute-start | bytes 344072 | tf_op jit(solution)/shard_map/ppermute | solution.py:11
  11.6 8.5 %collective-permute-start.4 = (bf16[32,1792]{1,0:T(8,128)(2,1)S(1)}, bf16[32,1792]{1,0:T(8,128)(2,1)S(1)}, u32[]{:S(2)}, u32[]{:S(2)}) collective-permute-start(bf16[32,1792]{1,0:T(8,128)(2,1)S(1)} %pad_maximum_fusion.1), channel_id=1, source_target_pairs={{0,6},{1,7},{2,4},{3,5},{4,2},{5,3},{6,0},{7,1},{8,14},{9,15},{10,... | collective-permute-start | bytes 344072 | tf_op jit(solution)/shard_map/ppermute | solution.py:11
  13.6 11.0 %copy-start.11 = (s32[2,1,12]{2,1,0:T(1,128)S(1)}, s32[2,1,12]{2,1,0:T(1,128)}, u32[]{:S(2)}) copy-start(s32[2,1,12]{2,1,0:T(1,128)} %param.11) | copy-start | bytes 292
  13.6 28.0 %collective-permute-start.9 = (bf16[256,896]{1,0:T(8,128)(2,1)}, bf16[256,896]{1,0:T(8,128)(2,1)S(1)}, u32[]{:S(2)}, u32[]{:S(2)}) collective-permute-start(bf16[256,896]{1,0:T(8,128)(2,1)} %dynamic-slice_bitcast_fusion), channel_id=1, source_target_pairs={{0,1},{1,0},{2,3},{3,2},{4,5},{5,4},{6,7},{7,6},{8,9},{9,8},{10,11... | collective-permute-start | bytes 1376264 | tf_op jit(solution)/shard_map/ppermute | solution.py:11
  22.1 7.1 %collective-permute-start.13 = (bf16[2,16,896]{2,1,0:T(8,128)(2,1)}, bf16[2,16,896]{2,1,0:T(8,128)(2,1)S(1)}, u32[]{:S(2)}, u32[]{:S(2)}) collective-permute-start(bf16[2,16,896]{2,1,0:T(8,128)(2,1)} %pad_maximum_fusion.3), channel_id=1, source_target_pairs={{0,1},{1,0},{2,3},{3,2},{4,5},{5,4},{6,7},{7,6},{8,9},{9,8},{10,11... | collective-permute-start | bytes 172040 | tf_op jit(solution)/shard_map/ppermute | solution.py:11
  23.6 11.4 %copy-start.1 = (bf16[128,1792]{1,0:T(8,128)(2,1)}, bf16[128,1792]{1,0:T(8,128)(2,1)S(1)}, u32[]{:S(2)}) copy-start(bf16[128,1792]{1,0:T(8,128)(2,1)S(1)} %constant_dynamic-update-slice_fusion) | copy-start | bytes 1376260
  23.6 41.9 %collective-permute-start.22 = (bf16[128,1792]{1,0:T(8,128)(2,1)S(1)}, bf16[128,1792]{1,0:T(8,128)(2,1)}, u32[]{:S(2)}, u32[]{:S(2)}) collective-permute-start(bf16[128,1792]{1,0:T(8,128)(2,1)S(1)} %constant_dynamic-update-slice_fusion), channel_id=1, source_target_pairs={{0,8},{8,0},{16,24},{24,16},{1,9},{9,1},{17,25},{25,17},{2,10},{10... | collective-permute-start | bytes 1376264 | tf_op jit(solution)/shard_map/ppermute | solution.py:11
  24.0 5.8 %collective-permute-start.5 = (f32[128,256]{1,0:T(8,128)S(1)}, f32[128,256]{1,0:T(8,128)S(1)}, u32[]{:S(2)}, u32[]{:S(2)}) collective-permute-start(f32[128,256]{1,0:T(8,128)S(1)} %convolution_add_fusion.5), channel_id=1, source_target_pairs={{0,8},{8,0},{16,24},{24,16},{1,9},{9,1},{17,25},{25,17},{2,10},{10... | collective-permute-start | bytes 393224 | tf_op jit(solution)/shard_map/ppermute | solution.py:11
  29.2 0.6 copy-start.9
  29.9 4.3 %collective-permute-start.6 = (bf16[128,256]{1,0:T(8,128)(2,1)S(1)}, bf16[128,256]{1,0:T(8,128)(2,1)S(1)}, u32[]{:S(2)}, u32[]{:S(2)}) collective-permute-start(bf16[128,256]{1,0:T(8,128)(2,1)S(1)} %multiply_convert_fusion), channel_id=1, source_target_pairs={{0,1},{1,0},{2,3},{3,2},{4,5},{5,4},{6,7},{7,6},{8,9},{9,8},{10,11... | collective-permute-start | bytes 196616 | tf_op jit(solution)/shard_map/ppermute | solution.py:11
  34.2 2.4 %copy-start.5 = (bf16[128,256]{1,0:T(8,128)(2,1)}, bf16[128,256]{1,0:T(8,128)(2,1)S(1)}, u32[]{:S(2)}) copy-start(bf16[128,256]{1,0:T(8,128)(2,1)S(1)} %collective-permute-done.6) | copy-start | bytes 196612
  35.1 5.1 %collective-permute-start.8 = (bf16[64,896]{1,0:T(8,128)(2,1)}, bf16[64,896]{1,0:T(8,128)(2,1)}, u32[]{:S(2)}, u32[]{:S(2)}) collective-permute-start(bf16[64,896]{1,0:T(8,128)(2,1)} %fusion.2), channel_id=1, source_target_pairs={{0,16},{8,24},{16,0},{24,8},{1,17},{9,25},{17,1},{25,9},{2,18},{10... | collective-permute-start | bytes 344072 | tf_op jit(solution)/shard_map/ppermute | solution.py:11
  38.3 3.3 %copy-start.4 = (bf16[4,2,16,256]{3,2,1,0:T(8,128)(2,1)S(1)}, bf16[4,2,16,256]{3,2,1,0:T(8,128)(2,1)}, u32[]{:S(2)}) copy-start(bf16[4,2,16,256]{3,2,1,0:T(8,128)(2,1)} %rev.6) | copy-start | bytes 196612
  41.3 11.1 %copy-start.7 = (bf16[16,896]{1,0:T(8,128)(2,1)S(1)}, bf16[16,896]{1,0:T(8,128)(2,1)}, u32[]{:S(2)}) copy-start(bf16[16,896]{1,0:T(8,128)(2,1)} %slice_bitcast_fusion) | copy-start | bytes 86020
  41.3 11.1 %copy-start.8 = (bf16[16,896]{1,0:T(8,128)(2,1)S(1)}, bf16[16,896]{1,0:T(8,128)(2,1)}, u32[]{:S(2)}) copy-start(bf16[16,896]{1,0:T(8,128)(2,1)} %get-tuple-element.37) | copy-start | bytes 86020
  41.3 13.5 %copy-start.10 = (bf16[2,16,896]{2,1,0:T(8,128)(2,1)S(1)}, bf16[2,16,896]{2,1,0:T(8,128)(2,1)}, u32[]{:S(2)}) copy-start(bf16[2,16,896]{2,1,0:T(8,128)(2,1)} %copy-done.9) | copy-start | bytes 172036
  41.6 24.0 %copy-start.2 = (bf16[256,896]{1,0:T(8,128)(2,1)}, bf16[256,896]{1,0:T(8,128)(2,1)S(1)}, u32[]{:S(2)}) copy-start(bf16[256,896]{1,0:T(8,128)(2,1)S(1)} %collective-permute-done.9) | copy-start | bytes 1376260
  41.9 8.1 %collective-permute-start.10 = (bf16[32,896]{1,0:T(8,128)(2,1)S(1)}, bf16[32,896]{1,0:T(8,128)(2,1)S(1)}, u32[]{:S(2)}, u32[]{:S(2)}) collective-permute-start(bf16[32,896]{1,0:T(8,128)(2,1)S(1)} %get-tuple-element.40), channel_id=1, source_target_pairs={{0,6},{1,7},{2,4},{3,5},{4,2},{5,3},{6,0},{7,1},{8,14},{9,15},{10,... | collective-permute-start | bytes 172040 | tf_op jit(solution)/shard_map/ppermute | solution.py:11
  45.5 5.1 %collective-permute-start.11 = (bf16[32,896]{1,0:T(8,128)(2,1)S(1)}, bf16[32,896]{1,0:T(8,128)(2,1)S(1)}, u32[]{:S(2)}, u32[]{:S(2)}) collective-permute-start(bf16[32,896]{1,0:T(8,128)(2,1)S(1)} %get-tuple-element.42), channel_id=1, source_target_pairs={{0,4},{1,5},{2,6},{3,7},{4,0},{5,1},{6,2},{7,3},{8,12},{9,13},{10,... | collective-permute-start | bytes 172040 | tf_op jit(solution)/shard_map/ppermute | solution.py:11
  45.5 6.9 %collective-permute-start.12 = (bf16[32,896]{1,0:T(8,128)(2,1)S(1)}, bf16[32,896]{1,0:T(8,128)(2,1)S(1)}, u32[]{:S(2)}, u32[]{:S(2)}) collective-permute-start(bf16[32,896]{1,0:T(8,128)(2,1)S(1)} %get-tuple-element.41), channel_id=1, source_target_pairs={{0,2},{1,3},{2,0},{3,1},{4,6},{5,7},{6,4},{7,5},{8,10},{9,11},{10,... | collective-permute-start | bytes 172040 | tf_op jit(solution)/shard_map/ppermute | solution.py:11
  46.3 6.1 %collective-permute-start.14 = (bf16[16,896]{1,0:T(8,128)(2,1)S(1)}, bf16[16,896]{1,0:T(8,128)(2,1)S(1)}, u32[]{:S(2)}, u32[]{:S(2)}) collective-permute-start(bf16[16,896]{1,0:T(8,128)(2,1)S(1)} %get-tuple-element.45), channel_id=1, source_target_pairs={{0,6},{1,7},{2,4},{3,5},{4,2},{5,3},{6,0},{7,1},{8,14},{9,15},{10,... | collective-permute-start | bytes 86024 | tf_op jit(solution)/shard_map/ppermute | solution.py:11
  50.0 4.8 %collective-permute-start.15 = (bf16[16,896]{1,0:T(8,128)(2,1)S(1)}, bf16[16,896]{1,0:T(8,128)(2,1)S(1)}, u32[]{:S(2)}, u32[]{:S(2)}) collective-permute-start(bf16[16,896]{1,0:T(8,128)(2,1)S(1)} %get-tuple-element.47), channel_id=1, source_target_pairs={{0,4},{1,5},{2,6},{3,7},{4,0},{5,1},{6,2},{7,3},{8,12},{9,13},{10,... | collective-permute-start | bytes 86024 | tf_op jit(solution)/shard_map/ppermute | solution.py:11
  50.6 4.2 %collective-permute-start.16 = (bf16[16,896]{1,0:T(8,128)(2,1)S(1)}, bf16[16,896]{1,0:T(8,128)(2,1)S(1)}, u32[]{:S(2)}, u32[]{:S(2)}) collective-permute-start(bf16[16,896]{1,0:T(8,128)(2,1)S(1)} %get-tuple-element.46), channel_id=1, source_target_pairs={{0,2},{1,3},{2,0},{3,1},{4,6},{5,7},{6,4},{7,5},{8,10},{9,11},{10,... | collective-permute-start | bytes 86024 | tf_op jit(solution)/shard_map/ppermute | solution.py:11
  56.2 5.0 %collective-permute-start.17 = (bf16[16,896]{1,0:T(8,128)(2,1)S(1)}, bf16[16,896]{1,0:T(8,128)(2,1)S(1)}, u32[]{:S(2)}, u32[]{:S(2)}) collective-permute-start(bf16[16,896]{1,0:T(8,128)(2,1)S(1)} %get-tuple-element.32), channel_id=1, source_target_pairs={{0,2},{1,3},{2,0},{3,1},{4,6},{5,7},{6,4},{7,5},{8,10},{9,11},{10,... | collective-permute-start | bytes 86024 | tf_op jit(solution)/shard_map/ppermute | solution.py:11
  57.7 5.7 %collective-permute-start.18 = (bf16[16,896]{1,0:T(8,128)(2,1)S(1)}, bf16[16,896]{1,0:T(8,128)(2,1)S(1)}, u32[]{:S(2)}, u32[]{:S(2)}) collective-permute-start(bf16[16,896]{1,0:T(8,128)(2,1)S(1)} %get-tuple-element.32), channel_id=1, source_target_pairs={{0,4},{1,5},{2,6},{3,7},{4,0},{5,1},{6,2},{7,3},{8,12},{9,13},{10,... | collective-permute-start | bytes 86024 | tf_op jit(solution)/shard_map/ppermute | solution.py:11
  58.9 6.1 %collective-permute-start.19 = (bf16[16,896]{1,0:T(8,128)(2,1)S(1)}, bf16[16,896]{1,0:T(8,128)(2,1)S(1)}, u32[]{:S(2)}, u32[]{:S(2)}) collective-permute-start(bf16[16,896]{1,0:T(8,128)(2,1)S(1)} %get-tuple-element.32), channel_id=1, source_target_pairs={{0,6},{1,7},{2,4},{3,5},{4,2},{5,3},{6,0},{7,1},{8,14},{9,15},{10,... | collective-permute-start | bytes 86024 | tf_op jit(solution)/shard_map/ppermute | solution.py:11
  60.6 7.8 %collective-permute-start.23 = (bf16[32,896]{1,0:T(8,128)(2,1)S(1)}, bf16[32,896]{1,0:T(8,128)(2,1)S(1)}, u32[]{:S(2)}, u32[]{:S(2)}) collective-permute-start(bf16[32,896]{1,0:T(8,128)(2,1)S(1)} %fusion.27), channel_id=1, source_target_pairs={{0,2},{1,3},{2,0},{3,1},{4,6},{5,7},{6,4},{7,5},{8,10},{9,11},{10,... | collective-permute-start | bytes 172040 | tf_op jit(solution)/shard_map/ppermute | solution.py:11
  61.2 7.3 %collective-permute-start.24 = (bf16[32,896]{1,0:T(8,128)(2,1)S(1)}, bf16[32,896]{1,0:T(8,128)(2,1)S(1)}, u32[]{:S(2)}, u32[]{:S(2)}) collective-permute-start(bf16[32,896]{1,0:T(8,128)(2,1)S(1)} %fusion.27), channel_id=1, source_target_pairs={{0,4},{1,5},{2,6},{3,7},{4,0},{5,1},{6,2},{7,3},{8,12},{9,13},{10,... | collective-permute-start | bytes 172040 | tf_op jit(solution)/shard_map/ppermute | solution.py:11
  63.4 6.0 %collective-permute-start.25 = (bf16[32,896]{1,0:T(8,128)(2,1)S(1)}, bf16[32,896]{1,0:T(8,128)(2,1)S(1)}, u32[]{:S(2)}, u32[]{:S(2)}) collective-permute-start(bf16[32,896]{1,0:T(8,128)(2,1)S(1)} %fusion.27), channel_id=1, source_target_pairs={{0,6},{1,7},{2,4},{3,5},{4,2},{5,3},{6,0},{7,1},{8,14},{9,15},{10,... | collective-permute-start | bytes 172040 | tf_op jit(solution)/shard_map/ppermute | solution.py:11
  65.0 8.5 %collective-permute-start.21 = (bf16[16,896]{1,0:T(8,128)(2,1)}, bf16[16,896]{1,0:T(8,128)(2,1)}, u32[]{:S(2)}, u32[]{:S(2)}) collective-permute-start(bf16[16,896]{1,0:T(8,128)(2,1)} %get-tuple-element.31), channel_id=1, source_target_pairs={{0,1},{1,0},{2,3},{3,2},{4,5},{5,4},{6,7},{7,6},{8,9},{9,8},{10,11... | collective-permute-start | bytes 86024 | tf_op jit(solution)/shard_map/ppermute | solution.py:11
  65.6 4.9 %collective-permute-start.20 = (bf16[64,896]{1,0:T(8,128)(2,1)S(1)}, bf16[64,896]{1,0:T(8,128)(2,1)S(1)}, u32[]{:S(2)}, u32[]{:S(2)}) collective-permute-start(bf16[64,896]{1,0:T(8,128)(2,1)S(1)} %pad_maximum_fusion.2), channel_id=1, source_target_pairs={{0,16},{8,24},{16,0},{24,8},{1,17},{9,25},{17,1},{25,9},{2,18},{10... | collective-permute-start | bytes 344072 | tf_op jit(solution)/shard_map/ppermute | solution.py:11
  67.2 2.2 %copy-start.3 = (bf16[256,896]{1,0:T(8,128)(2,1)S(1)}, bf16[256,896]{1,0:T(8,128)(2,1)}, u32[]{:S(2)}) copy-start(bf16[256,896]{1,0:T(8,128)(2,1)} %copy-done.2) | copy-start | bytes 1376260
  70.4 1.1 %copy-start.6 = (bf16[64,896]{1,0:T(8,128)(2,1)}, bf16[64,896]{1,0:T(8,128)(2,1)S(1)}, u32[]{:S(2)}) copy-start(bf16[64,896]{1,0:T(8,128)(2,1)S(1)} %collective-permute-done.20) | copy-start | bytes 344068
  71.1 5.3 %collective-permute-start.26 = (f32[128,128]{1,0:T(8,128)S(1)}, f32[128,128]{1,0:T(8,128)}, u32[]{:S(2)}, u32[]{:S(2)}) collective-permute-start(f32[128,128]{1,0:T(8,128)S(1)} %slice_select_fusion), channel_id=1, source_target_pairs={{0,8},{8,0},{16,24},{24,16},{1,9},{9,1},{17,25},{25,17},{2,10},{10... | collective-permute-start | bytes 196616 | tf_op jit(solution)/shard_map/ppermute | solution.py:11
  71.5 4.0 %collective-permute-start.27 = (bf16[128,128]{1,0:T(8,128)(2,1)S(1)}, bf16[128,128]{1,0:T(8,128)(2,1)S(1)}, u32[]{:S(2)}, u32[]{:S(2)}) collective-permute-start(bf16[128,128]{1,0:T(8,128)(2,1)S(1)} %get-tuple-element.48), channel_id=1, source_target_pairs={{0,1},{1,0},{2,3},{3,2},{4,5},{5,4},{6,7},{7,6},{8,9},{9,8},{10,11... | collective-permute-start | bytes 98312 | tf_op jit(solution)/shard_map/ppermute | solution.py:11
  73.1 3.3 %collective-permute-start.28 = (bf16[128,128]{1,0:T(8,128)(2,1)S(1)}, bf16[128,128]{1,0:T(8,128)(2,1)S(1)}, u32[]{:S(2)}, u32[]{:S(2)}) collective-permute-start(bf16[128,128]{1,0:T(8,128)(2,1)S(1)} %get-tuple-element.49), channel_id=1, source_target_pairs={{0,9},{1,8},{2,11},{3,10},{4,13},{5,12},{6,15},{7,14},{8,1},{9,0},... | collective-permute-start | bytes 98312 | tf_op jit(solution)/shard_map/ppermute | solution.py:157

commit v5 on v4

--- a/solution.py
+++ b/solution.py
@@ -1,6 +1,8 @@
 import jax
 import jax.numpy as jnp
 from jax import lax
+from jax.experimental import pallas as pl
+from jax.experimental.pallas import tpu as pltpu
 from jax.sharding import PartitionSpec as P
 
 BLOCK = 128
@@ -35,6 +37,36 @@
     return out
 
 
+def side_by_side(half_ref, mine_ref, other_ref, out_ref, sems):
+    rows, latents = out_ref.shape[0], mine_ref.shape[1]
+    half = half_ref[0]
+    here = pl.ds(pl.multiple_of(half * rows, rows), rows)
+    copies = []
+    for i, (ref, place) in enumerate(((mine_ref, half), (other_ref, 1 - half))):
+        columns = pl.ds(pl.multiple_of(place * latents, latents), latents)
+        copies.append(pltpu.make_async_copy(ref.at[here], out_ref.at[:, columns], sems.at[i]))
+        copies[-1].start()
+    for copy in copies:
+        copy.wait()
+
+
+def paired_weights(weight, weight_other, half, cols):
+    latents = weight.shape[1]
+    return pl.pallas_call(
+        side_by_side,
+        out_shape=jax.ShapeDtypeStruct((cols, 2 * latents), weight.dtype),
+        in_specs=[
+            pl.BlockSpec(memory_space=pltpu.SMEM),
+            pl.BlockSpec(memory_space=pl.ANY),
+            pl.BlockSpec(memory_space=pl.ANY),
+        ],
+        out_specs=pl.BlockSpec(memory_space=pltpu.VMEM),
+        scratch_shapes=[pltpu.SemaphoreType.DMA((2,))],
+        cost_estimate=pl.CostEstimate(flops=2 * 10**10, bytes_accessed=4 * cols * latents * 2, transcendentals=0),
+        name="paired_weights",
+    )(half.reshape(1), weight, weight_other)
+
+
 def half_preacts(resid_half, weight, weight_other, bias, half):
     cols = resid_half.shape[1]
     mine = lax.dynamic_slice_in_dim(weight, half * cols, cols, 0)
@@ -50,6 +82,7 @@
 
 
 def two_layers(resid, target, enc_weight, enc_bias, dec_weight, blocks):
+    hold = lax.optimization_barrier
     slots = lax.axis_size("latent")
     far = slots // 2
     layer, half = lax.axis_index("layer") // 2, lax.axis_index("layer") % 2
@@ -69,93 +102,92 @@
             out[k] = crossed(block, "latent", 2 * k)
         return out
 
+    def sent_along_z(total):
+        count = total.shape[0] // far
+        pieces = [total[k * count:(k + 1) * count].astype(BF16) for k in range(1, far)]
+        return [crossed(pieces[k - 1], "latent", 2 * k) for k in range(1, far)] + [total[:count]]
+
+    def added(terms):
+        return sum(term.astype(F32) for term in terms[::-1])
+
     def decoder_part(decoder, which, where):
         return lax.dynamic_slice(decoder, (which, 0, where * part), (1, 2 * latents, part))[0]
 
-    def turned(array):
-        return array.reshape(far, 2, rows, array.shape[1])[:, ::-1].reshape(array.shape)
+    def ordered(which, lower, upper, axis=0):
+        return jnp.concatenate([jnp.where(which == 0, lower, upper), jnp.where(which == 0, upper, lower)], axis=axis)
+
+    def rows_at(array, which):
+        split = array.reshape(-1, 2, rows, array.shape[1])
+        return jnp.where(which == 0, split[:, 0], split[:, 1]).reshape(-1, array.shape[1])
 
     weight_other = crossed(enc_weight[0], "layer", 1)
     mine = lax.dynamic_slice(resid, (layer, 0, half * cols), (1, rows, cols))[0]
-    pair = jnp.concatenate([mine, over_x(mine)], axis=0)
-    pair, weight_other, later = lax.optimization_barrier((pair, weight_other, decoder))
+    pair, weight_other, later, target, blocks = hold(
+        (ordered(side, mine, over_x(mine)), weight_other, decoder, target, blocks)
+    )
+    weight_pair = paired_weights(enc_weight[0], weight_other, half, cols)
     column = along_z(pair)
 
     shared_other = over_x(decoder_part(decoder, 1 - layer, 1 - side))
     own_other = over_x(decoder_part(later, layer, 1 - side))
-    decoder, target, blocks, *column = lax.optimization_barrier((decoder, target, blocks, *column))
+
+    def aims_for(where):
+        start = half * cols + where * part
+        own = lax.dynamic_slice(target, (2 * layer, 0, start), (1, rows, part))
+        return jnp.concatenate([own, lax.dynamic_slice(target, (1, 0, start), (1, rows, part))], axis=0)
+
+    aims, aims_other = aims_for(side), over_x(aims_for(1 - side))
+    decoder, aims_other, shared_other, *column = hold((decoder, aims_other, shared_other, *column))
     shared_mine, own_mine = decoder_part(decoder, 1 - layer, side), decoder_part(decoder, layer, side)
     resid_half = jnp.concatenate(column, axis=0)
     firing = gates(blocks, layer, slot, slots, latents, tokens)
     gate = jnp.where(half == 0, firing[0], firing[1])
 
-    def aims_for(where):
-        start = half * cols + where * part
-        own = lax.dynamic_slice(target, (2 * layer, 0, start), (1, rows, part))
-        return jnp.concatenate([own, lax.dynamic_slice(target, (1, 0, start), (1, rows, part))], axis=0)
-
-    aims, aims_other = aims_for(side), over_x(aims_for(1 - side))
-    aim_own = jnp.concatenate([aims[0], aims_other[0]], axis=0).astype(F32)
-    aim_shared = jnp.where(layer == 0, aims[1], aims_other[1]).astype(F32)
-
-    partial = half_preacts(resid_half, enc_weight[0], weight_other, enc_bias[0], half)
+    bias_pair = ordered(half, enc_bias[0], jnp.zeros_like(enc_bias[0]))
+    partial = times(resid_half, weight_pair) + bias_pair
     acts = ((partial + crossed(partial, "layer", 1)) * jnp.concatenate(firing, axis=1)).astype(BF16)
-    acts_other = turned(over_x(acts))
-    resid_other = crossed(resid_half, "layer", 1)
-
-    def rows_of(array, which):
-        split = array.reshape(far, 2, rows, array.shape[1])
-        return jnp.where(which == 0, split[:, 0], split[:, 1]).reshape(tokens // 2, array.shape[1])
-
-    def kept(array):
-        return rows_of(array, layer)
-
-    def left(array):
-        return rows_of(array, 1 - layer)
-
-    leaving = times(left(acts), shared_mine) + times(left(acts_other), shared_other)
-    staying = times(kept(acts), shared_mine) + times(kept(acts_other), shared_other)
-    staying = staying + crossed(leaving.astype(BF16), "layer", 2).astype(F32)
-    sum_shared = staying[:rows]
-    for k in range(far - 1, 0, -1):
-        piece = staying[k * rows:(k + 1) * rows].astype(BF16)
-        sum_shared = sum_shared + crossed(piece, "latent", 2 * k).astype(F32)
-    err_shared = (sum_shared - aim_shared).astype(BF16)
-
-    acts, acts_other, staying = lax.optimization_barrier((acts, acts_other, staying))
+    acts_other = over_x(acts)
+    resid_swapped, _ = hold((resid_half, acts_other))
+    resid_other = crossed(resid_swapped, "layer", 1)
+    aim_own = ordered(side, aims[0], aims_other[0]).astype(F32)
+    aim_shared = jnp.where(layer == side, aims[1], aims_other[1]).astype(F32)
+
+    leaving = times(rows_at(acts, 1 - layer), shared_mine) + times(rows_at(acts_other, 1 - layer), shared_other)
+    staying = times(rows_at(acts, layer), shared_mine) + times(rows_at(acts_other, layer), shared_other)
+    arrived = crossed(leaving.astype(BF16), "layer", 2)
     product = times(acts, own_mine) + times(acts_other, own_other)
-    sum_own = product[:2 * rows]
-    for k in range(far - 1, 0, -1):
-        piece = product[2 * k * rows:2 * (k + 1) * rows].astype(BF16)
-        sum_own = sum_own + crossed(piece, "latent", 2 * k).astype(F32)
-    err_own = (sum_own - aim_own).astype(BF16)
+    arrived, staying = hold((arrived, staying))
+    shared_terms = sent_along_z(staying + arrived.astype(F32))
+    own_terms = sent_along_z(product)
+    err_shared = (added(shared_terms) - aim_shared).astype(BF16)
+    err_own = (added(own_terms) - aim_own).astype(BF16)
 
     shared_near = jnp.concatenate(along_z(err_shared), axis=0)
     shared_far = crossed(shared_near, "layer", 2)
-    halves = [block.reshape(far, 1, rows, part) for block in (shared_near, shared_far)]
-    errs_shared = jnp.where(
-        layer == 0, jnp.concatenate(halves, axis=1), jnp.concatenate(halves[::-1], axis=1)
-    ).reshape(tokens, part)
+    pairs = [block.reshape(far, 1, rows, part) for block in (shared_near, shared_far)]
+    errs_shared = ordered(layer, *pairs, axis=1).reshape(tokens, part)
     errs_own = jnp.concatenate(along_z(err_own), axis=0)
-
-    here = jnp.where(layer == 0, err_own[:rows], shared_far[:rows])
-    there = over_x(jnp.where(layer == 0, err_own[rows:], err_shared))
-    errors = jnp.concatenate([jnp.where(side == 0, here, there), jnp.where(side == 0, there, here)], axis=1)
 
     to_mine = times_transposed(errs_shared, shared_mine) + times_transposed(errs_own, own_mine)
     to_other = times_transposed(errs_shared, shared_other) + times_transposed(errs_own, own_other)
-    to_other = turned(to_other.astype(BF16))
 
     def of_half(pair, which):
         return jnp.where(which == 0, pair[:, :latents], pair[:, latents:])
 
-    diagonal = of_half(to_other, 1 - half)
     count = lax.axis_size("layer")
-    route = [(i * slots + j, (i ^ 1) * slots + (j ^ 1)) for i in range(count) for j in range(slots)]
+    diagonal = [(i * slots + j, (i ^ 1) * slots + (j ^ 1)) for i in range(count) for j in range(slots)]
+
+    here = jnp.where(layer == 0, rows_at(err_own, side), rows_at(errs_shared[:2 * rows], side))
+    sent = jnp.where(layer == 0, rows_at(err_own, 1 - side), rows_at(errs_shared[:2 * rows], 1 - side))
+    tiles = [sent[:, at:at + latents] for at in range(0, part, latents)]
+    from_x = over_x(jnp.concatenate([of_half(to_other, half).astype(BF16)] + tiles, axis=0))
+    there = from_x[tokens:].reshape(part // latents, rows, latents)
+    there = jnp.concatenate([there[i] for i in range(part // latents)], axis=1)
+    errors = ordered(side, here, there, axis=1)
+    from_x = from_x[:tokens]
+    from_diagonal = lax.ppermute(of_half(to_other, 1 - half).astype(BF16), ("layer", "latent"), diagonal)
     grad = of_half(to_mine, half) + crossed(of_half(to_mine, 1 - half), "layer", 1)
-    grad = grad + over_x(of_half(to_other, half)).astype(F32)
-    grad = grad + lax.ppermute(diagonal, ("layer", "latent"), route).astype(F32)
-    grad_pre = grad * gate
+    grad_pre = (grad + from_x.astype(F32) + from_diagonal.astype(F32)) * gate
     bias_grad = jnp.sum(grad_pre, axis=0)[None, :]
     enc_grad = encoder_gradient(resid_half, resid_other, grad_pre.astype(BF16), half)
     return errors[None], enc_grad[None], bias_grad

time: 79.7 us -> 73.8 us (0.926)
  waiting for transfers between devices: 19.3 us -> 17.1 us
  Pallas kernels: 0 us -> 2.1 us
  starting transfers between devices: 37 us -> 35.2 us
  local copies, waits for them, and re-layouts: 6.08 us -> 4.46 us
  other arithmetic: 8.81 us -> 7.2 us
  matrix products: 5.72 us -> 4.83 us
    select_n x3 -> x1, other arithmetic: 3.13 us -> 0.06 us  [both_halves(): jnp.where(half == 0, mine, other)]
    pallas_call x0 -> x1, Pallas kernels: none -> 2.1 us  [paired_weights(): pl.pallas_call(side_by_side, out_shape=jax.ShapeDtypeStruct((cols, 2 * la...]
    squeeze x2 -> x0, local copies, waits for them, and re-layouts: 2.01 us -> none  [two_layers(): aim_own = jnp.concatenate([aims[0], aims_other[0]], axis=0).astype(F32)]
    rev x2 -> x0, local copies, waits for them, and re-layouts: 1.47 us -> none  [turned(): array.reshape(far, 2, rows, array.shape[1])[:, ::-1].reshape(array.shape)]
    ppermute x28 -> x27, starting transfers between devices: 36.6 us -> 35.2 us  [crossed(): lax.ppermute(block, axis, [(i, i ^ mask) for i in range(lax.axis_size(axi...]
    ppermute x28 -> x27, waiting for transfers between devices: 18.4 us -> 17.1 us  [crossed(): lax.ppermute(block, axis, [(i, i ^ mask) for i in range(lax.axis_size(axi...]
    unnamed x27 -> x21, local copies, waits for them, and re-layouts: 0.09 us -> 1.04 us
    ppermute x1, waiting for transfers between devices: 0.91 us -> 0.01 us  [two_layers(): lax.ppermute(of_half(to_other, 1 - half).astype(BF16), ('layer', 'latent'...]
  transfers between devices with their start and end apart: 29 -> 28, of which waited for: 12 -> 9; matrix products, arithmetic and copies ran while one was open for 22% -> 19% of each run, Pallas kernels for 0% -> 3%
where the time goes in v5:
time: 73.8 us; the launch traced here: 73.3 us
  starting transfers between devices  35.2 us (48%)
  waiting for transfers between devices  17.1 us (23%)
  other arithmetic  7.2 us (10%)
  matrix products  4.83 us (7%)
  local copies, waits for them, and re-layouts  4.46 us (6%)
  between operations  2.33 us (3%)
  Pallas kernels  2.1 us (3%)
    ppermute x27, starting transfers between devices, crossed(): lax.ppermute(block, axis, [(i, i ^ mask) for i in range(lax.axis_size(axi...  35.2 us
    ppermute x27, waiting for transfers between devices, crossed(): lax.ppermute(block, axis, [(i, i ^ mask) for i in range(lax.axis_size(axi...  17.1 us
    select_n x5, other arithmetic, ordered(): jnp.where(which == 0, lower, upper)  2.34 us
    dot_general x7, matrix products, times(): return jnp.dot(left, right, preferred_element_type=F32)  2.28 us
    pallas_call x1, Pallas kernels, paired_weights(): pl.pallas_call(side_by_side, out_shape=jax.ShapeDtypeStruct((cols, 2 * la...  2.1 us
    squeeze x2, local copies, waits for them, and re-layouts, decoder_part(): lax.dynamic_slice(decoder, (which, 0, where * part), (1, 2 * latents, part))  1.64 us
  transfers between devices with their start and end apart: 28, of which 9 were waited for; matrix products, arithmetic and copies ran while one was open for 19% of the time, Pallas kernels for 3%

profile of v5, /device:TPU:0, one launch (start us, length us, event | category | flops | bytes accessed | tf_op | source)
XLA Modules:
  0.0 73.3 jit_solution(15510146329162598248)
XLA Ops:
  0.6 0.0 copy-start
  0.7 1.0 %dynamic-slice_bitcast_fusion.2 = bf16[16,1792]{1,0:T(8,128)(2,1)S(1)} fusion(bf16[2,16,3584]{2,1,0:T(8,128)(2,1)} %param.6, s32[]{:T(128)S(6)} %select_n.295, s32[]{:T(128)S(6)} %select_n.297), kind=kLoop, calls=%fused_computation.53 | loop fusion | bytes 114696 | tf_op jit(solution)/shard_map/squeeze | solution.py:124
  1.6 2.9 %collective-permute-start = (bf16[16,1792]{1,0:T(8,128)(2,1)S(1)}, bf16[16,1792]{1,0:T(8,128)(2,1)S(1)}, u32[]{:S(2)}, u32[]{:S(2)}) collective-permute-start(bf16[16,1792]{1,0:T(8,128)(2,1)S(1)} %dynamic-slice_bitcast_fusion.2), channel_id=1, source_target_pairs={{0,1},{1,0},{2,3},{3,2},{4,5},{5,4},{6,7},{7,6},{8,9},{9,8},{10,11... | collective-permute-start | bytes 172040 | tf_op jit(solution)/shard_map/ppermute | solution.py:13
  4.6 0.8 %dynamic-slice_bitcast_fusion.1 = bf16[256,896]{1,0:T(8,128)(2,1)} fusion(bf16[2,256,1792]{2,1,0:T(8,128)(2,1)S(1)} %bitcast.84, s32[]{:T(128)S(6)} %select_n.302, s32[]{:T(128)S(6)} %select_n.303), kind=kLoop, calls=%fused_computation.21 | loop fusion | bytes 917512 | tf_op jit(solution)/shard_map/squeeze | solution.py:114
  5.4 0.5 collective-permute-start.3
  5.9 0.0 collective-permute-start.1
  5.9 0.7 fusion.34
  6.6 0.6 pad_maximum_fusion.7
  7.2 0.0 collective-permute-done
  7.2 0.8 %broadcast_select_fusion.5 = (bf16[16,1792]{1,0:T(8,128)(2,1)S(1)}, bf16[16,1792]{1,0:T(8,128)(2,1)S(1)}) fusion(bf16[16,1792]{1,0:T(8,128)(2,1)S(1)} %collective-permute-done, pred[]{:T(512)S(6)} %eq.79, bf16[2,16,3584]{2,1,0:T(8,128)(2,1)} %param.6, s32[]{:T(128)S(6)} %select_n.295, s32[]{:T(128)S(6)} %select_n.297), kind=kLoop, calls=%fused_computation.55 | loop fusion | flops 57344 | bytes 229385 | tf_op jit(solution)/shard_map/jit(_where)/select_n | solution.py:117
  8.0 0.6 collective-permute-done.1.other_ref
  8.6 3.6 %collective-permute-start.6 = (bf16[32,1792]{1,0:T(8,128)(2,1)S(1)}, bf16[32,1792]{1,0:T(8,128)(2,1)S(1)}, u32[]{:S(2)}, u32[]{:S(2)}) collective-permute-start(bf16[32,1792]{1,0:T(8,128)(2,1)S(1)} %pad_maximum_fusion.2), channel_id=1, source_target_pairs={{0,6},{1,7},{2,4},{3,5},{4,2},{5,3},{6,0},{7,1},{8,14},{9,15},{10,... | collective-permute-start | bytes 344072 | tf_op jit(solution)/shard_map/ppermute | solution.py:13
  12.2 0.0 collective-permute-start.5
  12.2 0.8 %collective-permute-start.4 = (bf16[32,1792]{1,0:T(8,128)(2,1)S(1)}, bf16[32,1792]{1,0:T(8,128)(2,1)}, u32[]{:S(2)}, u32[]{:S(2)}) collective-permute-start(bf16[32,1792]{1,0:T(8,128)(2,1)S(1)} %pad_maximum_fusion.2), channel_id=1, source_target_pairs={{0,2},{1,3},{2,0},{3,1},{4,6},{5,7},{6,4},{7,5},{8,10},{9,11},{10,... | collective-permute-start | bytes 344072 | tf_op jit(solution)/shard_map/ppermute | solution.py:13
  13.0 0.8 %constant_dynamic-slice_fusion.2 = (bf16[1,16,896]{2,1,0:T(8,128)(2,1)S(1)}, bf16[1,16,896]{2,1,0:T(8,128)(2,1)S(1)}) fusion(bf16[3,16,3584]{2,1,0:T(8,128)(2,1)} %param.7, s32[]{:T(128)S(6)} %select_n.300, s32[]{:T(128)S(6)} %select_n.301), kind=kLoop, calls=%fused_computation.95 | loop fusion | bytes 114696 | tf_op jit(solution)/shard_map/dynamic_slice | solution.py:136
  13.8 0.6 pad_maximum_fusion.4
  14.4 1.5 %collective-permute-start.2 = (bf16[2,16,896]{2,1,0:T(8,128)(2,1)}, bf16[2,16,896]{2,1,0:T(8,128)(2,1)}, u32[]{:S(2)}, u32[]{:S(2)}) collective-permute-start(bf16[2,16,896]{2,1,0:T(8,128)(2,1)} %pad_maximum_fusion.4), channel_id=1, source_target_pairs={{0,1},{1,0},{2,3},{3,2},{4,5},{5,4},{6,7},{7,6},{8,9},{9,8},{10,11... | collective-permute-start | bytes 172040 | tf_op jit(solution)/shard_map/ppermute | solution.py:13
  15.9 2.1 %paired_weights.1 = bf16[1792,256]{1,0:T(8,128)(2,1)} custom-call(s32[1]{0:T(128)} %bitcast.4.half_ref, bf16[3584,128]{1,0:T(8,128)(2,1)} %bitcast.104, bf16[3584,128]{1,0:T(8,128)(2,1)} %copy-done.2), custom_call_target="tpu_custom_call" | custom-call | flops 20000000000 | bytes 1835008 | tf_op jit(solution)/shard_map/paired_weights/pallas_call | solution.py:55
  18.0 0.8 %dynamic-slice_bitcast_fusion = bf16[256,896]{1,0:T(8,128)(2,1)} fusion(bf16[2,256,1792]{2,1,0:T(8,128)(2,1)S(1)} %bitcast.83, s32[]{:T(128)S(6)} %select_n.295, s32[]{:T(128)S(6)} %select_n.303), kind=kLoop, calls=%fused_computation.20 | loop fusion | bytes 917512 | tf_op jit(solution)/shard_map/squeeze | solution.py:114
  18.9 1.4 %compare_reduce_fusion = (pred[]{:T(512)}, pred[]{:T(512)}) fusion(s32[]{:T(128)S(6)} %add_shard_map.3, s32[2,1,12]{2,1,0:T(1,128)} %param.11, s32[]{:T(128)S(6)} %select_n.295, s32[]{:T(128)S(6)} %axis_index.26), kind=kLoop, calls=%fused_computation.96 | loop fusion | flops 46 | bytes 62 | tf_op jit(solution)/shard_map/reduce_or | solution.py:35
  21.6 0.6 collective-permute-start.9
  22.2 0.0 collective-permute-done.5
  22.2 0.9 %constant_dynamic-update-slice_fusion.2 = bf16[128,1792]{1,0:T(8,128)(2,1)S(1)} fusion(bf16[128,1792]{1,0:T(8,128)(2,1)S(1)} %constant_dynamic-update-slice_fusion.3, bf16[32,1792]{1,0:T(8,128)(2,1)} %collective-permute-done.4), kind=kLoop, calls=%fused_computation.58 | loop fusion | bytes 229376
  23.2 1.0 %convolution_add_fusion.5 = f32[128,256]{1,0:T(8,128)S(1)} fusion(bf16[128,1792]{1,0:T(8,128)(2,1)S(1)} %constant_dynamic-update-slice_fusion, bf16[1792,256]{1,0:T(8,128)(2,1)S(1)} %copy-done.1, f32[256]{0:T(256)} %pad_maximum_fusion.7), kind=kOutput, calls=%fused_computation.8 | convolution fusion | flops 117473280 | bytes 1508352 | tf_op jit(solution)/shard_map/dot_general | solution.py:17
  24.1 0.1 collective-permute-start.7
  24.2 0.8 %select_bitcast_fusion.1 = (bf16[16,896]{1,0:T(8,128)(2,1)S(1)}, bf16[16,896]{1,0:T(8,128)(2,1)S(1)}) fusion(pred[]{:T(512)S(6)} %eq.79, bf16[2,16,896]{2,1,0:T(8,128)(2,1)} %collective-permute-done.2, bf16[3,16,3584]{2,1,0:T(8,128)(2,1)} %param.7, s32[]{:T(128)S(6)} %select_n.300, s32[]{:T(128)S(6)} %select_n.311), kind=kLoop, calls=%fused_computation.87 | loop fusion | flops 28672 | bytes 114697 | tf_op jit(solution)/shard_map/jit(_where)/select_n | solution.py:117
  25.0 0.5 collective-permute-done.7
  25.6 1.6 %collective-permute-start.8 = (bf16[128,256]{1,0:T(8,128)(2,1)S(1)}, bf16[128,256]{1,0:T(8,128)(2,1)S(1)}, u32[]{:S(2)}, u32[]{:S(2)}) collective-permute-start(bf16[128,256]{1,0:T(8,128)(2,1)S(1)} %multiply_convert_fusion), channel_id=1, source_target_pairs={{0,1},{1,0},{2,3},{3,2},{4,5},{5,4},{6,7},{7,6},{8,9},{9,8},{10,11... | collective-permute-start | bytes 196616 | tf_op jit(solution)/shard_map/ppermute | solution.py:13
  27.2 0.2 fusion.9
  27.4 0.2 fusion.7
  27.6 7.2 %collective-permute-done.8 = bf16[128,256]{1,0:T(8,128)(2,1)S(1)} collective-permute-done((bf16[128,256]{1,0:T(8,128)(2,1)S(1)}, bf16[128,256]{1,0:T(8,128)(2,1)S(1)}, u32[]{:S(2)}, u32[]{:S(2)}) %collective-permute-start.8) | collective-permute-done | bytes 65568 | tf_op jit(solution)/shard_map/ppermute | solution.py:13
  34.8 0.2 fusion.1
  35.0 1.6 %collective-permute-start.13 = (bf16[64,896]{1,0:T(8,128)(2,1)S(1)}, bf16[64,896]{1,0:T(8,128)(2,1)S(1)}, u32[]{:S(2)}, u32[]{:S(2)}) collective-permute-start(bf16[64,896]{1,0:T(8,128)(2,1)S(1)} %fusion.1), channel_id=1, source_target_pairs={{0,16},{8,24},{16,0},{24,8},{1,17},{9,25},{17,1},{25,9},{2,18},{10... | collective-permute-start | bytes 344072 | tf_op jit(solution)/shard_map/ppermute | solution.py:13
  36.6 0.2 convolution_add_fusion.1
  36.8 3.1 %collective-permute-done.13 = bf16[64,896]{1,0:T(8,128)(2,1)S(1)} collective-permute-done((bf16[64,896]{1,0:T(8,128)(2,1)S(1)}, bf16[64,896]{1,0:T(8,128)(2,1)S(1)}, u32[]{:S(2)}, u32[]{:S(2)}) %collective-permute-start.13) | collective-permute-done | bytes 114720 | tf_op jit(solution)/shard_map/ppermute | solution.py:13
  39.9 3.6 %collective-permute-start.14 = (bf16[16,896]{1,0:T(8,128)(2,1)S(1)}, bf16[16,896]{1,0:T(8,128)(2,1)S(1)}, u32[]{:S(2)}, u32[]{:S(2)}) collective-permute-start(bf16[16,896]{1,0:T(8,128)(2,1)S(1)} %get-tuple-element.52), channel_id=1, source_target_pairs={{0,6},{1,7},{2,4},{3,5},{4,2},{5,3},{6,0},{7,1},{8,14},{9,15},{10,... | collective-permute-start | bytes 86024 | tf_op jit(solution)/shard_map/ppermute | solution.py:13
  43.5 0.8 %collective-permute-start.15 = (bf16[16,896]{1,0:T(8,128)(2,1)S(1)}, bf16[16,896]{1,0:T(8,128)(2,1)S(1)}, u32[]{:S(2)}, u32[]{:S(2)}) collective-permute-start(bf16[16,896]{1,0:T(8,128)(2,1)S(1)} %get-tuple-element.54), channel_id=1, source_target_pairs={{0,4},{1,5},{2,6},{3,7},{4,0},{5,1},{6,2},{7,3},{8,12},{9,13},{10,... | collective-permute-start | bytes 86024 | tf_op jit(solution)/shard_map/ppermute | solution.py:13
  44.4 0.2 fusion.44
  44.6 0.2 fusion.43
  44.9 3.6 %collective-permute-start.10 = (bf16[32,896]{1,0:T(8,128)(2,1)S(1)}, bf16[32,896]{1,0:T(8,128)(2,1)S(1)}, u32[]{:S(2)}, u32[]{:S(2)}) collective-permute-start(bf16[32,896]{1,0:T(8,128)(2,1)S(1)} %get-tuple-element.49), channel_id=1, source_target_pairs={{0,6},{1,7},{2,4},{3,5},{4,2},{5,3},{6,0},{7,1},{8,14},{9,15},{10,... | collective-permute-start | bytes 172040 | tf_op jit(solution)/shard_map/ppermute | solution.py:13
  48.5 0.0 collective-permute-done.14
  48.5 1.3 %collective-permute-start.11 = (bf16[32,896]{1,0:T(8,128)(2,1)S(1)}, bf16[32,896]{1,0:T(8,128)(2,1)S(1)}, u32[]{:S(2)}, u32[]{:S(2)}) collective-permute-start(bf16[32,896]{1,0:T(8,128)(2,1)S(1)} %get-tuple-element.51), channel_id=1, source_target_pairs={{0,4},{1,5},{2,6},{3,7},{4,0},{5,1},{6,2},{7,3},{8,12},{9,13},{10,... | collective-permute-start | bytes 172040 | tf_op jit(solution)/shard_map/ppermute | solution.py:13
  49.7 0.8 %fusion.25 = bf16[16,896]{1,0:T(8,128)(2,1)S(1)} fusion(f32[64,896]{1,0:T(8,128)S(1)} %get-tuple-element.40, bf16[16,896]{1,0:T(8,128)(2,1)S(1)} %collective-permute-done.16, bf16[16,896]{1,0:T(8,128)(2,1)S(1)} %collective-permute-done.15, bf16[16,896]{1,0:T(8,128)(2,1)S(1)} %collective-permute-done.14, bf16[2,16,896]{2,1,0:T(8,128)(2,1)} %collective-permute-done.2, ...), kind=kLoop, calls=%fused_computation.50 | loop fusion | flops 143360 | bytes 229381 | tf_op jit(solution)/shard_map/convert_element_type | solution.py:162
  50.5 3.2 %collective-permute-start.19 = (bf16[16,896]{1,0:T(8,128)(2,1)S(1)}, bf16[16,896]{1,0:T(8,128)(2,1)S(1)}, u32[]{:S(2)}, u32[]{:S(2)}) collective-permute-start(bf16[16,896]{1,0:T(8,128)(2,1)S(1)} %fusion.25), channel_id=1, source_target_pairs={{0,6},{1,7},{2,4},{3,5},{4,2},{5,3},{6,0},{7,1},{8,14},{9,15},{10,... | collective-permute-start | bytes 86024 | tf_op jit(solution)/shard_map/ppermute | solution.py:13
  53.7 1.9 %collective-permute-start.17 = (bf16[16,896]{1,0:T(8,128)(2,1)S(1)}, bf16[16,896]{1,0:T(8,128)(2,1)S(1)}, u32[]{:S(2)}, u32[]{:S(2)}) collective-permute-start(bf16[16,896]{1,0:T(8,128)(2,1)S(1)} %fusion.25), channel_id=1, source_target_pairs={{0,2},{1,3},{2,0},{3,1},{4,6},{5,7},{6,4},{7,5},{8,10},{9,11},{10,... | collective-permute-start | bytes 86024 | tf_op jit(solution)/shard_map/ppermute | solution.py:13
  55.7 2.5 %collective-permute-start.23 = (bf16[32,896]{1,0:T(8,128)(2,1)S(1)}, bf16[32,896]{1,0:T(8,128)(2,1)S(1)}, u32[]{:S(2)}, u32[]{:S(2)}) collective-permute-start(bf16[32,896]{1,0:T(8,128)(2,1)S(1)} %fusion.21), channel_id=1, source_target_pairs={{0,6},{1,7},{2,4},{3,5},{4,2},{5,3},{6,0},{7,1},{8,14},{9,15},{10,... | collective-permute-start | bytes 172040 | tf_op jit(solution)/shard_map/ppermute | solution.py:13
  58.3 0.3 collective-permute-done.18
  58.5 1.7 %collective-permute-start.21 = (bf16[32,896]{1,0:T(8,128)(2,1)S(1)}, bf16[32,896]{1,0:T(8,128)(2,1)S(1)}, u32[]{:S(2)}, u32[]{:S(2)}) collective-permute-start(bf16[32,896]{1,0:T(8,128)(2,1)S(1)} %fusion.21), channel_id=1, source_target_pairs={{0,2},{1,3},{2,0},{3,1},{4,6},{5,7},{6,4},{7,5},{8,10},{9,11},{10,... | collective-permute-start | bytes 172040 | tf_op jit(solution)/shard_map/ppermute | solution.py:13
  60.2 1.4 %collective-permute-start.20 = (bf16[64,896]{1,0:T(8,128)(2,1)S(1)}, bf16[64,896]{1,0:T(8,128)(2,1)S(1)}, u32[]{:S(2)}, u32[]{:S(2)}) collective-permute-start(bf16[64,896]{1,0:T(8,128)(2,1)S(1)} %pad_maximum_fusion.3), channel_id=1, source_target_pairs={{0,16},{8,24},{16,0},{24,8},{1,17},{9,25},{17,1},{25,9},{2,18},{10... | collective-permute-start | bytes 344072 | tf_op jit(solution)/shard_map/ppermute | solution.py:13
  61.6 0.1 collective-permute-done.23
  61.7 1.6 %collective-permute-done.22 = bf16[32,896]{1,0:T(8,128)(2,1)S(1)} collective-permute-done((bf16[32,896]{1,0:T(8,128)(2,1)S(1)}, bf16[32,896]{1,0:T(8,128)(2,1)S(1)}, u32[]{:S(2)}, u32[]{:S(2)}) %collective-permute-start.22) | collective-permute-done | bytes 57376 | tf_op jit(solution)/shard_map/ppermute | solution.py:13
  63.3 0.3 fusion.26
  63.6 1.4 %collective-permute-done.20 = bf16[64,896]{1,0:T(8,128)(2,1)S(1)} collective-permute-done((bf16[64,896]{1,0:T(8,128)(2,1)S(1)}, bf16[64,896]{1,0:T(8,128)(2,1)S(1)}, u32[]{:S(2)}, u32[]{:S(2)}) %collective-permute-start.20) | collective-permute-done | bytes 114720 | tf_op jit(solution)/shard_map/ppermute | solution.py:13
  65.1 0.3 fusion.5
  65.4 0.3 convolution_add_fusion.4
  65.8 0.1 collective-permute-start.27
  65.9 0.6 collective-permute-start.24
  66.5 0.3 convolution_add_fusion.3
  66.9 1.4 %collective-permute-start.26 = (f32[128,128]{1,0:T(8,128)S(1)}, f32[128,128]{1,0:T(8,128)S(1)}, u32[]{:S(2)}, u32[]{:S(2)}) collective-permute-start(f32[128,128]{1,0:T(8,128)S(1)} %slice_select_fusion), channel_id=1, source_target_pairs={{0,8},{8,0},{16,24},{24,16},{1,9},{9,1},{17,25},{25,17},{2,10},{10... | collective-permute-start | bytes 196616 | tf_op jit(solution)/shard_map/ppermute | solution.py:13
  68.2 2.3 %collective-permute-done.24 = bf16[240,128]{1,0:T(8,128)(2,1)S(1)} collective-permute-done((bf16[240,128]{1,0:T(8,128)(2,1)S(1)}, bf16[240,128]{1,0:T(8,128)(2,1)S(1)}, u32[]{:S(2)}, u32[]{:S(2)}) %collective-permute-start.24) | collective-permute-done | bytes 61472 | tf_op jit(solution)/shard_map/ppermute | solution.py:13
  70.6 0.6 maximum_bitcast_fusion
  71.3 0.6 fusion.39
  71.8 0.1 broadcast_select_fusion.1
  71.9 1.4 %fusion = bf16[1,3584,128]{2,1,0:T(8,128)(2,1)} fusion(bf16[128,1792]{1,0:T(8,128)(2,1)S(1)} %get-tuple-element.42, bf16[128,1792]{1,0:T(8,128)(2,1)S(1)} %get-tuple-element.41, bf16[128,128]{1,0:T(8,128)(2,1)S(1)} %get-tuple-element.36), kind=kOutput, calls=%fused_computation.1 | convolution fusion | flops 119734272 | bytes 1867776 | tf_op jit(solution)/shard_map/dot_general | solution.py:80
  (61 shorter events, 0.5 us)
Async XLA Ops:
  0.6 3.9 %copy-start = (bf16[1,2,2,128,1792]{4,3,2,1,0:T(8,128)(2,1)S(1)}, bf16[1,2,2,128,1792]{4,3,2,1,0:T(8,128)(2,1)}, u32[]{:S(2)}) copy-start(bf16[1,2,2,128,1792]{4,3,2,1,0:T(8,128)(2,1)} %param.10) | copy-start | bytes 5505028
  1.6 5.5 %collective-permute-start = (bf16[16,1792]{1,0:T(8,128)(2,1)S(1)}, bf16[16,1792]{1,0:T(8,128)(2,1)S(1)}, u32[]{:S(2)}, u32[]{:S(2)}) collective-permute-start(bf16[16,1792]{1,0:T(8,128)(2,1)S(1)} %dynamic-slice_bitcast_fusion.2), channel_id=1, source_target_pairs={{0,1},{1,0},{2,3},{3,2},{4,5},{5,4},{6,7},{7,6},{8,9},{9,8},{10,11... | collective-permute-start | bytes 172040 | tf_op jit(solution)/shard_map/ppermute | solution.py:13
  5.4 16.2 %collective-permute-start.3 = (bf16[256,896]{1,0:T(8,128)(2,1)}, bf16[256,896]{1,0:T(8,128)(2,1)S(1)}, u32[]{:S(2)}, u32[]{:S(2)}) collective-permute-start(bf16[256,896]{1,0:T(8,128)(2,1)} %dynamic-slice_bitcast_fusion.1), channel_id=1, source_target_pairs={{0,1},{1,0},{2,3},{3,2},{4,5},{5,4},{6,7},{7,6},{8,9},{9,8},{10,11... | collective-permute-start | bytes 1376264 | tf_op jit(solution)/shard_map/ppermute | solution.py:13
  5.9 2.7 %collective-permute-start.1 = (bf16[3584,128]{1,0:T(8,128)(2,1)}, bf16[3584,128]{1,0:T(8,128)(2,1)S(1)}, u32[]{:S(2)}, u32[]{:S(2)}) collective-permute-start(bf16[3584,128]{1,0:T(8,128)(2,1)} %bitcast.103), channel_id=1, source_target_pairs={{0,8},{8,0},{16,24},{24,16},{1,9},{9,1},{17,25},{25,17},{2,10},{10... | collective-permute-start | bytes 2752520 | tf_op jit(solution)/shard_map/ppermute | solution.py:13
  8.6 7.3 %copy-start.2 = (bf16[3584,128]{1,0:T(8,128)(2,1)}, bf16[3584,128]{1,0:T(8,128)(2,1)S(1)}, u32[]{:S(2)}) copy-start(bf16[3584,128]{1,0:T(8,128)(2,1)S(1)} %collective-permute-done.1.other_ref) | copy-start | bytes 2752516
  8.6 13.6 %collective-permute-start.6 = (bf16[32,1792]{1,0:T(8,128)(2,1)S(1)}, bf16[32,1792]{1,0:T(8,128)(2,1)S(1)}, u32[]{:S(2)}, u32[]{:S(2)}) collective-permute-start(bf16[32,1792]{1,0:T(8,128)(2,1)S(1)} %pad_maximum_fusion.2), channel_id=1, source_target_pairs={{0,6},{1,7},{2,4},{3,5},{4,2},{5,3},{6,0},{7,1},{8,14},{9,15},{10,... | collective-permute-start | bytes 344072 | tf_op jit(solution)/shard_map/ppermute | solution.py:13
  12.2 10.0 %collective-permute-start.5 = (bf16[32,1792]{1,0:T(8,128)(2,1)S(1)}, bf16[32,1792]{1,0:T(8,128)(2,1)S(1)}, u32[]{:S(2)}, u32[]{:S(2)}) collective-permute-start(bf16[32,1792]{1,0:T(8,128)(2,1)S(1)} %pad_maximum_fusion.2), channel_id=1, source_target_pairs={{0,4},{1,5},{2,6},{3,7},{4,0},{5,1},{6,2},{7,3},{8,12},{9,13},{10,... | collective-permute-start | bytes 344072 | tf_op jit(solution)/shard_map/ppermute | solution.py:13
  12.2 10.0 %collective-permute-start.4 = (bf16[32,1792]{1,0:T(8,128)(2,1)S(1)}, bf16[32,1792]{1,0:T(8,128)(2,1)}, u32[]{:S(2)}, u32[]{:S(2)}) collective-permute-start(bf16[32,1792]{1,0:T(8,128)(2,1)S(1)} %pad_maximum_fusion.2), channel_id=1, source_target_pairs={{0,2},{1,3},{2,0},{3,1},{4,6},{5,7},{6,4},{7,5},{8,10},{9,11},{10,... | collective-permute-start | bytes 344072 | tf_op jit(solution)/shard_map/ppermute | solution.py:13
  14.4 7.8 %collective-permute-start.2 = (bf16[2,16,896]{2,1,0:T(8,128)(2,1)}, bf16[2,16,896]{2,1,0:T(8,128)(2,1)}, u32[]{:S(2)}, u32[]{:S(2)}) collective-permute-start(bf16[2,16,896]{2,1,0:T(8,128)(2,1)} %pad_maximum_fusion.4), channel_id=1, source_target_pairs={{0,1},{1,0},{2,3},{3,2},{4,5},{5,4},{6,7},{7,6},{8,9},{9,8},{10,11... | collective-permute-start | bytes 172040 | tf_op jit(solution)/shard_map/ppermute | solution.py:13
  18.0 5.1 %copy-start.1 = (bf16[1792,256]{1,0:T(8,128)(2,1)S(1)}, bf16[1792,256]{1,0:T(8,128)(2,1)}, u32[]{:S(2)}) copy-start(bf16[1792,256]{1,0:T(8,128)(2,1)} %paired_weights.1) | copy-start | bytes 2752516
  21.6 22.8 %collective-permute-start.9 = (bf16[256,896]{1,0:T(8,128)(2,1)}, bf16[256,896]{1,0:T(8,128)(2,1)S(1)}, u32[]{:S(2)}, u32[]{:S(2)}) collective-permute-start(bf16[256,896]{1,0:T(8,128)(2,1)} %dynamic-slice_bitcast_fusion), channel_id=1, source_target_pairs={{0,1},{1,0},{2,3},{3,2},{4,5},{5,4},{6,7},{7,6},{8,9},{9,8},{10,11... | collective-permute-start | bytes 1376264 | tf_op jit(solution)/shard_map/ppermute | solution.py:13
  24.1 1.4 %collective-permute-start.7 = (f32[128,256]{1,0:T(8,128)S(1)}, f32[128,256]{1,0:T(8,128)S(1)}, u32[]{:S(2)}, u32[]{:S(2)}) collective-permute-start(f32[128,256]{1,0:T(8,128)S(1)} %convolution_add_fusion.5), channel_id=1, source_target_pairs={{0,8},{8,0},{16,24},{24,16},{1,9},{9,1},{17,25},{25,17},{2,10},{10... | collective-permute-start | bytes 393224 | tf_op jit(solution)/shard_map/ppermute | solution.py:13
  25.6 9.2 %collective-permute-start.8 = (bf16[128,256]{1,0:T(8,128)(2,1)S(1)}, bf16[128,256]{1,0:T(8,128)(2,1)S(1)}, u32[]{:S(2)}, u32[]{:S(2)}) collective-permute-start(bf16[128,256]{1,0:T(8,128)(2,1)S(1)} %multiply_convert_fusion), channel_id=1, source_target_pairs={{0,1},{1,0},{2,3},{3,2},{4,5},{5,4},{6,7},{7,6},{8,9},{9,8},{10,11... | collective-permute-start | bytes 196616 | tf_op jit(solution)/shard_map/ppermute | solution.py:13
  35.0 4.9 %collective-permute-start.13 = (bf16[64,896]{1,0:T(8,128)(2,1)S(1)}, bf16[64,896]{1,0:T(8,128)(2,1)S(1)}, u32[]{:S(2)}, u32[]{:S(2)}) collective-permute-start(bf16[64,896]{1,0:T(8,128)(2,1)S(1)} %fusion.1), channel_id=1, source_target_pairs={{0,16},{8,24},{16,0},{24,8},{1,17},{9,25},{17,1},{25,9},{2,18},{10... | collective-permute-start | bytes 344072 | tf_op jit(solution)/shard_map/ppermute | solution.py:13
  36.6 35.3 %collective-permute-start.25 = (bf16[128,1792]{1,0:T(8,128)(2,1)S(1)}, bf16[128,1792]{1,0:T(8,128)(2,1)S(1)}, u32[]{:S(2)}, u32[]{:S(2)}) collective-permute-start(bf16[128,1792]{1,0:T(8,128)(2,1)S(1)} %constant_dynamic-update-slice_fusion), channel_id=1, source_target_pairs={{0,8},{8,0},{16,24},{24,16},{1,9},{9,1},{17,25},{25,17},{2,10},{10... | collective-permute-start | bytes 1376264 | tf_op jit(solution)/shard_map/ppermute | solution.py:13
  39.9 8.6 %collective-permute-start.14 = (bf16[16,896]{1,0:T(8,128)(2,1)S(1)}, bf16[16,896]{1,0:T(8,128)(2,1)S(1)}, u32[]{:S(2)}, u32[]{:S(2)}) collective-permute-start(bf16[16,896]{1,0:T(8,128)(2,1)S(1)} %get-tuple-element.52), channel_id=1, source_target_pairs={{0,6},{1,7},{2,4},{3,5},{4,2},{5,3},{6,0},{7,1},{8,14},{9,15},{10,... | collective-permute-start | bytes 86024 | tf_op jit(solution)/shard_map/ppermute | solution.py:13
  43.5 5.0 %collective-permute-start.16 = (bf16[16,896]{1,0:T(8,128)(2,1)S(1)}, bf16[16,896]{1,0:T(8,128)(2,1)S(1)}, u32[]{:S(2)}, u32[]{:S(2)}) collective-permute-start(bf16[16,896]{1,0:T(8,128)(2,1)S(1)} %get-tuple-element.53), channel_id=1, source_target_pairs={{0,2},{1,3},{2,0},{3,1},{4,6},{5,7},{6,4},{7,5},{8,10},{9,11},{10,... | collective-permute-start | bytes 86024 | tf_op jit(solution)/shard_map/ppermute | solution.py:13
  43.5 6.2 %collective-permute-start.15 = (bf16[16,896]{1,0:T(8,128)(2,1)S(1)}, bf16[16,896]{1,0:T(8,128)(2,1)S(1)}, u32[]{:S(2)}, u32[]{:S(2)}) collective-permute-start(bf16[16,896]{1,0:T(8,128)(2,1)S(1)} %get-tuple-element.54), channel_id=1, source_target_pairs={{0,4},{1,5},{2,6},{3,7},{4,0},{5,1},{6,2},{7,3},{8,12},{9,13},{10,... | collective-permute-start | bytes 86024 | tf_op jit(solution)/shard_map/ppermute | solution.py:13
  44.9 8.9 %collective-permute-start.10 = (bf16[32,896]{1,0:T(8,128)(2,1)S(1)}, bf16[32,896]{1,0:T(8,128)(2,1)S(1)}, u32[]{:S(2)}, u32[]{:S(2)}) collective-permute-start(bf16[32,896]{1,0:T(8,128)(2,1)S(1)} %get-tuple-element.49), channel_id=1, source_target_pairs={{0,6},{1,7},{2,4},{3,5},{4,2},{5,3},{6,0},{7,1},{8,14},{9,15},{10,... | collective-permute-start | bytes 172040 | tf_op jit(solution)/shard_map/ppermute | solution.py:13
  48.5 5.3 %collective-permute-start.12 = (bf16[32,896]{1,0:T(8,128)(2,1)S(1)}, bf16[32,896]{1,0:T(8,128)(2,1)S(1)}, u32[]{:S(2)}, u32[]{:S(2)}) collective-permute-start(bf16[32,896]{1,0:T(8,128)(2,1)S(1)} %get-tuple-element.50), channel_id=1, source_target_pairs={{0,2},{1,3},{2,0},{3,1},{4,6},{5,7},{6,4},{7,5},{8,10},{9,11},{10,... | collective-permute-start | bytes 172040 | tf_op jit(solution)/shard_map/ppermute | solution.py:13
  48.5 7.2 %collective-permute-start.11 = (bf16[32,896]{1,0:T(8,128)(2,1)S(1)}, bf16[32,896]{1,0:T(8,128)(2,1)S(1)}, u32[]{:S(2)}, u32[]{:S(2)}) collective-permute-start(bf16[32,896]{1,0:T(8,128)(2,1)S(1)} %get-tuple-element.51), channel_id=1, source_target_pairs={{0,4},{1,5},{2,6},{3,7},{4,0},{5,1},{6,2},{7,3},{8,12},{9,13},{10,... | collective-permute-start | bytes 172040 | tf_op jit(solution)/shard_map/ppermute | solution.py:13
  50.5 7.7 %collective-permute-start.19 = (bf16[16,896]{1,0:T(8,128)(2,1)S(1)}, bf16[16,896]{1,0:T(8,128)(2,1)S(1)}, u32[]{:S(2)}, u32[]{:S(2)}) collective-permute-start(bf16[16,896]{1,0:T(8,128)(2,1)S(1)} %fusion.25), channel_id=1, source_target_pairs={{0,6},{1,7},{2,4},{3,5},{4,2},{5,3},{6,0},{7,1},{8,14},{9,15},{10,... | collective-permute-start | bytes 86024 | tf_op jit(solution)/shard_map/ppermute | solution.py:13
  53.7 4.8 %collective-permute-start.18 = (bf16[16,896]{1,0:T(8,128)(2,1)S(1)}, bf16[16,896]{1,0:T(8,128)(2,1)S(1)}, u32[]{:S(2)}, u32[]{:S(2)}) collective-permute-start(bf16[16,896]{1,0:T(8,128)(2,1)S(1)} %fusion.25), channel_id=1, source_target_pairs={{0,4},{1,5},{2,6},{3,7},{4,0},{5,1},{6,2},{7,3},{8,12},{9,13},{10,... | collective-permute-start | bytes 86024 | tf_op jit(solution)/shard_map/ppermute | solution.py:13
  53.7 6.4 %collective-permute-start.17 = (bf16[16,896]{1,0:T(8,128)(2,1)S(1)}, bf16[16,896]{1,0:T(8,128)(2,1)S(1)}, u32[]{:S(2)}, u32[]{:S(2)}) collective-permute-start(bf16[16,896]{1,0:T(8,128)(2,1)S(1)} %fusion.25), channel_id=1, source_target_pairs={{0,2},{1,3},{2,0},{3,1},{4,6},{5,7},{6,4},{7,5},{8,10},{9,11},{10,... | collective-permute-start | bytes 86024 | tf_op jit(solution)/shard_map/ppermute | solution.py:13
  55.7 6.0 %collective-permute-start.23 = (bf16[32,896]{1,0:T(8,128)(2,1)S(1)}, bf16[32,896]{1,0:T(8,128)(2,1)S(1)}, u32[]{:S(2)}, u32[]{:S(2)}) collective-permute-start(bf16[32,896]{1,0:T(8,128)(2,1)S(1)} %fusion.21), channel_id=1, source_target_pairs={{0,6},{1,7},{2,4},{3,5},{4,2},{5,3},{6,0},{7,1},{8,14},{9,15},{10,... | collective-permute-start | bytes 172040 | tf_op jit(solution)/shard_map/ppermute | solution.py:13
  58.2 5.1 %collective-permute-start.22 = (bf16[32,896]{1,0:T(8,128)(2,1)S(1)}, bf16[32,896]{1,0:T(8,128)(2,1)S(1)}, u32[]{:S(2)}, u32[]{:S(2)}) collective-permute-start(bf16[32,896]{1,0:T(8,128)(2,1)S(1)} %fusion.21), channel_id=1, source_target_pairs={{0,4},{1,5},{2,6},{3,7},{4,0},{5,1},{6,2},{7,3},{8,12},{9,13},{10,... | collective-permute-start | bytes 172040 | tf_op jit(solution)/shard_map/ppermute | solution.py:13
  58.5 4.8 %collective-permute-start.21 = (bf16[32,896]{1,0:T(8,128)(2,1)S(1)}, bf16[32,896]{1,0:T(8,128)(2,1)S(1)}, u32[]{:S(2)}, u32[]{:S(2)}) collective-permute-start(bf16[32,896]{1,0:T(8,128)(2,1)S(1)} %fusion.21), channel_id=1, source_target_pairs={{0,2},{1,3},{2,0},{3,1},{4,6},{5,7},{6,4},{7,5},{8,10},{9,11},{10,... | collective-permute-start | bytes 172040 | tf_op jit(solution)/shard_map/ppermute | solution.py:13
  60.2 4.9 %collective-permute-start.20 = (bf16[64,896]{1,0:T(8,128)(2,1)S(1)}, bf16[64,896]{1,0:T(8,128)(2,1)S(1)}, u32[]{:S(2)}, u32[]{:S(2)}) collective-permute-start(bf16[64,896]{1,0:T(8,128)(2,1)S(1)} %pad_maximum_fusion.3), channel_id=1, source_target_pairs={{0,16},{8,24},{16,0},{24,8},{1,17},{9,25},{17,1},{25,9},{2,18},{10... | collective-permute-start | bytes 344072 | tf_op jit(solution)/shard_map/ppermute | solution.py:13
  65.8 5.5 %collective-permute-start.27 = (bf16[128,128]{1,0:T(8,128)(2,1)S(1)}, bf16[128,128]{1,0:T(8,128)(2,1)S(1)}, u32[]{:S(2)}, u32[]{:S(2)}) collective-permute-start(bf16[128,128]{1,0:T(8,128)(2,1)S(1)} %get-tuple-element.57), channel_id=1, source_target_pairs={{0,9},{1,8},{2,11},{3,10},{4,13},{5,12},{6,15},{7,14},{8,1},{9,0},... | collective-permute-start | bytes 98312 | tf_op jit(solution)/shard_map/ppermute | solution.py:188
  65.9 4.6 %collective-permute-start.24 = (bf16[240,128]{1,0:T(8,128)(2,1)S(1)}, bf16[240,128]{1,0:T(8,128)(2,1)S(1)}, u32[]{:S(2)}, u32[]{:S(2)}) collective-permute-start(bf16[240,128]{1,0:T(8,128)(2,1)S(1)} %constant_dynamic-update-slice_fusion.4), channel_id=1, source_target_pairs={{0,1},{1,0},{2,3},{3,2},{4,5},{5,4},{6,7},{7,6},{8,9},{9,8},{10,11... | collective-permute-start | bytes 184328 | tf_op jit(solution)/shard_map/ppermute | solution.py:13
  66.9 4.4 %collective-permute-start.26 = (f32[128,128]{1,0:T(8,128)S(1)}, f32[128,128]{1,0:T(8,128)S(1)}, u32[]{:S(2)}, u32[]{:S(2)}) collective-permute-start(f32[128,128]{1,0:T(8,128)S(1)} %slice_select_fusion), channel_id=1, source_target_pairs={{0,8},{8,0},{16,24},{24,16},{1,9},{9,1},{17,25},{25,17},{2,10},{10... | collective-permute-start | bytes 196616 | tf_op jit(solution)/shard_map/ppermute | solution.py:13

commit v6 on v5

--- a/solution.py
+++ b/solution.py
@@ -122,8 +122,8 @@
 
     weight_other = crossed(enc_weight[0], "layer", 1)
     mine = lax.dynamic_slice(resid, (layer, 0, half * cols), (1, rows, cols))[0]
-    pair, weight_other, later, target, blocks = hold(
-        (ordered(side, mine, over_x(mine)), weight_other, decoder, target, blocks)
+    pair, weight_other, later, bias, blocks = hold(
+        (ordered(side, mine, over_x(mine)), weight_other, decoder, enc_bias[0], blocks)
     )
     weight_pair = paired_weights(enc_weight[0], weight_other, half, cols)
     column = along_z(pair)
@@ -136,34 +136,35 @@
         own = lax.dynamic_slice(target, (2 * layer, 0, start), (1, rows, part))
         return jnp.concatenate([own, lax.dynamic_slice(target, (1, 0, start), (1, rows, part))], axis=0)
 
-    aims, aims_other = aims_for(side), over_x(aims_for(1 - side))
-    decoder, aims_other, shared_other, *column = hold((decoder, aims_other, shared_other, *column))
+    decoder, shared_other, *column = hold((decoder, shared_other, *column))
     shared_mine, own_mine = decoder_part(decoder, 1 - layer, side), decoder_part(decoder, layer, side)
     resid_half = jnp.concatenate(column, axis=0)
     firing = gates(blocks, layer, slot, slots, latents, tokens)
     gate = jnp.where(half == 0, firing[0], firing[1])
 
-    bias_pair = ordered(half, enc_bias[0], jnp.zeros_like(enc_bias[0]))
+    bias_pair = ordered(half, bias, jnp.zeros_like(bias))
     partial = times(resid_half, weight_pair) + bias_pair
     acts = ((partial + crossed(partial, "layer", 1)) * jnp.concatenate(firing, axis=1)).astype(BF16)
-    acts_other = over_x(acts)
+    acts_other, own_other = hold((over_x(acts), own_other))
+    target, _ = hold((target, acts))
+    aims, aims_other = aims_for(side), over_x(aims_for(1 - side))
     resid_swapped, _ = hold((resid_half, acts_other))
     resid_other = crossed(resid_swapped, "layer", 1)
-    aim_own = ordered(side, aims[0], aims_other[0]).astype(F32)
-    aim_shared = jnp.where(layer == side, aims[1], aims_other[1]).astype(F32)
-
     leaving = times(rows_at(acts, 1 - layer), shared_mine) + times(rows_at(acts_other, 1 - layer), shared_other)
     staying = times(rows_at(acts, layer), shared_mine) + times(rows_at(acts_other, layer), shared_other)
     arrived = crossed(leaving.astype(BF16), "layer", 2)
     product = times(acts, own_mine) + times(acts_other, own_other)
-    arrived, staying = hold((arrived, staying))
+    arrived, staying, aims_other = hold((arrived, staying, aims_other))
     shared_terms = sent_along_z(staying + arrived.astype(F32))
     own_terms = sent_along_z(product)
+    aim_own = ordered(side, aims[0], aims_other[0]).astype(F32)
+    aim_shared = jnp.where(layer == side, aims[1], aims_other[1]).astype(F32)
     err_shared = (added(shared_terms) - aim_shared).astype(BF16)
     err_own = (added(own_terms) - aim_own).astype(BF16)
 
     shared_near = jnp.concatenate(along_z(err_shared), axis=0)
     shared_far = crossed(shared_near, "layer", 2)
+    resid_turned, shared_far = hold((both_halves(half, resid_half, resid_other, 1).T, shared_far))
     pairs = [block.reshape(far, 1, rows, part) for block in (shared_near, shared_far)]
     errs_shared = ordered(layer, *pairs, axis=1).reshape(tokens, part)
     errs_own = jnp.concatenate(along_z(err_own), axis=0)
@@ -189,7 +190,7 @@
     grad = of_half(to_mine, half) + crossed(of_half(to_mine, 1 - half), "layer", 1)
     grad_pre = (grad + from_x.astype(F32) + from_diagonal.astype(F32)) * gate
     bias_grad = jnp.sum(grad_pre, axis=0)[None, :]
-    enc_grad = encoder_gradient(resid_half, resid_other, grad_pre.astype(BF16), half)
+    enc_grad = times(resid_turned, grad_pre.astype(BF16)).astype(BF16)
     return errors[None], enc_grad[None], bias_grad
 
 

time: 73.8 us -> 75.9 us (1.028)
  waiting for transfers between devices: 17.1 us -> 27.6 us
  starting transfers between devices: 35.2 us -> 31.4 us
  local copies, waits for them, and re-layouts: 4.46 us -> 1.91 us
  other arithmetic: 7.2 us -> 4.69 us
    ppermute x27, waiting for transfers between devices: 17.1 us -> 27.6 us  [crossed(): lax.ppermute(block, axis, [(i, i ^ mask) for i in range(lax.axis_size(axi...]
    ppermute x27, starting transfers between devices: 35.2 us -> 31.3 us  [crossed(): lax.ppermute(block, axis, [(i, i ^ mask) for i in range(lax.axis_size(axi...]
    dot_general x7 -> x8, matrix products: 2.28 us -> 4.15 us  [times(): return jnp.dot(left, right, preferred_element_type=F32)]
    squeeze x2, local copies, waits for them, and re-layouts: 1.64 us -> 0.08 us  [decoder_part(): lax.dynamic_slice(decoder, (which, 0, where * part), (1, 2 * latents, part))]
    dot_general x1 -> x0, matrix products: 1.36 us -> none  [encoder_gradient(): lax.dot_general(whole, grad_low, (((0,), (0,)), ((), ())), preferred_elem...]
    unnamed x21, local copies, waits for them, and re-layouts: 1.04 us -> 0.14 us
  transfers between devices with their start and end apart: 28 -> 28, of which waited for: 9 -> 13; matrix products, arithmetic and copies ran while one was open for 19% -> 10% of each run, Pallas kernels for 3% -> 3%
where the time goes in v6:
time: 75.9 us; the launch traced here: 75.4 us
  starting transfers between devices  31.4 us (41%)
  waiting for transfers between devices  27.6 us (36%)
  matrix products  5.34 us (7%)
  other arithmetic  4.69 us (6%)
  between operations  2.39 us (3%)
  Pallas kernels  2.11 us (3%)
  local copies, waits for them, and re-layouts  1.91 us (3%)
    ppermute x27, starting transfers between devices, crossed(): lax.ppermute(block, axis, [(i, i ^ mask) for i in range(lax.axis_size(axi...  31.3 us
    ppermute x27, waiting for transfers between devices, crossed(): lax.ppermute(block, axis, [(i, i ^ mask) for i in range(lax.axis_size(axi...  27.6 us
    dot_general x8, matrix products, times(): return jnp.dot(left, right, preferred_element_type=F32)  4.15 us
    pallas_call x1, Pallas kernels, paired_weights(): pl.pallas_call(side_by_side, out_shape=jax.ShapeDtypeStruct((cols, 2 * la...  2.11 us
    select_n x5, other arithmetic, ordered(): jnp.where(which == 0, lower, upper)  1.67 us
  transfers between devices with their start and end apart: 28, of which 13 were waited for; matrix products, arithmetic and copies ran while one was open for 10% of the time, Pallas kernels for 3%

profile of v6, /device:TPU:0, one launch (start us, length us, event | category | flops | bytes accessed | tf_op | source)
XLA Modules:
  0.0 75.4 jit_solution(14510787326941642417)
XLA Ops:
  0.6 0.0 copy-start
  0.6 0.5 collective-permute-start.2
  1.2 0.9 %dynamic-slice_bitcast_fusion.2 = bf16[16,1792]{1,0:T(8,128)(2,1)S(1)} fusion(bf16[2,16,3584]{2,1,0:T(8,128)(2,1)} %param.6, s32[]{:T(128)S(6)} %select_n.291, s32[]{:T(128)S(6)} %select_n.293), kind=kLoop, calls=%fused_computation.51 | loop fusion | bytes 114696 | tf_op jit(solution)/shard_map/squeeze | solution.py:124
  2.0 2.6 %collective-permute-start.1 = (bf16[16,1792]{1,0:T(8,128)(2,1)S(1)}, bf16[16,1792]{1,0:T(8,128)(2,1)S(1)}, u32[]{:S(2)}, u32[]{:S(2)}) collective-permute-start(bf16[16,1792]{1,0:T(8,128)(2,1)S(1)} %dynamic-slice_bitcast_fusion.2), channel_id=1, source_target_pairs={{0,1},{1,0},{2,3},{3,2},{4,5},{5,4},{6,7},{7,6},{8,9},{9,8},{10,11... | collective-permute-start | bytes 172040 | tf_op jit(solution)/shard_map/ppermute | solution.py:13
  4.7 0.5 collective-permute-start
  5.2 1.9 %collective-permute-done.1 = bf16[16,1792]{1,0:T(8,128)(2,1)S(1)} collective-permute-done((bf16[16,1792]{1,0:T(8,128)(2,1)S(1)}, bf16[16,1792]{1,0:T(8,128)(2,1)S(1)}, u32[]{:S(2)}, u32[]{:S(2)}) %collective-permute-start.1) | collective-permute-done | bytes 57376 | tf_op jit(solution)/shard_map/ppermute | solution.py:13
  7.1 0.8 %broadcast_select_fusion.5 = (bf16[16,1792]{1,0:T(8,128)(2,1)S(1)}, bf16[16,1792]{1,0:T(8,128)(2,1)S(1)}) fusion(bf16[16,1792]{1,0:T(8,128)(2,1)S(1)} %collective-permute-done.1, pred[]{:T(512)S(6)} %eq.79, bf16[2,16,3584]{2,1,0:T(8,128)(2,1)} %param.6, s32[]{:T(128)S(6)} %select_n.291, s32[]{:T(128)S(6)} %select_n.293), kind=kLoop, calls=%fused_computation.53 | loop fusion | flops 57344 | bytes 229385 | tf_op jit(solution)/shard_map/jit(_where)/select_n | solution.py:117
  7.9 0.0 collective-permute-done.2.other_ref
  7.9 3.9 %collective-permute-start.5 = (bf16[32,1792]{1,0:T(8,128)(2,1)S(1)}, bf16[32,1792]{1,0:T(8,128)(2,1)S(1)}, u32[]{:S(2)}, u32[]{:S(2)}) collective-permute-start(bf16[32,1792]{1,0:T(8,128)(2,1)S(1)} %pad_maximum_fusion.2), channel_id=1, source_target_pairs={{0,6},{1,7},{2,4},{3,5},{4,2},{5,3},{6,0},{7,1},{8,14},{9,15},{10,... | collective-permute-start | bytes 344072 | tf_op jit(solution)/shard_map/ppermute | solution.py:13
  11.9 0.0 collective-permute-start.4
  11.9 0.6 collective-permute-start.3
  12.5 2.1 %paired_weights.1 = bf16[1792,256]{1,0:T(8,128)(2,1)} custom-call(s32[1]{0:T(128)} %bitcast.5.half_ref, bf16[3584,128]{1,0:T(8,128)(2,1)} %bitcast.105, bf16[3584,128]{1,0:T(8,128)(2,1)} %collective-permute-done.2.other_ref), custom_call_target="tpu_custom_call" | custom-call | flops 20000000000 | bytes 1835008 | tf_op jit(solution)/shard_map/paired_weights/pallas_call | solution.py:55
  14.6 0.0 copy-start.2
  14.7 2.6 %collective-permute-done = bf16[256,896]{1,0:T(8,128)(2,1)S(1)} collective-permute-done((bf16[256,896]{1,0:T(8,128)(2,1)S(1)}, bf16[256,896]{1,0:T(8,128)(2,1)S(1)}, u32[]{:S(2)}, u32[]{:S(2)}) %collective-permute-start) | collective-permute-done | bytes 458784 | tf_op jit(solution)/shard_map/ppermute | solution.py:13
  17.2 0.0 collective-permute-done.5
  17.2 3.7 %collective-permute-done.4 = bf16[32,1792]{1,0:T(8,128)(2,1)S(1)} collective-permute-done((bf16[32,1792]{1,0:T(8,128)(2,1)S(1)}, bf16[32,1792]{1,0:T(8,128)(2,1)S(1)}, u32[]{:S(2)}, u32[]{:S(2)}) %collective-permute-start.4) | collective-permute-done | bytes 114720 | tf_op jit(solution)/shard_map/ppermute | solution.py:13
  21.0 1.5 %convolution_add_fusion.5 = f32[128,256]{1,0:T(8,128)S(1)} fusion(bf16[128,1792]{1,0:T(8,128)(2,1)S(1)} %constant_dynamic-update-slice_fusion, bf16[1792,256]{1,0:T(8,128)(2,1)} %paired_weights.1, f32[256]{0:T(256)S(1)} %pad_maximum_fusion.7), kind=kOutput, calls=%fused_computation.8 | convolution fusion | flops 117473280 | bytes 1508352 | tf_op jit(solution)/shard_map/dot_general | solution.py:17
  22.4 0.1 collective-permute-start.6
  22.6 0.6 compare_reduce_fusion
  24.6 1.6 %collective-permute-start.8 = (bf16[256,896]{1,0:T(8,128)(2,1)S(1)}, bf16[256,896]{1,0:T(8,128)(2,1)S(1)}, u32[]{:S(2)}, u32[]{:S(2)}) collective-permute-start(bf16[256,896]{1,0:T(8,128)(2,1)S(1)} %dynamic-slice_bitcast_fusion), channel_id=1, source_target_pairs={{0,1},{1,0},{2,3},{3,2},{4,5},{5,4},{6,7},{7,6},{8,9},{9,8},{10,11... | collective-permute-start | bytes 1376264 | tf_op jit(solution)/shard_map/ppermute | solution.py:13
  26.2 0.6 collective-permute-start.7
  26.8 0.8 %constant_dynamic-slice_fusion.1 = (bf16[1,16,896]{2,1,0:T(8,128)(2,1)S(1)}, bf16[1,16,896]{2,1,0:T(8,128)(2,1)S(1)}) fusion(bf16[3,16,3584]{2,1,0:T(8,128)(2,1)} %param.7, s32[]{:T(128)S(6)} %select_n.301, s32[]{:T(128)S(6)} %select_n.313), kind=kLoop, calls=%fused_computation.90 | loop fusion | bytes 114696 | tf_op jit(solution)/shard_map/dynamic_slice | solution.py:136
  27.6 1.6 %collective-permute-start.13 = (bf16[2,16,896]{2,1,0:T(8,128)(2,1)S(1)}, bf16[2,16,896]{2,1,0:T(8,128)(2,1)S(1)}, u32[]{:S(2)}, u32[]{:S(2)}) collective-permute-start(bf16[2,16,896]{2,1,0:T(8,128)(2,1)S(1)} %pad_maximum_fusion.4), channel_id=1, source_target_pairs={{0,1},{1,0},{2,3},{3,2},{4,5},{5,4},{6,7},{7,6},{8,9},{9,8},{10,11... | collective-permute-start | bytes 172040 | tf_op jit(solution)/shard_map/ppermute | solution.py:13
  29.2 0.2 fusion.6
  29.4 0.2 fusion.4
  29.6 9.8 %collective-permute-done.7 = bf16[128,256]{1,0:T(8,128)(2,1)S(1)} collective-permute-done((bf16[128,256]{1,0:T(8,128)(2,1)S(1)}, bf16[128,256]{1,0:T(8,128)(2,1)S(1)}, u32[]{:S(2)}, u32[]{:S(2)}) %collective-permute-start.7) | collective-permute-done | bytes 65568 | tf_op jit(solution)/shard_map/ppermute | solution.py:13
  39.4 0.2 fusion.1
  39.6 1.6 %collective-permute-start.12 = (bf16[64,896]{1,0:T(8,128)(2,1)S(1)}, bf16[64,896]{1,0:T(8,128)(2,1)S(1)}, u32[]{:S(2)}, u32[]{:S(2)}) collective-permute-start(bf16[64,896]{1,0:T(8,128)(2,1)S(1)} %fusion.1), channel_id=1, source_target_pairs={{0,16},{8,24},{16,0},{24,8},{1,17},{9,25},{17,1},{25,9},{2,18},{10... | collective-permute-start | bytes 344072 | tf_op jit(solution)/shard_map/ppermute | solution.py:13
  41.2 0.2 fusion.38
  41.5 0.2 fusion.37
  41.7 2.5 %collective-permute-start.9 = (bf16[32,896]{1,0:T(8,128)(2,1)S(1)}, bf16[32,896]{1,0:T(8,128)(2,1)S(1)}, u32[]{:S(2)}, u32[]{:S(2)}) collective-permute-start(bf16[32,896]{1,0:T(8,128)(2,1)S(1)} %get-tuple-element.59), channel_id=1, source_target_pairs={{0,6},{1,7},{2,4},{3,5},{4,2},{5,3},{6,0},{7,1},{8,14},{9,15},{10,... | collective-permute-start | bytes 172040 | tf_op jit(solution)/shard_map/ppermute | solution.py:13
  44.3 0.2 convolution_add_fusion.1
  44.6 2.6 %collective-permute-start.14 = (bf16[16,896]{1,0:T(8,128)(2,1)S(1)}, bf16[16,896]{1,0:T(8,128)(2,1)S(1)}, u32[]{:S(2)}, u32[]{:S(2)}) collective-permute-start(bf16[16,896]{1,0:T(8,128)(2,1)S(1)} %get-tuple-element.62), channel_id=1, source_target_pairs={{0,6},{1,7},{2,4},{3,5},{4,2},{5,3},{6,0},{7,1},{8,14},{9,15},{10,... | collective-permute-start | bytes 86024 | tf_op jit(solution)/shard_map/ppermute | solution.py:13
  47.2 1.8 %collective-permute-start.15 = (bf16[16,896]{1,0:T(8,128)(2,1)S(1)}, bf16[16,896]{1,0:T(8,128)(2,1)S(1)}, u32[]{:S(2)}, u32[]{:S(2)}) collective-permute-start(bf16[16,896]{1,0:T(8,128)(2,1)S(1)} %get-tuple-element.64), channel_id=1, source_target_pairs={{0,4},{1,5},{2,6},{3,7},{4,0},{5,1},{6,2},{7,3},{8,12},{9,13},{10,... | collective-permute-start | bytes 86024 | tf_op jit(solution)/shard_map/ppermute | solution.py:13
  49.0 0.8 %select_bitcast_fusion.1 = (bf16[16,896]{1,0:T(8,128)(2,1)S(1)}, bf16[16,896]{1,0:T(8,128)(2,1)S(1)}) fusion(pred[]{:T(512)S(6)} %eq.79, bf16[2,16,896]{2,1,0:T(8,128)(2,1)S(1)} %collective-permute-done.13, bf16[3,16,3584]{2,1,0:T(8,128)(2,1)} %param.7, s32[]{:T(128)S(6)} %select_n.301, s32[]{:T(128)S(6)} %select_n.302), kind=kLoop, calls=%fused_computation.85 | loop fusion | flops 28672 | bytes 114697 | tf_op jit(solution)/shard_map/jit(_where)/select_n | solution.py:117
  49.8 0.5 collective-permute-done.14
  50.3 0.6 collective-permute-start.10
  51.0 0.1 collective-permute-done.16
  51.1 1.7 %collective-permute-done.15 = bf16[16,896]{1,0:T(8,128)(2,1)S(1)} collective-permute-done((bf16[16,896]{1,0:T(8,128)(2,1)S(1)}, bf16[16,896]{1,0:T(8,128)(2,1)S(1)}, u32[]{:S(2)}, u32[]{:S(2)}) %collective-permute-start.15) | collective-permute-done | bytes 28704 | tf_op jit(solution)/shard_map/ppermute | solution.py:13
  52.8 0.8 %fusion.22 = bf16[16,896]{1,0:T(8,128)(2,1)S(1)} fusion(f32[64,896]{1,0:T(8,128)S(1)} %get-tuple-element.50, bf16[16,896]{1,0:T(8,128)(2,1)S(1)} %collective-permute-done.16, bf16[16,896]{1,0:T(8,128)(2,1)S(1)} %collective-permute-done.15, bf16[16,896]{1,0:T(8,128)(2,1)S(1)} %collective-permute-done.14, bf16[2,16,896]{2,1,0:T(8,128)(2,1)S(1)} %collective-permute-done.13, ...), kind=kLoop, calls=%fused_computation.48 | loop fusion | flops 143360 | bytes 229381 | tf_op jit(solution)/shard_map/convert_element_type | solution.py:162
  53.6 2.2 %collective-permute-start.19 = (bf16[16,896]{1,0:T(8,128)(2,1)S(1)}, bf16[16,896]{1,0:T(8,128)(2,1)S(1)}, u32[]{:S(2)}, u32[]{:S(2)}) collective-permute-start(bf16[16,896]{1,0:T(8,128)(2,1)S(1)} %fusion.22), channel_id=1, source_target_pairs={{0,6},{1,7},{2,4},{3,5},{4,2},{5,3},{6,0},{7,1},{8,14},{9,15},{10,... | collective-permute-start | bytes 86024 | tf_op jit(solution)/shard_map/ppermute | solution.py:13
  55.8 0.5 collective-permute-start.18
  56.3 1.7 %collective-permute-start.17 = (bf16[16,896]{1,0:T(8,128)(2,1)S(1)}, bf16[16,896]{1,0:T(8,128)(2,1)S(1)}, u32[]{:S(2)}, u32[]{:S(2)}) collective-permute-start(bf16[16,896]{1,0:T(8,128)(2,1)S(1)} %fusion.22), channel_id=1, source_target_pairs={{0,2},{1,3},{2,0},{3,1},{4,6},{5,7},{6,4},{7,5},{8,10},{9,11},{10,... | collective-permute-start | bytes 86024 | tf_op jit(solution)/shard_map/ppermute | solution.py:13
  58.1 2.2 %collective-permute-start.24 = (bf16[32,896]{1,0:T(8,128)(2,1)S(1)}, bf16[32,896]{1,0:T(8,128)(2,1)S(1)}, u32[]{:S(2)}, u32[]{:S(2)}) collective-permute-start(bf16[32,896]{1,0:T(8,128)(2,1)S(1)} %fusion.18), channel_id=1, source_target_pairs={{0,6},{1,7},{2,4},{3,5},{4,2},{5,3},{6,0},{7,1},{8,14},{9,15},{10,... | collective-permute-start | bytes 172040 | tf_op jit(solution)/shard_map/ppermute | solution.py:13
  60.3 1.8 %collective-permute-done.18 = bf16[16,896]{1,0:T(8,128)(2,1)S(1)} collective-permute-done((bf16[16,896]{1,0:T(8,128)(2,1)S(1)}, bf16[16,896]{1,0:T(8,128)(2,1)S(1)}, u32[]{:S(2)}, u32[]{:S(2)}) %collective-permute-start.18) | collective-permute-done | bytes 28704 | tf_op jit(solution)/shard_map/ppermute | solution.py:13
  62.1 0.4 collective-permute-start.22
  62.6 1.0 %collective-permute-start.21 = (bf16[64,896]{1,0:T(8,128)(2,1)S(1)}, bf16[64,896]{1,0:T(8,128)(2,1)S(1)}, u32[]{:S(2)}, u32[]{:S(2)}) collective-permute-start(bf16[64,896]{1,0:T(8,128)(2,1)S(1)} %pad_maximum_fusion.3), channel_id=1, source_target_pairs={{0,16},{8,24},{16,0},{24,8},{1,17},{9,25},{17,1},{25,9},{2,18},{10... | collective-permute-start | bytes 344072 | tf_op jit(solution)/shard_map/ppermute | solution.py:13
  63.5 0.6 collective-permute-done.24
  64.2 1.2 %collective-permute-done.23 = bf16[32,896]{1,0:T(8,128)(2,1)S(1)} collective-permute-done((bf16[32,896]{1,0:T(8,128)(2,1)S(1)}, bf16[32,896]{1,0:T(8,128)(2,1)S(1)}, u32[]{:S(2)}, u32[]{:S(2)}) %collective-permute-start.23) | collective-permute-done | bytes 57376 | tf_op jit(solution)/shard_map/ppermute | solution.py:13
  65.4 0.9 %collective-permute-done.22 = bf16[32,896]{1,0:T(8,128)(2,1)S(1)} collective-permute-done((bf16[32,896]{1,0:T(8,128)(2,1)S(1)}, bf16[32,896]{1,0:T(8,128)(2,1)S(1)}, u32[]{:S(2)}, u32[]{:S(2)}) %collective-permute-start.22) | collective-permute-done | bytes 57376 | tf_op jit(solution)/shard_map/ppermute | solution.py:13
  66.3 0.3 fusion.23
  66.6 0.1 broadcast_select_fusion.1
  66.7 0.1 maximum_bitcast_fusion
  66.8 0.6 collective-permute-done.21
  67.5 0.3 fusion.2
  67.8 0.3 convolution_add_fusion.4
  68.2 0.1 collective-permute-start.27
  68.4 1.5 %collective-permute-start.25 = (bf16[240,128]{1,0:T(8,128)(2,1)S(1)}, bf16[240,128]{1,0:T(8,128)(2,1)S(1)}, u32[]{:S(2)}, u32[]{:S(2)}) collective-permute-start(bf16[240,128]{1,0:T(8,128)(2,1)S(1)} %constant_dynamic-update-slice_fusion.4), channel_id=1, source_target_pairs={{0,1},{1,0},{2,3},{3,2},{4,5},{5,4},{6,7},{7,6},{8,9},{9,8},{10,11... | collective-permute-start | bytes 184328 | tf_op jit(solution)/shard_map/ppermute | solution.py:13
  69.9 0.3 convolution_add_fusion.3
  70.2 0.4 collective-permute-start.26
  70.6 2.1 %collective-permute-done.25 = bf16[240,128]{1,0:T(8,128)(2,1)S(1)} collective-permute-done((bf16[240,128]{1,0:T(8,128)(2,1)S(1)}, bf16[240,128]{1,0:T(8,128)(2,1)S(1)}, u32[]{:S(2)}, u32[]{:S(2)}) %collective-permute-start.25) | collective-permute-done | bytes 61472 | tf_op jit(solution)/shard_map/ppermute | solution.py:13
  72.9 0.6 maximum_bitcast_fusion.1
  73.5 0.6 fusion.33
  74.0 1.4 %fusion = bf16[1,3584,128]{2,1,0:T(8,128)(2,1)} fusion(bf16[3584,128]{0,1:T(8,128)(2,1)S(1)} %maximum_bitcast_fusion, bf16[128,128]{1,0:T(8,128)(2,1)S(1)} %get-tuple-element.46), kind=kOutput, calls=%fused_computation.1 | convolution fusion | flops 117899264 | bytes 1867776 | tf_op jit(solution)/shard_map/dot_general | solution.py:17
  (62 shorter events, 0.6 us)
Async XLA Ops:
  0.6 4.0 %copy-start = (bf16[1,2,2,128,1792]{4,3,2,1,0:T(8,128)(2,1)S(1)}, bf16[1,2,2,128,1792]{4,3,2,1,0:T(8,128)(2,1)}, u32[]{:S(2)}) copy-start(bf16[1,2,2,128,1792]{4,3,2,1,0:T(8,128)(2,1)} %param.10) | copy-start | bytes 5505028
  0.6 7.3 %collective-permute-start.2 = (bf16[3584,128]{1,0:T(8,128)(2,1)}, bf16[3584,128]{1,0:T(8,128)(2,1)}, u32[]{:S(2)}, u32[]{:S(2)}) collective-permute-start(bf16[3584,128]{1,0:T(8,128)(2,1)} %bitcast.104), channel_id=1, source_target_pairs={{0,8},{8,0},{16,24},{24,16},{1,9},{9,1},{17,25},{25,17},{2,10},{10... | collective-permute-start | bytes 2752520 | tf_op jit(solution)/shard_map/ppermute | solution.py:13
  2.0 5.0 %collective-permute-start.1 = (bf16[16,1792]{1,0:T(8,128)(2,1)S(1)}, bf16[16,1792]{1,0:T(8,128)(2,1)S(1)}, u32[]{:S(2)}, u32[]{:S(2)}) collective-permute-start(bf16[16,1792]{1,0:T(8,128)(2,1)S(1)} %dynamic-slice_bitcast_fusion.2), channel_id=1, source_target_pairs={{0,1},{1,0},{2,3},{3,2},{4,5},{5,4},{6,7},{7,6},{8,9},{9,8},{10,11... | collective-permute-start | bytes 172040 | tf_op jit(solution)/shard_map/ppermute | solution.py:13
  4.7 12.6 %collective-permute-start = (bf16[256,896]{1,0:T(8,128)(2,1)S(1)}, bf16[256,896]{1,0:T(8,128)(2,1)S(1)}, u32[]{:S(2)}, u32[]{:S(2)}) collective-permute-start(bf16[256,896]{1,0:T(8,128)(2,1)S(1)} %dynamic-slice_bitcast_fusion.1), channel_id=1, source_target_pairs={{0,1},{1,0},{2,3},{3,2},{4,5},{5,4},{6,7},{7,6},{8,9},{9,8},{10,11... | collective-permute-start | bytes 1376264 | tf_op jit(solution)/shard_map/ppermute | solution.py:13
  7.9 9.3 %collective-permute-start.5 = (bf16[32,1792]{1,0:T(8,128)(2,1)S(1)}, bf16[32,1792]{1,0:T(8,128)(2,1)S(1)}, u32[]{:S(2)}, u32[]{:S(2)}) collective-permute-start(bf16[32,1792]{1,0:T(8,128)(2,1)S(1)} %pad_maximum_fusion.2), channel_id=1, source_target_pairs={{0,6},{1,7},{2,4},{3,5},{4,2},{5,3},{6,0},{7,1},{8,14},{9,15},{10,... | collective-permute-start | bytes 344072 | tf_op jit(solution)/shard_map/ppermute | solution.py:13
  11.9 9.0 %collective-permute-start.4 = (bf16[32,1792]{1,0:T(8,128)(2,1)S(1)}, bf16[32,1792]{1,0:T(8,128)(2,1)S(1)}, u32[]{:S(2)}, u32[]{:S(2)}) collective-permute-start(bf16[32,1792]{1,0:T(8,128)(2,1)S(1)} %pad_maximum_fusion.2), channel_id=1, source_target_pairs={{0,4},{1,5},{2,6},{3,7},{4,0},{5,1},{6,2},{7,3},{8,12},{9,13},{10,... | collective-permute-start | bytes 344072 | tf_op jit(solution)/shard_map/ppermute | solution.py:13
  11.9 9.0 %collective-permute-start.3 = (bf16[32,1792]{1,0:T(8,128)(2,1)S(1)}, bf16[32,1792]{1,0:T(8,128)(2,1)S(1)}, u32[]{:S(2)}, u32[]{:S(2)}) collective-permute-start(bf16[32,1792]{1,0:T(8,128)(2,1)S(1)} %pad_maximum_fusion.2), channel_id=1, source_target_pairs={{0,2},{1,3},{2,0},{3,1},{4,6},{5,7},{6,4},{7,5},{8,10},{9,11},{10,... | collective-permute-start | bytes 344072 | tf_op jit(solution)/shard_map/ppermute | solution.py:13
  12.5 2.1 %copy-start.1 = (f32[1,128]{1,0:T(1,128)S(1)}, f32[1,128]{1,0:T(1,128)}, u32[]{:S(2)}) copy-start(f32[1,128]{1,0:T(1,128)} %param.9) | copy-start | bytes 1540
  14.6 7.9 %copy-start.2 = (s32[2,1,12]{2,1,0:T(1,128)S(1)}, s32[2,1,12]{2,1,0:T(1,128)}, u32[]{:S(2)}) copy-start(s32[2,1,12]{2,1,0:T(1,128)} %param.11) | copy-start | bytes 292
  22.4 3.7 %collective-permute-start.6 = (f32[128,256]{1,0:T(8,128)S(1)}, f32[128,256]{1,0:T(8,128)S(1)}, u32[]{:S(2)}, u32[]{:S(2)}) collective-permute-start(f32[128,256]{1,0:T(8,128)S(1)} %convolution_add_fusion.5), channel_id=1, source_target_pairs={{0,8},{8,0},{16,24},{24,16},{1,9},{9,1},{17,25},{25,17},{2,10},{10... | collective-permute-start | bytes 393224 | tf_op jit(solution)/shard_map/ppermute | solution.py:13
  24.6 14.8 %collective-permute-start.8 = (bf16[256,896]{1,0:T(8,128)(2,1)S(1)}, bf16[256,896]{1,0:T(8,128)(2,1)S(1)}, u32[]{:S(2)}, u32[]{:S(2)}) collective-permute-start(bf16[256,896]{1,0:T(8,128)(2,1)S(1)} %dynamic-slice_bitcast_fusion), channel_id=1, source_target_pairs={{0,1},{1,0},{2,3},{3,2},{4,5},{5,4},{6,7},{7,6},{8,9},{9,8},{10,11... | collective-permute-start | bytes 1376264 | tf_op jit(solution)/shard_map/ppermute | solution.py:13
  26.2 13.2 %collective-permute-start.7 = (bf16[128,256]{1,0:T(8,128)(2,1)S(1)}, bf16[128,256]{1,0:T(8,128)(2,1)S(1)}, u32[]{:S(2)}, u32[]{:S(2)}) collective-permute-start(bf16[128,256]{1,0:T(8,128)(2,1)S(1)} %multiply_convert_fusion), channel_id=1, source_target_pairs={{0,1},{1,0},{2,3},{3,2},{4,5},{5,4},{6,7},{7,6},{8,9},{9,8},{10,11... | collective-permute-start | bytes 196616 | tf_op jit(solution)/shard_map/ppermute | solution.py:13
  27.6 16.9 %collective-permute-start.13 = (bf16[2,16,896]{2,1,0:T(8,128)(2,1)S(1)}, bf16[2,16,896]{2,1,0:T(8,128)(2,1)S(1)}, u32[]{:S(2)}, u32[]{:S(2)}) collective-permute-start(bf16[2,16,896]{2,1,0:T(8,128)(2,1)S(1)} %pad_maximum_fusion.4), channel_id=1, source_target_pairs={{0,1},{1,0},{2,3},{3,2},{4,5},{5,4},{6,7},{7,6},{8,9},{9,8},{10,11... | collective-permute-start | bytes 172040 | tf_op jit(solution)/shard_map/ppermute | solution.py:13
  39.6 4.9 %collective-permute-start.12 = (bf16[64,896]{1,0:T(8,128)(2,1)S(1)}, bf16[64,896]{1,0:T(8,128)(2,1)S(1)}, u32[]{:S(2)}, u32[]{:S(2)}) collective-permute-start(bf16[64,896]{1,0:T(8,128)(2,1)S(1)} %fusion.1), channel_id=1, source_target_pairs={{0,16},{8,24},{16,0},{24,8},{1,17},{9,25},{17,1},{25,9},{2,18},{10... | collective-permute-start | bytes 344072 | tf_op jit(solution)/shard_map/ppermute | solution.py:13
  41.7 14.1 %collective-permute-start.9 = (bf16[32,896]{1,0:T(8,128)(2,1)S(1)}, bf16[32,896]{1,0:T(8,128)(2,1)S(1)}, u32[]{:S(2)}, u32[]{:S(2)}) collective-permute-start(bf16[32,896]{1,0:T(8,128)(2,1)S(1)} %get-tuple-element.59), channel_id=1, source_target_pairs={{0,6},{1,7},{2,4},{3,5},{4,2},{5,3},{6,0},{7,1},{8,14},{9,15},{10,... | collective-permute-start | bytes 172040 | tf_op jit(solution)/shard_map/ppermute | solution.py:13
  44.3 12.1 %collective-permute-start.11 = (bf16[32,896]{1,0:T(8,128)(2,1)S(1)}, bf16[32,896]{1,0:T(8,128)(2,1)S(1)}, u32[]{:S(2)}, u32[]{:S(2)}) collective-permute-start(bf16[32,896]{1,0:T(8,128)(2,1)S(1)} %get-tuple-element.60), channel_id=1, source_target_pairs={{0,2},{1,3},{2,0},{3,1},{4,6},{5,7},{6,4},{7,5},{8,10},{9,11},{10,... | collective-permute-start | bytes 172040 | tf_op jit(solution)/shard_map/ppermute | solution.py:13
  44.6 5.8 %collective-permute-start.14 = (bf16[16,896]{1,0:T(8,128)(2,1)S(1)}, bf16[16,896]{1,0:T(8,128)(2,1)S(1)}, u32[]{:S(2)}, u32[]{:S(2)}) collective-permute-start(bf16[16,896]{1,0:T(8,128)(2,1)S(1)} %get-tuple-element.62), channel_id=1, source_target_pairs={{0,6},{1,7},{2,4},{3,5},{4,2},{5,3},{6,0},{7,1},{8,14},{9,15},{10,... | collective-permute-start | bytes 86024 | tf_op jit(solution)/shard_map/ppermute | solution.py:13
  47.2 3.9 %collective-permute-start.16 = (bf16[16,896]{1,0:T(8,128)(2,1)S(1)}, bf16[16,896]{1,0:T(8,128)(2,1)S(1)}, u32[]{:S(2)}, u32[]{:S(2)}) collective-permute-start(bf16[16,896]{1,0:T(8,128)(2,1)S(1)} %get-tuple-element.63), channel_id=1, source_target_pairs={{0,2},{1,3},{2,0},{3,1},{4,6},{5,7},{6,4},{7,5},{8,10},{9,11},{10,... | collective-permute-start | bytes 86024 | tf_op jit(solution)/shard_map/ppermute | solution.py:13
  47.2 5.6 %collective-permute-start.15 = (bf16[16,896]{1,0:T(8,128)(2,1)S(1)}, bf16[16,896]{1,0:T(8,128)(2,1)S(1)}, u32[]{:S(2)}, u32[]{:S(2)}) collective-permute-start(bf16[16,896]{1,0:T(8,128)(2,1)S(1)} %get-tuple-element.64), channel_id=1, source_target_pairs={{0,4},{1,5},{2,6},{3,7},{4,0},{5,1},{6,2},{7,3},{8,12},{9,13},{10,... | collective-permute-start | bytes 86024 | tf_op jit(solution)/shard_map/ppermute | solution.py:13
  50.3 7.7 %collective-permute-start.10 = (bf16[32,896]{1,0:T(8,128)(2,1)S(1)}, bf16[32,896]{1,0:T(8,128)(2,1)S(1)}, u32[]{:S(2)}, u32[]{:S(2)}) collective-permute-start(bf16[32,896]{1,0:T(8,128)(2,1)S(1)} %get-tuple-element.61), channel_id=1, source_target_pairs={{0,4},{1,5},{2,6},{3,7},{4,0},{5,1},{6,2},{7,3},{8,12},{9,13},{10,... | collective-permute-start | bytes 172040 | tf_op jit(solution)/shard_map/ppermute | solution.py:13
  51.1 15.5 %collective-permute-start.20 = (bf16[128,1792]{1,0:T(8,128)(2,1)S(1)}, bf16[128,1792]{1,0:T(8,128)(2,1)S(1)}, u32[]{:S(2)}, u32[]{:S(2)}) collective-permute-start(bf16[128,1792]{1,0:T(8,128)(2,1)S(1)} %constant_dynamic-update-slice_fusion), channel_id=1, source_target_pairs={{0,8},{8,0},{16,24},{24,16},{1,9},{9,1},{17,25},{25,17},{2,10},{10... | collective-permute-start | bytes 1376264 | tf_op jit(solution)/shard_map/ppermute | solution.py:13
  53.6 6.7 %collective-permute-start.19 = (bf16[16,896]{1,0:T(8,128)(2,1)S(1)}, bf16[16,896]{1,0:T(8,128)(2,1)S(1)}, u32[]{:S(2)}, u32[]{:S(2)}) collective-permute-start(bf16[16,896]{1,0:T(8,128)(2,1)S(1)} %fusion.22), channel_id=1, source_target_pairs={{0,6},{1,7},{2,4},{3,5},{4,2},{5,3},{6,0},{7,1},{8,14},{9,15},{10,... | collective-permute-start | bytes 86024 | tf_op jit(solution)/shard_map/ppermute | solution.py:13
  55.8 6.3 %collective-permute-start.18 = (bf16[16,896]{1,0:T(8,128)(2,1)S(1)}, bf16[16,896]{1,0:T(8,128)(2,1)S(1)}, u32[]{:S(2)}, u32[]{:S(2)}) collective-permute-start(bf16[16,896]{1,0:T(8,128)(2,1)S(1)} %fusion.22), channel_id=1, source_target_pairs={{0,4},{1,5},{2,6},{3,7},{4,0},{5,1},{6,2},{7,3},{8,12},{9,13},{10,... | collective-permute-start | bytes 86024 | tf_op jit(solution)/shard_map/ppermute | solution.py:13
  56.3 6.2 %collective-permute-start.17 = (bf16[16,896]{1,0:T(8,128)(2,1)S(1)}, bf16[16,896]{1,0:T(8,128)(2,1)S(1)}, u32[]{:S(2)}, u32[]{:S(2)}) collective-permute-start(bf16[16,896]{1,0:T(8,128)(2,1)S(1)} %fusion.22), channel_id=1, source_target_pairs={{0,2},{1,3},{2,0},{3,1},{4,6},{5,7},{6,4},{7,5},{8,10},{9,11},{10,... | collective-permute-start | bytes 86024 | tf_op jit(solution)/shard_map/ppermute | solution.py:13
  58.1 6.1 %collective-permute-start.24 = (bf16[32,896]{1,0:T(8,128)(2,1)S(1)}, bf16[32,896]{1,0:T(8,128)(2,1)S(1)}, u32[]{:S(2)}, u32[]{:S(2)}) collective-permute-start(bf16[32,896]{1,0:T(8,128)(2,1)S(1)} %fusion.18), channel_id=1, source_target_pairs={{0,6},{1,7},{2,4},{3,5},{4,2},{5,3},{6,0},{7,1},{8,14},{9,15},{10,... | collective-permute-start | bytes 172040 | tf_op jit(solution)/shard_map/ppermute | solution.py:13
  60.3 5.1 %collective-permute-start.23 = (bf16[32,896]{1,0:T(8,128)(2,1)S(1)}, bf16[32,896]{1,0:T(8,128)(2,1)S(1)}, u32[]{:S(2)}, u32[]{:S(2)}) collective-permute-start(bf16[32,896]{1,0:T(8,128)(2,1)S(1)} %fusion.18), channel_id=1, source_target_pairs={{0,4},{1,5},{2,6},{3,7},{4,0},{5,1},{6,2},{7,3},{8,12},{9,13},{10,... | collective-permute-start | bytes 172040 | tf_op jit(solution)/shard_map/ppermute | solution.py:13
  62.1 4.2 %collective-permute-start.22 = (bf16[32,896]{1,0:T(8,128)(2,1)S(1)}, bf16[32,896]{1,0:T(8,128)(2,1)S(1)}, u32[]{:S(2)}, u32[]{:S(2)}) collective-permute-start(bf16[32,896]{1,0:T(8,128)(2,1)S(1)} %fusion.18), channel_id=1, source_target_pairs={{0,2},{1,3},{2,0},{3,1},{4,6},{5,7},{6,4},{7,5},{8,10},{9,11},{10,... | collective-permute-start | bytes 172040 | tf_op jit(solution)/shard_map/ppermute | solution.py:13
  62.6 4.9 %collective-permute-start.21 = (bf16[64,896]{1,0:T(8,128)(2,1)S(1)}, bf16[64,896]{1,0:T(8,128)(2,1)S(1)}, u32[]{:S(2)}, u32[]{:S(2)}) collective-permute-start(bf16[64,896]{1,0:T(8,128)(2,1)S(1)} %pad_maximum_fusion.3), channel_id=1, source_target_pairs={{0,16},{8,24},{16,0},{24,8},{1,17},{9,25},{17,1},{25,9},{2,18},{10... | collective-permute-start | bytes 344072 | tf_op jit(solution)/shard_map/ppermute | solution.py:13
  68.2 5.3 %collective-permute-start.27 = (bf16[128,128]{1,0:T(8,128)(2,1)S(1)}, bf16[128,128]{1,0:T(8,128)(2,1)S(1)}, u32[]{:S(2)}, u32[]{:S(2)}) collective-permute-start(bf16[128,128]{1,0:T(8,128)(2,1)S(1)} %get-tuple-element.67), channel_id=1, source_target_pairs={{0,9},{1,8},{2,11},{3,10},{4,13},{5,12},{6,15},{7,14},{8,1},{9,0},... | collective-permute-start | bytes 98312 | tf_op jit(solution)/shard_map/ppermute | solution.py:189
  68.4 4.4 %collective-permute-start.25 = (bf16[240,128]{1,0:T(8,128)(2,1)S(1)}, bf16[240,128]{1,0:T(8,128)(2,1)S(1)}, u32[]{:S(2)}, u32[]{:S(2)}) collective-permute-start(bf16[240,128]{1,0:T(8,128)(2,1)S(1)} %constant_dynamic-update-slice_fusion.4), channel_id=1, source_target_pairs={{0,1},{1,0},{2,3},{3,2},{4,5},{5,4},{6,7},{7,6},{8,9},{9,8},{10,11... | collective-permute-start | bytes 184328 | tf_op jit(solution)/shard_map/ppermute | solution.py:13
  70.2 3.3 %collective-permute-start.26 = (f32[128,128]{1,0:T(8,128)S(1)}, f32[128,128]{1,0:T(8,128)S(1)}, u32[]{:S(2)}, u32[]{:S(2)}) collective-permute-start(f32[128,128]{1,0:T(8,128)S(1)} %slice_select_fusion), channel_id=1, source_target_pairs={{0,8},{8,0},{16,24},{24,16},{1,9},{9,1},{17,25},{25,17},{2,10},{10... | collective-permute-start | bytes 196616 | tf_op jit(solution)/shard_map/ppermute | solution.py:13

commit v7 on v4

--- a/solution.py
+++ b/solution.py
@@ -50,6 +50,7 @@
 
 
 def two_layers(resid, target, enc_weight, enc_bias, dec_weight, blocks):
+    hold = lax.optimization_barrier
     slots = lax.axis_size("latent")
     far = slots // 2
     layer, half = lax.axis_index("layer") // 2, lax.axis_index("layer") % 2
@@ -63,99 +64,105 @@
     def over_x(block):
         return crossed(block, "latent", 1)
 
+    def over_y(block):
+        return crossed(block, "layer", 2)
+
+    def over_core(block):
+        return crossed(block, "layer", 1)
+
     def along_z(block):
         out = [block] + [None] * (far - 1)
         for k in range(far - 1, 0, -1):
             out[k] = crossed(block, "latent", 2 * k)
         return out
 
+    def sent_along_z(total):
+        count = total.shape[0] // far
+        pieces = [total[k * count:(k + 1) * count].astype(BF16) for k in range(1, far)]
+        return [crossed(pieces[k - 1], "latent", 2 * k) for k in range(1, far)] + [total[:count]]
+
+    def added(terms):
+        return sum(term.astype(F32) for term in terms[::-1])
+
     def decoder_part(decoder, which, where):
         return lax.dynamic_slice(decoder, (which, 0, where * part), (1, 2 * latents, part))[0]
 
-    def turned(array):
-        return array.reshape(far, 2, rows, array.shape[1])[:, ::-1].reshape(array.shape)
-
-    weight_other = crossed(enc_weight[0], "layer", 1)
+    def ordered(which, lower, upper, axis=0):
+        return jnp.concatenate([jnp.where(which == 0, lower, upper), jnp.where(which == 0, upper, lower)], axis=axis)
+
+    def rows_at(array, which):
+        split = array.reshape(-1, 2, rows, array.shape[1])
+        return jnp.where(which == 0, split[:, 0], split[:, 1]).reshape(-1, array.shape[1])
+
+    weight_other = over_core(enc_weight[0])
     mine = lax.dynamic_slice(resid, (layer, 0, half * cols), (1, rows, cols))[0]
-    pair = jnp.concatenate([mine, over_x(mine)], axis=0)
-    pair, weight_other, later = lax.optimization_barrier((pair, weight_other, decoder))
+    pair, weight_other, bias, blocks = hold((ordered(side, mine, over_x(mine)), weight_other, enc_bias[0], blocks))
     column = along_z(pair)
 
-    shared_other = over_x(decoder_part(decoder, 1 - layer, 1 - side))
-    own_other = over_x(decoder_part(later, layer, 1 - side))
-    decoder, target, blocks, *column = lax.optimization_barrier((decoder, target, blocks, *column))
-    shared_mine, own_mine = decoder_part(decoder, 1 - layer, side), decoder_part(decoder, layer, side)
+    own_other = over_x(decoder_part(decoder, layer, 1 - side))
+    shared_other = over_y(decoder_part(decoder, 1 - layer, 1 - layer))
+    decoder, own_other, shared_other, *column = hold((decoder, own_other, shared_other, *column))
+    own_mine, shared_mine = decoder_part(decoder, layer, side), decoder_part(decoder, 1 - layer, layer)
     resid_half = jnp.concatenate(column, axis=0)
     firing = gates(blocks, layer, slot, slots, latents, tokens)
     gate = jnp.where(half == 0, firing[0], firing[1])
 
-    def aims_for(where):
-        start = half * cols + where * part
-        own = lax.dynamic_slice(target, (2 * layer, 0, start), (1, rows, part))
-        return jnp.concatenate([own, lax.dynamic_slice(target, (1, 0, start), (1, rows, part))], axis=0)
-
-    aims, aims_other = aims_for(side), over_x(aims_for(1 - side))
-    aim_own = jnp.concatenate([aims[0], aims_other[0]], axis=0).astype(F32)
-    aim_shared = jnp.where(layer == 0, aims[1], aims_other[1]).astype(F32)
-
-    partial = half_preacts(resid_half, enc_weight[0], weight_other, enc_bias[0], half)
-    acts = ((partial + crossed(partial, "layer", 1)) * jnp.concatenate(firing, axis=1)).astype(BF16)
-    acts_other = turned(over_x(acts))
-    resid_other = crossed(resid_half, "layer", 1)
-
-    def rows_of(array, which):
-        split = array.reshape(far, 2, rows, array.shape[1])
-        return jnp.where(which == 0, split[:, 0], split[:, 1]).reshape(tokens // 2, array.shape[1])
-
-    def kept(array):
-        return rows_of(array, layer)
-
-    def left(array):
-        return rows_of(array, 1 - layer)
-
-    leaving = times(left(acts), shared_mine) + times(left(acts_other), shared_other)
-    staying = times(kept(acts), shared_mine) + times(kept(acts_other), shared_other)
-    staying = staying + crossed(leaving.astype(BF16), "layer", 2).astype(F32)
-    sum_shared = staying[:rows]
-    for k in range(far - 1, 0, -1):
-        piece = staying[k * rows:(k + 1) * rows].astype(BF16)
-        sum_shared = sum_shared + crossed(piece, "latent", 2 * k).astype(F32)
-    err_shared = (sum_shared - aim_shared).astype(BF16)
-
-    acts, acts_other, staying = lax.optimization_barrier((acts, acts_other, staying))
-    product = times(acts, own_mine) + times(acts_other, own_other)
-    sum_own = product[:2 * rows]
-    for k in range(far - 1, 0, -1):
-        piece = product[2 * k * rows:2 * (k + 1) * rows].astype(BF16)
-        sum_own = sum_own + crossed(piece, "latent", 2 * k).astype(F32)
-    err_own = (sum_own - aim_own).astype(BF16)
+    partial = half_preacts(resid_half, enc_weight[0], weight_other, bias, half)
+    acts = ((partial + over_core(partial)) * jnp.concatenate(firing, axis=1)).astype(BF16)
+    acts_y, acts_x = over_y(acts), over_x(acts)
+    target, _ = hold((target, acts))
+    start = half * cols
+
+    def aim_own(where):
+        return lax.dynamic_slice(target, (2 * layer, 0, start + where * part), (1, rows, part))[0]
+
+    aim_other = over_x(aim_own(1 - side))
+    aim_shared = lax.dynamic_slice(target, (1, 0, start + layer * part), (1, rows, part))[0]
+    resid_swapped, _ = hold((resid_half, acts_x))
+    resid_other = over_core(resid_swapped)
+
+    leaving = times(rows_at(acts, 1 - side), shared_mine) + times(rows_at(acts_y, 1 - side), shared_other)
+    staying = times(rows_at(acts, side), shared_mine) + times(rows_at(acts_y, side), shared_other)
+    arrived = over_x(leaving.astype(BF16))
+    product = times(acts, own_mine) + times(acts_x, own_other)
+    arrived, staying, aim_other = hold((arrived, staying, aim_other))
+    shared_terms = sent_along_z(staying + arrived.astype(F32))
+    own_terms = sent_along_z(product)
+    err_shared = (added(shared_terms) - aim_shared.astype(F32)).astype(BF16)
+    err_own = (added(own_terms) - ordered(side, aim_own(side), aim_other).astype(F32)).astype(BF16)
 
     shared_near = jnp.concatenate(along_z(err_shared), axis=0)
-    shared_far = crossed(shared_near, "layer", 2)
-    halves = [block.reshape(far, 1, rows, part) for block in (shared_near, shared_far)]
-    errs_shared = jnp.where(
-        layer == 0, jnp.concatenate(halves, axis=1), jnp.concatenate(halves[::-1], axis=1)
-    ).reshape(tokens, part)
+    pairs = [block.reshape(far, 1, rows, part) for block in (shared_near, over_x(shared_near))]
+    errs_shared = ordered(side, *pairs, axis=1).reshape(tokens, part)
     errs_own = jnp.concatenate(along_z(err_own), axis=0)
 
-    here = jnp.where(layer == 0, err_own[:rows], shared_far[:rows])
-    there = over_x(jnp.where(layer == 0, err_own[rows:], err_shared))
-    errors = jnp.concatenate([jnp.where(side == 0, here, there), jnp.where(side == 0, there, here)], axis=1)
-
-    to_mine = times_transposed(errs_shared, shared_mine) + times_transposed(errs_own, own_mine)
-    to_other = times_transposed(errs_shared, shared_other) + times_transposed(errs_own, own_other)
-    to_other = turned(to_other.astype(BF16))
-
-    def of_half(pair, which):
-        return jnp.where(which == 0, pair[:, :latents], pair[:, latents:])
-
-    diagonal = of_half(to_other, 1 - half)
-    count = lax.axis_size("layer")
-    route = [(i * slots + j, (i ^ 1) * slots + (j ^ 1)) for i in range(count) for j in range(slots)]
-    grad = of_half(to_mine, half) + crossed(of_half(to_mine, 1 - half), "layer", 1)
-    grad = grad + over_x(of_half(to_other, half)).astype(F32)
-    grad = grad + lax.ppermute(diagonal, ("layer", "latent"), route).astype(F32)
-    grad_pre = grad * gate
+    grads = jnp.concatenate(
+        [
+            times_transposed(errs_own, own_mine) + times_transposed(errs_shared, shared_mine),
+            times_transposed(errs_own, own_other),
+            times_transposed(errs_shared, shared_other),
+        ],
+        axis=0,
+    )
+    lower, upper = grads[:, :latents], grads[:, latents:]
+    grads = jnp.where(half == 0, lower, upper) + over_core(jnp.where(half == 0, upper, lower))
+
+    def with_errors(grad, block):
+        tiles = [block[:, at:at + latents] for at in range(0, part, latents)]
+        return jnp.concatenate([grad.astype(BF16)] + tiles, axis=0)
+
+    def without_errors(message):
+        tiles = message[tokens:].reshape(part // latents, rows, latents)
+        return message[:tokens].astype(F32), jnp.concatenate([tiles[i] for i in range(part // latents)], axis=1)
+
+    from_x, own_there = without_errors(over_x(with_errors(grads[tokens:2 * tokens], rows_at(err_own, 1 - side))))
+    from_y, shared_there = without_errors(over_y(with_errors(grads[2 * tokens:], err_shared)))
+    errors = jnp.where(
+        layer == 0,
+        ordered(side, rows_at(err_own, side), own_there, axis=1),
+        jnp.concatenate([shared_there, err_shared], axis=1),
+    )
+    grad_pre = (grads[:tokens] + from_x + from_y) * gate
     bias_grad = jnp.sum(grad_pre, axis=0)[None, :]
     enc_grad = encoder_gradient(resid_half, resid_other, grad_pre.astype(BF16), half)
     return errors[None], enc_grad[None], bias_grad

time: 79.7 us -> 71.5 us (0.90)
  starting transfers between devices: 37 us -> 32.7 us
  other arithmetic: 8.81 us -> 4.84 us
  waiting for transfers between devices: 19.3 us -> 23 us
  local copies, waits for them, and re-layouts: 6.08 us -> 3.91 us
  matrix products: 5.72 us -> 4.17 us
    ppermute x28 -> x29, waiting for transfers between devices: 18.4 us -> 23 us  [crossed(): lax.ppermute(block, axis, [(i, i ^ mask) for i in range(lax.axis_size(axi...]
    ppermute x28 -> x29, starting transfers between devices: 36.6 us -> 32.7 us  [crossed(): lax.ppermute(block, axis, [(i, i ^ mask) for i in range(lax.axis_size(axi...]
    select_n x3, other arithmetic: 3.13 us -> 0.3 us  [both_halves(): jnp.where(half == 0, mine, other)]
    dot_general x7, matrix products: 3.16 us -> 1.61 us  [times(): return jnp.dot(left, right, preferred_element_type=F32)]
    rev x2 -> x0, local copies, waits for them, and re-layouts: 1.47 us -> none  [turned(): array.reshape(far, 2, rows, array.shape[1])[:, ::-1].reshape(array.shape)]
    squeeze x2 -> x1, local copies, waits for them, and re-layouts: 2.01 us -> 0.75 us  [aim_own(): lax.dynamic_slice(target, (2 * layer, 0, start + where * part), (1, rows,...]
    ppermute x1 -> x0, waiting for transfers between devices: 0.91 us -> none  [two_layers(): grad = grad + lax.ppermute(diagonal, ('layer', 'latent'), route).astype(F32)]
    reduce_sum x1, other arithmetic: 1.39 us -> 0.55 us  [two_layers(): bias_grad = jnp.sum(grad_pre, axis=0)[None, :]]
  transfers between devices with their start and end apart: 29 -> 29, of which waited for: 12 -> 15; matrix products, arithmetic and copies ran while one was open for 22% -> 14% of each run, Pallas kernels for 0% -> 0%
where the time goes in v7:
time: 71.5 us; the launch traced here: 71.1 us
  starting transfers between devices  32.7 us (46%)
  waiting for transfers between devices  23 us (32%)
  other arithmetic  4.84 us (7%)
  matrix products  4.17 us (6%)
  local copies, waits for them, and re-layouts  3.91 us (5%)
  between operations  2.45 us (3%)
    ppermute x29, starting transfers between devices, crossed(): lax.ppermute(block, axis, [(i, i ^ mask) for i in range(lax.axis_size(axi...  32.7 us
    ppermute x29, waiting for transfers between devices, crossed(): lax.ppermute(block, axis, [(i, i ^ mask) for i in range(lax.axis_size(axi...  23 us
    squeeze x1, local copies, waits for them, and re-layouts, decoder_part(): lax.dynamic_slice(decoder, (which, 0, where * part), (1, 2 * latents, part))  2.01 us
    select_n x3, other arithmetic, ordered(): jnp.where(which == 0, lower, upper)  1.65 us
    dot_general x7, matrix products, times(): return jnp.dot(left, right, preferred_element_type=F32)  1.61 us
  transfers between devices with their start and end apart: 29, of which 15 were waited for; matrix products, arithmetic and copies ran while one was open for 14% of the time, Pallas kernels for 0%

profile of v7, /device:TPU:0, one launch (start us, length us, event | category | flops | bytes accessed | tf_op | source)
XLA Modules:
  0.0 71.1 jit_solution(5038274361678006645)
XLA Ops:
  0.6 0.5 collective-permute-start.3
  1.2 0.8 %dynamic-slice_bitcast_fusion.2 = bf16[16,1792]{1,0:T(8,128)(2,1)S(1)} fusion(bf16[2,16,3584]{2,1,0:T(8,128)(2,1)} %param.6, s32[]{:T(128)S(6)} %select_n.285, s32[]{:T(128)S(6)} %select_n.291), kind=kLoop, calls=%fused_computation.93 | loop fusion | bytes 114696 | tf_op jit(solution)/shard_map/squeeze | solution.py:98
  2.0 2.6 %collective-permute-start.2 = (bf16[16,1792]{1,0:T(8,128)(2,1)S(1)}, bf16[16,1792]{1,0:T(8,128)(2,1)S(1)}, u32[]{:S(2)}, u32[]{:S(2)}) collective-permute-start(bf16[16,1792]{1,0:T(8,128)(2,1)S(1)} %dynamic-slice_bitcast_fusion.2), channel_id=1, source_target_pairs={{0,1},{1,0},{2,3},{3,2},{4,5},{5,4},{6,7},{7,6},{8,9},{9,8},{10,11... | collective-permute-start | bytes 172040 | tf_op jit(solution)/shard_map/ppermute | solution.py:11
  4.6 2.0 %dynamic-slice_bitcast_fusion = (bf16[256,896]{1,0:T(8,128)(2,1)}, bf16[256,896]{1,0:T(8,128)(2,1)S(1)}) fusion(bf16[2,256,1792]{2,1,0:T(8,128)(2,1)} %bitcast.110, s32[]{:T(128)S(6)} %select_n.287, s32[]{:T(128)S(6)} %select_n.288, s32[]{:T(128)S(6)} %select_n.285, s32[]{:T(128)S(6)} %select_n.286), kind=kLoop, calls=%fused_computation.24 | loop fusion | bytes 1835024 | tf_op jit(solution)/shard_map/squeeze | solution.py:88
  6.6 1.5 %collective-permute-start.1 = (bf16[256,896]{1,0:T(8,128)(2,1)}, bf16[256,896]{1,0:T(8,128)(2,1)S(1)}, u32[]{:S(2)}, u32[]{:S(2)}) collective-permute-start(bf16[256,896]{1,0:T(8,128)(2,1)} %get-tuple-element.43), channel_id=1, source_target_pairs={{0,16},{8,24},{16,0},{24,8},{1,17},{9,25},{17,1},{25,9},{2,18},{10... | collective-permute-start | bytes 1376264 | tf_op jit(solution)/shard_map/ppermute | solution.py:11
  8.1 0.5 collective-permute-start
  8.7 0.8 %broadcast_select_fusion.5 = (bf16[16,1792]{1,0:T(8,128)(2,1)S(1)}, bf16[16,1792]{1,0:T(8,128)(2,1)S(1)}) fusion(bf16[16,1792]{1,0:T(8,128)(2,1)S(1)} %collective-permute-done.2, pred[]{:T(512)S(6)} %eq.70, bf16[2,16,3584]{2,1,0:T(8,128)(2,1)} %param.6, s32[]{:T(128)S(6)} %select_n.285, s32[]{:T(128)S(6)} %select_n.291), kind=kLoop, calls=%fused_computation.95 | loop fusion | flops 57344 | bytes 229385 | tf_op jit(solution)/shard_map/jit(_where)/select_n | solution.py:91
  9.6 3.7 %collective-permute-start.6 = (bf16[32,1792]{1,0:T(8,128)(2,1)S(1)}, bf16[32,1792]{1,0:T(8,128)(2,1)S(1)}, u32[]{:S(2)}, u32[]{:S(2)}) collective-permute-start(bf16[32,1792]{1,0:T(8,128)(2,1)S(1)} %pad_maximum_fusion.3), channel_id=1, source_target_pairs={{0,6},{1,7},{2,4},{3,5},{4,2},{5,3},{6,0},{7,1},{8,14},{9,15},{10,... | collective-permute-start | bytes 344072 | tf_op jit(solution)/shard_map/ppermute | solution.py:11
  13.2 0.8 %collective-permute-start.4 = (bf16[32,1792]{1,0:T(8,128)(2,1)S(1)}, bf16[32,1792]{1,0:T(8,128)(2,1)S(1)}, u32[]{:S(2)}, u32[]{:S(2)}) collective-permute-start(bf16[32,1792]{1,0:T(8,128)(2,1)S(1)} %pad_maximum_fusion.3), channel_id=1, source_target_pairs={{0,2},{1,3},{2,0},{3,1},{4,6},{5,7},{6,4},{7,5},{8,10},{9,11},{10,... | collective-permute-start | bytes 344072 | tf_op jit(solution)/shard_map/ppermute | solution.py:11
  14.0 0.2 bitcast_select_fusion.1
  14.3 5.1 %collective-permute-done.1 = bf16[256,896]{1,0:T(8,128)(2,1)S(1)} collective-permute-done((bf16[256,896]{1,0:T(8,128)(2,1)}, bf16[256,896]{1,0:T(8,128)(2,1)S(1)}, u32[]{:S(2)}, u32[]{:S(2)}) %collective-permute-start.1) | collective-permute-done | bytes 458784 | tf_op jit(solution)/shard_map/ppermute | solution.py:11
  19.3 1.0 %collective-permute-done = bf16[256,896]{1,0:T(8,128)(2,1)S(1)} collective-permute-done((bf16[256,896]{1,0:T(8,128)(2,1)S(1)}, bf16[256,896]{1,0:T(8,128)(2,1)S(1)}, u32[]{:S(2)}, u32[]{:S(2)}) %collective-permute-start) | collective-permute-done | bytes 458784 | tf_op jit(solution)/shard_map/ppermute | solution.py:11
  20.4 2.2 %collective-permute-done.5 = bf16[32,1792]{1,0:T(8,128)(2,1)S(1)} collective-permute-done((bf16[32,1792]{1,0:T(8,128)(2,1)S(1)}, bf16[32,1792]{1,0:T(8,128)(2,1)S(1)}, u32[]{:S(2)}, u32[]{:S(2)}) %collective-permute-start.5) | collective-permute-done | bytes 114720 | tf_op jit(solution)/shard_map/ppermute | solution.py:11
  22.7 0.3 convolution_add_fusion.4
  23.0 0.1 collective-permute-start.7
  23.1 0.6 compare_reduce_fusion
  25.1 0.6 collective-permute-start.12
  25.7 1.5 %collective-permute-start.8 = (bf16[128,256]{1,0:T(8,128)(2,1)S(1)}, bf16[128,256]{1,0:T(8,128)(2,1)S(1)}, u32[]{:S(2)}, u32[]{:S(2)}) collective-permute-start(bf16[128,256]{1,0:T(8,128)(2,1)S(1)} %multiply_convert_fusion), channel_id=1, source_target_pairs={{0,1},{1,0},{2,3},{3,2},{4,5},{5,4},{6,7},{7,6},{8,9},{9,8},{10,11... | collective-permute-start | bytes 196616 | tf_op jit(solution)/shard_map/ppermute | solution.py:11
  27.2 0.8 %dynamic-slice_bitcast_fusion.3 = bf16[16,896]{1,0:T(8,128)(2,1)S(1)} fusion(bf16[3,16,3584]{2,1,0:T(8,128)(2,1)} %param.7, s32[]{:T(128)S(6)} %select_n.301, s32[]{:T(128)S(6)} %select_n.314), kind=kLoop, calls=%fused_computation.109 | loop fusion | bytes 57352 | tf_op jit(solution)/shard_map/squeeze | solution.py:117
  27.9 0.5 collective-permute-start.14
  28.5 0.2 fusion.12
  28.7 0.2 fusion.10
  28.9 0.7 collective-permute-done.12
  29.6 0.3 collective-permute-done.8
  29.9 0.2 fusion.1
  30.2 1.9 %collective-permute-start.13 = (bf16[64,896]{1,0:T(8,128)(2,1)S(1)}, bf16[64,896]{1,0:T(8,128)(2,1)S(1)}, u32[]{:S(2)}, u32[]{:S(2)}) collective-permute-start(bf16[64,896]{1,0:T(8,128)(2,1)S(1)} %fusion.1), channel_id=1, source_target_pairs={{0,1},{1,0},{2,3},{3,2},{4,5},{5,4},{6,7},{7,6},{8,9},{9,8},{10,11... | collective-permute-start | bytes 344072 | tf_op jit(solution)/shard_map/ppermute | solution.py:11
  32.0 0.2 fusion.51
  32.3 0.2 fusion.50
  32.5 2.5 %collective-permute-start.9 = (bf16[32,896]{1,0:T(8,128)(2,1)S(1)}, bf16[32,896]{1,0:T(8,128)(2,1)S(1)}, u32[]{:S(2)}, u32[]{:S(2)}) collective-permute-start(bf16[32,896]{1,0:T(8,128)(2,1)S(1)} %get-tuple-element.49), channel_id=1, source_target_pairs={{0,6},{1,7},{2,4},{3,5},{4,2},{5,3},{6,0},{7,1},{8,14},{9,15},{10,... | collective-permute-start | bytes 172040 | tf_op jit(solution)/shard_map/ppermute | solution.py:11
  35.1 1.9 %collective-permute-start.10 = (bf16[32,896]{1,0:T(8,128)(2,1)S(1)}, bf16[32,896]{1,0:T(8,128)(2,1)S(1)}, u32[]{:S(2)}, u32[]{:S(2)}) collective-permute-start(bf16[32,896]{1,0:T(8,128)(2,1)S(1)} %get-tuple-element.51), channel_id=1, source_target_pairs={{0,4},{1,5},{2,6},{3,7},{4,0},{5,1},{6,2},{7,3},{8,12},{9,13},{10,... | collective-permute-start | bytes 172040 | tf_op jit(solution)/shard_map/ppermute | solution.py:11
  37.0 0.2 convolution_add_fusion.1
  37.2 0.1 collective-permute-start.28
  37.4 2.5 %collective-permute-start.18 = (bf16[16,896]{1,0:T(8,128)(2,1)S(1)}, bf16[16,896]{1,0:T(8,128)(2,1)S(1)}, u32[]{:S(2)}, u32[]{:S(2)}) collective-permute-start(bf16[16,896]{1,0:T(8,128)(2,1)S(1)} %get-tuple-element.54), channel_id=1, source_target_pairs={{0,6},{1,7},{2,4},{3,5},{4,2},{5,3},{6,0},{7,1},{8,14},{9,15},{10,... | collective-permute-start | bytes 86024 | tf_op jit(solution)/shard_map/ppermute | solution.py:11
  39.9 0.8 %bitcast_select_fusion.5 = (bf16[16,896]{1,0:T(8,128)(2,1)S(1)}, bf16[16,896]{1,0:T(8,128)(2,1)S(1)}) fusion(bf16[16,896]{1,0:T(8,128)(2,1)S(1)} %collective-permute-done.14, pred[]{:T(512)S(6)} %eq.70, bf16[3,16,3584]{2,1,0:T(8,128)(2,1)} %param.7, s32[]{:T(128)S(6)} %select_n.301, s32[]{:T(128)S(6)} %select_n.302), kind=kLoop, calls=%fused_computation.107 | loop fusion | flops 28672 | bytes 114697 | tf_op jit(solution)/shard_map/jit(_where)/select_n | solution.py:91
  40.7 0.1 collective-permute-start.20
  40.8 1.9 %collective-permute-start.19 = (bf16[16,896]{1,0:T(8,128)(2,1)S(1)}, bf16[16,896]{1,0:T(8,128)(2,1)S(1)}, u32[]{:S(2)}, u32[]{:S(2)}) collective-permute-start(bf16[16,896]{1,0:T(8,128)(2,1)S(1)} %get-tuple-element.56), channel_id=1, source_target_pairs={{0,4},{1,5},{2,6},{3,7},{4,0},{5,1},{6,2},{7,3},{8,12},{9,13},{10,... | collective-permute-start | bytes 86024 | tf_op jit(solution)/shard_map/ppermute | solution.py:11
  42.7 2.5 %collective-permute-start.17 = (bf16[32,896]{1,0:T(8,128)(2,1)S(1)}, bf16[32,896]{1,0:T(8,128)(2,1)S(1)}, u32[]{:S(2)}, u32[]{:S(2)}) collective-permute-start(bf16[32,896]{1,0:T(8,128)(2,1)S(1)} %fusion.24), channel_id=1, source_target_pairs={{0,6},{1,7},{2,4},{3,5},{4,2},{5,3},{6,0},{7,1},{8,14},{9,15},{10,... | collective-permute-start | bytes 172040 | tf_op jit(solution)/shard_map/ppermute | solution.py:11
  45.2 0.8 %collective-permute-done.19 = bf16[16,896]{1,0:T(8,128)(2,1)S(1)} collective-permute-done((bf16[16,896]{1,0:T(8,128)(2,1)S(1)}, bf16[16,896]{1,0:T(8,128)(2,1)S(1)}, u32[]{:S(2)}, u32[]{:S(2)}) %collective-permute-start.19) | collective-permute-done | bytes 28704 | tf_op jit(solution)/shard_map/ppermute | solution.py:11
  46.1 0.8 %fusion.30 = bf16[16,896]{1,0:T(8,128)(2,1)S(1)} fusion(f32[64,896]{1,0:T(8,128)S(1)} %get-tuple-element.40, bf16[16,896]{1,0:T(8,128)(2,1)S(1)} %collective-permute-done.20, bf16[16,896]{1,0:T(8,128)(2,1)S(1)} %collective-permute-done.19, bf16[16,896]{1,0:T(8,128)(2,1)S(1)} %collective-permute-done.18, bf16[3,16,3584]{2,1,0:T(8,128)(2,1)} %param.7, ...), kind=kLoop, calls=%fused_computation.91 | loop fusion | flops 129024 | bytes 200708 | tf_op jit(solution)/shard_map/convert_element_type | solution.py:131
  46.8 1.0 %collective-permute-start.23 = (bf16[16,896]{1,0:T(8,128)(2,1)S(1)}, bf16[16,896]{1,0:T(8,128)(2,1)S(1)}, u32[]{:S(2)}, u32[]{:S(2)}) collective-permute-start(bf16[16,896]{1,0:T(8,128)(2,1)S(1)} %fusion.30), channel_id=1, source_target_pairs={{0,6},{1,7},{2,4},{3,5},{4,2},{5,3},{6,0},{7,1},{8,14},{9,15},{10,... | collective-permute-start | bytes 86024 | tf_op jit(solution)/shard_map/ppermute | solution.py:11
  47.8 2.2 %collective-permute-start.22 = (bf16[16,896]{1,0:T(8,128)(2,1)S(1)}, bf16[16,896]{1,0:T(8,128)(2,1)S(1)}, u32[]{:S(2)}, u32[]{:S(2)}) collective-permute-start(bf16[16,896]{1,0:T(8,128)(2,1)S(1)} %fusion.30), channel_id=1, source_target_pairs={{0,4},{1,5},{2,6},{3,7},{4,0},{5,1},{6,2},{7,3},{8,12},{9,13},{10,... | collective-permute-start | bytes 86024 | tf_op jit(solution)/shard_map/ppermute | solution.py:11
  50.0 1.3 %collective-permute-start.21 = (bf16[16,896]{1,0:T(8,128)(2,1)S(1)}, bf16[16,896]{1,0:T(8,128)(2,1)S(1)}, u32[]{:S(2)}, u32[]{:S(2)}) collective-permute-start(bf16[16,896]{1,0:T(8,128)(2,1)S(1)} %fusion.30), channel_id=1, source_target_pairs={{0,2},{1,3},{2,0},{3,1},{4,6},{5,7},{6,4},{7,5},{8,10},{9,11},{10,... | collective-permute-start | bytes 86024 | tf_op jit(solution)/shard_map/ppermute | solution.py:11
  51.3 1.3 %collective-permute-done.23 = bf16[16,896]{1,0:T(8,128)(2,1)S(1)} collective-permute-done((bf16[16,896]{1,0:T(8,128)(2,1)S(1)}, bf16[16,896]{1,0:T(8,128)(2,1)S(1)}, u32[]{:S(2)}, u32[]{:S(2)}) %collective-permute-start.23) | collective-permute-done | bytes 28704 | tf_op jit(solution)/shard_map/ppermute | solution.py:11
  52.6 0.3 collective-permute-start.16
  52.9 1.1 %collective-permute-done.22 = bf16[16,896]{1,0:T(8,128)(2,1)S(1)} collective-permute-done((bf16[16,896]{1,0:T(8,128)(2,1)S(1)}, bf16[16,896]{1,0:T(8,128)(2,1)S(1)}, u32[]{:S(2)}, u32[]{:S(2)}) %collective-permute-start.22) | collective-permute-done | bytes 28704 | tf_op jit(solution)/shard_map/ppermute | solution.py:11
  54.1 0.9 %collective-permute-done.21 = bf16[16,896]{1,0:T(8,128)(2,1)S(1)} collective-permute-done((bf16[16,896]{1,0:T(8,128)(2,1)S(1)}, bf16[16,896]{1,0:T(8,128)(2,1)S(1)}, u32[]{:S(2)}, u32[]{:S(2)}) %collective-permute-start.21) | collective-permute-done | bytes 28704 | tf_op jit(solution)/shard_map/ppermute | solution.py:11
  55.0 0.3 collective-permute-start.24
  55.3 2.4 %collective-permute-done.16 = bf16[32,896]{1,0:T(8,128)(2,1)S(1)} collective-permute-done((bf16[32,896]{1,0:T(8,128)(2,1)S(1)}, bf16[32,896]{1,0:T(8,128)(2,1)S(1)}, u32[]{:S(2)}, u32[]{:S(2)}) %collective-permute-start.16) | collective-permute-done | bytes 57376 | tf_op jit(solution)/shard_map/ppermute | solution.py:11
  57.7 0.6 collective-permute-done.15
  58.3 0.3 fusion.31
  58.6 1.3 %collective-permute-done.24 = bf16[64,896]{1,0:T(8,128)(2,1)S(1)} collective-permute-done((bf16[64,896]{1,0:T(8,128)(2,1)S(1)}, bf16[64,896]{1,0:T(8,128)(2,1)S(1)}, u32[]{:S(2)}, u32[]{:S(2)}) %collective-permute-start.24) | collective-permute-done | bytes 114720 | tf_op jit(solution)/shard_map/ppermute | solution.py:11
  59.9 0.3 fusion.52
  60.2 0.3 fusion.8
  60.5 0.3 convolution_add_fusion.3
  60.9 0.1 collective-permute-start.25
  61.0 0.1 broadcast_select_fusion.1
  61.1 1.3 %collective-permute-done.25 = f32[384,128]{1,0:T(8,128)S(1)} collective-permute-done((f32[384,128]{1,0:T(8,128)S(1)}, f32[384,128]{1,0:T(8,128)S(1)}, u32[]{:S(2)}, u32[]{:S(2)}) %collective-permute-start.25) | collective-permute-done | bytes 196640 | tf_op jit(solution)/shard_map/ppermute | solution.py:11
  62.6 1.6 %collective-permute-start.27 = (bf16[240,128]{1,0:T(8,128)(2,1)S(1)}, bf16[240,128]{1,0:T(8,128)(2,1)S(1)}, u32[]{:S(2)}, u32[]{:S(2)}) collective-permute-start(bf16[240,128]{1,0:T(8,128)(2,1)S(1)} %constant_dynamic-update-slice_fusion.19), channel_id=1, source_target_pairs={{0,16},{8,24},{16,0},{24,8},{1,17},{9,25},{17,1},{25,9},{2,18},{10... | collective-permute-start | bytes 184328 | tf_op jit(solution)/shard_map/ppermute | solution.py:11
  64.2 0.2 collective-permute-start.26
  64.4 2.5 %collective-permute-done.27 = bf16[240,128]{1,0:T(8,128)(2,1)S(1)} collective-permute-done((bf16[240,128]{1,0:T(8,128)(2,1)S(1)}, bf16[240,128]{1,0:T(8,128)(2,1)S(1)}, u32[]{:S(2)}, u32[]{:S(2)}) %collective-permute-start.27) | collective-permute-done | bytes 61472 | tf_op jit(solution)/shard_map/ppermute | solution.py:11
  67.0 1.5 %collective-permute-done.26 = bf16[240,128]{1,0:T(8,128)(2,1)S(1)} collective-permute-done((bf16[240,128]{1,0:T(8,128)(2,1)S(1)}, bf16[240,128]{1,0:T(8,128)(2,1)S(1)}, u32[]{:S(2)}, u32[]{:S(2)}) %collective-permute-start.26) | collective-permute-done | bytes 61472 | tf_op jit(solution)/shard_map/ppermute | solution.py:11
  68.5 0.6 maximum_select_fusion
  69.2 0.5 fusion.35
  69.7 1.4 %fusion = bf16[1,3584,128]{2,1,0:T(8,128)(2,1)} fusion(bf16[128,1792]{1,0:T(8,128)(2,1)S(1)} %get-tuple-element.46, bf16[128,1792]{1,0:T(8,128)(2,1)S(1)} %get-tuple-element.45, f32[384,128]{1,0:T(8,128)S(1)} %get-tuple-element.38, bf16[240,128]{1,0:T(8,128)(2,1)S(1)} %collective-permute-done.27, bf16[240,128]{1,0:T(8,128)(2,1)S(1)} %collective-permute-done.26, ...), kind=kOutput, calls=%fused_computation.1 | convolution fusion | flops 119832576 | bytes 1966084 | tf_op jit(solution)/shard_map/dot_general | solution.py:48
  (78 shorter events, 0.7 us)
Async XLA Ops:
  0.6 13.4 %copy-start.1 = (bf16[1,3584,128]{2,1,0:T(8,128)(2,1)S(1)}, bf16[1,3584,128]{2,1,0:T(8,128)(2,1)}, u32[]{:S(2)}) copy-start(bf16[1,3584,128]{2,1,0:T(8,128)(2,1)} %param.8) | copy-start | bytes 2752516
  0.6 8.9 %collective-permute-start.3 = (bf16[3584,128]{1,0:T(8,128)(2,1)}, bf16[3584,128]{1,0:T(8,128)(2,1)S(1)}, u32[]{:S(2)}, u32[]{:S(2)}) collective-permute-start(bf16[3584,128]{1,0:T(8,128)(2,1)} %bitcast.123), channel_id=1, source_target_pairs={{0,8},{8,0},{16,24},{24,16},{1,9},{9,1},{17,25},{25,17},{2,10},{10... | collective-permute-start | bytes 2752520 | tf_op jit(solution)/shard_map/ppermute | solution.py:11
  2.0 6.7 %collective-permute-start.2 = (bf16[16,1792]{1,0:T(8,128)(2,1)S(1)}, bf16[16,1792]{1,0:T(8,128)(2,1)S(1)}, u32[]{:S(2)}, u32[]{:S(2)}) collective-permute-start(bf16[16,1792]{1,0:T(8,128)(2,1)S(1)} %dynamic-slice_bitcast_fusion.2), channel_id=1, source_target_pairs={{0,1},{1,0},{2,3},{3,2},{4,5},{5,4},{6,7},{7,6},{8,9},{9,8},{10,11... | collective-permute-start | bytes 172040 | tf_op jit(solution)/shard_map/ppermute | solution.py:11
  4.6 9.6 %copy-start.2 = (f32[1,128]{1,0:T(1,128)S(1)}, f32[1,128]{1,0:T(1,128)}, u32[]{:S(2)}) copy-start(f32[1,128]{1,0:T(1,128)} %param.9) | copy-start | bytes 1540
  6.6 12.7 %collective-permute-start.1 = (bf16[256,896]{1,0:T(8,128)(2,1)}, bf16[256,896]{1,0:T(8,128)(2,1)S(1)}, u32[]{:S(2)}, u32[]{:S(2)}) collective-permute-start(bf16[256,896]{1,0:T(8,128)(2,1)} %get-tuple-element.43), channel_id=1, source_target_pairs={{0,16},{8,24},{16,0},{24,8},{1,17},{9,25},{17,1},{25,9},{2,18},{10... | collective-permute-start | bytes 1376264 | tf_op jit(solution)/shard_map/ppermute | solution.py:11
  8.1 12.2 %collective-permute-start = (bf16[256,896]{1,0:T(8,128)(2,1)S(1)}, bf16[256,896]{1,0:T(8,128)(2,1)S(1)}, u32[]{:S(2)}, u32[]{:S(2)}) collective-permute-start(bf16[256,896]{1,0:T(8,128)(2,1)S(1)} %get-tuple-element.44), channel_id=1, source_target_pairs={{0,1},{1,0},{2,3},{3,2},{4,5},{5,4},{6,7},{7,6},{8,9},{9,8},{10,11... | collective-permute-start | bytes 1376264 | tf_op jit(solution)/shard_map/ppermute | solution.py:11
  9.6 10.8 %collective-permute-start.6 = (bf16[32,1792]{1,0:T(8,128)(2,1)S(1)}, bf16[32,1792]{1,0:T(8,128)(2,1)S(1)}, u32[]{:S(2)}, u32[]{:S(2)}) collective-permute-start(bf16[32,1792]{1,0:T(8,128)(2,1)S(1)} %pad_maximum_fusion.3), channel_id=1, source_target_pairs={{0,6},{1,7},{2,4},{3,5},{4,2},{5,3},{6,0},{7,1},{8,14},{9,15},{10,... | collective-permute-start | bytes 344072 | tf_op jit(solution)/shard_map/ppermute | solution.py:11
  13.2 9.4 %collective-permute-start.5 = (bf16[32,1792]{1,0:T(8,128)(2,1)S(1)}, bf16[32,1792]{1,0:T(8,128)(2,1)S(1)}, u32[]{:S(2)}, u32[]{:S(2)}) collective-permute-start(bf16[32,1792]{1,0:T(8,128)(2,1)S(1)} %pad_maximum_fusion.3), channel_id=1, source_target_pairs={{0,4},{1,5},{2,6},{3,7},{4,0},{5,1},{6,2},{7,3},{8,12},{9,13},{10,... | collective-permute-start | bytes 344072 | tf_op jit(solution)/shard_map/ppermute | solution.py:11
  13.2 9.4 %collective-permute-start.4 = (bf16[32,1792]{1,0:T(8,128)(2,1)S(1)}, bf16[32,1792]{1,0:T(8,128)(2,1)S(1)}, u32[]{:S(2)}, u32[]{:S(2)}) collective-permute-start(bf16[32,1792]{1,0:T(8,128)(2,1)S(1)} %pad_maximum_fusion.3), channel_id=1, source_target_pairs={{0,2},{1,3},{2,0},{3,1},{4,6},{5,7},{6,4},{7,5},{8,10},{9,11},{10,... | collective-permute-start | bytes 344072 | tf_op jit(solution)/shard_map/ppermute | solution.py:11
  14.2 8.9 %copy-start.3 = (s32[2,1,12]{2,1,0:T(1,128)S(1)}, s32[2,1,12]{2,1,0:T(1,128)}, u32[]{:S(2)}) copy-start(s32[2,1,12]{2,1,0:T(1,128)} %param.11) | copy-start | bytes 292
  14.2 14.2 %copy-start = (bf16[1,2,2,128,1792]{4,3,2,1,0:T(8,128)(2,1)S(1)}, bf16[1,2,2,128,1792]{4,3,2,1,0:T(8,128)(2,1)}, u32[]{:S(2)}) copy-start(bf16[1,2,2,128,1792]{4,3,2,1,0:T(8,128)(2,1)} %param.10) | copy-start | bytes 5505028
  23.0 2.1 %collective-permute-start.7 = (f32[128,256]{1,0:T(8,128)S(1)}, f32[128,256]{1,0:T(8,128)S(1)}, u32[]{:S(2)}, u32[]{:S(2)}) collective-permute-start(f32[128,256]{1,0:T(8,128)S(1)} %convolution_add_fusion.4), channel_id=1, source_target_pairs={{0,8},{8,0},{16,24},{24,16},{1,9},{9,1},{17,25},{25,17},{2,10},{10... | collective-permute-start | bytes 393224 | tf_op jit(solution)/shard_map/ppermute | solution.py:11
  25.1 4.5 %collective-permute-start.12 = (bf16[128,256]{1,0:T(8,128)(2,1)S(1)}, bf16[128,256]{1,0:T(8,128)(2,1)S(1)}, u32[]{:S(2)}, u32[]{:S(2)}) collective-permute-start(bf16[128,256]{1,0:T(8,128)(2,1)S(1)} %multiply_convert_fusion), channel_id=1, source_target_pairs={{0,16},{8,24},{16,0},{24,8},{1,17},{9,25},{17,1},{25,9},{2,18},{10... | collective-permute-start | bytes 196616 | tf_op jit(solution)/shard_map/ppermute | solution.py:11
  25.7 4.3 %collective-permute-start.8 = (bf16[128,256]{1,0:T(8,128)(2,1)S(1)}, bf16[128,256]{1,0:T(8,128)(2,1)S(1)}, u32[]{:S(2)}, u32[]{:S(2)}) collective-permute-start(bf16[128,256]{1,0:T(8,128)(2,1)S(1)} %multiply_convert_fusion), channel_id=1, source_target_pairs={{0,1},{1,0},{2,3},{3,2},{4,5},{5,4},{6,7},{7,6},{8,9},{9,8},{10,11... | collective-permute-start | bytes 196616 | tf_op jit(solution)/shard_map/ppermute | solution.py:11
  27.9 9.3 %collective-permute-start.14 = (bf16[16,896]{1,0:T(8,128)(2,1)S(1)}, bf16[16,896]{1,0:T(8,128)(2,1)S(1)}, u32[]{:S(2)}, u32[]{:S(2)}) collective-permute-start(bf16[16,896]{1,0:T(8,128)(2,1)S(1)} %dynamic-slice_bitcast_fusion.3), channel_id=1, source_target_pairs={{0,1},{1,0},{2,3},{3,2},{4,5},{5,4},{6,7},{7,6},{8,9},{9,8},{10,11... | collective-permute-start | bytes 86024 | tf_op jit(solution)/shard_map/ppermute | solution.py:11
  30.2 7.1 %collective-permute-start.13 = (bf16[64,896]{1,0:T(8,128)(2,1)S(1)}, bf16[64,896]{1,0:T(8,128)(2,1)S(1)}, u32[]{:S(2)}, u32[]{:S(2)}) collective-permute-start(bf16[64,896]{1,0:T(8,128)(2,1)S(1)} %fusion.1), channel_id=1, source_target_pairs={{0,1},{1,0},{2,3},{3,2},{4,5},{5,4},{6,7},{7,6},{8,9},{9,8},{10,11... | collective-permute-start | bytes 344072 | tf_op jit(solution)/shard_map/ppermute | solution.py:11
  32.5 8.1 %collective-permute-start.9 = (bf16[32,896]{1,0:T(8,128)(2,1)S(1)}, bf16[32,896]{1,0:T(8,128)(2,1)S(1)}, u32[]{:S(2)}, u32[]{:S(2)}) collective-permute-start(bf16[32,896]{1,0:T(8,128)(2,1)S(1)} %get-tuple-element.49), channel_id=1, source_target_pairs={{0,6},{1,7},{2,4},{3,5},{4,2},{5,3},{6,0},{7,1},{8,14},{9,15},{10,... | collective-permute-start | bytes 172040 | tf_op jit(solution)/shard_map/ppermute | solution.py:11
  35.1 5.7 %collective-permute-start.11 = (bf16[32,896]{1,0:T(8,128)(2,1)S(1)}, bf16[32,896]{1,0:T(8,128)(2,1)S(1)}, u32[]{:S(2)}, u32[]{:S(2)}) collective-permute-start(bf16[32,896]{1,0:T(8,128)(2,1)S(1)} %get-tuple-element.50), channel_id=1, source_target_pairs={{0,2},{1,3},{2,0},{3,1},{4,6},{5,7},{6,4},{7,5},{8,10},{9,11},{10,... | collective-permute-start | bytes 172040 | tf_op jit(solution)/shard_map/ppermute | solution.py:11
  35.1 7.6 %collective-permute-start.10 = (bf16[32,896]{1,0:T(8,128)(2,1)S(1)}, bf16[32,896]{1,0:T(8,128)(2,1)S(1)}, u32[]{:S(2)}, u32[]{:S(2)}) collective-permute-start(bf16[32,896]{1,0:T(8,128)(2,1)S(1)} %get-tuple-element.51), channel_id=1, source_target_pairs={{0,4},{1,5},{2,6},{3,7},{4,0},{5,1},{6,2},{7,3},{8,12},{9,13},{10,... | collective-permute-start | bytes 172040 | tf_op jit(solution)/shard_map/ppermute | solution.py:11
  37.2 23.8 %collective-permute-start.28 = (bf16[128,1792]{1,0:T(8,128)(2,1)S(1)}, bf16[128,1792]{1,0:T(8,128)(2,1)S(1)}, u32[]{:S(2)}, u32[]{:S(2)}) collective-permute-start(bf16[128,1792]{1,0:T(8,128)(2,1)S(1)} %constant_dynamic-update-slice_fusion), channel_id=1, source_target_pairs={{0,8},{8,0},{16,24},{24,16},{1,9},{9,1},{17,25},{25,17},{2,10},{10... | collective-permute-start | bytes 1376264 | tf_op jit(solution)/shard_map/ppermute | solution.py:11
  37.4 7.9 %collective-permute-start.18 = (bf16[16,896]{1,0:T(8,128)(2,1)S(1)}, bf16[16,896]{1,0:T(8,128)(2,1)S(1)}, u32[]{:S(2)}, u32[]{:S(2)}) collective-permute-start(bf16[16,896]{1,0:T(8,128)(2,1)S(1)} %get-tuple-element.54), channel_id=1, source_target_pairs={{0,6},{1,7},{2,4},{3,5},{4,2},{5,3},{6,0},{7,1},{8,14},{9,15},{10,... | collective-permute-start | bytes 86024 | tf_op jit(solution)/shard_map/ppermute | solution.py:11
  40.7 4.6 %collective-permute-start.20 = (bf16[16,896]{1,0:T(8,128)(2,1)S(1)}, bf16[16,896]{1,0:T(8,128)(2,1)S(1)}, u32[]{:S(2)}, u32[]{:S(2)}) collective-permute-start(bf16[16,896]{1,0:T(8,128)(2,1)S(1)} %get-tuple-element.55), channel_id=1, source_target_pairs={{0,2},{1,3},{2,0},{3,1},{4,6},{5,7},{6,4},{7,5},{8,10},{9,11},{10,... | collective-permute-start | bytes 86024 | tf_op jit(solution)/shard_map/ppermute | solution.py:11
  40.8 5.3 %collective-permute-start.19 = (bf16[16,896]{1,0:T(8,128)(2,1)S(1)}, bf16[16,896]{1,0:T(8,128)(2,1)S(1)}, u32[]{:S(2)}, u32[]{:S(2)}) collective-permute-start(bf16[16,896]{1,0:T(8,128)(2,1)S(1)} %get-tuple-element.56), channel_id=1, source_target_pairs={{0,4},{1,5},{2,6},{3,7},{4,0},{5,1},{6,2},{7,3},{8,12},{9,13},{10,... | collective-permute-start | bytes 86024 | tf_op jit(solution)/shard_map/ppermute | solution.py:11
  42.7 12.6 %collective-permute-start.17 = (bf16[32,896]{1,0:T(8,128)(2,1)S(1)}, bf16[32,896]{1,0:T(8,128)(2,1)S(1)}, u32[]{:S(2)}, u32[]{:S(2)}) collective-permute-start(bf16[32,896]{1,0:T(8,128)(2,1)S(1)} %fusion.24), channel_id=1, source_target_pairs={{0,6},{1,7},{2,4},{3,5},{4,2},{5,3},{6,0},{7,1},{8,14},{9,15},{10,... | collective-permute-start | bytes 172040 | tf_op jit(solution)/shard_map/ppermute | solution.py:11
  46.8 5.8 %collective-permute-start.23 = (bf16[16,896]{1,0:T(8,128)(2,1)S(1)}, bf16[16,896]{1,0:T(8,128)(2,1)S(1)}, u32[]{:S(2)}, u32[]{:S(2)}) collective-permute-start(bf16[16,896]{1,0:T(8,128)(2,1)S(1)} %fusion.30), channel_id=1, source_target_pairs={{0,6},{1,7},{2,4},{3,5},{4,2},{5,3},{6,0},{7,1},{8,14},{9,15},{10,... | collective-permute-start | bytes 86024 | tf_op jit(solution)/shard_map/ppermute | solution.py:11
  47.8 6.2 %collective-permute-start.22 = (bf16[16,896]{1,0:T(8,128)(2,1)S(1)}, bf16[16,896]{1,0:T(8,128)(2,1)S(1)}, u32[]{:S(2)}, u32[]{:S(2)}) collective-permute-start(bf16[16,896]{1,0:T(8,128)(2,1)S(1)} %fusion.30), channel_id=1, source_target_pairs={{0,4},{1,5},{2,6},{3,7},{4,0},{5,1},{6,2},{7,3},{8,12},{9,13},{10,... | collective-permute-start | bytes 86024 | tf_op jit(solution)/shard_map/ppermute | solution.py:11
  50.0 5.0 %collective-permute-start.21 = (bf16[16,896]{1,0:T(8,128)(2,1)S(1)}, bf16[16,896]{1,0:T(8,128)(2,1)S(1)}, u32[]{:S(2)}, u32[]{:S(2)}) collective-permute-start(bf16[16,896]{1,0:T(8,128)(2,1)S(1)} %fusion.30), channel_id=1, source_target_pairs={{0,2},{1,3},{2,0},{3,1},{4,6},{5,7},{6,4},{7,5},{8,10},{9,11},{10,... | collective-permute-start | bytes 86024 | tf_op jit(solution)/shard_map/ppermute | solution.py:11
  52.6 5.1 %collective-permute-start.16 = (bf16[32,896]{1,0:T(8,128)(2,1)S(1)}, bf16[32,896]{1,0:T(8,128)(2,1)S(1)}, u32[]{:S(2)}, u32[]{:S(2)}) collective-permute-start(bf16[32,896]{1,0:T(8,128)(2,1)S(1)} %fusion.24), channel_id=1, source_target_pairs={{0,4},{1,5},{2,6},{3,7},{4,0},{5,1},{6,2},{7,3},{8,12},{9,13},{10,... | collective-permute-start | bytes 172040 | tf_op jit(solution)/shard_map/ppermute | solution.py:11
  54.1 4.2 %collective-permute-start.15 = (bf16[32,896]{1,0:T(8,128)(2,1)S(1)}, bf16[32,896]{1,0:T(8,128)(2,1)S(1)}, u32[]{:S(2)}, u32[]{:S(2)}) collective-permute-start(bf16[32,896]{1,0:T(8,128)(2,1)S(1)} %fusion.24), channel_id=1, source_target_pairs={{0,2},{1,3},{2,0},{3,1},{4,6},{5,7},{6,4},{7,5},{8,10},{9,11},{10,... | collective-permute-start | bytes 172040 | tf_op jit(solution)/shard_map/ppermute | solution.py:11
  55.0 4.9 %collective-permute-start.24 = (bf16[64,896]{1,0:T(8,128)(2,1)S(1)}, bf16[64,896]{1,0:T(8,128)(2,1)S(1)}, u32[]{:S(2)}, u32[]{:S(2)}) collective-permute-start(bf16[64,896]{1,0:T(8,128)(2,1)S(1)} %pad_maximum_fusion.4), channel_id=1, source_target_pairs={{0,1},{1,0},{2,3},{3,2},{4,5},{5,4},{6,7},{7,6},{8,9},{9,8},{10,11... | collective-permute-start | bytes 344072 | tf_op jit(solution)/shard_map/ppermute | solution.py:11
  60.9 1.5 %collective-permute-start.25 = (f32[384,128]{1,0:T(8,128)S(1)}, f32[384,128]{1,0:T(8,128)S(1)}, u32[]{:S(2)}, u32[]{:S(2)}) collective-permute-start(f32[384,128]{1,0:T(8,128)S(1)} %slice_select_fusion), channel_id=1, source_target_pairs={{0,8},{8,0},{16,24},{24,16},{1,9},{9,1},{17,25},{25,17},{2,10},{10... | collective-permute-start | bytes 589832 | tf_op jit(solution)/shard_map/ppermute | solution.py:11
  62.6 4.3 %collective-permute-start.27 = (bf16[240,128]{1,0:T(8,128)(2,1)S(1)}, bf16[240,128]{1,0:T(8,128)(2,1)S(1)}, u32[]{:S(2)}, u32[]{:S(2)}) collective-permute-start(bf16[240,128]{1,0:T(8,128)(2,1)S(1)} %constant_dynamic-update-slice_fusion.19), channel_id=1, source_target_pairs={{0,16},{8,24},{16,0},{24,8},{1,17},{9,25},{17,1},{25,9},{2,18},{10... | collective-permute-start | bytes 184328 | tf_op jit(solution)/shard_map/ppermute | solution.py:11
  64.2 4.2 %collective-permute-start.26 = (bf16[240,128]{1,0:T(8,128)(2,1)S(1)}, bf16[240,128]{1,0:T(8,128)(2,1)S(1)}, u32[]{:S(2)}, u32[]{:S(2)}) collective-permute-start(bf16[240,128]{1,0:T(8,128)(2,1)S(1)} %constant_dynamic-update-slice_fusion.4), channel_id=1, source_target_pairs={{0,1},{1,0},{2,3},{3,2},{4,5},{5,4},{6,7},{7,6},{8,9},{9,8},{10,11... | collective-permute-start | bytes 184328 | tf_op jit(solution)/shard_map/ppermute | solution.py:11

commit v8 on v7

--- a/solution.py
+++ b/solution.py
@@ -91,12 +91,18 @@
         return jnp.concatenate([jnp.where(which == 0, lower, upper), jnp.where(which == 0, upper, lower)], axis=axis)
 
     def rows_at(array, which):
-        split = array.reshape(-1, 2, rows, array.shape[1])
-        return jnp.where(which == 0, split[:, 0], split[:, 1]).reshape(-1, array.shape[1])
+        return array.reshape(-1, 2, rows, array.shape[1])[:, which].reshape(-1, array.shape[1])
+
+    def paired(first, second):
+        blocks = [block.reshape(-1, 1, rows, block.shape[1]) for block in (first, second)]
+        return jnp.concatenate(blocks, axis=1).reshape(-1, first.shape[1])
+
+    def turned(array):
+        return paired(rows_at(array, 1), rows_at(array, 0))
 
     weight_other = over_core(enc_weight[0])
     mine = lax.dynamic_slice(resid, (layer, 0, half * cols), (1, rows, cols))[0]
-    pair, weight_other, bias, blocks = hold((ordered(side, mine, over_x(mine)), weight_other, enc_bias[0], blocks))
+    pair, weight_other, bias, blocks = hold((paired(mine, over_x(mine)), weight_other, enc_bias[0], blocks))
     column = along_z(pair)
 
     own_other = over_x(decoder_part(decoder, layer, 1 - side))
@@ -109,8 +115,9 @@
 
     partial = half_preacts(resid_half, enc_weight[0], weight_other, bias, half)
     acts = ((partial + over_core(partial)) * jnp.concatenate(firing, axis=1)).astype(BF16)
-    acts_y, acts_x = over_y(acts), over_x(acts)
-    target, _ = hold((target, acts))
+    acts_turned = turned(acts)
+    acts_y, acts_x = over_y(acts), over_x(acts_turned)
+    target, _ = hold((target, acts_turned))
     start = half * cols
 
     def aim_own(where):
@@ -118,28 +125,30 @@
 
     aim_other = over_x(aim_own(1 - side))
     aim_shared = lax.dynamic_slice(target, (1, 0, start + layer * part), (1, rows, part))[0]
-    resid_swapped, _ = hold((resid_half, acts_x))
-    resid_other = over_core(resid_swapped)
-
-    leaving = times(rows_at(acts, 1 - side), shared_mine) + times(rows_at(acts_y, 1 - side), shared_other)
-    staying = times(rows_at(acts, side), shared_mine) + times(rows_at(acts_y, side), shared_other)
+
+    leaving = times(rows_at(acts, 1), shared_mine) + times(rows_at(acts_y, 1), shared_other)
+    staying = times(rows_at(acts, 0), shared_mine) + times(rows_at(acts_y, 0), shared_other)
     arrived = over_x(leaving.astype(BF16))
     product = times(acts, own_mine) + times(acts_x, own_other)
-    arrived, staying, aim_other = hold((arrived, staying, aim_other))
+    arrived, staying = hold((arrived, staying))
+    own_terms = sent_along_z(product)
     shared_terms = sent_along_z(staying + arrived.astype(F32))
-    own_terms = sent_along_z(product)
+    terms = hold((*shared_terms, *own_terms))
+    shared_terms, own_terms = terms[:far], terms[far:]
+    err_own = (added(own_terms) - paired(aim_own(side), aim_other).astype(F32)).astype(BF16)
+    own_column = along_z(err_own)
     err_shared = (added(shared_terms) - aim_shared.astype(F32)).astype(BF16)
-    err_own = (added(own_terms) - ordered(side, aim_own(side), aim_other).astype(F32)).astype(BF16)
 
     shared_near = jnp.concatenate(along_z(err_shared), axis=0)
-    pairs = [block.reshape(far, 1, rows, part) for block in (shared_near, over_x(shared_near))]
-    errs_shared = ordered(side, *pairs, axis=1).reshape(tokens, part)
-    errs_own = jnp.concatenate(along_z(err_own), axis=0)
+    resid_swapped, _ = hold((resid_half, shared_near))
+    resid_other = over_core(resid_swapped)
+    errs_shared = paired(shared_near, over_x(shared_near))
+    errs_own = jnp.concatenate(own_column, axis=0)
 
     grads = jnp.concatenate(
         [
             times_transposed(errs_own, own_mine) + times_transposed(errs_shared, shared_mine),
-            times_transposed(errs_own, own_other),
+            turned(times_transposed(errs_own, own_other)),
             times_transposed(errs_shared, shared_other),
         ],
         axis=0,
@@ -155,11 +164,11 @@
         tiles = message[tokens:].reshape(part // latents, rows, latents)
         return message[:tokens].astype(F32), jnp.concatenate([tiles[i] for i in range(part // latents)], axis=1)
 
-    from_x, own_there = without_errors(over_x(with_errors(grads[tokens:2 * tokens], rows_at(err_own, 1 - side))))
+    from_x, own_there = without_errors(over_x(with_errors(grads[tokens:2 * tokens], rows_at(err_own, 1))))
     from_y, shared_there = without_errors(over_y(with_errors(grads[2 * tokens:], err_shared)))
     errors = jnp.where(
         layer == 0,
-        ordered(side, rows_at(err_own, side), own_there, axis=1),
+        ordered(side, rows_at(err_own, 0), own_there, axis=1),
         jnp.concatenate([shared_there, err_shared], axis=1),
     )
     grad_pre = (grads[:tokens] + from_x + from_y) * gate

time: 71.5 us -> 68.7 us (0.961)
  waiting for transfers between devices: 23 us -> 19.7 us
  starting transfers between devices: 32.7 us -> 34.9 us
  other arithmetic: 4.84 us -> 3.16 us
    ppermute x29, waiting for transfers between devices: 23 us -> 19.7 us  [crossed(): lax.ppermute(block, axis, [(i, i ^ mask) for i in range(lax.axis_size(axi...]
    ppermute x29, starting transfers between devices: 32.7 us -> 34.9 us  [crossed(): lax.ppermute(block, axis, [(i, i ^ mask) for i in range(lax.axis_size(axi...]
    select_n x7 -> x1, other arithmetic: 2.32 us -> 0.64 us  [two_layers(): jnp.where(layer == 0, ordered(side, rows_at(err_own, 0), own_there, axis=...]
    another operation x0 -> x3, local copies, waits for them, and re-layouts: none -> 1.6 us  [the longest x2 1.6 us: paired(): block.reshape(-1, 1, rows, block.shape[1])]
    squeeze x2 -> x0, local copies, waits for them, and re-layouts: 1.57 us -> none  [the longest x1 0.82 us: two_layers(): mine = lax.dynamic_slice(resid, (layer, 0, half * cols), (1, rows, cols))[0]]
  transfers between devices with their start and end apart: 29 -> 29, of which waited for: 15 -> 12; matrix products, arithmetic and copies ran while one was open for 14% -> 11% of each run, Pallas kernels for 0% -> 0%
where the time goes in v8:
time: 68.7 us; the launch traced here: 68.4 us
  starting transfers between devices  34.9 us (51%)
  waiting for transfers between devices  19.7 us (29%)
  matrix products  4.17 us (6%)
  local copies, waits for them, and re-layouts  3.97 us (6%)
  other arithmetic  3.16 us (5%)
  between operations  2.43 us (4%)
    ppermute x29, starting transfers between devices, crossed(): lax.ppermute(block, axis, [(i, i ^ mask) for i in range(lax.axis_size(axi...  34.9 us
    ppermute x29, waiting for transfers between devices, crossed(): lax.ppermute(block, axis, [(i, i ^ mask) for i in range(lax.axis_size(axi...  19.7 us
    squeeze x1, local copies, waits for them, and re-layouts, decoder_part(): lax.dynamic_slice(decoder, (which, 0, where * part), (1, 2 * latents, part))  2.01 us
    dot_general x7, matrix products, times(): return jnp.dot(left, right, preferred_element_type=F32)  1.61 us
    another operation x2, local copies, waits for them, and re-layouts, paired(): block.reshape(-1, 1, rows, block.shape[1])  1.6 us
  transfers between devices with their start and end apart: 29, of which 12 were waited for; matrix products, arithmetic and copies ran while one was open for 11% of the time, Pallas kernels for 0%

profile of v8, /device:TPU:0, one launch (start us, length us, event | category | flops | bytes accessed | tf_op | source)
XLA Modules:
  0.0 68.4 jit_solution(4094845146123631488)
XLA Ops:
  0.6 0.5 collective-permute-start.3
  1.2 0.8 %dynamic-slice_bitcast_fusion.3 = (bf16[1,1,16,1792]{3,2,1,0:T(8,128)(2,1)S(1)}, bf16[16,1792]{1,0:T(8,128)(2,1)S(1)}) fusion(bf16[2,16,3584]{2,1,0:T(8,128)(2,1)} %param.6, s32[]{:T(128)S(6)} %select_n.156, s32[]{:T(128)S(6)} %select_n.161), kind=kLoop, calls=%fused_computation.89 | loop fusion | bytes 172040 | tf_op jit(solution)/shard_map/reshape;squeeze | solution.py:97
  2.0 2.6 %collective-permute-start.2 = (bf16[16,1792]{1,0:T(8,128)(2,1)S(1)}, bf16[16,1792]{1,0:T(8,128)(2,1)S(1)}, u32[]{:S(2)}, u32[]{:S(2)}) collective-permute-start(bf16[16,1792]{1,0:T(8,128)(2,1)S(1)} %get-tuple-element.67), channel_id=1, source_target_pairs={{0,1},{1,0},{2,3},{3,2},{4,5},{5,4},{6,7},{7,6},{8,9},{9,8},{10,11... | collective-permute-start | bytes 172040 | tf_op jit(solution)/shard_map/ppermute | solution.py:11
  4.6 2.0 %dynamic-slice_bitcast_fusion = (bf16[256,896]{1,0:T(8,128)(2,1)}, bf16[256,896]{1,0:T(8,128)(2,1)S(1)}) fusion(bf16[2,256,1792]{2,1,0:T(8,128)(2,1)} %bitcast.117, s32[]{:T(128)S(6)} %select_n.158, s32[]{:T(128)S(6)} %select_n.159, s32[]{:T(128)S(6)} %select_n.156, s32[]{:T(128)S(6)} %select_n.157), kind=kLoop, calls=%fused_computation.24 | loop fusion | bytes 1835024 | tf_op jit(solution)/shard_map/squeeze | solution.py:88
  6.6 1.5 %collective-permute-start.1 = (bf16[256,896]{1,0:T(8,128)(2,1)}, bf16[256,896]{1,0:T(8,128)(2,1)S(1)}, u32[]{:S(2)}, u32[]{:S(2)}) collective-permute-start(bf16[256,896]{1,0:T(8,128)(2,1)} %get-tuple-element.57), channel_id=1, source_target_pairs={{0,16},{8,24},{16,0},{24,8},{1,17},{9,25},{17,1},{25,9},{2,18},{10... | collective-permute-start | bytes 1376264 | tf_op jit(solution)/shard_map/ppermute | solution.py:11
  8.2 0.5 collective-permute-start
  8.7 0.0 collective-permute-done.2
  8.7 3.7 %collective-permute-start.6 = (bf16[32,1792]{1,0:T(8,128)(2,1)S(1)}, bf16[32,1792]{1,0:T(8,128)(2,1)S(1)}, u32[]{:S(2)}, u32[]{:S(2)}) collective-permute-start(bf16[32,1792]{1,0:T(8,128)(2,1)S(1)} %bitcast.128), channel_id=1, source_target_pairs={{0,6},{1,7},{2,4},{3,5},{4,2},{5,3},{6,0},{7,1},{8,14},{9,15},{10,... | collective-permute-start | bytes 344072 | tf_op jit(solution)/shard_map/ppermute | solution.py:11
  12.4 0.0 collective-permute-start.5
  12.4 0.8 %collective-permute-start.4 = (bf16[32,1792]{1,0:T(8,128)(2,1)S(1)}, bf16[32,1792]{1,0:T(8,128)(2,1)S(1)}, u32[]{:S(2)}, u32[]{:S(2)}) collective-permute-start(bf16[32,1792]{1,0:T(8,128)(2,1)S(1)} %bitcast.130), channel_id=1, source_target_pairs={{0,2},{1,3},{2,0},{3,1},{4,6},{5,7},{6,4},{7,5},{8,10},{9,11},{10,... | collective-permute-start | bytes 344072 | tf_op jit(solution)/shard_map/ppermute | solution.py:11
  13.2 0.2 bitcast_select_fusion.1
  13.4 0.0 copy-start.3
  13.4 0.0 copy-start
  13.4 5.9 %collective-permute-done.1 = bf16[256,896]{1,0:T(8,128)(2,1)S(1)} collective-permute-done((bf16[256,896]{1,0:T(8,128)(2,1)}, bf16[256,896]{1,0:T(8,128)(2,1)S(1)}, u32[]{:S(2)}, u32[]{:S(2)}) %collective-permute-start.1) | collective-permute-done | bytes 458784 | tf_op jit(solution)/shard_map/ppermute | solution.py:11
  19.3 1.0 %collective-permute-done = bf16[256,896]{1,0:T(8,128)(2,1)S(1)} collective-permute-done((bf16[256,896]{1,0:T(8,128)(2,1)S(1)}, bf16[256,896]{1,0:T(8,128)(2,1)S(1)}, u32[]{:S(2)}, u32[]{:S(2)}) %collective-permute-start) | collective-permute-done | bytes 458784 | tf_op jit(solution)/shard_map/ppermute | solution.py:11
  20.4 1.4 %collective-permute-done.5 = bf16[32,1792]{1,0:T(8,128)(2,1)S(1)} collective-permute-done((bf16[32,1792]{1,0:T(8,128)(2,1)S(1)}, bf16[32,1792]{1,0:T(8,128)(2,1)S(1)}, u32[]{:S(2)}, u32[]{:S(2)}) %collective-permute-start.5) | collective-permute-done | bytes 114720 | tf_op jit(solution)/shard_map/ppermute | solution.py:11
  21.7 0.0 collective-permute-done.4
  21.8 0.3 convolution_add_fusion.4
  22.1 0.1 collective-permute-start.7
  22.3 0.6 compare_reduce_fusion
  24.3 0.6 collective-permute-start.8
  24.9 1.6 %collective-permute-start.13 = (bf16[128,256]{1,0:T(8,128)(2,1)S(1)}, bf16[128,256]{1,0:T(8,128)(2,1)S(1)}, u32[]{:S(2)}, u32[]{:S(2)}) collective-permute-start(bf16[128,256]{1,0:T(8,128)(2,1)S(1)} %bitcast.141), channel_id=1, source_target_pairs={{0,1},{1,0},{2,3},{3,2},{4,5},{5,4},{6,7},{7,6},{8,9},{9,8},{10,11... | collective-permute-start | bytes 196616 | tf_op jit(solution)/shard_map/ppermute | solution.py:11
  26.4 0.8 %dynamic-slice_bitcast_fusion.5 = (bf16[1,1,16,896]{3,2,1,0:T(8,128)(2,1)S(1)}, bf16[16,896]{1,0:T(8,128)(2,1)S(1)}) fusion(bf16[3,16,3584]{2,1,0:T(8,128)(2,1)} %param.7, s32[]{:T(128)S(6)} %select_n.170, s32[]{:T(128)S(6)} %select_n.171, s32[]{:T(128)S(6)} %select_n.172), kind=kLoop, calls=%fused_computation.97 | loop fusion | bytes 114700 | tf_op jit(solution)/shard_map/reshape;squeeze | solution.py:97
  27.2 0.5 collective-permute-start.17
  27.7 0.2 fusion.14
  27.9 0.2 fusion.12
  28.1 0.6 collective-permute-done.8
  28.8 0.2 fusion.1
  29.0 1.6 %collective-permute-start.9 = (bf16[64,896]{1,0:T(8,128)(2,1)S(1)}, bf16[64,896]{1,0:T(8,128)(2,1)S(1)}, u32[]{:S(2)}, u32[]{:S(2)}) collective-permute-start(bf16[64,896]{1,0:T(8,128)(2,1)S(1)} %fusion.1), channel_id=1, source_target_pairs={{0,1},{1,0},{2,3},{3,2},{4,5},{5,4},{6,7},{7,6},{8,9},{9,8},{10,11... | collective-permute-start | bytes 344072 | tf_op jit(solution)/shard_map/ppermute | solution.py:11
  30.6 0.2 fusion.46
  30.8 0.2 fusion.45
  31.1 2.5 %collective-permute-start.16 = (bf16[32,896]{1,0:T(8,128)(2,1)S(1)}, bf16[32,896]{1,0:T(8,128)(2,1)S(1)}, u32[]{:S(2)}, u32[]{:S(2)}) collective-permute-start(bf16[32,896]{1,0:T(8,128)(2,1)S(1)} %get-tuple-element.63), channel_id=1, source_target_pairs={{0,6},{1,7},{2,4},{3,5},{4,2},{5,3},{6,0},{7,1},{8,14},{9,15},{10,... | collective-permute-start | bytes 172040 | tf_op jit(solution)/shard_map/ppermute | solution.py:11
  33.6 1.9 %collective-permute-start.14 = (bf16[32,896]{1,0:T(8,128)(2,1)S(1)}, bf16[32,896]{1,0:T(8,128)(2,1)S(1)}, u32[]{:S(2)}, u32[]{:S(2)}) collective-permute-start(bf16[32,896]{1,0:T(8,128)(2,1)S(1)} %get-tuple-element.65), channel_id=1, source_target_pairs={{0,2},{1,3},{2,0},{3,1},{4,6},{5,7},{6,4},{7,5},{8,10},{9,11},{10,... | collective-permute-start | bytes 172040 | tf_op jit(solution)/shard_map/ppermute | solution.py:11
  35.5 0.2 convolution_add_fusion.1
  35.8 2.5 %collective-permute-start.12 = (bf16[16,896]{1,0:T(8,128)(2,1)S(1)}, bf16[16,896]{1,0:T(8,128)(2,1)S(1)}, u32[]{:S(2)}, u32[]{:S(2)}) collective-permute-start(bf16[16,896]{1,0:T(8,128)(2,1)S(1)} %get-tuple-element.70), channel_id=1, source_target_pairs={{0,6},{1,7},{2,4},{3,5},{4,2},{5,3},{6,0},{7,1},{8,14},{9,15},{10,... | collective-permute-start | bytes 86024 | tf_op jit(solution)/shard_map/ppermute | solution.py:11
  38.3 1.9 %collective-permute-start.10 = (bf16[16,896]{1,0:T(8,128)(2,1)S(1)}, bf16[16,896]{1,0:T(8,128)(2,1)S(1)}, u32[]{:S(2)}, u32[]{:S(2)}) collective-permute-start(bf16[16,896]{1,0:T(8,128)(2,1)S(1)} %get-tuple-element.72), channel_id=1, source_target_pairs={{0,2},{1,3},{2,0},{3,1},{4,6},{5,7},{6,4},{7,5},{8,10},{9,11},{10,... | collective-permute-start | bytes 86024 | tf_op jit(solution)/shard_map/ppermute | solution.py:11
  40.3 1.5 %collective-permute-done.12 = bf16[16,896]{1,0:T(8,128)(2,1)S(1)} collective-permute-done((bf16[16,896]{1,0:T(8,128)(2,1)S(1)}, bf16[16,896]{1,0:T(8,128)(2,1)S(1)}, u32[]{:S(2)}, u32[]{:S(2)}) %collective-permute-start.12) | collective-permute-done | bytes 28704 | tf_op jit(solution)/shard_map/ppermute | solution.py:11
  41.8 1.3 %collective-permute-done.11 = bf16[16,896]{1,0:T(8,128)(2,1)S(1)} collective-permute-done((bf16[16,896]{1,0:T(8,128)(2,1)S(1)}, bf16[16,896]{1,0:T(8,128)(2,1)S(1)}, u32[]{:S(2)}, u32[]{:S(2)}) %collective-permute-start.11) | collective-permute-done | bytes 28704 | tf_op jit(solution)/shard_map/ppermute | solution.py:11
  43.1 0.8 %fusion.24 = bf16[16,896]{1,0:T(8,128)(2,1)S(1)} fusion(bf16[16,896]{1,0:T(8,128)(2,1)S(1)} %collective-permute-done.10, bf16[16,896]{1,0:T(8,128)(2,1)S(1)} %collective-permute-done.11, f32[16,896]{1,0:T(8,128)S(1)} %slice.251, bf16[16,896]{1,0:T(8,128)(2,1)S(1)} %collective-permute-done.12, bf16[3,16,3584]{2,1,0:T(8,128)(2,1)} %param.7, s32[]{:T(128)S(6)} %select_n.174), kind=kLoop, calls=%fused_computation.87 | loop fusion | flops 129024 | bytes 200708 | tf_op jit(solution)/shard_map/convert_element_type | solution.py:140
  43.9 1.8 %collective-permute-start.23 = (bf16[16,896]{1,0:T(8,128)(2,1)S(1)}, bf16[16,896]{1,0:T(8,128)(2,1)S(1)}, u32[]{:S(2)}, u32[]{:S(2)}) collective-permute-start(bf16[16,896]{1,0:T(8,128)(2,1)S(1)} %fusion.24), channel_id=1, source_target_pairs={{0,6},{1,7},{2,4},{3,5},{4,2},{5,3},{6,0},{7,1},{8,14},{9,15},{10,... | collective-permute-start | bytes 86024 | tf_op jit(solution)/shard_map/ppermute | solution.py:11
  45.7 0.7 %collective-permute-start.22 = (bf16[16,896]{1,0:T(8,128)(2,1)S(1)}, bf16[16,896]{1,0:T(8,128)(2,1)S(1)}, u32[]{:S(2)}, u32[]{:S(2)}) collective-permute-start(bf16[16,896]{1,0:T(8,128)(2,1)S(1)} %fusion.24), channel_id=1, source_target_pairs={{0,4},{1,5},{2,6},{3,7},{4,0},{5,1},{6,2},{7,3},{8,12},{9,13},{10,... | collective-permute-start | bytes 86024 | tf_op jit(solution)/shard_map/ppermute | solution.py:11
  46.4 1.9 %collective-permute-start.21 = (bf16[16,896]{1,0:T(8,128)(2,1)S(1)}, bf16[16,896]{1,0:T(8,128)(2,1)S(1)}, u32[]{:S(2)}, u32[]{:S(2)}) collective-permute-start(bf16[16,896]{1,0:T(8,128)(2,1)S(1)} %fusion.24), channel_id=1, source_target_pairs={{0,2},{1,3},{2,0},{3,1},{4,6},{5,7},{6,4},{7,5},{8,10},{9,11},{10,... | collective-permute-start | bytes 86024 | tf_op jit(solution)/shard_map/ppermute | solution.py:11
  48.4 1.8 %collective-permute-start.20 = (bf16[32,896]{1,0:T(8,128)(2,1)S(1)}, bf16[32,896]{1,0:T(8,128)(2,1)S(1)}, u32[]{:S(2)}, u32[]{:S(2)}) collective-permute-start(bf16[32,896]{1,0:T(8,128)(2,1)S(1)} %fusion.21), channel_id=1, source_target_pairs={{0,6},{1,7},{2,4},{3,5},{4,2},{5,3},{6,0},{7,1},{8,14},{9,15},{10,... | collective-permute-start | bytes 172040 | tf_op jit(solution)/shard_map/ppermute | solution.py:11
  50.2 2.6 %collective-permute-start.18 = (bf16[32,896]{1,0:T(8,128)(2,1)S(1)}, bf16[32,896]{1,0:T(8,128)(2,1)S(1)}, u32[]{:S(2)}, u32[]{:S(2)}) collective-permute-start(bf16[32,896]{1,0:T(8,128)(2,1)S(1)} %fusion.21), channel_id=1, source_target_pairs={{0,2},{1,3},{2,0},{3,1},{4,6},{5,7},{6,4},{7,5},{8,10},{9,11},{10,... | collective-permute-start | bytes 172040 | tf_op jit(solution)/shard_map/ppermute | solution.py:11
  52.9 0.6 collective-permute-start.24
  53.5 1.0 %collective-permute-done.20 = bf16[32,896]{1,0:T(8,128)(2,1)S(1)} collective-permute-done((bf16[32,896]{1,0:T(8,128)(2,1)S(1)}, bf16[32,896]{1,0:T(8,128)(2,1)S(1)}, u32[]{:S(2)}, u32[]{:S(2)}) %collective-permute-start.20) | collective-permute-done | bytes 57376 | tf_op jit(solution)/shard_map/ppermute | solution.py:11
  54.4 1.2 %collective-permute-done.19 = bf16[32,896]{1,0:T(8,128)(2,1)S(1)} collective-permute-done((bf16[32,896]{1,0:T(8,128)(2,1)S(1)}, bf16[32,896]{1,0:T(8,128)(2,1)S(1)}, u32[]{:S(2)}, u32[]{:S(2)}) %collective-permute-start.19) | collective-permute-done | bytes 57376 | tf_op jit(solution)/shard_map/ppermute | solution.py:11
  55.7 0.3 fusion.25
  56.0 1.7 %collective-permute-done.24 = bf16[64,896]{1,0:T(8,128)(2,1)S(1)} collective-permute-done((bf16[64,896]{1,0:T(8,128)(2,1)S(1)}, bf16[64,896]{1,0:T(8,128)(2,1)S(1)}, u32[]{:S(2)}, u32[]{:S(2)}) %collective-permute-start.24) | collective-permute-done | bytes 114720 | tf_op jit(solution)/shard_map/ppermute | solution.py:11
  57.8 0.3 fusion.47
  58.1 0.3 fusion.10
  58.4 0.3 convolution_add_fusion.3
  58.8 0.1 collective-permute-start.25
  58.8 0.5 collective-permute-start.28
  59.3 0.9 %collective-permute-done.25 = f32[384,128]{1,0:T(8,128)S(1)} collective-permute-done((f32[384,128]{1,0:T(8,128)S(1)}, f32[384,128]{1,0:T(8,128)S(1)}, u32[]{:S(2)}, u32[]{:S(2)}) %collective-permute-start.25) | collective-permute-done | bytes 196640 | tf_op jit(solution)/shard_map/ppermute | solution.py:11
  60.3 0.1 fusion.38
  60.5 1.0 %collective-permute-start.27 = (bf16[240,128]{1,0:T(8,128)(2,1)S(1)}, bf16[240,128]{1,0:T(8,128)(2,1)S(1)}, u32[]{:S(2)}, u32[]{:S(2)}) collective-permute-start(bf16[240,128]{1,0:T(8,128)(2,1)S(1)} %constant_dynamic-update-slice_fusion.19), channel_id=1, source_target_pairs={{0,16},{8,24},{16,0},{24,8},{1,17},{9,25},{17,1},{25,9},{2,18},{10... | collective-permute-start | bytes 184328 | tf_op jit(solution)/shard_map/ppermute | solution.py:11
  61.5 1.0 %collective-permute-start.26 = (bf16[240,128]{1,0:T(8,128)(2,1)S(1)}, bf16[240,128]{1,0:T(8,128)(2,1)S(1)}, u32[]{:S(2)}, u32[]{:S(2)}) collective-permute-start(bf16[240,128]{1,0:T(8,128)(2,1)S(1)} %constant_dynamic-update-slice_fusion.4), channel_id=1, source_target_pairs={{0,1},{1,0},{2,3},{3,2},{4,5},{5,4},{6,7},{7,6},{8,9},{9,8},{10,11... | collective-permute-start | bytes 184328 | tf_op jit(solution)/shard_map/ppermute | solution.py:11
  62.5 2.3 %collective-permute-done.27 = bf16[240,128]{1,0:T(8,128)(2,1)S(1)} collective-permute-done((bf16[240,128]{1,0:T(8,128)(2,1)S(1)}, bf16[240,128]{1,0:T(8,128)(2,1)S(1)}, u32[]{:S(2)}, u32[]{:S(2)}) %collective-permute-start.27) | collective-permute-done | bytes 61472 | tf_op jit(solution)/shard_map/ppermute | solution.py:11
  64.8 0.8 %collective-permute-done.26 = bf16[240,128]{1,0:T(8,128)(2,1)S(1)} collective-permute-done((bf16[240,128]{1,0:T(8,128)(2,1)S(1)}, bf16[240,128]{1,0:T(8,128)(2,1)S(1)}, u32[]{:S(2)}, u32[]{:S(2)}) %collective-permute-start.26) | collective-permute-done | bytes 61472 | tf_op jit(solution)/shard_map/ppermute | solution.py:11
  65.8 0.5 fusion.27
  66.3 0.6 maximum_select_fusion
  67.0 0.1 broadcast_select_fusion.1
  67.0 1.4 %fusion = bf16[1,3584,128]{2,1,0:T(8,128)(2,1)} fusion(bf16[128,1792]{1,0:T(8,128)(2,1)S(1)} %get-tuple-element.60, bf16[128,1792]{1,0:T(8,128)(2,1)S(1)} %get-tuple-element.59, f32[384,128]{1,0:T(8,128)S(1)} %get-tuple-element.52, bf16[240,128]{1,0:T(8,128)(2,1)S(1)} %collective-permute-done.27, bf16[240,128]{1,0:T(8,128)(2,1)S(1)} %collective-permute-done.26, ...), kind=kOutput, calls=%fused_computation.1 | convolution fusion | flops 119832576 | bytes 1966084 | tf_op jit(solution)/shard_map/dot_general | solution.py:48
  (81 shorter events, 0.7 us)
Async XLA Ops:
  0.6 12.5 %copy-start.1 = (bf16[1,3584,128]{2,1,0:T(8,128)(2,1)S(1)}, bf16[1,3584,128]{2,1,0:T(8,128)(2,1)}, u32[]{:S(2)}) copy-start(bf16[1,3584,128]{2,1,0:T(8,128)(2,1)} %param.8) | copy-start | bytes 2752516
  0.6 8.1 %collective-permute-start.3 = (bf16[3584,128]{1,0:T(8,128)(2,1)}, bf16[3584,128]{1,0:T(8,128)(2,1)S(1)}, u32[]{:S(2)}, u32[]{:S(2)}) collective-permute-start(bf16[3584,128]{1,0:T(8,128)(2,1)} %bitcast.136), channel_id=1, source_target_pairs={{0,8},{8,0},{16,24},{24,16},{1,9},{9,1},{17,25},{25,17},{2,10},{10... | collective-permute-start | bytes 2752520 | tf_op jit(solution)/shard_map/ppermute | solution.py:11
  2.0 6.7 %collective-permute-start.2 = (bf16[16,1792]{1,0:T(8,128)(2,1)S(1)}, bf16[16,1792]{1,0:T(8,128)(2,1)S(1)}, u32[]{:S(2)}, u32[]{:S(2)}) collective-permute-start(bf16[16,1792]{1,0:T(8,128)(2,1)S(1)} %get-tuple-element.67), channel_id=1, source_target_pairs={{0,1},{1,0},{2,3},{3,2},{4,5},{5,4},{6,7},{7,6},{8,9},{9,8},{10,11... | collective-permute-start | bytes 172040 | tf_op jit(solution)/shard_map/ppermute | solution.py:11
  4.6 8.7 %copy-start.2 = (f32[1,128]{1,0:T(1,128)S(1)}, f32[1,128]{1,0:T(1,128)}, u32[]{:S(2)}) copy-start(f32[1,128]{1,0:T(1,128)} %param.9) | copy-start | bytes 1540
  6.6 12.7 %collective-permute-start.1 = (bf16[256,896]{1,0:T(8,128)(2,1)}, bf16[256,896]{1,0:T(8,128)(2,1)S(1)}, u32[]{:S(2)}, u32[]{:S(2)}) collective-permute-start(bf16[256,896]{1,0:T(8,128)(2,1)} %get-tuple-element.57), channel_id=1, source_target_pairs={{0,16},{8,24},{16,0},{24,8},{1,17},{9,25},{17,1},{25,9},{2,18},{10... | collective-permute-start | bytes 1376264 | tf_op jit(solution)/shard_map/ppermute | solution.py:11
  8.2 12.2 %collective-permute-start = (bf16[256,896]{1,0:T(8,128)(2,1)S(1)}, bf16[256,896]{1,0:T(8,128)(2,1)S(1)}, u32[]{:S(2)}, u32[]{:S(2)}) collective-permute-start(bf16[256,896]{1,0:T(8,128)(2,1)S(1)} %get-tuple-element.58), channel_id=1, source_target_pairs={{0,1},{1,0},{2,3},{3,2},{4,5},{5,4},{6,7},{7,6},{8,9},{9,8},{10,11... | collective-permute-start | bytes 1376264 | tf_op jit(solution)/shard_map/ppermute | solution.py:11
  8.7 11.7 %collective-permute-start.6 = (bf16[32,1792]{1,0:T(8,128)(2,1)S(1)}, bf16[32,1792]{1,0:T(8,128)(2,1)S(1)}, u32[]{:S(2)}, u32[]{:S(2)}) collective-permute-start(bf16[32,1792]{1,0:T(8,128)(2,1)S(1)} %bitcast.128), channel_id=1, source_target_pairs={{0,6},{1,7},{2,4},{3,5},{4,2},{5,3},{6,0},{7,1},{8,14},{9,15},{10,... | collective-permute-start | bytes 344072 | tf_op jit(solution)/shard_map/ppermute | solution.py:11
  12.4 9.4 %collective-permute-start.5 = (bf16[32,1792]{1,0:T(8,128)(2,1)S(1)}, bf16[32,1792]{1,0:T(8,128)(2,1)S(1)}, u32[]{:S(2)}, u32[]{:S(2)}) collective-permute-start(bf16[32,1792]{1,0:T(8,128)(2,1)S(1)} %bitcast.129), channel_id=1, source_target_pairs={{0,4},{1,5},{2,6},{3,7},{4,0},{5,1},{6,2},{7,3},{8,12},{9,13},{10,... | collective-permute-start | bytes 344072 | tf_op jit(solution)/shard_map/ppermute | solution.py:11
  12.4 9.4 %collective-permute-start.4 = (bf16[32,1792]{1,0:T(8,128)(2,1)S(1)}, bf16[32,1792]{1,0:T(8,128)(2,1)S(1)}, u32[]{:S(2)}, u32[]{:S(2)}) collective-permute-start(bf16[32,1792]{1,0:T(8,128)(2,1)S(1)} %bitcast.130), channel_id=1, source_target_pairs={{0,2},{1,3},{2,0},{3,1},{4,6},{5,7},{6,4},{7,5},{8,10},{9,11},{10,... | collective-permute-start | bytes 344072 | tf_op jit(solution)/shard_map/ppermute | solution.py:11
  13.4 8.9 %copy-start.3 = (s32[2,1,12]{2,1,0:T(1,128)S(1)}, s32[2,1,12]{2,1,0:T(1,128)}, u32[]{:S(2)}) copy-start(s32[2,1,12]{2,1,0:T(1,128)} %param.11) | copy-start | bytes 292
  13.4 14.3 %copy-start = (bf16[1,2,2,128,1792]{4,3,2,1,0:T(8,128)(2,1)S(1)}, bf16[1,2,2,128,1792]{4,3,2,1,0:T(8,128)(2,1)}, u32[]{:S(2)}) copy-start(bf16[1,2,2,128,1792]{4,3,2,1,0:T(8,128)(2,1)} %param.10) | copy-start | bytes 5505028
  22.1 2.1 %collective-permute-start.7 = (f32[128,256]{1,0:T(8,128)S(1)}, f32[128,256]{1,0:T(8,128)S(1)}, u32[]{:S(2)}, u32[]{:S(2)}) collective-permute-start(f32[128,256]{1,0:T(8,128)S(1)} %convolution_add_fusion.4), channel_id=1, source_target_pairs={{0,8},{8,0},{16,24},{24,16},{1,9},{9,1},{17,25},{25,17},{2,10},{10... | collective-permute-start | bytes 393224 | tf_op jit(solution)/shard_map/ppermute | solution.py:11
  24.3 4.5 %collective-permute-start.8 = (bf16[128,256]{1,0:T(8,128)(2,1)S(1)}, bf16[128,256]{1,0:T(8,128)(2,1)S(1)}, u32[]{:S(2)}, u32[]{:S(2)}) collective-permute-start(bf16[128,256]{1,0:T(8,128)(2,1)S(1)} %multiply_convert_fusion), channel_id=1, source_target_pairs={{0,16},{8,24},{16,0},{24,8},{1,17},{9,25},{17,1},{25,9},{2,18},{10... | collective-permute-start | bytes 196616 | tf_op jit(solution)/shard_map/ppermute | solution.py:11
  24.9 5.7 %collective-permute-start.13 = (bf16[128,256]{1,0:T(8,128)(2,1)S(1)}, bf16[128,256]{1,0:T(8,128)(2,1)S(1)}, u32[]{:S(2)}, u32[]{:S(2)}) collective-permute-start(bf16[128,256]{1,0:T(8,128)(2,1)S(1)} %bitcast.141), channel_id=1, source_target_pairs={{0,1},{1,0},{2,3},{3,2},{4,5},{5,4},{6,7},{7,6},{8,9},{9,8},{10,11... | collective-permute-start | bytes 196616 | tf_op jit(solution)/shard_map/ppermute | solution.py:11
  27.2 11.2 %collective-permute-start.17 = (bf16[16,896]{1,0:T(8,128)(2,1)S(1)}, bf16[16,896]{1,0:T(8,128)(2,1)S(1)}, u32[]{:S(2)}, u32[]{:S(2)}) collective-permute-start(bf16[16,896]{1,0:T(8,128)(2,1)S(1)} %get-tuple-element.62), channel_id=1, source_target_pairs={{0,1},{1,0},{2,3},{3,2},{4,5},{5,4},{6,7},{7,6},{8,9},{9,8},{10,11... | collective-permute-start | bytes 86024 | tf_op jit(solution)/shard_map/ppermute | solution.py:11
  29.0 6.7 %collective-permute-start.9 = (bf16[64,896]{1,0:T(8,128)(2,1)S(1)}, bf16[64,896]{1,0:T(8,128)(2,1)S(1)}, u32[]{:S(2)}, u32[]{:S(2)}) collective-permute-start(bf16[64,896]{1,0:T(8,128)(2,1)S(1)} %fusion.1), channel_id=1, source_target_pairs={{0,1},{1,0},{2,3},{3,2},{4,5},{5,4},{6,7},{7,6},{8,9},{9,8},{10,11... | collective-permute-start | bytes 344072 | tf_op jit(solution)/shard_map/ppermute | solution.py:11
  31.1 7.3 %collective-permute-start.16 = (bf16[32,896]{1,0:T(8,128)(2,1)S(1)}, bf16[32,896]{1,0:T(8,128)(2,1)S(1)}, u32[]{:S(2)}, u32[]{:S(2)}) collective-permute-start(bf16[32,896]{1,0:T(8,128)(2,1)S(1)} %get-tuple-element.63), channel_id=1, source_target_pairs={{0,6},{1,7},{2,4},{3,5},{4,2},{5,3},{6,0},{7,1},{8,14},{9,15},{10,... | collective-permute-start | bytes 172040 | tf_op jit(solution)/shard_map/ppermute | solution.py:11
  33.6 6.7 %collective-permute-start.15 = (bf16[32,896]{1,0:T(8,128)(2,1)S(1)}, bf16[32,896]{1,0:T(8,128)(2,1)S(1)}, u32[]{:S(2)}, u32[]{:S(2)}) collective-permute-start(bf16[32,896]{1,0:T(8,128)(2,1)S(1)} %get-tuple-element.64), channel_id=1, source_target_pairs={{0,4},{1,5},{2,6},{3,7},{4,0},{5,1},{6,2},{7,3},{8,12},{9,13},{10,... | collective-permute-start | bytes 172040 | tf_op jit(solution)/shard_map/ppermute | solution.py:11
  33.6 6.7 %collective-permute-start.14 = (bf16[32,896]{1,0:T(8,128)(2,1)S(1)}, bf16[32,896]{1,0:T(8,128)(2,1)S(1)}, u32[]{:S(2)}, u32[]{:S(2)}) collective-permute-start(bf16[32,896]{1,0:T(8,128)(2,1)S(1)} %get-tuple-element.65), channel_id=1, source_target_pairs={{0,2},{1,3},{2,0},{3,1},{4,6},{5,7},{6,4},{7,5},{8,10},{9,11},{10,... | collective-permute-start | bytes 172040 | tf_op jit(solution)/shard_map/ppermute | solution.py:11
  35.8 6.0 %collective-permute-start.12 = (bf16[16,896]{1,0:T(8,128)(2,1)S(1)}, bf16[16,896]{1,0:T(8,128)(2,1)S(1)}, u32[]{:S(2)}, u32[]{:S(2)}) collective-permute-start(bf16[16,896]{1,0:T(8,128)(2,1)S(1)} %get-tuple-element.70), channel_id=1, source_target_pairs={{0,6},{1,7},{2,4},{3,5},{4,2},{5,3},{6,0},{7,1},{8,14},{9,15},{10,... | collective-permute-start | bytes 86024 | tf_op jit(solution)/shard_map/ppermute | solution.py:11
  38.3 4.8 %collective-permute-start.11 = (bf16[16,896]{1,0:T(8,128)(2,1)S(1)}, bf16[16,896]{1,0:T(8,128)(2,1)S(1)}, u32[]{:S(2)}, u32[]{:S(2)}) collective-permute-start(bf16[16,896]{1,0:T(8,128)(2,1)S(1)} %get-tuple-element.71), channel_id=1, source_target_pairs={{0,4},{1,5},{2,6},{3,7},{4,0},{5,1},{6,2},{7,3},{8,12},{9,13},{10,... | collective-permute-start | bytes 86024 | tf_op jit(solution)/shard_map/ppermute | solution.py:11
  38.3 4.8 %collective-permute-start.10 = (bf16[16,896]{1,0:T(8,128)(2,1)S(1)}, bf16[16,896]{1,0:T(8,128)(2,1)S(1)}, u32[]{:S(2)}, u32[]{:S(2)}) collective-permute-start(bf16[16,896]{1,0:T(8,128)(2,1)S(1)} %get-tuple-element.72), channel_id=1, source_target_pairs={{0,2},{1,3},{2,0},{3,1},{4,6},{5,7},{6,4},{7,5},{8,10},{9,11},{10,... | collective-permute-start | bytes 86024 | tf_op jit(solution)/shard_map/ppermute | solution.py:11
  43.9 6.3 %collective-permute-start.23 = (bf16[16,896]{1,0:T(8,128)(2,1)S(1)}, bf16[16,896]{1,0:T(8,128)(2,1)S(1)}, u32[]{:S(2)}, u32[]{:S(2)}) collective-permute-start(bf16[16,896]{1,0:T(8,128)(2,1)S(1)} %fusion.24), channel_id=1, source_target_pairs={{0,6},{1,7},{2,4},{3,5},{4,2},{5,3},{6,0},{7,1},{8,14},{9,15},{10,... | collective-permute-start | bytes 86024 | tf_op jit(solution)/shard_map/ppermute | solution.py:11
  45.7 7.1 %collective-permute-start.22 = (bf16[16,896]{1,0:T(8,128)(2,1)S(1)}, bf16[16,896]{1,0:T(8,128)(2,1)S(1)}, u32[]{:S(2)}, u32[]{:S(2)}) collective-permute-start(bf16[16,896]{1,0:T(8,128)(2,1)S(1)} %fusion.24), channel_id=1, source_target_pairs={{0,4},{1,5},{2,6},{3,7},{4,0},{5,1},{6,2},{7,3},{8,12},{9,13},{10,... | collective-permute-start | bytes 86024 | tf_op jit(solution)/shard_map/ppermute | solution.py:11
  46.4 6.4 %collective-permute-start.21 = (bf16[16,896]{1,0:T(8,128)(2,1)S(1)}, bf16[16,896]{1,0:T(8,128)(2,1)S(1)}, u32[]{:S(2)}, u32[]{:S(2)}) collective-permute-start(bf16[16,896]{1,0:T(8,128)(2,1)S(1)} %fusion.24), channel_id=1, source_target_pairs={{0,2},{1,3},{2,0},{3,1},{4,6},{5,7},{6,4},{7,5},{8,10},{9,11},{10,... | collective-permute-start | bytes 86024 | tf_op jit(solution)/shard_map/ppermute | solution.py:11
  48.4 6.0 %collective-permute-start.20 = (bf16[32,896]{1,0:T(8,128)(2,1)S(1)}, bf16[32,896]{1,0:T(8,128)(2,1)S(1)}, u32[]{:S(2)}, u32[]{:S(2)}) collective-permute-start(bf16[32,896]{1,0:T(8,128)(2,1)S(1)} %fusion.21), channel_id=1, source_target_pairs={{0,6},{1,7},{2,4},{3,5},{4,2},{5,3},{6,0},{7,1},{8,14},{9,15},{10,... | collective-permute-start | bytes 172040 | tf_op jit(solution)/shard_map/ppermute | solution.py:11
  50.2 5.4 %collective-permute-start.19 = (bf16[32,896]{1,0:T(8,128)(2,1)S(1)}, bf16[32,896]{1,0:T(8,128)(2,1)S(1)}, u32[]{:S(2)}, u32[]{:S(2)}) collective-permute-start(bf16[32,896]{1,0:T(8,128)(2,1)S(1)} %fusion.21), channel_id=1, source_target_pairs={{0,4},{1,5},{2,6},{3,7},{4,0},{5,1},{6,2},{7,3},{8,12},{9,13},{10,... | collective-permute-start | bytes 172040 | tf_op jit(solution)/shard_map/ppermute | solution.py:11
  50.2 5.4 %collective-permute-start.18 = (bf16[32,896]{1,0:T(8,128)(2,1)S(1)}, bf16[32,896]{1,0:T(8,128)(2,1)S(1)}, u32[]{:S(2)}, u32[]{:S(2)}) collective-permute-start(bf16[32,896]{1,0:T(8,128)(2,1)S(1)} %fusion.21), channel_id=1, source_target_pairs={{0,2},{1,3},{2,0},{3,1},{4,6},{5,7},{6,4},{7,5},{8,10},{9,11},{10,... | collective-permute-start | bytes 172040 | tf_op jit(solution)/shard_map/ppermute | solution.py:11
  52.9 4.9 %collective-permute-start.24 = (bf16[64,896]{1,0:T(8,128)(2,1)S(1)}, bf16[64,896]{1,0:T(8,128)(2,1)S(1)}, u32[]{:S(2)}, u32[]{:S(2)}) collective-permute-start(bf16[64,896]{1,0:T(8,128)(2,1)S(1)} %pad_maximum_fusion.5), channel_id=1, source_target_pairs={{0,1},{1,0},{2,3},{3,2},{4,5},{5,4},{6,7},{7,6},{8,9},{9,8},{10,11... | collective-permute-start | bytes 344072 | tf_op jit(solution)/shard_map/ppermute | solution.py:11
  58.8 1.5 %collective-permute-start.25 = (f32[384,128]{1,0:T(8,128)S(1)}, f32[384,128]{1,0:T(8,128)S(1)}, u32[]{:S(2)}, u32[]{:S(2)}) collective-permute-start(f32[384,128]{1,0:T(8,128)S(1)} %slice_select_fusion), channel_id=1, source_target_pairs={{0,8},{8,0},{16,24},{24,16},{1,9},{9,1},{17,25},{25,17},{2,10},{10... | collective-permute-start | bytes 589832 | tf_op jit(solution)/shard_map/ppermute | solution.py:11
  58.8 8.1 %collective-permute-start.28 = (bf16[128,1792]{1,0:T(8,128)(2,1)S(1)}, bf16[128,1792]{1,0:T(8,128)(2,1)S(1)}, u32[]{:S(2)}, u32[]{:S(2)}) collective-permute-start(bf16[128,1792]{1,0:T(8,128)(2,1)S(1)} %constant_dynamic-update-slice_fusion), channel_id=1, source_target_pairs={{0,8},{8,0},{16,24},{24,16},{1,9},{9,1},{17,25},{25,17},{2,10},{10... | collective-permute-start | bytes 1376264 | tf_op jit(solution)/shard_map/ppermute | solution.py:11
  60.5 4.3 %collective-permute-start.27 = (bf16[240,128]{1,0:T(8,128)(2,1)S(1)}, bf16[240,128]{1,0:T(8,128)(2,1)S(1)}, u32[]{:S(2)}, u32[]{:S(2)}) collective-permute-start(bf16[240,128]{1,0:T(8,128)(2,1)S(1)} %constant_dynamic-update-slice_fusion.19), channel_id=1, source_target_pairs={{0,16},{8,24},{16,0},{24,8},{1,17},{9,25},{17,1},{25,9},{2,18},{10... | collective-permute-start | bytes 184328 | tf_op jit(solution)/shard_map/ppermute | solution.py:11
  61.5 4.2 %collective-permute-start.26 = (bf16[240,128]{1,0:T(8,128)(2,1)S(1)}, bf16[240,128]{1,0:T(8,128)(2,1)S(1)}, u32[]{:S(2)}, u32[]{:S(2)}) collective-permute-start(bf16[240,128]{1,0:T(8,128)(2,1)S(1)} %constant_dynamic-update-slice_fusion.4), channel_id=1, source_target_pairs={{0,1},{1,0},{2,3},{3,2},{4,5},{5,4},{6,7},{7,6},{8,9},{9,8},{10,11... | collective-permute-start | bytes 184328 | tf_op jit(solution)/shard_map/ppermute | solution.py:11

commit v9 on v8

--- a/solution.py
+++ b/solution.py
@@ -1,6 +1,8 @@
 import jax
 import jax.numpy as jnp
 from jax import lax
+from jax.experimental import pallas as pl
+from jax.experimental.pallas import tpu as pltpu
 from jax.sharding import PartitionSpec as P
 
 BLOCK = 128
@@ -47,6 +49,50 @@
     whole = both_halves(half, resid_half, resid_other, 1)
     grad = lax.dot_general(whole, grad_low, (((0,), (0,)), ((), ())), preferred_element_type=F32)
     return grad.astype(BF16)
+
+
+def copy_parts(place_ref, decoder_ref, target_ref, x_ref, y_ref, sems):
+    layer, half, side = place_ref[0], place_ref[1], place_ref[2]
+    depth, part = y_ref.shape
+    cols = decoder_ref.shape[2]
+
+    def columns(where, start=0):
+        return pl.ds(pl.multiple_of(start + where * part, 128), part)
+
+    copies = [
+        pltpu.make_async_copy(decoder_ref.at[layer, :, columns(1 - side)], x_ref.at[pl.ds(0, depth)], sems.at[0]),
+        pltpu.make_async_copy(decoder_ref.at[1 - layer, :, columns(1 - layer)], y_ref, sems.at[1]),
+        pltpu.make_async_copy(
+            target_ref.at[2 * layer, :, columns(1 - side, half * cols)],
+            x_ref.at[pl.ds(depth, target_ref.shape[1])],
+            sems.at[2],
+        ),
+    ]
+    for copy in copies:
+        copy.start()
+    for copy in copies:
+        copy.wait()
+
+
+def neighbours_parts(decoder, target, layer, half, side, part):
+    depth, rows = decoder.shape[1], target.shape[1]
+    place = jnp.stack([layer, half, side]).astype(jnp.int32)
+    return pl.pallas_call(
+        copy_parts,
+        out_shape=[
+            jax.ShapeDtypeStruct((depth + rows, part), decoder.dtype),
+            jax.ShapeDtypeStruct((depth, part), decoder.dtype),
+        ],
+        in_specs=[
+            pl.BlockSpec(memory_space=pltpu.SMEM),
+            pl.BlockSpec(memory_space=pl.ANY),
+            pl.BlockSpec(memory_space=pl.ANY),
+        ],
+        out_specs=[pl.BlockSpec(memory_space=pl.ANY)] * 2,
+        scratch_shapes=[pltpu.SemaphoreType.DMA((3,))],
+        cost_estimate=pl.CostEstimate(flops=0, bytes_accessed=4 * depth * part * 2, transcendentals=0),
+        name="neighbours_parts",
+    )(place, decoder, target)
 
 
 def two_layers(resid, target, enc_weight, enc_bias, dec_weight, blocks):
@@ -70,19 +116,18 @@
     def over_core(block):
         return crossed(block, "layer", 1)
 
-    def along_z(block):
-        out = [block] + [None] * (far - 1)
+    def along_z(blocks):
+        out = [blocks[0]] + [None] * (far - 1)
         for k in range(far - 1, 0, -1):
-            out[k] = crossed(block, "latent", 2 * k)
+            out[k] = crossed(blocks[k], "latent", 2 * k)
         return out
 
-    def sent_along_z(total):
+    def pieces_of(total):
         count = total.shape[0] // far
-        pieces = [total[k * count:(k + 1) * count].astype(BF16) for k in range(1, far)]
-        return [crossed(pieces[k - 1], "latent", 2 * k) for k in range(1, far)] + [total[:count]]
+        return [total[:count]] + [total[k * count:(k + 1) * count].astype(BF16) for k in range(1, far)]
 
     def added(terms):
-        return sum(term.astype(F32) for term in terms[::-1])
+        return sum(term.astype(F32) for term in terms)
 
     def decoder_part(decoder, which, where):
         return lax.dynamic_slice(decoder, (which, 0, where * part), (1, 2 * latents, part))[0]
@@ -102,12 +147,22 @@
 
     weight_other = over_core(enc_weight[0])
     mine = lax.dynamic_slice(resid, (layer, 0, half * cols), (1, rows, cols))[0]
-    pair, weight_other, bias, blocks = hold((paired(mine, over_x(mine)), weight_other, enc_bias[0], blocks))
-    column = along_z(pair)
-
-    own_other = over_x(decoder_part(decoder, layer, 1 - side))
-    shared_other = over_y(decoder_part(decoder, 1 - layer, 1 - layer))
-    decoder, own_other, shared_other, *column = hold((decoder, own_other, shared_other, *column))
+    pair, weight_other, bias, blocks, early = hold(
+        (paired(mine, over_x(mine)), weight_other, enc_bias[0], blocks, target)
+    )
+    column = along_z([pair] * far)
+
+    start = half * cols
+
+    aim_mine = lax.dynamic_slice(early, (2 * layer, 0, start + side * part), (1, rows, part))[0]
+    aim_shared = lax.dynamic_slice(early, (1, 0, start + layer * part), (1, rows, part))[0]
+
+    for_x, for_y = neighbours_parts(decoder, target, layer, half, side, part)
+    from_side, shared_other = over_x(for_x), over_y(for_y)
+    decoder, from_side, shared_other, aim_mine, aim_shared, *column = hold(
+        (decoder, from_side, shared_other, aim_mine, aim_shared, *column)
+    )
+    own_other, aim_other = from_side[:2 * latents], from_side[2 * latents:]
     own_mine, shared_mine = decoder_part(decoder, layer, side), decoder_part(decoder, 1 - layer, layer)
     resid_half = jnp.concatenate(column, axis=0)
     firing = gates(blocks, layer, slot, slots, latents, tokens)
@@ -117,58 +172,45 @@
     acts = ((partial + over_core(partial)) * jnp.concatenate(firing, axis=1)).astype(BF16)
     acts_turned = turned(acts)
     acts_y, acts_x = over_y(acts), over_x(acts_turned)
-    target, _ = hold((target, acts_turned))
-    start = half * cols
-
-    def aim_own(where):
-        return lax.dynamic_slice(target, (2 * layer, 0, start + where * part), (1, rows, part))[0]
-
-    aim_other = over_x(aim_own(1 - side))
-    aim_shared = lax.dynamic_slice(target, (1, 0, start + layer * part), (1, rows, part))[0]
 
     leaving = times(rows_at(acts, 1), shared_mine) + times(rows_at(acts_y, 1), shared_other)
     staying = times(rows_at(acts, 0), shared_mine) + times(rows_at(acts_y, 0), shared_other)
     arrived = over_x(leaving.astype(BF16))
     product = times(acts, own_mine) + times(acts_x, own_other)
     arrived, staying = hold((arrived, staying))
-    own_terms = sent_along_z(product)
-    shared_terms = sent_along_z(staying + arrived.astype(F32))
-    terms = hold((*shared_terms, *own_terms))
-    shared_terms, own_terms = terms[:far], terms[far:]
-    err_own = (added(own_terms) - paired(aim_own(side), aim_other).astype(F32)).astype(BF16)
-    own_column = along_z(err_own)
+    shared_terms = along_z(pieces_of(staying + arrived.astype(F32)))
+    count = tokens // 2
+    arrived = crossed(product[count:].astype(BF16), "latent", 4)
+    sum_own = product[:count] + arrived.astype(F32)
+    count = tokens // 4
+    arrived = crossed(sum_own[count:].astype(BF16), "latent", 2)
+    arrived, *shared_terms = hold((arrived, *shared_terms))
     err_shared = (added(shared_terms) - aim_shared.astype(F32)).astype(BF16)
-
-    shared_near = jnp.concatenate(along_z(err_shared), axis=0)
-    resid_swapped, _ = hold((resid_half, shared_near))
+    sum_own = sum_own[:count] + arrived.astype(F32)
+    err_own = (sum_own - paired(aim_mine, aim_other).astype(F32)).astype(BF16)
+
+    arrived = crossed(err_own, "latent", 2)
+    message = jnp.concatenate(along_z([err_shared] * far) + [rows_at(err_own, 1)], axis=0)
+    message, arrived, resid_swapped = hold((message, arrived, resid_half))
+    errs_own = jnp.concatenate([err_own, arrived], axis=0)
+    errs_own = jnp.concatenate([errs_own, crossed(errs_own, "latent", 4)], axis=0)
+    returned = over_x(message)
     resid_other = over_core(resid_swapped)
-    errs_shared = paired(shared_near, over_x(shared_near))
-    errs_own = jnp.concatenate(own_column, axis=0)
-
-    grads = jnp.concatenate(
-        [
-            times_transposed(errs_own, own_mine) + times_transposed(errs_shared, shared_mine),
-            turned(times_transposed(errs_own, own_other)),
-            times_transposed(errs_shared, shared_other),
-        ],
-        axis=0,
-    )
+
+    own_grads = [times_transposed(errs_own, weights) for weights in (own_mine, own_other)]
+    errs_shared = paired(message[:tokens // 2], returned[:tokens // 2])
+    shared_grads = [times_transposed(errs_shared, weights) for weights in (shared_mine, shared_other)]
+    grads = jnp.concatenate([own_grads[0] + shared_grads[0], turned(own_grads[1]), shared_grads[1]], axis=0)
     lower, upper = grads[:, :latents], grads[:, latents:]
-    grads = jnp.where(half == 0, lower, upper) + over_core(jnp.where(half == 0, upper, lower))
-
-    def with_errors(grad, block):
-        tiles = [block[:, at:at + latents] for at in range(0, part, latents)]
-        return jnp.concatenate([grad.astype(BF16)] + tiles, axis=0)
-
-    def without_errors(message):
-        tiles = message[tokens:].reshape(part // latents, rows, latents)
-        return message[:tokens].astype(F32), jnp.concatenate([tiles[i] for i in range(part // latents)], axis=1)
-
-    from_x, own_there = without_errors(over_x(with_errors(grads[tokens:2 * tokens], rows_at(err_own, 1))))
-    from_y, shared_there = without_errors(over_y(with_errors(grads[2 * tokens:], err_shared)))
+    leaving, late_shared = hold((jnp.where(half == 0, upper, lower), err_shared))
+    grads = jnp.where(half == 0, lower, upper) + over_core(leaving)
+    shared_there = over_y(late_shared)
+
+    from_x = over_x(grads[tokens:2 * tokens].astype(BF16)).astype(F32)
+    from_y = over_y(grads[2 * tokens:].astype(BF16)).astype(F32)
     errors = jnp.where(
         layer == 0,
-        ordered(side, rows_at(err_own, 0), own_there, axis=1),
+        ordered(side, rows_at(err_own, 0), returned[tokens // 2:], axis=1),
         jnp.concatenate([shared_there, err_shared], axis=1),
     )
     grad_pre = (grads[:tokens] + from_x + from_y) * gate

time: 68.7 us -> 104 us (1.51)
  Pallas kernels: 0 us -> 30.6 us
  waiting for transfers between devices: 19.7 us -> 25 us
  starting transfers between devices: 34.9 us -> 30.4 us
  matrix products: 4.17 us -> 7.14 us
    pallas_call x0 -> x1, Pallas kernels: none -> 30.6 us  [neighbours_parts(): pl.pallas_call(copy_parts, out_shape=[jax.ShapeDtypeStruct((depth + rows,...]
    ppermute x29 -> x27, waiting for transfers between devices: 19.7 us -> 25 us  [crossed(): lax.ppermute(block, axis, [(i, i ^ mask) for i in range(lax.axis_size(axi...]
    ppermute x29 -> x27, starting transfers between devices: 34.9 us -> 30.4 us  [crossed(): lax.ppermute(block, axis, [(i, i ^ mask) for i in range(lax.axis_size(axi...]
    unnamed x36 -> x22, local copies, waits for them, and re-layouts: 0.24 us -> 2.49 us
    dot_general x4, matrix products: 1.2 us -> 2.99 us  [times_transposed(): lax.dot_general(left, right, (((1,), (1,)), ((), ())), preferred_element_...]
    squeeze x1, local copies, waits for them, and re-layouts: 2.01 us -> 0.8 us  [two_layers(): lax.dynamic_slice(early, (1, 0, start + layer * part), (1, rows, part))[0]]
    dot_general x7, matrix products: 1.61 us -> 2.77 us  [times(): return jnp.dot(left, right, preferred_element_type=F32)]
  transfers between devices with their start and end apart: 29 -> 27, of which waited for: 12 -> 17; matrix products, arithmetic and copies ran while one was open for 11% -> 10% of each run, Pallas kernels for 0% -> 29%
where the time goes in v9:
time: 104 us
  Pallas kernels  30.6 us (29%)
  starting transfers between devices  30.4 us (29%)
  waiting for transfers between devices  25 us (24%)
  matrix products  7.14 us (7%)
  local copies, waits for them, and re-layouts  4.23 us (4%)
  other arithmetic  4.05 us (4%)
  between operations  2.29 us (2%)
    pallas_call x1, Pallas kernels, neighbours_parts(): pl.pallas_call(copy_parts, out_shape=[jax.ShapeDtypeStruct((depth + rows,...  30.6 us
    ppermute x27, starting transfers between devices, crossed(): lax.ppermute(block, axis, [(i, i ^ mask) for i in range(lax.axis_size(axi...  30.4 us
    ppermute x27, waiting for transfers between devices, crossed(): lax.ppermute(block, axis, [(i, i ^ mask) for i in range(lax.axis_size(axi...  25 us
    dot_general x4, matrix products, times_transposed(): lax.dot_general(left, right, (((1,), (1,)), ((), ())), preferred_element_...  2.99 us
    dot_general x7, matrix products, times(): return jnp.dot(left, right, preferred_element_type=F32)  2.77 us
    unnamed x22, local copies, waits for them, and re-layouts  2.49 us
  transfers between devices with their start and end apart: 27, of which 17 were waited for; matrix products, arithmetic and copies ran while one was open for 10% of the time, Pallas kernels for 29%

profile of v9, /device:TPU:0, one launch (start us, length us, event | category | flops | bytes accessed | tf_op | source)
XLA Modules:
  0.0 103.7 jit_solution(11480579466483823212)
XLA Ops:
  0.6 0.5 collective-permute-start.3
  1.2 0.8 dynamic-slice_bitcast_fusion.1
  2.0 2.6 %collective-permute-start.2 = (bf16[16,1792]{1,0:T(8,128)(2,1)S(1)}, bf16[16,1792]{1,0:T(8,128)(2,1)S(1)}, u32[]{:S(2)}, u32[]{:S(2)}) collective-permute-start(bf16[16,1792]{1,0:T(8,128)(2,1)S(1)} %get-tuple-element.74), channel_id=1, source_target_pairs={{0,1},{1,0},{2,3},{3,2},{4,5},{5,4},{6,7},{7,6},{8,9},{9,8},{10,11... | collective-permute-start | bytes 172040 | tf_op jit(solution)/shard_map/ppermute | solution.py:13
  4.6 0.6 pad_add_fusion.place_ref
  5.2 30.6 %neighbours_parts.1 = (bf16[272,896]{1,0:T(8,128)(2,1)}, bf16[256,896]{1,0:T(8,128)(2,1)}) custom-call(s32[3]{0:T(128)} %pad_add_fusion.place_ref, bf16[2,256,1792]{2,1,0:T(8,128)(2,1)} %bitcast.85, bf16[3,16,3584]{2,1,0:T(8,128)(2,1)} %target_ref.1), custom_call_target="tpu_custom_call" | custom-call | bytes 1835008 | tf_op jit(solution)/shard_map/neighbours_parts/pallas_call | solution.py:80
  35.8 1.6 %collective-permute-start.1 = (bf16[256,896]{1,0:T(8,128)(2,1)}, bf16[256,896]{1,0:T(8,128)(2,1)S(1)}, u32[]{:S(2)}, u32[]{:S(2)}) collective-permute-start(bf16[256,896]{1,0:T(8,128)(2,1)} %get-tuple-element.32), channel_id=1, source_target_pairs={{0,16},{8,24},{16,0},{24,8},{1,17},{9,25},{17,1},{25,9},{2,18},{10... | collective-permute-start | bytes 1376264 | tf_op jit(solution)/shard_map/ppermute | solution.py:13
  37.4 0.5 collective-permute-start
  38.0 3.7 %collective-permute-start.6 = (bf16[32,1792]{1,0:T(8,128)(2,1)S(1)}, bf16[32,1792]{1,0:T(8,128)(2,1)S(1)}, u32[]{:S(2)}, u32[]{:S(2)}) collective-permute-start(bf16[32,1792]{1,0:T(8,128)(2,1)S(1)} %bitcast.99), channel_id=1, source_target_pairs={{0,6},{1,7},{2,4},{3,5},{4,2},{5,3},{6,0},{7,1},{8,14},{9,15},{10,... | collective-permute-start | bytes 344072 | tf_op jit(solution)/shard_map/ppermute | solution.py:13
  41.6 0.8 collective-permute-start.4
  42.4 1.2 %bitcast_select_fusion.1 = (bf16[1792,128]{1,0:T(8,128)(2,1)}, bf16[1792,128]{1,0:T(8,128)(2,1)}) fusion(pred[]{:T(512)S(6)} %eq.57, bf16[3584,128]{1,0:T(8,128)(2,1)S(1)} %collective-permute-done.3, s32[]{:T(128)S(6)} %select_n.134, bf16[1,3584,128]{2,1,0:T(8,128)(2,1)S(1)} %copy-done.1), kind=kLoop, calls=%fused_computation.23 | loop fusion | flops 458752 | bytes 1835013 | tf_op jit(solution)/shard_map/jit(_where)/select_n | solution.py:25
  43.6 0.7 compare_reduce_fusion
  45.6 0.8 dynamic-slice_bitcast_fusion.2
  46.4 2.2 %collective-permute-done.1 = bf16[256,896]{1,0:T(8,128)(2,1)S(1)} collective-permute-done((bf16[256,896]{1,0:T(8,128)(2,1)}, bf16[256,896]{1,0:T(8,128)(2,1)S(1)}, u32[]{:S(2)}, u32[]{:S(2)}) %collective-permute-start.1) | collective-permute-done | bytes 458784 | tf_op jit(solution)/shard_map/ppermute | solution.py:13
  48.6 1.9 %collective-permute-done = bf16[272,896]{1,0:T(8,128)(2,1)S(1)} collective-permute-done((bf16[272,896]{1,0:T(8,128)(2,1)}, bf16[272,896]{1,0:T(8,128)(2,1)S(1)}, u32[]{:S(2)}, u32[]{:S(2)}) %collective-permute-start) | collective-permute-done | bytes 487456 | tf_op jit(solution)/shard_map/ppermute | solution.py:13
  50.5 0.6 collective-permute-done.5
  51.1 0.9 constant_dynamic-update-slice_fusion.2
  52.0 0.9 constant_dynamic-update-slice_fusion.1
  53.0 1.5 %convolution_add_fusion.4 = f32[128,256]{1,0:T(8,128)S(1)} fusion(bf16[128,1792]{1,0:T(8,128)(2,1)S(1)} %constant_dynamic-update-slice_fusion, bf16[1792,128]{1,0:T(8,128)(2,1)} %get-tuple-element.68, bf16[1792,128]{1,0:T(8,128)(2,1)} %get-tuple-element.67, f32[256]{0:T(256)S(1)} %pad_maximum_fusion.10), kind=kOutput, calls=%fused_computation.7 | convolution fusion | flops 119308288 | bytes 1508352 | tf_op jit(solution)/shard_map/dot_general | solution.py:17
  54.4 0.1 collective-permute-start.7
  54.5 1.3 %collective-permute-done.7 = f32[128,256]{1,0:T(8,128)S(1)} collective-permute-done((f32[128,256]{1,0:T(8,128)S(1)}, f32[128,256]{1,0:T(8,128)S(1)}, u32[]{:S(2)}, u32[]{:S(2)}) %collective-permute-start.7) | collective-permute-done | bytes 131104 | tf_op jit(solution)/shard_map/ppermute | solution.py:13
  55.9 0.6 collective-permute-start.11
  56.4 1.6 %collective-permute-start.8 = (bf16[128,256]{1,0:T(8,128)(2,1)S(1)}, bf16[128,256]{1,0:T(8,128)(2,1)S(1)}, u32[]{:S(2)}, u32[]{:S(2)}) collective-permute-start(bf16[128,256]{1,0:T(8,128)(2,1)S(1)} %bitcast.111), channel_id=1, source_target_pairs={{0,1},{1,0},{2,3},{3,2},{4,5},{5,4},{6,7},{7,6},{8,9},{9,8},{10,11... | collective-permute-start | bytes 196616 | tf_op jit(solution)/shard_map/ppermute | solution.py:13
  58.0 0.2 fusion.10
  58.2 0.2 fusion.12
  58.4 1.8 %collective-permute-done.11 = bf16[128,256]{1,0:T(8,128)(2,1)S(1)} collective-permute-done((bf16[128,256]{1,0:T(8,128)(2,1)S(1)}, bf16[128,256]{1,0:T(8,128)(2,1)S(1)}, u32[]{:S(2)}, u32[]{:S(2)}) %collective-permute-start.11) | collective-permute-done | bytes 65568 | tf_op jit(solution)/shard_map/ppermute | solution.py:13
  60.2 0.2 fusion.1
  60.4 1.6 %collective-permute-start.12 = (bf16[64,896]{1,0:T(8,128)(2,1)S(1)}, bf16[64,896]{1,0:T(8,128)(2,1)S(1)}, u32[]{:S(2)}, u32[]{:S(2)}) collective-permute-start(bf16[64,896]{1,0:T(8,128)(2,1)S(1)} %fusion.1), channel_id=1, source_target_pairs={{0,1},{1,0},{2,3},{3,2},{4,5},{5,4},{6,7},{7,6},{8,9},{9,8},{10,11... | collective-permute-start | bytes 344072 | tf_op jit(solution)/shard_map/ppermute | solution.py:13
  62.0 0.2 fusion.18
  62.2 0.2 convolution_add_fusion
  62.5 1.1 %collective-permute-start.9 = (bf16[64,896]{1,0:T(8,128)(2,1)S(1)}, bf16[64,896]{1,0:T(8,128)(2,1)S(1)}, u32[]{:S(2)}, u32[]{:S(2)}) collective-permute-start(bf16[64,896]{1,0:T(8,128)(2,1)S(1)} %slice.173), channel_id=1, source_target_pairs={{0,4},{1,5},{2,6},{3,7},{4,0},{5,1},{6,2},{7,3},{8,12},{9,13},{10,... | collective-permute-start | bytes 344072 | tf_op jit(solution)/shard_map/ppermute | solution.py:13
  63.5 0.2 convolution_add_fusion.1
  63.8 1.5 %collective-permute-done.12 = bf16[64,896]{1,0:T(8,128)(2,1)S(1)} collective-permute-done((bf16[64,896]{1,0:T(8,128)(2,1)S(1)}, bf16[64,896]{1,0:T(8,128)(2,1)S(1)}, u32[]{:S(2)}, u32[]{:S(2)}) %collective-permute-start.12) | collective-permute-done | bytes 114720 | tf_op jit(solution)/shard_map/ppermute | solution.py:13
  65.3 3.0 %collective-permute-start.15 = (bf16[16,896]{1,0:T(8,128)(2,1)S(1)}, bf16[16,896]{1,0:T(8,128)(2,1)S(1)}, u32[]{:S(2)}, u32[]{:S(2)}) collective-permute-start(bf16[16,896]{1,0:T(8,128)(2,1)S(1)} %get-tuple-element.79), channel_id=1, source_target_pairs={{0,6},{1,7},{2,4},{3,5},{4,2},{5,3},{6,0},{7,1},{8,14},{9,15},{10,... | collective-permute-start | bytes 86024 | tf_op jit(solution)/shard_map/ppermute | solution.py:13
  68.4 1.4 %collective-permute-start.13 = (bf16[16,896]{1,0:T(8,128)(2,1)S(1)}, bf16[16,896]{1,0:T(8,128)(2,1)S(1)}, u32[]{:S(2)}, u32[]{:S(2)}) collective-permute-start(bf16[16,896]{1,0:T(8,128)(2,1)S(1)} %get-tuple-element.81), channel_id=1, source_target_pairs={{0,2},{1,3},{2,0},{3,1},{4,6},{5,7},{6,4},{7,5},{8,10},{9,11},{10,... | collective-permute-start | bytes 86024 | tf_op jit(solution)/shard_map/ppermute | solution.py:13
  69.8 1.0 collective-permute-done.9
  70.8 0.1 collective-permute-start.10
  70.9 0.4 collective-permute-done.15
  71.3 1.8 %collective-permute-done.14 = bf16[16,896]{1,0:T(8,128)(2,1)S(1)} collective-permute-done((bf16[16,896]{1,0:T(8,128)(2,1)S(1)}, bf16[16,896]{1,0:T(8,128)(2,1)S(1)}, u32[]{:S(2)}, u32[]{:S(2)}) %collective-permute-start.14) | collective-permute-done | bytes 28704 | tf_op jit(solution)/shard_map/ppermute | solution.py:13
  73.2 1.9 %collective-permute-done.10 = bf16[32,896]{1,0:T(8,128)(2,1)S(1)} collective-permute-done((bf16[32,896]{1,0:T(8,128)(2,1)S(1)}, bf16[32,896]{1,0:T(8,128)(2,1)S(1)}, u32[]{:S(2)}, u32[]{:S(2)}) %collective-permute-start.10) | collective-permute-done | bytes 57376 | tf_op jit(solution)/shard_map/ppermute | solution.py:13
  75.1 0.0 copy-start.2
  75.1 2.2 %collective-permute-start.18 = (bf16[16,896]{1,0:T(8,128)(2,1)S(1)}, bf16[16,896]{1,0:T(8,128)(2,1)S(1)}, u32[]{:S(2)}, u32[]{:S(2)}) collective-permute-start(bf16[16,896]{1,0:T(8,128)(2,1)S(1)} %get-tuple-element.56), channel_id=1, source_target_pairs={{0,6},{1,7},{2,4},{3,5},{4,2},{5,3},{6,0},{7,1},{8,14},{9,15},{10,... | collective-permute-start | bytes 86024 | tf_op jit(solution)/shard_map/ppermute | solution.py:13
  77.3 2.3 %collective-permute-start.16 = (bf16[16,896]{1,0:T(8,128)(2,1)S(1)}, bf16[16,896]{1,0:T(8,128)(2,1)S(1)}, u32[]{:S(2)}, u32[]{:S(2)}) collective-permute-start(bf16[16,896]{1,0:T(8,128)(2,1)S(1)} %get-tuple-element.56), channel_id=1, source_target_pairs={{0,2},{1,3},{2,0},{3,1},{4,6},{5,7},{6,4},{7,5},{8,10},{9,11},{10,... | collective-permute-start | bytes 86024 | tf_op jit(solution)/shard_map/ppermute | solution.py:13
  79.5 0.1 collective-permute-start.19
  79.6 1.7 %collective-permute-done.16 = bf16[16,896]{1,0:T(8,128)(2,1)S(1)} collective-permute-done((bf16[16,896]{1,0:T(8,128)(2,1)S(1)}, bf16[16,896]{1,0:T(8,128)(2,1)S(1)}, u32[]{:S(2)}, u32[]{:S(2)}) %collective-permute-start.16) | collective-permute-done | bytes 28704 | tf_op jit(solution)/shard_map/ppermute | solution.py:13
  81.4 0.6 collective-permute-done.17
  82.1 1.7 %collective-permute-done.19 = bf16[32,896]{1,0:T(8,128)(2,1)S(1)} collective-permute-done((bf16[32,896]{1,0:T(8,128)(2,1)S(1)}, bf16[32,896]{1,0:T(8,128)(2,1)S(1)}, u32[]{:S(2)}, u32[]{:S(2)}) %collective-permute-start.19) | collective-permute-done | bytes 57376 | tf_op jit(solution)/shard_map/ppermute | solution.py:13
  83.8 0.6 copy-done.4
  84.4 1.2 %collective-permute-start.21 = (bf16[64,896]{1,0:T(8,128)(2,1)S(1)}, bf16[64,896]{1,0:T(8,128)(2,1)}, u32[]{:S(2)}, u32[]{:S(2)}) collective-permute-start(bf16[64,896]{1,0:T(8,128)(2,1)S(1)} %pad_maximum_fusion.5), channel_id=1, source_target_pairs={{0,4},{1,5},{2,6},{3,7},{4,0},{5,1},{6,2},{7,3},{8,12},{9,13},{10,... | collective-permute-start | bytes 344072 | tf_op jit(solution)/shard_map/ppermute | solution.py:13
  85.7 2.1 %collective-permute-start.20 = (bf16[80,896]{1,0:T(8,128)(2,1)S(1)}, bf16[80,896]{1,0:T(8,128)(2,1)S(1)}, u32[]{:S(2)}, u32[]{:S(2)}) collective-permute-start(bf16[80,896]{1,0:T(8,128)(2,1)S(1)} %fusion.30), channel_id=1, source_target_pairs={{0,1},{1,0},{2,3},{3,2},{4,5},{5,4},{6,7},{7,6},{8,9},{9,8},{10,11... | collective-permute-start | bytes 430088 | tf_op jit(solution)/shard_map/ppermute | solution.py:13
  87.7 3.5 %collective-permute-done.21 = bf16[64,896]{1,0:T(8,128)(2,1)} collective-permute-done((bf16[64,896]{1,0:T(8,128)(2,1)S(1)}, bf16[64,896]{1,0:T(8,128)(2,1)}, u32[]{:S(2)}, u32[]{:S(2)}) %collective-permute-start.21) | collective-permute-done | bytes 114720 | tf_op jit(solution)/shard_map/ppermute | solution.py:13
  91.3 1.2 %fusion.16 = f32[128,256]{1,0:T(8,128)S(1)} fusion(bf16[272,896]{1,0:T(8,128)(2,1)S(1)} %collective-permute-done, bf16[64,896]{1,0:T(8,128)(2,1)} %collective-permute-done.21, bf16[32,896]{1,0:T(8,128)(2,1)} %copy-done.4, bf16[32,896]{1,0:T(8,128)(2,1)S(1)} %fusion.26), kind=kOutput, calls=%fused_computation.26 | convolution fusion | flops 59408384 | bytes 819200 | tf_op jit(solution)/shard_map/dot_general | solution.py:21
  92.6 0.3 fusion.49
  92.9 0.3 fusion.8
  93.2 1.2 %convolution_add_fusion.3 = f32[128,256]{1,0:T(8,128)S(1)} fusion(f32[128,256]{1,0:T(8,128)S(1)} %fusion.8, bf16[2,256,1792]{2,1,0:T(8,128)(2,1)S(1)} %bitcast.90, s32[]{:T(128)S(6)} %select_n.133, s32[]{:T(128)S(6)} %select_n.144, bf16[64,896]{1,0:T(8,128)(2,1)} %collective-permute-done.21, bf16[32,896]{1,0:T(8,128)(2,1)S(1)} %copy-done.5, ...), kind=kOutput, calls=%fused_computation.6 | convolution fusion | flops 59441152 | bytes 950280 | tf_op jit(solution)/shard_map/dot_general | solution.py:21
  94.5 0.7 collective-permute-start.22
  95.2 1.4 %collective-permute-done.24 = f32[384,128]{1,0:T(8,128)S(1)} collective-permute-done((f32[384,128]{1,0:T(8,128)S(1)}, f32[384,128]{1,0:T(8,128)S(1)}, u32[]{:S(2)}, u32[]{:S(2)}) %collective-permute-start.24) | collective-permute-done | bytes 196640 | tf_op jit(solution)/shard_map/ppermute | solution.py:13
  96.7 1.1 %collective-permute-start.25 = (bf16[128,128]{1,0:T(8,128)(2,1)S(1)}, bf16[128,128]{1,0:T(8,128)(2,1)S(1)}, u32[]{:S(2)}, u32[]{:S(2)}) collective-permute-start(bf16[128,128]{1,0:T(8,128)(2,1)S(1)} %get-tuple-element.82), channel_id=1, source_target_pairs={{0,1},{1,0},{2,3},{3,2},{4,5},{5,4},{6,7},{7,6},{8,9},{9,8},{10,11... | collective-permute-start | bytes 98312 | tf_op jit(solution)/shard_map/ppermute | solution.py:13
  97.8 1.7 %collective-permute-start.26 = (bf16[128,128]{1,0:T(8,128)(2,1)S(1)}, bf16[128,128]{1,0:T(8,128)(2,1)S(1)}, u32[]{:S(2)}, u32[]{:S(2)}) collective-permute-start(bf16[128,128]{1,0:T(8,128)(2,1)S(1)} %get-tuple-element.83), channel_id=1, source_target_pairs={{0,16},{8,24},{16,0},{24,8},{1,17},{9,25},{17,1},{25,9},{2,18},{10... | collective-permute-start | bytes 98312 | tf_op jit(solution)/shard_map/ppermute | solution.py:13
  99.5 0.6 maximum_select_fusion
  100.1 0.5 collective-permute-done.25
  100.7 1.0 collective-permute-done.26
  101.7 0.5 fusion.31
  102.2 0.1 broadcast_select_fusion.1
  102.3 1.4 %fusion = bf16[1,3584,128]{2,1,0:T(8,128)(2,1)} fusion(bf16[128,1792]{1,0:T(8,128)(2,1)S(1)} %get-tuple-element.70, bf16[128,1792]{1,0:T(8,128)(2,1)S(1)} %get-tuple-element.69, f32[384,128]{1,0:T(8,128)S(1)} %get-tuple-element.62, bf16[128,128]{1,0:T(8,128)(2,1)S(1)} %collective-permute-done.26, bf16[128,128]{1,0:T(8,128)(2,1)S(1)} %collective-permute-done.25, ...), kind=kOutput, calls=%fused_computation.1 | convolution fusion | flops 119832576 | bytes 1966084 | tf_op jit(solution)/shard_map/dot_general | solution.py:50
  (65 shorter events, 0.6 us)
Async XLA Ops:
  0.6 41.8 %copy-start.1 = (bf16[1,3584,128]{2,1,0:T(8,128)(2,1)S(1)}, bf16[1,3584,128]{2,1,0:T(8,128)(2,1)}, u32[]{:S(2)}) copy-start(bf16[1,3584,128]{2,1,0:T(8,128)(2,1)} %param.8) | copy-start | bytes 2752516
  0.6 37.3 %collective-permute-start.3 = (bf16[3584,128]{1,0:T(8,128)(2,1)}, bf16[3584,128]{1,0:T(8,128)(2,1)S(1)}, u32[]{:S(2)}, u32[]{:S(2)}) collective-permute-start(bf16[3584,128]{1,0:T(8,128)(2,1)} %bitcast.105), channel_id=1, source_target_pairs={{0,8},{8,0},{16,24},{24,16},{1,9},{9,1},{17,25},{25,17},{2,10},{10... | collective-permute-start | bytes 2752520 | tf_op jit(solution)/shard_map/ppermute | solution.py:13
  2.0 36.0 %collective-permute-start.2 = (bf16[16,1792]{1,0:T(8,128)(2,1)S(1)}, bf16[16,1792]{1,0:T(8,128)(2,1)S(1)}, u32[]{:S(2)}, u32[]{:S(2)}) collective-permute-start(bf16[16,1792]{1,0:T(8,128)(2,1)S(1)} %get-tuple-element.74), channel_id=1, source_target_pairs={{0,1},{1,0},{2,3},{3,2},{4,5},{5,4},{6,7},{7,6},{8,9},{9,8},{10,11... | collective-permute-start | bytes 172040 | tf_op jit(solution)/shard_map/ppermute | solution.py:13
  5.2 38.4 %copy-start.6 = (f32[1,128]{1,0:T(1,128)S(1)}, f32[1,128]{1,0:T(1,128)}, u32[]{:S(2)}) copy-start(f32[1,128]{1,0:T(1,128)} %param.9) | copy-start | bytes 1540
  5.2 38.4 %copy-start.7 = (s32[2,1,12]{2,1,0:T(1,128)S(1)}, s32[2,1,12]{2,1,0:T(1,128)}, u32[]{:S(2)}) copy-start(s32[2,1,12]{2,1,0:T(1,128)} %param.11) | copy-start | bytes 292
  35.8 12.8 %collective-permute-start.1 = (bf16[256,896]{1,0:T(8,128)(2,1)}, bf16[256,896]{1,0:T(8,128)(2,1)S(1)}, u32[]{:S(2)}, u32[]{:S(2)}) collective-permute-start(bf16[256,896]{1,0:T(8,128)(2,1)} %get-tuple-element.32), channel_id=1, source_target_pairs={{0,16},{8,24},{16,0},{24,8},{1,17},{9,25},{17,1},{25,9},{2,18},{10... | collective-permute-start | bytes 1376264 | tf_op jit(solution)/shard_map/ppermute | solution.py:13
  37.4 13.1 %collective-permute-start = (bf16[272,896]{1,0:T(8,128)(2,1)}, bf16[272,896]{1,0:T(8,128)(2,1)S(1)}, u32[]{:S(2)}, u32[]{:S(2)}) collective-permute-start(bf16[272,896]{1,0:T(8,128)(2,1)} %get-tuple-element.31), channel_id=1, source_target_pairs={{0,1},{1,0},{2,3},{3,2},{4,5},{5,4},{6,7},{7,6},{8,9},{9,8},{10,11... | collective-permute-start | bytes 1462280 | tf_op jit(solution)/shard_map/ppermute | solution.py:13
  38.0 12.5 %collective-permute-start.6 = (bf16[32,1792]{1,0:T(8,128)(2,1)S(1)}, bf16[32,1792]{1,0:T(8,128)(2,1)S(1)}, u32[]{:S(2)}, u32[]{:S(2)}) collective-permute-start(bf16[32,1792]{1,0:T(8,128)(2,1)S(1)} %bitcast.99), channel_id=1, source_target_pairs={{0,6},{1,7},{2,4},{3,5},{4,2},{5,3},{6,0},{7,1},{8,14},{9,15},{10,... | collective-permute-start | bytes 344072 | tf_op jit(solution)/shard_map/ppermute | solution.py:13
  41.6 9.5 %collective-permute-start.5 = (bf16[32,1792]{1,0:T(8,128)(2,1)S(1)}, bf16[32,1792]{1,0:T(8,128)(2,1)}, u32[]{:S(2)}, u32[]{:S(2)}) collective-permute-start(bf16[32,1792]{1,0:T(8,128)(2,1)S(1)} %bitcast.100), channel_id=1, source_target_pairs={{0,4},{1,5},{2,6},{3,7},{4,0},{5,1},{6,2},{7,3},{8,12},{9,13},{10,... | collective-permute-start | bytes 344072 | tf_op jit(solution)/shard_map/ppermute | solution.py:13
  41.6 9.5 %collective-permute-start.4 = (bf16[32,1792]{1,0:T(8,128)(2,1)S(1)}, bf16[32,1792]{1,0:T(8,128)(2,1)}, u32[]{:S(2)}, u32[]{:S(2)}) collective-permute-start(bf16[32,1792]{1,0:T(8,128)(2,1)S(1)} %bitcast.101), channel_id=1, source_target_pairs={{0,2},{1,3},{2,0},{3,1},{4,6},{5,7},{6,4},{7,5},{8,10},{9,11},{10,... | collective-permute-start | bytes 344072 | tf_op jit(solution)/shard_map/ppermute | solution.py:13
  46.4 11.6 %copy-start = (bf16[1,2,2,128,1792]{4,3,2,1,0:T(8,128)(2,1)S(1)}, bf16[1,2,2,128,1792]{4,3,2,1,0:T(8,128)(2,1)}, u32[]{:S(2)}) copy-start(bf16[1,2,2,128,1792]{4,3,2,1,0:T(8,128)(2,1)} %param.10) | copy-start | bytes 5505028
  54.4 1.4 %collective-permute-start.7 = (f32[128,256]{1,0:T(8,128)S(1)}, f32[128,256]{1,0:T(8,128)S(1)}, u32[]{:S(2)}, u32[]{:S(2)}) collective-permute-start(f32[128,256]{1,0:T(8,128)S(1)} %convolution_add_fusion.4), channel_id=1, source_target_pairs={{0,8},{8,0},{16,24},{24,16},{1,9},{9,1},{17,25},{25,17},{2,10},{10... | collective-permute-start | bytes 393224 | tf_op jit(solution)/shard_map/ppermute | solution.py:13
  55.9 4.3 %collective-permute-start.11 = (bf16[128,256]{1,0:T(8,128)(2,1)S(1)}, bf16[128,256]{1,0:T(8,128)(2,1)S(1)}, u32[]{:S(2)}, u32[]{:S(2)}) collective-permute-start(bf16[128,256]{1,0:T(8,128)(2,1)S(1)} %multiply_convert_fusion), channel_id=1, source_target_pairs={{0,16},{8,24},{16,0},{24,8},{1,17},{9,25},{17,1},{25,9},{2,18},{10... | collective-permute-start | bytes 196616 | tf_op jit(solution)/shard_map/ppermute | solution.py:13
  56.4 5.5 %collective-permute-start.8 = (bf16[128,256]{1,0:T(8,128)(2,1)S(1)}, bf16[128,256]{1,0:T(8,128)(2,1)S(1)}, u32[]{:S(2)}, u32[]{:S(2)}) collective-permute-start(bf16[128,256]{1,0:T(8,128)(2,1)S(1)} %bitcast.111), channel_id=1, source_target_pairs={{0,1},{1,0},{2,3},{3,2},{4,5},{5,4},{6,7},{7,6},{8,9},{9,8},{10,11... | collective-permute-start | bytes 196616 | tf_op jit(solution)/shard_map/ppermute | solution.py:13
  60.4 4.9 %collective-permute-start.12 = (bf16[64,896]{1,0:T(8,128)(2,1)S(1)}, bf16[64,896]{1,0:T(8,128)(2,1)S(1)}, u32[]{:S(2)}, u32[]{:S(2)}) collective-permute-start(bf16[64,896]{1,0:T(8,128)(2,1)S(1)} %fusion.1), channel_id=1, source_target_pairs={{0,1},{1,0},{2,3},{3,2},{4,5},{5,4},{6,7},{7,6},{8,9},{9,8},{10,11... | collective-permute-start | bytes 344072 | tf_op jit(solution)/shard_map/ppermute | solution.py:13
  62.5 8.3 %collective-permute-start.9 = (bf16[64,896]{1,0:T(8,128)(2,1)S(1)}, bf16[64,896]{1,0:T(8,128)(2,1)S(1)}, u32[]{:S(2)}, u32[]{:S(2)}) collective-permute-start(bf16[64,896]{1,0:T(8,128)(2,1)S(1)} %slice.173), channel_id=1, source_target_pairs={{0,4},{1,5},{2,6},{3,7},{4,0},{5,1},{6,2},{7,3},{8,12},{9,13},{10,... | collective-permute-start | bytes 344072 | tf_op jit(solution)/shard_map/ppermute | solution.py:13
  65.3 6.0 %collective-permute-start.15 = (bf16[16,896]{1,0:T(8,128)(2,1)S(1)}, bf16[16,896]{1,0:T(8,128)(2,1)S(1)}, u32[]{:S(2)}, u32[]{:S(2)}) collective-permute-start(bf16[16,896]{1,0:T(8,128)(2,1)S(1)} %get-tuple-element.79), channel_id=1, source_target_pairs={{0,6},{1,7},{2,4},{3,5},{4,2},{5,3},{6,0},{7,1},{8,14},{9,15},{10,... | collective-permute-start | bytes 86024 | tf_op jit(solution)/shard_map/ppermute | solution.py:13
  68.4 4.8 %collective-permute-start.14 = (bf16[16,896]{1,0:T(8,128)(2,1)S(1)}, bf16[16,896]{1,0:T(8,128)(2,1)S(1)}, u32[]{:S(2)}, u32[]{:S(2)}) collective-permute-start(bf16[16,896]{1,0:T(8,128)(2,1)S(1)} %get-tuple-element.80), channel_id=1, source_target_pairs={{0,4},{1,5},{2,6},{3,7},{4,0},{5,1},{6,2},{7,3},{8,12},{9,13},{10,... | collective-permute-start | bytes 86024 | tf_op jit(solution)/shard_map/ppermute | solution.py:13
  68.4 4.8 %collective-permute-start.13 = (bf16[16,896]{1,0:T(8,128)(2,1)S(1)}, bf16[16,896]{1,0:T(8,128)(2,1)S(1)}, u32[]{:S(2)}, u32[]{:S(2)}) collective-permute-start(bf16[16,896]{1,0:T(8,128)(2,1)S(1)} %get-tuple-element.81), channel_id=1, source_target_pairs={{0,2},{1,3},{2,0},{3,1},{4,6},{5,7},{6,4},{7,5},{8,10},{9,11},{10,... | collective-permute-start | bytes 86024 | tf_op jit(solution)/shard_map/ppermute | solution.py:13
  70.8 4.2 %collective-permute-start.10 = (bf16[32,896]{1,0:T(8,128)(2,1)S(1)}, bf16[32,896]{1,0:T(8,128)(2,1)S(1)}, u32[]{:S(2)}, u32[]{:S(2)}) collective-permute-start(bf16[32,896]{1,0:T(8,128)(2,1)S(1)} %slice.174), channel_id=1, source_target_pairs={{0,2},{1,3},{2,0},{3,1},{4,6},{5,7},{6,4},{7,5},{8,10},{9,11},{10,... | collective-permute-start | bytes 172040 | tf_op jit(solution)/shard_map/ppermute | solution.py:13
  75.1 8.7 %copy-start.2 = (bf16[16,896]{1,0:T(8,128)(2,1)}, bf16[16,896]{1,0:T(8,128)(2,1)S(1)}, u32[]{:S(2)}) copy-start(bf16[16,896]{1,0:T(8,128)(2,1)S(1)} %get-tuple-element.56) | copy-start | bytes 86020
  75.1 7.0 %collective-permute-start.18 = (bf16[16,896]{1,0:T(8,128)(2,1)S(1)}, bf16[16,896]{1,0:T(8,128)(2,1)S(1)}, u32[]{:S(2)}, u32[]{:S(2)}) collective-permute-start(bf16[16,896]{1,0:T(8,128)(2,1)S(1)} %get-tuple-element.56), channel_id=1, source_target_pairs={{0,6},{1,7},{2,4},{3,5},{4,2},{5,3},{6,0},{7,1},{8,14},{9,15},{10,... | collective-permute-start | bytes 86024 | tf_op jit(solution)/shard_map/ppermute | solution.py:13
  77.3 4.8 %collective-permute-start.17 = (bf16[16,896]{1,0:T(8,128)(2,1)S(1)}, bf16[16,896]{1,0:T(8,128)(2,1)S(1)}, u32[]{:S(2)}, u32[]{:S(2)}) collective-permute-start(bf16[16,896]{1,0:T(8,128)(2,1)S(1)} %get-tuple-element.56), channel_id=1, source_target_pairs={{0,4},{1,5},{2,6},{3,7},{4,0},{5,1},{6,2},{7,3},{8,12},{9,13},{10,... | collective-permute-start | bytes 86024 | tf_op jit(solution)/shard_map/ppermute | solution.py:13
  77.3 4.1 %collective-permute-start.16 = (bf16[16,896]{1,0:T(8,128)(2,1)S(1)}, bf16[16,896]{1,0:T(8,128)(2,1)S(1)}, u32[]{:S(2)}, u32[]{:S(2)}) collective-permute-start(bf16[16,896]{1,0:T(8,128)(2,1)S(1)} %get-tuple-element.56), channel_id=1, source_target_pairs={{0,2},{1,3},{2,0},{3,1},{4,6},{5,7},{6,4},{7,5},{8,10},{9,11},{10,... | collective-permute-start | bytes 86024 | tf_op jit(solution)/shard_map/ppermute | solution.py:13
  79.5 4.2 %collective-permute-start.19 = (bf16[32,896]{1,0:T(8,128)(2,1)S(1)}, bf16[32,896]{1,0:T(8,128)(2,1)S(1)}, u32[]{:S(2)}, u32[]{:S(2)}) collective-permute-start(bf16[32,896]{1,0:T(8,128)(2,1)S(1)} %fusion.26), channel_id=1, source_target_pairs={{0,2},{1,3},{2,0},{3,1},{4,6},{5,7},{6,4},{7,5},{8,10},{9,11},{10,... | collective-permute-start | bytes 172040 | tf_op jit(solution)/shard_map/ppermute | solution.py:13
  83.8 0.6 copy-start.4
  84.4 6.9 %collective-permute-start.21 = (bf16[64,896]{1,0:T(8,128)(2,1)S(1)}, bf16[64,896]{1,0:T(8,128)(2,1)}, u32[]{:S(2)}, u32[]{:S(2)}) collective-permute-start(bf16[64,896]{1,0:T(8,128)(2,1)S(1)} %pad_maximum_fusion.5), channel_id=1, source_target_pairs={{0,4},{1,5},{2,6},{3,7},{4,0},{5,1},{6,2},{7,3},{8,12},{9,13},{10,... | collective-permute-start | bytes 344072 | tf_op jit(solution)/shard_map/ppermute | solution.py:13
  85.7 7.6 %copy-start.5 = (bf16[32,896]{1,0:T(8,128)(2,1)S(1)}, bf16[32,896]{1,0:T(8,128)(2,1)}, u32[]{:S(2)}) copy-start(bf16[32,896]{1,0:T(8,128)(2,1)} %copy-done.4) | copy-start | bytes 172036
  85.7 6.9 %collective-permute-start.20 = (bf16[80,896]{1,0:T(8,128)(2,1)S(1)}, bf16[80,896]{1,0:T(8,128)(2,1)S(1)}, u32[]{:S(2)}, u32[]{:S(2)}) collective-permute-start(bf16[80,896]{1,0:T(8,128)(2,1)S(1)} %fusion.30), channel_id=1, source_target_pairs={{0,1},{1,0},{2,3},{3,2},{4,5},{5,4},{6,7},{7,6},{8,9},{9,8},{10,11... | collective-permute-start | bytes 430088 | tf_op jit(solution)/shard_map/ppermute | solution.py:13
  87.7 14.5 %collective-permute-start.23 = (bf16[128,1792]{1,0:T(8,128)(2,1)S(1)}, bf16[128,1792]{1,0:T(8,128)(2,1)S(1)}, u32[]{:S(2)}, u32[]{:S(2)}) collective-permute-start(bf16[128,1792]{1,0:T(8,128)(2,1)S(1)} %constant_dynamic-update-slice_fusion), channel_id=1, source_target_pairs={{0,8},{8,0},{16,24},{24,16},{1,9},{9,1},{17,25},{25,17},{2,10},{10... | collective-permute-start | bytes 1376264 | tf_op jit(solution)/shard_map/ppermute | solution.py:13
  92.6 1.9 %copy-start.3 = (bf16[16,896]{1,0:T(8,128)(2,1)S(1)}, bf16[16,896]{1,0:T(8,128)(2,1)}, u32[]{:S(2)}) copy-start(bf16[16,896]{1,0:T(8,128)(2,1)} %copy-done.2) | copy-start | bytes 86020
  94.5 5.0 %collective-permute-start.22 = (bf16[16,896]{1,0:T(8,128)(2,1)S(1)}, bf16[16,896]{1,0:T(8,128)(2,1)S(1)}, u32[]{:S(2)}, u32[]{:S(2)}) collective-permute-start(bf16[16,896]{1,0:T(8,128)(2,1)S(1)} %copy-done.3), channel_id=1, source_target_pairs={{0,16},{8,24},{16,0},{24,8},{1,17},{9,25},{17,1},{25,9},{2,18},{10... | collective-permute-start | bytes 86024 | tf_op jit(solution)/shard_map/ppermute | solution.py:13
  95.2 1.4 %collective-permute-start.24 = (f32[384,128]{1,0:T(8,128)S(1)}, f32[384,128]{1,0:T(8,128)S(1)}, u32[]{:S(2)}, u32[]{:S(2)}) collective-permute-start(f32[384,128]{1,0:T(8,128)S(1)} %slice_select_fusion), channel_id=1, source_target_pairs={{0,8},{8,0},{16,24},{24,16},{1,9},{9,1},{17,25},{25,17},{2,10},{10... | collective-permute-start | bytes 589832 | tf_op jit(solution)/shard_map/ppermute | solution.py:13
  96.7 4.0 %collective-permute-start.25 = (bf16[128,128]{1,0:T(8,128)(2,1)S(1)}, bf16[128,128]{1,0:T(8,128)(2,1)S(1)}, u32[]{:S(2)}, u32[]{:S(2)}) collective-permute-start(bf16[128,128]{1,0:T(8,128)(2,1)S(1)} %get-tuple-element.82), channel_id=1, source_target_pairs={{0,1},{1,0},{2,3},{3,2},{4,5},{5,4},{6,7},{7,6},{8,9},{9,8},{10,11... | collective-permute-start | bytes 98312 | tf_op jit(solution)/shard_map/ppermute | solution.py:13
  97.8 3.9 %collective-permute-start.26 = (bf16[128,128]{1,0:T(8,128)(2,1)S(1)}, bf16[128,128]{1,0:T(8,128)(2,1)S(1)}, u32[]{:S(2)}, u32[]{:S(2)}) collective-permute-start(bf16[128,128]{1,0:T(8,128)(2,1)S(1)} %get-tuple-element.83), channel_id=1, source_target_pairs={{0,16},{8,24},{16,0},{24,8},{1,17},{9,25},{17,1},{25,9},{2,18},{10... | collective-permute-start | bytes 98312 | tf_op jit(solution)/shard_map/ppermute | solution.py:13

commit v10 on v8

--- a/solution.py
+++ b/solution.py
@@ -23,16 +23,15 @@
     return jnp.concatenate([jnp.where(half == 0, mine, other), jnp.where(half == 0, other, mine)], axis=axis)
 
 
-def gates(blocks, layer, slot, slots, latents, tokens):
+def firing_flags(blocks, layer, slot, slots, latents):
     listed = lax.dynamic_index_in_dim(blocks, layer, 0, keepdims=False)
-    tile = tokens // listed.shape[0]
     here = latents // BLOCK
-    out = []
-    for side in range(2):
-        names = (side * slots + slot) * here + jnp.arange(here)
-        flags = jnp.any(listed[:, :, None] == names, axis=1).astype(F32)
-        out.append(jnp.repeat(jnp.repeat(flags, tile, axis=0), BLOCK, axis=1))
-    return out
+    names = [(side * slots + slot) * here + jnp.arange(here) for side in range(2)]
+    return [jnp.any(listed[:, :, None] == these, axis=1).astype(F32) for these in names]
+
+
+def gates(flags, tokens):
+    return [jnp.repeat(jnp.repeat(each, tokens // each.shape[0], axis=0), BLOCK, axis=1) for each in flags]
 
 
 def half_preacts(resid_half, weight, weight_other, bias, half):
@@ -70,19 +69,18 @@
     def over_core(block):
         return crossed(block, "layer", 1)
 
-    def along_z(block):
-        out = [block] + [None] * (far - 1)
+    def along_z(blocks):
+        out = [blocks[0]] + [None] * (far - 1)
         for k in range(far - 1, 0, -1):
-            out[k] = crossed(block, "latent", 2 * k)
+            out[k] = crossed(blocks[k], "latent", 2 * k)
         return out
 
-    def sent_along_z(total):
+    def pieces_of(total):
         count = total.shape[0] // far
-        pieces = [total[k * count:(k + 1) * count].astype(BF16) for k in range(1, far)]
-        return [crossed(pieces[k - 1], "latent", 2 * k) for k in range(1, far)] + [total[:count]]
+        return [total[:count]] + [total[k * count:(k + 1) * count].astype(BF16) for k in range(1, far)]
 
     def added(terms):
-        return sum(term.astype(F32) for term in terms[::-1])
+        return sum(term.astype(F32) for term in terms)
 
     def decoder_part(decoder, which, where):
         return lax.dynamic_slice(decoder, (which, 0, where * part), (1, 2 * latents, part))[0]
@@ -102,59 +100,64 @@
 
     weight_other = over_core(enc_weight[0])
     mine = lax.dynamic_slice(resid, (layer, 0, half * cols), (1, rows, cols))[0]
-    pair, weight_other, bias, blocks = hold((paired(mine, over_x(mine)), weight_other, enc_bias[0], blocks))
-    column = along_z(pair)
+    pair, weight_other, bias, blocks, early = hold(
+        (paired(mine, over_x(mine)), weight_other, enc_bias[0], blocks, target)
+    )
+    column = along_z([pair] * far)
+
+    start = half * cols
+
+    def aim_own(target, where):
+        return lax.dynamic_slice(target, (2 * layer, 0, start + where * part), (1, rows, part))[0]
+
+    aim_mine = aim_own(early, side)
+    aim_shared = lax.dynamic_slice(early, (1, 0, start + layer * part), (1, rows, part))[0]
 
     own_other = over_x(decoder_part(decoder, layer, 1 - side))
     shared_other = over_y(decoder_part(decoder, 1 - layer, 1 - layer))
-    decoder, own_other, shared_other, *column = hold((decoder, own_other, shared_other, *column))
+    flags = firing_flags(blocks, layer, slot, slots, latents)
+    decoder, own_other, shared_other, aim_mine, aim_shared, flags, *column = hold(
+        (decoder, own_other, shared_other, aim_mine, aim_shared, flags, *column[::-1])
+    )
+    column = column[::-1]
     own_mine, shared_mine = decoder_part(decoder, layer, side), decoder_part(decoder, 1 - layer, layer)
     resid_half = jnp.concatenate(column, axis=0)
-    firing = gates(blocks, layer, slot, slots, latents, tokens)
+    firing = gates(flags, tokens)
     gate = jnp.where(half == 0, firing[0], firing[1])
 
     partial = half_preacts(resid_half, enc_weight[0], weight_other, bias, half)
     acts = ((partial + over_core(partial)) * jnp.concatenate(firing, axis=1)).astype(BF16)
     acts_turned = turned(acts)
     acts_y, acts_x = over_y(acts), over_x(acts_turned)
-    target, _ = hold((target, acts_turned))
-    start = half * cols
-
-    def aim_own(where):
-        return lax.dynamic_slice(target, (2 * layer, 0, start + where * part), (1, rows, part))[0]
-
-    aim_other = over_x(aim_own(1 - side))
-    aim_shared = lax.dynamic_slice(target, (1, 0, start + layer * part), (1, rows, part))[0]
+    target, _ = hold((target, partial))
+    aim_other = over_x(aim_own(target, 1 - side))
 
     leaving = times(rows_at(acts, 1), shared_mine) + times(rows_at(acts_y, 1), shared_other)
     staying = times(rows_at(acts, 0), shared_mine) + times(rows_at(acts_y, 0), shared_other)
     arrived = over_x(leaving.astype(BF16))
     product = times(acts, own_mine) + times(acts_x, own_other)
-    arrived, staying = hold((arrived, staying))
-    own_terms = sent_along_z(product)
-    shared_terms = sent_along_z(staying + arrived.astype(F32))
-    terms = hold((*shared_terms, *own_terms))
-    shared_terms, own_terms = terms[:far], terms[far:]
-    err_own = (added(own_terms) - paired(aim_own(side), aim_other).astype(F32)).astype(BF16)
-    own_column = along_z(err_own)
-    err_shared = (added(shared_terms) - aim_shared.astype(F32)).astype(BF16)
-
-    shared_near = jnp.concatenate(along_z(err_shared), axis=0)
-    resid_swapped, _ = hold((resid_half, shared_near))
+    own_pieces = pieces_of(product)
+    arrived, staying, own_pieces[1] = hold((arrived, staying, own_pieces[1]))
+    own_terms = along_z(own_pieces)
+    shared_terms = along_z(pieces_of(staying + arrived.astype(F32)))
+    terms = hold((*shared_terms[::-1], *own_terms[::-1]))
+    err_shared = (added(terms[far - 1::-1]) - aim_shared.astype(F32)).astype(BF16)
+    err_own = (added(terms[:far - 1:-1]) - paired(aim_mine, aim_other).astype(F32)).astype(BF16)
+
+    own_column = along_z([err_own] * far)
+    message = jnp.concatenate(along_z([err_shared] * far), axis=0)
+    message, resid_swapped = hold((message, resid_half))
+    returned = over_x(message)
     resid_other = over_core(resid_swapped)
-    errs_shared = paired(shared_near, over_x(shared_near))
     errs_own = jnp.concatenate(own_column, axis=0)
 
-    grads = jnp.concatenate(
-        [
-            times_transposed(errs_own, own_mine) + times_transposed(errs_shared, shared_mine),
-            turned(times_transposed(errs_own, own_other)),
-            times_transposed(errs_shared, shared_other),
-        ],
-        axis=0,
-    )
+    own_grads = [times_transposed(errs_own, weights) for weights in (own_mine, own_other)]
+    errs_shared = paired(message, returned)
+    shared_grads = [times_transposed(errs_shared, weights) for weights in (shared_mine, shared_other)]
+    grads = jnp.concatenate([own_grads[0] + shared_grads[0], turned(own_grads[1]), shared_grads[1]], axis=0)
     lower, upper = grads[:, :latents], grads[:, latents:]
     grads = jnp.where(half == 0, lower, upper) + over_core(jnp.where(half == 0, upper, lower))
+
 
     def with_errors(grad, block):
         tiles = [block[:, at:at + latents] for at in range(0, part, latents)]
@@ -196,7 +199,7 @@
         return lax.ppermute(block, "layer", route)
 
     resid_half = to_all(lax.dynamic_slice(resid, (layer, 0, half * cols), (1, rows, cols))[0])
-    firing = gates(blocks, layer, slot, slots, latents, tokens)
+    firing = gates(firing_flags(blocks, layer, slot, slots, latents), tokens)
     gate = jnp.where(half == 0, firing[0], firing[1])
     weight_other = crossed(enc_weight[0], "layer", 1)
     partial = half_preacts(resid_half, enc_weight[0], weight_other, enc_bias[0], half)

time: 68.7 us -> 70.7 us (1.029)
  starting transfers between devices: 34.9 us -> 31.9 us
  local copies, waits for them, and re-layouts: 3.97 us -> 6.56 us
  matrix products: 4.17 us -> 5.32 us
  waiting for transfers between devices: 19.7 us -> 20.8 us
    ppermute x29, starting transfers between devices: 34.9 us -> 31.9 us  [crossed(): lax.ppermute(block, axis, [(i, i ^ mask) for i in range(lax.axis_size(axi...]
    unnamed x36, local copies, waits for them, and re-layouts: 0.24 us -> 2.03 us
    squeeze x0 -> x2, local copies, waits for them, and re-layouts: none -> 1.55 us  [the longest x1 0.8 us: two_layers(): lax.dynamic_slice(early, (1, 0, start + layer * part), (1, rows, part))[0]]
    dot_general x7, matrix products: 1.61 us -> 2.77 us  [times(): return jnp.dot(left, right, preferred_element_type=F32)]
    ppermute x29, waiting for transfers between devices: 19.7 us -> 20.8 us  [crossed(): lax.ppermute(block, axis, [(i, i ^ mask) for i in range(lax.axis_size(axi...]
    select_n x3, other arithmetic: 0.25 us -> 1.17 us  [both_halves(): jnp.where(half == 0, mine, other)]
    another operation x2 -> x1, local copies, waits for them, and re-layouts: 1.6 us -> 0.83 us  [paired(): block.reshape(-1, 1, rows, block.shape[1])]
    convert_element_type x2, other arithmetic: 0.82 us -> 0.07 us  [the longest x1 0.05 us: two_layers(): (added(terms[:far - 1:-1]) - paired(aim_mine, aim_other).astype(F32)).ast...]
  transfers between devices with their start and end apart: 29 -> 29, of which waited for: 12 -> 15; matrix products, arithmetic and copies ran while one was open for 11% -> 13% of each run, Pallas kernels for 0% -> 0%
where the time goes in v10:
time: 70.7 us; the launch traced here: 70.3 us
  starting transfers between devices  31.9 us (45%)
  waiting for transfers between devices  20.8 us (29%)
  local copies, waits for them, and re-layouts  6.56 us (9%)
  matrix products  5.32 us (8%)
  other arithmetic  3.31 us (5%)
  between operations  2.47 us (3%)
    ppermute x29, starting transfers between devices, crossed(): lax.ppermute(block, axis, [(i, i ^ mask) for i in range(lax.axis_size(axi...  31.9 us
    ppermute x29, waiting for transfers between devices, crossed(): lax.ppermute(block, axis, [(i, i ^ mask) for i in range(lax.axis_size(axi...  20.8 us
    dot_general x7, matrix products, times(): return jnp.dot(left, right, preferred_element_type=F32)  2.77 us
    squeeze x1, local copies, waits for them, and re-layouts, decoder_part(): lax.dynamic_slice(decoder, (which, 0, where * part), (1, 2 * latents, part))  2.04 us
    unnamed x36, local copies, waits for them, and re-layouts  2.03 us
  transfers between devices with their start and end apart: 29, of which 15 were waited for; matrix products, arithmetic and copies ran while one was open for 13% of the time, Pallas kernels for 0%

profile of v10, /device:TPU:0, one launch (start us, length us, event | category | flops | bytes accessed | tf_op | source)
XLA Modules:
  0.0 70.3 jit_solution(13786969671409279862)
XLA Ops:
  0.6 0.5 collective-permute-start.3
  1.2 0.8 %dynamic-slice_bitcast_fusion.3 = (bf16[1,1,16,1792]{3,2,1,0:T(8,128)(2,1)S(1)}, bf16[16,1792]{1,0:T(8,128)(2,1)S(1)}) fusion(bf16[2,16,3584]{2,1,0:T(8,128)(2,1)} %param.6, s32[]{:T(128)S(6)} %select_n.156, s32[]{:T(128)S(6)} %select_n.161), kind=kLoop, calls=%fused_computation.88 | loop fusion | bytes 172040 | tf_op jit(solution)/shard_map/reshape;squeeze | solution.py:95
  2.0 2.6 %collective-permute-start.2 = (bf16[16,1792]{1,0:T(8,128)(2,1)S(1)}, bf16[16,1792]{1,0:T(8,128)(2,1)S(1)}, u32[]{:S(2)}, u32[]{:S(2)}) collective-permute-start(bf16[16,1792]{1,0:T(8,128)(2,1)S(1)} %get-tuple-element.81), channel_id=1, source_target_pairs={{0,1},{1,0},{2,3},{3,2},{4,5},{5,4},{6,7},{7,6},{8,9},{9,8},{10,11... | collective-permute-start | bytes 172040 | tf_op jit(solution)/shard_map/ppermute | solution.py:11
  4.6 2.0 %dynamic-slice_bitcast_fusion = (bf16[256,896]{1,0:T(8,128)(2,1)S(1)}, bf16[256,896]{1,0:T(8,128)(2,1)}) fusion(bf16[2,256,1792]{2,1,0:T(8,128)(2,1)} %bitcast.121, s32[]{:T(128)S(6)} %select_n.158, s32[]{:T(128)S(6)} %select_n.159, s32[]{:T(128)S(6)} %select_n.156, s32[]{:T(128)S(6)} %select_n.157), kind=kLoop, calls=%fused_computation.24 | loop fusion | bytes 1835024 | tf_op jit(solution)/shard_map/squeeze | solution.py:86
  6.7 0.0 collective-permute-start
  6.7 2.0 %collective-permute-start.1 = (bf16[256,896]{1,0:T(8,128)(2,1)S(1)}, bf16[256,896]{1,0:T(8,128)(2,1)S(1)}, u32[]{:S(2)}, u32[]{:S(2)}) collective-permute-start(bf16[256,896]{1,0:T(8,128)(2,1)S(1)} %get-tuple-element.71), channel_id=1, source_target_pairs={{0,16},{8,24},{16,0},{24,8},{1,17},{9,25},{17,1},{25,9},{2,18},{10... | collective-permute-start | bytes 1376264 | tf_op jit(solution)/shard_map/ppermute | solution.py:11
  8.7 3.7 %collective-permute-start.4 = (bf16[32,1792]{1,0:T(8,128)(2,1)S(1)}, bf16[32,1792]{1,0:T(8,128)(2,1)S(1)}, u32[]{:S(2)}, u32[]{:S(2)}) collective-permute-start(bf16[32,1792]{1,0:T(8,128)(2,1)S(1)} %bitcast.132), channel_id=1, source_target_pairs={{0,6},{1,7},{2,4},{3,5},{4,2},{5,3},{6,0},{7,1},{8,14},{9,15},{10,... | collective-permute-start | bytes 344072 | tf_op jit(solution)/shard_map/ppermute | solution.py:11
  12.4 0.8 %collective-permute-start.6 = (bf16[32,1792]{1,0:T(8,128)(2,1)S(1)}, bf16[32,1792]{1,0:T(8,128)(2,1)}, u32[]{:S(2)}, u32[]{:S(2)}) collective-permute-start(bf16[32,1792]{1,0:T(8,128)(2,1)S(1)} %bitcast.134), channel_id=1, source_target_pairs={{0,2},{1,3},{2,0},{3,1},{4,6},{5,7},{6,4},{7,5},{8,10},{9,11},{10,... | collective-permute-start | bytes 344072 | tf_op jit(solution)/shard_map/ppermute | solution.py:11
  13.2 1.1 %bitcast_select_fusion.1 = (bf16[1792,128]{1,0:T(8,128)(2,1)}, bf16[1792,128]{1,0:T(8,128)(2,1)}) fusion(pred[]{:T(512)S(6)} %eq.61, bf16[3584,128]{1,0:T(8,128)(2,1)S(1)} %collective-permute-done.3, s32[]{:T(128)S(6)} %select_n.161, bf16[1,3584,128]{2,1,0:T(8,128)(2,1)S(1)} %copy-done.1), kind=kLoop, calls=%fused_computation.23 | loop fusion | flops 458752 | bytes 1835013 | tf_op jit(solution)/shard_map/jit(_where)/select_n | solution.py:23
  14.3 0.6 compare_reduce_fusion
  15.6 0.0 copy-start
  16.4 0.8 %dynamic-slice_bitcast_fusion.5 = (bf16[16,896]{1,0:T(8,128)(2,1)S(1)}, bf16[16,896]{1,0:T(8,128)(2,1)S(1)}) fusion(bf16[3,16,3584]{2,1,0:T(8,128)(2,1)} %param.7, s32[]{:T(128)S(6)} %select_n.164, s32[]{:T(128)S(6)} %select_n.162, s32[]{:T(128)S(6)} %select_n.163), kind=kLoop, calls=%fused_computation.96 | loop fusion | bytes 114700 | tf_op jit(solution)/shard_map/squeeze | solution.py:114
  17.2 2.2 %collective-permute-done = bf16[256,896]{1,0:T(8,128)(2,1)S(1)} collective-permute-done((bf16[256,896]{1,0:T(8,128)(2,1)}, bf16[256,896]{1,0:T(8,128)(2,1)S(1)}, u32[]{:S(2)}, u32[]{:S(2)}) %collective-permute-start) | collective-permute-done | bytes 458784 | tf_op jit(solution)/shard_map/ppermute | solution.py:11
  19.4 2.5 %collective-permute-done.5 = bf16[32,1792]{1,0:T(8,128)(2,1)} collective-permute-done((bf16[32,1792]{1,0:T(8,128)(2,1)S(1)}, bf16[32,1792]{1,0:T(8,128)(2,1)}, u32[]{:S(2)}, u32[]{:S(2)}) %collective-permute-start.5) | collective-permute-done | bytes 114720 | tf_op jit(solution)/shard_map/ppermute | solution.py:11
  21.9 0.9 %constant_dynamic-update-slice_fusion.2 = bf16[128,1792]{1,0:T(8,128)(2,1)S(1)} fusion(bf16[128,1792]{1,0:T(8,128)(2,1)S(1)} %constant_dynamic-update-slice_fusion.3, bf16[32,1792]{1,0:T(8,128)(2,1)} %collective-permute-done.6), kind=kLoop, calls=%fused_computation.47 | loop fusion | bytes 229376
  22.8 0.9 %constant_dynamic-update-slice_fusion.1 = bf16[128,1792]{1,0:T(8,128)(2,1)S(1)} fusion(bf16[128,1792]{1,0:T(8,128)(2,1)S(1)} %constant_dynamic-update-slice_fusion.2, bf16[32,1792]{1,0:T(8,128)(2,1)} %collective-permute-done.5), kind=kLoop, calls=%fused_computation.46 | loop fusion | bytes 229376
  23.7 1.5 %convolution_add_fusion.4 = f32[128,256]{1,0:T(8,128)S(1)} fusion(bf16[128,1792]{1,0:T(8,128)(2,1)S(1)} %constant_dynamic-update-slice_fusion, bf16[1792,128]{1,0:T(8,128)(2,1)} %get-tuple-element.70, bf16[1792,128]{1,0:T(8,128)(2,1)} %get-tuple-element.69, f32[256]{0:T(256)S(1)} %pad_maximum_fusion.10), kind=kOutput, calls=%fused_computation.7 | convolution fusion | flops 119308288 | bytes 1508352 | tf_op jit(solution)/shard_map/dot_general | solution.py:15
  25.2 0.1 collective-permute-start.7
  25.3 0.8 %dynamic-slice_bitcast_fusion.4 = bf16[16,896]{1,0:T(8,128)(2,1)S(1)} fusion(bf16[3,16,3584]{2,1,0:T(8,128)(2,1)} %param.7, s32[]{:T(128)S(6)} %select_n.162, s32[]{:T(128)S(6)} %select_n.173), kind=kLoop, calls=%fused_computation.95 | loop fusion | bytes 57352 | tf_op jit(solution)/shard_map/squeeze | solution.py:111
  26.1 1.5 %collective-permute-start.17 = (bf16[16,896]{1,0:T(8,128)(2,1)S(1)}, bf16[16,896]{1,0:T(8,128)(2,1)S(1)}, u32[]{:S(2)}, u32[]{:S(2)}) collective-permute-start(bf16[16,896]{1,0:T(8,128)(2,1)S(1)} %dynamic-slice_bitcast_fusion.4), channel_id=1, source_target_pairs={{0,1},{1,0},{2,3},{3,2},{4,5},{5,4},{6,7},{7,6},{8,9},{9,8},{10,11... | collective-permute-start | bytes 86024 | tf_op jit(solution)/shard_map/ppermute | solution.py:11
  27.6 0.6 collective-permute-start.8
  28.2 0.2 fusion.14
  28.4 0.2 fusion.12
  28.6 0.6 collective-permute-start.10
  29.2 2.7 %collective-permute-done.8 = bf16[128,256]{1,0:T(8,128)(2,1)S(1)} collective-permute-done((bf16[128,256]{1,0:T(8,128)(2,1)S(1)}, bf16[128,256]{1,0:T(8,128)(2,1)S(1)}, u32[]{:S(2)}, u32[]{:S(2)}) %collective-permute-start.8) | collective-permute-done | bytes 65568 | tf_op jit(solution)/shard_map/ppermute | solution.py:11
  31.9 0.2 fusion.1
  32.1 0.6 collective-permute-start.9
  32.7 0.2 collective-permute-done.10
  33.0 0.2 fusion.45
  33.2 0.2 fusion.44
  33.5 2.5 %collective-permute-start.14 = (bf16[32,896]{1,0:T(8,128)(2,1)S(1)}, bf16[32,896]{1,0:T(8,128)(2,1)S(1)}, u32[]{:S(2)}, u32[]{:S(2)}) collective-permute-start(bf16[32,896]{1,0:T(8,128)(2,1)S(1)} %get-tuple-element.78), channel_id=1, source_target_pairs={{0,6},{1,7},{2,4},{3,5},{4,2},{5,3},{6,0},{7,1},{8,14},{9,15},{10,... | collective-permute-start | bytes 172040 | tf_op jit(solution)/shard_map/ppermute | solution.py:11
  36.0 0.2 convolution_add_fusion.1
  36.2 0.8 %collective-permute-done.9 = bf16[64,896]{1,0:T(8,128)(2,1)S(1)} collective-permute-done((bf16[64,896]{1,0:T(8,128)(2,1)S(1)}, bf16[64,896]{1,0:T(8,128)(2,1)S(1)}, u32[]{:S(2)}, u32[]{:S(2)}) %collective-permute-start.9) | collective-permute-done | bytes 114720 | tf_op jit(solution)/shard_map/ppermute | solution.py:11
  37.1 2.5 %collective-permute-start.11 = (bf16[16,896]{1,0:T(8,128)(2,1)S(1)}, bf16[16,896]{1,0:T(8,128)(2,1)S(1)}, u32[]{:S(2)}, u32[]{:S(2)}) collective-permute-start(bf16[16,896]{1,0:T(8,128)(2,1)S(1)} %get-tuple-element.86), channel_id=1, source_target_pairs={{0,6},{1,7},{2,4},{3,5},{4,2},{5,3},{6,0},{7,1},{8,14},{9,15},{10,... | collective-permute-start | bytes 86024 | tf_op jit(solution)/shard_map/ppermute | solution.py:11
  39.6 0.1 collective-permute-start.12
  39.7 1.8 %collective-permute-start.13 = (bf16[16,896]{1,0:T(8,128)(2,1)S(1)}, bf16[16,896]{1,0:T(8,128)(2,1)S(1)}, u32[]{:S(2)}, u32[]{:S(2)}) collective-permute-start(bf16[16,896]{1,0:T(8,128)(2,1)S(1)} %get-tuple-element.84), channel_id=1, source_target_pairs={{0,2},{1,3},{2,0},{3,1},{4,6},{5,7},{6,4},{7,5},{8,10},{9,11},{10,... | collective-permute-start | bytes 86024 | tf_op jit(solution)/shard_map/ppermute | solution.py:11
  41.5 0.3 collective-permute-start.16
  41.8 0.4 collective-permute-done.15
  42.2 0.9 %collective-permute-done.11 = bf16[16,896]{1,0:T(8,128)(2,1)S(1)} collective-permute-done((bf16[16,896]{1,0:T(8,128)(2,1)S(1)}, bf16[16,896]{1,0:T(8,128)(2,1)S(1)}, u32[]{:S(2)}, u32[]{:S(2)}) %collective-permute-start.11) | collective-permute-done | bytes 28704 | tf_op jit(solution)/shard_map/ppermute | solution.py:11
  43.1 1.3 %collective-permute-done.12 = bf16[16,896]{1,0:T(8,128)(2,1)S(1)} collective-permute-done((bf16[16,896]{1,0:T(8,128)(2,1)S(1)}, bf16[16,896]{1,0:T(8,128)(2,1)S(1)}, u32[]{:S(2)}, u32[]{:S(2)}) %collective-permute-start.12) | collective-permute-done | bytes 28704 | tf_op jit(solution)/shard_map/ppermute | solution.py:11
  44.4 1.3 %collective-permute-done.16 = bf16[32,896]{1,0:T(8,128)(2,1)S(1)} collective-permute-done((bf16[32,896]{1,0:T(8,128)(2,1)S(1)}, bf16[32,896]{1,0:T(8,128)(2,1)S(1)}, u32[]{:S(2)}, u32[]{:S(2)}) %collective-permute-start.16) | collective-permute-done | bytes 57376 | tf_op jit(solution)/shard_map/ppermute | solution.py:11
  45.7 2.5 %collective-permute-start.23 = (bf16[16,896]{1,0:T(8,128)(2,1)S(1)}, bf16[16,896]{1,0:T(8,128)(2,1)S(1)}, u32[]{:S(2)}, u32[]{:S(2)}) collective-permute-start(bf16[16,896]{1,0:T(8,128)(2,1)S(1)} %subtract_convert_fusion), channel_id=1, source_target_pairs={{0,6},{1,7},{2,4},{3,5},{4,2},{5,3},{6,0},{7,1},{8,14},{9,15},{10,... | collective-permute-start | bytes 86024 | tf_op jit(solution)/shard_map/ppermute | solution.py:11
  48.3 1.9 %collective-permute-start.21 = (bf16[16,896]{1,0:T(8,128)(2,1)S(1)}, bf16[16,896]{1,0:T(8,128)(2,1)S(1)}, u32[]{:S(2)}, u32[]{:S(2)}) collective-permute-start(bf16[16,896]{1,0:T(8,128)(2,1)S(1)} %subtract_convert_fusion), channel_id=1, source_target_pairs={{0,2},{1,3},{2,0},{3,1},{4,6},{5,7},{6,4},{7,5},{8,10},{9,11},{10,... | collective-permute-start | bytes 86024 | tf_op jit(solution)/shard_map/ppermute | solution.py:11
  50.2 2.5 %collective-permute-start.20 = (bf16[32,896]{1,0:T(8,128)(2,1)S(1)}, bf16[32,896]{1,0:T(8,128)(2,1)S(1)}, u32[]{:S(2)}, u32[]{:S(2)}) collective-permute-start(bf16[32,896]{1,0:T(8,128)(2,1)S(1)} %fusion.21), channel_id=1, source_target_pairs={{0,6},{1,7},{2,4},{3,5},{4,2},{5,3},{6,0},{7,1},{8,14},{9,15},{10,... | collective-permute-start | bytes 172040 | tf_op jit(solution)/shard_map/ppermute | solution.py:11
  52.8 1.9 %collective-permute-start.18 = (bf16[32,896]{1,0:T(8,128)(2,1)S(1)}, bf16[32,896]{1,0:T(8,128)(2,1)S(1)}, u32[]{:S(2)}, u32[]{:S(2)}) collective-permute-start(bf16[32,896]{1,0:T(8,128)(2,1)S(1)} %fusion.21), channel_id=1, source_target_pairs={{0,2},{1,3},{2,0},{3,1},{4,6},{5,7},{6,4},{7,5},{8,10},{9,11},{10,... | collective-permute-start | bytes 172040 | tf_op jit(solution)/shard_map/ppermute | solution.py:11
  54.7 0.6 collective-permute-start.24
  55.3 1.0 %collective-permute-done.20 = bf16[32,896]{1,0:T(8,128)(2,1)S(1)} collective-permute-done((bf16[32,896]{1,0:T(8,128)(2,1)S(1)}, bf16[32,896]{1,0:T(8,128)(2,1)S(1)}, u32[]{:S(2)}, u32[]{:S(2)}) %collective-permute-start.20) | collective-permute-done | bytes 57376 | tf_op jit(solution)/shard_map/ppermute | solution.py:11
  56.3 1.6 %collective-permute-done.19 = bf16[32,896]{1,0:T(8,128)(2,1)S(1)} collective-permute-done((bf16[32,896]{1,0:T(8,128)(2,1)S(1)}, bf16[32,896]{1,0:T(8,128)(2,1)S(1)}, u32[]{:S(2)}, u32[]{:S(2)}) %collective-permute-start.19) | collective-permute-done | bytes 57376 | tf_op jit(solution)/shard_map/ppermute | solution.py:11
  57.8 0.3 fusion.24
  58.2 1.4 %collective-permute-done.24 = bf16[64,896]{1,0:T(8,128)(2,1)S(1)} collective-permute-done((bf16[64,896]{1,0:T(8,128)(2,1)S(1)}, bf16[64,896]{1,0:T(8,128)(2,1)S(1)}, u32[]{:S(2)}, u32[]{:S(2)}) %collective-permute-start.24) | collective-permute-done | bytes 114720 | tf_op jit(solution)/shard_map/ppermute | solution.py:11
  59.6 0.3 fusion.46
  59.9 0.3 fusion.10
  60.2 0.3 convolution_add_fusion.3
  60.6 0.1 collective-permute-start.25
  60.7 0.5 collective-permute-start.28
  61.2 0.9 %collective-permute-done.25 = f32[384,128]{1,0:T(8,128)S(1)} collective-permute-done((f32[384,128]{1,0:T(8,128)S(1)}, f32[384,128]{1,0:T(8,128)S(1)}, u32[]{:S(2)}, u32[]{:S(2)}) %collective-permute-start.25) | collective-permute-done | bytes 196640 | tf_op jit(solution)/shard_map/ppermute | solution.py:11
  62.2 1.1 %collective-permute-start.27 = (bf16[240,128]{1,0:T(8,128)(2,1)S(1)}, bf16[240,128]{1,0:T(8,128)(2,1)S(1)}, u32[]{:S(2)}, u32[]{:S(2)}) collective-permute-start(bf16[240,128]{1,0:T(8,128)(2,1)S(1)} %constant_dynamic-update-slice_fusion.19), channel_id=1, source_target_pairs={{0,16},{8,24},{16,0},{24,8},{1,17},{9,25},{17,1},{25,9},{2,18},{10... | collective-permute-start | bytes 184328 | tf_op jit(solution)/shard_map/ppermute | solution.py:11
  63.3 0.5 collective-permute-start.26
  63.8 2.7 %collective-permute-done.27 = bf16[240,128]{1,0:T(8,128)(2,1)S(1)} collective-permute-done((bf16[240,128]{1,0:T(8,128)(2,1)S(1)}, bf16[240,128]{1,0:T(8,128)(2,1)S(1)}, u32[]{:S(2)}, u32[]{:S(2)}) %collective-permute-start.27) | collective-permute-done | bytes 61472 | tf_op jit(solution)/shard_map/ppermute | solution.py:11
  66.6 1.0 %collective-permute-done.26 = bf16[240,128]{1,0:T(8,128)(2,1)S(1)} collective-permute-done((bf16[240,128]{1,0:T(8,128)(2,1)S(1)}, bf16[240,128]{1,0:T(8,128)(2,1)S(1)}, u32[]{:S(2)}, u32[]{:S(2)}) %collective-permute-start.26) | collective-permute-done | bytes 61472 | tf_op jit(solution)/shard_map/ppermute | solution.py:11
  67.7 0.5 fusion.26
  68.3 0.6 maximum_select_fusion
  68.9 0.1 broadcast_select_fusion.1
  69.0 1.4 %fusion = bf16[1,3584,128]{2,1,0:T(8,128)(2,1)} fusion(bf16[128,1792]{1,0:T(8,128)(2,1)S(1)} %get-tuple-element.74, bf16[128,1792]{1,0:T(8,128)(2,1)S(1)} %get-tuple-element.73, f32[384,128]{1,0:T(8,128)S(1)} %get-tuple-element.66, bf16[240,128]{1,0:T(8,128)(2,1)S(1)} %collective-permute-done.27, bf16[240,128]{1,0:T(8,128)(2,1)S(1)} %collective-permute-done.26, ...), kind=kOutput, calls=%fused_computation.1 | convolution fusion | flops 119832576 | bytes 1966084 | tf_op jit(solution)/shard_map/dot_general | solution.py:47
  (82 shorter events, 0.7 us)
Async XLA Ops:
  0.6 12.6 %copy-start.1 = (bf16[1,3584,128]{2,1,0:T(8,128)(2,1)S(1)}, bf16[1,3584,128]{2,1,0:T(8,128)(2,1)}, u32[]{:S(2)}) copy-start(bf16[1,3584,128]{2,1,0:T(8,128)(2,1)} %param.8) | copy-start | bytes 2752516
  0.6 8.1 %collective-permute-start.3 = (bf16[3584,128]{1,0:T(8,128)(2,1)}, bf16[3584,128]{1,0:T(8,128)(2,1)S(1)}, u32[]{:S(2)}, u32[]{:S(2)}) collective-permute-start(bf16[3584,128]{1,0:T(8,128)(2,1)} %bitcast.140), channel_id=1, source_target_pairs={{0,8},{8,0},{16,24},{24,16},{1,9},{9,1},{17,25},{25,17},{2,10},{10... | collective-permute-start | bytes 2752520 | tf_op jit(solution)/shard_map/ppermute | solution.py:11
  2.0 6.7 %collective-permute-start.2 = (bf16[16,1792]{1,0:T(8,128)(2,1)S(1)}, bf16[16,1792]{1,0:T(8,128)(2,1)S(1)}, u32[]{:S(2)}, u32[]{:S(2)}) collective-permute-start(bf16[16,1792]{1,0:T(8,128)(2,1)S(1)} %get-tuple-element.81), channel_id=1, source_target_pairs={{0,1},{1,0},{2,3},{3,2},{4,5},{5,4},{6,7},{7,6},{8,9},{9,8},{10,11... | collective-permute-start | bytes 172040 | tf_op jit(solution)/shard_map/ppermute | solution.py:11
  4.6 9.7 %copy-start.2 = (f32[1,128]{1,0:T(1,128)S(1)}, f32[1,128]{1,0:T(1,128)}, u32[]{:S(2)}) copy-start(f32[1,128]{1,0:T(1,128)} %param.9) | copy-start | bytes 1540
  4.6 9.7 %copy-start.3 = (s32[2,1,12]{2,1,0:T(1,128)S(1)}, s32[2,1,12]{2,1,0:T(1,128)}, u32[]{:S(2)}) copy-start(s32[2,1,12]{2,1,0:T(1,128)} %param.11) | copy-start | bytes 292
  6.7 12.7 %collective-permute-start = (bf16[256,896]{1,0:T(8,128)(2,1)}, bf16[256,896]{1,0:T(8,128)(2,1)S(1)}, u32[]{:S(2)}, u32[]{:S(2)}) collective-permute-start(bf16[256,896]{1,0:T(8,128)(2,1)} %get-tuple-element.72), channel_id=1, source_target_pairs={{0,1},{1,0},{2,3},{3,2},{4,5},{5,4},{6,7},{7,6},{8,9},{9,8},{10,11... | collective-permute-start | bytes 1376264 | tf_op jit(solution)/shard_map/ppermute | solution.py:11
  6.7 12.7 %collective-permute-start.1 = (bf16[256,896]{1,0:T(8,128)(2,1)S(1)}, bf16[256,896]{1,0:T(8,128)(2,1)S(1)}, u32[]{:S(2)}, u32[]{:S(2)}) collective-permute-start(bf16[256,896]{1,0:T(8,128)(2,1)S(1)} %get-tuple-element.71), channel_id=1, source_target_pairs={{0,16},{8,24},{16,0},{24,8},{1,17},{9,25},{17,1},{25,9},{2,18},{10... | collective-permute-start | bytes 1376264 | tf_op jit(solution)/shard_map/ppermute | solution.py:11
  8.7 10.6 %collective-permute-start.4 = (bf16[32,1792]{1,0:T(8,128)(2,1)S(1)}, bf16[32,1792]{1,0:T(8,128)(2,1)S(1)}, u32[]{:S(2)}, u32[]{:S(2)}) collective-permute-start(bf16[32,1792]{1,0:T(8,128)(2,1)S(1)} %bitcast.132), channel_id=1, source_target_pairs={{0,6},{1,7},{2,4},{3,5},{4,2},{5,3},{6,0},{7,1},{8,14},{9,15},{10,... | collective-permute-start | bytes 344072 | tf_op jit(solution)/shard_map/ppermute | solution.py:11
  12.4 9.5 %collective-permute-start.5 = (bf16[32,1792]{1,0:T(8,128)(2,1)S(1)}, bf16[32,1792]{1,0:T(8,128)(2,1)}, u32[]{:S(2)}, u32[]{:S(2)}) collective-permute-start(bf16[32,1792]{1,0:T(8,128)(2,1)S(1)} %bitcast.133), channel_id=1, source_target_pairs={{0,4},{1,5},{2,6},{3,7},{4,0},{5,1},{6,2},{7,3},{8,12},{9,13},{10,... | collective-permute-start | bytes 344072 | tf_op jit(solution)/shard_map/ppermute | solution.py:11
  12.4 9.5 %collective-permute-start.6 = (bf16[32,1792]{1,0:T(8,128)(2,1)S(1)}, bf16[32,1792]{1,0:T(8,128)(2,1)}, u32[]{:S(2)}, u32[]{:S(2)}) collective-permute-start(bf16[32,1792]{1,0:T(8,128)(2,1)S(1)} %bitcast.134), channel_id=1, source_target_pairs={{0,2},{1,3},{2,0},{3,1},{4,6},{5,7},{6,4},{7,5},{8,10},{9,11},{10,... | collective-permute-start | bytes 344072 | tf_op jit(solution)/shard_map/ppermute | solution.py:11
  15.6 12.5 %copy-start = (bf16[1,2,2,128,1792]{4,3,2,1,0:T(8,128)(2,1)S(1)}, bf16[1,2,2,128,1792]{4,3,2,1,0:T(8,128)(2,1)}, u32[]{:S(2)}) copy-start(bf16[1,2,2,128,1792]{4,3,2,1,0:T(8,128)(2,1)} %param.10) | copy-start | bytes 5505028
  25.2 2.4 %collective-permute-start.7 = (f32[128,256]{1,0:T(8,128)S(1)}, f32[128,256]{1,0:T(8,128)S(1)}, u32[]{:S(2)}, u32[]{:S(2)}) collective-permute-start(f32[128,256]{1,0:T(8,128)S(1)} %convolution_add_fusion.4), channel_id=1, source_target_pairs={{0,8},{8,0},{16,24},{24,16},{1,9},{9,1},{17,25},{25,17},{2,10},{10... | collective-permute-start | bytes 393224 | tf_op jit(solution)/shard_map/ppermute | solution.py:11
  26.1 13.7 %collective-permute-start.17 = (bf16[16,896]{1,0:T(8,128)(2,1)S(1)}, bf16[16,896]{1,0:T(8,128)(2,1)S(1)}, u32[]{:S(2)}, u32[]{:S(2)}) collective-permute-start(bf16[16,896]{1,0:T(8,128)(2,1)S(1)} %dynamic-slice_bitcast_fusion.4), channel_id=1, source_target_pairs={{0,1},{1,0},{2,3},{3,2},{4,5},{5,4},{6,7},{7,6},{8,9},{9,8},{10,11... | collective-permute-start | bytes 86024 | tf_op jit(solution)/shard_map/ppermute | solution.py:11
  27.6 4.3 %collective-permute-start.8 = (bf16[128,256]{1,0:T(8,128)(2,1)S(1)}, bf16[128,256]{1,0:T(8,128)(2,1)S(1)}, u32[]{:S(2)}, u32[]{:S(2)}) collective-permute-start(bf16[128,256]{1,0:T(8,128)(2,1)S(1)} %multiply_convert_fusion), channel_id=1, source_target_pairs={{0,16},{8,24},{16,0},{24,8},{1,17},{9,25},{17,1},{25,9},{2,18},{10... | collective-permute-start | bytes 196616 | tf_op jit(solution)/shard_map/ppermute | solution.py:11
  28.6 4.3 %collective-permute-start.10 = (bf16[128,256]{1,0:T(8,128)(2,1)S(1)}, bf16[128,256]{1,0:T(8,128)(2,1)S(1)}, u32[]{:S(2)}, u32[]{:S(2)}) collective-permute-start(bf16[128,256]{1,0:T(8,128)(2,1)S(1)} %bitcast.146), channel_id=1, source_target_pairs={{0,1},{1,0},{2,3},{3,2},{4,5},{5,4},{6,7},{7,6},{8,9},{9,8},{10,11... | collective-permute-start | bytes 196616 | tf_op jit(solution)/shard_map/ppermute | solution.py:11
  32.1 4.9 %collective-permute-start.9 = (bf16[64,896]{1,0:T(8,128)(2,1)S(1)}, bf16[64,896]{1,0:T(8,128)(2,1)S(1)}, u32[]{:S(2)}, u32[]{:S(2)}) collective-permute-start(bf16[64,896]{1,0:T(8,128)(2,1)S(1)} %fusion.1), channel_id=1, source_target_pairs={{0,1},{1,0},{2,3},{3,2},{4,5},{5,4},{6,7},{7,6},{8,9},{9,8},{10,11... | collective-permute-start | bytes 344072 | tf_op jit(solution)/shard_map/ppermute | solution.py:11
  33.5 8.0 %collective-permute-start.14 = (bf16[32,896]{1,0:T(8,128)(2,1)S(1)}, bf16[32,896]{1,0:T(8,128)(2,1)S(1)}, u32[]{:S(2)}, u32[]{:S(2)}) collective-permute-start(bf16[32,896]{1,0:T(8,128)(2,1)S(1)} %get-tuple-element.78), channel_id=1, source_target_pairs={{0,6},{1,7},{2,4},{3,5},{4,2},{5,3},{6,0},{7,1},{8,14},{9,15},{10,... | collective-permute-start | bytes 172040 | tf_op jit(solution)/shard_map/ppermute | solution.py:11
  36.0 6.2 %collective-permute-start.15 = (bf16[32,896]{1,0:T(8,128)(2,1)S(1)}, bf16[32,896]{1,0:T(8,128)(2,1)S(1)}, u32[]{:S(2)}, u32[]{:S(2)}) collective-permute-start(bf16[32,896]{1,0:T(8,128)(2,1)S(1)} %get-tuple-element.77), channel_id=1, source_target_pairs={{0,4},{1,5},{2,6},{3,7},{4,0},{5,1},{6,2},{7,3},{8,12},{9,13},{10,... | collective-permute-start | bytes 172040 | tf_op jit(solution)/shard_map/ppermute | solution.py:11
  37.1 6.0 %collective-permute-start.11 = (bf16[16,896]{1,0:T(8,128)(2,1)S(1)}, bf16[16,896]{1,0:T(8,128)(2,1)S(1)}, u32[]{:S(2)}, u32[]{:S(2)}) collective-permute-start(bf16[16,896]{1,0:T(8,128)(2,1)S(1)} %get-tuple-element.86), channel_id=1, source_target_pairs={{0,6},{1,7},{2,4},{3,5},{4,2},{5,3},{6,0},{7,1},{8,14},{9,15},{10,... | collective-permute-start | bytes 86024 | tf_op jit(solution)/shard_map/ppermute | solution.py:11
  39.6 4.8 %collective-permute-start.12 = (bf16[16,896]{1,0:T(8,128)(2,1)S(1)}, bf16[16,896]{1,0:T(8,128)(2,1)S(1)}, u32[]{:S(2)}, u32[]{:S(2)}) collective-permute-start(bf16[16,896]{1,0:T(8,128)(2,1)S(1)} %get-tuple-element.85), channel_id=1, source_target_pairs={{0,4},{1,5},{2,6},{3,7},{4,0},{5,1},{6,2},{7,3},{8,12},{9,13},{10,... | collective-permute-start | bytes 86024 | tf_op jit(solution)/shard_map/ppermute | solution.py:11
  39.7 4.6 %collective-permute-start.13 = (bf16[16,896]{1,0:T(8,128)(2,1)S(1)}, bf16[16,896]{1,0:T(8,128)(2,1)S(1)}, u32[]{:S(2)}, u32[]{:S(2)}) collective-permute-start(bf16[16,896]{1,0:T(8,128)(2,1)S(1)} %get-tuple-element.84), channel_id=1, source_target_pairs={{0,2},{1,3},{2,0},{3,1},{4,6},{5,7},{6,4},{7,5},{8,10},{9,11},{10,... | collective-permute-start | bytes 86024 | tf_op jit(solution)/shard_map/ppermute | solution.py:11
  41.5 4.2 %collective-permute-start.16 = (bf16[32,896]{1,0:T(8,128)(2,1)S(1)}, bf16[32,896]{1,0:T(8,128)(2,1)S(1)}, u32[]{:S(2)}, u32[]{:S(2)}) collective-permute-start(bf16[32,896]{1,0:T(8,128)(2,1)S(1)} %get-tuple-element.49), channel_id=1, source_target_pairs={{0,2},{1,3},{2,0},{3,1},{4,6},{5,7},{6,4},{7,5},{8,10},{9,11},{10,... | collective-permute-start | bytes 172040 | tf_op jit(solution)/shard_map/ppermute | solution.py:11
  45.7 7.0 %collective-permute-start.23 = (bf16[16,896]{1,0:T(8,128)(2,1)S(1)}, bf16[16,896]{1,0:T(8,128)(2,1)S(1)}, u32[]{:S(2)}, u32[]{:S(2)}) collective-permute-start(bf16[16,896]{1,0:T(8,128)(2,1)S(1)} %subtract_convert_fusion), channel_id=1, source_target_pairs={{0,6},{1,7},{2,4},{3,5},{4,2},{5,3},{6,0},{7,1},{8,14},{9,15},{10,... | collective-permute-start | bytes 86024 | tf_op jit(solution)/shard_map/ppermute | solution.py:11
  48.3 6.4 %collective-permute-start.22 = (bf16[16,896]{1,0:T(8,128)(2,1)S(1)}, bf16[16,896]{1,0:T(8,128)(2,1)S(1)}, u32[]{:S(2)}, u32[]{:S(2)}) collective-permute-start(bf16[16,896]{1,0:T(8,128)(2,1)S(1)} %subtract_convert_fusion), channel_id=1, source_target_pairs={{0,4},{1,5},{2,6},{3,7},{4,0},{5,1},{6,2},{7,3},{8,12},{9,13},{10,... | collective-permute-start | bytes 86024 | tf_op jit(solution)/shard_map/ppermute | solution.py:11
  48.3 6.4 %collective-permute-start.21 = (bf16[16,896]{1,0:T(8,128)(2,1)S(1)}, bf16[16,896]{1,0:T(8,128)(2,1)S(1)}, u32[]{:S(2)}, u32[]{:S(2)}) collective-permute-start(bf16[16,896]{1,0:T(8,128)(2,1)S(1)} %subtract_convert_fusion), channel_id=1, source_target_pairs={{0,2},{1,3},{2,0},{3,1},{4,6},{5,7},{6,4},{7,5},{8,10},{9,11},{10,... | collective-permute-start | bytes 86024 | tf_op jit(solution)/shard_map/ppermute | solution.py:11
  50.2 6.0 %collective-permute-start.20 = (bf16[32,896]{1,0:T(8,128)(2,1)S(1)}, bf16[32,896]{1,0:T(8,128)(2,1)S(1)}, u32[]{:S(2)}, u32[]{:S(2)}) collective-permute-start(bf16[32,896]{1,0:T(8,128)(2,1)S(1)} %fusion.21), channel_id=1, source_target_pairs={{0,6},{1,7},{2,4},{3,5},{4,2},{5,3},{6,0},{7,1},{8,14},{9,15},{10,... | collective-permute-start | bytes 172040 | tf_op jit(solution)/shard_map/ppermute | solution.py:11
  52.8 5.1 %collective-permute-start.19 = (bf16[32,896]{1,0:T(8,128)(2,1)S(1)}, bf16[32,896]{1,0:T(8,128)(2,1)S(1)}, u32[]{:S(2)}, u32[]{:S(2)}) collective-permute-start(bf16[32,896]{1,0:T(8,128)(2,1)S(1)} %fusion.21), channel_id=1, source_target_pairs={{0,4},{1,5},{2,6},{3,7},{4,0},{5,1},{6,2},{7,3},{8,12},{9,13},{10,... | collective-permute-start | bytes 172040 | tf_op jit(solution)/shard_map/ppermute | solution.py:11
  52.8 5.1 %collective-permute-start.18 = (bf16[32,896]{1,0:T(8,128)(2,1)S(1)}, bf16[32,896]{1,0:T(8,128)(2,1)S(1)}, u32[]{:S(2)}, u32[]{:S(2)}) collective-permute-start(bf16[32,896]{1,0:T(8,128)(2,1)S(1)} %fusion.21), channel_id=1, source_target_pairs={{0,2},{1,3},{2,0},{3,1},{4,6},{5,7},{6,4},{7,5},{8,10},{9,11},{10,... | collective-permute-start | bytes 172040 | tf_op jit(solution)/shard_map/ppermute | solution.py:11
  54.7 4.9 %collective-permute-start.24 = (bf16[64,896]{1,0:T(8,128)(2,1)S(1)}, bf16[64,896]{1,0:T(8,128)(2,1)S(1)}, u32[]{:S(2)}, u32[]{:S(2)}) collective-permute-start(bf16[64,896]{1,0:T(8,128)(2,1)S(1)} %pad_maximum_fusion.5), channel_id=1, source_target_pairs={{0,1},{1,0},{2,3},{3,2},{4,5},{5,4},{6,7},{7,6},{8,9},{9,8},{10,11... | collective-permute-start | bytes 344072 | tf_op jit(solution)/shard_map/ppermute | solution.py:11
  60.6 1.5 %collective-permute-start.25 = (f32[384,128]{1,0:T(8,128)S(1)}, f32[384,128]{1,0:T(8,128)S(1)}, u32[]{:S(2)}, u32[]{:S(2)}) collective-permute-start(f32[384,128]{1,0:T(8,128)S(1)} %slice_select_fusion), channel_id=1, source_target_pairs={{0,8},{8,0},{16,24},{24,16},{1,9},{9,1},{17,25},{25,17},{2,10},{10... | collective-permute-start | bytes 589832 | tf_op jit(solution)/shard_map/ppermute | solution.py:11
  60.7 8.2 %collective-permute-start.28 = (bf16[128,1792]{1,0:T(8,128)(2,1)S(1)}, bf16[128,1792]{1,0:T(8,128)(2,1)S(1)}, u32[]{:S(2)}, u32[]{:S(2)}) collective-permute-start(bf16[128,1792]{1,0:T(8,128)(2,1)S(1)} %constant_dynamic-update-slice_fusion), channel_id=1, source_target_pairs={{0,8},{8,0},{16,24},{24,16},{1,9},{9,1},{17,25},{25,17},{2,10},{10... | collective-permute-start | bytes 1376264 | tf_op jit(solution)/shard_map/ppermute | solution.py:11
  62.2 4.3 %collective-permute-start.27 = (bf16[240,128]{1,0:T(8,128)(2,1)S(1)}, bf16[240,128]{1,0:T(8,128)(2,1)S(1)}, u32[]{:S(2)}, u32[]{:S(2)}) collective-permute-start(bf16[240,128]{1,0:T(8,128)(2,1)S(1)} %constant_dynamic-update-slice_fusion.19), channel_id=1, source_target_pairs={{0,16},{8,24},{16,0},{24,8},{1,17},{9,25},{17,1},{25,9},{2,18},{10... | collective-permute-start | bytes 184328 | tf_op jit(solution)/shard_map/ppermute | solution.py:11
  63.3 4.3 %collective-permute-start.26 = (bf16[240,128]{1,0:T(8,128)(2,1)S(1)}, bf16[240,128]{1,0:T(8,128)(2,1)S(1)}, u32[]{:S(2)}, u32[]{:S(2)}) collective-permute-start(bf16[240,128]{1,0:T(8,128)(2,1)S(1)} %constant_dynamic-update-slice_fusion.4), channel_id=1, source_target_pairs={{0,1},{1,0},{2,3},{3,2},{4,5},{5,4},{6,7},{7,6},{8,9},{9,8},{10,11... | collective-permute-start | bytes 184328 | tf_op jit(solution)/shard_map/ppermute | solution.py:11

commit v11 on v8

--- a/solution.py
+++ b/solution.py
@@ -76,10 +76,12 @@
             out[k] = crossed(block, "latent", 2 * k)
         return out
 
-    def sent_along_z(total):
+    def pieces_of(total):
         count = total.shape[0] // far
-        pieces = [total[k * count:(k + 1) * count].astype(BF16) for k in range(1, far)]
-        return [crossed(pieces[k - 1], "latent", 2 * k) for k in range(1, far)] + [total[:count]]
+        return [total[k * count:(k + 1) * count].astype(BF16) for k in range(1, far)] + [total[:count]]
+
+    def sent_along_z(pieces):
+        return [crossed(pieces[k - 1], "latent", 2 * k) for k in range(1, far)] + pieces[far - 1:]
 
     def added(terms):
         return sum(term.astype(F32) for term in terms[::-1])
@@ -130,9 +132,10 @@
     staying = times(rows_at(acts, 0), shared_mine) + times(rows_at(acts_y, 0), shared_other)
     arrived = over_x(leaving.astype(BF16))
     product = times(acts, own_mine) + times(acts_x, own_other)
-    arrived, staying = hold((arrived, staying))
-    own_terms = sent_along_z(product)
-    shared_terms = sent_along_z(staying + arrived.astype(F32))
+    own_pieces = pieces_of(product)
+    arrived, staying, own_pieces[0] = hold((arrived, staying, own_pieces[0]))
+    own_terms = sent_along_z(own_pieces)
+    shared_terms = sent_along_z(pieces_of(staying + arrived.astype(F32)))
     terms = hold((*shared_terms, *own_terms))
     shared_terms, own_terms = terms[:far], terms[far:]
     err_own = (added(own_terms) - paired(aim_own(side), aim_other).astype(F32)).astype(BF16)

time: 68.7 us -> 68.3 us (level)
  waiting for transfers between devices: 19.7 us -> 18.9 us
    ppermute x29, waiting for transfers between devices: 19.7 us -> 18.9 us  [crossed(): lax.ppermute(block, axis, [(i, i ^ mask) for i in range(lax.axis_size(axi...]
  transfers between devices with their start and end apart: 29 -> 29, of which waited for: 12 -> 13; matrix products, arithmetic and copies ran while one was open for 11% -> 11% of each run, Pallas kernels for 0% -> 0%
where the time goes in v11:
time: 68.3 us; the launch traced here: 68 us
  starting transfers between devices  35.4 us (52%)
  waiting for transfers between devices  18.9 us (28%)
  matrix products  4.17 us (6%)
  local copies, waits for them, and re-layouts  3.97 us (6%)
  other arithmetic  3.16 us (5%)
  between operations  2.41 us (4%)
    ppermute x29, starting transfers between devices, crossed(): lax.ppermute(block, axis, [(i, i ^ mask) for i in range(lax.axis_size(axi...  35.4 us
    ppermute x29, waiting for transfers between devices, crossed(): lax.ppermute(block, axis, [(i, i ^ mask) for i in range(lax.axis_size(axi...  18.9 us
    squeeze x1, local copies, waits for them, and re-layouts, decoder_part(): lax.dynamic_slice(decoder, (which, 0, where * part), (1, 2 * latents, part))  2.01 us
    dot_general x7, matrix products, times(): return jnp.dot(left, right, preferred_element_type=F32)  1.61 us
    another operation x2, local copies, waits for them, and re-layouts, paired(): block.reshape(-1, 1, rows, block.shape[1])  1.6 us
  transfers between devices with their start and end apart: 29, of which 13 were waited for; matrix products, arithmetic and copies ran while one was open for 11% of the time, Pallas kernels for 0%

profile of v11, /device:TPU:0, one launch (start us, length us, event | category | flops | bytes accessed | tf_op | source)
XLA Modules:
  0.0 68.0 jit_solution(7647246230518736693)
XLA Ops:
  0.6 0.5 collective-permute-start.3
  1.2 0.8 %dynamic-slice_bitcast_fusion.3 = (bf16[1,1,16,1792]{3,2,1,0:T(8,128)(2,1)S(1)}, bf16[16,1792]{1,0:T(8,128)(2,1)S(1)}) fusion(bf16[2,16,3584]{2,1,0:T(8,128)(2,1)} %param.6, s32[]{:T(128)S(6)} %select_n.156, s32[]{:T(128)S(6)} %select_n.161), kind=kLoop, calls=%fused_computation.89 | loop fusion | bytes 172040 | tf_op jit(solution)/shard_map/reshape;squeeze | solution.py:99
  2.0 2.6 %collective-permute-start.2 = (bf16[16,1792]{1,0:T(8,128)(2,1)S(1)}, bf16[16,1792]{1,0:T(8,128)(2,1)S(1)}, u32[]{:S(2)}, u32[]{:S(2)}) collective-permute-start(bf16[16,1792]{1,0:T(8,128)(2,1)S(1)} %get-tuple-element.69), channel_id=1, source_target_pairs={{0,1},{1,0},{2,3},{3,2},{4,5},{5,4},{6,7},{7,6},{8,9},{9,8},{10,11... | collective-permute-start | bytes 172040 | tf_op jit(solution)/shard_map/ppermute | solution.py:11
  4.6 2.0 %dynamic-slice_bitcast_fusion = (bf16[256,896]{1,0:T(8,128)(2,1)}, bf16[256,896]{1,0:T(8,128)(2,1)S(1)}) fusion(bf16[2,256,1792]{2,1,0:T(8,128)(2,1)} %bitcast.117, s32[]{:T(128)S(6)} %select_n.158, s32[]{:T(128)S(6)} %select_n.159, s32[]{:T(128)S(6)} %select_n.156, s32[]{:T(128)S(6)} %select_n.157), kind=kLoop, calls=%fused_computation.24 | loop fusion | bytes 1835024 | tf_op jit(solution)/shard_map/squeeze | solution.py:90
  6.6 1.5 %collective-permute-start.1 = (bf16[256,896]{1,0:T(8,128)(2,1)}, bf16[256,896]{1,0:T(8,128)(2,1)S(1)}, u32[]{:S(2)}, u32[]{:S(2)}) collective-permute-start(bf16[256,896]{1,0:T(8,128)(2,1)} %get-tuple-element.59), channel_id=1, source_target_pairs={{0,16},{8,24},{16,0},{24,8},{1,17},{9,25},{17,1},{25,9},{2,18},{10... | collective-permute-start | bytes 1376264 | tf_op jit(solution)/shard_map/ppermute | solution.py:11
  8.2 0.5 collective-permute-start
  8.7 3.7 %collective-permute-start.6 = (bf16[32,1792]{1,0:T(8,128)(2,1)S(1)}, bf16[32,1792]{1,0:T(8,128)(2,1)S(1)}, u32[]{:S(2)}, u32[]{:S(2)}) collective-permute-start(bf16[32,1792]{1,0:T(8,128)(2,1)S(1)} %bitcast.128), channel_id=1, source_target_pairs={{0,6},{1,7},{2,4},{3,5},{4,2},{5,3},{6,0},{7,1},{8,14},{9,15},{10,... | collective-permute-start | bytes 344072 | tf_op jit(solution)/shard_map/ppermute | solution.py:11
  12.4 0.8 %collective-permute-start.4 = (bf16[32,1792]{1,0:T(8,128)(2,1)S(1)}, bf16[32,1792]{1,0:T(8,128)(2,1)S(1)}, u32[]{:S(2)}, u32[]{:S(2)}) collective-permute-start(bf16[32,1792]{1,0:T(8,128)(2,1)S(1)} %bitcast.130), channel_id=1, source_target_pairs={{0,2},{1,3},{2,0},{3,1},{4,6},{5,7},{6,4},{7,5},{8,10},{9,11},{10,... | collective-permute-start | bytes 344072 | tf_op jit(solution)/shard_map/ppermute | solution.py:11
  13.2 0.2 bitcast_select_fusion.1
  13.4 0.0 copy-start.3
  13.4 5.9 %collective-permute-done.1 = bf16[256,896]{1,0:T(8,128)(2,1)S(1)} collective-permute-done((bf16[256,896]{1,0:T(8,128)(2,1)}, bf16[256,896]{1,0:T(8,128)(2,1)S(1)}, u32[]{:S(2)}, u32[]{:S(2)}) %collective-permute-start.1) | collective-permute-done | bytes 458784 | tf_op jit(solution)/shard_map/ppermute | solution.py:11
  19.3 1.0 %collective-permute-done = bf16[256,896]{1,0:T(8,128)(2,1)S(1)} collective-permute-done((bf16[256,896]{1,0:T(8,128)(2,1)S(1)}, bf16[256,896]{1,0:T(8,128)(2,1)S(1)}, u32[]{:S(2)}, u32[]{:S(2)}) %collective-permute-start) | collective-permute-done | bytes 458784 | tf_op jit(solution)/shard_map/ppermute | solution.py:11
  20.4 1.4 %collective-permute-done.5 = bf16[32,1792]{1,0:T(8,128)(2,1)S(1)} collective-permute-done((bf16[32,1792]{1,0:T(8,128)(2,1)S(1)}, bf16[32,1792]{1,0:T(8,128)(2,1)S(1)}, u32[]{:S(2)}, u32[]{:S(2)}) %collective-permute-start.5) | collective-permute-done | bytes 114720 | tf_op jit(solution)/shard_map/ppermute | solution.py:11
  21.8 0.3 convolution_add_fusion.4
  22.1 0.1 collective-permute-start.7
  22.3 0.6 compare_reduce_fusion
  24.3 0.6 collective-permute-start.8
  24.9 1.6 %collective-permute-start.10 = (bf16[128,256]{1,0:T(8,128)(2,1)S(1)}, bf16[128,256]{1,0:T(8,128)(2,1)S(1)}, u32[]{:S(2)}, u32[]{:S(2)}) collective-permute-start(bf16[128,256]{1,0:T(8,128)(2,1)S(1)} %bitcast.141), channel_id=1, source_target_pairs={{0,1},{1,0},{2,3},{3,2},{4,5},{5,4},{6,7},{7,6},{8,9},{9,8},{10,11... | collective-permute-start | bytes 196616 | tf_op jit(solution)/shard_map/ppermute | solution.py:11
  26.4 0.8 %dynamic-slice_bitcast_fusion.5 = (bf16[1,1,16,896]{3,2,1,0:T(8,128)(2,1)S(1)}, bf16[16,896]{1,0:T(8,128)(2,1)S(1)}) fusion(bf16[3,16,3584]{2,1,0:T(8,128)(2,1)} %param.7, s32[]{:T(128)S(6)} %select_n.170, s32[]{:T(128)S(6)} %select_n.171, s32[]{:T(128)S(6)} %select_n.172), kind=kLoop, calls=%fused_computation.97 | loop fusion | bytes 114700 | tf_op jit(solution)/shard_map/reshape;squeeze | solution.py:99
  27.2 0.5 collective-permute-start.17
  27.7 0.2 fusion.14
  27.9 0.2 fusion.12
  28.1 0.6 collective-permute-done.8
  28.8 0.2 fusion.1
  29.0 1.6 %collective-permute-start.9 = (bf16[64,896]{1,0:T(8,128)(2,1)S(1)}, bf16[64,896]{1,0:T(8,128)(2,1)S(1)}, u32[]{:S(2)}, u32[]{:S(2)}) collective-permute-start(bf16[64,896]{1,0:T(8,128)(2,1)S(1)} %fusion.1), channel_id=1, source_target_pairs={{0,1},{1,0},{2,3},{3,2},{4,5},{5,4},{6,7},{7,6},{8,9},{9,8},{10,11... | collective-permute-start | bytes 344072 | tf_op jit(solution)/shard_map/ppermute | solution.py:11
  30.6 0.2 fusion.46
  30.8 0.2 fusion.45
  31.1 2.5 %collective-permute-start.16 = (bf16[32,896]{1,0:T(8,128)(2,1)S(1)}, bf16[32,896]{1,0:T(8,128)(2,1)S(1)}, u32[]{:S(2)}, u32[]{:S(2)}) collective-permute-start(bf16[32,896]{1,0:T(8,128)(2,1)S(1)} %get-tuple-element.65), channel_id=1, source_target_pairs={{0,6},{1,7},{2,4},{3,5},{4,2},{5,3},{6,0},{7,1},{8,14},{9,15},{10,... | collective-permute-start | bytes 172040 | tf_op jit(solution)/shard_map/ppermute | solution.py:11
  33.6 0.2 convolution_add_fusion.1
  33.8 0.0 collective-permute-done.9
  33.9 2.5 %collective-permute-start.13 = (bf16[16,896]{1,0:T(8,128)(2,1)S(1)}, bf16[16,896]{1,0:T(8,128)(2,1)S(1)}, u32[]{:S(2)}, u32[]{:S(2)}) collective-permute-start(bf16[16,896]{1,0:T(8,128)(2,1)S(1)} %get-tuple-element.72), channel_id=1, source_target_pairs={{0,6},{1,7},{2,4},{3,5},{4,2},{5,3},{6,0},{7,1},{8,14},{9,15},{10,... | collective-permute-start | bytes 86024 | tf_op jit(solution)/shard_map/ppermute | solution.py:11
  36.4 0.9 %collective-permute-start.12 = (bf16[16,896]{1,0:T(8,128)(2,1)S(1)}, bf16[16,896]{1,0:T(8,128)(2,1)S(1)}, u32[]{:S(2)}, u32[]{:S(2)}) collective-permute-start(bf16[16,896]{1,0:T(8,128)(2,1)S(1)} %get-tuple-element.73), channel_id=1, source_target_pairs={{0,4},{1,5},{2,6},{3,7},{4,0},{5,1},{6,2},{7,3},{8,12},{9,13},{10,... | collective-permute-start | bytes 86024 | tf_op jit(solution)/shard_map/ppermute | solution.py:11
  37.3 1.0 %collective-permute-start.11 = (bf16[16,896]{1,0:T(8,128)(2,1)S(1)}, bf16[16,896]{1,0:T(8,128)(2,1)S(1)}, u32[]{:S(2)}, u32[]{:S(2)}) collective-permute-start(bf16[16,896]{1,0:T(8,128)(2,1)S(1)} %get-tuple-element.74), channel_id=1, source_target_pairs={{0,2},{1,3},{2,0},{3,1},{4,6},{5,7},{6,4},{7,5},{8,10},{9,11},{10,... | collective-permute-start | bytes 86024 | tf_op jit(solution)/shard_map/ppermute | solution.py:11
  38.4 1.0 %collective-permute-start.14 = (bf16[32,896]{1,0:T(8,128)(2,1)S(1)}, bf16[32,896]{1,0:T(8,128)(2,1)S(1)}, u32[]{:S(2)}, u32[]{:S(2)}) collective-permute-start(bf16[32,896]{1,0:T(8,128)(2,1)S(1)} %get-tuple-element.40), channel_id=1, source_target_pairs={{0,2},{1,3},{2,0},{3,1},{4,6},{5,7},{6,4},{7,5},{8,10},{9,11},{10,... | collective-permute-start | bytes 172040 | tf_op jit(solution)/shard_map/ppermute | solution.py:11
  39.4 0.5 collective-permute-done.15
  39.9 0.0 collective-permute-done.13
  39.9 1.3 %collective-permute-done.12 = bf16[16,896]{1,0:T(8,128)(2,1)S(1)} collective-permute-done((bf16[16,896]{1,0:T(8,128)(2,1)S(1)}, bf16[16,896]{1,0:T(8,128)(2,1)S(1)}, u32[]{:S(2)}, u32[]{:S(2)}) %collective-permute-start.12) | collective-permute-done | bytes 28704 | tf_op jit(solution)/shard_map/ppermute | solution.py:11
  41.3 0.3 collective-permute-done.11
  41.5 1.0 %collective-permute-done.14 = bf16[32,896]{1,0:T(8,128)(2,1)S(1)} collective-permute-done((bf16[32,896]{1,0:T(8,128)(2,1)S(1)}, bf16[32,896]{1,0:T(8,128)(2,1)S(1)}, u32[]{:S(2)}, u32[]{:S(2)}) %collective-permute-start.14) | collective-permute-done | bytes 57376 | tf_op jit(solution)/shard_map/ppermute | solution.py:11
  42.5 0.8 %fusion.24 = bf16[16,896]{1,0:T(8,128)(2,1)S(1)} fusion(bf16[16,896]{1,0:T(8,128)(2,1)S(1)} %collective-permute-done.11, bf16[16,896]{1,0:T(8,128)(2,1)S(1)} %collective-permute-done.12, f32[16,896]{1,0:T(8,128)S(1)} %slice.252, bf16[16,896]{1,0:T(8,128)(2,1)S(1)} %collective-permute-done.13, bf16[3,16,3584]{2,1,0:T(8,128)(2,1)} %param.7, s32[]{:T(128)S(6)} %select_n.174), kind=kLoop, calls=%fused_computation.87 | loop fusion | flops 129024 | bytes 200708 | tf_op jit(solution)/shard_map/convert_element_type | solution.py:143
  43.3 2.5 %collective-permute-start.23 = (bf16[16,896]{1,0:T(8,128)(2,1)S(1)}, bf16[16,896]{1,0:T(8,128)(2,1)S(1)}, u32[]{:S(2)}, u32[]{:S(2)}) collective-permute-start(bf16[16,896]{1,0:T(8,128)(2,1)S(1)} %fusion.24), channel_id=1, source_target_pairs={{0,6},{1,7},{2,4},{3,5},{4,2},{5,3},{6,0},{7,1},{8,14},{9,15},{10,... | collective-permute-start | bytes 86024 | tf_op jit(solution)/shard_map/ppermute | solution.py:11
  45.9 1.9 %collective-permute-start.21 = (bf16[16,896]{1,0:T(8,128)(2,1)S(1)}, bf16[16,896]{1,0:T(8,128)(2,1)S(1)}, u32[]{:S(2)}, u32[]{:S(2)}) collective-permute-start(bf16[16,896]{1,0:T(8,128)(2,1)S(1)} %fusion.24), channel_id=1, source_target_pairs={{0,2},{1,3},{2,0},{3,1},{4,6},{5,7},{6,4},{7,5},{8,10},{9,11},{10,... | collective-permute-start | bytes 86024 | tf_op jit(solution)/shard_map/ppermute | solution.py:11
  47.8 2.5 %collective-permute-start.20 = (bf16[32,896]{1,0:T(8,128)(2,1)S(1)}, bf16[32,896]{1,0:T(8,128)(2,1)S(1)}, u32[]{:S(2)}, u32[]{:S(2)}) collective-permute-start(bf16[32,896]{1,0:T(8,128)(2,1)S(1)} %fusion.21), channel_id=1, source_target_pairs={{0,6},{1,7},{2,4},{3,5},{4,2},{5,3},{6,0},{7,1},{8,14},{9,15},{10,... | collective-permute-start | bytes 172040 | tf_op jit(solution)/shard_map/ppermute | solution.py:11
  50.4 1.9 %collective-permute-start.18 = (bf16[32,896]{1,0:T(8,128)(2,1)S(1)}, bf16[32,896]{1,0:T(8,128)(2,1)S(1)}, u32[]{:S(2)}, u32[]{:S(2)}) collective-permute-start(bf16[32,896]{1,0:T(8,128)(2,1)S(1)} %fusion.21), channel_id=1, source_target_pairs={{0,2},{1,3},{2,0},{3,1},{4,6},{5,7},{6,4},{7,5},{8,10},{9,11},{10,... | collective-permute-start | bytes 172040 | tf_op jit(solution)/shard_map/ppermute | solution.py:11
  52.3 1.6 %collective-permute-start.24 = (bf16[64,896]{1,0:T(8,128)(2,1)S(1)}, bf16[64,896]{1,0:T(8,128)(2,1)S(1)}, u32[]{:S(2)}, u32[]{:S(2)}) collective-permute-start(bf16[64,896]{1,0:T(8,128)(2,1)S(1)} %pad_maximum_fusion.5), channel_id=1, source_target_pairs={{0,1},{1,0},{2,3},{3,2},{4,5},{5,4},{6,7},{7,6},{8,9},{9,8},{10,11... | collective-permute-start | bytes 344072 | tf_op jit(solution)/shard_map/ppermute | solution.py:11
  53.9 0.0 collective-permute-done.20
  53.9 1.6 %collective-permute-done.19 = bf16[32,896]{1,0:T(8,128)(2,1)S(1)} collective-permute-done((bf16[32,896]{1,0:T(8,128)(2,1)S(1)}, bf16[32,896]{1,0:T(8,128)(2,1)S(1)}, u32[]{:S(2)}, u32[]{:S(2)}) %collective-permute-start.19) | collective-permute-done | bytes 57376 | tf_op jit(solution)/shard_map/ppermute | solution.py:11
  55.4 0.3 fusion.25
  55.8 1.4 %collective-permute-done.24 = bf16[64,896]{1,0:T(8,128)(2,1)S(1)} collective-permute-done((bf16[64,896]{1,0:T(8,128)(2,1)S(1)}, bf16[64,896]{1,0:T(8,128)(2,1)S(1)}, u32[]{:S(2)}, u32[]{:S(2)}) %collective-permute-start.24) | collective-permute-done | bytes 114720 | tf_op jit(solution)/shard_map/ppermute | solution.py:11
  57.2 0.3 fusion.47
  57.5 0.3 fusion.10
  57.8 0.3 convolution_add_fusion.3
  58.2 0.1 collective-permute-start.25
  58.3 0.5 collective-permute-start.28
  58.8 0.9 %collective-permute-done.25 = f32[384,128]{1,0:T(8,128)S(1)} collective-permute-done((f32[384,128]{1,0:T(8,128)S(1)}, f32[384,128]{1,0:T(8,128)S(1)}, u32[]{:S(2)}, u32[]{:S(2)}) %collective-permute-start.25) | collective-permute-done | bytes 196640 | tf_op jit(solution)/shard_map/ppermute | solution.py:11
  59.7 0.1 fusion.38
  59.9 1.1 %collective-permute-start.27 = (bf16[240,128]{1,0:T(8,128)(2,1)S(1)}, bf16[240,128]{1,0:T(8,128)(2,1)S(1)}, u32[]{:S(2)}, u32[]{:S(2)}) collective-permute-start(bf16[240,128]{1,0:T(8,128)(2,1)S(1)} %constant_dynamic-update-slice_fusion.19), channel_id=1, source_target_pairs={{0,16},{8,24},{16,0},{24,8},{1,17},{9,25},{17,1},{25,9},{2,18},{10... | collective-permute-start | bytes 184328 | tf_op jit(solution)/shard_map/ppermute | solution.py:11
  61.1 1.3 %collective-permute-start.26 = (bf16[240,128]{1,0:T(8,128)(2,1)S(1)}, bf16[240,128]{1,0:T(8,128)(2,1)S(1)}, u32[]{:S(2)}, u32[]{:S(2)}) collective-permute-start(bf16[240,128]{1,0:T(8,128)(2,1)S(1)} %constant_dynamic-update-slice_fusion.4), channel_id=1, source_target_pairs={{0,1},{1,0},{2,3},{3,2},{4,5},{5,4},{6,7},{7,6},{8,9},{9,8},{10,11... | collective-permute-start | bytes 184328 | tf_op jit(solution)/shard_map/ppermute | solution.py:11
  62.4 1.8 %collective-permute-done.27 = bf16[240,128]{1,0:T(8,128)(2,1)S(1)} collective-permute-done((bf16[240,128]{1,0:T(8,128)(2,1)S(1)}, bf16[240,128]{1,0:T(8,128)(2,1)S(1)}, u32[]{:S(2)}, u32[]{:S(2)}) %collective-permute-start.27) | collective-permute-done | bytes 61472 | tf_op jit(solution)/shard_map/ppermute | solution.py:11
  64.3 1.0 %collective-permute-done.26 = bf16[240,128]{1,0:T(8,128)(2,1)S(1)} collective-permute-done((bf16[240,128]{1,0:T(8,128)(2,1)S(1)}, bf16[240,128]{1,0:T(8,128)(2,1)S(1)}, u32[]{:S(2)}, u32[]{:S(2)}) %collective-permute-start.26) | collective-permute-done | bytes 61472 | tf_op jit(solution)/shard_map/ppermute | solution.py:11
  65.4 0.5 fusion.27
  65.9 0.6 maximum_select_fusion
  66.6 0.1 broadcast_select_fusion.1
  66.6 1.4 %fusion = bf16[1,3584,128]{2,1,0:T(8,128)(2,1)} fusion(bf16[128,1792]{1,0:T(8,128)(2,1)S(1)} %get-tuple-element.62, bf16[128,1792]{1,0:T(8,128)(2,1)S(1)} %get-tuple-element.61, f32[384,128]{1,0:T(8,128)S(1)} %get-tuple-element.54, bf16[240,128]{1,0:T(8,128)(2,1)S(1)} %collective-permute-done.27, bf16[240,128]{1,0:T(8,128)(2,1)S(1)} %collective-permute-done.26, ...), kind=kOutput, calls=%fused_computation.1 | convolution fusion | flops 119832576 | bytes 1966084 | tf_op jit(solution)/shard_map/dot_general | solution.py:48
  (81 shorter events, 0.7 us)
Async XLA Ops:
  0.6 12.5 %copy-start.1 = (bf16[1,3584,128]{2,1,0:T(8,128)(2,1)S(1)}, bf16[1,3584,128]{2,1,0:T(8,128)(2,1)}, u32[]{:S(2)}) copy-start(bf16[1,3584,128]{2,1,0:T(8,128)(2,1)} %param.8) | copy-start | bytes 2752516
  0.6 8.1 %collective-permute-start.3 = (bf16[3584,128]{1,0:T(8,128)(2,1)}, bf16[3584,128]{1,0:T(8,128)(2,1)S(1)}, u32[]{:S(2)}, u32[]{:S(2)}) collective-permute-start(bf16[3584,128]{1,0:T(8,128)(2,1)} %bitcast.136), channel_id=1, source_target_pairs={{0,8},{8,0},{16,24},{24,16},{1,9},{9,1},{17,25},{25,17},{2,10},{10... | collective-permute-start | bytes 2752520 | tf_op jit(solution)/shard_map/ppermute | solution.py:11
  2.0 6.7 %collective-permute-start.2 = (bf16[16,1792]{1,0:T(8,128)(2,1)S(1)}, bf16[16,1792]{1,0:T(8,128)(2,1)S(1)}, u32[]{:S(2)}, u32[]{:S(2)}) collective-permute-start(bf16[16,1792]{1,0:T(8,128)(2,1)S(1)} %get-tuple-element.69), channel_id=1, source_target_pairs={{0,1},{1,0},{2,3},{3,2},{4,5},{5,4},{6,7},{7,6},{8,9},{9,8},{10,11... | collective-permute-start | bytes 172040 | tf_op jit(solution)/shard_map/ppermute | solution.py:11
  4.6 8.7 %copy-start.2 = (f32[1,128]{1,0:T(1,128)S(1)}, f32[1,128]{1,0:T(1,128)}, u32[]{:S(2)}) copy-start(f32[1,128]{1,0:T(1,128)} %param.9) | copy-start | bytes 1540
  6.6 12.7 %collective-permute-start.1 = (bf16[256,896]{1,0:T(8,128)(2,1)}, bf16[256,896]{1,0:T(8,128)(2,1)S(1)}, u32[]{:S(2)}, u32[]{:S(2)}) collective-permute-start(bf16[256,896]{1,0:T(8,128)(2,1)} %get-tuple-element.59), channel_id=1, source_target_pairs={{0,16},{8,24},{16,0},{24,8},{1,17},{9,25},{17,1},{25,9},{2,18},{10... | collective-permute-start | bytes 1376264 | tf_op jit(solution)/shard_map/ppermute | solution.py:11
  8.2 12.2 %collective-permute-start = (bf16[256,896]{1,0:T(8,128)(2,1)S(1)}, bf16[256,896]{1,0:T(8,128)(2,1)S(1)}, u32[]{:S(2)}, u32[]{:S(2)}) collective-permute-start(bf16[256,896]{1,0:T(8,128)(2,1)S(1)} %get-tuple-element.60), channel_id=1, source_target_pairs={{0,1},{1,0},{2,3},{3,2},{4,5},{5,4},{6,7},{7,6},{8,9},{9,8},{10,11... | collective-permute-start | bytes 1376264 | tf_op jit(solution)/shard_map/ppermute | solution.py:11
  8.7 11.7 %collective-permute-start.6 = (bf16[32,1792]{1,0:T(8,128)(2,1)S(1)}, bf16[32,1792]{1,0:T(8,128)(2,1)S(1)}, u32[]{:S(2)}, u32[]{:S(2)}) collective-permute-start(bf16[32,1792]{1,0:T(8,128)(2,1)S(1)} %bitcast.128), channel_id=1, source_target_pairs={{0,6},{1,7},{2,4},{3,5},{4,2},{5,3},{6,0},{7,1},{8,14},{9,15},{10,... | collective-permute-start | bytes 344072 | tf_op jit(solution)/shard_map/ppermute | solution.py:11
  12.4 9.4 %collective-permute-start.5 = (bf16[32,1792]{1,0:T(8,128)(2,1)S(1)}, bf16[32,1792]{1,0:T(8,128)(2,1)S(1)}, u32[]{:S(2)}, u32[]{:S(2)}) collective-permute-start(bf16[32,1792]{1,0:T(8,128)(2,1)S(1)} %bitcast.129), channel_id=1, source_target_pairs={{0,4},{1,5},{2,6},{3,7},{4,0},{5,1},{6,2},{7,3},{8,12},{9,13},{10,... | collective-permute-start | bytes 344072 | tf_op jit(solution)/shard_map/ppermute | solution.py:11
  12.4 9.4 %collective-permute-start.4 = (bf16[32,1792]{1,0:T(8,128)(2,1)S(1)}, bf16[32,1792]{1,0:T(8,128)(2,1)S(1)}, u32[]{:S(2)}, u32[]{:S(2)}) collective-permute-start(bf16[32,1792]{1,0:T(8,128)(2,1)S(1)} %bitcast.130), channel_id=1, source_target_pairs={{0,2},{1,3},{2,0},{3,1},{4,6},{5,7},{6,4},{7,5},{8,10},{9,11},{10,... | collective-permute-start | bytes 344072 | tf_op jit(solution)/shard_map/ppermute | solution.py:11
  13.4 8.9 %copy-start.3 = (s32[2,1,12]{2,1,0:T(1,128)S(1)}, s32[2,1,12]{2,1,0:T(1,128)}, u32[]{:S(2)}) copy-start(s32[2,1,12]{2,1,0:T(1,128)} %param.11) | copy-start | bytes 292
  13.4 14.3 %copy-start = (bf16[1,2,2,128,1792]{4,3,2,1,0:T(8,128)(2,1)S(1)}, bf16[1,2,2,128,1792]{4,3,2,1,0:T(8,128)(2,1)}, u32[]{:S(2)}) copy-start(bf16[1,2,2,128,1792]{4,3,2,1,0:T(8,128)(2,1)} %param.10) | copy-start | bytes 5505028
  22.1 2.1 %collective-permute-start.7 = (f32[128,256]{1,0:T(8,128)S(1)}, f32[128,256]{1,0:T(8,128)S(1)}, u32[]{:S(2)}, u32[]{:S(2)}) collective-permute-start(f32[128,256]{1,0:T(8,128)S(1)} %convolution_add_fusion.4), channel_id=1, source_target_pairs={{0,8},{8,0},{16,24},{24,16},{1,9},{9,1},{17,25},{25,17},{2,10},{10... | collective-permute-start | bytes 393224 | tf_op jit(solution)/shard_map/ppermute | solution.py:11
  24.3 4.5 %collective-permute-start.8 = (bf16[128,256]{1,0:T(8,128)(2,1)S(1)}, bf16[128,256]{1,0:T(8,128)(2,1)S(1)}, u32[]{:S(2)}, u32[]{:S(2)}) collective-permute-start(bf16[128,256]{1,0:T(8,128)(2,1)S(1)} %multiply_convert_fusion), channel_id=1, source_target_pairs={{0,16},{8,24},{16,0},{24,8},{1,17},{9,25},{17,1},{25,9},{2,18},{10... | collective-permute-start | bytes 196616 | tf_op jit(solution)/shard_map/ppermute | solution.py:11
  24.9 5.7 %collective-permute-start.10 = (bf16[128,256]{1,0:T(8,128)(2,1)S(1)}, bf16[128,256]{1,0:T(8,128)(2,1)S(1)}, u32[]{:S(2)}, u32[]{:S(2)}) collective-permute-start(bf16[128,256]{1,0:T(8,128)(2,1)S(1)} %bitcast.141), channel_id=1, source_target_pairs={{0,1},{1,0},{2,3},{3,2},{4,5},{5,4},{6,7},{7,6},{8,9},{9,8},{10,11... | collective-permute-start | bytes 196616 | tf_op jit(solution)/shard_map/ppermute | solution.py:11
  27.2 10.1 %collective-permute-start.17 = (bf16[16,896]{1,0:T(8,128)(2,1)S(1)}, bf16[16,896]{1,0:T(8,128)(2,1)S(1)}, u32[]{:S(2)}, u32[]{:S(2)}) collective-permute-start(bf16[16,896]{1,0:T(8,128)(2,1)S(1)} %get-tuple-element.64), channel_id=1, source_target_pairs={{0,1},{1,0},{2,3},{3,2},{4,5},{5,4},{6,7},{7,6},{8,9},{9,8},{10,11... | collective-permute-start | bytes 86024 | tf_op jit(solution)/shard_map/ppermute | solution.py:11
  29.0 4.9 %collective-permute-start.9 = (bf16[64,896]{1,0:T(8,128)(2,1)S(1)}, bf16[64,896]{1,0:T(8,128)(2,1)S(1)}, u32[]{:S(2)}, u32[]{:S(2)}) collective-permute-start(bf16[64,896]{1,0:T(8,128)(2,1)S(1)} %fusion.1), channel_id=1, source_target_pairs={{0,1},{1,0},{2,3},{3,2},{4,5},{5,4},{6,7},{7,6},{8,9},{9,8},{10,11... | collective-permute-start | bytes 344072 | tf_op jit(solution)/shard_map/ppermute | solution.py:11
  31.1 7.3 %collective-permute-start.16 = (bf16[32,896]{1,0:T(8,128)(2,1)S(1)}, bf16[32,896]{1,0:T(8,128)(2,1)S(1)}, u32[]{:S(2)}, u32[]{:S(2)}) collective-permute-start(bf16[32,896]{1,0:T(8,128)(2,1)S(1)} %get-tuple-element.65), channel_id=1, source_target_pairs={{0,6},{1,7},{2,4},{3,5},{4,2},{5,3},{6,0},{7,1},{8,14},{9,15},{10,... | collective-permute-start | bytes 172040 | tf_op jit(solution)/shard_map/ppermute | solution.py:11
  33.6 6.3 %collective-permute-start.15 = (bf16[32,896]{1,0:T(8,128)(2,1)S(1)}, bf16[32,896]{1,0:T(8,128)(2,1)S(1)}, u32[]{:S(2)}, u32[]{:S(2)}) collective-permute-start(bf16[32,896]{1,0:T(8,128)(2,1)S(1)} %get-tuple-element.66), channel_id=1, source_target_pairs={{0,4},{1,5},{2,6},{3,7},{4,0},{5,1},{6,2},{7,3},{8,12},{9,13},{10,... | collective-permute-start | bytes 172040 | tf_op jit(solution)/shard_map/ppermute | solution.py:11
  33.9 6.0 %collective-permute-start.13 = (bf16[16,896]{1,0:T(8,128)(2,1)S(1)}, bf16[16,896]{1,0:T(8,128)(2,1)S(1)}, u32[]{:S(2)}, u32[]{:S(2)}) collective-permute-start(bf16[16,896]{1,0:T(8,128)(2,1)S(1)} %get-tuple-element.72), channel_id=1, source_target_pairs={{0,6},{1,7},{2,4},{3,5},{4,2},{5,3},{6,0},{7,1},{8,14},{9,15},{10,... | collective-permute-start | bytes 86024 | tf_op jit(solution)/shard_map/ppermute | solution.py:11
  36.4 4.8 %collective-permute-start.12 = (bf16[16,896]{1,0:T(8,128)(2,1)S(1)}, bf16[16,896]{1,0:T(8,128)(2,1)S(1)}, u32[]{:S(2)}, u32[]{:S(2)}) collective-permute-start(bf16[16,896]{1,0:T(8,128)(2,1)S(1)} %get-tuple-element.73), channel_id=1, source_target_pairs={{0,4},{1,5},{2,6},{3,7},{4,0},{5,1},{6,2},{7,3},{8,12},{9,13},{10,... | collective-permute-start | bytes 86024 | tf_op jit(solution)/shard_map/ppermute | solution.py:11
  37.3 4.2 %collective-permute-start.11 = (bf16[16,896]{1,0:T(8,128)(2,1)S(1)}, bf16[16,896]{1,0:T(8,128)(2,1)S(1)}, u32[]{:S(2)}, u32[]{:S(2)}) collective-permute-start(bf16[16,896]{1,0:T(8,128)(2,1)S(1)} %get-tuple-element.74), channel_id=1, source_target_pairs={{0,2},{1,3},{2,0},{3,1},{4,6},{5,7},{6,4},{7,5},{8,10},{9,11},{10,... | collective-permute-start | bytes 86024 | tf_op jit(solution)/shard_map/ppermute | solution.py:11
  38.4 4.2 %collective-permute-start.14 = (bf16[32,896]{1,0:T(8,128)(2,1)S(1)}, bf16[32,896]{1,0:T(8,128)(2,1)S(1)}, u32[]{:S(2)}, u32[]{:S(2)}) collective-permute-start(bf16[32,896]{1,0:T(8,128)(2,1)S(1)} %get-tuple-element.40), channel_id=1, source_target_pairs={{0,2},{1,3},{2,0},{3,1},{4,6},{5,7},{6,4},{7,5},{8,10},{9,11},{10,... | collective-permute-start | bytes 172040 | tf_op jit(solution)/shard_map/ppermute | solution.py:11
  43.3 7.0 %collective-permute-start.23 = (bf16[16,896]{1,0:T(8,128)(2,1)S(1)}, bf16[16,896]{1,0:T(8,128)(2,1)S(1)}, u32[]{:S(2)}, u32[]{:S(2)}) collective-permute-start(bf16[16,896]{1,0:T(8,128)(2,1)S(1)} %fusion.24), channel_id=1, source_target_pairs={{0,6},{1,7},{2,4},{3,5},{4,2},{5,3},{6,0},{7,1},{8,14},{9,15},{10,... | collective-permute-start | bytes 86024 | tf_op jit(solution)/shard_map/ppermute | solution.py:11
  45.9 6.4 %collective-permute-start.22 = (bf16[16,896]{1,0:T(8,128)(2,1)S(1)}, bf16[16,896]{1,0:T(8,128)(2,1)S(1)}, u32[]{:S(2)}, u32[]{:S(2)}) collective-permute-start(bf16[16,896]{1,0:T(8,128)(2,1)S(1)} %fusion.24), channel_id=1, source_target_pairs={{0,4},{1,5},{2,6},{3,7},{4,0},{5,1},{6,2},{7,3},{8,12},{9,13},{10,... | collective-permute-start | bytes 86024 | tf_op jit(solution)/shard_map/ppermute | solution.py:11
  45.9 6.4 %collective-permute-start.21 = (bf16[16,896]{1,0:T(8,128)(2,1)S(1)}, bf16[16,896]{1,0:T(8,128)(2,1)S(1)}, u32[]{:S(2)}, u32[]{:S(2)}) collective-permute-start(bf16[16,896]{1,0:T(8,128)(2,1)S(1)} %fusion.24), channel_id=1, source_target_pairs={{0,2},{1,3},{2,0},{3,1},{4,6},{5,7},{6,4},{7,5},{8,10},{9,11},{10,... | collective-permute-start | bytes 86024 | tf_op jit(solution)/shard_map/ppermute | solution.py:11
  47.8 6.0 %collective-permute-start.20 = (bf16[32,896]{1,0:T(8,128)(2,1)S(1)}, bf16[32,896]{1,0:T(8,128)(2,1)S(1)}, u32[]{:S(2)}, u32[]{:S(2)}) collective-permute-start(bf16[32,896]{1,0:T(8,128)(2,1)S(1)} %fusion.21), channel_id=1, source_target_pairs={{0,6},{1,7},{2,4},{3,5},{4,2},{5,3},{6,0},{7,1},{8,14},{9,15},{10,... | collective-permute-start | bytes 172040 | tf_op jit(solution)/shard_map/ppermute | solution.py:11
  50.4 5.1 %collective-permute-start.19 = (bf16[32,896]{1,0:T(8,128)(2,1)S(1)}, bf16[32,896]{1,0:T(8,128)(2,1)S(1)}, u32[]{:S(2)}, u32[]{:S(2)}) collective-permute-start(bf16[32,896]{1,0:T(8,128)(2,1)S(1)} %fusion.21), channel_id=1, source_target_pairs={{0,4},{1,5},{2,6},{3,7},{4,0},{5,1},{6,2},{7,3},{8,12},{9,13},{10,... | collective-permute-start | bytes 172040 | tf_op jit(solution)/shard_map/ppermute | solution.py:11
  50.4 5.1 %collective-permute-start.18 = (bf16[32,896]{1,0:T(8,128)(2,1)S(1)}, bf16[32,896]{1,0:T(8,128)(2,1)S(1)}, u32[]{:S(2)}, u32[]{:S(2)}) collective-permute-start(bf16[32,896]{1,0:T(8,128)(2,1)S(1)} %fusion.21), channel_id=1, source_target_pairs={{0,2},{1,3},{2,0},{3,1},{4,6},{5,7},{6,4},{7,5},{8,10},{9,11},{10,... | collective-permute-start | bytes 172040 | tf_op jit(solution)/shard_map/ppermute | solution.py:11
  52.3 4.9 %collective-permute-start.24 = (bf16[64,896]{1,0:T(8,128)(2,1)S(1)}, bf16[64,896]{1,0:T(8,128)(2,1)S(1)}, u32[]{:S(2)}, u32[]{:S(2)}) collective-permute-start(bf16[64,896]{1,0:T(8,128)(2,1)S(1)} %pad_maximum_fusion.5), channel_id=1, source_target_pairs={{0,1},{1,0},{2,3},{3,2},{4,5},{5,4},{6,7},{7,6},{8,9},{9,8},{10,11... | collective-permute-start | bytes 344072 | tf_op jit(solution)/shard_map/ppermute | solution.py:11
  58.2 1.5 %collective-permute-start.25 = (f32[384,128]{1,0:T(8,128)S(1)}, f32[384,128]{1,0:T(8,128)S(1)}, u32[]{:S(2)}, u32[]{:S(2)}) collective-permute-start(f32[384,128]{1,0:T(8,128)S(1)} %slice_select_fusion), channel_id=1, source_target_pairs={{0,8},{8,0},{16,24},{24,16},{1,9},{9,1},{17,25},{25,17},{2,10},{10... | collective-permute-start | bytes 589832 | tf_op jit(solution)/shard_map/ppermute | solution.py:11
  58.3 8.3 %collective-permute-start.28 = (bf16[128,1792]{1,0:T(8,128)(2,1)S(1)}, bf16[128,1792]{1,0:T(8,128)(2,1)S(1)}, u32[]{:S(2)}, u32[]{:S(2)}) collective-permute-start(bf16[128,1792]{1,0:T(8,128)(2,1)S(1)} %constant_dynamic-update-slice_fusion), channel_id=1, source_target_pairs={{0,8},{8,0},{16,24},{24,16},{1,9},{9,1},{17,25},{25,17},{2,10},{10... | collective-permute-start | bytes 1376264 | tf_op jit(solution)/shard_map/ppermute | solution.py:11
  59.9 4.3 %collective-permute-start.27 = (bf16[240,128]{1,0:T(8,128)(2,1)S(1)}, bf16[240,128]{1,0:T(8,128)(2,1)S(1)}, u32[]{:S(2)}, u32[]{:S(2)}) collective-permute-start(bf16[240,128]{1,0:T(8,128)(2,1)S(1)} %constant_dynamic-update-slice_fusion.19), channel_id=1, source_target_pairs={{0,16},{8,24},{16,0},{24,8},{1,17},{9,25},{17,1},{25,9},{2,18},{10... | collective-permute-start | bytes 184328 | tf_op jit(solution)/shard_map/ppermute | solution.py:11
  61.1 4.2 %collective-permute-start.26 = (bf16[240,128]{1,0:T(8,128)(2,1)S(1)}, bf16[240,128]{1,0:T(8,128)(2,1)S(1)}, u32[]{:S(2)}, u32[]{:S(2)}) collective-permute-start(bf16[240,128]{1,0:T(8,128)(2,1)S(1)} %constant_dynamic-update-slice_fusion.4), channel_id=1, source_target_pairs={{0,1},{1,0},{2,3},{3,2},{4,5},{5,4},{6,7},{7,6},{8,9},{9,8},{10,11... | collective-permute-start | bytes 184328 | tf_op jit(solution)/shard_map/ppermute | solution.py:11

commit v12 on v11

--- a/solution.py
+++ b/solution.py
@@ -51,7 +51,7 @@
 
 def two_layers(resid, target, enc_weight, enc_bias, dec_weight, blocks):
     hold = lax.optimization_barrier
-    slots = lax.axis_size("latent")
+    slots, count = lax.axis_size("latent"), lax.axis_size("layer")
     far = slots // 2
     layer, half = lax.axis_index("layer") // 2, lax.axis_index("layer") % 2
     slot = lax.axis_index("latent")
@@ -61,30 +61,41 @@
     latents = enc_weight.shape[2]
     decoder = dec_weight[0].reshape(2, 2 * latents, cols)
 
-    def over_x(block):
-        return crossed(block, "latent", 1)
-
-    def over_y(block):
-        return crossed(block, "layer", 2)
+    def routed(block, from_core_0=None, from_core_1=None):
+        route = []
+        for i in range(count):
+            bits = (from_core_0, from_core_1)[i % 2]
+            if bits is not None:
+                route += [(i * slots + j, (i ^ bits[0]) * slots + (j ^ bits[1])) for j in range(slots)]
+        return lax.ppermute(block, ("layer", "latent"), route)
 
     def over_core(block):
         return crossed(block, "layer", 1)
 
-    def along_z(block):
-        out = [block] + [None] * (far - 1)
+    def along_z(pieces, bits_of):
+        out = [None] * (far - 1) + pieces[far - 1:]
         for k in range(far - 1, 0, -1):
-            out[k] = crossed(block, "latent", 2 * k)
+            out[k - 1] = routed(pieces[k - 1], **bits_of(k))
         return out
 
+    def core_0_z(k):
+        return {"from_core_0": (0, 2 * k)}
+
+    def core_1_z(k):
+        return {"from_core_1": (0, 2 * k)}
+
     def pieces_of(total):
-        count = total.shape[0] // far
-        return [total[k * count:(k + 1) * count].astype(BF16) for k in range(1, far)] + [total[:count]]
-
-    def sent_along_z(pieces):
-        return [crossed(pieces[k - 1], "latent", 2 * k) for k in range(1, far)] + pieces[far - 1:]
+        each = total.shape[0] // far
+        return [total[k * each:(k + 1) * each].astype(BF16) for k in range(1, far)] + [total[:each]]
 
     def added(terms):
         return sum(term.astype(F32) for term in terms[::-1])
+
+    def gathered(terms):
+        return jnp.concatenate(terms[-1:] + terms[:-1], axis=0)
+
+    def by_core(zero, one):
+        return jnp.where(half == 0, zero, one)
 
     def decoder_part(decoder, which, where):
         return lax.dynamic_slice(decoder, (which, 0, where * part), (1, 2 * latents, part))[0]
@@ -104,60 +115,61 @@
 
     weight_other = over_core(enc_weight[0])
     mine = lax.dynamic_slice(resid, (layer, 0, half * cols), (1, rows, cols))[0]
-    pair, weight_other, bias, blocks = hold((paired(mine, over_x(mine)), weight_other, enc_bias[0], blocks))
-    column = along_z(pair)
-
-    own_other = over_x(decoder_part(decoder, layer, 1 - side))
-    shared_other = over_y(decoder_part(decoder, 1 - layer, 1 - layer))
-    decoder, own_other, shared_other, *column = hold((decoder, own_other, shared_other, *column))
-    own_mine, shared_mine = decoder_part(decoder, layer, side), decoder_part(decoder, 1 - layer, layer)
+    pair, weight_other, bias, blocks, later = hold(
+        (paired(mine, crossed(mine, "latent", 1)), weight_other, enc_bias[0], blocks, decoder)
+    )
+    column = [pair] + [None] * (far - 1)
+    for k in range(far - 1, 0, -1):
+        column[k] = crossed(pair, "latent", 2 * k)
+
+    shared_away, own_away = (1 - layer, 1 - layer), (layer, 1 - side)
+    same_away = [by_core(zero, one) for zero, one in zip(shared_away, own_away)]
+    cross_away = [by_core(one, zero) for zero, one in zip(shared_away, own_away)]
+    same_half = routed(decoder_part(decoder, *same_away), (2, 0), (0, 1))
+    cross_half = routed(decoder_part(decoder, *cross_away), (1, 1), (3, 0))
+    later, same_half, cross_half, *column = hold((later, same_half, cross_half, *column))
     resid_half = jnp.concatenate(column, axis=0)
+
+    shared_here, own_here = (1 - layer, layer), (layer, side)
+    kept = decoder_part(later, *[by_core(zero, one) for zero, one in zip(shared_here, own_here)])
+    swapped = over_core(decoder_part(later, *[by_core(one, zero) for zero, one in zip(shared_here, own_here)]))
+    rows_here = jnp.concatenate([kept, swapped], axis=1)
+    rows_there = jnp.concatenate([same_half, cross_half], axis=1)
+
     firing = gates(blocks, layer, slot, slots, latents, tokens)
     gate = jnp.where(half == 0, firing[0], firing[1])
-
     partial = half_preacts(resid_half, enc_weight[0], weight_other, bias, half)
     acts = ((partial + over_core(partial)) * jnp.concatenate(firing, axis=1)).astype(BF16)
-    acts_turned = turned(acts)
-    acts_y, acts_x = over_y(acts), over_x(acts_turned)
-    target, _ = hold((target, acts_turned))
-    start = half * cols
-
-    def aim_own(where):
-        return lax.dynamic_slice(target, (2 * layer, 0, start + where * part), (1, rows, part))[0]
-
-    aim_other = over_x(aim_own(1 - side))
-    aim_shared = lax.dynamic_slice(target, (1, 0, start + layer * part), (1, rows, part))[0]
-
-    leaving = times(rows_at(acts, 1), shared_mine) + times(rows_at(acts_y, 1), shared_other)
-    staying = times(rows_at(acts, 0), shared_mine) + times(rows_at(acts_y, 0), shared_other)
-    arrived = over_x(leaving.astype(BF16))
-    product = times(acts, own_mine) + times(acts_x, own_other)
-    own_pieces = pieces_of(product)
-    arrived, staying, own_pieces[0] = hold((arrived, staying, own_pieces[0]))
-    own_terms = sent_along_z(own_pieces)
-    shared_terms = sent_along_z(pieces_of(staying + arrived.astype(F32)))
+    acts_there = routed(by_core(acts, turned(acts)), (2, 0), (0, 1))
+    target, _ = hold((target, acts))
+
+    def aim(which, where):
+        halves = [
+            lax.dynamic_slice(target, (which, 0, this * cols + where * part), (1, rows, part))[0]
+            for this in (half, 1 - half)
+        ]
+        return jnp.concatenate(halves, axis=1)
+
+    aim_other = routed(aim(2 * layer, 1 - side), from_core_1=(0, 1))
+
+    product = times(acts, rows_here) + times(acts_there, rows_there)
+    arrived = routed(rows_at(product, 1).astype(BF16), from_core_0=(0, 1))
+    own_terms = along_z(pieces_of(product), core_1_z)
+    shared_terms = along_z(pieces_of(rows_at(product, 0) + arrived.astype(F32)), core_0_z)
     terms = hold((*shared_terms, *own_terms))
-    shared_terms, own_terms = terms[:far], terms[far:]
-    err_own = (added(own_terms) - paired(aim_own(side), aim_other).astype(F32)).astype(BF16)
-    own_column = along_z(err_own)
-    err_shared = (added(shared_terms) - aim_shared.astype(F32)).astype(BF16)
-
-    shared_near = jnp.concatenate(along_z(err_shared), axis=0)
+    err_shared = (added(terms[:far]) - aim(1, layer).astype(F32)).astype(BF16)
+    err_own = (added(terms[far:]) - paired(aim(2 * layer, side), aim_other).astype(F32)).astype(BF16)
+
+    shared_near = gathered(along_z([err_shared] * far, core_0_z))
+    errs_shared = paired(shared_near, routed(shared_near, from_core_0=(0, 1)))
+    errs_own = gathered(along_z([err_own] * far, core_1_z))
+    errs = by_core(errs_shared, errs_own)
     resid_swapped, _ = hold((resid_half, shared_near))
     resid_other = over_core(resid_swapped)
-    errs_shared = paired(shared_near, over_x(shared_near))
-    errs_own = jnp.concatenate(own_column, axis=0)
-
-    grads = jnp.concatenate(
-        [
-            times_transposed(errs_own, own_mine) + times_transposed(errs_shared, shared_mine),
-            turned(times_transposed(errs_own, own_other)),
-            times_transposed(errs_shared, shared_other),
-        ],
-        axis=0,
-    )
-    lower, upper = grads[:, :latents], grads[:, latents:]
-    grads = jnp.where(half == 0, lower, upper) + over_core(jnp.where(half == 0, upper, lower))
+
+    found = by_core(err_shared, rows_at(err_own, 0))
+    found_swapped = over_core(found[:, part:])
+    sent = by_core(err_shared, rows_at(err_own, 1))
 
     def with_errors(grad, block):
         tiles = [block[:, at:at + latents] for at in range(0, part, latents)]
@@ -167,14 +179,20 @@
         tiles = message[tokens:].reshape(part // latents, rows, latents)
         return message[:tokens].astype(F32), jnp.concatenate([tiles[i] for i in range(part // latents)], axis=1)
 
-    from_x, own_there = without_errors(over_x(with_errors(grads[tokens:2 * tokens], rows_at(err_own, 1))))
-    from_y, shared_there = without_errors(over_y(with_errors(grads[2 * tokens:], err_shared)))
-    errors = jnp.where(
-        layer == 0,
-        ordered(side, rows_at(err_own, 0), own_there, axis=1),
-        jnp.concatenate([shared_there, err_shared], axis=1),
-    )
-    grad_pre = (grads[:tokens] + from_x + from_y) * gate
+    def of_core(pair, which):
+        return jnp.where(which == 0, pair[:, :latents], pair[:, latents:])
+
+    away = times_transposed(errs, rows_there)
+    away = by_core(away, turned(away))
+    same, same_there = without_errors(routed(with_errors(of_core(away, half), sent[:, :part]), (2, 0), (0, 1)))
+    cross, cross_there = without_errors(routed(with_errors(of_core(away, 1 - half), sent[:, part:]), (3, 0), (1, 1)))
+    here = times_transposed(errs, rows_here)
+    grad = of_core(here, half) + over_core(of_core(here, 1 - half)) + same + cross
+    at_home = layer != half
+    near_part = jnp.where(at_home, found[:, :part], found_swapped)
+    far_part = jnp.where(at_home, same_there, cross_there)
+    errors = ordered(jnp.where(layer == 0, side, 1), near_part, far_part, axis=1)
+    grad_pre = grad * gate
     bias_grad = jnp.sum(grad_pre, axis=0)[None, :]
     enc_grad = encoder_gradient(resid_half, resid_other, grad_pre.astype(BF16), half)
     return errors[None], enc_grad[None], bias_grad

time: 68.3 us -> 81.5 us (1.19)
  starting transfers between devices: 35.4 us -> 44.7 us
  waiting for transfers between devices: 18.9 us -> 22 us
  other arithmetic: 3.16 us -> 4.74 us
  matrix products: 4.17 us -> 3.13 us
    ppermute x0 -> x20, starting transfers between devices: none -> 36.5 us  [routed(): return lax.ppermute(block, ('layer', 'latent'), route)]
    ppermute x29 -> x10, starting transfers between devices: 35.4 us -> 8.22 us  [crossed(): lax.ppermute(block, axis, [(i, i ^ mask) for i in range(lax.axis_size(axi...]
    ppermute x0 -> x20, waiting for transfers between devices: none -> 18.7 us  [routed(): return lax.ppermute(block, ('layer', 'latent'), route)]
    ppermute x29 -> x10, waiting for transfers between devices: 18.9 us -> 3.34 us  [crossed(): lax.ppermute(block, axis, [(i, i ^ mask) for i in range(lax.axis_size(axi...]
    select_n x3, other arithmetic: 0.25 us -> 2.34 us  [both_halves(): jnp.where(half == 0, mine, other)]
    squeeze x1 -> x2, local copies, waits for them, and re-layouts: 2.01 us -> 2.41 us  [decoder_part(): lax.dynamic_slice(decoder, (which, 0, where * part), (1, 2 * latents, part))]
  transfers between devices with their start and end apart: 29 -> 30, of which waited for: 13 -> 12; matrix products, arithmetic and copies ran while one was open for 11% -> 12% of each run, Pallas kernels for 0% -> 0%
where the time goes in v12:
time: 81.5 us; the launch traced here: 81 us
  starting transfers between devices  44.7 us (55%)
  waiting for transfers between devices  22 us (27%)
  other arithmetic  4.74 us (6%)
  local copies, waits for them, and re-layouts  3.77 us (5%)
  matrix products  3.13 us (4%)
  between operations  2.64 us (3%)
    ppermute x20, starting transfers between devices, routed(): return lax.ppermute(block, ('layer', 'latent'), route)  36.5 us
    ppermute x20, waiting for transfers between devices, routed(): return lax.ppermute(block, ('layer', 'latent'), route)  18.7 us
    ppermute x10, starting transfers between devices, crossed(): lax.ppermute(block, axis, [(i, i ^ mask) for i in range(lax.axis_size(axi...  8.22 us
    ppermute x10, waiting for transfers between devices, crossed(): lax.ppermute(block, axis, [(i, i ^ mask) for i in range(lax.axis_size(axi...  3.34 us
    squeeze x2, local copies, waits for them, and re-layouts, decoder_part(): lax.dynamic_slice(decoder, (which, 0, where * part), (1, 2 * latents, part))  2.41 us
    select_n x3, other arithmetic, both_halves(): jnp.where(half == 0, mine, other)  2.34 us
  transfers between devices with their start and end apart: 30, of which 12 were waited for; matrix products, arithmetic and copies ran while one was open for 12% of the time, Pallas kernels for 0%

profile of v12, /device:TPU:0, one launch (start us, length us, event | category | flops | bytes accessed | tf_op | source)
XLA Modules:
  0.0 81.0 jit_solution(1489516430874596856)
XLA Ops:
  0.6 0.5 collective-permute-start.1
  1.1 0.8 %dynamic-slice_bitcast_fusion.5 = (bf16[1,1,16,1792]{3,2,1,0:T(8,128)(2,1)S(1)}, bf16[16,1792]{1,0:T(8,128)(2,1)S(1)}) fusion(bf16[2,16,3584]{2,1,0:T(8,128)(2,1)} %param.6, s32[]{:T(128)S(6)} %select_n.217, s32[]{:T(128)S(6)} %select_n.218), kind=kLoop, calls=%fused_computation.83 | loop fusion | bytes 172040 | tf_op jit(solution)/shard_map/reshape;squeeze | solution.py:110
  2.0 2.5 %collective-permute-start = (bf16[16,1792]{1,0:T(8,128)(2,1)S(1)}, bf16[16,1792]{1,0:T(8,128)(2,1)S(1)}, u32[]{:S(2)}, u32[]{:S(2)}) collective-permute-start(bf16[16,1792]{1,0:T(8,128)(2,1)S(1)} %get-tuple-element.76), channel_id=1, source_target_pairs={{0,1},{1,0},{2,3},{3,2},{4,5},{5,4},{6,7},{7,6},{8,9},{9,8},{10,11... | collective-permute-start | bytes 172040 | tf_op jit(solution)/shard_map/ppermute | solution.py:11
  4.5 2.3 %dynamic-slice_bitcast_fusion.2 = (bf16[256,896]{1,0:T(8,128)(2,1)}, bf16[256,896]{1,0:T(8,128)(2,1)}) fusion(bf16[2,256,1792]{2,1,0:T(8,128)(2,1)} %bitcast.79, s32[]{:T(128)S(6)} %select_n.224, s32[]{:T(128)S(6)} %select_n.226, s32[]{:T(128)S(6)} %select_n.220, s32[]{:T(128)S(6)} %select_n.222), kind=kLoop, calls=%fused_computation.20 | loop fusion | bytes 1835024 | tf_op jit(solution)/shard_map/squeeze | solution.py:101
  6.8 0.2 collective-permute-start.3
  7.0 1.7 %collective-permute-start.2 = (bf16[256,896]{1,0:T(8,128)(2,1)}, bf16[256,896]{1,0:T(8,128)(2,1)S(1)}, u32[]{:S(2)}, u32[]{:S(2)}) collective-permute-start(bf16[256,896]{1,0:T(8,128)(2,1)} %get-tuple-element.60), channel_id=1, source_target_pairs={{0,16},{1,17},{2,18},{3,19},{4,20},{5,21},{6,22},{7,23},{8,9},{9,8... | collective-permute-start | bytes 1376264 | tf_op jit(solution)/shard_map/ppermute | solution.py:70
  8.7 0.0 collective-permute-done.1
  8.7 3.7 %collective-permute-start.6 = (bf16[32,1792]{1,0:T(8,128)(2,1)S(1)}, bf16[32,1792]{1,0:T(8,128)(2,1)S(1)}, u32[]{:S(2)}, u32[]{:S(2)}) collective-permute-start(bf16[32,1792]{1,0:T(8,128)(2,1)S(1)} %bitcast.86), channel_id=1, source_target_pairs={{0,6},{1,7},{2,4},{3,5},{4,2},{5,3},{6,0},{7,1},{8,14},{9,15},{10,... | collective-permute-start | bytes 344072 | tf_op jit(solution)/shard_map/ppermute | solution.py:11
  12.4 0.0 collective-permute-start.5
  12.4 0.8 collective-permute-start.4
  13.2 2.3 %bitcast_select_fusion.1 = (bf16[1792,128]{1,0:T(8,128)(2,1)}, bf16[1792,128]{1,0:T(8,128)(2,1)}) fusion(pred[]{:T(512)S(6)} %eq.74, bf16[3584,128]{1,0:T(8,128)(2,1)} %collective-permute-done.1, s32[]{:T(128)S(6)} %select_n.218, bf16[1,3584,128]{2,1,0:T(8,128)(2,1)} %param.8), kind=kLoop, calls=%fused_computation.17 | loop fusion | flops 458752 | bytes 1835013 | tf_op jit(solution)/shard_map/jit(_where)/select_n | solution.py:23
  15.4 0.6 compare_reduce_fusion
  17.4 0.0 copy-start.3
  17.4 1.7 %collective-permute-done.3 = bf16[256,896]{1,0:T(8,128)(2,1)S(1)} collective-permute-done((bf16[256,896]{1,0:T(8,128)(2,1)}, bf16[256,896]{1,0:T(8,128)(2,1)S(1)}, u32[]{:S(2)}, u32[]{:S(2)}) %collective-permute-start.3) | collective-permute-done | bytes 458784 | tf_op jit(solution)/shard_map/ppermute | solution.py:70
  19.2 0.7 collective-permute-done.2
  19.9 0.0 collective-permute-done.6
  19.9 2.4 %collective-permute-done.5 = bf16[32,1792]{1,0:T(8,128)(2,1)S(1)} collective-permute-done((bf16[32,1792]{1,0:T(8,128)(2,1)S(1)}, bf16[32,1792]{1,0:T(8,128)(2,1)S(1)}, u32[]{:S(2)}, u32[]{:S(2)}) %collective-permute-start.5) | collective-permute-done | bytes 114720 | tf_op jit(solution)/shard_map/ppermute | solution.py:11
  22.3 0.0 collective-permute-done.4
  22.3 0.1 dynamic-slice_bitcast_fusion.1
  22.4 0.1 collective-permute-start.8
  22.6 0.0 copy-start.5
  22.6 0.3 convolution_add_fusion.1
  22.9 0.6 collective-permute-start.7
  23.5 0.1 constant_dynamic-update-slice_fusion.4
  23.5 0.9 %collective-permute-done.7 = f32[128,256]{1,0:T(8,128)S(1)} collective-permute-done((f32[128,256]{1,0:T(8,128)S(1)}, f32[128,256]{1,0:T(8,128)S(1)}, u32[]{:S(2)}, u32[]{:S(2)}) %collective-permute-start.7) | collective-permute-done | bytes 131104 | tf_op jit(solution)/shard_map/ppermute | solution.py:11
  24.5 0.6 collective-permute-start.9
  25.1 0.7 collective-permute-start.17
  25.8 3.0 %collective-permute-done.9 = bf16[128,256]{1,0:T(8,128)(2,1)S(1)} collective-permute-done((bf16[128,256]{1,0:T(8,128)(2,1)S(1)}, bf16[128,256]{1,0:T(8,128)(2,1)S(1)}, u32[]{:S(2)}, u32[]{:S(2)}) %collective-permute-start.9) | collective-permute-done | bytes 65568 | tf_op jit(solution)/shard_map/ppermute | solution.py:70
  28.9 0.3 fusion.23
  29.2 0.3 fusion.22
  29.6 3.4 %collective-permute-start.10 = (bf16[64,1792]{1,0:T(8,128)(2,1)S(1)}, bf16[64,1792]{1,0:T(8,128)(2,1)S(1)}, u32[]{:S(2)}, u32[]{:S(2)}) collective-permute-start(bf16[64,1792]{1,0:T(8,128)(2,1)S(1)} %bitcast.91), channel_id=1, source_target_pairs={{0,1},{1,0},{2,3},{3,2},{4,5},{5,4},{6,7},{7,6},{16,17},{17,16},{1... | collective-permute-start | bytes 688136 | tf_op jit(solution)/shard_map/ppermute | solution.py:70
  33.0 0.7 collective-permute-start.16
  33.7 0.7 collective-permute-start.15
  34.4 0.7 collective-permute-start.14
  35.0 2.4 %collective-permute-done.10 = bf16[64,1792]{1,0:T(8,128)(2,1)S(1)} collective-permute-done((bf16[64,1792]{1,0:T(8,128)(2,1)S(1)}, bf16[64,1792]{1,0:T(8,128)(2,1)S(1)}, u32[]{:S(2)}, u32[]{:S(2)}) %collective-permute-start.10) | collective-permute-done | bytes 229408 | tf_op jit(solution)/shard_map/ppermute | solution.py:70
  37.6 4.5 %collective-permute-start.13 = (bf16[16,1792]{1,0:T(8,128)(2,1)S(1)}, bf16[16,1792]{1,0:T(8,128)(2,1)S(1)}, u32[]{:S(2)}, u32[]{:S(2)}) collective-permute-start(bf16[16,1792]{1,0:T(8,128)(2,1)S(1)} %get-tuple-element.72), channel_id=1, source_target_pairs={{0,6},{1,7},{2,4},{3,5},{4,2},{5,3},{6,0},{7,1},{16,22},{17,23},{1... | collective-permute-start | bytes 172040 | tf_op jit(solution)/shard_map/ppermute | solution.py:70
  42.1 1.9 %collective-permute-start.12 = (bf16[16,1792]{1,0:T(8,128)(2,1)S(1)}, bf16[16,1792]{1,0:T(8,128)(2,1)S(1)}, u32[]{:S(2)}, u32[]{:S(2)}) collective-permute-start(bf16[16,1792]{1,0:T(8,128)(2,1)S(1)} %get-tuple-element.73), channel_id=1, source_target_pairs={{0,4},{1,5},{2,6},{3,7},{4,0},{5,1},{6,2},{7,3},{16,20},{17,21},{1... | collective-permute-start | bytes 172040 | tf_op jit(solution)/shard_map/ppermute | solution.py:70
  44.0 0.0 collective-permute-done.16
  44.0 3.8 %collective-permute-start.11 = (bf16[16,1792]{1,0:T(8,128)(2,1)S(1)}, bf16[16,1792]{1,0:T(8,128)(2,1)S(1)}, u32[]{:S(2)}, u32[]{:S(2)}) collective-permute-start(bf16[16,1792]{1,0:T(8,128)(2,1)S(1)} %get-tuple-element.74), channel_id=1, source_target_pairs={{0,2},{1,3},{2,0},{3,1},{4,6},{5,7},{6,4},{7,5},{16,18},{17,19},{1... | collective-permute-start | bytes 172040 | tf_op jit(solution)/shard_map/ppermute | solution.py:70
  48.0 1.1 %collective-permute-done.12 = bf16[16,1792]{1,0:T(8,128)(2,1)S(1)} collective-permute-done((bf16[16,1792]{1,0:T(8,128)(2,1)S(1)}, bf16[16,1792]{1,0:T(8,128)(2,1)S(1)}, u32[]{:S(2)}, u32[]{:S(2)}) %collective-permute-start.12) | collective-permute-done | bytes 57376 | tf_op jit(solution)/shard_map/ppermute | solution.py:70
  49.1 1.1 %collective-permute-done.11 = bf16[16,1792]{1,0:T(8,128)(2,1)S(1)} collective-permute-done((bf16[16,1792]{1,0:T(8,128)(2,1)S(1)}, bf16[16,1792]{1,0:T(8,128)(2,1)S(1)}, u32[]{:S(2)}, u32[]{:S(2)}) %collective-permute-start.11) | collective-permute-done | bytes 57376 | tf_op jit(solution)/shard_map/ppermute | solution.py:70
  50.1 0.1 fusion.8
  50.2 0.1 fusion.10
  50.3 4.3 %collective-permute-start.21 = (bf16[16,1792]{1,0:T(8,128)(2,1)S(1)}, bf16[16,1792]{1,0:T(8,128)(2,1)S(1)}, u32[]{:S(2)}, u32[]{:S(2)}) collective-permute-start(bf16[16,1792]{1,0:T(8,128)(2,1)S(1)} %get-tuple-element.52), channel_id=1, source_target_pairs={{0,6},{1,7},{2,4},{3,5},{4,2},{5,3},{6,0},{7,1},{16,22},{17,23},{1... | collective-permute-start | bytes 172040 | tf_op jit(solution)/shard_map/ppermute | solution.py:70
  54.5 3.4 %collective-permute-start.20 = (bf16[16,1792]{1,0:T(8,128)(2,1)S(1)}, bf16[16,1792]{1,0:T(8,128)(2,1)S(1)}, u32[]{:S(2)}, u32[]{:S(2)}) collective-permute-start(bf16[16,1792]{1,0:T(8,128)(2,1)S(1)} %get-tuple-element.52), channel_id=1, source_target_pairs={{0,4},{1,5},{2,6},{3,7},{4,0},{5,1},{6,2},{7,3},{16,20},{17,21},{1... | collective-permute-start | bytes 172040 | tf_op jit(solution)/shard_map/ppermute | solution.py:70
  58.0 2.4 %collective-permute-start.19 = (bf16[16,1792]{1,0:T(8,128)(2,1)S(1)}, bf16[16,1792]{1,0:T(8,128)(2,1)S(1)}, u32[]{:S(2)}, u32[]{:S(2)}) collective-permute-start(bf16[16,1792]{1,0:T(8,128)(2,1)S(1)} %get-tuple-element.52), channel_id=1, source_target_pairs={{0,2},{1,3},{2,0},{3,1},{4,6},{5,7},{6,4},{7,5},{16,18},{17,19},{1... | collective-permute-start | bytes 172040 | tf_op jit(solution)/shard_map/ppermute | solution.py:70
  60.4 0.7 collective-permute-start.25
  61.1 0.7 collective-permute-start.24
  61.8 0.7 collective-permute-start.23
  62.5 0.1 collective-permute-start.18
  62.6 1.5 %collective-permute-done.19 = bf16[16,1792]{1,0:T(8,128)(2,1)S(1)} collective-permute-done((bf16[16,1792]{1,0:T(8,128)(2,1)S(1)}, bf16[16,1792]{1,0:T(8,128)(2,1)S(1)}, u32[]{:S(2)}, u32[]{:S(2)}) %collective-permute-start.19) | collective-permute-done | bytes 57376 | tf_op jit(solution)/shard_map/ppermute | solution.py:70
  64.0 3.4 %collective-permute-start.22 = (bf16[64,1792]{1,0:T(8,128)(2,1)S(1)}, bf16[64,1792]{1,0:T(8,128)(2,1)S(1)}, u32[]{:S(2)}, u32[]{:S(2)}) collective-permute-start(bf16[64,1792]{1,0:T(8,128)(2,1)S(1)} %pad_maximum_fusion.4), channel_id=1, source_target_pairs={{0,1},{1,0},{2,3},{3,2},{4,5},{5,4},{6,7},{7,6},{16,17},{17,16},{1... | collective-permute-start | bytes 688136 | tf_op jit(solution)/shard_map/ppermute | solution.py:70
  67.5 4.5 %collective-permute-done.22 = bf16[64,1792]{1,0:T(8,128)(2,1)S(1)} collective-permute-done((bf16[64,1792]{1,0:T(8,128)(2,1)S(1)}, bf16[64,1792]{1,0:T(8,128)(2,1)S(1)}, u32[]{:S(2)}, u32[]{:S(2)}) %collective-permute-start.22) | collective-permute-done | bytes 229408 | tf_op jit(solution)/shard_map/ppermute | solution.py:70
  72.1 0.1 maximum_select_fusion
  72.2 0.4 fusion.24
  72.9 0.7 collective-permute-start.27
  73.5 0.4 fusion.7
  74.0 1.6 %collective-permute-start.26 = (bf16[240,128]{1,0:T(8,128)(2,1)S(1)}, bf16[240,128]{1,0:T(8,128)(2,1)S(1)}, u32[]{:S(2)}, u32[]{:S(2)}) collective-permute-start(bf16[240,128]{1,0:T(8,128)(2,1)S(1)} %get-tuple-element.86), channel_id=1, source_target_pairs={{0,16},{1,17},{2,18},{3,19},{4,20},{5,21},{6,22},{7,23},{8,9},{9,8... | collective-permute-start | bytes 184328 | tf_op jit(solution)/shard_map/ppermute | solution.py:70
  75.6 1.0 %collective-permute-done.27 = bf16[240,128]{1,0:T(8,128)(2,1)S(1)} collective-permute-done((bf16[240,128]{1,0:T(8,128)(2,1)S(1)}, bf16[240,128]{1,0:T(8,128)(2,1)S(1)}, u32[]{:S(2)}, u32[]{:S(2)}) %collective-permute-start.27) | collective-permute-done | bytes 61472 | tf_op jit(solution)/shard_map/ppermute | solution.py:70
  76.6 1.7 %collective-permute-done.26 = bf16[240,128]{1,0:T(8,128)(2,1)S(1)} collective-permute-done((bf16[240,128]{1,0:T(8,128)(2,1)S(1)}, bf16[240,128]{1,0:T(8,128)(2,1)S(1)}, u32[]{:S(2)}, u32[]{:S(2)}) %collective-permute-start.26) | collective-permute-done | bytes 61472 | tf_op jit(solution)/shard_map/ppermute | solution.py:70
  78.4 0.6 maximum_bitcast_fusion.1
  79.0 0.6 fusion.16
  79.6 0.1 broadcast_select_fusion.1
  79.6 1.4 %fusion = bf16[1,3584,128]{2,1,0:T(8,128)(2,1)} fusion(bf16[128,1792]{1,0:T(8,128)(2,1)S(1)} %get-tuple-element.62, bf16[128,1792]{1,0:T(8,128)(2,1)S(1)} %get-tuple-element.61, bf16[128,128]{1,0:T(8,128)(2,1)S(1)} %get-tuple-element.50), kind=kOutput, calls=%fused_computation.1 | convolution fusion | flops 119734272 | bytes 1867776 | tf_op jit(solution)/shard_map/dot_general | solution.py:48
  (88 shorter events, 0.8 us)
Async XLA Ops:
  0.6 8.1 %collective-permute-start.1 = (bf16[3584,128]{1,0:T(8,128)(2,1)}, bf16[3584,128]{1,0:T(8,128)(2,1)}, u32[]{:S(2)}, u32[]{:S(2)}) collective-permute-start(bf16[3584,128]{1,0:T(8,128)(2,1)} %bitcast.92), channel_id=1, source_target_pairs={{0,8},{8,0},{16,24},{24,16},{1,9},{9,1},{17,25},{25,17},{2,10},{10... | collective-permute-start | bytes 2752520 | tf_op jit(solution)/shard_map/ppermute | solution.py:11
  2.0 6.7 %collective-permute-start = (bf16[16,1792]{1,0:T(8,128)(2,1)S(1)}, bf16[16,1792]{1,0:T(8,128)(2,1)S(1)}, u32[]{:S(2)}, u32[]{:S(2)}) collective-permute-start(bf16[16,1792]{1,0:T(8,128)(2,1)S(1)} %get-tuple-element.76), channel_id=1, source_target_pairs={{0,1},{1,0},{2,3},{3,2},{4,5},{5,4},{6,7},{7,6},{8,9},{9,8},{10,11... | collective-permute-start | bytes 172040 | tf_op jit(solution)/shard_map/ppermute | solution.py:11
  4.5 10.9 %copy-start.6 = (f32[1,128]{1,0:T(1,128)S(1)}, f32[1,128]{1,0:T(1,128)}, u32[]{:S(2)}) copy-start(f32[1,128]{1,0:T(1,128)} %param.9) | copy-start | bytes 1540
  4.5 10.9 %copy-start.7 = (s32[2,1,12]{2,1,0:T(1,128)S(1)}, s32[2,1,12]{2,1,0:T(1,128)}, u32[]{:S(2)}) copy-start(s32[2,1,12]{2,1,0:T(1,128)} %param.11) | copy-start | bytes 292
  4.5 17.8 %copy-start = (bf16[1,2,2,128,1792]{4,3,2,1,0:T(8,128)(2,1)S(1)}, bf16[1,2,2,128,1792]{4,3,2,1,0:T(8,128)(2,1)}, u32[]{:S(2)}) copy-start(bf16[1,2,2,128,1792]{4,3,2,1,0:T(8,128)(2,1)} %param.10) | copy-start | bytes 5505028
  6.8 12.3 %collective-permute-start.3 = (bf16[256,896]{1,0:T(8,128)(2,1)}, bf16[256,896]{1,0:T(8,128)(2,1)S(1)}, u32[]{:S(2)}, u32[]{:S(2)}) collective-permute-start(bf16[256,896]{1,0:T(8,128)(2,1)} %get-tuple-element.59), channel_id=1, source_target_pairs={{0,9},{1,8},{2,11},{3,10},{4,13},{5,12},{6,15},{7,14},{8,16},{9,17... | collective-permute-start | bytes 1376264 | tf_op jit(solution)/shard_map/ppermute | solution.py:70
  7.0 12.9 %collective-permute-start.2 = (bf16[256,896]{1,0:T(8,128)(2,1)}, bf16[256,896]{1,0:T(8,128)(2,1)S(1)}, u32[]{:S(2)}, u32[]{:S(2)}) collective-permute-start(bf16[256,896]{1,0:T(8,128)(2,1)} %get-tuple-element.60), channel_id=1, source_target_pairs={{0,16},{1,17},{2,18},{3,19},{4,20},{5,21},{6,22},{7,23},{8,9},{9,8... | collective-permute-start | bytes 1376264 | tf_op jit(solution)/shard_map/ppermute | solution.py:70
  8.7 11.2 %collective-permute-start.6 = (bf16[32,1792]{1,0:T(8,128)(2,1)S(1)}, bf16[32,1792]{1,0:T(8,128)(2,1)S(1)}, u32[]{:S(2)}, u32[]{:S(2)}) collective-permute-start(bf16[32,1792]{1,0:T(8,128)(2,1)S(1)} %bitcast.86), channel_id=1, source_target_pairs={{0,6},{1,7},{2,4},{3,5},{4,2},{5,3},{6,0},{7,1},{8,14},{9,15},{10,... | collective-permute-start | bytes 344072 | tf_op jit(solution)/shard_map/ppermute | solution.py:11
  12.4 9.9 %collective-permute-start.5 = (bf16[32,1792]{1,0:T(8,128)(2,1)S(1)}, bf16[32,1792]{1,0:T(8,128)(2,1)S(1)}, u32[]{:S(2)}, u32[]{:S(2)}) collective-permute-start(bf16[32,1792]{1,0:T(8,128)(2,1)S(1)} %bitcast.87), channel_id=1, source_target_pairs={{0,4},{1,5},{2,6},{3,7},{4,0},{5,1},{6,2},{7,3},{8,12},{9,13},{10,... | collective-permute-start | bytes 344072 | tf_op jit(solution)/shard_map/ppermute | solution.py:11
  12.4 9.9 %collective-permute-start.4 = (bf16[32,1792]{1,0:T(8,128)(2,1)S(1)}, bf16[32,1792]{1,0:T(8,128)(2,1)S(1)}, u32[]{:S(2)}, u32[]{:S(2)}) collective-permute-start(bf16[32,1792]{1,0:T(8,128)(2,1)S(1)} %bitcast.88), channel_id=1, source_target_pairs={{0,2},{1,3},{2,0},{3,1},{4,6},{5,7},{6,4},{7,5},{8,10},{9,11},{10,... | collective-permute-start | bytes 344072 | tf_op jit(solution)/shard_map/ppermute | solution.py:11
  17.4 5.1 %copy-start.3 = (bf16[1792,128]{1,0:T(8,128)(2,1)S(1)}, bf16[1792,128]{1,0:T(8,128)(2,1)}, u32[]{:S(2)}) copy-start(bf16[1792,128]{1,0:T(8,128)(2,1)} %get-tuple-element.57) | copy-start | bytes 1376260
  17.4 5.1 %copy-start.4 = (bf16[1792,128]{1,0:T(8,128)(2,1)S(1)}, bf16[1792,128]{1,0:T(8,128)(2,1)}, u32[]{:S(2)}) copy-start(bf16[1792,128]{1,0:T(8,128)(2,1)} %get-tuple-element.58) | copy-start | bytes 1376260
  22.4 6.8 %collective-permute-start.8 = (bf16[256,896]{1,0:T(8,128)(2,1)S(1)}, bf16[256,896]{1,0:T(8,128)(2,1)S(1)}, u32[]{:S(2)}, u32[]{:S(2)}) collective-permute-start(bf16[256,896]{1,0:T(8,128)(2,1)S(1)} %get-tuple-element.56), channel_id=1, source_target_pairs={{0,8},{8,0},{16,24},{24,16},{1,9},{9,1},{17,25},{25,17},{2,10},{10... | collective-permute-start | bytes 1376264 | tf_op jit(solution)/shard_map/ppermute | solution.py:11
  22.5 1.0 %copy-start.1 = (bf16[128,1792]{1,0:T(8,128)(2,1)}, bf16[128,1792]{1,0:T(8,128)(2,1)S(1)}, u32[]{:S(2)}) copy-start(bf16[128,1792]{1,0:T(8,128)(2,1)S(1)} %constant_dynamic-update-slice_fusion) | copy-start | bytes 1376260
  22.6 2.6 %copy-start.5 = (bf16[3,16,3584]{2,1,0:T(8,128)(2,1)S(1)}, bf16[3,16,3584]{2,1,0:T(8,128)(2,1)}, u32[]{:S(2)}) copy-start(bf16[3,16,3584]{2,1,0:T(8,128)(2,1)} %param.7) | copy-start | bytes 1032196
  22.9 1.6 %collective-permute-start.7 = (f32[128,256]{1,0:T(8,128)S(1)}, f32[128,256]{1,0:T(8,128)S(1)}, u32[]{:S(2)}, u32[]{:S(2)}) collective-permute-start(f32[128,256]{1,0:T(8,128)S(1)} %convolution_add_fusion.1), channel_id=1, source_target_pairs={{0,8},{8,0},{16,24},{24,16},{1,9},{9,1},{17,25},{25,17},{2,10},{10... | collective-permute-start | bytes 393224 | tf_op jit(solution)/shard_map/ppermute | solution.py:11
  24.5 4.3 %collective-permute-start.9 = (bf16[128,256]{1,0:T(8,128)(2,1)S(1)}, bf16[128,256]{1,0:T(8,128)(2,1)S(1)}, u32[]{:S(2)}, u32[]{:S(2)}) collective-permute-start(bf16[128,256]{1,0:T(8,128)(2,1)S(1)} %bitcast_select_fusion.3), channel_id=1, source_target_pairs={{0,16},{1,17},{2,18},{3,19},{4,20},{5,21},{6,22},{7,23},{8,9},{9,8... | collective-permute-start | bytes 196616 | tf_op jit(solution)/shard_map/ppermute | solution.py:70
  25.1 17.0 %collective-permute-start.17 = (bf16[16,1792]{1,0:T(8,128)(2,1)S(1)}, bf16[16,1792]{1,0:T(8,128)(2,1)S(1)}, u32[]{:S(2)}, u32[]{:S(2)}) collective-permute-start(bf16[16,1792]{1,0:T(8,128)(2,1)S(1)} %pad_maximum_fusion.9), channel_id=1, source_target_pairs={{8,9},{9,8},{10,11},{11,10},{12,13},{13,12},{14,15},{15,14},{24,25... | collective-permute-start | bytes 172040 | tf_op jit(solution)/shard_map/ppermute | solution.py:70
  29.6 7.9 %collective-permute-start.10 = (bf16[64,1792]{1,0:T(8,128)(2,1)S(1)}, bf16[64,1792]{1,0:T(8,128)(2,1)S(1)}, u32[]{:S(2)}, u32[]{:S(2)}) collective-permute-start(bf16[64,1792]{1,0:T(8,128)(2,1)S(1)} %bitcast.91), channel_id=1, source_target_pairs={{0,1},{1,0},{2,3},{3,2},{4,5},{5,4},{6,7},{7,6},{16,17},{17,16},{1... | collective-permute-start | bytes 688136 | tf_op jit(solution)/shard_map/ppermute | solution.py:70
  33.0 11.0 %collective-permute-start.16 = (bf16[32,1792]{1,0:T(8,128)(2,1)S(1)}, bf16[32,1792]{1,0:T(8,128)(2,1)S(1)}, u32[]{:S(2)}, u32[]{:S(2)}) collective-permute-start(bf16[32,1792]{1,0:T(8,128)(2,1)S(1)} %get-tuple-element.63), channel_id=1, source_target_pairs={{8,14},{9,15},{10,12},{11,13},{12,10},{13,11},{14,8},{15,9},{24,30... | collective-permute-start | bytes 344072 | tf_op jit(solution)/shard_map/ppermute | solution.py:70
  33.7 14.2 %collective-permute-start.15 = (bf16[32,1792]{1,0:T(8,128)(2,1)S(1)}, bf16[32,1792]{1,0:T(8,128)(2,1)S(1)}, u32[]{:S(2)}, u32[]{:S(2)}) collective-permute-start(bf16[32,1792]{1,0:T(8,128)(2,1)S(1)} %get-tuple-element.64), channel_id=1, source_target_pairs={{8,12},{9,13},{10,14},{11,15},{12,8},{13,9},{14,10},{15,11},{24,28... | collective-permute-start | bytes 344072 | tf_op jit(solution)/shard_map/ppermute | solution.py:70
  34.4 13.6 %collective-permute-start.14 = (bf16[32,1792]{1,0:T(8,128)(2,1)S(1)}, bf16[32,1792]{1,0:T(8,128)(2,1)S(1)}, u32[]{:S(2)}, u32[]{:S(2)}) collective-permute-start(bf16[32,1792]{1,0:T(8,128)(2,1)S(1)} %get-tuple-element.65), channel_id=1, source_target_pairs={{8,10},{9,11},{10,8},{11,9},{12,14},{13,15},{14,12},{15,13},{24,26... | collective-permute-start | bytes 344072 | tf_op jit(solution)/shard_map/ppermute | solution.py:70
  37.5 34.4 %copy-start.2 = (bf16[128,1792]{1,0:T(8,128)(2,1)S(1)}, bf16[128,1792]{1,0:T(8,128)(2,1)}, u32[]{:S(2)}) copy-start(bf16[128,1792]{1,0:T(8,128)(2,1)} %copy-done.1) | copy-start | bytes 1376260
  37.6 10.4 %collective-permute-start.13 = (bf16[16,1792]{1,0:T(8,128)(2,1)S(1)}, bf16[16,1792]{1,0:T(8,128)(2,1)S(1)}, u32[]{:S(2)}, u32[]{:S(2)}) collective-permute-start(bf16[16,1792]{1,0:T(8,128)(2,1)S(1)} %get-tuple-element.72), channel_id=1, source_target_pairs={{0,6},{1,7},{2,4},{3,5},{4,2},{5,3},{6,0},{7,1},{16,22},{17,23},{1... | collective-permute-start | bytes 172040 | tf_op jit(solution)/shard_map/ppermute | solution.py:70
  42.1 7.0 %collective-permute-start.12 = (bf16[16,1792]{1,0:T(8,128)(2,1)S(1)}, bf16[16,1792]{1,0:T(8,128)(2,1)S(1)}, u32[]{:S(2)}, u32[]{:S(2)}) collective-permute-start(bf16[16,1792]{1,0:T(8,128)(2,1)S(1)} %get-tuple-element.73), channel_id=1, source_target_pairs={{0,4},{1,5},{2,6},{3,7},{4,0},{5,1},{6,2},{7,3},{16,20},{17,21},{1... | collective-permute-start | bytes 172040 | tf_op jit(solution)/shard_map/ppermute | solution.py:70
  44.0 6.1 %collective-permute-start.11 = (bf16[16,1792]{1,0:T(8,128)(2,1)S(1)}, bf16[16,1792]{1,0:T(8,128)(2,1)S(1)}, u32[]{:S(2)}, u32[]{:S(2)}) collective-permute-start(bf16[16,1792]{1,0:T(8,128)(2,1)S(1)} %get-tuple-element.74), channel_id=1, source_target_pairs={{0,2},{1,3},{2,0},{3,1},{4,6},{5,7},{6,4},{7,5},{16,18},{17,19},{1... | collective-permute-start | bytes 172040 | tf_op jit(solution)/shard_map/ppermute | solution.py:70
  50.3 11.5 %collective-permute-start.21 = (bf16[16,1792]{1,0:T(8,128)(2,1)S(1)}, bf16[16,1792]{1,0:T(8,128)(2,1)S(1)}, u32[]{:S(2)}, u32[]{:S(2)}) collective-permute-start(bf16[16,1792]{1,0:T(8,128)(2,1)S(1)} %get-tuple-element.52), channel_id=1, source_target_pairs={{0,6},{1,7},{2,4},{3,5},{4,2},{5,3},{6,0},{7,1},{16,22},{17,23},{1... | collective-permute-start | bytes 172040 | tf_op jit(solution)/shard_map/ppermute | solution.py:70
  54.5 7.9 %collective-permute-start.20 = (bf16[16,1792]{1,0:T(8,128)(2,1)S(1)}, bf16[16,1792]{1,0:T(8,128)(2,1)S(1)}, u32[]{:S(2)}, u32[]{:S(2)}) collective-permute-start(bf16[16,1792]{1,0:T(8,128)(2,1)S(1)} %get-tuple-element.52), channel_id=1, source_target_pairs={{0,4},{1,5},{2,6},{3,7},{4,0},{5,1},{6,2},{7,3},{16,20},{17,21},{1... | collective-permute-start | bytes 172040 | tf_op jit(solution)/shard_map/ppermute | solution.py:70
  58.0 6.1 %collective-permute-start.19 = (bf16[16,1792]{1,0:T(8,128)(2,1)S(1)}, bf16[16,1792]{1,0:T(8,128)(2,1)S(1)}, u32[]{:S(2)}, u32[]{:S(2)}) collective-permute-start(bf16[16,1792]{1,0:T(8,128)(2,1)S(1)} %get-tuple-element.52), channel_id=1, source_target_pairs={{0,2},{1,3},{2,0},{3,1},{4,6},{5,7},{6,4},{7,5},{16,18},{17,19},{1... | collective-permute-start | bytes 172040 | tf_op jit(solution)/shard_map/ppermute | solution.py:70
  60.4 11.6 %collective-permute-start.25 = (bf16[32,1792]{1,0:T(8,128)(2,1)S(1)}, bf16[32,1792]{1,0:T(8,128)(2,1)S(1)}, u32[]{:S(2)}, u32[]{:S(2)}) collective-permute-start(bf16[32,1792]{1,0:T(8,128)(2,1)S(1)} %fusion.8), channel_id=1, source_target_pairs={{8,14},{9,15},{10,12},{11,13},{12,10},{13,11},{14,8},{15,9},{24,30... | collective-permute-start | bytes 344072 | tf_op jit(solution)/shard_map/ppermute | solution.py:70
  61.1 11.0 %collective-permute-start.24 = (bf16[32,1792]{1,0:T(8,128)(2,1)S(1)}, bf16[32,1792]{1,0:T(8,128)(2,1)S(1)}, u32[]{:S(2)}, u32[]{:S(2)}) collective-permute-start(bf16[32,1792]{1,0:T(8,128)(2,1)S(1)} %fusion.8), channel_id=1, source_target_pairs={{8,12},{9,13},{10,14},{11,15},{12,8},{13,9},{14,10},{15,11},{24,28... | collective-permute-start | bytes 344072 | tf_op jit(solution)/shard_map/ppermute | solution.py:70
  61.8 10.3 %collective-permute-start.23 = (bf16[32,1792]{1,0:T(8,128)(2,1)S(1)}, bf16[32,1792]{1,0:T(8,128)(2,1)S(1)}, u32[]{:S(2)}, u32[]{:S(2)}) collective-permute-start(bf16[32,1792]{1,0:T(8,128)(2,1)S(1)} %fusion.8), channel_id=1, source_target_pairs={{8,10},{9,11},{10,8},{11,9},{12,14},{13,15},{14,12},{15,13},{24,26... | collective-permute-start | bytes 344072 | tf_op jit(solution)/shard_map/ppermute | solution.py:70
  62.5 15.8 %collective-permute-start.18 = (bf16[16,896]{1,0:T(8,128)(2,1)S(1)}, bf16[16,896]{1,0:T(8,128)(2,1)S(1)}, u32[]{:S(2)}, u32[]{:S(2)}) collective-permute-start(bf16[16,896]{1,0:T(8,128)(2,1)S(1)} %slice.279), channel_id=1, source_target_pairs={{0,8},{8,0},{16,24},{24,16},{1,9},{9,1},{17,25},{25,17},{2,10},{10... | collective-permute-start | bytes 86024 | tf_op jit(solution)/shard_map/ppermute | solution.py:11
  64.0 7.9 %collective-permute-start.22 = (bf16[64,1792]{1,0:T(8,128)(2,1)S(1)}, bf16[64,1792]{1,0:T(8,128)(2,1)S(1)}, u32[]{:S(2)}, u32[]{:S(2)}) collective-permute-start(bf16[64,1792]{1,0:T(8,128)(2,1)S(1)} %pad_maximum_fusion.4), channel_id=1, source_target_pairs={{0,1},{1,0},{2,3},{3,2},{4,5},{5,4},{6,7},{7,6},{16,17},{17,16},{1... | collective-permute-start | bytes 688136 | tf_op jit(solution)/shard_map/ppermute | solution.py:70
  72.0 7.6 %collective-permute-start.28 = (bf16[128,1792]{1,0:T(8,128)(2,1)S(1)}, bf16[128,1792]{1,0:T(8,128)(2,1)S(1)}, u32[]{:S(2)}, u32[]{:S(2)}) collective-permute-start(bf16[128,1792]{1,0:T(8,128)(2,1)S(1)} %copy-done.2), channel_id=1, source_target_pairs={{0,8},{8,0},{16,24},{24,16},{1,9},{9,1},{17,25},{25,17},{2,10},{10... | collective-permute-start | bytes 1376264 | tf_op jit(solution)/shard_map/ppermute | solution.py:11
  72.9 3.7 %collective-permute-start.27 = (bf16[240,128]{1,0:T(8,128)(2,1)S(1)}, bf16[240,128]{1,0:T(8,128)(2,1)S(1)}, u32[]{:S(2)}, u32[]{:S(2)}) collective-permute-start(bf16[240,128]{1,0:T(8,128)(2,1)S(1)} %get-tuple-element.85), channel_id=1, source_target_pairs={{0,24},{1,25},{2,26},{3,27},{4,28},{5,29},{6,30},{7,31},{8,1},{9,0... | collective-permute-start | bytes 184328 | tf_op jit(solution)/shard_map/ppermute | solution.py:70
  74.0 4.3 %collective-permute-start.26 = (bf16[240,128]{1,0:T(8,128)(2,1)S(1)}, bf16[240,128]{1,0:T(8,128)(2,1)S(1)}, u32[]{:S(2)}, u32[]{:S(2)}) collective-permute-start(bf16[240,128]{1,0:T(8,128)(2,1)S(1)} %get-tuple-element.86), channel_id=1, source_target_pairs={{0,16},{1,17},{2,18},{3,19},{4,20},{5,21},{6,22},{7,23},{8,9},{9,8... | collective-permute-start | bytes 184328 | tf_op jit(solution)/shard_map/ppermute | solution.py:70
  75.6 3.4 %collective-permute-start.29 = (f32[128,128]{1,0:T(8,128)S(1)}, f32[128,128]{1,0:T(8,128)S(1)}, u32[]{:S(2)}, u32[]{:S(2)}) collective-permute-start(f32[128,128]{1,0:T(8,128)S(1)} %slice_select_fusion), channel_id=1, source_target_pairs={{0,8},{8,0},{16,24},{24,16},{1,9},{9,1},{17,25},{25,17},{2,10},{10... | collective-permute-start | bytes 196616 | tf_op jit(solution)/shard_map/ppermute | solution.py:11

commit v13 on v12

--- a/solution.py
+++ b/solution.py
@@ -61,12 +61,11 @@
     latents = enc_weight.shape[2]
     decoder = dec_weight[0].reshape(2, 2 * latents, cols)
 
-    def routed(block, from_core_0=None, from_core_1=None):
+    def routed(block, from_core_0=(0, 0), from_core_1=(0, 0)):
         route = []
         for i in range(count):
             bits = (from_core_0, from_core_1)[i % 2]
-            if bits is not None:
-                route += [(i * slots + j, (i ^ bits[0]) * slots + (j ^ bits[1])) for j in range(slots)]
+            route += [(i * slots + j, (i ^ bits[0]) * slots + (j ^ bits[1])) for j in range(slots)]
         return lax.ppermute(block, ("layer", "latent"), route)
 
     def over_core(block):

time: 81.5 us -> 81.5 us (level)
  no operation moved by 1% of the time
where the time goes in v13:
time: 81.5 us; the launch traced here: 81 us
  starting transfers between devices  44.7 us (55%)
  waiting for transfers between devices  22 us (27%)
  other arithmetic  4.74 us (6%)
  local copies, waits for them, and re-layouts  3.77 us (5%)
  matrix products  3.13 us (4%)
  between operations  2.64 us (3%)
    ppermute x20, starting transfers between devices, routed(): return lax.ppermute(block, ('layer', 'latent'), route)  36.5 us
    ppermute x20, waiting for transfers between devices, routed(): return lax.ppermute(block, ('layer', 'latent'), route)  18.7 us
    ppermute x10, starting transfers between devices, crossed(): lax.ppermute(block, axis, [(i, i ^ mask) for i in range(lax.axis_size(axi...  8.22 us
    ppermute x10, waiting for transfers between devices, crossed(): lax.ppermute(block, axis, [(i, i ^ mask) for i in range(lax.axis_size(axi...  3.34 us
    squeeze x2, local copies, waits for them, and re-layouts, decoder_part(): lax.dynamic_slice(decoder, (which, 0, where * part), (1, 2 * latents, part))  2.41 us
    select_n x3, other arithmetic, both_halves(): jnp.where(half == 0, mine, other)  2.34 us
  transfers between devices with their start and end apart: 30, of which 12 were waited for; matrix products, arithmetic and copies ran while one was open for 12% of the time, Pallas kernels for 0%

profile of v13, /device:TPU:0, one launch (start us, length us, event | category | flops | bytes accessed | tf_op | source)
XLA Modules:
  0.0 81.0 jit_solution(3703070389977079645)
XLA Ops:
  0.6 0.5 collective-permute-start.1
  1.1 0.8 %dynamic-slice_bitcast_fusion.5 = (bf16[1,1,16,1792]{3,2,1,0:T(8,128)(2,1)S(1)}, bf16[16,1792]{1,0:T(8,128)(2,1)S(1)}) fusion(bf16[2,16,3584]{2,1,0:T(8,128)(2,1)} %param.6, s32[]{:T(128)S(6)} %select_n.217, s32[]{:T(128)S(6)} %select_n.218), kind=kLoop, calls=%fused_computation.83 | loop fusion | bytes 172040 | tf_op jit(solution)/shard_map/reshape;squeeze | solution.py:109
  2.0 2.5 %collective-permute-start = (bf16[16,1792]{1,0:T(8,128)(2,1)S(1)}, bf16[16,1792]{1,0:T(8,128)(2,1)S(1)}, u32[]{:S(2)}, u32[]{:S(2)}) collective-permute-start(bf16[16,1792]{1,0:T(8,128)(2,1)S(1)} %get-tuple-element.76), channel_id=1, source_target_pairs={{0,1},{1,0},{2,3},{3,2},{4,5},{5,4},{6,7},{7,6},{8,9},{9,8},{10,11... | collective-permute-start | bytes 172040 | tf_op jit(solution)/shard_map/ppermute | solution.py:11
  4.5 2.3 %dynamic-slice_bitcast_fusion.2 = (bf16[256,896]{1,0:T(8,128)(2,1)}, bf16[256,896]{1,0:T(8,128)(2,1)}) fusion(bf16[2,256,1792]{2,1,0:T(8,128)(2,1)} %bitcast.79, s32[]{:T(128)S(6)} %select_n.224, s32[]{:T(128)S(6)} %select_n.226, s32[]{:T(128)S(6)} %select_n.220, s32[]{:T(128)S(6)} %select_n.222), kind=kLoop, calls=%fused_computation.20 | loop fusion | bytes 1835024 | tf_op jit(solution)/shard_map/squeeze | solution.py:100
  6.8 0.2 collective-permute-start.3
  7.0 1.7 %collective-permute-start.2 = (bf16[256,896]{1,0:T(8,128)(2,1)}, bf16[256,896]{1,0:T(8,128)(2,1)S(1)}, u32[]{:S(2)}, u32[]{:S(2)}) collective-permute-start(bf16[256,896]{1,0:T(8,128)(2,1)} %get-tuple-element.60), channel_id=1, source_target_pairs={{0,16},{1,17},{2,18},{3,19},{4,20},{5,21},{6,22},{7,23},{8,9},{9,8... | collective-permute-start | bytes 1376264 | tf_op jit(solution)/shard_map/ppermute | solution.py:69
  8.7 0.0 collective-permute-done.1
  8.7 3.7 %collective-permute-start.6 = (bf16[32,1792]{1,0:T(8,128)(2,1)S(1)}, bf16[32,1792]{1,0:T(8,128)(2,1)S(1)}, u32[]{:S(2)}, u32[]{:S(2)}) collective-permute-start(bf16[32,1792]{1,0:T(8,128)(2,1)S(1)} %bitcast.86), channel_id=1, source_target_pairs={{0,6},{1,7},{2,4},{3,5},{4,2},{5,3},{6,0},{7,1},{8,14},{9,15},{10,... | collective-permute-start | bytes 344072 | tf_op jit(solution)/shard_map/ppermute | solution.py:11
  12.4 0.0 collective-permute-start.5
  12.4 0.8 collective-permute-start.4
  13.2 2.3 %bitcast_select_fusion.1 = (bf16[1792,128]{1,0:T(8,128)(2,1)}, bf16[1792,128]{1,0:T(8,128)(2,1)}) fusion(pred[]{:T(512)S(6)} %eq.74, bf16[3584,128]{1,0:T(8,128)(2,1)} %collective-permute-done.1, s32[]{:T(128)S(6)} %select_n.218, bf16[1,3584,128]{2,1,0:T(8,128)(2,1)} %param.8), kind=kLoop, calls=%fused_computation.17 | loop fusion | flops 458752 | bytes 1835013 | tf_op jit(solution)/shard_map/jit(_where)/select_n | solution.py:23
  15.4 0.6 compare_reduce_fusion
  17.4 0.0 copy-start.3
  17.4 1.7 %collective-permute-done.3 = bf16[256,896]{1,0:T(8,128)(2,1)S(1)} collective-permute-done((bf16[256,896]{1,0:T(8,128)(2,1)}, bf16[256,896]{1,0:T(8,128)(2,1)S(1)}, u32[]{:S(2)}, u32[]{:S(2)}) %collective-permute-start.3) | collective-permute-done | bytes 458784 | tf_op jit(solution)/shard_map/ppermute | solution.py:69
  19.2 0.7 collective-permute-done.2
  19.9 0.0 collective-permute-done.6
  19.9 2.4 %collective-permute-done.5 = bf16[32,1792]{1,0:T(8,128)(2,1)S(1)} collective-permute-done((bf16[32,1792]{1,0:T(8,128)(2,1)S(1)}, bf16[32,1792]{1,0:T(8,128)(2,1)S(1)}, u32[]{:S(2)}, u32[]{:S(2)}) %collective-permute-start.5) | collective-permute-done | bytes 114720 | tf_op jit(solution)/shard_map/ppermute | solution.py:11
  22.3 0.0 collective-permute-done.4
  22.3 0.1 dynamic-slice_bitcast_fusion.1
  22.4 0.1 collective-permute-start.8
  22.6 0.0 copy-start.5
  22.6 0.3 convolution_add_fusion.1
  22.9 0.6 collective-permute-start.7
  23.5 0.1 constant_dynamic-update-slice_fusion.4
  23.5 0.9 %collective-permute-done.7 = f32[128,256]{1,0:T(8,128)S(1)} collective-permute-done((f32[128,256]{1,0:T(8,128)S(1)}, f32[128,256]{1,0:T(8,128)S(1)}, u32[]{:S(2)}, u32[]{:S(2)}) %collective-permute-start.7) | collective-permute-done | bytes 131104 | tf_op jit(solution)/shard_map/ppermute | solution.py:11
  24.5 0.6 collective-permute-start.9
  25.1 0.7 collective-permute-start.17
  25.8 3.0 %collective-permute-done.9 = bf16[128,256]{1,0:T(8,128)(2,1)S(1)} collective-permute-done((bf16[128,256]{1,0:T(8,128)(2,1)S(1)}, bf16[128,256]{1,0:T(8,128)(2,1)S(1)}, u32[]{:S(2)}, u32[]{:S(2)}) %collective-permute-start.9) | collective-permute-done | bytes 65568 | tf_op jit(solution)/shard_map/ppermute | solution.py:69
  28.9 0.3 fusion.23
  29.2 0.3 fusion.22
  29.6 3.4 %collective-permute-start.10 = (bf16[64,1792]{1,0:T(8,128)(2,1)S(1)}, bf16[64,1792]{1,0:T(8,128)(2,1)S(1)}, u32[]{:S(2)}, u32[]{:S(2)}) collective-permute-start(bf16[64,1792]{1,0:T(8,128)(2,1)S(1)} %bitcast.91), channel_id=1, source_target_pairs={{0,1},{1,0},{2,3},{3,2},{4,5},{5,4},{6,7},{7,6},{8,8},{9,9},{10,10... | collective-permute-start | bytes 688136 | tf_op jit(solution)/shard_map/ppermute | solution.py:69
  33.0 0.7 collective-permute-start.16
  33.7 0.7 collective-permute-start.15
  34.4 0.7 collective-permute-start.14
  35.0 2.4 %collective-permute-done.10 = bf16[64,1792]{1,0:T(8,128)(2,1)S(1)} collective-permute-done((bf16[64,1792]{1,0:T(8,128)(2,1)S(1)}, bf16[64,1792]{1,0:T(8,128)(2,1)S(1)}, u32[]{:S(2)}, u32[]{:S(2)}) %collective-permute-start.10) | collective-permute-done | bytes 229408 | tf_op jit(solution)/shard_map/ppermute | solution.py:69
  37.6 4.5 %collective-permute-start.13 = (bf16[16,1792]{1,0:T(8,128)(2,1)S(1)}, bf16[16,1792]{1,0:T(8,128)(2,1)S(1)}, u32[]{:S(2)}, u32[]{:S(2)}) collective-permute-start(bf16[16,1792]{1,0:T(8,128)(2,1)S(1)} %get-tuple-element.72), channel_id=1, source_target_pairs={{0,6},{1,7},{2,4},{3,5},{4,2},{5,3},{6,0},{7,1},{8,8},{9,9},{10,10... | collective-permute-start | bytes 172040 | tf_op jit(solution)/shard_map/ppermute | solution.py:69
  42.1 1.9 %collective-permute-start.12 = (bf16[16,1792]{1,0:T(8,128)(2,1)S(1)}, bf16[16,1792]{1,0:T(8,128)(2,1)S(1)}, u32[]{:S(2)}, u32[]{:S(2)}) collective-permute-start(bf16[16,1792]{1,0:T(8,128)(2,1)S(1)} %get-tuple-element.73), channel_id=1, source_target_pairs={{0,4},{1,5},{2,6},{3,7},{4,0},{5,1},{6,2},{7,3},{8,8},{9,9},{10,10... | collective-permute-start | bytes 172040 | tf_op jit(solution)/shard_map/ppermute | solution.py:69
  44.0 0.0 collective-permute-done.16
  44.0 3.8 %collective-permute-start.11 = (bf16[16,1792]{1,0:T(8,128)(2,1)S(1)}, bf16[16,1792]{1,0:T(8,128)(2,1)S(1)}, u32[]{:S(2)}, u32[]{:S(2)}) collective-permute-start(bf16[16,1792]{1,0:T(8,128)(2,1)S(1)} %get-tuple-element.74), channel_id=1, source_target_pairs={{0,2},{1,3},{2,0},{3,1},{4,6},{5,7},{6,4},{7,5},{8,8},{9,9},{10,10... | collective-permute-start | bytes 172040 | tf_op jit(solution)/shard_map/ppermute | solution.py:69
  48.0 1.1 %collective-permute-done.12 = bf16[16,1792]{1,0:T(8,128)(2,1)S(1)} collective-permute-done((bf16[16,1792]{1,0:T(8,128)(2,1)S(1)}, bf16[16,1792]{1,0:T(8,128)(2,1)S(1)}, u32[]{:S(2)}, u32[]{:S(2)}) %collective-permute-start.12) | collective-permute-done | bytes 57376 | tf_op jit(solution)/shard_map/ppermute | solution.py:69
  49.1 1.1 %collective-permute-done.11 = bf16[16,1792]{1,0:T(8,128)(2,1)S(1)} collective-permute-done((bf16[16,1792]{1,0:T(8,128)(2,1)S(1)}, bf16[16,1792]{1,0:T(8,128)(2,1)S(1)}, u32[]{:S(2)}, u32[]{:S(2)}) %collective-permute-start.11) | collective-permute-done | bytes 57376 | tf_op jit(solution)/shard_map/ppermute | solution.py:69
  50.1 0.1 fusion.8
  50.2 0.1 fusion.10
  50.3 4.3 %collective-permute-start.21 = (bf16[16,1792]{1,0:T(8,128)(2,1)S(1)}, bf16[16,1792]{1,0:T(8,128)(2,1)S(1)}, u32[]{:S(2)}, u32[]{:S(2)}) collective-permute-start(bf16[16,1792]{1,0:T(8,128)(2,1)S(1)} %get-tuple-element.52), channel_id=1, source_target_pairs={{0,6},{1,7},{2,4},{3,5},{4,2},{5,3},{6,0},{7,1},{8,8},{9,9},{10,10... | collective-permute-start | bytes 172040 | tf_op jit(solution)/shard_map/ppermute | solution.py:69
  54.5 3.4 %collective-permute-start.20 = (bf16[16,1792]{1,0:T(8,128)(2,1)S(1)}, bf16[16,1792]{1,0:T(8,128)(2,1)S(1)}, u32[]{:S(2)}, u32[]{:S(2)}) collective-permute-start(bf16[16,1792]{1,0:T(8,128)(2,1)S(1)} %get-tuple-element.52), channel_id=1, source_target_pairs={{0,4},{1,5},{2,6},{3,7},{4,0},{5,1},{6,2},{7,3},{8,8},{9,9},{10,10... | collective-permute-start | bytes 172040 | tf_op jit(solution)/shard_map/ppermute | solution.py:69
  58.0 2.4 %collective-permute-start.19 = (bf16[16,1792]{1,0:T(8,128)(2,1)S(1)}, bf16[16,1792]{1,0:T(8,128)(2,1)S(1)}, u32[]{:S(2)}, u32[]{:S(2)}) collective-permute-start(bf16[16,1792]{1,0:T(8,128)(2,1)S(1)} %get-tuple-element.52), channel_id=1, source_target_pairs={{0,2},{1,3},{2,0},{3,1},{4,6},{5,7},{6,4},{7,5},{8,8},{9,9},{10,10... | collective-permute-start | bytes 172040 | tf_op jit(solution)/shard_map/ppermute | solution.py:69
  60.4 0.7 collective-permute-start.25
  61.1 0.7 collective-permute-start.24
  61.8 0.7 collective-permute-start.23
  62.5 0.1 collective-permute-start.18
  62.6 1.5 %collective-permute-done.19 = bf16[16,1792]{1,0:T(8,128)(2,1)S(1)} collective-permute-done((bf16[16,1792]{1,0:T(8,128)(2,1)S(1)}, bf16[16,1792]{1,0:T(8,128)(2,1)S(1)}, u32[]{:S(2)}, u32[]{:S(2)}) %collective-permute-start.19) | collective-permute-done | bytes 57376 | tf_op jit(solution)/shard_map/ppermute | solution.py:69
  64.0 3.4 %collective-permute-start.22 = (bf16[64,1792]{1,0:T(8,128)(2,1)S(1)}, bf16[64,1792]{1,0:T(8,128)(2,1)S(1)}, u32[]{:S(2)}, u32[]{:S(2)}) collective-permute-start(bf16[64,1792]{1,0:T(8,128)(2,1)S(1)} %pad_maximum_fusion.4), channel_id=1, source_target_pairs={{0,1},{1,0},{2,3},{3,2},{4,5},{5,4},{6,7},{7,6},{8,8},{9,9},{10,10... | collective-permute-start | bytes 688136 | tf_op jit(solution)/shard_map/ppermute | solution.py:69
  67.5 4.5 %collective-permute-done.22 = bf16[64,1792]{1,0:T(8,128)(2,1)S(1)} collective-permute-done((bf16[64,1792]{1,0:T(8,128)(2,1)S(1)}, bf16[64,1792]{1,0:T(8,128)(2,1)S(1)}, u32[]{:S(2)}, u32[]{:S(2)}) %collective-permute-start.22) | collective-permute-done | bytes 229408 | tf_op jit(solution)/shard_map/ppermute | solution.py:69
  72.1 0.1 maximum_select_fusion
  72.2 0.4 fusion.24
  72.9 0.7 collective-permute-start.27
  73.5 0.4 fusion.7
  74.0 1.6 %collective-permute-start.26 = (bf16[240,128]{1,0:T(8,128)(2,1)S(1)}, bf16[240,128]{1,0:T(8,128)(2,1)S(1)}, u32[]{:S(2)}, u32[]{:S(2)}) collective-permute-start(bf16[240,128]{1,0:T(8,128)(2,1)S(1)} %get-tuple-element.86), channel_id=1, source_target_pairs={{0,16},{1,17},{2,18},{3,19},{4,20},{5,21},{6,22},{7,23},{8,9},{9,8... | collective-permute-start | bytes 184328 | tf_op jit(solution)/shard_map/ppermute | solution.py:69
  75.6 1.0 %collective-permute-done.27 = bf16[240,128]{1,0:T(8,128)(2,1)S(1)} collective-permute-done((bf16[240,128]{1,0:T(8,128)(2,1)S(1)}, bf16[240,128]{1,0:T(8,128)(2,1)S(1)}, u32[]{:S(2)}, u32[]{:S(2)}) %collective-permute-start.27) | collective-permute-done | bytes 61472 | tf_op jit(solution)/shard_map/ppermute | solution.py:69
  76.6 1.7 %collective-permute-done.26 = bf16[240,128]{1,0:T(8,128)(2,1)S(1)} collective-permute-done((bf16[240,128]{1,0:T(8,128)(2,1)S(1)}, bf16[240,128]{1,0:T(8,128)(2,1)S(1)}, u32[]{:S(2)}, u32[]{:S(2)}) %collective-permute-start.26) | collective-permute-done | bytes 61472 | tf_op jit(solution)/shard_map/ppermute | solution.py:69
  78.4 0.6 maximum_bitcast_fusion.1
  79.0 0.6 fusion.16
  79.6 0.1 broadcast_select_fusion.1
  79.6 1.4 %fusion = bf16[1,3584,128]{2,1,0:T(8,128)(2,1)} fusion(bf16[128,1792]{1,0:T(8,128)(2,1)S(1)} %get-tuple-element.62, bf16[128,1792]{1,0:T(8,128)(2,1)S(1)} %get-tuple-element.61, bf16[128,128]{1,0:T(8,128)(2,1)S(1)} %get-tuple-element.50), kind=kOutput, calls=%fused_computation.1 | convolution fusion | flops 119734272 | bytes 1867776 | tf_op jit(solution)/shard_map/dot_general | solution.py:48
  (88 shorter events, 0.8 us)
Async XLA Ops:
  0.6 8.1 %collective-permute-start.1 = (bf16[3584,128]{1,0:T(8,128)(2,1)}, bf16[3584,128]{1,0:T(8,128)(2,1)}, u32[]{:S(2)}, u32[]{:S(2)}) collective-permute-start(bf16[3584,128]{1,0:T(8,128)(2,1)} %bitcast.92), channel_id=1, source_target_pairs={{0,8},{8,0},{16,24},{24,16},{1,9},{9,1},{17,25},{25,17},{2,10},{10... | collective-permute-start | bytes 2752520 | tf_op jit(solution)/shard_map/ppermute | solution.py:11
  2.0 6.7 %collective-permute-start = (bf16[16,1792]{1,0:T(8,128)(2,1)S(1)}, bf16[16,1792]{1,0:T(8,128)(2,1)S(1)}, u32[]{:S(2)}, u32[]{:S(2)}) collective-permute-start(bf16[16,1792]{1,0:T(8,128)(2,1)S(1)} %get-tuple-element.76), channel_id=1, source_target_pairs={{0,1},{1,0},{2,3},{3,2},{4,5},{5,4},{6,7},{7,6},{8,9},{9,8},{10,11... | collective-permute-start | bytes 172040 | tf_op jit(solution)/shard_map/ppermute | solution.py:11
  4.5 10.9 %copy-start.6 = (f32[1,128]{1,0:T(1,128)S(1)}, f32[1,128]{1,0:T(1,128)}, u32[]{:S(2)}) copy-start(f32[1,128]{1,0:T(1,128)} %param.9) | copy-start | bytes 1540
  4.5 10.9 %copy-start.7 = (s32[2,1,12]{2,1,0:T(1,128)S(1)}, s32[2,1,12]{2,1,0:T(1,128)}, u32[]{:S(2)}) copy-start(s32[2,1,12]{2,1,0:T(1,128)} %param.11) | copy-start | bytes 292
  4.5 17.8 %copy-start = (bf16[1,2,2,128,1792]{4,3,2,1,0:T(8,128)(2,1)S(1)}, bf16[1,2,2,128,1792]{4,3,2,1,0:T(8,128)(2,1)}, u32[]{:S(2)}) copy-start(bf16[1,2,2,128,1792]{4,3,2,1,0:T(8,128)(2,1)} %param.10) | copy-start | bytes 5505028
  6.8 12.3 %collective-permute-start.3 = (bf16[256,896]{1,0:T(8,128)(2,1)}, bf16[256,896]{1,0:T(8,128)(2,1)S(1)}, u32[]{:S(2)}, u32[]{:S(2)}) collective-permute-start(bf16[256,896]{1,0:T(8,128)(2,1)} %get-tuple-element.59), channel_id=1, source_target_pairs={{0,9},{1,8},{2,11},{3,10},{4,13},{5,12},{6,15},{7,14},{8,16},{9,17... | collective-permute-start | bytes 1376264 | tf_op jit(solution)/shard_map/ppermute | solution.py:69
  7.0 12.9 %collective-permute-start.2 = (bf16[256,896]{1,0:T(8,128)(2,1)}, bf16[256,896]{1,0:T(8,128)(2,1)S(1)}, u32[]{:S(2)}, u32[]{:S(2)}) collective-permute-start(bf16[256,896]{1,0:T(8,128)(2,1)} %get-tuple-element.60), channel_id=1, source_target_pairs={{0,16},{1,17},{2,18},{3,19},{4,20},{5,21},{6,22},{7,23},{8,9},{9,8... | collective-permute-start | bytes 1376264 | tf_op jit(solution)/shard_map/ppermute | solution.py:69
  8.7 11.2 %collective-permute-start.6 = (bf16[32,1792]{1,0:T(8,128)(2,1)S(1)}, bf16[32,1792]{1,0:T(8,128)(2,1)S(1)}, u32[]{:S(2)}, u32[]{:S(2)}) collective-permute-start(bf16[32,1792]{1,0:T(8,128)(2,1)S(1)} %bitcast.86), channel_id=1, source_target_pairs={{0,6},{1,7},{2,4},{3,5},{4,2},{5,3},{6,0},{7,1},{8,14},{9,15},{10,... | collective-permute-start | bytes 344072 | tf_op jit(solution)/shard_map/ppermute | solution.py:11
  12.4 9.9 %collective-permute-start.5 = (bf16[32,1792]{1,0:T(8,128)(2,1)S(1)}, bf16[32,1792]{1,0:T(8,128)(2,1)S(1)}, u32[]{:S(2)}, u32[]{:S(2)}) collective-permute-start(bf16[32,1792]{1,0:T(8,128)(2,1)S(1)} %bitcast.87), channel_id=1, source_target_pairs={{0,4},{1,5},{2,6},{3,7},{4,0},{5,1},{6,2},{7,3},{8,12},{9,13},{10,... | collective-permute-start | bytes 344072 | tf_op jit(solution)/shard_map/ppermute | solution.py:11
  12.4 9.9 %collective-permute-start.4 = (bf16[32,1792]{1,0:T(8,128)(2,1)S(1)}, bf16[32,1792]{1,0:T(8,128)(2,1)S(1)}, u32[]{:S(2)}, u32[]{:S(2)}) collective-permute-start(bf16[32,1792]{1,0:T(8,128)(2,1)S(1)} %bitcast.88), channel_id=1, source_target_pairs={{0,2},{1,3},{2,0},{3,1},{4,6},{5,7},{6,4},{7,5},{8,10},{9,11},{10,... | collective-permute-start | bytes 344072 | tf_op jit(solution)/shard_map/ppermute | solution.py:11
  17.4 5.1 %copy-start.3 = (bf16[1792,128]{1,0:T(8,128)(2,1)S(1)}, bf16[1792,128]{1,0:T(8,128)(2,1)}, u32[]{:S(2)}) copy-start(bf16[1792,128]{1,0:T(8,128)(2,1)} %get-tuple-element.57) | copy-start | bytes 1376260
  17.4 5.1 %copy-start.4 = (bf16[1792,128]{1,0:T(8,128)(2,1)S(1)}, bf16[1792,128]{1,0:T(8,128)(2,1)}, u32[]{:S(2)}) copy-start(bf16[1792,128]{1,0:T(8,128)(2,1)} %get-tuple-element.58) | copy-start | bytes 1376260
  22.4 6.8 %collective-permute-start.8 = (bf16[256,896]{1,0:T(8,128)(2,1)S(1)}, bf16[256,896]{1,0:T(8,128)(2,1)S(1)}, u32[]{:S(2)}, u32[]{:S(2)}) collective-permute-start(bf16[256,896]{1,0:T(8,128)(2,1)S(1)} %get-tuple-element.56), channel_id=1, source_target_pairs={{0,8},{8,0},{16,24},{24,16},{1,9},{9,1},{17,25},{25,17},{2,10},{10... | collective-permute-start | bytes 1376264 | tf_op jit(solution)/shard_map/ppermute | solution.py:11
  22.5 1.0 %copy-start.1 = (bf16[128,1792]{1,0:T(8,128)(2,1)}, bf16[128,1792]{1,0:T(8,128)(2,1)S(1)}, u32[]{:S(2)}) copy-start(bf16[128,1792]{1,0:T(8,128)(2,1)S(1)} %constant_dynamic-update-slice_fusion) | copy-start | bytes 1376260
  22.6 2.6 %copy-start.5 = (bf16[3,16,3584]{2,1,0:T(8,128)(2,1)S(1)}, bf16[3,16,3584]{2,1,0:T(8,128)(2,1)}, u32[]{:S(2)}) copy-start(bf16[3,16,3584]{2,1,0:T(8,128)(2,1)} %param.7) | copy-start | bytes 1032196
  22.9 1.6 %collective-permute-start.7 = (f32[128,256]{1,0:T(8,128)S(1)}, f32[128,256]{1,0:T(8,128)S(1)}, u32[]{:S(2)}, u32[]{:S(2)}) collective-permute-start(f32[128,256]{1,0:T(8,128)S(1)} %convolution_add_fusion.1), channel_id=1, source_target_pairs={{0,8},{8,0},{16,24},{24,16},{1,9},{9,1},{17,25},{25,17},{2,10},{10... | collective-permute-start | bytes 393224 | tf_op jit(solution)/shard_map/ppermute | solution.py:11
  24.5 4.3 %collective-permute-start.9 = (bf16[128,256]{1,0:T(8,128)(2,1)S(1)}, bf16[128,256]{1,0:T(8,128)(2,1)S(1)}, u32[]{:S(2)}, u32[]{:S(2)}) collective-permute-start(bf16[128,256]{1,0:T(8,128)(2,1)S(1)} %bitcast_select_fusion.3), channel_id=1, source_target_pairs={{0,16},{1,17},{2,18},{3,19},{4,20},{5,21},{6,22},{7,23},{8,9},{9,8... | collective-permute-start | bytes 196616 | tf_op jit(solution)/shard_map/ppermute | solution.py:69
  25.1 17.0 %collective-permute-start.17 = (bf16[16,1792]{1,0:T(8,128)(2,1)S(1)}, bf16[16,1792]{1,0:T(8,128)(2,1)S(1)}, u32[]{:S(2)}, u32[]{:S(2)}) collective-permute-start(bf16[16,1792]{1,0:T(8,128)(2,1)S(1)} %pad_maximum_fusion.9), channel_id=1, source_target_pairs={{0,0},{1,1},{2,2},{3,3},{4,4},{5,5},{6,6},{7,7},{8,9},{9,8},{10,11... | collective-permute-start | bytes 172040 | tf_op jit(solution)/shard_map/ppermute | solution.py:69
  29.6 7.9 %collective-permute-start.10 = (bf16[64,1792]{1,0:T(8,128)(2,1)S(1)}, bf16[64,1792]{1,0:T(8,128)(2,1)S(1)}, u32[]{:S(2)}, u32[]{:S(2)}) collective-permute-start(bf16[64,1792]{1,0:T(8,128)(2,1)S(1)} %bitcast.91), channel_id=1, source_target_pairs={{0,1},{1,0},{2,3},{3,2},{4,5},{5,4},{6,7},{7,6},{8,8},{9,9},{10,10... | collective-permute-start | bytes 688136 | tf_op jit(solution)/shard_map/ppermute | solution.py:69
  33.0 11.0 %collective-permute-start.16 = (bf16[32,1792]{1,0:T(8,128)(2,1)S(1)}, bf16[32,1792]{1,0:T(8,128)(2,1)S(1)}, u32[]{:S(2)}, u32[]{:S(2)}) collective-permute-start(bf16[32,1792]{1,0:T(8,128)(2,1)S(1)} %get-tuple-element.63), channel_id=1, source_target_pairs={{0,0},{1,1},{2,2},{3,3},{4,4},{5,5},{6,6},{7,7},{8,14},{9,15},{10,... | collective-permute-start | bytes 344072 | tf_op jit(solution)/shard_map/ppermute | solution.py:69
  33.7 14.2 %collective-permute-start.15 = (bf16[32,1792]{1,0:T(8,128)(2,1)S(1)}, bf16[32,1792]{1,0:T(8,128)(2,1)S(1)}, u32[]{:S(2)}, u32[]{:S(2)}) collective-permute-start(bf16[32,1792]{1,0:T(8,128)(2,1)S(1)} %get-tuple-element.64), channel_id=1, source_target_pairs={{0,0},{1,1},{2,2},{3,3},{4,4},{5,5},{6,6},{7,7},{8,12},{9,13},{10,... | collective-permute-start | bytes 344072 | tf_op jit(solution)/shard_map/ppermute | solution.py:69
  34.4 13.6 %collective-permute-start.14 = (bf16[32,1792]{1,0:T(8,128)(2,1)S(1)}, bf16[32,1792]{1,0:T(8,128)(2,1)S(1)}, u32[]{:S(2)}, u32[]{:S(2)}) collective-permute-start(bf16[32,1792]{1,0:T(8,128)(2,1)S(1)} %get-tuple-element.65), channel_id=1, source_target_pairs={{0,0},{1,1},{2,2},{3,3},{4,4},{5,5},{6,6},{7,7},{8,10},{9,11},{10,... | collective-permute-start | bytes 344072 | tf_op jit(solution)/shard_map/ppermute | solution.py:69
  37.5 34.4 %copy-start.2 = (bf16[128,1792]{1,0:T(8,128)(2,1)S(1)}, bf16[128,1792]{1,0:T(8,128)(2,1)}, u32[]{:S(2)}) copy-start(bf16[128,1792]{1,0:T(8,128)(2,1)} %copy-done.1) | copy-start | bytes 1376260
  37.6 10.4 %collective-permute-start.13 = (bf16[16,1792]{1,0:T(8,128)(2,1)S(1)}, bf16[16,1792]{1,0:T(8,128)(2,1)S(1)}, u32[]{:S(2)}, u32[]{:S(2)}) collective-permute-start(bf16[16,1792]{1,0:T(8,128)(2,1)S(1)} %get-tuple-element.72), channel_id=1, source_target_pairs={{0,6},{1,7},{2,4},{3,5},{4,2},{5,3},{6,0},{7,1},{8,8},{9,9},{10,10... | collective-permute-start | bytes 172040 | tf_op jit(solution)/shard_map/ppermute | solution.py:69
  42.1 7.0 %collective-permute-start.12 = (bf16[16,1792]{1,0:T(8,128)(2,1)S(1)}, bf16[16,1792]{1,0:T(8,128)(2,1)S(1)}, u32[]{:S(2)}, u32[]{:S(2)}) collective-permute-start(bf16[16,1792]{1,0:T(8,128)(2,1)S(1)} %get-tuple-element.73), channel_id=1, source_target_pairs={{0,4},{1,5},{2,6},{3,7},{4,0},{5,1},{6,2},{7,3},{8,8},{9,9},{10,10... | collective-permute-start | bytes 172040 | tf_op jit(solution)/shard_map/ppermute | solution.py:69
  44.0 6.1 %collective-permute-start.11 = (bf16[16,1792]{1,0:T(8,128)(2,1)S(1)}, bf16[16,1792]{1,0:T(8,128)(2,1)S(1)}, u32[]{:S(2)}, u32[]{:S(2)}) collective-permute-start(bf16[16,1792]{1,0:T(8,128)(2,1)S(1)} %get-tuple-element.74), channel_id=1, source_target_pairs={{0,2},{1,3},{2,0},{3,1},{4,6},{5,7},{6,4},{7,5},{8,8},{9,9},{10,10... | collective-permute-start | bytes 172040 | tf_op jit(solution)/shard_map/ppermute | solution.py:69
  50.3 11.5 %collective-permute-start.21 = (bf16[16,1792]{1,0:T(8,128)(2,1)S(1)}, bf16[16,1792]{1,0:T(8,128)(2,1)S(1)}, u32[]{:S(2)}, u32[]{:S(2)}) collective-permute-start(bf16[16,1792]{1,0:T(8,128)(2,1)S(1)} %get-tuple-element.52), channel_id=1, source_target_pairs={{0,6},{1,7},{2,4},{3,5},{4,2},{5,3},{6,0},{7,1},{8,8},{9,9},{10,10... | collective-permute-start | bytes 172040 | tf_op jit(solution)/shard_map/ppermute | solution.py:69
  54.5 7.9 %collective-permute-start.20 = (bf16[16,1792]{1,0:T(8,128)(2,1)S(1)}, bf16[16,1792]{1,0:T(8,128)(2,1)S(1)}, u32[]{:S(2)}, u32[]{:S(2)}) collective-permute-start(bf16[16,1792]{1,0:T(8,128)(2,1)S(1)} %get-tuple-element.52), channel_id=1, source_target_pairs={{0,4},{1,5},{2,6},{3,7},{4,0},{5,1},{6,2},{7,3},{8,8},{9,9},{10,10... | collective-permute-start | bytes 172040 | tf_op jit(solution)/shard_map/ppermute | solution.py:69
  58.0 6.1 %collective-permute-start.19 = (bf16[16,1792]{1,0:T(8,128)(2,1)S(1)}, bf16[16,1792]{1,0:T(8,128)(2,1)S(1)}, u32[]{:S(2)}, u32[]{:S(2)}) collective-permute-start(bf16[16,1792]{1,0:T(8,128)(2,1)S(1)} %get-tuple-element.52), channel_id=1, source_target_pairs={{0,2},{1,3},{2,0},{3,1},{4,6},{5,7},{6,4},{7,5},{8,8},{9,9},{10,10... | collective-permute-start | bytes 172040 | tf_op jit(solution)/shard_map/ppermute | solution.py:69
  60.4 11.6 %collective-permute-start.25 = (bf16[32,1792]{1,0:T(8,128)(2,1)S(1)}, bf16[32,1792]{1,0:T(8,128)(2,1)S(1)}, u32[]{:S(2)}, u32[]{:S(2)}) collective-permute-start(bf16[32,1792]{1,0:T(8,128)(2,1)S(1)} %fusion.8), channel_id=1, source_target_pairs={{0,0},{1,1},{2,2},{3,3},{4,4},{5,5},{6,6},{7,7},{8,14},{9,15},{10,... | collective-permute-start | bytes 344072 | tf_op jit(solution)/shard_map/ppermute | solution.py:69
  61.1 11.0 %collective-permute-start.24 = (bf16[32,1792]{1,0:T(8,128)(2,1)S(1)}, bf16[32,1792]{1,0:T(8,128)(2,1)S(1)}, u32[]{:S(2)}, u32[]{:S(2)}) collective-permute-start(bf16[32,1792]{1,0:T(8,128)(2,1)S(1)} %fusion.8), channel_id=1, source_target_pairs={{0,0},{1,1},{2,2},{3,3},{4,4},{5,5},{6,6},{7,7},{8,12},{9,13},{10,... | collective-permute-start | bytes 344072 | tf_op jit(solution)/shard_map/ppermute | solution.py:69
  61.8 10.3 %collective-permute-start.23 = (bf16[32,1792]{1,0:T(8,128)(2,1)S(1)}, bf16[32,1792]{1,0:T(8,128)(2,1)S(1)}, u32[]{:S(2)}, u32[]{:S(2)}) collective-permute-start(bf16[32,1792]{1,0:T(8,128)(2,1)S(1)} %fusion.8), channel_id=1, source_target_pairs={{0,0},{1,1},{2,2},{3,3},{4,4},{5,5},{6,6},{7,7},{8,10},{9,11},{10,... | collective-permute-start | bytes 344072 | tf_op jit(solution)/shard_map/ppermute | solution.py:69
  62.5 15.8 %collective-permute-start.18 = (bf16[16,896]{1,0:T(8,128)(2,1)S(1)}, bf16[16,896]{1,0:T(8,128)(2,1)S(1)}, u32[]{:S(2)}, u32[]{:S(2)}) collective-permute-start(bf16[16,896]{1,0:T(8,128)(2,1)S(1)} %slice.279), channel_id=1, source_target_pairs={{0,8},{8,0},{16,24},{24,16},{1,9},{9,1},{17,25},{25,17},{2,10},{10... | collective-permute-start | bytes 86024 | tf_op jit(solution)/shard_map/ppermute | solution.py:11
  64.0 7.9 %collective-permute-start.22 = (bf16[64,1792]{1,0:T(8,128)(2,1)S(1)}, bf16[64,1792]{1,0:T(8,128)(2,1)S(1)}, u32[]{:S(2)}, u32[]{:S(2)}) collective-permute-start(bf16[64,1792]{1,0:T(8,128)(2,1)S(1)} %pad_maximum_fusion.4), channel_id=1, source_target_pairs={{0,1},{1,0},{2,3},{3,2},{4,5},{5,4},{6,7},{7,6},{8,8},{9,9},{10,10... | collective-permute-start | bytes 688136 | tf_op jit(solution)/shard_map/ppermute | solution.py:69
  72.0 7.6 %collective-permute-start.28 = (bf16[128,1792]{1,0:T(8,128)(2,1)S(1)}, bf16[128,1792]{1,0:T(8,128)(2,1)S(1)}, u32[]{:S(2)}, u32[]{:S(2)}) collective-permute-start(bf16[128,1792]{1,0:T(8,128)(2,1)S(1)} %copy-done.2), channel_id=1, source_target_pairs={{0,8},{8,0},{16,24},{24,16},{1,9},{9,1},{17,25},{25,17},{2,10},{10... | collective-permute-start | bytes 1376264 | tf_op jit(solution)/shard_map/ppermute | solution.py:11
  72.9 3.7 %collective-permute-start.27 = (bf16[240,128]{1,0:T(8,128)(2,1)S(1)}, bf16[240,128]{1,0:T(8,128)(2,1)S(1)}, u32[]{:S(2)}, u32[]{:S(2)}) collective-permute-start(bf16[240,128]{1,0:T(8,128)(2,1)S(1)} %get-tuple-element.85), channel_id=1, source_target_pairs={{0,24},{1,25},{2,26},{3,27},{4,28},{5,29},{6,30},{7,31},{8,1},{9,0... | collective-permute-start | bytes 184328 | tf_op jit(solution)/shard_map/ppermute | solution.py:69
  74.0 4.3 %collective-permute-start.26 = (bf16[240,128]{1,0:T(8,128)(2,1)S(1)}, bf16[240,128]{1,0:T(8,128)(2,1)S(1)}, u32[]{:S(2)}, u32[]{:S(2)}) collective-permute-start(bf16[240,128]{1,0:T(8,128)(2,1)S(1)} %get-tuple-element.86), channel_id=1, source_target_pairs={{0,16},{1,17},{2,18},{3,19},{4,20},{5,21},{6,22},{7,23},{8,9},{9,8... | collective-permute-start | bytes 184328 | tf_op jit(solution)/shard_map/ppermute | solution.py:69
  75.6 3.4 %collective-permute-start.29 = (f32[128,128]{1,0:T(8,128)S(1)}, f32[128,128]{1,0:T(8,128)S(1)}, u32[]{:S(2)}, u32[]{:S(2)}) collective-permute-start(f32[128,128]{1,0:T(8,128)S(1)} %slice_select_fusion), channel_id=1, source_target_pairs={{0,8},{8,0},{16,24},{24,16},{1,9},{9,1},{17,25},{25,17},{2,10},{10... | collective-permute-start | bytes 196616 | tf_op jit(solution)/shard_map/ppermute | solution.py:11

commit v14 on v8

--- a/solution.py
+++ b/solution.py
@@ -76,13 +76,23 @@
             out[k] = crossed(block, "latent", 2 * k)
         return out
 
-    def sent_along_z(total):
+    def both_along_z(shared, own):
+        count = shared[1].shape[0]
+        out = [[shared[0]] + [None] * (far - 1), [own[0]] + [None] * (far - 1)]
+        for k in range(far - 1, 1, -1):
+            out[0][k] = crossed(shared[k], "latent", 2 * k)
+        nearest = crossed(jnp.concatenate([shared[1], own[1]], axis=0), "latent", 2)
+        out[0][1], out[1][1] = nearest[:count], nearest[count:]
+        for k in range(far - 1, 1, -1):
+            out[1][k] = crossed(own[k], "latent", 2 * k)
+        return out
+
+    def pieces_of(total):
         count = total.shape[0] // far
-        pieces = [total[k * count:(k + 1) * count].astype(BF16) for k in range(1, far)]
-        return [crossed(pieces[k - 1], "latent", 2 * k) for k in range(1, far)] + [total[:count]]
+        return [total[:count]] + [total[k * count:(k + 1) * count].astype(BF16) for k in range(1, far)]
 
     def added(terms):
-        return sum(term.astype(F32) for term in terms[::-1])
+        return sum(term.astype(F32) for term in terms)
 
     def decoder_part(decoder, which, where):
         return lax.dynamic_slice(decoder, (which, 0, where * part), (1, 2 * latents, part))[0]
@@ -131,14 +141,12 @@
     arrived = over_x(leaving.astype(BF16))
     product = times(acts, own_mine) + times(acts_x, own_other)
     arrived, staying = hold((arrived, staying))
-    own_terms = sent_along_z(product)
-    shared_terms = sent_along_z(staying + arrived.astype(F32))
+    shared_terms, own_terms = both_along_z(pieces_of(staying + arrived.astype(F32)), pieces_of(product))
     terms = hold((*shared_terms, *own_terms))
-    shared_terms, own_terms = terms[:far], terms[far:]
-    err_own = (added(own_terms) - paired(aim_own(side), aim_other).astype(F32)).astype(BF16)
+    err_shared = (added(terms[:far]) - aim_shared.astype(F32)).astype(BF16)
+    err_own = (added(terms[far:]) - paired(aim_own(side), aim_other).astype(F32)).astype(BF16)
+
     own_column = along_z(err_own)
-    err_shared = (added(shared_terms) - aim_shared.astype(F32)).astype(BF16)
-
     shared_near = jnp.concatenate(along_z(err_shared), axis=0)
     resid_swapped, _ = hold((resid_half, shared_near))
     resid_other = over_core(resid_swapped)
@@ -155,6 +163,7 @@
     )
     lower, upper = grads[:, :latents], grads[:, latents:]
     grads = jnp.where(half == 0, lower, upper) + over_core(jnp.where(half == 0, upper, lower))
+
 
     def with_errors(grad, block):
         tiles = [block[:, at:at + latents] for at in range(0, part, latents)]

time: 68.7 us -> 67.9 us (0.988)
  starting transfers between devices: 34.9 us -> 33.3 us
  waiting for transfers between devices: 19.7 us -> 20.5 us
    ppermute x29 -> x28, starting transfers between devices: 34.9 us -> 33.3 us  [crossed(): lax.ppermute(block, axis, [(i, i ^ mask) for i in range(lax.axis_size(axi...]
    ppermute x29 -> x28, waiting for transfers between devices: 19.7 us -> 20.5 us  [crossed(): lax.ppermute(block, axis, [(i, i ^ mask) for i in range(lax.axis_size(axi...]
  transfers between devices with their start and end apart: 29 -> 28, of which waited for: 12 -> 11; matrix products, arithmetic and copies ran while one was open for 11% -> 11% of each run, Pallas kernels for 0% -> 0%
where the time goes in v14:
time: 67.9 us; the launch traced here: 67.5 us
  starting transfers between devices  33.3 us (49%)
  waiting for transfers between devices  20.5 us (30%)
  matrix products  4.17 us (6%)
  local copies, waits for them, and re-layouts  3.98 us (6%)
  other arithmetic  3.18 us (5%)
  between operations  2.45 us (4%)
    ppermute x28, starting transfers between devices, crossed(): lax.ppermute(block, axis, [(i, i ^ mask) for i in range(lax.axis_size(axi...  33.3 us
    ppermute x28, waiting for transfers between devices, crossed(): lax.ppermute(block, axis, [(i, i ^ mask) for i in range(lax.axis_size(axi...  20.5 us
    squeeze x1, local copies, waits for them, and re-layouts, decoder_part(): lax.dynamic_slice(decoder, (which, 0, where * part), (1, 2 * latents, part))  2.01 us
    dot_general x7, matrix products, times(): return jnp.dot(left, right, preferred_element_type=F32)  1.61 us
    another operation x2, local copies, waits for them, and re-layouts, paired(): block.reshape(-1, 1, rows, block.shape[1])  1.6 us
    dot_general x1, matrix products, encoder_gradient(): lax.dot_general(whole, grad_low, (((0,), (0,)), ((), ())), preferred_elem...  1.37 us
  transfers between devices with their start and end apart: 28, of which 11 were waited for; matrix products, arithmetic and copies ran while one was open for 11% of the time, Pallas kernels for 0%

profile of v14, /device:TPU:0, one launch (start us, length us, event | category | flops | bytes accessed | tf_op | source)
XLA Modules:
  0.0 67.5 jit_solution(12131010790182610882)
XLA Ops:
  0.6 0.5 collective-permute-start.3
  1.2 0.8 %dynamic-slice_bitcast_fusion.3 = (bf16[1,1,16,1792]{3,2,1,0:T(8,128)(2,1)S(1)}, bf16[16,1792]{1,0:T(8,128)(2,1)S(1)}) fusion(bf16[2,16,3584]{2,1,0:T(8,128)(2,1)} %param.6, s32[]{:T(128)S(6)} %select_n.156, s32[]{:T(128)S(6)} %select_n.161), kind=kLoop, calls=%fused_computation.90 | loop fusion | bytes 172040 | tf_op jit(solution)/shard_map/reshape;squeeze | solution.py:107
  2.0 2.6 %collective-permute-start.2 = (bf16[16,1792]{1,0:T(8,128)(2,1)S(1)}, bf16[16,1792]{1,0:T(8,128)(2,1)S(1)}, u32[]{:S(2)}, u32[]{:S(2)}) collective-permute-start(bf16[16,1792]{1,0:T(8,128)(2,1)S(1)} %get-tuple-element.67), channel_id=1, source_target_pairs={{0,1},{1,0},{2,3},{3,2},{4,5},{5,4},{6,7},{7,6},{8,9},{9,8},{10,11... | collective-permute-start | bytes 172040 | tf_op jit(solution)/shard_map/ppermute | solution.py:11
  4.6 2.0 %dynamic-slice_bitcast_fusion = (bf16[256,896]{1,0:T(8,128)(2,1)}, bf16[256,896]{1,0:T(8,128)(2,1)S(1)}) fusion(bf16[2,256,1792]{2,1,0:T(8,128)(2,1)} %bitcast.117, s32[]{:T(128)S(6)} %select_n.158, s32[]{:T(128)S(6)} %select_n.159, s32[]{:T(128)S(6)} %select_n.156, s32[]{:T(128)S(6)} %select_n.157), kind=kLoop, calls=%fused_computation.24 | loop fusion | bytes 1835024 | tf_op jit(solution)/shard_map/squeeze | solution.py:98
  6.6 1.5 %collective-permute-start.1 = (bf16[256,896]{1,0:T(8,128)(2,1)}, bf16[256,896]{1,0:T(8,128)(2,1)S(1)}, u32[]{:S(2)}, u32[]{:S(2)}) collective-permute-start(bf16[256,896]{1,0:T(8,128)(2,1)} %get-tuple-element.57), channel_id=1, source_target_pairs={{0,16},{8,24},{16,0},{24,8},{1,17},{9,25},{17,1},{25,9},{2,18},{10... | collective-permute-start | bytes 1376264 | tf_op jit(solution)/shard_map/ppermute | solution.py:11
  8.2 0.5 collective-permute-start
  8.7 0.0 collective-permute-done.2
  8.7 0.0 collective-permute-done.3
  8.7 3.7 %collective-permute-start.6 = (bf16[32,1792]{1,0:T(8,128)(2,1)S(1)}, bf16[32,1792]{1,0:T(8,128)(2,1)S(1)}, u32[]{:S(2)}, u32[]{:S(2)}) collective-permute-start(bf16[32,1792]{1,0:T(8,128)(2,1)S(1)} %bitcast.128), channel_id=1, source_target_pairs={{0,6},{1,7},{2,4},{3,5},{4,2},{5,3},{6,0},{7,1},{8,14},{9,15},{10,... | collective-permute-start | bytes 344072 | tf_op jit(solution)/shard_map/ppermute | solution.py:11
  12.4 0.8 %collective-permute-start.4 = (bf16[32,1792]{1,0:T(8,128)(2,1)S(1)}, bf16[32,1792]{1,0:T(8,128)(2,1)S(1)}, u32[]{:S(2)}, u32[]{:S(2)}) collective-permute-start(bf16[32,1792]{1,0:T(8,128)(2,1)S(1)} %bitcast.130), channel_id=1, source_target_pairs={{0,2},{1,3},{2,0},{3,1},{4,6},{5,7},{6,4},{7,5},{8,10},{9,11},{10,... | collective-permute-start | bytes 344072 | tf_op jit(solution)/shard_map/ppermute | solution.py:11
  13.2 0.2 bitcast_select_fusion.1
  13.4 0.0 copy-start.3
  13.4 0.0 copy-start
  13.4 5.9 %collective-permute-done.1 = bf16[256,896]{1,0:T(8,128)(2,1)S(1)} collective-permute-done((bf16[256,896]{1,0:T(8,128)(2,1)}, bf16[256,896]{1,0:T(8,128)(2,1)S(1)}, u32[]{:S(2)}, u32[]{:S(2)}) %collective-permute-start.1) | collective-permute-done | bytes 458784 | tf_op jit(solution)/shard_map/ppermute | solution.py:11
  19.3 1.0 %collective-permute-done = bf16[256,896]{1,0:T(8,128)(2,1)S(1)} collective-permute-done((bf16[256,896]{1,0:T(8,128)(2,1)S(1)}, bf16[256,896]{1,0:T(8,128)(2,1)S(1)}, u32[]{:S(2)}, u32[]{:S(2)}) %collective-permute-start) | collective-permute-done | bytes 458784 | tf_op jit(solution)/shard_map/ppermute | solution.py:11
  20.4 0.0 collective-permute-done.6
  20.4 1.4 %collective-permute-done.5 = bf16[32,1792]{1,0:T(8,128)(2,1)S(1)} collective-permute-done((bf16[32,1792]{1,0:T(8,128)(2,1)S(1)}, bf16[32,1792]{1,0:T(8,128)(2,1)S(1)}, u32[]{:S(2)}, u32[]{:S(2)}) %collective-permute-start.5) | collective-permute-done | bytes 114720 | tf_op jit(solution)/shard_map/ppermute | solution.py:11
  21.7 0.0 collective-permute-done.4
  21.8 0.3 convolution_add_fusion.4
  22.1 0.1 collective-permute-start.7
  22.3 0.6 compare_reduce_fusion
  24.3 0.6 collective-permute-start.8
  24.9 1.6 %collective-permute-start.10 = (bf16[128,256]{1,0:T(8,128)(2,1)S(1)}, bf16[128,256]{1,0:T(8,128)(2,1)S(1)}, u32[]{:S(2)}, u32[]{:S(2)}) collective-permute-start(bf16[128,256]{1,0:T(8,128)(2,1)S(1)} %bitcast.141), channel_id=1, source_target_pairs={{0,1},{1,0},{2,3},{3,2},{4,5},{5,4},{6,7},{7,6},{8,9},{9,8},{10,11... | collective-permute-start | bytes 196616 | tf_op jit(solution)/shard_map/ppermute | solution.py:11
  26.4 0.8 %dynamic-slice_bitcast_fusion.5 = (bf16[1,1,16,896]{3,2,1,0:T(8,128)(2,1)S(1)}, bf16[16,896]{1,0:T(8,128)(2,1)S(1)}) fusion(bf16[3,16,3584]{2,1,0:T(8,128)(2,1)} %param.7, s32[]{:T(128)S(6)} %select_n.170, s32[]{:T(128)S(6)} %select_n.171, s32[]{:T(128)S(6)} %select_n.172), kind=kLoop, calls=%fused_computation.98 | loop fusion | bytes 114700 | tf_op jit(solution)/shard_map/reshape;squeeze | solution.py:107
  27.2 0.5 collective-permute-start.16
  27.7 0.2 fusion.14
  27.9 0.2 fusion.12
  28.1 0.6 collective-permute-done.8
  28.8 0.2 fusion.1
  29.0 1.6 %collective-permute-start.9 = (bf16[64,896]{1,0:T(8,128)(2,1)S(1)}, bf16[64,896]{1,0:T(8,128)(2,1)S(1)}, u32[]{:S(2)}, u32[]{:S(2)}) collective-permute-start(bf16[64,896]{1,0:T(8,128)(2,1)S(1)} %fusion.1), channel_id=1, source_target_pairs={{0,1},{1,0},{2,3},{3,2},{4,5},{5,4},{6,7},{7,6},{8,9},{9,8},{10,11... | collective-permute-start | bytes 344072 | tf_op jit(solution)/shard_map/ppermute | solution.py:11
  30.6 0.2 fusion.46
  30.8 0.2 fusion.45
  31.1 2.5 %collective-permute-start.15 = (bf16[32,896]{1,0:T(8,128)(2,1)S(1)}, bf16[32,896]{1,0:T(8,128)(2,1)S(1)}, u32[]{:S(2)}, u32[]{:S(2)}) collective-permute-start(bf16[32,896]{1,0:T(8,128)(2,1)S(1)} %get-tuple-element.63), channel_id=1, source_target_pairs={{0,6},{1,7},{2,4},{3,5},{4,2},{5,3},{6,0},{7,1},{8,14},{9,15},{10,... | collective-permute-start | bytes 172040 | tf_op jit(solution)/shard_map/ppermute | solution.py:11
  33.6 0.2 convolution_add_fusion.1
  33.8 0.0 collective-permute-done.9
  33.9 2.5 %collective-permute-start.13 = (bf16[16,896]{1,0:T(8,128)(2,1)S(1)}, bf16[16,896]{1,0:T(8,128)(2,1)S(1)}, u32[]{:S(2)}, u32[]{:S(2)}) collective-permute-start(bf16[16,896]{1,0:T(8,128)(2,1)S(1)} %get-tuple-element.70), channel_id=1, source_target_pairs={{0,6},{1,7},{2,4},{3,5},{4,2},{5,3},{6,0},{7,1},{8,14},{9,15},{10,... | collective-permute-start | bytes 86024 | tf_op jit(solution)/shard_map/ppermute | solution.py:11
  36.4 0.9 %collective-permute-start.12 = (bf16[16,896]{1,0:T(8,128)(2,1)S(1)}, bf16[16,896]{1,0:T(8,128)(2,1)S(1)}, u32[]{:S(2)}, u32[]{:S(2)}) collective-permute-start(bf16[16,896]{1,0:T(8,128)(2,1)S(1)} %get-tuple-element.71), channel_id=1, source_target_pairs={{0,4},{1,5},{2,6},{3,7},{4,0},{5,1},{6,2},{7,3},{8,12},{9,13},{10,... | collective-permute-start | bytes 86024 | tf_op jit(solution)/shard_map/ppermute | solution.py:11
  37.3 1.1 %collective-permute-start.11 = (bf16[48,896]{1,0:T(8,128)(2,1)S(1)}, bf16[48,896]{1,0:T(8,128)(2,1)S(1)}, u32[]{:S(2)}, u32[]{:S(2)}) collective-permute-start(bf16[48,896]{1,0:T(8,128)(2,1)S(1)} %pad_maximum_fusion.6), channel_id=1, source_target_pairs={{0,2},{1,3},{2,0},{3,1},{4,6},{5,7},{6,4},{7,5},{8,10},{9,11},{10,... | collective-permute-start | bytes 258056 | tf_op jit(solution)/shard_map/ppermute | solution.py:11
  38.5 3.6 %collective-permute-done.11 = bf16[48,896]{1,0:T(8,128)(2,1)S(1)} collective-permute-done((bf16[48,896]{1,0:T(8,128)(2,1)S(1)}, bf16[48,896]{1,0:T(8,128)(2,1)S(1)}, u32[]{:S(2)}, u32[]{:S(2)}) %collective-permute-start.11) | collective-permute-done | bytes 86048 | tf_op jit(solution)/shard_map/ppermute | solution.py:11
  42.2 0.8 %fusion.24 = bf16[16,896]{1,0:T(8,128)(2,1)S(1)} fusion(bf16[16,896]{1,0:T(8,128)(2,1)S(1)} %collective-permute-done.13, bf16[16,896]{1,0:T(8,128)(2,1)S(1)} %collective-permute-done.12, f32[16,896]{1,0:T(8,128)S(1)} %slice.256, bf16[16,896]{1,0:T(8,128)(2,1)S(1)} %slice.259, bf16[3,16,3584]{2,1,0:T(8,128)(2,1)} %param.7, s32[]{:T(128)S(6)} %select_n.174), kind=kLoop, calls=%fused_computation.88 | loop fusion | flops 129024 | bytes 200708 | tf_op jit(solution)/shard_map/convert_element_type | solution.py:146
  43.0 2.4 %collective-permute-start.22 = (bf16[16,896]{1,0:T(8,128)(2,1)S(1)}, bf16[16,896]{1,0:T(8,128)(2,1)S(1)}, u32[]{:S(2)}, u32[]{:S(2)}) collective-permute-start(bf16[16,896]{1,0:T(8,128)(2,1)S(1)} %fusion.24), channel_id=1, source_target_pairs={{0,6},{1,7},{2,4},{3,5},{4,2},{5,3},{6,0},{7,1},{8,14},{9,15},{10,... | collective-permute-start | bytes 86024 | tf_op jit(solution)/shard_map/ppermute | solution.py:11
  45.4 2.1 %collective-permute-start.20 = (bf16[16,896]{1,0:T(8,128)(2,1)S(1)}, bf16[16,896]{1,0:T(8,128)(2,1)S(1)}, u32[]{:S(2)}, u32[]{:S(2)}) collective-permute-start(bf16[16,896]{1,0:T(8,128)(2,1)S(1)} %fusion.24), channel_id=1, source_target_pairs={{0,2},{1,3},{2,0},{3,1},{4,6},{5,7},{6,4},{7,5},{8,10},{9,11},{10,... | collective-permute-start | bytes 86024 | tf_op jit(solution)/shard_map/ppermute | solution.py:11
  47.5 2.4 %collective-permute-start.19 = (bf16[32,896]{1,0:T(8,128)(2,1)S(1)}, bf16[32,896]{1,0:T(8,128)(2,1)S(1)}, u32[]{:S(2)}, u32[]{:S(2)}) collective-permute-start(bf16[32,896]{1,0:T(8,128)(2,1)S(1)} %fusion.21), channel_id=1, source_target_pairs={{0,6},{1,7},{2,4},{3,5},{4,2},{5,3},{6,0},{7,1},{8,14},{9,15},{10,... | collective-permute-start | bytes 172040 | tf_op jit(solution)/shard_map/ppermute | solution.py:11
  49.9 2.1 %collective-permute-start.17 = (bf16[32,896]{1,0:T(8,128)(2,1)S(1)}, bf16[32,896]{1,0:T(8,128)(2,1)S(1)}, u32[]{:S(2)}, u32[]{:S(2)}) collective-permute-start(bf16[32,896]{1,0:T(8,128)(2,1)S(1)} %fusion.21), channel_id=1, source_target_pairs={{0,2},{1,3},{2,0},{3,1},{4,6},{5,7},{6,4},{7,5},{8,10},{9,11},{10,... | collective-permute-start | bytes 172040 | tf_op jit(solution)/shard_map/ppermute | solution.py:11
  52.0 0.7 %collective-permute-start.23 = (bf16[64,896]{1,0:T(8,128)(2,1)S(1)}, bf16[64,896]{1,0:T(8,128)(2,1)S(1)}, u32[]{:S(2)}, u32[]{:S(2)}) collective-permute-start(bf16[64,896]{1,0:T(8,128)(2,1)S(1)} %pad_maximum_fusion.5), channel_id=1, source_target_pairs={{0,1},{1,0},{2,3},{3,2},{4,5},{5,4},{6,7},{7,6},{8,9},{9,8},{10,11... | collective-permute-start | bytes 344072 | tf_op jit(solution)/shard_map/ppermute | solution.py:11
  52.7 0.8 %collective-permute-done.19 = bf16[32,896]{1,0:T(8,128)(2,1)S(1)} collective-permute-done((bf16[32,896]{1,0:T(8,128)(2,1)S(1)}, bf16[32,896]{1,0:T(8,128)(2,1)S(1)}, u32[]{:S(2)}, u32[]{:S(2)}) %collective-permute-start.19) | collective-permute-done | bytes 57376 | tf_op jit(solution)/shard_map/ppermute | solution.py:11
  53.5 1.4 %collective-permute-done.18 = bf16[32,896]{1,0:T(8,128)(2,1)S(1)} collective-permute-done((bf16[32,896]{1,0:T(8,128)(2,1)S(1)}, bf16[32,896]{1,0:T(8,128)(2,1)S(1)}, u32[]{:S(2)}, u32[]{:S(2)}) %collective-permute-start.18) | collective-permute-done | bytes 57376 | tf_op jit(solution)/shard_map/ppermute | solution.py:11
  54.9 0.3 fusion.25
  55.3 1.5 %collective-permute-done.23 = bf16[64,896]{1,0:T(8,128)(2,1)S(1)} collective-permute-done((bf16[64,896]{1,0:T(8,128)(2,1)S(1)}, bf16[64,896]{1,0:T(8,128)(2,1)S(1)}, u32[]{:S(2)}, u32[]{:S(2)}) %collective-permute-start.23) | collective-permute-done | bytes 114720 | tf_op jit(solution)/shard_map/ppermute | solution.py:11
  56.8 0.3 fusion.47
  57.2 0.3 fusion.10
  57.5 0.3 convolution_add_fusion.3
  57.8 0.1 collective-permute-start.24
  57.9 0.5 collective-permute-start.27
  58.4 0.9 %collective-permute-done.24 = f32[384,128]{1,0:T(8,128)S(1)} collective-permute-done((f32[384,128]{1,0:T(8,128)S(1)}, f32[384,128]{1,0:T(8,128)S(1)}, u32[]{:S(2)}, u32[]{:S(2)}) %collective-permute-start.24) | collective-permute-done | bytes 196640 | tf_op jit(solution)/shard_map/ppermute | solution.py:11
  59.4 0.1 fusion.38
  59.6 1.0 %collective-permute-start.26 = (bf16[240,128]{1,0:T(8,128)(2,1)S(1)}, bf16[240,128]{1,0:T(8,128)(2,1)S(1)}, u32[]{:S(2)}, u32[]{:S(2)}) collective-permute-start(bf16[240,128]{1,0:T(8,128)(2,1)S(1)} %constant_dynamic-update-slice_fusion.19), channel_id=1, source_target_pairs={{0,16},{8,24},{16,0},{24,8},{1,17},{9,25},{17,1},{25,9},{2,18},{10... | collective-permute-start | bytes 184328 | tf_op jit(solution)/shard_map/ppermute | solution.py:11
  60.6 1.0 %collective-permute-start.25 = (bf16[240,128]{1,0:T(8,128)(2,1)S(1)}, bf16[240,128]{1,0:T(8,128)(2,1)S(1)}, u32[]{:S(2)}, u32[]{:S(2)}) collective-permute-start(bf16[240,128]{1,0:T(8,128)(2,1)S(1)} %constant_dynamic-update-slice_fusion.4), channel_id=1, source_target_pairs={{0,1},{1,0},{2,3},{3,2},{4,5},{5,4},{6,7},{7,6},{8,9},{9,8},{10,11... | collective-permute-start | bytes 184328 | tf_op jit(solution)/shard_map/ppermute | solution.py:11
  61.7 2.2 %collective-permute-done.26 = bf16[240,128]{1,0:T(8,128)(2,1)S(1)} collective-permute-done((bf16[240,128]{1,0:T(8,128)(2,1)S(1)}, bf16[240,128]{1,0:T(8,128)(2,1)S(1)}, u32[]{:S(2)}, u32[]{:S(2)}) %collective-permute-start.26) | collective-permute-done | bytes 61472 | tf_op jit(solution)/shard_map/ppermute | solution.py:11
  63.9 0.9 %collective-permute-done.25 = bf16[240,128]{1,0:T(8,128)(2,1)S(1)} collective-permute-done((bf16[240,128]{1,0:T(8,128)(2,1)S(1)}, bf16[240,128]{1,0:T(8,128)(2,1)S(1)}, u32[]{:S(2)}, u32[]{:S(2)}) %collective-permute-start.25) | collective-permute-done | bytes 61472 | tf_op jit(solution)/shard_map/ppermute | solution.py:11
  64.9 0.5 fusion.27
  65.5 0.6 maximum_select_fusion
  66.1 0.1 broadcast_select_fusion.1
  66.2 1.4 %fusion = bf16[1,3584,128]{2,1,0:T(8,128)(2,1)} fusion(bf16[128,1792]{1,0:T(8,128)(2,1)S(1)} %get-tuple-element.60, bf16[128,1792]{1,0:T(8,128)(2,1)S(1)} %get-tuple-element.59, f32[384,128]{1,0:T(8,128)S(1)} %get-tuple-element.52, bf16[240,128]{1,0:T(8,128)(2,1)S(1)} %collective-permute-done.26, bf16[240,128]{1,0:T(8,128)(2,1)S(1)} %collective-permute-done.25, ...), kind=kOutput, calls=%fused_computation.1 | convolution fusion | flops 119832576 | bytes 1966084 | tf_op jit(solution)/shard_map/dot_general | solution.py:48
  (82 shorter events, 0.7 us)
Async XLA Ops:
  0.6 12.5 %copy-start.1 = (bf16[1,3584,128]{2,1,0:T(8,128)(2,1)S(1)}, bf16[1,3584,128]{2,1,0:T(8,128)(2,1)}, u32[]{:S(2)}) copy-start(bf16[1,3584,128]{2,1,0:T(8,128)(2,1)} %param.8) | copy-start | bytes 2752516
  0.6 8.1 %collective-permute-start.3 = (bf16[3584,128]{1,0:T(8,128)(2,1)}, bf16[3584,128]{1,0:T(8,128)(2,1)S(1)}, u32[]{:S(2)}, u32[]{:S(2)}) collective-permute-start(bf16[3584,128]{1,0:T(8,128)(2,1)} %bitcast.136), channel_id=1, source_target_pairs={{0,8},{8,0},{16,24},{24,16},{1,9},{9,1},{17,25},{25,17},{2,10},{10... | collective-permute-start | bytes 2752520 | tf_op jit(solution)/shard_map/ppermute | solution.py:11
  2.0 6.7 %collective-permute-start.2 = (bf16[16,1792]{1,0:T(8,128)(2,1)S(1)}, bf16[16,1792]{1,0:T(8,128)(2,1)S(1)}, u32[]{:S(2)}, u32[]{:S(2)}) collective-permute-start(bf16[16,1792]{1,0:T(8,128)(2,1)S(1)} %get-tuple-element.67), channel_id=1, source_target_pairs={{0,1},{1,0},{2,3},{3,2},{4,5},{5,4},{6,7},{7,6},{8,9},{9,8},{10,11... | collective-permute-start | bytes 172040 | tf_op jit(solution)/shard_map/ppermute | solution.py:11
  4.6 8.7 %copy-start.2 = (f32[1,128]{1,0:T(1,128)S(1)}, f32[1,128]{1,0:T(1,128)}, u32[]{:S(2)}) copy-start(f32[1,128]{1,0:T(1,128)} %param.9) | copy-start | bytes 1540
  6.6 12.7 %collective-permute-start.1 = (bf16[256,896]{1,0:T(8,128)(2,1)}, bf16[256,896]{1,0:T(8,128)(2,1)S(1)}, u32[]{:S(2)}, u32[]{:S(2)}) collective-permute-start(bf16[256,896]{1,0:T(8,128)(2,1)} %get-tuple-element.57), channel_id=1, source_target_pairs={{0,16},{8,24},{16,0},{24,8},{1,17},{9,25},{17,1},{25,9},{2,18},{10... | collective-permute-start | bytes 1376264 | tf_op jit(solution)/shard_map/ppermute | solution.py:11
  8.2 12.2 %collective-permute-start = (bf16[256,896]{1,0:T(8,128)(2,1)S(1)}, bf16[256,896]{1,0:T(8,128)(2,1)S(1)}, u32[]{:S(2)}, u32[]{:S(2)}) collective-permute-start(bf16[256,896]{1,0:T(8,128)(2,1)S(1)} %get-tuple-element.58), channel_id=1, source_target_pairs={{0,1},{1,0},{2,3},{3,2},{4,5},{5,4},{6,7},{7,6},{8,9},{9,8},{10,11... | collective-permute-start | bytes 1376264 | tf_op jit(solution)/shard_map/ppermute | solution.py:11
  8.7 11.7 %collective-permute-start.6 = (bf16[32,1792]{1,0:T(8,128)(2,1)S(1)}, bf16[32,1792]{1,0:T(8,128)(2,1)S(1)}, u32[]{:S(2)}, u32[]{:S(2)}) collective-permute-start(bf16[32,1792]{1,0:T(8,128)(2,1)S(1)} %bitcast.128), channel_id=1, source_target_pairs={{0,6},{1,7},{2,4},{3,5},{4,2},{5,3},{6,0},{7,1},{8,14},{9,15},{10,... | collective-permute-start | bytes 344072 | tf_op jit(solution)/shard_map/ppermute | solution.py:11
  12.4 9.4 %collective-permute-start.5 = (bf16[32,1792]{1,0:T(8,128)(2,1)S(1)}, bf16[32,1792]{1,0:T(8,128)(2,1)S(1)}, u32[]{:S(2)}, u32[]{:S(2)}) collective-permute-start(bf16[32,1792]{1,0:T(8,128)(2,1)S(1)} %bitcast.129), channel_id=1, source_target_pairs={{0,4},{1,5},{2,6},{3,7},{4,0},{5,1},{6,2},{7,3},{8,12},{9,13},{10,... | collective-permute-start | bytes 344072 | tf_op jit(solution)/shard_map/ppermute | solution.py:11
  12.4 9.4 %collective-permute-start.4 = (bf16[32,1792]{1,0:T(8,128)(2,1)S(1)}, bf16[32,1792]{1,0:T(8,128)(2,1)S(1)}, u32[]{:S(2)}, u32[]{:S(2)}) collective-permute-start(bf16[32,1792]{1,0:T(8,128)(2,1)S(1)} %bitcast.130), channel_id=1, source_target_pairs={{0,2},{1,3},{2,0},{3,1},{4,6},{5,7},{6,4},{7,5},{8,10},{9,11},{10,... | collective-permute-start | bytes 344072 | tf_op jit(solution)/shard_map/ppermute | solution.py:11
  13.4 8.9 %copy-start.3 = (s32[2,1,12]{2,1,0:T(1,128)S(1)}, s32[2,1,12]{2,1,0:T(1,128)}, u32[]{:S(2)}) copy-start(s32[2,1,12]{2,1,0:T(1,128)} %param.11) | copy-start | bytes 292
  13.4 14.3 %copy-start = (bf16[1,2,2,128,1792]{4,3,2,1,0:T(8,128)(2,1)S(1)}, bf16[1,2,2,128,1792]{4,3,2,1,0:T(8,128)(2,1)}, u32[]{:S(2)}) copy-start(bf16[1,2,2,128,1792]{4,3,2,1,0:T(8,128)(2,1)} %param.10) | copy-start | bytes 5505028
  22.1 2.1 %collective-permute-start.7 = (f32[128,256]{1,0:T(8,128)S(1)}, f32[128,256]{1,0:T(8,128)S(1)}, u32[]{:S(2)}, u32[]{:S(2)}) collective-permute-start(f32[128,256]{1,0:T(8,128)S(1)} %convolution_add_fusion.4), channel_id=1, source_target_pairs={{0,8},{8,0},{16,24},{24,16},{1,9},{9,1},{17,25},{25,17},{2,10},{10... | collective-permute-start | bytes 393224 | tf_op jit(solution)/shard_map/ppermute | solution.py:11
  24.3 4.5 %collective-permute-start.8 = (bf16[128,256]{1,0:T(8,128)(2,1)S(1)}, bf16[128,256]{1,0:T(8,128)(2,1)S(1)}, u32[]{:S(2)}, u32[]{:S(2)}) collective-permute-start(bf16[128,256]{1,0:T(8,128)(2,1)S(1)} %multiply_convert_fusion), channel_id=1, source_target_pairs={{0,16},{8,24},{16,0},{24,8},{1,17},{9,25},{17,1},{25,9},{2,18},{10... | collective-permute-start | bytes 196616 | tf_op jit(solution)/shard_map/ppermute | solution.py:11
  24.9 5.7 %collective-permute-start.10 = (bf16[128,256]{1,0:T(8,128)(2,1)S(1)}, bf16[128,256]{1,0:T(8,128)(2,1)S(1)}, u32[]{:S(2)}, u32[]{:S(2)}) collective-permute-start(bf16[128,256]{1,0:T(8,128)(2,1)S(1)} %bitcast.141), channel_id=1, source_target_pairs={{0,1},{1,0},{2,3},{3,2},{4,5},{5,4},{6,7},{7,6},{8,9},{9,8},{10,11... | collective-permute-start | bytes 196616 | tf_op jit(solution)/shard_map/ppermute | solution.py:11
  27.2 10.2 %collective-permute-start.16 = (bf16[16,896]{1,0:T(8,128)(2,1)S(1)}, bf16[16,896]{1,0:T(8,128)(2,1)S(1)}, u32[]{:S(2)}, u32[]{:S(2)}) collective-permute-start(bf16[16,896]{1,0:T(8,128)(2,1)S(1)} %get-tuple-element.62), channel_id=1, source_target_pairs={{0,1},{1,0},{2,3},{3,2},{4,5},{5,4},{6,7},{7,6},{8,9},{9,8},{10,11... | collective-permute-start | bytes 86024 | tf_op jit(solution)/shard_map/ppermute | solution.py:11
  29.0 4.9 %collective-permute-start.9 = (bf16[64,896]{1,0:T(8,128)(2,1)S(1)}, bf16[64,896]{1,0:T(8,128)(2,1)S(1)}, u32[]{:S(2)}, u32[]{:S(2)}) collective-permute-start(bf16[64,896]{1,0:T(8,128)(2,1)S(1)} %fusion.1), channel_id=1, source_target_pairs={{0,1},{1,0},{2,3},{3,2},{4,5},{5,4},{6,7},{7,6},{8,9},{9,8},{10,11... | collective-permute-start | bytes 344072 | tf_op jit(solution)/shard_map/ppermute | solution.py:11
  31.1 11.1 %collective-permute-start.15 = (bf16[32,896]{1,0:T(8,128)(2,1)S(1)}, bf16[32,896]{1,0:T(8,128)(2,1)S(1)}, u32[]{:S(2)}, u32[]{:S(2)}) collective-permute-start(bf16[32,896]{1,0:T(8,128)(2,1)S(1)} %get-tuple-element.63), channel_id=1, source_target_pairs={{0,6},{1,7},{2,4},{3,5},{4,2},{5,3},{6,0},{7,1},{8,14},{9,15},{10,... | collective-permute-start | bytes 172040 | tf_op jit(solution)/shard_map/ppermute | solution.py:11
  33.6 8.6 %collective-permute-start.14 = (bf16[32,896]{1,0:T(8,128)(2,1)S(1)}, bf16[32,896]{1,0:T(8,128)(2,1)S(1)}, u32[]{:S(2)}, u32[]{:S(2)}) collective-permute-start(bf16[32,896]{1,0:T(8,128)(2,1)S(1)} %get-tuple-element.64), channel_id=1, source_target_pairs={{0,4},{1,5},{2,6},{3,7},{4,0},{5,1},{6,2},{7,3},{8,12},{9,13},{10,... | collective-permute-start | bytes 172040 | tf_op jit(solution)/shard_map/ppermute | solution.py:11
  33.9 8.3 %collective-permute-start.13 = (bf16[16,896]{1,0:T(8,128)(2,1)S(1)}, bf16[16,896]{1,0:T(8,128)(2,1)S(1)}, u32[]{:S(2)}, u32[]{:S(2)}) collective-permute-start(bf16[16,896]{1,0:T(8,128)(2,1)S(1)} %get-tuple-element.70), channel_id=1, source_target_pairs={{0,6},{1,7},{2,4},{3,5},{4,2},{5,3},{6,0},{7,1},{8,14},{9,15},{10,... | collective-permute-start | bytes 86024 | tf_op jit(solution)/shard_map/ppermute | solution.py:11
  36.4 5.7 %collective-permute-start.12 = (bf16[16,896]{1,0:T(8,128)(2,1)S(1)}, bf16[16,896]{1,0:T(8,128)(2,1)S(1)}, u32[]{:S(2)}, u32[]{:S(2)}) collective-permute-start(bf16[16,896]{1,0:T(8,128)(2,1)S(1)} %get-tuple-element.71), channel_id=1, source_target_pairs={{0,4},{1,5},{2,6},{3,7},{4,0},{5,1},{6,2},{7,3},{8,12},{9,13},{10,... | collective-permute-start | bytes 86024 | tf_op jit(solution)/shard_map/ppermute | solution.py:11
  37.3 4.8 %collective-permute-start.11 = (bf16[48,896]{1,0:T(8,128)(2,1)S(1)}, bf16[48,896]{1,0:T(8,128)(2,1)S(1)}, u32[]{:S(2)}, u32[]{:S(2)}) collective-permute-start(bf16[48,896]{1,0:T(8,128)(2,1)S(1)} %pad_maximum_fusion.6), channel_id=1, source_target_pairs={{0,2},{1,3},{2,0},{3,1},{4,6},{5,7},{6,4},{7,5},{8,10},{9,11},{10,... | collective-permute-start | bytes 258056 | tf_op jit(solution)/shard_map/ppermute | solution.py:11
  43.0 6.9 %collective-permute-start.22 = (bf16[16,896]{1,0:T(8,128)(2,1)S(1)}, bf16[16,896]{1,0:T(8,128)(2,1)S(1)}, u32[]{:S(2)}, u32[]{:S(2)}) collective-permute-start(bf16[16,896]{1,0:T(8,128)(2,1)S(1)} %fusion.24), channel_id=1, source_target_pairs={{0,6},{1,7},{2,4},{3,5},{4,2},{5,3},{6,0},{7,1},{8,14},{9,15},{10,... | collective-permute-start | bytes 86024 | tf_op jit(solution)/shard_map/ppermute | solution.py:11
  45.3 6.6 %collective-permute-start.21 = (bf16[16,896]{1,0:T(8,128)(2,1)S(1)}, bf16[16,896]{1,0:T(8,128)(2,1)S(1)}, u32[]{:S(2)}, u32[]{:S(2)}) collective-permute-start(bf16[16,896]{1,0:T(8,128)(2,1)S(1)} %fusion.24), channel_id=1, source_target_pairs={{0,4},{1,5},{2,6},{3,7},{4,0},{5,1},{6,2},{7,3},{8,12},{9,13},{10,... | collective-permute-start | bytes 86024 | tf_op jit(solution)/shard_map/ppermute | solution.py:11
  45.4 6.6 %collective-permute-start.20 = (bf16[16,896]{1,0:T(8,128)(2,1)S(1)}, bf16[16,896]{1,0:T(8,128)(2,1)S(1)}, u32[]{:S(2)}, u32[]{:S(2)}) collective-permute-start(bf16[16,896]{1,0:T(8,128)(2,1)S(1)} %fusion.24), channel_id=1, source_target_pairs={{0,2},{1,3},{2,0},{3,1},{4,6},{5,7},{6,4},{7,5},{8,10},{9,11},{10,... | collective-permute-start | bytes 86024 | tf_op jit(solution)/shard_map/ppermute | solution.py:11
  47.5 6.0 %collective-permute-start.19 = (bf16[32,896]{1,0:T(8,128)(2,1)S(1)}, bf16[32,896]{1,0:T(8,128)(2,1)S(1)}, u32[]{:S(2)}, u32[]{:S(2)}) collective-permute-start(bf16[32,896]{1,0:T(8,128)(2,1)S(1)} %fusion.21), channel_id=1, source_target_pairs={{0,6},{1,7},{2,4},{3,5},{4,2},{5,3},{6,0},{7,1},{8,14},{9,15},{10,... | collective-permute-start | bytes 172040 | tf_op jit(solution)/shard_map/ppermute | solution.py:11
  49.9 5.1 %collective-permute-start.18 = (bf16[32,896]{1,0:T(8,128)(2,1)S(1)}, bf16[32,896]{1,0:T(8,128)(2,1)S(1)}, u32[]{:S(2)}, u32[]{:S(2)}) collective-permute-start(bf16[32,896]{1,0:T(8,128)(2,1)S(1)} %fusion.21), channel_id=1, source_target_pairs={{0,4},{1,5},{2,6},{3,7},{4,0},{5,1},{6,2},{7,3},{8,12},{9,13},{10,... | collective-permute-start | bytes 172040 | tf_op jit(solution)/shard_map/ppermute | solution.py:11
  49.9 5.1 %collective-permute-start.17 = (bf16[32,896]{1,0:T(8,128)(2,1)S(1)}, bf16[32,896]{1,0:T(8,128)(2,1)S(1)}, u32[]{:S(2)}, u32[]{:S(2)}) collective-permute-start(bf16[32,896]{1,0:T(8,128)(2,1)S(1)} %fusion.21), channel_id=1, source_target_pairs={{0,2},{1,3},{2,0},{3,1},{4,6},{5,7},{6,4},{7,5},{8,10},{9,11},{10,... | collective-permute-start | bytes 172040 | tf_op jit(solution)/shard_map/ppermute | solution.py:11
  52.0 4.9 %collective-permute-start.23 = (bf16[64,896]{1,0:T(8,128)(2,1)S(1)}, bf16[64,896]{1,0:T(8,128)(2,1)S(1)}, u32[]{:S(2)}, u32[]{:S(2)}) collective-permute-start(bf16[64,896]{1,0:T(8,128)(2,1)S(1)} %pad_maximum_fusion.5), channel_id=1, source_target_pairs={{0,1},{1,0},{2,3},{3,2},{4,5},{5,4},{6,7},{7,6},{8,9},{9,8},{10,11... | collective-permute-start | bytes 344072 | tf_op jit(solution)/shard_map/ppermute | solution.py:11
  57.8 1.5 %collective-permute-start.24 = (f32[384,128]{1,0:T(8,128)S(1)}, f32[384,128]{1,0:T(8,128)S(1)}, u32[]{:S(2)}, u32[]{:S(2)}) collective-permute-start(f32[384,128]{1,0:T(8,128)S(1)} %slice_select_fusion), channel_id=1, source_target_pairs={{0,8},{8,0},{16,24},{24,16},{1,9},{9,1},{17,25},{25,17},{2,10},{10... | collective-permute-start | bytes 589832 | tf_op jit(solution)/shard_map/ppermute | solution.py:11
  57.9 8.2 %collective-permute-start.27 = (bf16[128,1792]{1,0:T(8,128)(2,1)S(1)}, bf16[128,1792]{1,0:T(8,128)(2,1)S(1)}, u32[]{:S(2)}, u32[]{:S(2)}) collective-permute-start(bf16[128,1792]{1,0:T(8,128)(2,1)S(1)} %constant_dynamic-update-slice_fusion), channel_id=1, source_target_pairs={{0,8},{8,0},{16,24},{24,16},{1,9},{9,1},{17,25},{25,17},{2,10},{10... | collective-permute-start | bytes 1376264 | tf_op jit(solution)/shard_map/ppermute | solution.py:11
  59.6 4.3 %collective-permute-start.26 = (bf16[240,128]{1,0:T(8,128)(2,1)S(1)}, bf16[240,128]{1,0:T(8,128)(2,1)S(1)}, u32[]{:S(2)}, u32[]{:S(2)}) collective-permute-start(bf16[240,128]{1,0:T(8,128)(2,1)S(1)} %constant_dynamic-update-slice_fusion.19), channel_id=1, source_target_pairs={{0,16},{8,24},{16,0},{24,8},{1,17},{9,25},{17,1},{25,9},{2,18},{10... | collective-permute-start | bytes 184328 | tf_op jit(solution)/shard_map/ppermute | solution.py:11
  60.6 4.2 %collective-permute-start.25 = (bf16[240,128]{1,0:T(8,128)(2,1)S(1)}, bf16[240,128]{1,0:T(8,128)(2,1)S(1)}, u32[]{:S(2)}, u32[]{:S(2)}) collective-permute-start(bf16[240,128]{1,0:T(8,128)(2,1)S(1)} %constant_dynamic-update-slice_fusion.4), channel_id=1, source_target_pairs={{0,1},{1,0},{2,3},{3,2},{4,5},{5,4},{6,7},{7,6},{8,9},{9,8},{10,11... | collective-permute-start | bytes 184328 | tf_op jit(solution)/shard_map/ppermute | solution.py:11

commit v15 on v14

--- a/solution.py
+++ b/solution.py
@@ -25,14 +25,10 @@
 
 def gates(blocks, layer, slot, slots, latents, tokens):
     listed = lax.dynamic_index_in_dim(blocks, layer, 0, keepdims=False)
-    tile = tokens // listed.shape[0]
-    here = latents // BLOCK
-    out = []
-    for side in range(2):
-        names = (side * slots + slot) * here + jnp.arange(here)
-        flags = jnp.any(listed[:, :, None] == names, axis=1).astype(F32)
-        out.append(jnp.repeat(jnp.repeat(flags, tile, axis=0), BLOCK, axis=1))
-    return out
+    column = jnp.arange(2 * latents)
+    names = (column // latents * slots + slot) * (latents // BLOCK) + column % latents // BLOCK
+    flags = jnp.any(listed[:, :, None] == names, axis=1).astype(F32)
+    return jnp.repeat(flags, tokens // listed.shape[0], axis=0)
 
 
 def half_preacts(resid_half, weight, weight_other, bias, half):
@@ -121,10 +117,10 @@
     own_mine, shared_mine = decoder_part(decoder, layer, side), decoder_part(decoder, 1 - layer, layer)
     resid_half = jnp.concatenate(column, axis=0)
     firing = gates(blocks, layer, slot, slots, latents, tokens)
-    gate = jnp.where(half == 0, firing[0], firing[1])
+    gate = jnp.where(half == 0, firing[:, :latents], firing[:, latents:])
 
     partial = half_preacts(resid_half, enc_weight[0], weight_other, bias, half)
-    acts = ((partial + over_core(partial)) * jnp.concatenate(firing, axis=1)).astype(BF16)
+    acts = ((partial + over_core(partial)) * firing).astype(BF16)
     acts_turned = turned(acts)
     acts_y, acts_x = over_y(acts), over_x(acts_turned)
     target, _ = hold((target, acts_turned))
@@ -143,8 +139,9 @@
     arrived, staying = hold((arrived, staying))
     shared_terms, own_terms = both_along_z(pieces_of(staying + arrived.astype(F32)), pieces_of(product))
     terms = hold((*shared_terms, *own_terms))
+    aim_mine, aim_shared = hold((aim_own(side), aim_shared))
     err_shared = (added(terms[:far]) - aim_shared.astype(F32)).astype(BF16)
-    err_own = (added(terms[far:]) - paired(aim_own(side), aim_other).astype(F32)).astype(BF16)
+    err_own = (added(terms[far:]) - paired(aim_mine, aim_other).astype(F32)).astype(BF16)
 
     own_column = along_z(err_own)
     shared_near = jnp.concatenate(along_z(err_shared), axis=0)
@@ -206,11 +203,11 @@
 
     resid_half = to_all(lax.dynamic_slice(resid, (layer, 0, half * cols), (1, rows, cols))[0])
     firing = gates(blocks, layer, slot, slots, latents, tokens)
-    gate = jnp.where(half == 0, firing[0], firing[1])
+    gate = jnp.where(half == 0, firing[:, :latents], firing[:, latents:])
     weight_other = crossed(enc_weight[0], "layer", 1)
     partial = half_preacts(resid_half, enc_weight[0], weight_other, enc_bias[0], half)
     preact = partial + crossed(partial, "layer", 1)
-    acts = (preact * jnp.concatenate(firing, axis=1)).astype(BF16)
+    acts = (preact * firing).astype(BF16)
     resid_other = crossed(resid_half, "layer", 1)
 
     sums = jnp.concatenate([times(acts, decoder[t]).astype(BF16) for t in range(2)], axis=1)

time: 67.9 us -> 65.7 us (0.968)
  between operations: 2.45 us -> 1.11 us
  starting transfers between devices: 33.3 us -> 34.3 us
  waiting for transfers between devices: 20.5 us -> 19.7 us
  local copies, waits for them, and re-layouts: 3.98 us -> 3.24 us
    select_n x3, other arithmetic: 0.25 us -> 1.27 us  [both_halves(): jnp.where(half == 0, mine, other)]
    ppermute x28, starting transfers between devices: 33.3 us -> 34.3 us  [crossed(): lax.ppermute(block, axis, [(i, i ^ mask) for i in range(lax.axis_size(axi...]
    squeeze x0 -> x1, local copies, waits for them, and re-layouts: none -> 0.79 us  [aim_own(): lax.dynamic_slice(target, (2 * layer, 0, start + where * part), (1, rows,...]
    another operation x2 -> x1, local copies, waits for them, and re-layouts: 1.6 us -> 0.83 us  [paired(): block.reshape(-1, 1, rows, block.shape[1])]
    squeeze x1, local copies, waits for them, and re-layouts: 2.01 us -> 1.24 us  [decoder_part(): lax.dynamic_slice(decoder, (which, 0, where * part), (1, 2 * latents, part))]
    convert_element_type x1, other arithmetic: 0.78 us -> 0.03 us  [two_layers(): err_shared = (added(terms[:far]) - aim_shared.astype(F32)).astype(BF16)]
    ppermute x28, waiting for transfers between devices: 20.5 us -> 19.7 us  [crossed(): lax.ppermute(block, axis, [(i, i ^ mask) for i in range(lax.axis_size(axi...]
where the time goes in v15:
time: 65.7 us; the launch traced here: 65.4 us
  starting transfers between devices  34.3 us (52%)
  waiting for transfers between devices  19.7 us (30%)
  matrix products  4.16 us (6%)
  local copies, waits for them, and re-layouts  3.24 us (5%)
  other arithmetic  2.89 us (4%)
  between operations  1.11 us (2%)
    ppermute x28, starting transfers between devices, crossed(): lax.ppermute(block, axis, [(i, i ^ mask) for i in range(lax.axis_size(axi...  34.3 us
    ppermute x28, waiting for transfers between devices, crossed(): lax.ppermute(block, axis, [(i, i ^ mask) for i in range(lax.axis_size(axi...  19.7 us
    dot_general x7, matrix products, times(): return jnp.dot(left, right, preferred_element_type=F32)  1.6 us
    dot_general x1, matrix products, encoder_gradient(): lax.dot_general(whole, grad_low, (((0,), (0,)), ((), ())), preferred_elem...  1.36 us
  transfers between devices with their start and end apart: 28, of which 11 were waited for; matrix products, arithmetic and copies ran while one was open for 11% of the time, Pallas kernels for 0%

profile of v15, /device:TPU:0, one launch (start us, length us, event | category | flops | bytes accessed | tf_op | source)
XLA Modules:
  0.0 65.4 jit_solution(11370325696372402983)
XLA Ops:
  0.6 0.0 copy-start
  0.7 0.5 collective-permute-start.3
  1.2 0.8 %dynamic-slice_bitcast_fusion.3 = (bf16[1,1,16,1792]{3,2,1,0:T(8,128)(2,1)S(1)}, bf16[16,1792]{1,0:T(8,128)(2,1)S(1)}) fusion(bf16[2,16,3584]{2,1,0:T(8,128)(2,1)} %param.6, s32[]{:T(128)S(6)} %select_n.180, s32[]{:T(128)S(6)} %select_n.185), kind=kLoop, calls=%fused_computation.89 | loop fusion | bytes 172040 | tf_op jit(solution)/shard_map/reshape;squeeze | solution.py:103
  2.0 2.6 %collective-permute-start.2 = (bf16[16,1792]{1,0:T(8,128)(2,1)S(1)}, bf16[16,1792]{1,0:T(8,128)(2,1)S(1)}, u32[]{:S(2)}, u32[]{:S(2)}) collective-permute-start(bf16[16,1792]{1,0:T(8,128)(2,1)S(1)} %get-tuple-element.70), channel_id=1, source_target_pairs={{0,1},{1,0},{2,3},{3,2},{4,5},{5,4},{6,7},{7,6},{8,9},{9,8},{10,11... | collective-permute-start | bytes 172040 | tf_op jit(solution)/shard_map/ppermute | solution.py:11
  4.6 1.2 %dynamic-slice_bitcast_fusion = (bf16[256,896]{1,0:T(8,128)(2,1)S(1)}, bf16[256,896]{1,0:T(8,128)(2,1)S(1)}) fusion(bf16[2,256,1792]{2,1,0:T(8,128)(2,1)} %bitcast.119, s32[]{:T(128)S(6)} %select_n.182, s32[]{:T(128)S(6)} %select_n.183, s32[]{:T(128)S(6)} %select_n.180, s32[]{:T(128)S(6)} %select_n.181), kind=kLoop, calls=%fused_computation.24 | loop fusion | bytes 1835024 | tf_op jit(solution)/shard_map/squeeze | solution.py:94
  5.9 1.6 %collective-permute-start.1 = (bf16[256,896]{1,0:T(8,128)(2,1)S(1)}, bf16[256,896]{1,0:T(8,128)(2,1)S(1)}, u32[]{:S(2)}, u32[]{:S(2)}) collective-permute-start(bf16[256,896]{1,0:T(8,128)(2,1)S(1)} %get-tuple-element.59), channel_id=1, source_target_pairs={{0,16},{8,24},{16,0},{24,8},{1,17},{9,25},{17,1},{25,9},{2,18},{10... | collective-permute-start | bytes 1376264 | tf_op jit(solution)/shard_map/ppermute | solution.py:11
  7.5 0.5 collective-permute-start
  8.0 0.0 collective-permute-done.2
  8.0 3.7 %collective-permute-start.6 = (bf16[32,1792]{1,0:T(8,128)(2,1)S(1)}, bf16[32,1792]{1,0:T(8,128)(2,1)S(1)}, u32[]{:S(2)}, u32[]{:S(2)}) collective-permute-start(bf16[32,1792]{1,0:T(8,128)(2,1)S(1)} %bitcast.130), channel_id=1, source_target_pairs={{0,6},{1,7},{2,4},{3,5},{4,2},{5,3},{6,0},{7,1},{8,14},{9,15},{10,... | collective-permute-start | bytes 344072 | tf_op jit(solution)/shard_map/ppermute | solution.py:11
  11.7 0.8 %collective-permute-start.4 = (bf16[32,1792]{1,0:T(8,128)(2,1)S(1)}, bf16[32,1792]{1,0:T(8,128)(2,1)S(1)}, u32[]{:S(2)}, u32[]{:S(2)}) collective-permute-start(bf16[32,1792]{1,0:T(8,128)(2,1)S(1)} %bitcast.132), channel_id=1, source_target_pairs={{0,2},{1,3},{2,0},{3,1},{4,6},{5,7},{6,4},{7,5},{8,10},{9,11},{10,... | collective-permute-start | bytes 344072 | tf_op jit(solution)/shard_map/ppermute | solution.py:11
  12.5 1.2 %bitcast_select_fusion.1 = (bf16[1792,128]{1,0:T(8,128)(2,1)S(1)}, bf16[1792,128]{1,0:T(8,128)(2,1)S(1)}) fusion(pred[]{:T(512)S(6)} %eq.48, bf16[3584,128]{1,0:T(8,128)(2,1)} %collective-permute-done.3, s32[]{:T(128)S(6)} %select_n.185, bf16[1,3584,128]{2,1,0:T(8,128)(2,1)S(1)} %copy-done.2), kind=kLoop, calls=%fused_computation.23 | loop fusion | flops 458752 | bytes 1835013 | tf_op jit(solution)/shard_map/jit(_where)/select_n | solution.py:23
  13.8 0.1 compare_reduce_fusion
  13.9 0.0 copy-start.1
  13.9 4.6 %collective-permute-done.1 = bf16[256,896]{1,0:T(8,128)(2,1)S(1)} collective-permute-done((bf16[256,896]{1,0:T(8,128)(2,1)S(1)}, bf16[256,896]{1,0:T(8,128)(2,1)S(1)}, u32[]{:S(2)}, u32[]{:S(2)}) %collective-permute-start.1) | collective-permute-done | bytes 458784 | tf_op jit(solution)/shard_map/ppermute | solution.py:11
  18.5 1.2 %collective-permute-done = bf16[256,896]{1,0:T(8,128)(2,1)S(1)} collective-permute-done((bf16[256,896]{1,0:T(8,128)(2,1)S(1)}, bf16[256,896]{1,0:T(8,128)(2,1)S(1)}, u32[]{:S(2)}, u32[]{:S(2)}) %collective-permute-start) | collective-permute-done | bytes 458784 | tf_op jit(solution)/shard_map/ppermute | solution.py:11
  19.7 1.4 %collective-permute-done.5 = bf16[32,1792]{1,0:T(8,128)(2,1)S(1)} collective-permute-done((bf16[32,1792]{1,0:T(8,128)(2,1)S(1)}, bf16[32,1792]{1,0:T(8,128)(2,1)S(1)}, u32[]{:S(2)}, u32[]{:S(2)}) %collective-permute-start.5) | collective-permute-done | bytes 114720 | tf_op jit(solution)/shard_map/ppermute | solution.py:11
  21.1 0.3 convolution_add_fusion.4
  21.4 0.1 collective-permute-start.7
  21.5 1.3 %collective-permute-done.7 = f32[128,256]{1,0:T(8,128)S(1)} collective-permute-done((f32[128,256]{1,0:T(8,128)S(1)}, f32[128,256]{1,0:T(8,128)S(1)}, u32[]{:S(2)}, u32[]{:S(2)}) %collective-permute-start.7) | collective-permute-done | bytes 131104 | tf_op jit(solution)/shard_map/ppermute | solution.py:11
  22.9 0.9 %collective-permute-start.8 = (bf16[128,256]{1,0:T(8,128)(2,1)S(1)}, bf16[128,256]{1,0:T(8,128)(2,1)S(1)}, u32[]{:S(2)}, u32[]{:S(2)}) collective-permute-start(bf16[128,256]{1,0:T(8,128)(2,1)S(1)} %multiply_convert_fusion), channel_id=1, source_target_pairs={{0,16},{8,24},{16,0},{24,8},{1,17},{9,25},{17,1},{25,9},{2,18},{10... | collective-permute-start | bytes 196616 | tf_op jit(solution)/shard_map/ppermute | solution.py:11
  23.8 1.6 %collective-permute-start.10 = (bf16[128,256]{1,0:T(8,128)(2,1)S(1)}, bf16[128,256]{1,0:T(8,128)(2,1)S(1)}, u32[]{:S(2)}, u32[]{:S(2)}) collective-permute-start(bf16[128,256]{1,0:T(8,128)(2,1)S(1)} %bitcast.144), channel_id=1, source_target_pairs={{0,1},{1,0},{2,3},{3,2},{4,5},{5,4},{6,7},{7,6},{8,9},{9,8},{10,11... | collective-permute-start | bytes 196616 | tf_op jit(solution)/shard_map/ppermute | solution.py:11
  25.4 0.8 %dynamic-slice_bitcast_fusion.4 = (bf16[16,896]{1,0:T(8,128)(2,1)S(1)}, bf16[16,896]{1,0:T(8,128)(2,1)S(1)}, bf16[16,896]{1,0:T(8,128)(2,1)S(1)}) fusion(bf16[3,16,3584]{2,1,0:T(8,128)(2,1)} %param.7, s32[]{:T(128)S(6)} %select_n.197, s32[]{:T(128)S(6)} %select_n.200, s32[]{:T(128)S(6)} %select_n.199, s32[]{:T(128)S(6)} %select_n.198), kind=kLoop, calls=%fused_computation.96 | loop fusion | bytes 172048 | tf_op jit(solution)/shard_map/squeeze | solution.py:130
  26.2 0.6 collective-permute-start.16
  26.8 0.2 fusion.12
  27.0 0.2 fusion.14
  27.2 0.0 collective-permute-done.8
  27.2 0.2 fusion.1
  27.4 1.5 %collective-permute-start.9 = (bf16[64,896]{1,0:T(8,128)(2,1)S(1)}, bf16[64,896]{1,0:T(8,128)(2,1)S(1)}, u32[]{:S(2)}, u32[]{:S(2)}) collective-permute-start(bf16[64,896]{1,0:T(8,128)(2,1)S(1)} %fusion.1), channel_id=1, source_target_pairs={{0,1},{1,0},{2,3},{3,2},{4,5},{5,4},{6,7},{7,6},{8,9},{9,8},{10,11... | collective-permute-start | bytes 344072 | tf_op jit(solution)/shard_map/ppermute | solution.py:11
  29.0 0.0 collective-permute-done.10
  29.0 0.2 fusion.51
  29.2 0.2 fusion.50
  29.5 2.5 %collective-permute-start.15 = (bf16[32,896]{1,0:T(8,128)(2,1)S(1)}, bf16[32,896]{1,0:T(8,128)(2,1)S(1)}, u32[]{:S(2)}, u32[]{:S(2)}) collective-permute-start(bf16[32,896]{1,0:T(8,128)(2,1)S(1)} %get-tuple-element.66), channel_id=1, source_target_pairs={{0,6},{1,7},{2,4},{3,5},{4,2},{5,3},{6,0},{7,1},{8,14},{9,15},{10,... | collective-permute-start | bytes 172040 | tf_op jit(solution)/shard_map/ppermute | solution.py:11
  32.0 0.0 collective-permute-start.14
  32.0 0.2 convolution_add_fusion.1
  32.3 0.0 collective-permute-done.9
  32.4 2.5 %collective-permute-start.13 = (bf16[16,896]{1,0:T(8,128)(2,1)S(1)}, bf16[16,896]{1,0:T(8,128)(2,1)S(1)}, u32[]{:S(2)}, u32[]{:S(2)}) collective-permute-start(bf16[16,896]{1,0:T(8,128)(2,1)S(1)} %get-tuple-element.73), channel_id=1, source_target_pairs={{0,6},{1,7},{2,4},{3,5},{4,2},{5,3},{6,0},{7,1},{8,14},{9,15},{10,... | collective-permute-start | bytes 86024 | tf_op jit(solution)/shard_map/ppermute | solution.py:11
  34.9 0.9 %collective-permute-start.12 = (bf16[16,896]{1,0:T(8,128)(2,1)S(1)}, bf16[16,896]{1,0:T(8,128)(2,1)S(1)}, u32[]{:S(2)}, u32[]{:S(2)}) collective-permute-start(bf16[16,896]{1,0:T(8,128)(2,1)S(1)} %get-tuple-element.74), channel_id=1, source_target_pairs={{0,4},{1,5},{2,6},{3,7},{4,0},{5,1},{6,2},{7,3},{8,12},{9,13},{10,... | collective-permute-start | bytes 86024 | tf_op jit(solution)/shard_map/ppermute | solution.py:11
  35.8 0.0 collective-permute-done.16
  35.8 1.1 %collective-permute-start.11 = (bf16[48,896]{1,0:T(8,128)(2,1)S(1)}, bf16[48,896]{1,0:T(8,128)(2,1)S(1)}, u32[]{:S(2)}, u32[]{:S(2)}) collective-permute-start(bf16[48,896]{1,0:T(8,128)(2,1)S(1)} %pad_maximum_fusion.6), channel_id=1, source_target_pairs={{0,2},{1,3},{2,0},{3,1},{4,6},{5,7},{6,4},{7,5},{8,10},{9,11},{10,... | collective-permute-start | bytes 258056 | tf_op jit(solution)/shard_map/ppermute | solution.py:11
  36.9 3.6 %collective-permute-done.11 = bf16[48,896]{1,0:T(8,128)(2,1)S(1)} collective-permute-done((bf16[48,896]{1,0:T(8,128)(2,1)S(1)}, bf16[48,896]{1,0:T(8,128)(2,1)S(1)}, u32[]{:S(2)}, u32[]{:S(2)}) %collective-permute-start.11) | collective-permute-done | bytes 86048 | tf_op jit(solution)/shard_map/ppermute | solution.py:11
  40.7 2.3 %collective-permute-start.22 = (bf16[16,896]{1,0:T(8,128)(2,1)S(1)}, bf16[16,896]{1,0:T(8,128)(2,1)S(1)}, u32[]{:S(2)}, u32[]{:S(2)}) collective-permute-start(bf16[16,896]{1,0:T(8,128)(2,1)S(1)} %subtract_convert_fusion), channel_id=1, source_target_pairs={{0,6},{1,7},{2,4},{3,5},{4,2},{5,3},{6,0},{7,1},{8,14},{9,15},{10,... | collective-permute-start | bytes 86024 | tf_op jit(solution)/shard_map/ppermute | solution.py:11
  43.0 0.0 collective-permute-start.21
  43.0 2.1 %collective-permute-start.20 = (bf16[16,896]{1,0:T(8,128)(2,1)S(1)}, bf16[16,896]{1,0:T(8,128)(2,1)S(1)}, u32[]{:S(2)}, u32[]{:S(2)}) collective-permute-start(bf16[16,896]{1,0:T(8,128)(2,1)S(1)} %subtract_convert_fusion), channel_id=1, source_target_pairs={{0,2},{1,3},{2,0},{3,1},{4,6},{5,7},{6,4},{7,5},{8,10},{9,11},{10,... | collective-permute-start | bytes 86024 | tf_op jit(solution)/shard_map/ppermute | solution.py:11
  45.2 2.3 %collective-permute-start.19 = (bf16[32,896]{1,0:T(8,128)(2,1)S(1)}, bf16[32,896]{1,0:T(8,128)(2,1)S(1)}, u32[]{:S(2)}, u32[]{:S(2)}) collective-permute-start(bf16[32,896]{1,0:T(8,128)(2,1)S(1)} %fusion.21), channel_id=1, source_target_pairs={{0,6},{1,7},{2,4},{3,5},{4,2},{5,3},{6,0},{7,1},{8,14},{9,15},{10,... | collective-permute-start | bytes 172040 | tf_op jit(solution)/shard_map/ppermute | solution.py:11
  47.5 2.2 %collective-permute-start.17 = (bf16[32,896]{1,0:T(8,128)(2,1)S(1)}, bf16[32,896]{1,0:T(8,128)(2,1)S(1)}, u32[]{:S(2)}, u32[]{:S(2)}) collective-permute-start(bf16[32,896]{1,0:T(8,128)(2,1)S(1)} %fusion.21), channel_id=1, source_target_pairs={{0,2},{1,3},{2,0},{3,1},{4,6},{5,7},{6,4},{7,5},{8,10},{9,11},{10,... | collective-permute-start | bytes 172040 | tf_op jit(solution)/shard_map/ppermute | solution.py:11
  49.7 1.1 %collective-permute-start.23 = (bf16[64,896]{1,0:T(8,128)(2,1)S(1)}, bf16[64,896]{1,0:T(8,128)(2,1)S(1)}, u32[]{:S(2)}, u32[]{:S(2)}) collective-permute-start(bf16[64,896]{1,0:T(8,128)(2,1)S(1)} %pad_maximum_fusion.5), channel_id=1, source_target_pairs={{0,1},{1,0},{2,3},{3,2},{4,5},{5,4},{6,7},{7,6},{8,9},{9,8},{10,11... | collective-permute-start | bytes 344072 | tf_op jit(solution)/shard_map/ppermute | solution.py:11
  50.7 0.5 collective-permute-done.19
  51.2 1.3 %collective-permute-done.18 = bf16[32,896]{1,0:T(8,128)(2,1)S(1)} collective-permute-done((bf16[32,896]{1,0:T(8,128)(2,1)S(1)}, bf16[32,896]{1,0:T(8,128)(2,1)S(1)}, u32[]{:S(2)}, u32[]{:S(2)}) %collective-permute-start.18) | collective-permute-done | bytes 57376 | tf_op jit(solution)/shard_map/ppermute | solution.py:11
  52.5 0.3 fusion.24
  52.9 1.6 %collective-permute-done.23 = bf16[64,896]{1,0:T(8,128)(2,1)S(1)} collective-permute-done((bf16[64,896]{1,0:T(8,128)(2,1)S(1)}, bf16[64,896]{1,0:T(8,128)(2,1)S(1)}, u32[]{:S(2)}, u32[]{:S(2)}) %collective-permute-start.23) | collective-permute-done | bytes 114720 | tf_op jit(solution)/shard_map/ppermute | solution.py:11
  54.5 0.3 fusion.52
  54.8 0.3 fusion.10
  55.2 0.3 convolution_add_fusion.3
  55.5 0.1 collective-permute-start.24
  55.6 0.5 collective-permute-start.27
  56.1 0.9 %collective-permute-done.24 = f32[384,128]{1,0:T(8,128)S(1)} collective-permute-done((f32[384,128]{1,0:T(8,128)S(1)}, f32[384,128]{1,0:T(8,128)S(1)}, u32[]{:S(2)}, u32[]{:S(2)}) %collective-permute-start.24) | collective-permute-done | bytes 196640 | tf_op jit(solution)/shard_map/ppermute | solution.py:11
  57.2 1.2 %collective-permute-start.26 = (bf16[240,128]{1,0:T(8,128)(2,1)S(1)}, bf16[240,128]{1,0:T(8,128)(2,1)S(1)}, u32[]{:S(2)}, u32[]{:S(2)}) collective-permute-start(bf16[240,128]{1,0:T(8,128)(2,1)S(1)} %constant_dynamic-update-slice_fusion.19), channel_id=1, source_target_pairs={{0,16},{8,24},{16,0},{24,8},{1,17},{9,25},{17,1},{25,9},{2,18},{10... | collective-permute-start | bytes 184328 | tf_op jit(solution)/shard_map/ppermute | solution.py:11
  58.5 1.0 %collective-permute-start.25 = (bf16[240,128]{1,0:T(8,128)(2,1)S(1)}, bf16[240,128]{1,0:T(8,128)(2,1)S(1)}, u32[]{:S(2)}, u32[]{:S(2)}) collective-permute-start(bf16[240,128]{1,0:T(8,128)(2,1)S(1)} %constant_dynamic-update-slice_fusion.4), channel_id=1, source_target_pairs={{0,1},{1,0},{2,3},{3,2},{4,5},{5,4},{6,7},{7,6},{8,9},{9,8},{10,11... | collective-permute-start | bytes 184328 | tf_op jit(solution)/shard_map/ppermute | solution.py:11
  59.5 2.0 %collective-permute-done.26 = bf16[240,128]{1,0:T(8,128)(2,1)S(1)} collective-permute-done((bf16[240,128]{1,0:T(8,128)(2,1)S(1)}, bf16[240,128]{1,0:T(8,128)(2,1)S(1)}, u32[]{:S(2)}, u32[]{:S(2)}) %collective-permute-start.26) | collective-permute-done | bytes 61472 | tf_op jit(solution)/shard_map/ppermute | solution.py:11
  61.6 1.1 %collective-permute-done.25 = bf16[240,128]{1,0:T(8,128)(2,1)S(1)} collective-permute-done((bf16[240,128]{1,0:T(8,128)(2,1)S(1)}, bf16[240,128]{1,0:T(8,128)(2,1)S(1)}, u32[]{:S(2)}, u32[]{:S(2)}) %collective-permute-start.25) | collective-permute-done | bytes 61472 | tf_op jit(solution)/shard_map/ppermute | solution.py:11
  62.8 0.5 fusion.26
  63.3 0.6 maximum_select_fusion
  64.0 0.1 broadcast_select_fusion.1
  64.1 1.4 %fusion = bf16[1,3584,128]{2,1,0:T(8,128)(2,1)} fusion(bf16[128,1792]{1,0:T(8,128)(2,1)S(1)} %get-tuple-element.62, bf16[128,1792]{1,0:T(8,128)(2,1)S(1)} %get-tuple-element.61, f32[384,128]{1,0:T(8,128)S(1)} %get-tuple-element.54, bf16[240,128]{1,0:T(8,128)(2,1)S(1)} %collective-permute-done.26, bf16[240,128]{1,0:T(8,128)(2,1)S(1)} %collective-permute-done.25, ...), kind=kOutput, calls=%fused_computation.1 | convolution fusion | flops 119832576 | bytes 1966592 | tf_op jit(solution)/shard_map/dot_general | solution.py:44
  (84 shorter events, 0.7 us)
Async XLA Ops:
  0.6 13.1 %copy-start = (s32[2,1,12]{2,1,0:T(1,128)S(1)}, s32[2,1,12]{2,1,0:T(1,128)}, u32[]{:S(2)}) copy-start(s32[2,1,12]{2,1,0:T(1,128)} %param.11) | copy-start | bytes 292
  0.6 11.9 %copy-start.2 = (bf16[1,3584,128]{2,1,0:T(8,128)(2,1)S(1)}, bf16[1,3584,128]{2,1,0:T(8,128)(2,1)}, u32[]{:S(2)}) copy-start(bf16[1,3584,128]{2,1,0:T(8,128)(2,1)} %param.8) | copy-start | bytes 2752516
  0.7 7.4 %collective-permute-start.3 = (bf16[3584,128]{1,0:T(8,128)(2,1)}, bf16[3584,128]{1,0:T(8,128)(2,1)}, u32[]{:S(2)}, u32[]{:S(2)}) collective-permute-start(bf16[3584,128]{1,0:T(8,128)(2,1)} %bitcast.138), channel_id=1, source_target_pairs={{0,8},{8,0},{16,24},{24,16},{1,9},{9,1},{17,25},{25,17},{2,10},{10... | collective-permute-start | bytes 2752520 | tf_op jit(solution)/shard_map/ppermute | solution.py:11
  2.0 6.0 %collective-permute-start.2 = (bf16[16,1792]{1,0:T(8,128)(2,1)S(1)}, bf16[16,1792]{1,0:T(8,128)(2,1)S(1)}, u32[]{:S(2)}, u32[]{:S(2)}) collective-permute-start(bf16[16,1792]{1,0:T(8,128)(2,1)S(1)} %get-tuple-element.70), channel_id=1, source_target_pairs={{0,1},{1,0},{2,3},{3,2},{4,5},{5,4},{6,7},{7,6},{8,9},{9,8},{10,11... | collective-permute-start | bytes 172040 | tf_op jit(solution)/shard_map/ppermute | solution.py:11
  4.6 9.1 %copy-start.3 = (f32[1,128]{1,0:T(1,128)S(1)}, f32[1,128]{1,0:T(1,128)}, u32[]{:S(2)}) copy-start(f32[1,128]{1,0:T(1,128)} %param.9) | copy-start | bytes 1540
  5.9 12.6 %collective-permute-start.1 = (bf16[256,896]{1,0:T(8,128)(2,1)S(1)}, bf16[256,896]{1,0:T(8,128)(2,1)S(1)}, u32[]{:S(2)}, u32[]{:S(2)}) collective-permute-start(bf16[256,896]{1,0:T(8,128)(2,1)S(1)} %get-tuple-element.59), channel_id=1, source_target_pairs={{0,16},{8,24},{16,0},{24,8},{1,17},{9,25},{17,1},{25,9},{2,18},{10... | collective-permute-start | bytes 1376264 | tf_op jit(solution)/shard_map/ppermute | solution.py:11
  7.5 12.2 %collective-permute-start = (bf16[256,896]{1,0:T(8,128)(2,1)S(1)}, bf16[256,896]{1,0:T(8,128)(2,1)S(1)}, u32[]{:S(2)}, u32[]{:S(2)}) collective-permute-start(bf16[256,896]{1,0:T(8,128)(2,1)S(1)} %get-tuple-element.60), channel_id=1, source_target_pairs={{0,1},{1,0},{2,3},{3,2},{4,5},{5,4},{6,7},{7,6},{8,9},{9,8},{10,11... | collective-permute-start | bytes 1376264 | tf_op jit(solution)/shard_map/ppermute | solution.py:11
  8.0 11.7 %collective-permute-start.6 = (bf16[32,1792]{1,0:T(8,128)(2,1)S(1)}, bf16[32,1792]{1,0:T(8,128)(2,1)S(1)}, u32[]{:S(2)}, u32[]{:S(2)}) collective-permute-start(bf16[32,1792]{1,0:T(8,128)(2,1)S(1)} %bitcast.130), channel_id=1, source_target_pairs={{0,6},{1,7},{2,4},{3,5},{4,2},{5,3},{6,0},{7,1},{8,14},{9,15},{10,... | collective-permute-start | bytes 344072 | tf_op jit(solution)/shard_map/ppermute | solution.py:11
  11.7 9.4 %collective-permute-start.5 = (bf16[32,1792]{1,0:T(8,128)(2,1)S(1)}, bf16[32,1792]{1,0:T(8,128)(2,1)S(1)}, u32[]{:S(2)}, u32[]{:S(2)}) collective-permute-start(bf16[32,1792]{1,0:T(8,128)(2,1)S(1)} %bitcast.131), channel_id=1, source_target_pairs={{0,4},{1,5},{2,6},{3,7},{4,0},{5,1},{6,2},{7,3},{8,12},{9,13},{10,... | collective-permute-start | bytes 344072 | tf_op jit(solution)/shard_map/ppermute | solution.py:11
  11.7 9.4 %collective-permute-start.4 = (bf16[32,1792]{1,0:T(8,128)(2,1)S(1)}, bf16[32,1792]{1,0:T(8,128)(2,1)S(1)}, u32[]{:S(2)}, u32[]{:S(2)}) collective-permute-start(bf16[32,1792]{1,0:T(8,128)(2,1)S(1)} %bitcast.132), channel_id=1, source_target_pairs={{0,2},{1,3},{2,0},{3,1},{4,6},{5,7},{6,4},{7,5},{8,10},{9,11},{10,... | collective-permute-start | bytes 344072 | tf_op jit(solution)/shard_map/ppermute | solution.py:11
  13.9 12.9 %copy-start.1 = (bf16[1,2,2,128,1792]{4,3,2,1,0:T(8,128)(2,1)S(1)}, bf16[1,2,2,128,1792]{4,3,2,1,0:T(8,128)(2,1)}, u32[]{:S(2)}) copy-start(bf16[1,2,2,128,1792]{4,3,2,1,0:T(8,128)(2,1)} %param.10) | copy-start | bytes 5505028
  21.4 1.4 %collective-permute-start.7 = (f32[128,256]{1,0:T(8,128)S(1)}, f32[128,256]{1,0:T(8,128)S(1)}, u32[]{:S(2)}, u32[]{:S(2)}) collective-permute-start(f32[128,256]{1,0:T(8,128)S(1)} %convolution_add_fusion.4), channel_id=1, source_target_pairs={{0,8},{8,0},{16,24},{24,16},{1,9},{9,1},{17,25},{25,17},{2,10},{10... | collective-permute-start | bytes 393224 | tf_op jit(solution)/shard_map/ppermute | solution.py:11
  22.9 4.3 %collective-permute-start.8 = (bf16[128,256]{1,0:T(8,128)(2,1)S(1)}, bf16[128,256]{1,0:T(8,128)(2,1)S(1)}, u32[]{:S(2)}, u32[]{:S(2)}) collective-permute-start(bf16[128,256]{1,0:T(8,128)(2,1)S(1)} %multiply_convert_fusion), channel_id=1, source_target_pairs={{0,16},{8,24},{16,0},{24,8},{1,17},{9,25},{17,1},{25,9},{2,18},{10... | collective-permute-start | bytes 196616 | tf_op jit(solution)/shard_map/ppermute | solution.py:11
  23.8 5.2 %collective-permute-start.10 = (bf16[128,256]{1,0:T(8,128)(2,1)S(1)}, bf16[128,256]{1,0:T(8,128)(2,1)S(1)}, u32[]{:S(2)}, u32[]{:S(2)}) collective-permute-start(bf16[128,256]{1,0:T(8,128)(2,1)S(1)} %bitcast.144), channel_id=1, source_target_pairs={{0,1},{1,0},{2,3},{3,2},{4,5},{5,4},{6,7},{7,6},{8,9},{9,8},{10,11... | collective-permute-start | bytes 196616 | tf_op jit(solution)/shard_map/ppermute | solution.py:11
  26.2 9.6 %collective-permute-start.16 = (bf16[16,896]{1,0:T(8,128)(2,1)S(1)}, bf16[16,896]{1,0:T(8,128)(2,1)S(1)}, u32[]{:S(2)}, u32[]{:S(2)}) collective-permute-start(bf16[16,896]{1,0:T(8,128)(2,1)S(1)} %get-tuple-element.63), channel_id=1, source_target_pairs={{0,1},{1,0},{2,3},{3,2},{4,5},{5,4},{6,7},{7,6},{8,9},{9,8},{10,11... | collective-permute-start | bytes 86024 | tf_op jit(solution)/shard_map/ppermute | solution.py:11
  27.4 4.9 %collective-permute-start.9 = (bf16[64,896]{1,0:T(8,128)(2,1)S(1)}, bf16[64,896]{1,0:T(8,128)(2,1)S(1)}, u32[]{:S(2)}, u32[]{:S(2)}) collective-permute-start(bf16[64,896]{1,0:T(8,128)(2,1)S(1)} %fusion.1), channel_id=1, source_target_pairs={{0,1},{1,0},{2,3},{3,2},{4,5},{5,4},{6,7},{7,6},{8,9},{9,8},{10,11... | collective-permute-start | bytes 344072 | tf_op jit(solution)/shard_map/ppermute | solution.py:11
  29.5 11.1 %collective-permute-start.15 = (bf16[32,896]{1,0:T(8,128)(2,1)S(1)}, bf16[32,896]{1,0:T(8,128)(2,1)S(1)}, u32[]{:S(2)}, u32[]{:S(2)}) collective-permute-start(bf16[32,896]{1,0:T(8,128)(2,1)S(1)} %get-tuple-element.66), channel_id=1, source_target_pairs={{0,6},{1,7},{2,4},{3,5},{4,2},{5,3},{6,0},{7,1},{8,14},{9,15},{10,... | collective-permute-start | bytes 172040 | tf_op jit(solution)/shard_map/ppermute | solution.py:11
  32.0 8.6 %collective-permute-start.14 = (bf16[32,896]{1,0:T(8,128)(2,1)S(1)}, bf16[32,896]{1,0:T(8,128)(2,1)S(1)}, u32[]{:S(2)}, u32[]{:S(2)}) collective-permute-start(bf16[32,896]{1,0:T(8,128)(2,1)S(1)} %get-tuple-element.67), channel_id=1, source_target_pairs={{0,4},{1,5},{2,6},{3,7},{4,0},{5,1},{6,2},{7,3},{8,12},{9,13},{10,... | collective-permute-start | bytes 172040 | tf_op jit(solution)/shard_map/ppermute | solution.py:11
  32.4 8.3 %collective-permute-start.13 = (bf16[16,896]{1,0:T(8,128)(2,1)S(1)}, bf16[16,896]{1,0:T(8,128)(2,1)S(1)}, u32[]{:S(2)}, u32[]{:S(2)}) collective-permute-start(bf16[16,896]{1,0:T(8,128)(2,1)S(1)} %get-tuple-element.73), channel_id=1, source_target_pairs={{0,6},{1,7},{2,4},{3,5},{4,2},{5,3},{6,0},{7,1},{8,14},{9,15},{10,... | collective-permute-start | bytes 86024 | tf_op jit(solution)/shard_map/ppermute | solution.py:11
  34.9 5.7 %collective-permute-start.12 = (bf16[16,896]{1,0:T(8,128)(2,1)S(1)}, bf16[16,896]{1,0:T(8,128)(2,1)S(1)}, u32[]{:S(2)}, u32[]{:S(2)}) collective-permute-start(bf16[16,896]{1,0:T(8,128)(2,1)S(1)} %get-tuple-element.74), channel_id=1, source_target_pairs={{0,4},{1,5},{2,6},{3,7},{4,0},{5,1},{6,2},{7,3},{8,12},{9,13},{10,... | collective-permute-start | bytes 86024 | tf_op jit(solution)/shard_map/ppermute | solution.py:11
  35.8 4.8 %collective-permute-start.11 = (bf16[48,896]{1,0:T(8,128)(2,1)S(1)}, bf16[48,896]{1,0:T(8,128)(2,1)S(1)}, u32[]{:S(2)}, u32[]{:S(2)}) collective-permute-start(bf16[48,896]{1,0:T(8,128)(2,1)S(1)} %pad_maximum_fusion.6), channel_id=1, source_target_pairs={{0,2},{1,3},{2,0},{3,1},{4,6},{5,7},{6,4},{7,5},{8,10},{9,11},{10,... | collective-permute-start | bytes 258056 | tf_op jit(solution)/shard_map/ppermute | solution.py:11
  40.7 6.8 %collective-permute-start.22 = (bf16[16,896]{1,0:T(8,128)(2,1)S(1)}, bf16[16,896]{1,0:T(8,128)(2,1)S(1)}, u32[]{:S(2)}, u32[]{:S(2)}) collective-permute-start(bf16[16,896]{1,0:T(8,128)(2,1)S(1)} %subtract_convert_fusion), channel_id=1, source_target_pairs={{0,6},{1,7},{2,4},{3,5},{4,2},{5,3},{6,0},{7,1},{8,14},{9,15},{10,... | collective-permute-start | bytes 86024 | tf_op jit(solution)/shard_map/ppermute | solution.py:11
  43.0 6.7 %collective-permute-start.21 = (bf16[16,896]{1,0:T(8,128)(2,1)S(1)}, bf16[16,896]{1,0:T(8,128)(2,1)S(1)}, u32[]{:S(2)}, u32[]{:S(2)}) collective-permute-start(bf16[16,896]{1,0:T(8,128)(2,1)S(1)} %subtract_convert_fusion), channel_id=1, source_target_pairs={{0,4},{1,5},{2,6},{3,7},{4,0},{5,1},{6,2},{7,3},{8,12},{9,13},{10,... | collective-permute-start | bytes 86024 | tf_op jit(solution)/shard_map/ppermute | solution.py:11
  43.0 6.6 %collective-permute-start.20 = (bf16[16,896]{1,0:T(8,128)(2,1)S(1)}, bf16[16,896]{1,0:T(8,128)(2,1)S(1)}, u32[]{:S(2)}, u32[]{:S(2)}) collective-permute-start(bf16[16,896]{1,0:T(8,128)(2,1)S(1)} %subtract_convert_fusion), channel_id=1, source_target_pairs={{0,2},{1,3},{2,0},{3,1},{4,6},{5,7},{6,4},{7,5},{8,10},{9,11},{10,... | collective-permute-start | bytes 86024 | tf_op jit(solution)/shard_map/ppermute | solution.py:11
  45.2 6.0 %collective-permute-start.19 = (bf16[32,896]{1,0:T(8,128)(2,1)S(1)}, bf16[32,896]{1,0:T(8,128)(2,1)S(1)}, u32[]{:S(2)}, u32[]{:S(2)}) collective-permute-start(bf16[32,896]{1,0:T(8,128)(2,1)S(1)} %fusion.21), channel_id=1, source_target_pairs={{0,6},{1,7},{2,4},{3,5},{4,2},{5,3},{6,0},{7,1},{8,14},{9,15},{10,... | collective-permute-start | bytes 172040 | tf_op jit(solution)/shard_map/ppermute | solution.py:11
  47.5 5.1 %collective-permute-start.18 = (bf16[32,896]{1,0:T(8,128)(2,1)S(1)}, bf16[32,896]{1,0:T(8,128)(2,1)S(1)}, u32[]{:S(2)}, u32[]{:S(2)}) collective-permute-start(bf16[32,896]{1,0:T(8,128)(2,1)S(1)} %fusion.21), channel_id=1, source_target_pairs={{0,4},{1,5},{2,6},{3,7},{4,0},{5,1},{6,2},{7,3},{8,12},{9,13},{10,... | collective-permute-start | bytes 172040 | tf_op jit(solution)/shard_map/ppermute | solution.py:11
  47.5 5.1 %collective-permute-start.17 = (bf16[32,896]{1,0:T(8,128)(2,1)S(1)}, bf16[32,896]{1,0:T(8,128)(2,1)S(1)}, u32[]{:S(2)}, u32[]{:S(2)}) collective-permute-start(bf16[32,896]{1,0:T(8,128)(2,1)S(1)} %fusion.21), channel_id=1, source_target_pairs={{0,2},{1,3},{2,0},{3,1},{4,6},{5,7},{6,4},{7,5},{8,10},{9,11},{10,... | collective-permute-start | bytes 172040 | tf_op jit(solution)/shard_map/ppermute | solution.py:11
  49.7 4.9 %collective-permute-start.23 = (bf16[64,896]{1,0:T(8,128)(2,1)S(1)}, bf16[64,896]{1,0:T(8,128)(2,1)S(1)}, u32[]{:S(2)}, u32[]{:S(2)}) collective-permute-start(bf16[64,896]{1,0:T(8,128)(2,1)S(1)} %pad_maximum_fusion.5), channel_id=1, source_target_pairs={{0,1},{1,0},{2,3},{3,2},{4,5},{5,4},{6,7},{7,6},{8,9},{9,8},{10,11... | collective-permute-start | bytes 344072 | tf_op jit(solution)/shard_map/ppermute | solution.py:11
  55.5 1.5 %collective-permute-start.24 = (f32[384,128]{1,0:T(8,128)S(1)}, f32[384,128]{1,0:T(8,128)S(1)}, u32[]{:S(2)}, u32[]{:S(2)}) collective-permute-start(f32[384,128]{1,0:T(8,128)S(1)} %slice_select_fusion), channel_id=1, source_target_pairs={{0,8},{8,0},{16,24},{24,16},{1,9},{9,1},{17,25},{25,17},{2,10},{10... | collective-permute-start | bytes 589832 | tf_op jit(solution)/shard_map/ppermute | solution.py:11
  55.6 8.4 %collective-permute-start.27 = (bf16[128,1792]{1,0:T(8,128)(2,1)S(1)}, bf16[128,1792]{1,0:T(8,128)(2,1)S(1)}, u32[]{:S(2)}, u32[]{:S(2)}) collective-permute-start(bf16[128,1792]{1,0:T(8,128)(2,1)S(1)} %constant_dynamic-update-slice_fusion), channel_id=1, source_target_pairs={{0,8},{8,0},{16,24},{24,16},{1,9},{9,1},{17,25},{25,17},{2,10},{10... | collective-permute-start | bytes 1376264 | tf_op jit(solution)/shard_map/ppermute | solution.py:11
  57.2 4.3 %collective-permute-start.26 = (bf16[240,128]{1,0:T(8,128)(2,1)S(1)}, bf16[240,128]{1,0:T(8,128)(2,1)S(1)}, u32[]{:S(2)}, u32[]{:S(2)}) collective-permute-start(bf16[240,128]{1,0:T(8,128)(2,1)S(1)} %constant_dynamic-update-slice_fusion.19), channel_id=1, source_target_pairs={{0,16},{8,24},{16,0},{24,8},{1,17},{9,25},{17,1},{25,9},{2,18},{10... | collective-permute-start | bytes 184328 | tf_op jit(solution)/shard_map/ppermute | solution.py:11
  58.5 4.2 %collective-permute-start.25 = (bf16[240,128]{1,0:T(8,128)(2,1)S(1)}, bf16[240,128]{1,0:T(8,128)(2,1)S(1)}, u32[]{:S(2)}, u32[]{:S(2)}) collective-permute-start(bf16[240,128]{1,0:T(8,128)(2,1)S(1)} %constant_dynamic-update-slice_fusion.4), channel_id=1, source_target_pairs={{0,1},{1,0},{2,3},{3,2},{4,5},{5,4},{6,7},{7,6},{8,9},{9,8},{10,11... | collective-permute-start | bytes 184328 | tf_op jit(solution)/shard_map/ppermute | solution.py:11

commit v16 on v15

--- a/solution.py
+++ b/solution.py
@@ -75,11 +75,8 @@
     def both_along_z(shared, own):
         count = shared[1].shape[0]
         out = [[shared[0]] + [None] * (far - 1), [own[0]] + [None] * (far - 1)]
-        for k in range(far - 1, 1, -1):
+        for k in range(far - 1, 0, -1):
             out[0][k] = crossed(shared[k], "latent", 2 * k)
-        nearest = crossed(jnp.concatenate([shared[1], own[1]], axis=0), "latent", 2)
-        out[0][1], out[1][1] = nearest[:count], nearest[count:]
-        for k in range(far - 1, 1, -1):
             out[1][k] = crossed(own[k], "latent", 2 * k)
         return out
 
@@ -136,9 +133,11 @@
     staying = times(rows_at(acts, 0), shared_mine) + times(rows_at(acts_y, 0), shared_other)
     arrived = over_x(leaving.astype(BF16))
     product = times(acts, own_mine) + times(acts_x, own_other)
-    arrived, staying = hold((arrived, staying))
-    shared_terms, own_terms = both_along_z(pieces_of(staying + arrived.astype(F32)), pieces_of(product))
-    terms = hold((*shared_terms, *own_terms))
+    own_pieces = pieces_of(product)
+    arrived, staying, own_pieces[1] = hold((arrived, staying, own_pieces[1]))
+    shared_terms, own_terms = both_along_z(pieces_of(staying + arrived.astype(F32)), own_pieces)
+    terms = hold((*shared_terms, *own_terms[2:]))
+    terms = (*terms[:far], own_terms[0], own_terms[1], *terms[far:])
     aim_mine, aim_shared = hold((aim_own(side), aim_shared))
     err_shared = (added(terms[:far]) - aim_shared.astype(F32)).astype(BF16)
     err_own = (added(terms[far:]) - paired(aim_mine, aim_other).astype(F32)).astype(BF16)

time: 65.7 us -> 65 us (0.989)
  waiting for transfers between devices: 19.7 us -> 17.3 us
  starting transfers between devices: 34.3 us -> 36.1 us
    ppermute x28 -> x29, waiting for transfers between devices: 19.7 us -> 17.3 us  [crossed(): lax.ppermute(block, axis, [(i, i ^ mask) for i in range(lax.axis_size(axi...]
    ppermute x28 -> x29, starting transfers between devices: 34.3 us -> 36.1 us  [crossed(): lax.ppermute(block, axis, [(i, i ^ mask) for i in range(lax.axis_size(axi...]
  transfers between devices with their start and end apart: 28 -> 29, of which waited for: 11 -> 12; matrix products, arithmetic and copies ran while one was open for 11% -> 13% of each run, Pallas kernels for 0% -> 0%
where the time goes in v16:
time: 65 us; the launch traced here: 64.8 us
  starting transfers between devices  36.1 us (56%)
  waiting for transfers between devices  17.3 us (27%)
  matrix products  4.15 us (6%)
  local copies, waits for them, and re-layouts  3.22 us (5%)
  other arithmetic  2.89 us (4%)
  between operations  1.06 us (2%)
    ppermute x29, starting transfers between devices, crossed(): lax.ppermute(block, axis, [(i, i ^ mask) for i in range(lax.axis_size(axi...  36.1 us
    ppermute x29, waiting for transfers between devices, crossed(): lax.ppermute(block, axis, [(i, i ^ mask) for i in range(lax.axis_size(axi...  17.3 us
    dot_general x7, matrix products, times(): return jnp.dot(left, right, preferred_element_type=F32)  1.6 us
    dot_general x1, matrix products, encoder_gradient(): lax.dot_general(whole, grad_low, (((0,), (0,)), ((), ())), preferred_elem...  1.37 us
  transfers between devices with their start and end apart: 29, of which 12 were waited for; matrix products, arithmetic and copies ran while one was open for 13% of the time, Pallas kernels for 0%

profile of v16, /device:TPU:0, one launch (start us, length us, event | category | flops | bytes accessed | tf_op | source)
XLA Modules:
  0.0 64.8 jit_solution(15055243465769764081)
XLA Ops:
  0.6 0.0 copy-start
  0.7 0.5 collective-permute-start.3
  1.2 0.8 %dynamic-slice_bitcast_fusion.3 = (bf16[1,1,16,1792]{3,2,1,0:T(8,128)(2,1)S(1)}, bf16[16,1792]{1,0:T(8,128)(2,1)S(1)}) fusion(bf16[2,16,3584]{2,1,0:T(8,128)(2,1)} %param.6, s32[]{:T(128)S(6)} %select_n.180, s32[]{:T(128)S(6)} %select_n.185), kind=kLoop, calls=%fused_computation.91 | loop fusion | bytes 172040 | tf_op jit(solution)/shard_map/reshape;squeeze | solution.py:100
  2.0 2.6 %collective-permute-start.2 = (bf16[16,1792]{1,0:T(8,128)(2,1)S(1)}, bf16[16,1792]{1,0:T(8,128)(2,1)S(1)}, u32[]{:S(2)}, u32[]{:S(2)}) collective-permute-start(bf16[16,1792]{1,0:T(8,128)(2,1)S(1)} %get-tuple-element.68), channel_id=1, source_target_pairs={{0,1},{1,0},{2,3},{3,2},{4,5},{5,4},{6,7},{7,6},{8,9},{9,8},{10,11... | collective-permute-start | bytes 172040 | tf_op jit(solution)/shard_map/ppermute | solution.py:11
  4.6 1.2 %dynamic-slice_bitcast_fusion = (bf16[256,896]{1,0:T(8,128)(2,1)S(1)}, bf16[256,896]{1,0:T(8,128)(2,1)S(1)}) fusion(bf16[2,256,1792]{2,1,0:T(8,128)(2,1)} %bitcast.119, s32[]{:T(128)S(6)} %select_n.182, s32[]{:T(128)S(6)} %select_n.183, s32[]{:T(128)S(6)} %select_n.180, s32[]{:T(128)S(6)} %select_n.181), kind=kLoop, calls=%fused_computation.24 | loop fusion | bytes 1835024 | tf_op jit(solution)/shard_map/squeeze | solution.py:91
  5.9 1.6 %collective-permute-start.1 = (bf16[256,896]{1,0:T(8,128)(2,1)S(1)}, bf16[256,896]{1,0:T(8,128)(2,1)S(1)}, u32[]{:S(2)}, u32[]{:S(2)}) collective-permute-start(bf16[256,896]{1,0:T(8,128)(2,1)S(1)} %get-tuple-element.57), channel_id=1, source_target_pairs={{0,16},{8,24},{16,0},{24,8},{1,17},{9,25},{17,1},{25,9},{2,18},{10... | collective-permute-start | bytes 1376264 | tf_op jit(solution)/shard_map/ppermute | solution.py:11
  7.5 0.5 collective-permute-start
  8.0 0.0 collective-permute-done.3
  8.0 3.7 %collective-permute-start.6 = (bf16[32,1792]{1,0:T(8,128)(2,1)S(1)}, bf16[32,1792]{1,0:T(8,128)(2,1)S(1)}, u32[]{:S(2)}, u32[]{:S(2)}) collective-permute-start(bf16[32,1792]{1,0:T(8,128)(2,1)S(1)} %bitcast.130), channel_id=1, source_target_pairs={{0,6},{1,7},{2,4},{3,5},{4,2},{5,3},{6,0},{7,1},{8,14},{9,15},{10,... | collective-permute-start | bytes 344072 | tf_op jit(solution)/shard_map/ppermute | solution.py:11
  11.7 0.0 collective-permute-start.5
  11.7 0.8 %collective-permute-start.4 = (bf16[32,1792]{1,0:T(8,128)(2,1)S(1)}, bf16[32,1792]{1,0:T(8,128)(2,1)S(1)}, u32[]{:S(2)}, u32[]{:S(2)}) collective-permute-start(bf16[32,1792]{1,0:T(8,128)(2,1)S(1)} %bitcast.132), channel_id=1, source_target_pairs={{0,2},{1,3},{2,0},{3,1},{4,6},{5,7},{6,4},{7,5},{8,10},{9,11},{10,... | collective-permute-start | bytes 344072 | tf_op jit(solution)/shard_map/ppermute | solution.py:11
  12.5 1.2 %bitcast_select_fusion.1 = (bf16[1792,128]{1,0:T(8,128)(2,1)S(1)}, bf16[1792,128]{1,0:T(8,128)(2,1)S(1)}) fusion(pred[]{:T(512)S(6)} %eq.48, bf16[3584,128]{1,0:T(8,128)(2,1)} %collective-permute-done.3, s32[]{:T(128)S(6)} %select_n.185, bf16[1,3584,128]{2,1,0:T(8,128)(2,1)S(1)} %copy-done.2), kind=kLoop, calls=%fused_computation.23 | loop fusion | flops 458752 | bytes 1835013 | tf_op jit(solution)/shard_map/jit(_where)/select_n | solution.py:23
  13.8 0.1 compare_reduce_fusion
  13.9 0.0 copy-start.1
  13.9 4.6 %collective-permute-done.1 = bf16[256,896]{1,0:T(8,128)(2,1)S(1)} collective-permute-done((bf16[256,896]{1,0:T(8,128)(2,1)S(1)}, bf16[256,896]{1,0:T(8,128)(2,1)S(1)}, u32[]{:S(2)}, u32[]{:S(2)}) %collective-permute-start.1) | collective-permute-done | bytes 458784 | tf_op jit(solution)/shard_map/ppermute | solution.py:11
  18.5 1.2 %collective-permute-done = bf16[256,896]{1,0:T(8,128)(2,1)S(1)} collective-permute-done((bf16[256,896]{1,0:T(8,128)(2,1)S(1)}, bf16[256,896]{1,0:T(8,128)(2,1)S(1)}, u32[]{:S(2)}, u32[]{:S(2)}) %collective-permute-start) | collective-permute-done | bytes 458784 | tf_op jit(solution)/shard_map/ppermute | solution.py:11
  19.7 0.0 collective-permute-done.6
  19.7 1.4 %collective-permute-done.5 = bf16[32,1792]{1,0:T(8,128)(2,1)S(1)} collective-permute-done((bf16[32,1792]{1,0:T(8,128)(2,1)S(1)}, bf16[32,1792]{1,0:T(8,128)(2,1)S(1)}, u32[]{:S(2)}, u32[]{:S(2)}) %collective-permute-start.5) | collective-permute-done | bytes 114720 | tf_op jit(solution)/shard_map/ppermute | solution.py:11
  21.1 0.0 collective-permute-done.4
  21.1 0.3 convolution_add_fusion.4
  21.4 0.1 collective-permute-start.7
  21.5 1.3 %collective-permute-done.7 = f32[128,256]{1,0:T(8,128)S(1)} collective-permute-done((f32[128,256]{1,0:T(8,128)S(1)}, f32[128,256]{1,0:T(8,128)S(1)}, u32[]{:S(2)}, u32[]{:S(2)}) %collective-permute-start.7) | collective-permute-done | bytes 131104 | tf_op jit(solution)/shard_map/ppermute | solution.py:11
  22.9 0.9 %collective-permute-start.9 = (bf16[128,256]{1,0:T(8,128)(2,1)S(1)}, bf16[128,256]{1,0:T(8,128)(2,1)S(1)}, u32[]{:S(2)}, u32[]{:S(2)}) collective-permute-start(bf16[128,256]{1,0:T(8,128)(2,1)S(1)} %multiply_convert_fusion), channel_id=1, source_target_pairs={{0,16},{8,24},{16,0},{24,8},{1,17},{9,25},{17,1},{25,9},{2,18},{10... | collective-permute-start | bytes 196616 | tf_op jit(solution)/shard_map/ppermute | solution.py:11
  23.8 1.6 %collective-permute-start.8 = (bf16[128,256]{1,0:T(8,128)(2,1)S(1)}, bf16[128,256]{1,0:T(8,128)(2,1)S(1)}, u32[]{:S(2)}, u32[]{:S(2)}) collective-permute-start(bf16[128,256]{1,0:T(8,128)(2,1)S(1)} %bitcast.144), channel_id=1, source_target_pairs={{0,1},{1,0},{2,3},{3,2},{4,5},{5,4},{6,7},{7,6},{8,9},{9,8},{10,11... | collective-permute-start | bytes 196616 | tf_op jit(solution)/shard_map/ppermute | solution.py:11
  25.4 0.8 %dynamic-slice_bitcast_fusion.4 = (bf16[16,896]{1,0:T(8,128)(2,1)S(1)}, bf16[16,896]{1,0:T(8,128)(2,1)S(1)}, bf16[16,896]{1,0:T(8,128)(2,1)S(1)}) fusion(bf16[3,16,3584]{2,1,0:T(8,128)(2,1)} %param.7, s32[]{:T(128)S(6)} %select_n.197, s32[]{:T(128)S(6)} %select_n.200, s32[]{:T(128)S(6)} %select_n.199, s32[]{:T(128)S(6)} %select_n.198), kind=kLoop, calls=%fused_computation.98 | loop fusion | bytes 172048 | tf_op jit(solution)/shard_map/squeeze | solution.py:127
  26.2 0.6 collective-permute-start.17
  26.8 0.2 fusion.10
  27.0 0.2 fusion.12
  27.2 0.2 fusion.1
  27.4 1.5 %collective-permute-start.10 = (bf16[64,896]{1,0:T(8,128)(2,1)S(1)}, bf16[64,896]{1,0:T(8,128)(2,1)S(1)}, u32[]{:S(2)}, u32[]{:S(2)}) collective-permute-start(bf16[64,896]{1,0:T(8,128)(2,1)S(1)} %fusion.1), channel_id=1, source_target_pairs={{0,1},{1,0},{2,3},{3,2},{4,5},{5,4},{6,7},{7,6},{8,9},{9,8},{10,11... | collective-permute-start | bytes 344072 | tf_op jit(solution)/shard_map/ppermute | solution.py:11
  29.0 0.2 fusion.54
  29.2 0.2 fusion.53
  29.5 2.5 %collective-permute-start.16 = (bf16[32,896]{1,0:T(8,128)(2,1)S(1)}, bf16[32,896]{1,0:T(8,128)(2,1)S(1)}, u32[]{:S(2)}, u32[]{:S(2)}) collective-permute-start(bf16[32,896]{1,0:T(8,128)(2,1)S(1)} %get-tuple-element.64), channel_id=1, source_target_pairs={{0,6},{1,7},{2,4},{3,5},{4,2},{5,3},{6,0},{7,1},{8,14},{9,15},{10,... | collective-permute-start | bytes 172040 | tf_op jit(solution)/shard_map/ppermute | solution.py:11
  32.0 0.2 convolution_add_fusion.1
  32.3 0.0 collective-permute-done.10
  32.4 2.5 %collective-permute-start.14 = (bf16[16,896]{1,0:T(8,128)(2,1)S(1)}, bf16[16,896]{1,0:T(8,128)(2,1)S(1)}, u32[]{:S(2)}, u32[]{:S(2)}) collective-permute-start(bf16[16,896]{1,0:T(8,128)(2,1)S(1)} %get-tuple-element.71), channel_id=1, source_target_pairs={{0,6},{1,7},{2,4},{3,5},{4,2},{5,3},{6,0},{7,1},{8,14},{9,15},{10,... | collective-permute-start | bytes 86024 | tf_op jit(solution)/shard_map/ppermute | solution.py:11
  34.9 0.9 %collective-permute-start.13 = (bf16[16,896]{1,0:T(8,128)(2,1)S(1)}, bf16[16,896]{1,0:T(8,128)(2,1)S(1)}, u32[]{:S(2)}, u32[]{:S(2)}) collective-permute-start(bf16[16,896]{1,0:T(8,128)(2,1)S(1)} %get-tuple-element.72), channel_id=1, source_target_pairs={{0,4},{1,5},{2,6},{3,7},{4,0},{5,1},{6,2},{7,3},{8,12},{9,13},{10,... | collective-permute-start | bytes 86024 | tf_op jit(solution)/shard_map/ppermute | solution.py:11
  35.8 1.0 %collective-permute-start.12 = (bf16[16,896]{1,0:T(8,128)(2,1)S(1)}, bf16[16,896]{1,0:T(8,128)(2,1)S(1)}, u32[]{:S(2)}, u32[]{:S(2)}) collective-permute-start(bf16[16,896]{1,0:T(8,128)(2,1)S(1)} %get-tuple-element.73), channel_id=1, source_target_pairs={{0,2},{1,3},{2,0},{3,1},{4,6},{5,7},{6,4},{7,5},{8,10},{9,11},{10,... | collective-permute-start | bytes 86024 | tf_op jit(solution)/shard_map/ppermute | solution.py:11
  36.9 1.0 %collective-permute-start.11 = (bf16[32,896]{1,0:T(8,128)(2,1)S(1)}, bf16[32,896]{1,0:T(8,128)(2,1)S(1)}, u32[]{:S(2)}, u32[]{:S(2)}) collective-permute-start(bf16[32,896]{1,0:T(8,128)(2,1)S(1)} %get-tuple-element.38), channel_id=1, source_target_pairs={{0,2},{1,3},{2,0},{3,1},{4,6},{5,7},{6,4},{7,5},{8,10},{9,11},{10,... | collective-permute-start | bytes 172040 | tf_op jit(solution)/shard_map/ppermute | solution.py:11
  37.9 0.6 collective-permute-done.15
  38.5 1.2 %collective-permute-done.13 = bf16[16,896]{1,0:T(8,128)(2,1)S(1)} collective-permute-done((bf16[16,896]{1,0:T(8,128)(2,1)S(1)}, bf16[16,896]{1,0:T(8,128)(2,1)S(1)}, u32[]{:S(2)}, u32[]{:S(2)}) %collective-permute-start.13) | collective-permute-done | bytes 28704 | tf_op jit(solution)/shard_map/ppermute | solution.py:11
  39.8 0.2 collective-permute-done.12
  40.0 2.2 %collective-permute-start.23 = (bf16[16,896]{1,0:T(8,128)(2,1)S(1)}, bf16[16,896]{1,0:T(8,128)(2,1)S(1)}, u32[]{:S(2)}, u32[]{:S(2)}) collective-permute-start(bf16[16,896]{1,0:T(8,128)(2,1)S(1)} %subtract_convert_fusion), channel_id=1, source_target_pairs={{0,6},{1,7},{2,4},{3,5},{4,2},{5,3},{6,0},{7,1},{8,14},{9,15},{10,... | collective-permute-start | bytes 86024 | tf_op jit(solution)/shard_map/ppermute | solution.py:11
  42.2 0.0 collective-permute-start.22
  42.2 2.2 %collective-permute-start.21 = (bf16[16,896]{1,0:T(8,128)(2,1)S(1)}, bf16[16,896]{1,0:T(8,128)(2,1)S(1)}, u32[]{:S(2)}, u32[]{:S(2)}) collective-permute-start(bf16[16,896]{1,0:T(8,128)(2,1)S(1)} %subtract_convert_fusion), channel_id=1, source_target_pairs={{0,2},{1,3},{2,0},{3,1},{4,6},{5,7},{6,4},{7,5},{8,10},{9,11},{10,... | collective-permute-start | bytes 86024 | tf_op jit(solution)/shard_map/ppermute | solution.py:11
  44.5 2.2 %collective-permute-start.20 = (bf16[32,896]{1,0:T(8,128)(2,1)S(1)}, bf16[32,896]{1,0:T(8,128)(2,1)S(1)}, u32[]{:S(2)}, u32[]{:S(2)}) collective-permute-start(bf16[32,896]{1,0:T(8,128)(2,1)S(1)} %fusion.24), channel_id=1, source_target_pairs={{0,6},{1,7},{2,4},{3,5},{4,2},{5,3},{6,0},{7,1},{8,14},{9,15},{10,... | collective-permute-start | bytes 172040 | tf_op jit(solution)/shard_map/ppermute | solution.py:11
  46.7 2.2 %collective-permute-start.18 = (bf16[32,896]{1,0:T(8,128)(2,1)S(1)}, bf16[32,896]{1,0:T(8,128)(2,1)S(1)}, u32[]{:S(2)}, u32[]{:S(2)}) collective-permute-start(bf16[32,896]{1,0:T(8,128)(2,1)S(1)} %fusion.24), channel_id=1, source_target_pairs={{0,2},{1,3},{2,0},{3,1},{4,6},{5,7},{6,4},{7,5},{8,10},{9,11},{10,... | collective-permute-start | bytes 172040 | tf_op jit(solution)/shard_map/ppermute | solution.py:11
  49.0 1.7 %collective-permute-start.24 = (bf16[64,896]{1,0:T(8,128)(2,1)S(1)}, bf16[64,896]{1,0:T(8,128)(2,1)S(1)}, u32[]{:S(2)}, u32[]{:S(2)}) collective-permute-start(bf16[64,896]{1,0:T(8,128)(2,1)S(1)} %pad_maximum_fusion.5), channel_id=1, source_target_pairs={{0,1},{1,0},{2,3},{3,2},{4,5},{5,4},{6,7},{7,6},{8,9},{9,8},{10,11... | collective-permute-start | bytes 344072 | tf_op jit(solution)/shard_map/ppermute | solution.py:11
  50.7 1.1 %collective-permute-done.19 = bf16[32,896]{1,0:T(8,128)(2,1)S(1)} collective-permute-done((bf16[32,896]{1,0:T(8,128)(2,1)S(1)}, bf16[32,896]{1,0:T(8,128)(2,1)S(1)}, u32[]{:S(2)}, u32[]{:S(2)}) %collective-permute-start.19) | collective-permute-done | bytes 57376 | tf_op jit(solution)/shard_map/ppermute | solution.py:11
  51.8 0.3 fusion.27
  52.1 1.7 %collective-permute-done.24 = bf16[64,896]{1,0:T(8,128)(2,1)S(1)} collective-permute-done((bf16[64,896]{1,0:T(8,128)(2,1)S(1)}, bf16[64,896]{1,0:T(8,128)(2,1)S(1)}, u32[]{:S(2)}, u32[]{:S(2)}) %collective-permute-start.24) | collective-permute-done | bytes 114720 | tf_op jit(solution)/shard_map/ppermute | solution.py:11
  53.8 0.3 fusion.55
  54.1 0.3 fusion.8
  54.5 0.3 convolution_add_fusion.3
  54.8 0.1 collective-permute-start.25
  54.9 1.4 %collective-permute-done.25 = f32[384,128]{1,0:T(8,128)S(1)} collective-permute-done((f32[384,128]{1,0:T(8,128)S(1)}, f32[384,128]{1,0:T(8,128)S(1)}, u32[]{:S(2)}, u32[]{:S(2)}) %collective-permute-start.25) | collective-permute-done | bytes 196640 | tf_op jit(solution)/shard_map/ppermute | solution.py:11
  56.6 1.3 %collective-permute-start.27 = (bf16[240,128]{1,0:T(8,128)(2,1)S(1)}, bf16[240,128]{1,0:T(8,128)(2,1)S(1)}, u32[]{:S(2)}, u32[]{:S(2)}) collective-permute-start(bf16[240,128]{1,0:T(8,128)(2,1)S(1)} %constant_dynamic-update-slice_fusion.19), channel_id=1, source_target_pairs={{0,16},{8,24},{16,0},{24,8},{1,17},{9,25},{17,1},{25,9},{2,18},{10... | collective-permute-start | bytes 184328 | tf_op jit(solution)/shard_map/ppermute | solution.py:11
  57.8 1.7 %collective-permute-start.26 = (bf16[240,128]{1,0:T(8,128)(2,1)S(1)}, bf16[240,128]{1,0:T(8,128)(2,1)S(1)}, u32[]{:S(2)}, u32[]{:S(2)}) collective-permute-start(bf16[240,128]{1,0:T(8,128)(2,1)S(1)} %constant_dynamic-update-slice_fusion.4), channel_id=1, source_target_pairs={{0,1},{1,0},{2,3},{3,2},{4,5},{5,4},{6,7},{7,6},{8,9},{9,8},{10,11... | collective-permute-start | bytes 184328 | tf_op jit(solution)/shard_map/ppermute | solution.py:11
  59.5 1.3 %collective-permute-done.27 = bf16[240,128]{1,0:T(8,128)(2,1)S(1)} collective-permute-done((bf16[240,128]{1,0:T(8,128)(2,1)S(1)}, bf16[240,128]{1,0:T(8,128)(2,1)S(1)}, u32[]{:S(2)}, u32[]{:S(2)}) %collective-permute-start.27) | collective-permute-done | bytes 61472 | tf_op jit(solution)/shard_map/ppermute | solution.py:11
  60.9 1.1 %collective-permute-done.26 = bf16[240,128]{1,0:T(8,128)(2,1)S(1)} collective-permute-done((bf16[240,128]{1,0:T(8,128)(2,1)S(1)}, bf16[240,128]{1,0:T(8,128)(2,1)S(1)}, u32[]{:S(2)}, u32[]{:S(2)}) %collective-permute-start.26) | collective-permute-done | bytes 61472 | tf_op jit(solution)/shard_map/ppermute | solution.py:11
  62.1 0.5 fusion.29
  62.7 0.6 maximum_select_fusion
  63.3 0.1 broadcast_select_fusion.1
  63.4 1.4 %fusion = bf16[1,3584,128]{2,1,0:T(8,128)(2,1)} fusion(bf16[128,1792]{1,0:T(8,128)(2,1)S(1)} %get-tuple-element.60, bf16[128,1792]{1,0:T(8,128)(2,1)S(1)} %get-tuple-element.59, f32[384,128]{1,0:T(8,128)S(1)} %get-tuple-element.52, bf16[240,128]{1,0:T(8,128)(2,1)S(1)} %collective-permute-done.27, bf16[240,128]{1,0:T(8,128)(2,1)S(1)} %collective-permute-done.26, ...), kind=kOutput, calls=%fused_computation.1 | convolution fusion | flops 119832576 | bytes 1966592 | tf_op jit(solution)/shard_map/dot_general | solution.py:44
  (82 shorter events, 0.7 us)
Async XLA Ops:
  0.6 13.1 %copy-start = (s32[2,1,12]{2,1,0:T(1,128)S(1)}, s32[2,1,12]{2,1,0:T(1,128)}, u32[]{:S(2)}) copy-start(s32[2,1,12]{2,1,0:T(1,128)} %param.11) | copy-start | bytes 292
  0.6 11.9 %copy-start.2 = (bf16[1,3584,128]{2,1,0:T(8,128)(2,1)S(1)}, bf16[1,3584,128]{2,1,0:T(8,128)(2,1)}, u32[]{:S(2)}) copy-start(bf16[1,3584,128]{2,1,0:T(8,128)(2,1)} %param.8) | copy-start | bytes 2752516
  0.7 7.4 %collective-permute-start.3 = (bf16[3584,128]{1,0:T(8,128)(2,1)}, bf16[3584,128]{1,0:T(8,128)(2,1)}, u32[]{:S(2)}, u32[]{:S(2)}) collective-permute-start(bf16[3584,128]{1,0:T(8,128)(2,1)} %bitcast.138), channel_id=1, source_target_pairs={{0,8},{8,0},{16,24},{24,16},{1,9},{9,1},{17,25},{25,17},{2,10},{10... | collective-permute-start | bytes 2752520 | tf_op jit(solution)/shard_map/ppermute | solution.py:11
  2.0 6.0 %collective-permute-start.2 = (bf16[16,1792]{1,0:T(8,128)(2,1)S(1)}, bf16[16,1792]{1,0:T(8,128)(2,1)S(1)}, u32[]{:S(2)}, u32[]{:S(2)}) collective-permute-start(bf16[16,1792]{1,0:T(8,128)(2,1)S(1)} %get-tuple-element.68), channel_id=1, source_target_pairs={{0,1},{1,0},{2,3},{3,2},{4,5},{5,4},{6,7},{7,6},{8,9},{9,8},{10,11... | collective-permute-start | bytes 172040 | tf_op jit(solution)/shard_map/ppermute | solution.py:11
  4.6 9.1 %copy-start.3 = (f32[1,128]{1,0:T(1,128)S(1)}, f32[1,128]{1,0:T(1,128)}, u32[]{:S(2)}) copy-start(f32[1,128]{1,0:T(1,128)} %param.9) | copy-start | bytes 1540
  5.9 12.6 %collective-permute-start.1 = (bf16[256,896]{1,0:T(8,128)(2,1)S(1)}, bf16[256,896]{1,0:T(8,128)(2,1)S(1)}, u32[]{:S(2)}, u32[]{:S(2)}) collective-permute-start(bf16[256,896]{1,0:T(8,128)(2,1)S(1)} %get-tuple-element.57), channel_id=1, source_target_pairs={{0,16},{8,24},{16,0},{24,8},{1,17},{9,25},{17,1},{25,9},{2,18},{10... | collective-permute-start | bytes 1376264 | tf_op jit(solution)/shard_map/ppermute | solution.py:11
  7.5 12.2 %collective-permute-start = (bf16[256,896]{1,0:T(8,128)(2,1)S(1)}, bf16[256,896]{1,0:T(8,128)(2,1)S(1)}, u32[]{:S(2)}, u32[]{:S(2)}) collective-permute-start(bf16[256,896]{1,0:T(8,128)(2,1)S(1)} %get-tuple-element.58), channel_id=1, source_target_pairs={{0,1},{1,0},{2,3},{3,2},{4,5},{5,4},{6,7},{7,6},{8,9},{9,8},{10,11... | collective-permute-start | bytes 1376264 | tf_op jit(solution)/shard_map/ppermute | solution.py:11
  8.0 11.7 %collective-permute-start.6 = (bf16[32,1792]{1,0:T(8,128)(2,1)S(1)}, bf16[32,1792]{1,0:T(8,128)(2,1)S(1)}, u32[]{:S(2)}, u32[]{:S(2)}) collective-permute-start(bf16[32,1792]{1,0:T(8,128)(2,1)S(1)} %bitcast.130), channel_id=1, source_target_pairs={{0,6},{1,7},{2,4},{3,5},{4,2},{5,3},{6,0},{7,1},{8,14},{9,15},{10,... | collective-permute-start | bytes 344072 | tf_op jit(solution)/shard_map/ppermute | solution.py:11
  11.7 9.4 %collective-permute-start.5 = (bf16[32,1792]{1,0:T(8,128)(2,1)S(1)}, bf16[32,1792]{1,0:T(8,128)(2,1)S(1)}, u32[]{:S(2)}, u32[]{:S(2)}) collective-permute-start(bf16[32,1792]{1,0:T(8,128)(2,1)S(1)} %bitcast.131), channel_id=1, source_target_pairs={{0,4},{1,5},{2,6},{3,7},{4,0},{5,1},{6,2},{7,3},{8,12},{9,13},{10,... | collective-permute-start | bytes 344072 | tf_op jit(solution)/shard_map/ppermute | solution.py:11
  11.7 9.4 %collective-permute-start.4 = (bf16[32,1792]{1,0:T(8,128)(2,1)S(1)}, bf16[32,1792]{1,0:T(8,128)(2,1)S(1)}, u32[]{:S(2)}, u32[]{:S(2)}) collective-permute-start(bf16[32,1792]{1,0:T(8,128)(2,1)S(1)} %bitcast.132), channel_id=1, source_target_pairs={{0,2},{1,3},{2,0},{3,1},{4,6},{5,7},{6,4},{7,5},{8,10},{9,11},{10,... | collective-permute-start | bytes 344072 | tf_op jit(solution)/shard_map/ppermute | solution.py:11
  13.9 12.9 %copy-start.1 = (bf16[1,2,2,128,1792]{4,3,2,1,0:T(8,128)(2,1)S(1)}, bf16[1,2,2,128,1792]{4,3,2,1,0:T(8,128)(2,1)}, u32[]{:S(2)}) copy-start(bf16[1,2,2,128,1792]{4,3,2,1,0:T(8,128)(2,1)} %param.10) | copy-start | bytes 5505028
  21.4 1.4 %collective-permute-start.7 = (f32[128,256]{1,0:T(8,128)S(1)}, f32[128,256]{1,0:T(8,128)S(1)}, u32[]{:S(2)}, u32[]{:S(2)}) collective-permute-start(f32[128,256]{1,0:T(8,128)S(1)} %convolution_add_fusion.4), channel_id=1, source_target_pairs={{0,8},{8,0},{16,24},{24,16},{1,9},{9,1},{17,25},{25,17},{2,10},{10... | collective-permute-start | bytes 393224 | tf_op jit(solution)/shard_map/ppermute | solution.py:11
  22.9 4.3 %collective-permute-start.9 = (bf16[128,256]{1,0:T(8,128)(2,1)S(1)}, bf16[128,256]{1,0:T(8,128)(2,1)S(1)}, u32[]{:S(2)}, u32[]{:S(2)}) collective-permute-start(bf16[128,256]{1,0:T(8,128)(2,1)S(1)} %multiply_convert_fusion), channel_id=1, source_target_pairs={{0,16},{8,24},{16,0},{24,8},{1,17},{9,25},{17,1},{25,9},{2,18},{10... | collective-permute-start | bytes 196616 | tf_op jit(solution)/shard_map/ppermute | solution.py:11
  23.8 5.2 %collective-permute-start.8 = (bf16[128,256]{1,0:T(8,128)(2,1)S(1)}, bf16[128,256]{1,0:T(8,128)(2,1)S(1)}, u32[]{:S(2)}, u32[]{:S(2)}) collective-permute-start(bf16[128,256]{1,0:T(8,128)(2,1)S(1)} %bitcast.144), channel_id=1, source_target_pairs={{0,1},{1,0},{2,3},{3,2},{4,5},{5,4},{6,7},{7,6},{8,9},{9,8},{10,11... | collective-permute-start | bytes 196616 | tf_op jit(solution)/shard_map/ppermute | solution.py:11
  26.2 9.6 %collective-permute-start.17 = (bf16[16,896]{1,0:T(8,128)(2,1)S(1)}, bf16[16,896]{1,0:T(8,128)(2,1)S(1)}, u32[]{:S(2)}, u32[]{:S(2)}) collective-permute-start(bf16[16,896]{1,0:T(8,128)(2,1)S(1)} %get-tuple-element.61), channel_id=1, source_target_pairs={{0,1},{1,0},{2,3},{3,2},{4,5},{5,4},{6,7},{7,6},{8,9},{9,8},{10,11... | collective-permute-start | bytes 86024 | tf_op jit(solution)/shard_map/ppermute | solution.py:11
  27.4 4.9 %collective-permute-start.10 = (bf16[64,896]{1,0:T(8,128)(2,1)S(1)}, bf16[64,896]{1,0:T(8,128)(2,1)S(1)}, u32[]{:S(2)}, u32[]{:S(2)}) collective-permute-start(bf16[64,896]{1,0:T(8,128)(2,1)S(1)} %fusion.1), channel_id=1, source_target_pairs={{0,1},{1,0},{2,3},{3,2},{4,5},{5,4},{6,7},{7,6},{8,9},{9,8},{10,11... | collective-permute-start | bytes 344072 | tf_op jit(solution)/shard_map/ppermute | solution.py:11
  29.5 7.3 %collective-permute-start.16 = (bf16[32,896]{1,0:T(8,128)(2,1)S(1)}, bf16[32,896]{1,0:T(8,128)(2,1)S(1)}, u32[]{:S(2)}, u32[]{:S(2)}) collective-permute-start(bf16[32,896]{1,0:T(8,128)(2,1)S(1)} %get-tuple-element.64), channel_id=1, source_target_pairs={{0,6},{1,7},{2,4},{3,5},{4,2},{5,3},{6,0},{7,1},{8,14},{9,15},{10,... | collective-permute-start | bytes 172040 | tf_op jit(solution)/shard_map/ppermute | solution.py:11
  32.0 6.5 %collective-permute-start.15 = (bf16[32,896]{1,0:T(8,128)(2,1)S(1)}, bf16[32,896]{1,0:T(8,128)(2,1)S(1)}, u32[]{:S(2)}, u32[]{:S(2)}) collective-permute-start(bf16[32,896]{1,0:T(8,128)(2,1)S(1)} %get-tuple-element.65), channel_id=1, source_target_pairs={{0,4},{1,5},{2,6},{3,7},{4,0},{5,1},{6,2},{7,3},{8,12},{9,13},{10,... | collective-permute-start | bytes 172040 | tf_op jit(solution)/shard_map/ppermute | solution.py:11
  32.4 6.2 %collective-permute-start.14 = (bf16[16,896]{1,0:T(8,128)(2,1)S(1)}, bf16[16,896]{1,0:T(8,128)(2,1)S(1)}, u32[]{:S(2)}, u32[]{:S(2)}) collective-permute-start(bf16[16,896]{1,0:T(8,128)(2,1)S(1)} %get-tuple-element.71), channel_id=1, source_target_pairs={{0,6},{1,7},{2,4},{3,5},{4,2},{5,3},{6,0},{7,1},{8,14},{9,15},{10,... | collective-permute-start | bytes 86024 | tf_op jit(solution)/shard_map/ppermute | solution.py:11
  34.9 4.9 %collective-permute-start.13 = (bf16[16,896]{1,0:T(8,128)(2,1)S(1)}, bf16[16,896]{1,0:T(8,128)(2,1)S(1)}, u32[]{:S(2)}, u32[]{:S(2)}) collective-permute-start(bf16[16,896]{1,0:T(8,128)(2,1)S(1)} %get-tuple-element.72), channel_id=1, source_target_pairs={{0,4},{1,5},{2,6},{3,7},{4,0},{5,1},{6,2},{7,3},{8,12},{9,13},{10,... | collective-permute-start | bytes 86024 | tf_op jit(solution)/shard_map/ppermute | solution.py:11
  35.8 4.2 %collective-permute-start.12 = (bf16[16,896]{1,0:T(8,128)(2,1)S(1)}, bf16[16,896]{1,0:T(8,128)(2,1)S(1)}, u32[]{:S(2)}, u32[]{:S(2)}) collective-permute-start(bf16[16,896]{1,0:T(8,128)(2,1)S(1)} %get-tuple-element.73), channel_id=1, source_target_pairs={{0,2},{1,3},{2,0},{3,1},{4,6},{5,7},{6,4},{7,5},{8,10},{9,11},{10,... | collective-permute-start | bytes 86024 | tf_op jit(solution)/shard_map/ppermute | solution.py:11
  36.9 7.6 %collective-permute-start.11 = (bf16[32,896]{1,0:T(8,128)(2,1)S(1)}, bf16[32,896]{1,0:T(8,128)(2,1)S(1)}, u32[]{:S(2)}, u32[]{:S(2)}) collective-permute-start(bf16[32,896]{1,0:T(8,128)(2,1)S(1)} %get-tuple-element.38), channel_id=1, source_target_pairs={{0,2},{1,3},{2,0},{3,1},{4,6},{5,7},{6,4},{7,5},{8,10},{9,11},{10,... | collective-permute-start | bytes 172040 | tf_op jit(solution)/shard_map/ppermute | solution.py:11
  40.0 6.7 %collective-permute-start.23 = (bf16[16,896]{1,0:T(8,128)(2,1)S(1)}, bf16[16,896]{1,0:T(8,128)(2,1)S(1)}, u32[]{:S(2)}, u32[]{:S(2)}) collective-permute-start(bf16[16,896]{1,0:T(8,128)(2,1)S(1)} %subtract_convert_fusion), channel_id=1, source_target_pairs={{0,6},{1,7},{2,4},{3,5},{4,2},{5,3},{6,0},{7,1},{8,14},{9,15},{10,... | collective-permute-start | bytes 86024 | tf_op jit(solution)/shard_map/ppermute | solution.py:11
  42.2 6.7 %collective-permute-start.22 = (bf16[16,896]{1,0:T(8,128)(2,1)S(1)}, bf16[16,896]{1,0:T(8,128)(2,1)S(1)}, u32[]{:S(2)}, u32[]{:S(2)}) collective-permute-start(bf16[16,896]{1,0:T(8,128)(2,1)S(1)} %subtract_convert_fusion), channel_id=1, source_target_pairs={{0,4},{1,5},{2,6},{3,7},{4,0},{5,1},{6,2},{7,3},{8,12},{9,13},{10,... | collective-permute-start | bytes 86024 | tf_op jit(solution)/shard_map/ppermute | solution.py:11
  42.2 6.7 %collective-permute-start.21 = (bf16[16,896]{1,0:T(8,128)(2,1)S(1)}, bf16[16,896]{1,0:T(8,128)(2,1)S(1)}, u32[]{:S(2)}, u32[]{:S(2)}) collective-permute-start(bf16[16,896]{1,0:T(8,128)(2,1)S(1)} %subtract_convert_fusion), channel_id=1, source_target_pairs={{0,2},{1,3},{2,0},{3,1},{4,6},{5,7},{6,4},{7,5},{8,10},{9,11},{10,... | collective-permute-start | bytes 86024 | tf_op jit(solution)/shard_map/ppermute | solution.py:11
  44.5 6.2 %collective-permute-start.20 = (bf16[32,896]{1,0:T(8,128)(2,1)S(1)}, bf16[32,896]{1,0:T(8,128)(2,1)S(1)}, u32[]{:S(2)}, u32[]{:S(2)}) collective-permute-start(bf16[32,896]{1,0:T(8,128)(2,1)S(1)} %fusion.24), channel_id=1, source_target_pairs={{0,6},{1,7},{2,4},{3,5},{4,2},{5,3},{6,0},{7,1},{8,14},{9,15},{10,... | collective-permute-start | bytes 172040 | tf_op jit(solution)/shard_map/ppermute | solution.py:11
  46.7 5.1 %collective-permute-start.19 = (bf16[32,896]{1,0:T(8,128)(2,1)S(1)}, bf16[32,896]{1,0:T(8,128)(2,1)S(1)}, u32[]{:S(2)}, u32[]{:S(2)}) collective-permute-start(bf16[32,896]{1,0:T(8,128)(2,1)S(1)} %fusion.24), channel_id=1, source_target_pairs={{0,4},{1,5},{2,6},{3,7},{4,0},{5,1},{6,2},{7,3},{8,12},{9,13},{10,... | collective-permute-start | bytes 172040 | tf_op jit(solution)/shard_map/ppermute | solution.py:11
  46.7 5.1 %collective-permute-start.18 = (bf16[32,896]{1,0:T(8,128)(2,1)S(1)}, bf16[32,896]{1,0:T(8,128)(2,1)S(1)}, u32[]{:S(2)}, u32[]{:S(2)}) collective-permute-start(bf16[32,896]{1,0:T(8,128)(2,1)S(1)} %fusion.24), channel_id=1, source_target_pairs={{0,2},{1,3},{2,0},{3,1},{4,6},{5,7},{6,4},{7,5},{8,10},{9,11},{10,... | collective-permute-start | bytes 172040 | tf_op jit(solution)/shard_map/ppermute | solution.py:11
  49.0 4.9 %collective-permute-start.24 = (bf16[64,896]{1,0:T(8,128)(2,1)S(1)}, bf16[64,896]{1,0:T(8,128)(2,1)S(1)}, u32[]{:S(2)}, u32[]{:S(2)}) collective-permute-start(bf16[64,896]{1,0:T(8,128)(2,1)S(1)} %pad_maximum_fusion.5), channel_id=1, source_target_pairs={{0,1},{1,0},{2,3},{3,2},{4,5},{5,4},{6,7},{7,6},{8,9},{9,8},{10,11... | collective-permute-start | bytes 344072 | tf_op jit(solution)/shard_map/ppermute | solution.py:11
  50.7 12.6 %collective-permute-start.28 = (bf16[128,1792]{1,0:T(8,128)(2,1)S(1)}, bf16[128,1792]{1,0:T(8,128)(2,1)S(1)}, u32[]{:S(2)}, u32[]{:S(2)}) collective-permute-start(bf16[128,1792]{1,0:T(8,128)(2,1)S(1)} %constant_dynamic-update-slice_fusion), channel_id=1, source_target_pairs={{0,8},{8,0},{16,24},{24,16},{1,9},{9,1},{17,25},{25,17},{2,10},{10... | collective-permute-start | bytes 1376264 | tf_op jit(solution)/shard_map/ppermute | solution.py:11
  54.8 1.5 %collective-permute-start.25 = (f32[384,128]{1,0:T(8,128)S(1)}, f32[384,128]{1,0:T(8,128)S(1)}, u32[]{:S(2)}, u32[]{:S(2)}) collective-permute-start(f32[384,128]{1,0:T(8,128)S(1)} %slice_select_fusion), channel_id=1, source_target_pairs={{0,8},{8,0},{16,24},{24,16},{1,9},{9,1},{17,25},{25,17},{2,10},{10... | collective-permute-start | bytes 589832 | tf_op jit(solution)/shard_map/ppermute | solution.py:11
  56.6 4.3 %collective-permute-start.27 = (bf16[240,128]{1,0:T(8,128)(2,1)S(1)}, bf16[240,128]{1,0:T(8,128)(2,1)S(1)}, u32[]{:S(2)}, u32[]{:S(2)}) collective-permute-start(bf16[240,128]{1,0:T(8,128)(2,1)S(1)} %constant_dynamic-update-slice_fusion.19), channel_id=1, source_target_pairs={{0,16},{8,24},{16,0},{24,8},{1,17},{9,25},{17,1},{25,9},{2,18},{10... | collective-permute-start | bytes 184328 | tf_op jit(solution)/shard_map/ppermute | solution.py:11
  57.8 4.2 %collective-permute-start.26 = (bf16[240,128]{1,0:T(8,128)(2,1)S(1)}, bf16[240,128]{1,0:T(8,128)(2,1)S(1)}, u32[]{:S(2)}, u32[]{:S(2)}) collective-permute-start(bf16[240,128]{1,0:T(8,128)(2,1)S(1)} %constant_dynamic-update-slice_fusion.4), channel_id=1, source_target_pairs={{0,1},{1,0},{2,3},{3,2},{4,5},{5,4},{6,7},{7,6},{8,9},{9,8},{10,11... | collective-permute-start | bytes 184328 | tf_op jit(solution)/shard_map/ppermute | solution.py:11

commit v17 on v16

--- a/solution.py
+++ b/solution.py
@@ -161,24 +161,19 @@
     grads = jnp.where(half == 0, lower, upper) + over_core(jnp.where(half == 0, upper, lower))
 
 
-    def with_errors(grad, block):
-        tiles = [block[:, at:at + latents] for at in range(0, part, latents)]
-        return jnp.concatenate([grad.astype(BF16)] + tiles, axis=0)
-
-    def without_errors(message):
-        tiles = message[tokens:].reshape(part // latents, rows, latents)
-        return message[:tokens].astype(F32), jnp.concatenate([tiles[i] for i in range(part // latents)], axis=1)
-
-    from_x, own_there = without_errors(over_x(with_errors(grads[tokens:2 * tokens], rows_at(err_own, 1))))
-    from_y, shared_there = without_errors(over_y(with_errors(grads[2 * tokens:], err_shared)))
+    to_x, to_y = grads[tokens:2 * tokens].astype(BF16), grads[2 * tokens:].astype(BF16)
+    to_x, to_y, late_own, late_shared = hold((to_x, to_y, rows_at(err_own, 1), err_shared))
+    from_x, from_y = over_x(to_x).astype(F32), over_y(to_y).astype(F32)
+    own_there, shared_there = over_x(late_own), over_y(late_shared)
+    grad_pre = (grads[:tokens] + from_x + from_y) * gate
+    bias_grad = jnp.sum(grad_pre, axis=0)[None, :]
+    enc_grad = encoder_gradient(resid_half, resid_other, grad_pre.astype(BF16), half)
+    enc_grad, own_there, shared_there = hold((enc_grad, own_there, shared_there))
     errors = jnp.where(
         layer == 0,
         ordered(side, rows_at(err_own, 0), own_there, axis=1),
         jnp.concatenate([shared_there, err_shared], axis=1),
     )
-    grad_pre = (grads[:tokens] + from_x + from_y) * gate
-    bias_grad = jnp.sum(grad_pre, axis=0)[None, :]
-    enc_grad = encoder_gradient(resid_half, resid_other, grad_pre.astype(BF16), half)
     return errors[None], enc_grad[None], bias_grad
 
 

time: 65 us -> 65.2 us (level)
  starting transfers between devices: 36.1 us -> 37.3 us
  waiting for transfers between devices: 17.3 us -> 16.6 us
    ppermute x29 -> x31, starting transfers between devices: 36.1 us -> 37.3 us  [crossed(): lax.ppermute(block, axis, [(i, i ^ mask) for i in range(lax.axis_size(axi...]
    ppermute x29 -> x31, waiting for transfers between devices: 17.3 us -> 16.6 us  [crossed(): lax.ppermute(block, axis, [(i, i ^ mask) for i in range(lax.axis_size(axi...]
  transfers between devices with their start and end apart: 29 -> 31, of which waited for: 12 -> 11; matrix products, arithmetic and copies ran while one was open for 13% -> 14% of each run, Pallas kernels for 0% -> 0%
where the time goes in v17:
time: 65.2 us; the launch traced here: 65 us
  starting transfers between devices  37.3 us (57%)
  waiting for transfers between devices  16.6 us (25%)
  matrix products  4.16 us (6%)
  local copies, waits for them, and re-layouts  2.99 us (5%)
  other arithmetic  2.92 us (4%)
  between operations  0.99 us (2%)
    ppermute x31, starting transfers between devices, crossed(): lax.ppermute(block, axis, [(i, i ^ mask) for i in range(lax.axis_size(axi...  37.3 us
    ppermute x31, waiting for transfers between devices, crossed(): lax.ppermute(block, axis, [(i, i ^ mask) for i in range(lax.axis_size(axi...  16.6 us
    dot_general x7, matrix products, times(): return jnp.dot(left, right, preferred_element_type=F32)  1.6 us
    dot_general x1, matrix products, encoder_gradient(): lax.dot_general(whole, grad_low, (((0,), (0,)), ((), ())), preferred_elem...  1.36 us
    select_n x3, other arithmetic, both_halves(): jnp.where(half == 0, mine, other)  1.32 us
  transfers between devices with their start and end apart: 31, of which 11 were waited for; matrix products, arithmetic and copies ran while one was open for 14% of the time, Pallas kernels for 0%

profile of v17, /device:TPU:0, one launch (start us, length us, event | category | flops | bytes accessed | tf_op | source)
XLA Modules:
  0.0 65.0 jit_solution(2552469264859643254)
XLA Ops:
  0.6 0.0 copy-start
  0.7 0.5 collective-permute-start.3
  1.2 0.8 %dynamic-slice_bitcast_fusion.3 = (bf16[1,1,16,1792]{3,2,1,0:T(8,128)(2,1)S(1)}, bf16[16,1792]{1,0:T(8,128)(2,1)S(1)}) fusion(bf16[2,16,3584]{2,1,0:T(8,128)(2,1)} %param.6, s32[]{:T(128)S(6)} %select_n.168, s32[]{:T(128)S(6)} %select_n.173), kind=kLoop, calls=%fused_computation.55 | loop fusion | bytes 172040 | tf_op jit(solution)/shard_map/reshape;squeeze | solution.py:100
  2.0 2.6 %collective-permute-start.2 = (bf16[16,1792]{1,0:T(8,128)(2,1)S(1)}, bf16[16,1792]{1,0:T(8,128)(2,1)S(1)}, u32[]{:S(2)}, u32[]{:S(2)}) collective-permute-start(bf16[16,1792]{1,0:T(8,128)(2,1)S(1)} %get-tuple-element.82), channel_id=1, source_target_pairs={{0,1},{1,0},{2,3},{3,2},{4,5},{5,4},{6,7},{7,6},{8,9},{9,8},{10,11... | collective-permute-start | bytes 172040 | tf_op jit(solution)/shard_map/ppermute | solution.py:11
  4.6 1.2 %dynamic-slice_bitcast_fusion = (bf16[256,896]{1,0:T(8,128)(2,1)S(1)}, bf16[256,896]{1,0:T(8,128)(2,1)S(1)}) fusion(bf16[2,256,1792]{2,1,0:T(8,128)(2,1)} %bitcast.90, s32[]{:T(128)S(6)} %select_n.170, s32[]{:T(128)S(6)} %select_n.171, s32[]{:T(128)S(6)} %select_n.168, s32[]{:T(128)S(6)} %select_n.169), kind=kLoop, calls=%fused_computation.23 | loop fusion | bytes 1835024 | tf_op jit(solution)/shard_map/squeeze | solution.py:91
  5.9 1.6 %collective-permute-start.1 = (bf16[256,896]{1,0:T(8,128)(2,1)S(1)}, bf16[256,896]{1,0:T(8,128)(2,1)S(1)}, u32[]{:S(2)}, u32[]{:S(2)}) collective-permute-start(bf16[256,896]{1,0:T(8,128)(2,1)S(1)} %get-tuple-element.71), channel_id=1, source_target_pairs={{0,16},{8,24},{16,0},{24,8},{1,17},{9,25},{17,1},{25,9},{2,18},{10... | collective-permute-start | bytes 1376264 | tf_op jit(solution)/shard_map/ppermute | solution.py:11
  7.5 0.5 collective-permute-start
  8.0 0.0 collective-permute-done.2
  8.0 3.7 %collective-permute-start.6 = (bf16[32,1792]{1,0:T(8,128)(2,1)S(1)}, bf16[32,1792]{1,0:T(8,128)(2,1)S(1)}, u32[]{:S(2)}, u32[]{:S(2)}) collective-permute-start(bf16[32,1792]{1,0:T(8,128)(2,1)S(1)} %bitcast.102), channel_id=1, source_target_pairs={{0,6},{1,7},{2,4},{3,5},{4,2},{5,3},{6,0},{7,1},{8,14},{9,15},{10,... | collective-permute-start | bytes 344072 | tf_op jit(solution)/shard_map/ppermute | solution.py:11
  11.7 0.8 %collective-permute-start.4 = (bf16[32,1792]{1,0:T(8,128)(2,1)S(1)}, bf16[32,1792]{1,0:T(8,128)(2,1)S(1)}, u32[]{:S(2)}, u32[]{:S(2)}) collective-permute-start(bf16[32,1792]{1,0:T(8,128)(2,1)S(1)} %bitcast.104), channel_id=1, source_target_pairs={{0,2},{1,3},{2,0},{3,1},{4,6},{5,7},{6,4},{7,5},{8,10},{9,11},{10,... | collective-permute-start | bytes 344072 | tf_op jit(solution)/shard_map/ppermute | solution.py:11
  12.5 1.2 %bitcast_select_fusion.1 = (bf16[1792,128]{1,0:T(8,128)(2,1)S(1)}, bf16[1792,128]{1,0:T(8,128)(2,1)S(1)}) fusion(pred[]{:T(512)S(6)} %eq.48, bf16[3584,128]{1,0:T(8,128)(2,1)} %collective-permute-done.3, s32[]{:T(128)S(6)} %select_n.173, bf16[1,3584,128]{2,1,0:T(8,128)(2,1)S(1)} %copy-done.2), kind=kLoop, calls=%fused_computation.22 | loop fusion | flops 458752 | bytes 1835013 | tf_op jit(solution)/shard_map/jit(_where)/select_n | solution.py:23
  13.7 0.0 copy-start.1
  13.8 4.7 %collective-permute-done.1 = bf16[256,896]{1,0:T(8,128)(2,1)S(1)} collective-permute-done((bf16[256,896]{1,0:T(8,128)(2,1)S(1)}, bf16[256,896]{1,0:T(8,128)(2,1)S(1)}, u32[]{:S(2)}, u32[]{:S(2)}) %collective-permute-start.1) | collective-permute-done | bytes 458784 | tf_op jit(solution)/shard_map/ppermute | solution.py:11
  18.5 1.2 %collective-permute-done = bf16[256,896]{1,0:T(8,128)(2,1)S(1)} collective-permute-done((bf16[256,896]{1,0:T(8,128)(2,1)S(1)}, bf16[256,896]{1,0:T(8,128)(2,1)S(1)}, u32[]{:S(2)}, u32[]{:S(2)}) %collective-permute-start) | collective-permute-done | bytes 458784 | tf_op jit(solution)/shard_map/ppermute | solution.py:11
  19.7 1.4 %collective-permute-done.5 = bf16[32,1792]{1,0:T(8,128)(2,1)S(1)} collective-permute-done((bf16[32,1792]{1,0:T(8,128)(2,1)S(1)}, bf16[32,1792]{1,0:T(8,128)(2,1)S(1)}, u32[]{:S(2)}, u32[]{:S(2)}) %collective-permute-start.5) | collective-permute-done | bytes 114720 | tf_op jit(solution)/shard_map/ppermute | solution.py:11
  21.1 0.3 convolution_add_fusion.4
  21.4 0.1 collective-permute-start.7
  21.5 0.1 compare_reduce_fusion
  21.6 1.2 %collective-permute-done.7 = f32[128,256]{1,0:T(8,128)S(1)} collective-permute-done((f32[128,256]{1,0:T(8,128)S(1)}, f32[128,256]{1,0:T(8,128)S(1)}, u32[]{:S(2)}, u32[]{:S(2)}) %collective-permute-start.7) | collective-permute-done | bytes 131104 | tf_op jit(solution)/shard_map/ppermute | solution.py:11
  22.9 0.9 %collective-permute-start.9 = (bf16[128,256]{1,0:T(8,128)(2,1)S(1)}, bf16[128,256]{1,0:T(8,128)(2,1)S(1)}, u32[]{:S(2)}, u32[]{:S(2)}) collective-permute-start(bf16[128,256]{1,0:T(8,128)(2,1)S(1)} %multiply_convert_fusion), channel_id=1, source_target_pairs={{0,16},{8,24},{16,0},{24,8},{1,17},{9,25},{17,1},{25,9},{2,18},{10... | collective-permute-start | bytes 196616 | tf_op jit(solution)/shard_map/ppermute | solution.py:11
  23.8 1.6 %collective-permute-start.8 = (bf16[128,256]{1,0:T(8,128)(2,1)S(1)}, bf16[128,256]{1,0:T(8,128)(2,1)S(1)}, u32[]{:S(2)}, u32[]{:S(2)}) collective-permute-start(bf16[128,256]{1,0:T(8,128)(2,1)S(1)} %bitcast.117), channel_id=1, source_target_pairs={{0,1},{1,0},{2,3},{3,2},{4,5},{5,4},{6,7},{7,6},{8,9},{9,8},{10,11... | collective-permute-start | bytes 196616 | tf_op jit(solution)/shard_map/ppermute | solution.py:11
  25.4 0.8 %dynamic-slice_bitcast_fusion.4 = (bf16[16,896]{1,0:T(8,128)(2,1)S(1)}, bf16[16,896]{1,0:T(8,128)(2,1)S(1)}, bf16[16,896]{1,0:T(8,128)(2,1)S(1)}) fusion(bf16[3,16,3584]{2,1,0:T(8,128)(2,1)} %param.7, s32[]{:T(128)S(6)} %select_n.185, s32[]{:T(128)S(6)} %select_n.188, s32[]{:T(128)S(6)} %select_n.187, s32[]{:T(128)S(6)} %select_n.186), kind=kLoop, calls=%fused_computation.62 | loop fusion | bytes 172048 | tf_op jit(solution)/shard_map/squeeze | solution.py:127
  26.2 0.6 collective-permute-start.17
  26.8 0.2 fusion.9
  27.0 0.2 fusion.11
  27.2 0.0 collective-permute-done.9
  27.2 0.2 fusion
  27.4 1.5 %collective-permute-start.10 = (bf16[64,896]{1,0:T(8,128)(2,1)S(1)}, bf16[64,896]{1,0:T(8,128)(2,1)S(1)}, u32[]{:S(2)}, u32[]{:S(2)}) collective-permute-start(bf16[64,896]{1,0:T(8,128)(2,1)S(1)} %fusion), channel_id=1, source_target_pairs={{0,1},{1,0},{2,3},{3,2},{4,5},{5,4},{6,7},{7,6},{8,9},{9,8},{10,11... | collective-permute-start | bytes 344072 | tf_op jit(solution)/shard_map/ppermute | solution.py:11
  29.0 0.0 collective-permute-done.8
  29.0 0.2 fusion.54
  29.2 0.2 fusion.53
  29.5 2.5 %collective-permute-start.16 = (bf16[32,896]{1,0:T(8,128)(2,1)S(1)}, bf16[32,896]{1,0:T(8,128)(2,1)S(1)}, u32[]{:S(2)}, u32[]{:S(2)}) collective-permute-start(bf16[32,896]{1,0:T(8,128)(2,1)S(1)} %get-tuple-element.78), channel_id=1, source_target_pairs={{0,6},{1,7},{2,4},{3,5},{4,2},{5,3},{6,0},{7,1},{8,14},{9,15},{10,... | collective-permute-start | bytes 172040 | tf_op jit(solution)/shard_map/ppermute | solution.py:11
  32.0 0.2 convolution_add_fusion.1
  32.3 0.0 collective-permute-done.10
  32.3 2.5 %collective-permute-start.14 = (bf16[16,896]{1,0:T(8,128)(2,1)S(1)}, bf16[16,896]{1,0:T(8,128)(2,1)S(1)}, u32[]{:S(2)}, u32[]{:S(2)}) collective-permute-start(bf16[16,896]{1,0:T(8,128)(2,1)S(1)} %get-tuple-element.85), channel_id=1, source_target_pairs={{0,6},{1,7},{2,4},{3,5},{4,2},{5,3},{6,0},{7,1},{8,14},{9,15},{10,... | collective-permute-start | bytes 86024 | tf_op jit(solution)/shard_map/ppermute | solution.py:11
  34.9 0.9 %collective-permute-start.13 = (bf16[16,896]{1,0:T(8,128)(2,1)S(1)}, bf16[16,896]{1,0:T(8,128)(2,1)S(1)}, u32[]{:S(2)}, u32[]{:S(2)}) collective-permute-start(bf16[16,896]{1,0:T(8,128)(2,1)S(1)} %get-tuple-element.86), channel_id=1, source_target_pairs={{0,4},{1,5},{2,6},{3,7},{4,0},{5,1},{6,2},{7,3},{8,12},{9,13},{10,... | collective-permute-start | bytes 86024 | tf_op jit(solution)/shard_map/ppermute | solution.py:11
  35.8 1.0 %collective-permute-start.12 = (bf16[16,896]{1,0:T(8,128)(2,1)S(1)}, bf16[16,896]{1,0:T(8,128)(2,1)S(1)}, u32[]{:S(2)}, u32[]{:S(2)}) collective-permute-start(bf16[16,896]{1,0:T(8,128)(2,1)S(1)} %get-tuple-element.87), channel_id=1, source_target_pairs={{0,2},{1,3},{2,0},{3,1},{4,6},{5,7},{6,4},{7,5},{8,10},{9,11},{10,... | collective-permute-start | bytes 86024 | tf_op jit(solution)/shard_map/ppermute | solution.py:11
  36.8 1.0 %collective-permute-start.11 = (bf16[32,896]{1,0:T(8,128)(2,1)S(1)}, bf16[32,896]{1,0:T(8,128)(2,1)S(1)}, u32[]{:S(2)}, u32[]{:S(2)}) collective-permute-start(bf16[32,896]{1,0:T(8,128)(2,1)S(1)} %get-tuple-element.45), channel_id=1, source_target_pairs={{0,2},{1,3},{2,0},{3,1},{4,6},{5,7},{6,4},{7,5},{8,10},{9,11},{10,... | collective-permute-start | bytes 172040 | tf_op jit(solution)/shard_map/ppermute | solution.py:11
  37.9 0.7 %collective-permute-done.15 = bf16[32,896]{1,0:T(8,128)(2,1)S(1)} collective-permute-done((bf16[32,896]{1,0:T(8,128)(2,1)S(1)}, bf16[32,896]{1,0:T(8,128)(2,1)S(1)}, u32[]{:S(2)}, u32[]{:S(2)}) %collective-permute-start.15) | collective-permute-done | bytes 57376 | tf_op jit(solution)/shard_map/ppermute | solution.py:11
  38.6 1.2 %collective-permute-done.13 = bf16[16,896]{1,0:T(8,128)(2,1)S(1)} collective-permute-done((bf16[16,896]{1,0:T(8,128)(2,1)S(1)}, bf16[16,896]{1,0:T(8,128)(2,1)S(1)}, u32[]{:S(2)}, u32[]{:S(2)}) %collective-permute-start.13) | collective-permute-done | bytes 28704 | tf_op jit(solution)/shard_map/ppermute | solution.py:11
  39.8 0.2 collective-permute-done.12
  40.0 2.2 %collective-permute-start.20 = (bf16[16,896]{1,0:T(8,128)(2,1)S(1)}, bf16[16,896]{1,0:T(8,128)(2,1)S(1)}, u32[]{:S(2)}, u32[]{:S(2)}) collective-permute-start(bf16[16,896]{1,0:T(8,128)(2,1)S(1)} %subtract_convert_fusion), channel_id=1, source_target_pairs={{0,6},{1,7},{2,4},{3,5},{4,2},{5,3},{6,0},{7,1},{8,14},{9,15},{10,... | collective-permute-start | bytes 86024 | tf_op jit(solution)/shard_map/ppermute | solution.py:11
  42.2 0.0 collective-permute-start.19
  42.2 2.2 %collective-permute-start.18 = (bf16[16,896]{1,0:T(8,128)(2,1)S(1)}, bf16[16,896]{1,0:T(8,128)(2,1)S(1)}, u32[]{:S(2)}, u32[]{:S(2)}) collective-permute-start(bf16[16,896]{1,0:T(8,128)(2,1)S(1)} %subtract_convert_fusion), channel_id=1, source_target_pairs={{0,2},{1,3},{2,0},{3,1},{4,6},{5,7},{6,4},{7,5},{8,10},{9,11},{10,... | collective-permute-start | bytes 86024 | tf_op jit(solution)/shard_map/ppermute | solution.py:11
  44.5 2.2 %collective-permute-start.24 = (bf16[32,896]{1,0:T(8,128)(2,1)S(1)}, bf16[32,896]{1,0:T(8,128)(2,1)S(1)}, u32[]{:S(2)}, u32[]{:S(2)}) collective-permute-start(bf16[32,896]{1,0:T(8,128)(2,1)S(1)} %fusion.23), channel_id=1, source_target_pairs={{0,6},{1,7},{2,4},{3,5},{4,2},{5,3},{6,0},{7,1},{8,14},{9,15},{10,... | collective-permute-start | bytes 172040 | tf_op jit(solution)/shard_map/ppermute | solution.py:11
  46.7 2.2 %collective-permute-start.22 = (bf16[32,896]{1,0:T(8,128)(2,1)S(1)}, bf16[32,896]{1,0:T(8,128)(2,1)S(1)}, u32[]{:S(2)}, u32[]{:S(2)}) collective-permute-start(bf16[32,896]{1,0:T(8,128)(2,1)S(1)} %fusion.23), channel_id=1, source_target_pairs={{0,2},{1,3},{2,0},{3,1},{4,6},{5,7},{6,4},{7,5},{8,10},{9,11},{10,... | collective-permute-start | bytes 172040 | tf_op jit(solution)/shard_map/ppermute | solution.py:11
  49.0 1.7 %collective-permute-start.25 = (bf16[64,896]{1,0:T(8,128)(2,1)S(1)}, bf16[64,896]{1,0:T(8,128)(2,1)S(1)}, u32[]{:S(2)}, u32[]{:S(2)}) collective-permute-start(bf16[64,896]{1,0:T(8,128)(2,1)S(1)} %pad_maximum_fusion.5), channel_id=1, source_target_pairs={{0,1},{1,0},{2,3},{3,2},{4,5},{5,4},{6,7},{7,6},{8,9},{9,8},{10,11... | collective-permute-start | bytes 344072 | tf_op jit(solution)/shard_map/ppermute | solution.py:11
  50.7 1.1 %collective-permute-done.23 = bf16[32,896]{1,0:T(8,128)(2,1)S(1)} collective-permute-done((bf16[32,896]{1,0:T(8,128)(2,1)S(1)}, bf16[32,896]{1,0:T(8,128)(2,1)S(1)}, u32[]{:S(2)}, u32[]{:S(2)}) %collective-permute-start.23) | collective-permute-done | bytes 57376 | tf_op jit(solution)/shard_map/ppermute | solution.py:11
  51.8 0.3 fusion.26
  52.1 1.7 %collective-permute-done.25 = bf16[64,896]{1,0:T(8,128)(2,1)S(1)} collective-permute-done((bf16[64,896]{1,0:T(8,128)(2,1)S(1)}, bf16[64,896]{1,0:T(8,128)(2,1)S(1)}, u32[]{:S(2)}, u32[]{:S(2)}) %collective-permute-start.25) | collective-permute-done | bytes 114720 | tf_op jit(solution)/shard_map/ppermute | solution.py:11
  53.8 0.3 fusion.55
  54.1 0.3 fusion.7
  54.5 0.3 convolution_add_fusion.3
  54.8 0.1 collective-permute-start.26
  54.9 1.4 %collective-permute-done.26 = f32[384,128]{1,0:T(8,128)S(1)} collective-permute-done((f32[384,128]{1,0:T(8,128)S(1)}, f32[384,128]{1,0:T(8,128)S(1)}, u32[]{:S(2)}, u32[]{:S(2)}) %collective-permute-start.26) | collective-permute-done | bytes 196640 | tf_op jit(solution)/shard_map/ppermute | solution.py:11
  56.4 1.7 %collective-permute-start.27 = (bf16[128,128]{1,0:T(8,128)(2,1)S(1)}, bf16[128,128]{1,0:T(8,128)(2,1)S(1)}, u32[]{:S(2)}, u32[]{:S(2)}) collective-permute-start(bf16[128,128]{1,0:T(8,128)(2,1)S(1)} %get-tuple-element.58), channel_id=1, source_target_pairs={{0,1},{1,0},{2,3},{3,2},{4,5},{5,4},{6,7},{7,6},{8,9},{9,8},{10,11... | collective-permute-start | bytes 98312 | tf_op jit(solution)/shard_map/ppermute | solution.py:11
  58.1 1.2 %collective-permute-start.28 = (bf16[128,128]{1,0:T(8,128)(2,1)S(1)}, bf16[128,128]{1,0:T(8,128)(2,1)S(1)}, u32[]{:S(2)}, u32[]{:S(2)}) collective-permute-start(bf16[128,128]{1,0:T(8,128)(2,1)S(1)} %get-tuple-element.59), channel_id=1, source_target_pairs={{0,16},{8,24},{16,0},{24,8},{1,17},{9,25},{17,1},{25,9},{2,18},{10... | collective-permute-start | bytes 98312 | tf_op jit(solution)/shard_map/ppermute | solution.py:11
  59.3 0.3 collective-permute-start.29
  59.7 0.8 %collective-permute-start.30 = (bf16[16,896]{1,0:T(8,128)(2,1)S(1)}, bf16[16,896]{1,0:T(8,128)(2,1)S(1)}, u32[]{:S(2)}, u32[]{:S(2)}) collective-permute-start(bf16[16,896]{1,0:T(8,128)(2,1)S(1)} %subtract_convert_fusion), channel_id=1, source_target_pairs={{0,16},{8,24},{16,0},{24,8},{1,17},{9,25},{17,1},{25,9},{2,18},{10... | collective-permute-start | bytes 86024 | tf_op jit(solution)/shard_map/ppermute | solution.py:11
  60.5 1.7 %collective-permute-done.28 = bf16[128,128]{1,0:T(8,128)(2,1)S(1)} collective-permute-done((bf16[128,128]{1,0:T(8,128)(2,1)S(1)}, bf16[128,128]{1,0:T(8,128)(2,1)S(1)}, u32[]{:S(2)}, u32[]{:S(2)}) %collective-permute-start.28) | collective-permute-done | bytes 32800 | tf_op jit(solution)/shard_map/ppermute | solution.py:11
  62.3 0.5 fusion.28
  62.8 0.1 broadcast_select_fusion.1
  62.9 1.4 %convolution_convert_fusion = bf16[3584,128]{1,0:T(8,128)(2,1)} fusion(bf16[128,1792]{1,0:T(8,128)(2,1)S(1)} %get-tuple-element.74, bf16[128,1792]{1,0:T(8,128)(2,1)S(1)} %get-tuple-element.73, f32[384,128]{1,0:T(8,128)S(1)} %get-tuple-element.66, bf16[128,128]{1,0:T(8,128)(2,1)S(1)} %collective-permute-done.28, ...), kind=kOutput, calls=%fused_computation | convolution fusion | flops 119832576 | bytes 1966592 | tf_op jit(solution)/shard_map/dot_general | solution.py:44
  64.3 0.6 maximum_select_fusion
  (58 shorter events, 0.5 us)
Async XLA Ops:
  0.6 20.9 %copy-start = (s32[2,1,12]{2,1,0:T(1,128)S(1)}, s32[2,1,12]{2,1,0:T(1,128)}, u32[]{:S(2)}) copy-start(s32[2,1,12]{2,1,0:T(1,128)} %param.11) | copy-start | bytes 292
  0.6 11.9 %copy-start.2 = (bf16[1,3584,128]{2,1,0:T(8,128)(2,1)S(1)}, bf16[1,3584,128]{2,1,0:T(8,128)(2,1)}, u32[]{:S(2)}) copy-start(bf16[1,3584,128]{2,1,0:T(8,128)(2,1)} %param.8) | copy-start | bytes 2752516
  0.7 7.4 %collective-permute-start.3 = (bf16[3584,128]{1,0:T(8,128)(2,1)}, bf16[3584,128]{1,0:T(8,128)(2,1)}, u32[]{:S(2)}, u32[]{:S(2)}) collective-permute-start(bf16[3584,128]{1,0:T(8,128)(2,1)} %bitcast.111), channel_id=1, source_target_pairs={{0,8},{8,0},{16,24},{24,16},{1,9},{9,1},{17,25},{25,17},{2,10},{10... | collective-permute-start | bytes 2752520 | tf_op jit(solution)/shard_map/ppermute | solution.py:11
  2.0 6.0 %collective-permute-start.2 = (bf16[16,1792]{1,0:T(8,128)(2,1)S(1)}, bf16[16,1792]{1,0:T(8,128)(2,1)S(1)}, u32[]{:S(2)}, u32[]{:S(2)}) collective-permute-start(bf16[16,1792]{1,0:T(8,128)(2,1)S(1)} %get-tuple-element.82), channel_id=1, source_target_pairs={{0,1},{1,0},{2,3},{3,2},{4,5},{5,4},{6,7},{7,6},{8,9},{9,8},{10,11... | collective-permute-start | bytes 172040 | tf_op jit(solution)/shard_map/ppermute | solution.py:11
  4.6 9.1 %copy-start.3 = (f32[1,128]{1,0:T(1,128)S(1)}, f32[1,128]{1,0:T(1,128)}, u32[]{:S(2)}) copy-start(f32[1,128]{1,0:T(1,128)} %param.9) | copy-start | bytes 1540
  5.9 12.6 %collective-permute-start.1 = (bf16[256,896]{1,0:T(8,128)(2,1)S(1)}, bf16[256,896]{1,0:T(8,128)(2,1)S(1)}, u32[]{:S(2)}, u32[]{:S(2)}) collective-permute-start(bf16[256,896]{1,0:T(8,128)(2,1)S(1)} %get-tuple-element.71), channel_id=1, source_target_pairs={{0,16},{8,24},{16,0},{24,8},{1,17},{9,25},{17,1},{25,9},{2,18},{10... | collective-permute-start | bytes 1376264 | tf_op jit(solution)/shard_map/ppermute | solution.py:11
  7.5 12.2 %collective-permute-start = (bf16[256,896]{1,0:T(8,128)(2,1)S(1)}, bf16[256,896]{1,0:T(8,128)(2,1)S(1)}, u32[]{:S(2)}, u32[]{:S(2)}) collective-permute-start(bf16[256,896]{1,0:T(8,128)(2,1)S(1)} %get-tuple-element.72), channel_id=1, source_target_pairs={{0,1},{1,0},{2,3},{3,2},{4,5},{5,4},{6,7},{7,6},{8,9},{9,8},{10,11... | collective-permute-start | bytes 1376264 | tf_op jit(solution)/shard_map/ppermute | solution.py:11
  8.0 11.7 %collective-permute-start.6 = (bf16[32,1792]{1,0:T(8,128)(2,1)S(1)}, bf16[32,1792]{1,0:T(8,128)(2,1)S(1)}, u32[]{:S(2)}, u32[]{:S(2)}) collective-permute-start(bf16[32,1792]{1,0:T(8,128)(2,1)S(1)} %bitcast.102), channel_id=1, source_target_pairs={{0,6},{1,7},{2,4},{3,5},{4,2},{5,3},{6,0},{7,1},{8,14},{9,15},{10,... | collective-permute-start | bytes 344072 | tf_op jit(solution)/shard_map/ppermute | solution.py:11
  11.7 9.4 %collective-permute-start.5 = (bf16[32,1792]{1,0:T(8,128)(2,1)S(1)}, bf16[32,1792]{1,0:T(8,128)(2,1)S(1)}, u32[]{:S(2)}, u32[]{:S(2)}) collective-permute-start(bf16[32,1792]{1,0:T(8,128)(2,1)S(1)} %bitcast.103), channel_id=1, source_target_pairs={{0,4},{1,5},{2,6},{3,7},{4,0},{5,1},{6,2},{7,3},{8,12},{9,13},{10,... | collective-permute-start | bytes 344072 | tf_op jit(solution)/shard_map/ppermute | solution.py:11
  11.7 9.4 %collective-permute-start.4 = (bf16[32,1792]{1,0:T(8,128)(2,1)S(1)}, bf16[32,1792]{1,0:T(8,128)(2,1)S(1)}, u32[]{:S(2)}, u32[]{:S(2)}) collective-permute-start(bf16[32,1792]{1,0:T(8,128)(2,1)S(1)} %bitcast.104), channel_id=1, source_target_pairs={{0,2},{1,3},{2,0},{3,1},{4,6},{5,7},{6,4},{7,5},{8,10},{9,11},{10,... | collective-permute-start | bytes 344072 | tf_op jit(solution)/shard_map/ppermute | solution.py:11
  13.7 13.0 %copy-start.1 = (bf16[1,2,2,128,1792]{4,3,2,1,0:T(8,128)(2,1)S(1)}, bf16[1,2,2,128,1792]{4,3,2,1,0:T(8,128)(2,1)}, u32[]{:S(2)}) copy-start(bf16[1,2,2,128,1792]{4,3,2,1,0:T(8,128)(2,1)} %param.10) | copy-start | bytes 5505028
  21.4 1.4 %collective-permute-start.7 = (f32[128,256]{1,0:T(8,128)S(1)}, f32[128,256]{1,0:T(8,128)S(1)}, u32[]{:S(2)}, u32[]{:S(2)}) collective-permute-start(f32[128,256]{1,0:T(8,128)S(1)} %convolution_add_fusion.4), channel_id=1, source_target_pairs={{0,8},{8,0},{16,24},{24,16},{1,9},{9,1},{17,25},{25,17},{2,10},{10... | collective-permute-start | bytes 393224 | tf_op jit(solution)/shard_map/ppermute | solution.py:11
  22.9 4.3 %collective-permute-start.9 = (bf16[128,256]{1,0:T(8,128)(2,1)S(1)}, bf16[128,256]{1,0:T(8,128)(2,1)S(1)}, u32[]{:S(2)}, u32[]{:S(2)}) collective-permute-start(bf16[128,256]{1,0:T(8,128)(2,1)S(1)} %multiply_convert_fusion), channel_id=1, source_target_pairs={{0,16},{8,24},{16,0},{24,8},{1,17},{9,25},{17,1},{25,9},{2,18},{10... | collective-permute-start | bytes 196616 | tf_op jit(solution)/shard_map/ppermute | solution.py:11
  23.8 5.2 %collective-permute-start.8 = (bf16[128,256]{1,0:T(8,128)(2,1)S(1)}, bf16[128,256]{1,0:T(8,128)(2,1)S(1)}, u32[]{:S(2)}, u32[]{:S(2)}) collective-permute-start(bf16[128,256]{1,0:T(8,128)(2,1)S(1)} %bitcast.117), channel_id=1, source_target_pairs={{0,1},{1,0},{2,3},{3,2},{4,5},{5,4},{6,7},{7,6},{8,9},{9,8},{10,11... | collective-permute-start | bytes 196616 | tf_op jit(solution)/shard_map/ppermute | solution.py:11
  26.2 9.6 %collective-permute-start.17 = (bf16[16,896]{1,0:T(8,128)(2,1)S(1)}, bf16[16,896]{1,0:T(8,128)(2,1)S(1)}, u32[]{:S(2)}, u32[]{:S(2)}) collective-permute-start(bf16[16,896]{1,0:T(8,128)(2,1)S(1)} %get-tuple-element.75), channel_id=1, source_target_pairs={{0,1},{1,0},{2,3},{3,2},{4,5},{5,4},{6,7},{7,6},{8,9},{9,8},{10,11... | collective-permute-start | bytes 86024 | tf_op jit(solution)/shard_map/ppermute | solution.py:11
  27.4 4.9 %collective-permute-start.10 = (bf16[64,896]{1,0:T(8,128)(2,1)S(1)}, bf16[64,896]{1,0:T(8,128)(2,1)S(1)}, u32[]{:S(2)}, u32[]{:S(2)}) collective-permute-start(bf16[64,896]{1,0:T(8,128)(2,1)S(1)} %fusion), channel_id=1, source_target_pairs={{0,1},{1,0},{2,3},{3,2},{4,5},{5,4},{6,7},{7,6},{8,9},{9,8},{10,11... | collective-permute-start | bytes 344072 | tf_op jit(solution)/shard_map/ppermute | solution.py:11
  29.5 7.3 %collective-permute-start.16 = (bf16[32,896]{1,0:T(8,128)(2,1)S(1)}, bf16[32,896]{1,0:T(8,128)(2,1)S(1)}, u32[]{:S(2)}, u32[]{:S(2)}) collective-permute-start(bf16[32,896]{1,0:T(8,128)(2,1)S(1)} %get-tuple-element.78), channel_id=1, source_target_pairs={{0,6},{1,7},{2,4},{3,5},{4,2},{5,3},{6,0},{7,1},{8,14},{9,15},{10,... | collective-permute-start | bytes 172040 | tf_op jit(solution)/shard_map/ppermute | solution.py:11
  32.0 6.5 %collective-permute-start.15 = (bf16[32,896]{1,0:T(8,128)(2,1)S(1)}, bf16[32,896]{1,0:T(8,128)(2,1)S(1)}, u32[]{:S(2)}, u32[]{:S(2)}) collective-permute-start(bf16[32,896]{1,0:T(8,128)(2,1)S(1)} %get-tuple-element.79), channel_id=1, source_target_pairs={{0,4},{1,5},{2,6},{3,7},{4,0},{5,1},{6,2},{7,3},{8,12},{9,13},{10,... | collective-permute-start | bytes 172040 | tf_op jit(solution)/shard_map/ppermute | solution.py:11
  32.3 6.2 %collective-permute-start.14 = (bf16[16,896]{1,0:T(8,128)(2,1)S(1)}, bf16[16,896]{1,0:T(8,128)(2,1)S(1)}, u32[]{:S(2)}, u32[]{:S(2)}) collective-permute-start(bf16[16,896]{1,0:T(8,128)(2,1)S(1)} %get-tuple-element.85), channel_id=1, source_target_pairs={{0,6},{1,7},{2,4},{3,5},{4,2},{5,3},{6,0},{7,1},{8,14},{9,15},{10,... | collective-permute-start | bytes 86024 | tf_op jit(solution)/shard_map/ppermute | solution.py:11
  34.9 4.9 %collective-permute-start.13 = (bf16[16,896]{1,0:T(8,128)(2,1)S(1)}, bf16[16,896]{1,0:T(8,128)(2,1)S(1)}, u32[]{:S(2)}, u32[]{:S(2)}) collective-permute-start(bf16[16,896]{1,0:T(8,128)(2,1)S(1)} %get-tuple-element.86), channel_id=1, source_target_pairs={{0,4},{1,5},{2,6},{3,7},{4,0},{5,1},{6,2},{7,3},{8,12},{9,13},{10,... | collective-permute-start | bytes 86024 | tf_op jit(solution)/shard_map/ppermute | solution.py:11
  35.8 4.2 %collective-permute-start.12 = (bf16[16,896]{1,0:T(8,128)(2,1)S(1)}, bf16[16,896]{1,0:T(8,128)(2,1)S(1)}, u32[]{:S(2)}, u32[]{:S(2)}) collective-permute-start(bf16[16,896]{1,0:T(8,128)(2,1)S(1)} %get-tuple-element.87), channel_id=1, source_target_pairs={{0,2},{1,3},{2,0},{3,1},{4,6},{5,7},{6,4},{7,5},{8,10},{9,11},{10,... | collective-permute-start | bytes 86024 | tf_op jit(solution)/shard_map/ppermute | solution.py:11
  36.8 7.6 %collective-permute-start.11 = (bf16[32,896]{1,0:T(8,128)(2,1)S(1)}, bf16[32,896]{1,0:T(8,128)(2,1)S(1)}, u32[]{:S(2)}, u32[]{:S(2)}) collective-permute-start(bf16[32,896]{1,0:T(8,128)(2,1)S(1)} %get-tuple-element.45), channel_id=1, source_target_pairs={{0,2},{1,3},{2,0},{3,1},{4,6},{5,7},{6,4},{7,5},{8,10},{9,11},{10,... | collective-permute-start | bytes 172040 | tf_op jit(solution)/shard_map/ppermute | solution.py:11
  40.0 6.7 %collective-permute-start.20 = (bf16[16,896]{1,0:T(8,128)(2,1)S(1)}, bf16[16,896]{1,0:T(8,128)(2,1)S(1)}, u32[]{:S(2)}, u32[]{:S(2)}) collective-permute-start(bf16[16,896]{1,0:T(8,128)(2,1)S(1)} %subtract_convert_fusion), channel_id=1, source_target_pairs={{0,6},{1,7},{2,4},{3,5},{4,2},{5,3},{6,0},{7,1},{8,14},{9,15},{10,... | collective-permute-start | bytes 86024 | tf_op jit(solution)/shard_map/ppermute | solution.py:11
  42.2 6.7 %collective-permute-start.19 = (bf16[16,896]{1,0:T(8,128)(2,1)S(1)}, bf16[16,896]{1,0:T(8,128)(2,1)S(1)}, u32[]{:S(2)}, u32[]{:S(2)}) collective-permute-start(bf16[16,896]{1,0:T(8,128)(2,1)S(1)} %subtract_convert_fusion), channel_id=1, source_target_pairs={{0,4},{1,5},{2,6},{3,7},{4,0},{5,1},{6,2},{7,3},{8,12},{9,13},{10,... | collective-permute-start | bytes 86024 | tf_op jit(solution)/shard_map/ppermute | solution.py:11
  42.2 6.7 %collective-permute-start.18 = (bf16[16,896]{1,0:T(8,128)(2,1)S(1)}, bf16[16,896]{1,0:T(8,128)(2,1)S(1)}, u32[]{:S(2)}, u32[]{:S(2)}) collective-permute-start(bf16[16,896]{1,0:T(8,128)(2,1)S(1)} %subtract_convert_fusion), channel_id=1, source_target_pairs={{0,2},{1,3},{2,0},{3,1},{4,6},{5,7},{6,4},{7,5},{8,10},{9,11},{10,... | collective-permute-start | bytes 86024 | tf_op jit(solution)/shard_map/ppermute | solution.py:11
  44.5 6.2 %collective-permute-start.24 = (bf16[32,896]{1,0:T(8,128)(2,1)S(1)}, bf16[32,896]{1,0:T(8,128)(2,1)S(1)}, u32[]{:S(2)}, u32[]{:S(2)}) collective-permute-start(bf16[32,896]{1,0:T(8,128)(2,1)S(1)} %fusion.23), channel_id=1, source_target_pairs={{0,6},{1,7},{2,4},{3,5},{4,2},{5,3},{6,0},{7,1},{8,14},{9,15},{10,... | collective-permute-start | bytes 172040 | tf_op jit(solution)/shard_map/ppermute | solution.py:11
  46.7 5.1 %collective-permute-start.23 = (bf16[32,896]{1,0:T(8,128)(2,1)S(1)}, bf16[32,896]{1,0:T(8,128)(2,1)S(1)}, u32[]{:S(2)}, u32[]{:S(2)}) collective-permute-start(bf16[32,896]{1,0:T(8,128)(2,1)S(1)} %fusion.23), channel_id=1, source_target_pairs={{0,4},{1,5},{2,6},{3,7},{4,0},{5,1},{6,2},{7,3},{8,12},{9,13},{10,... | collective-permute-start | bytes 172040 | tf_op jit(solution)/shard_map/ppermute | solution.py:11
  46.7 5.1 %collective-permute-start.22 = (bf16[32,896]{1,0:T(8,128)(2,1)S(1)}, bf16[32,896]{1,0:T(8,128)(2,1)S(1)}, u32[]{:S(2)}, u32[]{:S(2)}) collective-permute-start(bf16[32,896]{1,0:T(8,128)(2,1)S(1)} %fusion.23), channel_id=1, source_target_pairs={{0,2},{1,3},{2,0},{3,1},{4,6},{5,7},{6,4},{7,5},{8,10},{9,11},{10,... | collective-permute-start | bytes 172040 | tf_op jit(solution)/shard_map/ppermute | solution.py:11
  49.0 4.9 %collective-permute-start.25 = (bf16[64,896]{1,0:T(8,128)(2,1)S(1)}, bf16[64,896]{1,0:T(8,128)(2,1)S(1)}, u32[]{:S(2)}, u32[]{:S(2)}) collective-permute-start(bf16[64,896]{1,0:T(8,128)(2,1)S(1)} %pad_maximum_fusion.5), channel_id=1, source_target_pairs={{0,1},{1,0},{2,3},{3,2},{4,5},{5,4},{6,7},{7,6},{8,9},{9,8},{10,11... | collective-permute-start | bytes 344072 | tf_op jit(solution)/shard_map/ppermute | solution.py:11
  50.7 12.1 %collective-permute-start.21 = (bf16[128,1792]{1,0:T(8,128)(2,1)S(1)}, bf16[128,1792]{1,0:T(8,128)(2,1)S(1)}, u32[]{:S(2)}, u32[]{:S(2)}) collective-permute-start(bf16[128,1792]{1,0:T(8,128)(2,1)S(1)} %constant_dynamic-update-slice_fusion), channel_id=1, source_target_pairs={{0,8},{8,0},{16,24},{24,16},{1,9},{9,1},{17,25},{25,17},{2,10},{10... | collective-permute-start | bytes 1376264 | tf_op jit(solution)/shard_map/ppermute | solution.py:11
  54.8 1.5 %collective-permute-start.26 = (f32[384,128]{1,0:T(8,128)S(1)}, f32[384,128]{1,0:T(8,128)S(1)}, u32[]{:S(2)}, u32[]{:S(2)}) collective-permute-start(f32[384,128]{1,0:T(8,128)S(1)} %slice_select_fusion), channel_id=1, source_target_pairs={{0,8},{8,0},{16,24},{24,16},{1,9},{9,1},{17,25},{25,17},{2,10},{10... | collective-permute-start | bytes 589832 | tf_op jit(solution)/shard_map/ppermute | solution.py:11
  56.4 4.1 %collective-permute-start.27 = (bf16[128,128]{1,0:T(8,128)(2,1)S(1)}, bf16[128,128]{1,0:T(8,128)(2,1)S(1)}, u32[]{:S(2)}, u32[]{:S(2)}) collective-permute-start(bf16[128,128]{1,0:T(8,128)(2,1)S(1)} %get-tuple-element.58), channel_id=1, source_target_pairs={{0,1},{1,0},{2,3},{3,2},{4,5},{5,4},{6,7},{7,6},{8,9},{9,8},{10,11... | collective-permute-start | bytes 98312 | tf_op jit(solution)/shard_map/ppermute | solution.py:11
  58.1 4.1 %collective-permute-start.28 = (bf16[128,128]{1,0:T(8,128)(2,1)S(1)}, bf16[128,128]{1,0:T(8,128)(2,1)S(1)}, u32[]{:S(2)}, u32[]{:S(2)}) collective-permute-start(bf16[128,128]{1,0:T(8,128)(2,1)S(1)} %get-tuple-element.59), channel_id=1, source_target_pairs={{0,16},{8,24},{16,0},{24,8},{1,17},{9,25},{17,1},{25,9},{2,18},{10... | collective-permute-start | bytes 98312 | tf_op jit(solution)/shard_map/ppermute | solution.py:11
  59.3 4.9 %collective-permute-start.29 = (bf16[16,896]{1,0:T(8,128)(2,1)S(1)}, bf16[16,896]{1,0:T(8,128)(2,1)S(1)}, u32[]{:S(2)}, u32[]{:S(2)}) collective-permute-start(bf16[16,896]{1,0:T(8,128)(2,1)S(1)} %slice_bitcast_fusion), channel_id=1, source_target_pairs={{0,1},{1,0},{2,3},{3,2},{4,5},{5,4},{6,7},{7,6},{8,9},{9,8},{10,11... | collective-permute-start | bytes 86024 | tf_op jit(solution)/shard_map/ppermute | solution.py:11
  59.7 4.6 %collective-permute-start.30 = (bf16[16,896]{1,0:T(8,128)(2,1)S(1)}, bf16[16,896]{1,0:T(8,128)(2,1)S(1)}, u32[]{:S(2)}, u32[]{:S(2)}) collective-permute-start(bf16[16,896]{1,0:T(8,128)(2,1)S(1)} %subtract_convert_fusion), channel_id=1, source_target_pairs={{0,16},{8,24},{16,0},{24,8},{1,17},{9,25},{17,1},{25,9},{2,18},{10... | collective-permute-start | bytes 86024 | tf_op jit(solution)/shard_map/ppermute | solution.py:11

commit v18 on v16

--- a/solution.py
+++ b/solution.py
@@ -144,8 +144,9 @@
 
     own_column = along_z(err_own)
     shared_near = jnp.concatenate(along_z(err_shared), axis=0)
-    resid_swapped, _ = hold((resid_half, shared_near))
+    resid_swapped, late_shared, _ = hold((resid_half, err_shared, shared_near))
     resid_other = over_core(resid_swapped)
+    shared_there = over_y(late_shared)
     errs_shared = paired(shared_near, over_x(shared_near))
     errs_own = jnp.concatenate(own_column, axis=0)
 
@@ -161,16 +162,16 @@
     grads = jnp.where(half == 0, lower, upper) + over_core(jnp.where(half == 0, upper, lower))
 
 
-    def with_errors(grad, block):
-        tiles = [block[:, at:at + latents] for at in range(0, part, latents)]
-        return jnp.concatenate([grad.astype(BF16)] + tiles, axis=0)
-
-    def without_errors(message):
-        tiles = message[tokens:].reshape(part // latents, rows, latents)
-        return message[:tokens].astype(F32), jnp.concatenate([tiles[i] for i in range(part // latents)], axis=1)
-
-    from_x, own_there = without_errors(over_x(with_errors(grads[tokens:2 * tokens], rows_at(err_own, 1))))
-    from_y, shared_there = without_errors(over_y(with_errors(grads[2 * tokens:], err_shared)))
+    grads, shared_there, resid_other = hold((grads, shared_there, resid_other))
+
+    away = rows_at(err_own, 1)
+    tiles = [away[:, at:at + latents] for at in range(0, part, latents)]
+    to_x = jnp.concatenate([grads[tokens:2 * tokens].astype(BF16)] + tiles, axis=0)
+    to_x, to_y = hold((to_x, grads[2 * tokens:].astype(BF16)))
+    from_x, from_y = over_x(to_x), over_y(to_y).astype(F32)
+    tiles = from_x[tokens:].reshape(part // latents, rows, latents)
+    own_there = jnp.concatenate([tiles[i] for i in range(part // latents)], axis=1)
+    from_x = from_x[:tokens].astype(F32)
     errors = jnp.where(
         layer == 0,
         ordered(side, rows_at(err_own, 0), own_there, axis=1),

time: 65 us -> 64.9 us (level)
  waiting for transfers between devices: 17.3 us -> 16.1 us
  starting transfers between devices: 36.1 us -> 37.3 us
    ppermute x29 -> x30, waiting for transfers between devices: 17.3 us -> 16.1 us  [crossed(): lax.ppermute(block, axis, [(i, i ^ mask) for i in range(lax.axis_size(axi...]
    ppermute x29 -> x30, starting transfers between devices: 36.1 us -> 37.3 us  [crossed(): lax.ppermute(block, axis, [(i, i ^ mask) for i in range(lax.axis_size(axi...]
  transfers between devices with their start and end apart: 29 -> 30, of which waited for: 12 -> 10; matrix products, arithmetic and copies ran while one was open for 13% -> 12% of each run, Pallas kernels for 0% -> 0%
where the time goes in v18:
time: 64.9 us; the launch traced here: 64.6 us
  starting transfers between devices  37.3 us (57%)
  waiting for transfers between devices  16.1 us (25%)
  matrix products  4.15 us (6%)
  local copies, waits for them, and re-layouts  3.11 us (5%)
  other arithmetic  2.93 us (5%)
  between operations  1.06 us (2%)
    ppermute x30, starting transfers between devices, crossed(): lax.ppermute(block, axis, [(i, i ^ mask) for i in range(lax.axis_size(axi...  37.3 us
    ppermute x30, waiting for transfers between devices, crossed(): lax.ppermute(block, axis, [(i, i ^ mask) for i in range(lax.axis_size(axi...  16.1 us
    dot_general x7, matrix products, times(): return jnp.dot(left, right, preferred_element_type=F32)  1.6 us
    dot_general x1, matrix products, encoder_gradient(): lax.dot_general(whole, grad_low, (((0,), (0,)), ((), ())), preferred_elem...  1.36 us
    select_n x3, other arithmetic, both_halves(): jnp.where(half == 0, mine, other)  1.32 us
  transfers between devices with their start and end apart: 30, of which 10 were waited for; matrix products, arithmetic and copies ran while one was open for 12% of the time, Pallas kernels for 0%

profile of v18, /device:TPU:0, one launch (start us, length us, event | category | flops | bytes accessed | tf_op | source)
XLA Modules:
  0.0 64.6 jit_solution(7255778031723623234)
XLA Ops:
  0.6 0.0 copy-start
  0.7 0.5 collective-permute-start.3
  1.2 0.8 %dynamic-slice_bitcast_fusion.3 = (bf16[1,1,16,1792]{3,2,1,0:T(8,128)(2,1)S(1)}, bf16[16,1792]{1,0:T(8,128)(2,1)S(1)}) fusion(bf16[2,16,3584]{2,1,0:T(8,128)(2,1)} %param.6, s32[]{:T(128)S(6)} %select_n.180, s32[]{:T(128)S(6)} %select_n.185), kind=kLoop, calls=%fused_computation.54 | loop fusion | bytes 172040 | tf_op jit(solution)/shard_map/reshape;squeeze | solution.py:100
  2.0 2.6 %collective-permute-start.2 = (bf16[16,1792]{1,0:T(8,128)(2,1)S(1)}, bf16[16,1792]{1,0:T(8,128)(2,1)S(1)}, u32[]{:S(2)}, u32[]{:S(2)}) collective-permute-start(bf16[16,1792]{1,0:T(8,128)(2,1)S(1)} %get-tuple-element.78), channel_id=1, source_target_pairs={{0,1},{1,0},{2,3},{3,2},{4,5},{5,4},{6,7},{7,6},{8,9},{9,8},{10,11... | collective-permute-start | bytes 172040 | tf_op jit(solution)/shard_map/ppermute | solution.py:11
  4.6 1.2 %dynamic-slice_bitcast_fusion = (bf16[256,896]{1,0:T(8,128)(2,1)S(1)}, bf16[256,896]{1,0:T(8,128)(2,1)S(1)}) fusion(bf16[2,256,1792]{2,1,0:T(8,128)(2,1)} %bitcast.91, s32[]{:T(128)S(6)} %select_n.182, s32[]{:T(128)S(6)} %select_n.183, s32[]{:T(128)S(6)} %select_n.180, s32[]{:T(128)S(6)} %select_n.181), kind=kLoop, calls=%fused_computation.24 | loop fusion | bytes 1835024 | tf_op jit(solution)/shard_map/squeeze | solution.py:91
  5.9 1.6 %collective-permute-start.1 = (bf16[256,896]{1,0:T(8,128)(2,1)S(1)}, bf16[256,896]{1,0:T(8,128)(2,1)S(1)}, u32[]{:S(2)}, u32[]{:S(2)}) collective-permute-start(bf16[256,896]{1,0:T(8,128)(2,1)S(1)} %get-tuple-element.67), channel_id=1, source_target_pairs={{0,16},{8,24},{16,0},{24,8},{1,17},{9,25},{17,1},{25,9},{2,18},{10... | collective-permute-start | bytes 1376264 | tf_op jit(solution)/shard_map/ppermute | solution.py:11
  7.5 0.5 collective-permute-start
  8.0 0.0 collective-permute-done.3
  8.0 3.7 %collective-permute-start.6 = (bf16[32,1792]{1,0:T(8,128)(2,1)S(1)}, bf16[32,1792]{1,0:T(8,128)(2,1)S(1)}, u32[]{:S(2)}, u32[]{:S(2)}) collective-permute-start(bf16[32,1792]{1,0:T(8,128)(2,1)S(1)} %bitcast.102), channel_id=1, source_target_pairs={{0,6},{1,7},{2,4},{3,5},{4,2},{5,3},{6,0},{7,1},{8,14},{9,15},{10,... | collective-permute-start | bytes 344072 | tf_op jit(solution)/shard_map/ppermute | solution.py:11
  11.7 0.0 collective-permute-start.5
  11.7 0.8 %collective-permute-start.4 = (bf16[32,1792]{1,0:T(8,128)(2,1)S(1)}, bf16[32,1792]{1,0:T(8,128)(2,1)S(1)}, u32[]{:S(2)}, u32[]{:S(2)}) collective-permute-start(bf16[32,1792]{1,0:T(8,128)(2,1)S(1)} %bitcast.104), channel_id=1, source_target_pairs={{0,2},{1,3},{2,0},{3,1},{4,6},{5,7},{6,4},{7,5},{8,10},{9,11},{10,... | collective-permute-start | bytes 344072 | tf_op jit(solution)/shard_map/ppermute | solution.py:11
  12.5 1.2 %bitcast_select_fusion.1 = (bf16[1792,128]{1,0:T(8,128)(2,1)S(1)}, bf16[1792,128]{1,0:T(8,128)(2,1)S(1)}) fusion(pred[]{:T(512)S(6)} %eq.48, bf16[3584,128]{1,0:T(8,128)(2,1)} %collective-permute-done.3, s32[]{:T(128)S(6)} %select_n.185, bf16[1,3584,128]{2,1,0:T(8,128)(2,1)S(1)} %copy-done.2), kind=kLoop, calls=%fused_computation.23 | loop fusion | flops 458752 | bytes 1835013 | tf_op jit(solution)/shard_map/jit(_where)/select_n | solution.py:23
  13.8 0.1 compare_reduce_fusion
  13.9 0.0 copy-start.1
  13.9 4.6 %collective-permute-done.1 = bf16[256,896]{1,0:T(8,128)(2,1)S(1)} collective-permute-done((bf16[256,896]{1,0:T(8,128)(2,1)S(1)}, bf16[256,896]{1,0:T(8,128)(2,1)S(1)}, u32[]{:S(2)}, u32[]{:S(2)}) %collective-permute-start.1) | collective-permute-done | bytes 458784 | tf_op jit(solution)/shard_map/ppermute | solution.py:11
  18.5 1.2 %collective-permute-done = bf16[256,896]{1,0:T(8,128)(2,1)S(1)} collective-permute-done((bf16[256,896]{1,0:T(8,128)(2,1)S(1)}, bf16[256,896]{1,0:T(8,128)(2,1)S(1)}, u32[]{:S(2)}, u32[]{:S(2)}) %collective-permute-start) | collective-permute-done | bytes 458784 | tf_op jit(solution)/shard_map/ppermute | solution.py:11
  19.7 0.0 collective-permute-done.6
  19.7 1.4 %collective-permute-done.5 = bf16[32,1792]{1,0:T(8,128)(2,1)S(1)} collective-permute-done((bf16[32,1792]{1,0:T(8,128)(2,1)S(1)}, bf16[32,1792]{1,0:T(8,128)(2,1)S(1)}, u32[]{:S(2)}, u32[]{:S(2)}) %collective-permute-start.5) | collective-permute-done | bytes 114720 | tf_op jit(solution)/shard_map/ppermute | solution.py:11
  21.1 0.0 collective-permute-done.4
  21.1 0.3 convolution_add_fusion.4
  21.4 0.1 collective-permute-start.7
  21.5 1.3 %collective-permute-done.7 = f32[128,256]{1,0:T(8,128)S(1)} collective-permute-done((f32[128,256]{1,0:T(8,128)S(1)}, f32[128,256]{1,0:T(8,128)S(1)}, u32[]{:S(2)}, u32[]{:S(2)}) %collective-permute-start.7) | collective-permute-done | bytes 131104 | tf_op jit(solution)/shard_map/ppermute | solution.py:11
  22.9 0.9 %collective-permute-start.9 = (bf16[128,256]{1,0:T(8,128)(2,1)S(1)}, bf16[128,256]{1,0:T(8,128)(2,1)S(1)}, u32[]{:S(2)}, u32[]{:S(2)}) collective-permute-start(bf16[128,256]{1,0:T(8,128)(2,1)S(1)} %multiply_convert_fusion), channel_id=1, source_target_pairs={{0,16},{8,24},{16,0},{24,8},{1,17},{9,25},{17,1},{25,9},{2,18},{10... | collective-permute-start | bytes 196616 | tf_op jit(solution)/shard_map/ppermute | solution.py:11
  23.8 1.6 %collective-permute-start.8 = (bf16[128,256]{1,0:T(8,128)(2,1)S(1)}, bf16[128,256]{1,0:T(8,128)(2,1)S(1)}, u32[]{:S(2)}, u32[]{:S(2)}) collective-permute-start(bf16[128,256]{1,0:T(8,128)(2,1)S(1)} %bitcast.117), channel_id=1, source_target_pairs={{0,1},{1,0},{2,3},{3,2},{4,5},{5,4},{6,7},{7,6},{8,9},{9,8},{10,11... | collective-permute-start | bytes 196616 | tf_op jit(solution)/shard_map/ppermute | solution.py:11
  25.4 0.8 %dynamic-slice_bitcast_fusion.4 = (bf16[16,896]{1,0:T(8,128)(2,1)S(1)}, bf16[16,896]{1,0:T(8,128)(2,1)S(1)}, bf16[16,896]{1,0:T(8,128)(2,1)S(1)}) fusion(bf16[3,16,3584]{2,1,0:T(8,128)(2,1)} %param.7, s32[]{:T(128)S(6)} %select_n.197, s32[]{:T(128)S(6)} %select_n.200, s32[]{:T(128)S(6)} %select_n.199, s32[]{:T(128)S(6)} %select_n.198), kind=kLoop, calls=%fused_computation.80 | loop fusion | bytes 172048 | tf_op jit(solution)/shard_map/squeeze | solution.py:127
  26.2 0.6 collective-permute-start.17
  26.8 0.2 fusion.10
  27.0 0.2 fusion.12
  27.2 0.0 collective-permute-done.9
  27.2 0.2 fusion.1
  27.4 1.5 %collective-permute-start.10 = (bf16[64,896]{1,0:T(8,128)(2,1)S(1)}, bf16[64,896]{1,0:T(8,128)(2,1)S(1)}, u32[]{:S(2)}, u32[]{:S(2)}) collective-permute-start(bf16[64,896]{1,0:T(8,128)(2,1)S(1)} %fusion.1), channel_id=1, source_target_pairs={{0,1},{1,0},{2,3},{3,2},{4,5},{5,4},{6,7},{7,6},{8,9},{9,8},{10,11... | collective-permute-start | bytes 344072 | tf_op jit(solution)/shard_map/ppermute | solution.py:11
  29.0 0.2 fusion.51
  29.2 0.2 fusion.50
  29.5 2.5 %collective-permute-start.16 = (bf16[32,896]{1,0:T(8,128)(2,1)S(1)}, bf16[32,896]{1,0:T(8,128)(2,1)S(1)}, u32[]{:S(2)}, u32[]{:S(2)}) collective-permute-start(bf16[32,896]{1,0:T(8,128)(2,1)S(1)} %get-tuple-element.74), channel_id=1, source_target_pairs={{0,6},{1,7},{2,4},{3,5},{4,2},{5,3},{6,0},{7,1},{8,14},{9,15},{10,... | collective-permute-start | bytes 172040 | tf_op jit(solution)/shard_map/ppermute | solution.py:11
  32.0 0.2 convolution_add_fusion.1
  32.3 0.0 collective-permute-done.10
  32.4 2.5 %collective-permute-start.14 = (bf16[16,896]{1,0:T(8,128)(2,1)S(1)}, bf16[16,896]{1,0:T(8,128)(2,1)S(1)}, u32[]{:S(2)}, u32[]{:S(2)}) collective-permute-start(bf16[16,896]{1,0:T(8,128)(2,1)S(1)} %get-tuple-element.81), channel_id=1, source_target_pairs={{0,6},{1,7},{2,4},{3,5},{4,2},{5,3},{6,0},{7,1},{8,14},{9,15},{10,... | collective-permute-start | bytes 86024 | tf_op jit(solution)/shard_map/ppermute | solution.py:11
  34.9 0.9 %collective-permute-start.13 = (bf16[16,896]{1,0:T(8,128)(2,1)S(1)}, bf16[16,896]{1,0:T(8,128)(2,1)S(1)}, u32[]{:S(2)}, u32[]{:S(2)}) collective-permute-start(bf16[16,896]{1,0:T(8,128)(2,1)S(1)} %get-tuple-element.82), channel_id=1, source_target_pairs={{0,4},{1,5},{2,6},{3,7},{4,0},{5,1},{6,2},{7,3},{8,12},{9,13},{10,... | collective-permute-start | bytes 86024 | tf_op jit(solution)/shard_map/ppermute | solution.py:11
  35.8 1.0 %collective-permute-start.12 = (bf16[16,896]{1,0:T(8,128)(2,1)S(1)}, bf16[16,896]{1,0:T(8,128)(2,1)S(1)}, u32[]{:S(2)}, u32[]{:S(2)}) collective-permute-start(bf16[16,896]{1,0:T(8,128)(2,1)S(1)} %get-tuple-element.83), channel_id=1, source_target_pairs={{0,2},{1,3},{2,0},{3,1},{4,6},{5,7},{6,4},{7,5},{8,10},{9,11},{10,... | collective-permute-start | bytes 86024 | tf_op jit(solution)/shard_map/ppermute | solution.py:11
  36.9 1.0 %collective-permute-start.11 = (bf16[32,896]{1,0:T(8,128)(2,1)S(1)}, bf16[32,896]{1,0:T(8,128)(2,1)S(1)}, u32[]{:S(2)}, u32[]{:S(2)}) collective-permute-start(bf16[32,896]{1,0:T(8,128)(2,1)S(1)} %get-tuple-element.44), channel_id=1, source_target_pairs={{0,2},{1,3},{2,0},{3,1},{4,6},{5,7},{6,4},{7,5},{8,10},{9,11},{10,... | collective-permute-start | bytes 172040 | tf_op jit(solution)/shard_map/ppermute | solution.py:11
  37.9 0.6 collective-permute-done.15
  38.5 1.2 %collective-permute-done.13 = bf16[16,896]{1,0:T(8,128)(2,1)S(1)} collective-permute-done((bf16[16,896]{1,0:T(8,128)(2,1)S(1)}, bf16[16,896]{1,0:T(8,128)(2,1)S(1)}, u32[]{:S(2)}, u32[]{:S(2)}) %collective-permute-start.13) | collective-permute-done | bytes 28704 | tf_op jit(solution)/shard_map/ppermute | solution.py:11
  39.8 0.2 collective-permute-done.12
  40.0 2.2 %collective-permute-start.23 = (bf16[16,896]{1,0:T(8,128)(2,1)S(1)}, bf16[16,896]{1,0:T(8,128)(2,1)S(1)}, u32[]{:S(2)}, u32[]{:S(2)}) collective-permute-start(bf16[16,896]{1,0:T(8,128)(2,1)S(1)} %subtract_convert_fusion), channel_id=1, source_target_pairs={{0,6},{1,7},{2,4},{3,5},{4,2},{5,3},{6,0},{7,1},{8,14},{9,15},{10,... | collective-permute-start | bytes 86024 | tf_op jit(solution)/shard_map/ppermute | solution.py:11
  42.2 0.0 collective-permute-start.22
  42.2 2.2 %collective-permute-start.21 = (bf16[16,896]{1,0:T(8,128)(2,1)S(1)}, bf16[16,896]{1,0:T(8,128)(2,1)S(1)}, u32[]{:S(2)}, u32[]{:S(2)}) collective-permute-start(bf16[16,896]{1,0:T(8,128)(2,1)S(1)} %subtract_convert_fusion), channel_id=1, source_target_pairs={{0,2},{1,3},{2,0},{3,1},{4,6},{5,7},{6,4},{7,5},{8,10},{9,11},{10,... | collective-permute-start | bytes 86024 | tf_op jit(solution)/shard_map/ppermute | solution.py:11
  44.5 2.2 %collective-permute-start.20 = (bf16[32,896]{1,0:T(8,128)(2,1)S(1)}, bf16[32,896]{1,0:T(8,128)(2,1)S(1)}, u32[]{:S(2)}, u32[]{:S(2)}) collective-permute-start(bf16[32,896]{1,0:T(8,128)(2,1)S(1)} %fusion.24), channel_id=1, source_target_pairs={{0,6},{1,7},{2,4},{3,5},{4,2},{5,3},{6,0},{7,1},{8,14},{9,15},{10,... | collective-permute-start | bytes 172040 | tf_op jit(solution)/shard_map/ppermute | solution.py:11
  46.7 2.2 %collective-permute-start.18 = (bf16[32,896]{1,0:T(8,128)(2,1)S(1)}, bf16[32,896]{1,0:T(8,128)(2,1)S(1)}, u32[]{:S(2)}, u32[]{:S(2)}) collective-permute-start(bf16[32,896]{1,0:T(8,128)(2,1)S(1)} %fusion.24), channel_id=1, source_target_pairs={{0,2},{1,3},{2,0},{3,1},{4,6},{5,7},{6,4},{7,5},{8,10},{9,11},{10,... | collective-permute-start | bytes 172040 | tf_op jit(solution)/shard_map/ppermute | solution.py:11
  49.0 1.7 %collective-permute-start.24 = (bf16[64,896]{1,0:T(8,128)(2,1)S(1)}, bf16[64,896]{1,0:T(8,128)(2,1)S(1)}, u32[]{:S(2)}, u32[]{:S(2)}) collective-permute-start(bf16[64,896]{1,0:T(8,128)(2,1)S(1)} %pad_maximum_fusion.5), channel_id=1, source_target_pairs={{0,1},{1,0},{2,3},{3,2},{4,5},{5,4},{6,7},{7,6},{8,9},{9,8},{10,11... | collective-permute-start | bytes 344072 | tf_op jit(solution)/shard_map/ppermute | solution.py:11
  50.7 1.2 %collective-permute-start.26 = (bf16[16,896]{1,0:T(8,128)(2,1)S(1)}, bf16[16,896]{1,0:T(8,128)(2,1)S(1)}, u32[]{:S(2)}, u32[]{:S(2)}) collective-permute-start(bf16[16,896]{1,0:T(8,128)(2,1)S(1)} %subtract_convert_fusion), channel_id=1, source_target_pairs={{0,16},{8,24},{16,0},{24,8},{1,17},{9,25},{17,1},{25,9},{2,18},{10... | collective-permute-start | bytes 86024 | tf_op jit(solution)/shard_map/ppermute | solution.py:11
  51.9 0.3 fusion.25
  52.3 1.6 %collective-permute-done.24 = bf16[64,896]{1,0:T(8,128)(2,1)S(1)} collective-permute-done((bf16[64,896]{1,0:T(8,128)(2,1)S(1)}, bf16[64,896]{1,0:T(8,128)(2,1)S(1)}, u32[]{:S(2)}, u32[]{:S(2)}) %collective-permute-start.24) | collective-permute-done | bytes 114720 | tf_op jit(solution)/shard_map/ppermute | solution.py:11
  53.8 0.3 fusion.52
  54.1 0.3 fusion.8
  54.5 0.3 convolution_add_fusion.3
  54.8 0.1 collective-permute-start.25
  54.9 1.4 %collective-permute-done.25 = f32[384,128]{1,0:T(8,128)S(1)} collective-permute-done((f32[384,128]{1,0:T(8,128)S(1)}, f32[384,128]{1,0:T(8,128)S(1)}, u32[]{:S(2)}, u32[]{:S(2)}) %collective-permute-start.25) | collective-permute-done | bytes 196640 | tf_op jit(solution)/shard_map/ppermute | solution.py:11
  56.5 1.3 %collective-permute-start.29 = (bf16[128,128]{1,0:T(8,128)(2,1)S(1)}, bf16[128,128]{1,0:T(8,128)(2,1)S(1)}, u32[]{:S(2)}, u32[]{:S(2)}) collective-permute-start(bf16[128,128]{1,0:T(8,128)(2,1)S(1)} %get-tuple-element.62), channel_id=1, source_target_pairs={{0,16},{8,24},{16,0},{24,8},{1,17},{9,25},{17,1},{25,9},{2,18},{10... | collective-permute-start | bytes 98312 | tf_op jit(solution)/shard_map/ppermute | solution.py:11
  57.8 1.7 %collective-permute-start.28 = (bf16[240,128]{1,0:T(8,128)(2,1)S(1)}, bf16[240,128]{1,0:T(8,128)(2,1)S(1)}, u32[]{:S(2)}, u32[]{:S(2)}) collective-permute-start(bf16[240,128]{1,0:T(8,128)(2,1)S(1)} %constant_dynamic-update-slice_fusion.4), channel_id=1, source_target_pairs={{0,1},{1,0},{2,3},{3,2},{4,5},{5,4},{6,7},{7,6},{8,9},{9,8},{10,11... | collective-permute-start | bytes 184328 | tf_op jit(solution)/shard_map/ppermute | solution.py:11
  59.4 0.1 broadcast_select_fusion.1
  59.6 2.4 %collective-permute-done.28 = bf16[240,128]{1,0:T(8,128)(2,1)S(1)} collective-permute-done((bf16[240,128]{1,0:T(8,128)(2,1)S(1)}, bf16[240,128]{1,0:T(8,128)(2,1)S(1)}, u32[]{:S(2)}, u32[]{:S(2)}) %collective-permute-start.28) | collective-permute-done | bytes 61472 | tf_op jit(solution)/shard_map/ppermute | solution.py:11
  62.1 0.6 maximum_select_fusion
  62.7 0.5 fusion.27
  63.3 1.4 %fusion = bf16[1,3584,128]{2,1,0:T(8,128)(2,1)} fusion(bf16[128,1792]{1,0:T(8,128)(2,1)S(1)} %get-tuple-element.70, bf16[128,1792]{1,0:T(8,128)(2,1)S(1)} %get-tuple-element.69, bf16[128,128]{1,0:T(8,128)(2,1)S(1)} %collective-permute-done.29, f32[384,128]{1,0:T(8,128)S(1)} %select_add_fusion, bf16[240,128]{1,0:T(8,128)(2,1)S(1)} %collective-permute-done.28, ...), kind=kOutput, calls=%fused_computation.1 | convolution fusion | flops 119832576 | bytes 1966592 | tf_op jit(solution)/shard_map/dot_general | solution.py:44
  (71 shorter events, 0.6 us)
Async XLA Ops:
  0.6 13.1 %copy-start = (s32[2,1,12]{2,1,0:T(1,128)S(1)}, s32[2,1,12]{2,1,0:T(1,128)}, u32[]{:S(2)}) copy-start(s32[2,1,12]{2,1,0:T(1,128)} %param.11) | copy-start | bytes 292
  0.6 11.9 %copy-start.2 = (bf16[1,3584,128]{2,1,0:T(8,128)(2,1)S(1)}, bf16[1,3584,128]{2,1,0:T(8,128)(2,1)}, u32[]{:S(2)}) copy-start(bf16[1,3584,128]{2,1,0:T(8,128)(2,1)} %param.8) | copy-start | bytes 2752516
  0.7 7.4 %collective-permute-start.3 = (bf16[3584,128]{1,0:T(8,128)(2,1)}, bf16[3584,128]{1,0:T(8,128)(2,1)}, u32[]{:S(2)}, u32[]{:S(2)}) collective-permute-start(bf16[3584,128]{1,0:T(8,128)(2,1)} %bitcast.111), channel_id=1, source_target_pairs={{0,8},{8,0},{16,24},{24,16},{1,9},{9,1},{17,25},{25,17},{2,10},{10... | collective-permute-start | bytes 2752520 | tf_op jit(solution)/shard_map/ppermute | solution.py:11
  2.0 6.0 %collective-permute-start.2 = (bf16[16,1792]{1,0:T(8,128)(2,1)S(1)}, bf16[16,1792]{1,0:T(8,128)(2,1)S(1)}, u32[]{:S(2)}, u32[]{:S(2)}) collective-permute-start(bf16[16,1792]{1,0:T(8,128)(2,1)S(1)} %get-tuple-element.78), channel_id=1, source_target_pairs={{0,1},{1,0},{2,3},{3,2},{4,5},{5,4},{6,7},{7,6},{8,9},{9,8},{10,11... | collective-permute-start | bytes 172040 | tf_op jit(solution)/shard_map/ppermute | solution.py:11
  4.6 9.1 %copy-start.3 = (f32[1,128]{1,0:T(1,128)S(1)}, f32[1,128]{1,0:T(1,128)}, u32[]{:S(2)}) copy-start(f32[1,128]{1,0:T(1,128)} %param.9) | copy-start | bytes 1540
  5.9 12.6 %collective-permute-start.1 = (bf16[256,896]{1,0:T(8,128)(2,1)S(1)}, bf16[256,896]{1,0:T(8,128)(2,1)S(1)}, u32[]{:S(2)}, u32[]{:S(2)}) collective-permute-start(bf16[256,896]{1,0:T(8,128)(2,1)S(1)} %get-tuple-element.67), channel_id=1, source_target_pairs={{0,16},{8,24},{16,0},{24,8},{1,17},{9,25},{17,1},{25,9},{2,18},{10... | collective-permute-start | bytes 1376264 | tf_op jit(solution)/shard_map/ppermute | solution.py:11
  7.5 12.2 %collective-permute-start = (bf16[256,896]{1,0:T(8,128)(2,1)S(1)}, bf16[256,896]{1,0:T(8,128)(2,1)S(1)}, u32[]{:S(2)}, u32[]{:S(2)}) collective-permute-start(bf16[256,896]{1,0:T(8,128)(2,1)S(1)} %get-tuple-element.68), channel_id=1, source_target_pairs={{0,1},{1,0},{2,3},{3,2},{4,5},{5,4},{6,7},{7,6},{8,9},{9,8},{10,11... | collective-permute-start | bytes 1376264 | tf_op jit(solution)/shard_map/ppermute | solution.py:11
  8.0 11.7 %collective-permute-start.6 = (bf16[32,1792]{1,0:T(8,128)(2,1)S(1)}, bf16[32,1792]{1,0:T(8,128)(2,1)S(1)}, u32[]{:S(2)}, u32[]{:S(2)}) collective-permute-start(bf16[32,1792]{1,0:T(8,128)(2,1)S(1)} %bitcast.102), channel_id=1, source_target_pairs={{0,6},{1,7},{2,4},{3,5},{4,2},{5,3},{6,0},{7,1},{8,14},{9,15},{10,... | collective-permute-start | bytes 344072 | tf_op jit(solution)/shard_map/ppermute | solution.py:11
  11.7 9.4 %collective-permute-start.5 = (bf16[32,1792]{1,0:T(8,128)(2,1)S(1)}, bf16[32,1792]{1,0:T(8,128)(2,1)S(1)}, u32[]{:S(2)}, u32[]{:S(2)}) collective-permute-start(bf16[32,1792]{1,0:T(8,128)(2,1)S(1)} %bitcast.103), channel_id=1, source_target_pairs={{0,4},{1,5},{2,6},{3,7},{4,0},{5,1},{6,2},{7,3},{8,12},{9,13},{10,... | collective-permute-start | bytes 344072 | tf_op jit(solution)/shard_map/ppermute | solution.py:11
  11.7 9.4 %collective-permute-start.4 = (bf16[32,1792]{1,0:T(8,128)(2,1)S(1)}, bf16[32,1792]{1,0:T(8,128)(2,1)S(1)}, u32[]{:S(2)}, u32[]{:S(2)}) collective-permute-start(bf16[32,1792]{1,0:T(8,128)(2,1)S(1)} %bitcast.104), channel_id=1, source_target_pairs={{0,2},{1,3},{2,0},{3,1},{4,6},{5,7},{6,4},{7,5},{8,10},{9,11},{10,... | collective-permute-start | bytes 344072 | tf_op jit(solution)/shard_map/ppermute | solution.py:11
  13.9 12.9 %copy-start.1 = (bf16[1,2,2,128,1792]{4,3,2,1,0:T(8,128)(2,1)S(1)}, bf16[1,2,2,128,1792]{4,3,2,1,0:T(8,128)(2,1)}, u32[]{:S(2)}) copy-start(bf16[1,2,2,128,1792]{4,3,2,1,0:T(8,128)(2,1)} %param.10) | copy-start | bytes 5505028
  21.4 1.4 %collective-permute-start.7 = (f32[128,256]{1,0:T(8,128)S(1)}, f32[128,256]{1,0:T(8,128)S(1)}, u32[]{:S(2)}, u32[]{:S(2)}) collective-permute-start(f32[128,256]{1,0:T(8,128)S(1)} %convolution_add_fusion.4), channel_id=1, source_target_pairs={{0,8},{8,0},{16,24},{24,16},{1,9},{9,1},{17,25},{25,17},{2,10},{10... | collective-permute-start | bytes 393224 | tf_op jit(solution)/shard_map/ppermute | solution.py:11
  22.9 4.3 %collective-permute-start.9 = (bf16[128,256]{1,0:T(8,128)(2,1)S(1)}, bf16[128,256]{1,0:T(8,128)(2,1)S(1)}, u32[]{:S(2)}, u32[]{:S(2)}) collective-permute-start(bf16[128,256]{1,0:T(8,128)(2,1)S(1)} %multiply_convert_fusion), channel_id=1, source_target_pairs={{0,16},{8,24},{16,0},{24,8},{1,17},{9,25},{17,1},{25,9},{2,18},{10... | collective-permute-start | bytes 196616 | tf_op jit(solution)/shard_map/ppermute | solution.py:11
  23.8 5.2 %collective-permute-start.8 = (bf16[128,256]{1,0:T(8,128)(2,1)S(1)}, bf16[128,256]{1,0:T(8,128)(2,1)S(1)}, u32[]{:S(2)}, u32[]{:S(2)}) collective-permute-start(bf16[128,256]{1,0:T(8,128)(2,1)S(1)} %bitcast.117), channel_id=1, source_target_pairs={{0,1},{1,0},{2,3},{3,2},{4,5},{5,4},{6,7},{7,6},{8,9},{9,8},{10,11... | collective-permute-start | bytes 196616 | tf_op jit(solution)/shard_map/ppermute | solution.py:11
  26.2 9.6 %collective-permute-start.17 = (bf16[16,896]{1,0:T(8,128)(2,1)S(1)}, bf16[16,896]{1,0:T(8,128)(2,1)S(1)}, u32[]{:S(2)}, u32[]{:S(2)}) collective-permute-start(bf16[16,896]{1,0:T(8,128)(2,1)S(1)} %get-tuple-element.71), channel_id=1, source_target_pairs={{0,1},{1,0},{2,3},{3,2},{4,5},{5,4},{6,7},{7,6},{8,9},{9,8},{10,11... | collective-permute-start | bytes 86024 | tf_op jit(solution)/shard_map/ppermute | solution.py:11
  27.4 4.9 %collective-permute-start.10 = (bf16[64,896]{1,0:T(8,128)(2,1)S(1)}, bf16[64,896]{1,0:T(8,128)(2,1)S(1)}, u32[]{:S(2)}, u32[]{:S(2)}) collective-permute-start(bf16[64,896]{1,0:T(8,128)(2,1)S(1)} %fusion.1), channel_id=1, source_target_pairs={{0,1},{1,0},{2,3},{3,2},{4,5},{5,4},{6,7},{7,6},{8,9},{9,8},{10,11... | collective-permute-start | bytes 344072 | tf_op jit(solution)/shard_map/ppermute | solution.py:11
  29.5 7.3 %collective-permute-start.16 = (bf16[32,896]{1,0:T(8,128)(2,1)S(1)}, bf16[32,896]{1,0:T(8,128)(2,1)S(1)}, u32[]{:S(2)}, u32[]{:S(2)}) collective-permute-start(bf16[32,896]{1,0:T(8,128)(2,1)S(1)} %get-tuple-element.74), channel_id=1, source_target_pairs={{0,6},{1,7},{2,4},{3,5},{4,2},{5,3},{6,0},{7,1},{8,14},{9,15},{10,... | collective-permute-start | bytes 172040 | tf_op jit(solution)/shard_map/ppermute | solution.py:11
  32.0 6.5 %collective-permute-start.15 = (bf16[32,896]{1,0:T(8,128)(2,1)S(1)}, bf16[32,896]{1,0:T(8,128)(2,1)S(1)}, u32[]{:S(2)}, u32[]{:S(2)}) collective-permute-start(bf16[32,896]{1,0:T(8,128)(2,1)S(1)} %get-tuple-element.75), channel_id=1, source_target_pairs={{0,4},{1,5},{2,6},{3,7},{4,0},{5,1},{6,2},{7,3},{8,12},{9,13},{10,... | collective-permute-start | bytes 172040 | tf_op jit(solution)/shard_map/ppermute | solution.py:11
  32.4 6.2 %collective-permute-start.14 = (bf16[16,896]{1,0:T(8,128)(2,1)S(1)}, bf16[16,896]{1,0:T(8,128)(2,1)S(1)}, u32[]{:S(2)}, u32[]{:S(2)}) collective-permute-start(bf16[16,896]{1,0:T(8,128)(2,1)S(1)} %get-tuple-element.81), channel_id=1, source_target_pairs={{0,6},{1,7},{2,4},{3,5},{4,2},{5,3},{6,0},{7,1},{8,14},{9,15},{10,... | collective-permute-start | bytes 86024 | tf_op jit(solution)/shard_map/ppermute | solution.py:11
  34.9 4.9 %collective-permute-start.13 = (bf16[16,896]{1,0:T(8,128)(2,1)S(1)}, bf16[16,896]{1,0:T(8,128)(2,1)S(1)}, u32[]{:S(2)}, u32[]{:S(2)}) collective-permute-start(bf16[16,896]{1,0:T(8,128)(2,1)S(1)} %get-tuple-element.82), channel_id=1, source_target_pairs={{0,4},{1,5},{2,6},{3,7},{4,0},{5,1},{6,2},{7,3},{8,12},{9,13},{10,... | collective-permute-start | bytes 86024 | tf_op jit(solution)/shard_map/ppermute | solution.py:11
  35.8 4.2 %collective-permute-start.12 = (bf16[16,896]{1,0:T(8,128)(2,1)S(1)}, bf16[16,896]{1,0:T(8,128)(2,1)S(1)}, u32[]{:S(2)}, u32[]{:S(2)}) collective-permute-start(bf16[16,896]{1,0:T(8,128)(2,1)S(1)} %get-tuple-element.83), channel_id=1, source_target_pairs={{0,2},{1,3},{2,0},{3,1},{4,6},{5,7},{6,4},{7,5},{8,10},{9,11},{10,... | collective-permute-start | bytes 86024 | tf_op jit(solution)/shard_map/ppermute | solution.py:11
  36.9 7.6 %collective-permute-start.11 = (bf16[32,896]{1,0:T(8,128)(2,1)S(1)}, bf16[32,896]{1,0:T(8,128)(2,1)S(1)}, u32[]{:S(2)}, u32[]{:S(2)}) collective-permute-start(bf16[32,896]{1,0:T(8,128)(2,1)S(1)} %get-tuple-element.44), channel_id=1, source_target_pairs={{0,2},{1,3},{2,0},{3,1},{4,6},{5,7},{6,4},{7,5},{8,10},{9,11},{10,... | collective-permute-start | bytes 172040 | tf_op jit(solution)/shard_map/ppermute | solution.py:11
  40.0 6.7 %collective-permute-start.23 = (bf16[16,896]{1,0:T(8,128)(2,1)S(1)}, bf16[16,896]{1,0:T(8,128)(2,1)S(1)}, u32[]{:S(2)}, u32[]{:S(2)}) collective-permute-start(bf16[16,896]{1,0:T(8,128)(2,1)S(1)} %subtract_convert_fusion), channel_id=1, source_target_pairs={{0,6},{1,7},{2,4},{3,5},{4,2},{5,3},{6,0},{7,1},{8,14},{9,15},{10,... | collective-permute-start | bytes 86024 | tf_op jit(solution)/shard_map/ppermute | solution.py:11
  42.2 6.7 %collective-permute-start.22 = (bf16[16,896]{1,0:T(8,128)(2,1)S(1)}, bf16[16,896]{1,0:T(8,128)(2,1)S(1)}, u32[]{:S(2)}, u32[]{:S(2)}) collective-permute-start(bf16[16,896]{1,0:T(8,128)(2,1)S(1)} %subtract_convert_fusion), channel_id=1, source_target_pairs={{0,4},{1,5},{2,6},{3,7},{4,0},{5,1},{6,2},{7,3},{8,12},{9,13},{10,... | collective-permute-start | bytes 86024 | tf_op jit(solution)/shard_map/ppermute | solution.py:11
  42.2 6.7 %collective-permute-start.21 = (bf16[16,896]{1,0:T(8,128)(2,1)S(1)}, bf16[16,896]{1,0:T(8,128)(2,1)S(1)}, u32[]{:S(2)}, u32[]{:S(2)}) collective-permute-start(bf16[16,896]{1,0:T(8,128)(2,1)S(1)} %subtract_convert_fusion), channel_id=1, source_target_pairs={{0,2},{1,3},{2,0},{3,1},{4,6},{5,7},{6,4},{7,5},{8,10},{9,11},{10,... | collective-permute-start | bytes 86024 | tf_op jit(solution)/shard_map/ppermute | solution.py:11
  44.5 7.4 %collective-permute-start.20 = (bf16[32,896]{1,0:T(8,128)(2,1)S(1)}, bf16[32,896]{1,0:T(8,128)(2,1)S(1)}, u32[]{:S(2)}, u32[]{:S(2)}) collective-permute-start(bf16[32,896]{1,0:T(8,128)(2,1)S(1)} %fusion.24), channel_id=1, source_target_pairs={{0,6},{1,7},{2,4},{3,5},{4,2},{5,3},{6,0},{7,1},{8,14},{9,15},{10,... | collective-permute-start | bytes 172040 | tf_op jit(solution)/shard_map/ppermute | solution.py:11
  46.7 5.2 %collective-permute-start.19 = (bf16[32,896]{1,0:T(8,128)(2,1)S(1)}, bf16[32,896]{1,0:T(8,128)(2,1)S(1)}, u32[]{:S(2)}, u32[]{:S(2)}) collective-permute-start(bf16[32,896]{1,0:T(8,128)(2,1)S(1)} %fusion.24), channel_id=1, source_target_pairs={{0,4},{1,5},{2,6},{3,7},{4,0},{5,1},{6,2},{7,3},{8,12},{9,13},{10,... | collective-permute-start | bytes 172040 | tf_op jit(solution)/shard_map/ppermute | solution.py:11
  46.7 5.2 %collective-permute-start.18 = (bf16[32,896]{1,0:T(8,128)(2,1)S(1)}, bf16[32,896]{1,0:T(8,128)(2,1)S(1)}, u32[]{:S(2)}, u32[]{:S(2)}) collective-permute-start(bf16[32,896]{1,0:T(8,128)(2,1)S(1)} %fusion.24), channel_id=1, source_target_pairs={{0,2},{1,3},{2,0},{3,1},{4,6},{5,7},{6,4},{7,5},{8,10},{9,11},{10,... | collective-permute-start | bytes 172040 | tf_op jit(solution)/shard_map/ppermute | solution.py:11
  49.0 4.9 %collective-permute-start.24 = (bf16[64,896]{1,0:T(8,128)(2,1)S(1)}, bf16[64,896]{1,0:T(8,128)(2,1)S(1)}, u32[]{:S(2)}, u32[]{:S(2)}) collective-permute-start(bf16[64,896]{1,0:T(8,128)(2,1)S(1)} %pad_maximum_fusion.5), channel_id=1, source_target_pairs={{0,1},{1,0},{2,3},{3,2},{4,5},{5,4},{6,7},{7,6},{8,9},{9,8},{10,11... | collective-permute-start | bytes 344072 | tf_op jit(solution)/shard_map/ppermute | solution.py:11
  50.7 5.7 %collective-permute-start.26 = (bf16[16,896]{1,0:T(8,128)(2,1)S(1)}, bf16[16,896]{1,0:T(8,128)(2,1)S(1)}, u32[]{:S(2)}, u32[]{:S(2)}) collective-permute-start(bf16[16,896]{1,0:T(8,128)(2,1)S(1)} %subtract_convert_fusion), channel_id=1, source_target_pairs={{0,16},{8,24},{16,0},{24,8},{1,17},{9,25},{17,1},{25,9},{2,18},{10... | collective-permute-start | bytes 86024 | tf_op jit(solution)/shard_map/ppermute | solution.py:11
  51.9 4.5 %collective-permute-start.27 = (bf16[128,1792]{1,0:T(8,128)(2,1)S(1)}, bf16[128,1792]{1,0:T(8,128)(2,1)S(1)}, u32[]{:S(2)}, u32[]{:S(2)}) collective-permute-start(bf16[128,1792]{1,0:T(8,128)(2,1)S(1)} %constant_dynamic-update-slice_fusion), channel_id=1, source_target_pairs={{0,8},{8,0},{16,24},{24,16},{1,9},{9,1},{17,25},{25,17},{2,10},{10... | collective-permute-start | bytes 1376264 | tf_op jit(solution)/shard_map/ppermute | solution.py:11
  54.8 1.5 %collective-permute-start.25 = (f32[384,128]{1,0:T(8,128)S(1)}, f32[384,128]{1,0:T(8,128)S(1)}, u32[]{:S(2)}, u32[]{:S(2)}) collective-permute-start(f32[384,128]{1,0:T(8,128)S(1)} %slice_select_fusion), channel_id=1, source_target_pairs={{0,8},{8,0},{16,24},{24,16},{1,9},{9,1},{17,25},{25,17},{2,10},{10... | collective-permute-start | bytes 589832 | tf_op jit(solution)/shard_map/ppermute | solution.py:11
  56.5 6.2 %collective-permute-start.29 = (bf16[128,128]{1,0:T(8,128)(2,1)S(1)}, bf16[128,128]{1,0:T(8,128)(2,1)S(1)}, u32[]{:S(2)}, u32[]{:S(2)}) collective-permute-start(bf16[128,128]{1,0:T(8,128)(2,1)S(1)} %get-tuple-element.62), channel_id=1, source_target_pairs={{0,16},{8,24},{16,0},{24,8},{1,17},{9,25},{17,1},{25,9},{2,18},{10... | collective-permute-start | bytes 98312 | tf_op jit(solution)/shard_map/ppermute | solution.py:11
  57.8 4.2 %collective-permute-start.28 = (bf16[240,128]{1,0:T(8,128)(2,1)S(1)}, bf16[240,128]{1,0:T(8,128)(2,1)S(1)}, u32[]{:S(2)}, u32[]{:S(2)}) collective-permute-start(bf16[240,128]{1,0:T(8,128)(2,1)S(1)} %constant_dynamic-update-slice_fusion.4), channel_id=1, source_target_pairs={{0,1},{1,0},{2,3},{3,2},{4,5},{5,4},{6,7},{7,6},{8,9},{9,8},{10,11... | collective-permute-start | bytes 184328 | tf_op jit(solution)/shard_map/ppermute | solution.py:11

commit v19 on v18

--- a/solution.py
+++ b/solution.py
@@ -159,19 +159,14 @@
         axis=0,
     )
     lower, upper = grads[:, :latents], grads[:, latents:]
-    grads = jnp.where(half == 0, lower, upper) + over_core(jnp.where(half == 0, upper, lower))
-
-
+    leaving, late_own = hold((jnp.where(half == 0, upper, lower), err_own))
+    grads = jnp.where(half == 0, lower, upper) + over_core(leaving)
+    own_there = over_x(rows_at(late_own, 1))
     grads, shared_there, resid_other = hold((grads, shared_there, resid_other))
-
-    away = rows_at(err_own, 1)
-    tiles = [away[:, at:at + latents] for at in range(0, part, latents)]
-    to_x = jnp.concatenate([grads[tokens:2 * tokens].astype(BF16)] + tiles, axis=0)
-    to_x, to_y = hold((to_x, grads[2 * tokens:].astype(BF16)))
-    from_x, from_y = over_x(to_x), over_y(to_y).astype(F32)
-    tiles = from_x[tokens:].reshape(part // latents, rows, latents)
-    own_there = jnp.concatenate([tiles[i] for i in range(part // latents)], axis=1)
-    from_x = from_x[:tokens].astype(F32)
+    from_x = over_x(grads[tokens:2 * tokens].astype(BF16))
+    from_y = over_y(grads[2 * tokens:].astype(BF16))
+    from_y, own_there = hold((from_y, own_there))
+    from_x, from_y = from_x.astype(F32), from_y.astype(F32)
     errors = jnp.where(
         layer == 0,
         ordered(side, rows_at(err_own, 0), own_there, axis=1),

time: 64.9 us -> 64.9 us (level)
  starting transfers between devices: 37.3 us -> 38.7 us
  waiting for transfers between devices: 16.1 us -> 14.8 us
    ppermute x30 -> x31, starting transfers between devices: 37.3 us -> 38.7 us  [crossed(): lax.ppermute(block, axis, [(i, i ^ mask) for i in range(lax.axis_size(axi...]
    ppermute x30 -> x31, waiting for transfers between devices: 16.1 us -> 14.8 us  [crossed(): lax.ppermute(block, axis, [(i, i ^ mask) for i in range(lax.axis_size(axi...]
  transfers between devices with their start and end apart: 30 -> 31, of which waited for: 10 -> 9; matrix products, arithmetic and copies ran while one was open for 12% -> 12% of each run, Pallas kernels for 0% -> 0%
where the time goes in v19:
time: 64.9 us; the launch traced here: 64.6 us
  starting transfers between devices  38.7 us (60%)
  waiting for transfers between devices  14.8 us (23%)
  matrix products  4.15 us (6%)
  local copies, waits for them, and re-layouts  2.99 us (5%)
  other arithmetic  2.93 us (5%)
  between operations  1.03 us (2%)
    ppermute x31, starting transfers between devices, crossed(): lax.ppermute(block, axis, [(i, i ^ mask) for i in range(lax.axis_size(axi...  38.7 us
    ppermute x31, waiting for transfers between devices, crossed(): lax.ppermute(block, axis, [(i, i ^ mask) for i in range(lax.axis_size(axi...  14.8 us
    dot_general x7, matrix products, times(): return jnp.dot(left, right, preferred_element_type=F32)  1.6 us
    dot_general x1, matrix products, encoder_gradient(): lax.dot_general(whole, grad_low, (((0,), (0,)), ((), ())), preferred_elem...  1.36 us
    select_n x3, other arithmetic, both_halves(): jnp.where(half == 0, mine, other)  1.32 us
  transfers between devices with their start and end apart: 31, of which 9 were waited for; matrix products, arithmetic and copies ran while one was open for 12% of the time, Pallas kernels for 0%

profile of v19, /device:TPU:0, one launch (start us, length us, event | category | flops | bytes accessed | tf_op | source)
XLA Modules:
  0.0 64.6 jit_solution(6911534793980498634)
XLA Ops:
  0.6 0.0 copy-start
  0.7 0.5 collective-permute-start.3
  1.2 0.8 %dynamic-slice_bitcast_fusion.3 = (bf16[1,1,16,1792]{3,2,1,0:T(8,128)(2,1)S(1)}, bf16[16,1792]{1,0:T(8,128)(2,1)S(1)}) fusion(bf16[2,16,3584]{2,1,0:T(8,128)(2,1)} %param.6, s32[]{:T(128)S(6)} %select_n.168, s32[]{:T(128)S(6)} %select_n.173), kind=kLoop, calls=%fused_computation.54 | loop fusion | bytes 172040 | tf_op jit(solution)/shard_map/reshape;squeeze | solution.py:100
  2.0 2.6 %collective-permute-start.2 = (bf16[16,1792]{1,0:T(8,128)(2,1)S(1)}, bf16[16,1792]{1,0:T(8,128)(2,1)S(1)}, u32[]{:S(2)}, u32[]{:S(2)}) collective-permute-start(bf16[16,1792]{1,0:T(8,128)(2,1)S(1)} %get-tuple-element.82), channel_id=1, source_target_pairs={{0,1},{1,0},{2,3},{3,2},{4,5},{5,4},{6,7},{7,6},{8,9},{9,8},{10,11... | collective-permute-start | bytes 172040 | tf_op jit(solution)/shard_map/ppermute | solution.py:11
  4.6 1.2 %dynamic-slice_bitcast_fusion = (bf16[256,896]{1,0:T(8,128)(2,1)S(1)}, bf16[256,896]{1,0:T(8,128)(2,1)S(1)}) fusion(bf16[2,256,1792]{2,1,0:T(8,128)(2,1)} %bitcast.92, s32[]{:T(128)S(6)} %select_n.170, s32[]{:T(128)S(6)} %select_n.171, s32[]{:T(128)S(6)} %select_n.168, s32[]{:T(128)S(6)} %select_n.169), kind=kLoop, calls=%fused_computation.24 | loop fusion | bytes 1835024 | tf_op jit(solution)/shard_map/squeeze | solution.py:91
  5.9 1.6 %collective-permute-start.1 = (bf16[256,896]{1,0:T(8,128)(2,1)S(1)}, bf16[256,896]{1,0:T(8,128)(2,1)S(1)}, u32[]{:S(2)}, u32[]{:S(2)}) collective-permute-start(bf16[256,896]{1,0:T(8,128)(2,1)S(1)} %get-tuple-element.71), channel_id=1, source_target_pairs={{0,16},{8,24},{16,0},{24,8},{1,17},{9,25},{17,1},{25,9},{2,18},{10... | collective-permute-start | bytes 1376264 | tf_op jit(solution)/shard_map/ppermute | solution.py:11
  7.5 0.5 collective-permute-start
  8.0 0.0 collective-permute-done.2
  8.0 0.0 collective-permute-done.3
  8.0 3.7 %collective-permute-start.6 = (bf16[32,1792]{1,0:T(8,128)(2,1)S(1)}, bf16[32,1792]{1,0:T(8,128)(2,1)S(1)}, u32[]{:S(2)}, u32[]{:S(2)}) collective-permute-start(bf16[32,1792]{1,0:T(8,128)(2,1)S(1)} %bitcast.103), channel_id=1, source_target_pairs={{0,6},{1,7},{2,4},{3,5},{4,2},{5,3},{6,0},{7,1},{8,14},{9,15},{10,... | collective-permute-start | bytes 344072 | tf_op jit(solution)/shard_map/ppermute | solution.py:11
  11.7 0.8 %collective-permute-start.4 = (bf16[32,1792]{1,0:T(8,128)(2,1)S(1)}, bf16[32,1792]{1,0:T(8,128)(2,1)S(1)}, u32[]{:S(2)}, u32[]{:S(2)}) collective-permute-start(bf16[32,1792]{1,0:T(8,128)(2,1)S(1)} %bitcast.105), channel_id=1, source_target_pairs={{0,2},{1,3},{2,0},{3,1},{4,6},{5,7},{6,4},{7,5},{8,10},{9,11},{10,... | collective-permute-start | bytes 344072 | tf_op jit(solution)/shard_map/ppermute | solution.py:11
  12.5 1.2 %bitcast_select_fusion.1 = (bf16[1792,128]{1,0:T(8,128)(2,1)S(1)}, bf16[1792,128]{1,0:T(8,128)(2,1)S(1)}) fusion(pred[]{:T(512)S(6)} %eq.48, bf16[3584,128]{1,0:T(8,128)(2,1)} %collective-permute-done.3, s32[]{:T(128)S(6)} %select_n.173, bf16[1,3584,128]{2,1,0:T(8,128)(2,1)S(1)} %copy-done.2), kind=kLoop, calls=%fused_computation.23 | loop fusion | flops 458752 | bytes 1835013 | tf_op jit(solution)/shard_map/jit(_where)/select_n | solution.py:23
  13.8 0.1 compare_reduce_fusion
  13.9 0.0 copy-start.1
  13.9 4.6 %collective-permute-done.1 = bf16[256,896]{1,0:T(8,128)(2,1)S(1)} collective-permute-done((bf16[256,896]{1,0:T(8,128)(2,1)S(1)}, bf16[256,896]{1,0:T(8,128)(2,1)S(1)}, u32[]{:S(2)}, u32[]{:S(2)}) %collective-permute-start.1) | collective-permute-done | bytes 458784 | tf_op jit(solution)/shard_map/ppermute | solution.py:11
  18.5 1.2 %collective-permute-done = bf16[256,896]{1,0:T(8,128)(2,1)S(1)} collective-permute-done((bf16[256,896]{1,0:T(8,128)(2,1)S(1)}, bf16[256,896]{1,0:T(8,128)(2,1)S(1)}, u32[]{:S(2)}, u32[]{:S(2)}) %collective-permute-start) | collective-permute-done | bytes 458784 | tf_op jit(solution)/shard_map/ppermute | solution.py:11
  19.7 0.0 collective-permute-done.6
  19.7 1.4 %collective-permute-done.5 = bf16[32,1792]{1,0:T(8,128)(2,1)S(1)} collective-permute-done((bf16[32,1792]{1,0:T(8,128)(2,1)S(1)}, bf16[32,1792]{1,0:T(8,128)(2,1)S(1)}, u32[]{:S(2)}, u32[]{:S(2)}) %collective-permute-start.5) | collective-permute-done | bytes 114720 | tf_op jit(solution)/shard_map/ppermute | solution.py:11
  21.1 0.0 collective-permute-done.4
  21.1 0.3 convolution_add_fusion.4
  21.4 0.1 collective-permute-start.7
  21.5 1.3 %collective-permute-done.7 = f32[128,256]{1,0:T(8,128)S(1)} collective-permute-done((f32[128,256]{1,0:T(8,128)S(1)}, f32[128,256]{1,0:T(8,128)S(1)}, u32[]{:S(2)}, u32[]{:S(2)}) %collective-permute-start.7) | collective-permute-done | bytes 131104 | tf_op jit(solution)/shard_map/ppermute | solution.py:11
  22.9 0.9 %collective-permute-start.9 = (bf16[128,256]{1,0:T(8,128)(2,1)S(1)}, bf16[128,256]{1,0:T(8,128)(2,1)S(1)}, u32[]{:S(2)}, u32[]{:S(2)}) collective-permute-start(bf16[128,256]{1,0:T(8,128)(2,1)S(1)} %multiply_convert_fusion), channel_id=1, source_target_pairs={{0,16},{8,24},{16,0},{24,8},{1,17},{9,25},{17,1},{25,9},{2,18},{10... | collective-permute-start | bytes 196616 | tf_op jit(solution)/shard_map/ppermute | solution.py:11
  23.8 1.6 %collective-permute-start.8 = (bf16[128,256]{1,0:T(8,128)(2,1)S(1)}, bf16[128,256]{1,0:T(8,128)(2,1)S(1)}, u32[]{:S(2)}, u32[]{:S(2)}) collective-permute-start(bf16[128,256]{1,0:T(8,128)(2,1)S(1)} %bitcast.118), channel_id=1, source_target_pairs={{0,1},{1,0},{2,3},{3,2},{4,5},{5,4},{6,7},{7,6},{8,9},{9,8},{10,11... | collective-permute-start | bytes 196616 | tf_op jit(solution)/shard_map/ppermute | solution.py:11
  25.4 0.8 %dynamic-slice_bitcast_fusion.4 = (bf16[16,896]{1,0:T(8,128)(2,1)S(1)}, bf16[16,896]{1,0:T(8,128)(2,1)S(1)}, bf16[16,896]{1,0:T(8,128)(2,1)S(1)}) fusion(bf16[3,16,3584]{2,1,0:T(8,128)(2,1)} %param.7, s32[]{:T(128)S(6)} %select_n.185, s32[]{:T(128)S(6)} %select_n.188, s32[]{:T(128)S(6)} %select_n.187, s32[]{:T(128)S(6)} %select_n.186), kind=kLoop, calls=%fused_computation.61 | loop fusion | bytes 172048 | tf_op jit(solution)/shard_map/squeeze | solution.py:127
  26.2 0.6 collective-permute-start.17
  26.8 0.2 fusion.10
  27.0 0.2 fusion.12
  27.2 0.2 fusion.1
  27.4 1.5 %collective-permute-start.10 = (bf16[64,896]{1,0:T(8,128)(2,1)S(1)}, bf16[64,896]{1,0:T(8,128)(2,1)S(1)}, u32[]{:S(2)}, u32[]{:S(2)}) collective-permute-start(bf16[64,896]{1,0:T(8,128)(2,1)S(1)} %fusion.1), channel_id=1, source_target_pairs={{0,1},{1,0},{2,3},{3,2},{4,5},{5,4},{6,7},{7,6},{8,9},{9,8},{10,11... | collective-permute-start | bytes 344072 | tf_op jit(solution)/shard_map/ppermute | solution.py:11
  29.0 0.2 fusion.51
  29.2 0.2 fusion.50
  29.5 2.5 %collective-permute-start.16 = (bf16[32,896]{1,0:T(8,128)(2,1)S(1)}, bf16[32,896]{1,0:T(8,128)(2,1)S(1)}, u32[]{:S(2)}, u32[]{:S(2)}) collective-permute-start(bf16[32,896]{1,0:T(8,128)(2,1)S(1)} %get-tuple-element.78), channel_id=1, source_target_pairs={{0,6},{1,7},{2,4},{3,5},{4,2},{5,3},{6,0},{7,1},{8,14},{9,15},{10,... | collective-permute-start | bytes 172040 | tf_op jit(solution)/shard_map/ppermute | solution.py:11
  32.0 0.2 convolution_add_fusion.1
  32.3 0.0 collective-permute-done.10
  32.4 2.5 %collective-permute-start.14 = (bf16[16,896]{1,0:T(8,128)(2,1)S(1)}, bf16[16,896]{1,0:T(8,128)(2,1)S(1)}, u32[]{:S(2)}, u32[]{:S(2)}) collective-permute-start(bf16[16,896]{1,0:T(8,128)(2,1)S(1)} %get-tuple-element.85), channel_id=1, source_target_pairs={{0,6},{1,7},{2,4},{3,5},{4,2},{5,3},{6,0},{7,1},{8,14},{9,15},{10,... | collective-permute-start | bytes 86024 | tf_op jit(solution)/shard_map/ppermute | solution.py:11
  34.9 0.9 %collective-permute-start.13 = (bf16[16,896]{1,0:T(8,128)(2,1)S(1)}, bf16[16,896]{1,0:T(8,128)(2,1)S(1)}, u32[]{:S(2)}, u32[]{:S(2)}) collective-permute-start(bf16[16,896]{1,0:T(8,128)(2,1)S(1)} %get-tuple-element.86), channel_id=1, source_target_pairs={{0,4},{1,5},{2,6},{3,7},{4,0},{5,1},{6,2},{7,3},{8,12},{9,13},{10,... | collective-permute-start | bytes 86024 | tf_op jit(solution)/shard_map/ppermute | solution.py:11
  35.8 0.0 collective-permute-done.17
  35.8 1.0 %collective-permute-start.12 = (bf16[16,896]{1,0:T(8,128)(2,1)S(1)}, bf16[16,896]{1,0:T(8,128)(2,1)S(1)}, u32[]{:S(2)}, u32[]{:S(2)}) collective-permute-start(bf16[16,896]{1,0:T(8,128)(2,1)S(1)} %get-tuple-element.87), channel_id=1, source_target_pairs={{0,2},{1,3},{2,0},{3,1},{4,6},{5,7},{6,4},{7,5},{8,10},{9,11},{10,... | collective-permute-start | bytes 86024 | tf_op jit(solution)/shard_map/ppermute | solution.py:11
  36.9 1.0 %collective-permute-start.11 = (bf16[32,896]{1,0:T(8,128)(2,1)S(1)}, bf16[32,896]{1,0:T(8,128)(2,1)S(1)}, u32[]{:S(2)}, u32[]{:S(2)}) collective-permute-start(bf16[32,896]{1,0:T(8,128)(2,1)S(1)} %get-tuple-element.46), channel_id=1, source_target_pairs={{0,2},{1,3},{2,0},{3,1},{4,6},{5,7},{6,4},{7,5},{8,10},{9,11},{10,... | collective-permute-start | bytes 172040 | tf_op jit(solution)/shard_map/ppermute | solution.py:11
  37.9 0.6 collective-permute-done.15
  38.5 1.2 %collective-permute-done.13 = bf16[16,896]{1,0:T(8,128)(2,1)S(1)} collective-permute-done((bf16[16,896]{1,0:T(8,128)(2,1)S(1)}, bf16[16,896]{1,0:T(8,128)(2,1)S(1)}, u32[]{:S(2)}, u32[]{:S(2)}) %collective-permute-start.13) | collective-permute-done | bytes 28704 | tf_op jit(solution)/shard_map/ppermute | solution.py:11
  39.8 0.2 collective-permute-done.12
  40.0 2.2 %collective-permute-start.23 = (bf16[16,896]{1,0:T(8,128)(2,1)S(1)}, bf16[16,896]{1,0:T(8,128)(2,1)S(1)}, u32[]{:S(2)}, u32[]{:S(2)}) collective-permute-start(bf16[16,896]{1,0:T(8,128)(2,1)S(1)} %subtract_convert_fusion), channel_id=1, source_target_pairs={{0,6},{1,7},{2,4},{3,5},{4,2},{5,3},{6,0},{7,1},{8,14},{9,15},{10,... | collective-permute-start | bytes 86024 | tf_op jit(solution)/shard_map/ppermute | solution.py:11
  42.2 0.0 collective-permute-start.22
  42.2 2.2 %collective-permute-start.21 = (bf16[16,896]{1,0:T(8,128)(2,1)S(1)}, bf16[16,896]{1,0:T(8,128)(2,1)S(1)}, u32[]{:S(2)}, u32[]{:S(2)}) collective-permute-start(bf16[16,896]{1,0:T(8,128)(2,1)S(1)} %subtract_convert_fusion), channel_id=1, source_target_pairs={{0,2},{1,3},{2,0},{3,1},{4,6},{5,7},{6,4},{7,5},{8,10},{9,11},{10,... | collective-permute-start | bytes 86024 | tf_op jit(solution)/shard_map/ppermute | solution.py:11
  44.5 2.2 %collective-permute-start.20 = (bf16[32,896]{1,0:T(8,128)(2,1)S(1)}, bf16[32,896]{1,0:T(8,128)(2,1)S(1)}, u32[]{:S(2)}, u32[]{:S(2)}) collective-permute-start(bf16[32,896]{1,0:T(8,128)(2,1)S(1)} %fusion.24), channel_id=1, source_target_pairs={{0,6},{1,7},{2,4},{3,5},{4,2},{5,3},{6,0},{7,1},{8,14},{9,15},{10,... | collective-permute-start | bytes 172040 | tf_op jit(solution)/shard_map/ppermute | solution.py:11
  46.7 2.2 %collective-permute-start.18 = (bf16[32,896]{1,0:T(8,128)(2,1)S(1)}, bf16[32,896]{1,0:T(8,128)(2,1)S(1)}, u32[]{:S(2)}, u32[]{:S(2)}) collective-permute-start(bf16[32,896]{1,0:T(8,128)(2,1)S(1)} %fusion.24), channel_id=1, source_target_pairs={{0,2},{1,3},{2,0},{3,1},{4,6},{5,7},{6,4},{7,5},{8,10},{9,11},{10,... | collective-permute-start | bytes 172040 | tf_op jit(solution)/shard_map/ppermute | solution.py:11
  49.0 1.7 %collective-permute-start.24 = (bf16[64,896]{1,0:T(8,128)(2,1)S(1)}, bf16[64,896]{1,0:T(8,128)(2,1)S(1)}, u32[]{:S(2)}, u32[]{:S(2)}) collective-permute-start(bf16[64,896]{1,0:T(8,128)(2,1)S(1)} %pad_maximum_fusion.5), channel_id=1, source_target_pairs={{0,1},{1,0},{2,3},{3,2},{4,5},{5,4},{6,7},{7,6},{8,9},{9,8},{10,11... | collective-permute-start | bytes 344072 | tf_op jit(solution)/shard_map/ppermute | solution.py:11
  50.7 1.2 %collective-permute-start.26 = (bf16[16,896]{1,0:T(8,128)(2,1)S(1)}, bf16[16,896]{1,0:T(8,128)(2,1)S(1)}, u32[]{:S(2)}, u32[]{:S(2)}) collective-permute-start(bf16[16,896]{1,0:T(8,128)(2,1)S(1)} %subtract_convert_fusion), channel_id=1, source_target_pairs={{0,16},{8,24},{16,0},{24,8},{1,17},{9,25},{17,1},{25,9},{2,18},{10... | collective-permute-start | bytes 86024 | tf_op jit(solution)/shard_map/ppermute | solution.py:11
  51.9 0.3 fusion.25
  52.3 1.6 %collective-permute-done.24 = bf16[64,896]{1,0:T(8,128)(2,1)S(1)} collective-permute-done((bf16[64,896]{1,0:T(8,128)(2,1)S(1)}, bf16[64,896]{1,0:T(8,128)(2,1)S(1)}, u32[]{:S(2)}, u32[]{:S(2)}) %collective-permute-start.24) | collective-permute-done | bytes 114720 | tf_op jit(solution)/shard_map/ppermute | solution.py:11
  53.8 0.3 fusion.52
  54.1 0.3 fusion.8
  54.5 0.3 convolution_add_fusion.3
  54.8 0.1 collective-permute-start.25
  54.9 1.7 %collective-permute-start.29 = (bf16[16,896]{1,0:T(8,128)(2,1)S(1)}, bf16[16,896]{1,0:T(8,128)(2,1)S(1)}, u32[]{:S(2)}, u32[]{:S(2)}) collective-permute-start(bf16[16,896]{1,0:T(8,128)(2,1)S(1)} %slice_bitcast_fusion), channel_id=1, source_target_pairs={{0,1},{1,0},{2,3},{3,2},{4,5},{5,4},{6,7},{7,6},{8,9},{9,8},{10,11... | collective-permute-start | bytes 86024 | tf_op jit(solution)/shard_map/ppermute | solution.py:11
  56.7 1.4 %collective-permute-start.30 = (bf16[128,128]{1,0:T(8,128)(2,1)S(1)}, bf16[128,128]{1,0:T(8,128)(2,1)S(1)}, u32[]{:S(2)}, u32[]{:S(2)}) collective-permute-start(bf16[128,128]{1,0:T(8,128)(2,1)S(1)} %get-tuple-element.88), channel_id=1, source_target_pairs={{0,1},{1,0},{2,3},{3,2},{4,5},{5,4},{6,7},{7,6},{8,9},{9,8},{10,11... | collective-permute-start | bytes 98312 | tf_op jit(solution)/shard_map/ppermute | solution.py:11
  58.1 1.2 %collective-permute-start.28 = (bf16[128,128]{1,0:T(8,128)(2,1)S(1)}, bf16[128,128]{1,0:T(8,128)(2,1)S(1)}, u32[]{:S(2)}, u32[]{:S(2)}) collective-permute-start(bf16[128,128]{1,0:T(8,128)(2,1)S(1)} %get-tuple-element.89), channel_id=1, source_target_pairs={{0,16},{8,24},{16,0},{24,8},{1,17},{9,25},{17,1},{25,9},{2,18},{10... | collective-permute-start | bytes 98312 | tf_op jit(solution)/shard_map/ppermute | solution.py:11
  59.4 0.1 broadcast_select_fusion.1
  59.5 2.6 %collective-permute-done.28 = bf16[128,128]{1,0:T(8,128)(2,1)S(1)} collective-permute-done((bf16[128,128]{1,0:T(8,128)(2,1)S(1)}, bf16[128,128]{1,0:T(8,128)(2,1)S(1)}, u32[]{:S(2)}, u32[]{:S(2)}) %collective-permute-start.28) | collective-permute-done | bytes 32800 | tf_op jit(solution)/shard_map/ppermute | solution.py:11
  62.1 0.6 maximum_select_fusion
  62.7 0.5 fusion.27
  63.3 1.4 %fusion = bf16[1,3584,128]{2,1,0:T(8,128)(2,1)} fusion(bf16[128,1792]{1,0:T(8,128)(2,1)S(1)} %get-tuple-element.74, bf16[128,1792]{1,0:T(8,128)(2,1)S(1)} %get-tuple-element.73, bf16[128,128]{1,0:T(8,128)(2,1)S(1)} %collective-permute-done.28, bf16[128,128]{1,0:T(8,128)(2,1)S(1)} %collective-permute-done.30, f32[384,128]{1,0:T(8,128)S(1)} %select_add_fusion, ...), kind=kOutput, calls=%fused_computation.1 | convolution fusion | flops 119832576 | bytes 1966592 | tf_op jit(solution)/shard_map/dot_general | solution.py:44
  (59 shorter events, 0.5 us)
Async XLA Ops:
  0.6 13.1 %copy-start = (s32[2,1,12]{2,1,0:T(1,128)S(1)}, s32[2,1,12]{2,1,0:T(1,128)}, u32[]{:S(2)}) copy-start(s32[2,1,12]{2,1,0:T(1,128)} %param.11) | copy-start | bytes 292
  0.6 11.9 %copy-start.2 = (bf16[1,3584,128]{2,1,0:T(8,128)(2,1)S(1)}, bf16[1,3584,128]{2,1,0:T(8,128)(2,1)}, u32[]{:S(2)}) copy-start(bf16[1,3584,128]{2,1,0:T(8,128)(2,1)} %param.8) | copy-start | bytes 2752516
  0.7 7.4 %collective-permute-start.3 = (bf16[3584,128]{1,0:T(8,128)(2,1)}, bf16[3584,128]{1,0:T(8,128)(2,1)}, u32[]{:S(2)}, u32[]{:S(2)}) collective-permute-start(bf16[3584,128]{1,0:T(8,128)(2,1)} %bitcast.112), channel_id=1, source_target_pairs={{0,8},{8,0},{16,24},{24,16},{1,9},{9,1},{17,25},{25,17},{2,10},{10... | collective-permute-start | bytes 2752520 | tf_op jit(solution)/shard_map/ppermute | solution.py:11
  2.0 6.0 %collective-permute-start.2 = (bf16[16,1792]{1,0:T(8,128)(2,1)S(1)}, bf16[16,1792]{1,0:T(8,128)(2,1)S(1)}, u32[]{:S(2)}, u32[]{:S(2)}) collective-permute-start(bf16[16,1792]{1,0:T(8,128)(2,1)S(1)} %get-tuple-element.82), channel_id=1, source_target_pairs={{0,1},{1,0},{2,3},{3,2},{4,5},{5,4},{6,7},{7,6},{8,9},{9,8},{10,11... | collective-permute-start | bytes 172040 | tf_op jit(solution)/shard_map/ppermute | solution.py:11
  4.6 9.1 %copy-start.3 = (f32[1,128]{1,0:T(1,128)S(1)}, f32[1,128]{1,0:T(1,128)}, u32[]{:S(2)}) copy-start(f32[1,128]{1,0:T(1,128)} %param.9) | copy-start | bytes 1540
  5.9 12.6 %collective-permute-start.1 = (bf16[256,896]{1,0:T(8,128)(2,1)S(1)}, bf16[256,896]{1,0:T(8,128)(2,1)S(1)}, u32[]{:S(2)}, u32[]{:S(2)}) collective-permute-start(bf16[256,896]{1,0:T(8,128)(2,1)S(1)} %get-tuple-element.71), channel_id=1, source_target_pairs={{0,16},{8,24},{16,0},{24,8},{1,17},{9,25},{17,1},{25,9},{2,18},{10... | collective-permute-start | bytes 1376264 | tf_op jit(solution)/shard_map/ppermute | solution.py:11
  7.5 12.2 %collective-permute-start = (bf16[256,896]{1,0:T(8,128)(2,1)S(1)}, bf16[256,896]{1,0:T(8,128)(2,1)S(1)}, u32[]{:S(2)}, u32[]{:S(2)}) collective-permute-start(bf16[256,896]{1,0:T(8,128)(2,1)S(1)} %get-tuple-element.72), channel_id=1, source_target_pairs={{0,1},{1,0},{2,3},{3,2},{4,5},{5,4},{6,7},{7,6},{8,9},{9,8},{10,11... | collective-permute-start | bytes 1376264 | tf_op jit(solution)/shard_map/ppermute | solution.py:11
  8.0 11.7 %collective-permute-start.6 = (bf16[32,1792]{1,0:T(8,128)(2,1)S(1)}, bf16[32,1792]{1,0:T(8,128)(2,1)S(1)}, u32[]{:S(2)}, u32[]{:S(2)}) collective-permute-start(bf16[32,1792]{1,0:T(8,128)(2,1)S(1)} %bitcast.103), channel_id=1, source_target_pairs={{0,6},{1,7},{2,4},{3,5},{4,2},{5,3},{6,0},{7,1},{8,14},{9,15},{10,... | collective-permute-start | bytes 344072 | tf_op jit(solution)/shard_map/ppermute | solution.py:11
  11.7 9.4 %collective-permute-start.5 = (bf16[32,1792]{1,0:T(8,128)(2,1)S(1)}, bf16[32,1792]{1,0:T(8,128)(2,1)S(1)}, u32[]{:S(2)}, u32[]{:S(2)}) collective-permute-start(bf16[32,1792]{1,0:T(8,128)(2,1)S(1)} %bitcast.104), channel_id=1, source_target_pairs={{0,4},{1,5},{2,6},{3,7},{4,0},{5,1},{6,2},{7,3},{8,12},{9,13},{10,... | collective-permute-start | bytes 344072 | tf_op jit(solution)/shard_map/ppermute | solution.py:11
  11.7 9.4 %collective-permute-start.4 = (bf16[32,1792]{1,0:T(8,128)(2,1)S(1)}, bf16[32,1792]{1,0:T(8,128)(2,1)S(1)}, u32[]{:S(2)}, u32[]{:S(2)}) collective-permute-start(bf16[32,1792]{1,0:T(8,128)(2,1)S(1)} %bitcast.105), channel_id=1, source_target_pairs={{0,2},{1,3},{2,0},{3,1},{4,6},{5,7},{6,4},{7,5},{8,10},{9,11},{10,... | collective-permute-start | bytes 344072 | tf_op jit(solution)/shard_map/ppermute | solution.py:11
  13.9 12.9 %copy-start.1 = (bf16[1,2,2,128,1792]{4,3,2,1,0:T(8,128)(2,1)S(1)}, bf16[1,2,2,128,1792]{4,3,2,1,0:T(8,128)(2,1)}, u32[]{:S(2)}) copy-start(bf16[1,2,2,128,1792]{4,3,2,1,0:T(8,128)(2,1)} %param.10) | copy-start | bytes 5505028
  21.4 1.4 %collective-permute-start.7 = (f32[128,256]{1,0:T(8,128)S(1)}, f32[128,256]{1,0:T(8,128)S(1)}, u32[]{:S(2)}, u32[]{:S(2)}) collective-permute-start(f32[128,256]{1,0:T(8,128)S(1)} %convolution_add_fusion.4), channel_id=1, source_target_pairs={{0,8},{8,0},{16,24},{24,16},{1,9},{9,1},{17,25},{25,17},{2,10},{10... | collective-permute-start | bytes 393224 | tf_op jit(solution)/shard_map/ppermute | solution.py:11
  22.9 4.3 %collective-permute-start.9 = (bf16[128,256]{1,0:T(8,128)(2,1)S(1)}, bf16[128,256]{1,0:T(8,128)(2,1)S(1)}, u32[]{:S(2)}, u32[]{:S(2)}) collective-permute-start(bf16[128,256]{1,0:T(8,128)(2,1)S(1)} %multiply_convert_fusion), channel_id=1, source_target_pairs={{0,16},{8,24},{16,0},{24,8},{1,17},{9,25},{17,1},{25,9},{2,18},{10... | collective-permute-start | bytes 196616 | tf_op jit(solution)/shard_map/ppermute | solution.py:11
  23.8 5.2 %collective-permute-start.8 = (bf16[128,256]{1,0:T(8,128)(2,1)S(1)}, bf16[128,256]{1,0:T(8,128)(2,1)S(1)}, u32[]{:S(2)}, u32[]{:S(2)}) collective-permute-start(bf16[128,256]{1,0:T(8,128)(2,1)S(1)} %bitcast.118), channel_id=1, source_target_pairs={{0,1},{1,0},{2,3},{3,2},{4,5},{5,4},{6,7},{7,6},{8,9},{9,8},{10,11... | collective-permute-start | bytes 196616 | tf_op jit(solution)/shard_map/ppermute | solution.py:11
  26.2 9.6 %collective-permute-start.17 = (bf16[16,896]{1,0:T(8,128)(2,1)S(1)}, bf16[16,896]{1,0:T(8,128)(2,1)S(1)}, u32[]{:S(2)}, u32[]{:S(2)}) collective-permute-start(bf16[16,896]{1,0:T(8,128)(2,1)S(1)} %get-tuple-element.75), channel_id=1, source_target_pairs={{0,1},{1,0},{2,3},{3,2},{4,5},{5,4},{6,7},{7,6},{8,9},{9,8},{10,11... | collective-permute-start | bytes 86024 | tf_op jit(solution)/shard_map/ppermute | solution.py:11
  27.4 4.9 %collective-permute-start.10 = (bf16[64,896]{1,0:T(8,128)(2,1)S(1)}, bf16[64,896]{1,0:T(8,128)(2,1)S(1)}, u32[]{:S(2)}, u32[]{:S(2)}) collective-permute-start(bf16[64,896]{1,0:T(8,128)(2,1)S(1)} %fusion.1), channel_id=1, source_target_pairs={{0,1},{1,0},{2,3},{3,2},{4,5},{5,4},{6,7},{7,6},{8,9},{9,8},{10,11... | collective-permute-start | bytes 344072 | tf_op jit(solution)/shard_map/ppermute | solution.py:11
  29.5 7.3 %collective-permute-start.16 = (bf16[32,896]{1,0:T(8,128)(2,1)S(1)}, bf16[32,896]{1,0:T(8,128)(2,1)S(1)}, u32[]{:S(2)}, u32[]{:S(2)}) collective-permute-start(bf16[32,896]{1,0:T(8,128)(2,1)S(1)} %get-tuple-element.78), channel_id=1, source_target_pairs={{0,6},{1,7},{2,4},{3,5},{4,2},{5,3},{6,0},{7,1},{8,14},{9,15},{10,... | collective-permute-start | bytes 172040 | tf_op jit(solution)/shard_map/ppermute | solution.py:11
  32.0 6.5 %collective-permute-start.15 = (bf16[32,896]{1,0:T(8,128)(2,1)S(1)}, bf16[32,896]{1,0:T(8,128)(2,1)S(1)}, u32[]{:S(2)}, u32[]{:S(2)}) collective-permute-start(bf16[32,896]{1,0:T(8,128)(2,1)S(1)} %get-tuple-element.79), channel_id=1, source_target_pairs={{0,4},{1,5},{2,6},{3,7},{4,0},{5,1},{6,2},{7,3},{8,12},{9,13},{10,... | collective-permute-start | bytes 172040 | tf_op jit(solution)/shard_map/ppermute | solution.py:11
  32.4 6.2 %collective-permute-start.14 = (bf16[16,896]{1,0:T(8,128)(2,1)S(1)}, bf16[16,896]{1,0:T(8,128)(2,1)S(1)}, u32[]{:S(2)}, u32[]{:S(2)}) collective-permute-start(bf16[16,896]{1,0:T(8,128)(2,1)S(1)} %get-tuple-element.85), channel_id=1, source_target_pairs={{0,6},{1,7},{2,4},{3,5},{4,2},{5,3},{6,0},{7,1},{8,14},{9,15},{10,... | collective-permute-start | bytes 86024 | tf_op jit(solution)/shard_map/ppermute | solution.py:11
  34.9 4.9 %collective-permute-start.13 = (bf16[16,896]{1,0:T(8,128)(2,1)S(1)}, bf16[16,896]{1,0:T(8,128)(2,1)S(1)}, u32[]{:S(2)}, u32[]{:S(2)}) collective-permute-start(bf16[16,896]{1,0:T(8,128)(2,1)S(1)} %get-tuple-element.86), channel_id=1, source_target_pairs={{0,4},{1,5},{2,6},{3,7},{4,0},{5,1},{6,2},{7,3},{8,12},{9,13},{10,... | collective-permute-start | bytes 86024 | tf_op jit(solution)/shard_map/ppermute | solution.py:11
  35.8 4.2 %collective-permute-start.12 = (bf16[16,896]{1,0:T(8,128)(2,1)S(1)}, bf16[16,896]{1,0:T(8,128)(2,1)S(1)}, u32[]{:S(2)}, u32[]{:S(2)}) collective-permute-start(bf16[16,896]{1,0:T(8,128)(2,1)S(1)} %get-tuple-element.87), channel_id=1, source_target_pairs={{0,2},{1,3},{2,0},{3,1},{4,6},{5,7},{6,4},{7,5},{8,10},{9,11},{10,... | collective-permute-start | bytes 86024 | tf_op jit(solution)/shard_map/ppermute | solution.py:11
  36.9 7.6 %collective-permute-start.11 = (bf16[32,896]{1,0:T(8,128)(2,1)S(1)}, bf16[32,896]{1,0:T(8,128)(2,1)S(1)}, u32[]{:S(2)}, u32[]{:S(2)}) collective-permute-start(bf16[32,896]{1,0:T(8,128)(2,1)S(1)} %get-tuple-element.46), channel_id=1, source_target_pairs={{0,2},{1,3},{2,0},{3,1},{4,6},{5,7},{6,4},{7,5},{8,10},{9,11},{10,... | collective-permute-start | bytes 172040 | tf_op jit(solution)/shard_map/ppermute | solution.py:11
  40.0 6.7 %collective-permute-start.23 = (bf16[16,896]{1,0:T(8,128)(2,1)S(1)}, bf16[16,896]{1,0:T(8,128)(2,1)S(1)}, u32[]{:S(2)}, u32[]{:S(2)}) collective-permute-start(bf16[16,896]{1,0:T(8,128)(2,1)S(1)} %subtract_convert_fusion), channel_id=1, source_target_pairs={{0,6},{1,7},{2,4},{3,5},{4,2},{5,3},{6,0},{7,1},{8,14},{9,15},{10,... | collective-permute-start | bytes 86024 | tf_op jit(solution)/shard_map/ppermute | solution.py:11
  42.2 6.7 %collective-permute-start.22 = (bf16[16,896]{1,0:T(8,128)(2,1)S(1)}, bf16[16,896]{1,0:T(8,128)(2,1)S(1)}, u32[]{:S(2)}, u32[]{:S(2)}) collective-permute-start(bf16[16,896]{1,0:T(8,128)(2,1)S(1)} %subtract_convert_fusion), channel_id=1, source_target_pairs={{0,4},{1,5},{2,6},{3,7},{4,0},{5,1},{6,2},{7,3},{8,12},{9,13},{10,... | collective-permute-start | bytes 86024 | tf_op jit(solution)/shard_map/ppermute | solution.py:11
  42.2 6.7 %collective-permute-start.21 = (bf16[16,896]{1,0:T(8,128)(2,1)S(1)}, bf16[16,896]{1,0:T(8,128)(2,1)S(1)}, u32[]{:S(2)}, u32[]{:S(2)}) collective-permute-start(bf16[16,896]{1,0:T(8,128)(2,1)S(1)} %subtract_convert_fusion), channel_id=1, source_target_pairs={{0,2},{1,3},{2,0},{3,1},{4,6},{5,7},{6,4},{7,5},{8,10},{9,11},{10,... | collective-permute-start | bytes 86024 | tf_op jit(solution)/shard_map/ppermute | solution.py:11
  44.5 7.4 %collective-permute-start.20 = (bf16[32,896]{1,0:T(8,128)(2,1)S(1)}, bf16[32,896]{1,0:T(8,128)(2,1)S(1)}, u32[]{:S(2)}, u32[]{:S(2)}) collective-permute-start(bf16[32,896]{1,0:T(8,128)(2,1)S(1)} %fusion.24), channel_id=1, source_target_pairs={{0,6},{1,7},{2,4},{3,5},{4,2},{5,3},{6,0},{7,1},{8,14},{9,15},{10,... | collective-permute-start | bytes 172040 | tf_op jit(solution)/shard_map/ppermute | solution.py:11
  46.7 5.2 %collective-permute-start.19 = (bf16[32,896]{1,0:T(8,128)(2,1)S(1)}, bf16[32,896]{1,0:T(8,128)(2,1)S(1)}, u32[]{:S(2)}, u32[]{:S(2)}) collective-permute-start(bf16[32,896]{1,0:T(8,128)(2,1)S(1)} %fusion.24), channel_id=1, source_target_pairs={{0,4},{1,5},{2,6},{3,7},{4,0},{5,1},{6,2},{7,3},{8,12},{9,13},{10,... | collective-permute-start | bytes 172040 | tf_op jit(solution)/shard_map/ppermute | solution.py:11
  46.7 5.2 %collective-permute-start.18 = (bf16[32,896]{1,0:T(8,128)(2,1)S(1)}, bf16[32,896]{1,0:T(8,128)(2,1)S(1)}, u32[]{:S(2)}, u32[]{:S(2)}) collective-permute-start(bf16[32,896]{1,0:T(8,128)(2,1)S(1)} %fusion.24), channel_id=1, source_target_pairs={{0,2},{1,3},{2,0},{3,1},{4,6},{5,7},{6,4},{7,5},{8,10},{9,11},{10,... | collective-permute-start | bytes 172040 | tf_op jit(solution)/shard_map/ppermute | solution.py:11
  49.0 4.9 %collective-permute-start.24 = (bf16[64,896]{1,0:T(8,128)(2,1)S(1)}, bf16[64,896]{1,0:T(8,128)(2,1)S(1)}, u32[]{:S(2)}, u32[]{:S(2)}) collective-permute-start(bf16[64,896]{1,0:T(8,128)(2,1)S(1)} %pad_maximum_fusion.5), channel_id=1, source_target_pairs={{0,1},{1,0},{2,3},{3,2},{4,5},{5,4},{6,7},{7,6},{8,9},{9,8},{10,11... | collective-permute-start | bytes 344072 | tf_op jit(solution)/shard_map/ppermute | solution.py:11
  50.7 6.0 %collective-permute-start.26 = (bf16[16,896]{1,0:T(8,128)(2,1)S(1)}, bf16[16,896]{1,0:T(8,128)(2,1)S(1)}, u32[]{:S(2)}, u32[]{:S(2)}) collective-permute-start(bf16[16,896]{1,0:T(8,128)(2,1)S(1)} %subtract_convert_fusion), channel_id=1, source_target_pairs={{0,16},{8,24},{16,0},{24,8},{1,17},{9,25},{17,1},{25,9},{2,18},{10... | collective-permute-start | bytes 86024 | tf_op jit(solution)/shard_map/ppermute | solution.py:11
  51.9 4.8 %collective-permute-start.27 = (bf16[128,1792]{1,0:T(8,128)(2,1)S(1)}, bf16[128,1792]{1,0:T(8,128)(2,1)S(1)}, u32[]{:S(2)}, u32[]{:S(2)}) collective-permute-start(bf16[128,1792]{1,0:T(8,128)(2,1)S(1)} %constant_dynamic-update-slice_fusion), channel_id=1, source_target_pairs={{0,8},{8,0},{16,24},{24,16},{1,9},{9,1},{17,25},{25,17},{2,10},{10... | collective-permute-start | bytes 1376264 | tf_op jit(solution)/shard_map/ppermute | solution.py:11
  54.8 1.8 %collective-permute-start.25 = (f32[384,128]{1,0:T(8,128)S(1)}, f32[384,128]{1,0:T(8,128)S(1)}, u32[]{:S(2)}, u32[]{:S(2)}) collective-permute-start(f32[384,128]{1,0:T(8,128)S(1)} %slice_select_fusion), channel_id=1, source_target_pairs={{0,8},{8,0},{16,24},{24,16},{1,9},{9,1},{17,25},{25,17},{2,10},{10... | collective-permute-start | bytes 589832 | tf_op jit(solution)/shard_map/ppermute | solution.py:11
  54.9 4.6 %collective-permute-start.29 = (bf16[16,896]{1,0:T(8,128)(2,1)S(1)}, bf16[16,896]{1,0:T(8,128)(2,1)S(1)}, u32[]{:S(2)}, u32[]{:S(2)}) collective-permute-start(bf16[16,896]{1,0:T(8,128)(2,1)S(1)} %slice_bitcast_fusion), channel_id=1, source_target_pairs={{0,1},{1,0},{2,3},{3,2},{4,5},{5,4},{6,7},{7,6},{8,9},{9,8},{10,11... | collective-permute-start | bytes 86024 | tf_op jit(solution)/shard_map/ppermute | solution.py:11
  56.7 6.0 %collective-permute-start.30 = (bf16[128,128]{1,0:T(8,128)(2,1)S(1)}, bf16[128,128]{1,0:T(8,128)(2,1)S(1)}, u32[]{:S(2)}, u32[]{:S(2)}) collective-permute-start(bf16[128,128]{1,0:T(8,128)(2,1)S(1)} %get-tuple-element.88), channel_id=1, source_target_pairs={{0,1},{1,0},{2,3},{3,2},{4,5},{5,4},{6,7},{7,6},{8,9},{9,8},{10,11... | collective-permute-start | bytes 98312 | tf_op jit(solution)/shard_map/ppermute | solution.py:11
  58.1 3.9 %collective-permute-start.28 = (bf16[128,128]{1,0:T(8,128)(2,1)S(1)}, bf16[128,128]{1,0:T(8,128)(2,1)S(1)}, u32[]{:S(2)}, u32[]{:S(2)}) collective-permute-start(bf16[128,128]{1,0:T(8,128)(2,1)S(1)} %get-tuple-element.89), channel_id=1, source_target_pairs={{0,16},{8,24},{16,0},{24,8},{1,17},{9,25},{17,1},{25,9},{2,18},{10... | collective-permute-start | bytes 98312 | tf_op jit(solution)/shard_map/ppermute | solution.py:11

commit v20 on v19

--- a/solution.py
+++ b/solution.py
@@ -150,10 +150,11 @@
     errs_shared = paired(shared_near, over_x(shared_near))
     errs_own = jnp.concatenate(own_column, axis=0)
 
+    own_grads = hold([times_transposed(errs_own, weights) for weights in (own_mine, own_other)])
     grads = jnp.concatenate(
         [
-            times_transposed(errs_own, own_mine) + times_transposed(errs_shared, shared_mine),
-            turned(times_transposed(errs_own, own_other)),
+            own_grads[0] + times_transposed(errs_shared, shared_mine),
+            turned(own_grads[1]),
             times_transposed(errs_shared, shared_other),
         ],
         axis=0,

time: 64.9 us -> 64.6 us (level)
  no operation moved by 1% of the time
where the time goes in v20:
time: 64.6 us; the launch traced here: 64.3 us
  starting transfers between devices  38.7 us (60%)
  waiting for transfers between devices  14.5 us (22%)
  matrix products  4.16 us (6%)
  local copies, waits for them, and re-layouts  2.99 us (5%)
  other arithmetic  2.94 us (5%)
  between operations  1.03 us (2%)
    ppermute x31, starting transfers between devices, crossed(): lax.ppermute(block, axis, [(i, i ^ mask) for i in range(lax.axis_size(axi...  38.7 us
    ppermute x31, waiting for transfers between devices, crossed(): lax.ppermute(block, axis, [(i, i ^ mask) for i in range(lax.axis_size(axi...  14.5 us
    dot_general x7, matrix products, times(): return jnp.dot(left, right, preferred_element_type=F32)  1.6 us
    dot_general x1, matrix products, encoder_gradient(): lax.dot_general(whole, grad_low, (((0,), (0,)), ((), ())), preferred_elem...  1.36 us
    select_n x3, other arithmetic, both_halves(): jnp.where(half == 0, mine, other)  1.32 us
  transfers between devices with their start and end apart: 31, of which 9 were waited for; matrix products, arithmetic and copies ran while one was open for 12% of the time, Pallas kernels for 0%

profile of v20, /device:TPU:0, one launch (start us, length us, event | category | flops | bytes accessed | tf_op | source)
XLA Modules:
  0.0 64.3 jit_solution(13163394727968146470)
XLA Ops:
  0.6 0.0 copy-start
  0.7 0.5 collective-permute-start.3
  1.2 0.8 %dynamic-slice_bitcast_fusion.3 = (bf16[1,1,16,1792]{3,2,1,0:T(8,128)(2,1)S(1)}, bf16[16,1792]{1,0:T(8,128)(2,1)S(1)}) fusion(bf16[2,16,3584]{2,1,0:T(8,128)(2,1)} %param.6, s32[]{:T(128)S(6)} %select_n.168, s32[]{:T(128)S(6)} %select_n.173), kind=kLoop, calls=%fused_computation.54 | loop fusion | bytes 172040 | tf_op jit(solution)/shard_map/reshape;squeeze | solution.py:100
  2.0 2.6 %collective-permute-start.2 = (bf16[16,1792]{1,0:T(8,128)(2,1)S(1)}, bf16[16,1792]{1,0:T(8,128)(2,1)S(1)}, u32[]{:S(2)}, u32[]{:S(2)}) collective-permute-start(bf16[16,1792]{1,0:T(8,128)(2,1)S(1)} %get-tuple-element.86), channel_id=1, source_target_pairs={{0,1},{1,0},{2,3},{3,2},{4,5},{5,4},{6,7},{7,6},{8,9},{9,8},{10,11... | collective-permute-start | bytes 172040 | tf_op jit(solution)/shard_map/ppermute | solution.py:11
  4.6 1.2 %dynamic-slice_bitcast_fusion = (bf16[256,896]{1,0:T(8,128)(2,1)S(1)}, bf16[256,896]{1,0:T(8,128)(2,1)S(1)}) fusion(bf16[2,256,1792]{2,1,0:T(8,128)(2,1)} %bitcast.92, s32[]{:T(128)S(6)} %select_n.170, s32[]{:T(128)S(6)} %select_n.171, s32[]{:T(128)S(6)} %select_n.168, s32[]{:T(128)S(6)} %select_n.169), kind=kLoop, calls=%fused_computation.24 | loop fusion | bytes 1835024 | tf_op jit(solution)/shard_map/squeeze | solution.py:91
  5.9 1.6 %collective-permute-start.1 = (bf16[256,896]{1,0:T(8,128)(2,1)S(1)}, bf16[256,896]{1,0:T(8,128)(2,1)S(1)}, u32[]{:S(2)}, u32[]{:S(2)}) collective-permute-start(bf16[256,896]{1,0:T(8,128)(2,1)S(1)} %get-tuple-element.75), channel_id=1, source_target_pairs={{0,16},{8,24},{16,0},{24,8},{1,17},{9,25},{17,1},{25,9},{2,18},{10... | collective-permute-start | bytes 1376264 | tf_op jit(solution)/shard_map/ppermute | solution.py:11
  7.5 0.5 collective-permute-start
  8.0 0.0 collective-permute-done.2
  8.0 3.7 %collective-permute-start.6 = (bf16[32,1792]{1,0:T(8,128)(2,1)S(1)}, bf16[32,1792]{1,0:T(8,128)(2,1)S(1)}, u32[]{:S(2)}, u32[]{:S(2)}) collective-permute-start(bf16[32,1792]{1,0:T(8,128)(2,1)S(1)} %bitcast.103), channel_id=1, source_target_pairs={{0,6},{1,7},{2,4},{3,5},{4,2},{5,3},{6,0},{7,1},{8,14},{9,15},{10,... | collective-permute-start | bytes 344072 | tf_op jit(solution)/shard_map/ppermute | solution.py:11
  11.7 0.8 %collective-permute-start.4 = (bf16[32,1792]{1,0:T(8,128)(2,1)S(1)}, bf16[32,1792]{1,0:T(8,128)(2,1)S(1)}, u32[]{:S(2)}, u32[]{:S(2)}) collective-permute-start(bf16[32,1792]{1,0:T(8,128)(2,1)S(1)} %bitcast.105), channel_id=1, source_target_pairs={{0,2},{1,3},{2,0},{3,1},{4,6},{5,7},{6,4},{7,5},{8,10},{9,11},{10,... | collective-permute-start | bytes 344072 | tf_op jit(solution)/shard_map/ppermute | solution.py:11
  12.5 1.2 %bitcast_select_fusion.1 = (bf16[1792,128]{1,0:T(8,128)(2,1)S(1)}, bf16[1792,128]{1,0:T(8,128)(2,1)S(1)}) fusion(pred[]{:T(512)S(6)} %eq.48, bf16[3584,128]{1,0:T(8,128)(2,1)} %collective-permute-done.3, s32[]{:T(128)S(6)} %select_n.173, bf16[1,3584,128]{2,1,0:T(8,128)(2,1)S(1)} %copy-done.2), kind=kLoop, calls=%fused_computation.23 | loop fusion | flops 458752 | bytes 1835013 | tf_op jit(solution)/shard_map/jit(_where)/select_n | solution.py:23
  13.8 0.1 compare_reduce_fusion
  13.9 0.0 copy-start.1
  13.9 4.6 %collective-permute-done.1 = bf16[256,896]{1,0:T(8,128)(2,1)S(1)} collective-permute-done((bf16[256,896]{1,0:T(8,128)(2,1)S(1)}, bf16[256,896]{1,0:T(8,128)(2,1)S(1)}, u32[]{:S(2)}, u32[]{:S(2)}) %collective-permute-start.1) | collective-permute-done | bytes 458784 | tf_op jit(solution)/shard_map/ppermute | solution.py:11
  18.5 1.2 %collective-permute-done = bf16[256,896]{1,0:T(8,128)(2,1)S(1)} collective-permute-done((bf16[256,896]{1,0:T(8,128)(2,1)S(1)}, bf16[256,896]{1,0:T(8,128)(2,1)S(1)}, u32[]{:S(2)}, u32[]{:S(2)}) %collective-permute-start) | collective-permute-done | bytes 458784 | tf_op jit(solution)/shard_map/ppermute | solution.py:11
  19.7 1.4 %collective-permute-done.5 = bf16[32,1792]{1,0:T(8,128)(2,1)S(1)} collective-permute-done((bf16[32,1792]{1,0:T(8,128)(2,1)S(1)}, bf16[32,1792]{1,0:T(8,128)(2,1)S(1)}, u32[]{:S(2)}, u32[]{:S(2)}) %collective-permute-start.5) | collective-permute-done | bytes 114720 | tf_op jit(solution)/shard_map/ppermute | solution.py:11
  21.1 0.3 convolution_add_fusion.4
  21.4 0.1 collective-permute-start.7
  21.5 1.3 %collective-permute-done.7 = f32[128,256]{1,0:T(8,128)S(1)} collective-permute-done((f32[128,256]{1,0:T(8,128)S(1)}, f32[128,256]{1,0:T(8,128)S(1)}, u32[]{:S(2)}, u32[]{:S(2)}) %collective-permute-start.7) | collective-permute-done | bytes 131104 | tf_op jit(solution)/shard_map/ppermute | solution.py:11
  22.9 0.9 %collective-permute-start.9 = (bf16[128,256]{1,0:T(8,128)(2,1)S(1)}, bf16[128,256]{1,0:T(8,128)(2,1)S(1)}, u32[]{:S(2)}, u32[]{:S(2)}) collective-permute-start(bf16[128,256]{1,0:T(8,128)(2,1)S(1)} %multiply_convert_fusion), channel_id=1, source_target_pairs={{0,16},{8,24},{16,0},{24,8},{1,17},{9,25},{17,1},{25,9},{2,18},{10... | collective-permute-start | bytes 196616 | tf_op jit(solution)/shard_map/ppermute | solution.py:11
  23.8 1.6 %collective-permute-start.8 = (bf16[128,256]{1,0:T(8,128)(2,1)S(1)}, bf16[128,256]{1,0:T(8,128)(2,1)S(1)}, u32[]{:S(2)}, u32[]{:S(2)}) collective-permute-start(bf16[128,256]{1,0:T(8,128)(2,1)S(1)} %bitcast.118), channel_id=1, source_target_pairs={{0,1},{1,0},{2,3},{3,2},{4,5},{5,4},{6,7},{7,6},{8,9},{9,8},{10,11... | collective-permute-start | bytes 196616 | tf_op jit(solution)/shard_map/ppermute | solution.py:11
  25.4 0.8 %dynamic-slice_bitcast_fusion.4 = (bf16[16,896]{1,0:T(8,128)(2,1)S(1)}, bf16[16,896]{1,0:T(8,128)(2,1)S(1)}, bf16[16,896]{1,0:T(8,128)(2,1)S(1)}) fusion(bf16[3,16,3584]{2,1,0:T(8,128)(2,1)} %param.7, s32[]{:T(128)S(6)} %select_n.185, s32[]{:T(128)S(6)} %select_n.188, s32[]{:T(128)S(6)} %select_n.187, s32[]{:T(128)S(6)} %select_n.186), kind=kLoop, calls=%fused_computation.61 | loop fusion | bytes 172048 | tf_op jit(solution)/shard_map/squeeze | solution.py:127
  26.2 0.6 collective-permute-start.17
  26.8 0.2 fusion.9
  27.0 0.2 fusion.11
  27.2 0.0 collective-permute-done.9
  27.2 0.2 fusion.1
  27.4 1.5 %collective-permute-start.10 = (bf16[64,896]{1,0:T(8,128)(2,1)S(1)}, bf16[64,896]{1,0:T(8,128)(2,1)S(1)}, u32[]{:S(2)}, u32[]{:S(2)}) collective-permute-start(bf16[64,896]{1,0:T(8,128)(2,1)S(1)} %fusion.1), channel_id=1, source_target_pairs={{0,1},{1,0},{2,3},{3,2},{4,5},{5,4},{6,7},{7,6},{8,9},{9,8},{10,11... | collective-permute-start | bytes 344072 | tf_op jit(solution)/shard_map/ppermute | solution.py:11
  29.0 0.0 collective-permute-done.8
  29.0 0.2 fusion.51
  29.2 0.2 fusion.50
  29.5 2.5 %collective-permute-start.16 = (bf16[32,896]{1,0:T(8,128)(2,1)S(1)}, bf16[32,896]{1,0:T(8,128)(2,1)S(1)}, u32[]{:S(2)}, u32[]{:S(2)}) collective-permute-start(bf16[32,896]{1,0:T(8,128)(2,1)S(1)} %get-tuple-element.82), channel_id=1, source_target_pairs={{0,6},{1,7},{2,4},{3,5},{4,2},{5,3},{6,0},{7,1},{8,14},{9,15},{10,... | collective-permute-start | bytes 172040 | tf_op jit(solution)/shard_map/ppermute | solution.py:11
  32.0 0.0 collective-permute-start.15
  32.0 0.2 convolution_add_fusion.1
  32.3 0.0 collective-permute-done.10
  32.4 2.5 %collective-permute-start.14 = (bf16[16,896]{1,0:T(8,128)(2,1)S(1)}, bf16[16,896]{1,0:T(8,128)(2,1)S(1)}, u32[]{:S(2)}, u32[]{:S(2)}) collective-permute-start(bf16[16,896]{1,0:T(8,128)(2,1)S(1)} %get-tuple-element.89), channel_id=1, source_target_pairs={{0,6},{1,7},{2,4},{3,5},{4,2},{5,3},{6,0},{7,1},{8,14},{9,15},{10,... | collective-permute-start | bytes 86024 | tf_op jit(solution)/shard_map/ppermute | solution.py:11
  34.9 0.9 %collective-permute-start.13 = (bf16[16,896]{1,0:T(8,128)(2,1)S(1)}, bf16[16,896]{1,0:T(8,128)(2,1)S(1)}, u32[]{:S(2)}, u32[]{:S(2)}) collective-permute-start(bf16[16,896]{1,0:T(8,128)(2,1)S(1)} %get-tuple-element.90), channel_id=1, source_target_pairs={{0,4},{1,5},{2,6},{3,7},{4,0},{5,1},{6,2},{7,3},{8,12},{9,13},{10,... | collective-permute-start | bytes 86024 | tf_op jit(solution)/shard_map/ppermute | solution.py:11
  35.8 1.0 %collective-permute-start.12 = (bf16[16,896]{1,0:T(8,128)(2,1)S(1)}, bf16[16,896]{1,0:T(8,128)(2,1)S(1)}, u32[]{:S(2)}, u32[]{:S(2)}) collective-permute-start(bf16[16,896]{1,0:T(8,128)(2,1)S(1)} %get-tuple-element.91), channel_id=1, source_target_pairs={{0,2},{1,3},{2,0},{3,1},{4,6},{5,7},{6,4},{7,5},{8,10},{9,11},{10,... | collective-permute-start | bytes 86024 | tf_op jit(solution)/shard_map/ppermute | solution.py:11
  36.8 0.0 collective-permute-done.16
  36.9 1.0 %collective-permute-start.11 = (bf16[32,896]{1,0:T(8,128)(2,1)S(1)}, bf16[32,896]{1,0:T(8,128)(2,1)S(1)}, u32[]{:S(2)}, u32[]{:S(2)}) collective-permute-start(bf16[32,896]{1,0:T(8,128)(2,1)S(1)} %get-tuple-element.48), channel_id=1, source_target_pairs={{0,2},{1,3},{2,0},{3,1},{4,6},{5,7},{6,4},{7,5},{8,10},{9,11},{10,... | collective-permute-start | bytes 172040 | tf_op jit(solution)/shard_map/ppermute | solution.py:11
  37.9 0.6 collective-permute-done.15
  38.5 1.2 %collective-permute-done.13 = bf16[16,896]{1,0:T(8,128)(2,1)S(1)} collective-permute-done((bf16[16,896]{1,0:T(8,128)(2,1)S(1)}, bf16[16,896]{1,0:T(8,128)(2,1)S(1)}, u32[]{:S(2)}, u32[]{:S(2)}) %collective-permute-start.13) | collective-permute-done | bytes 28704 | tf_op jit(solution)/shard_map/ppermute | solution.py:11
  39.8 0.2 collective-permute-done.12
  40.0 2.2 %collective-permute-start.23 = (bf16[16,896]{1,0:T(8,128)(2,1)S(1)}, bf16[16,896]{1,0:T(8,128)(2,1)S(1)}, u32[]{:S(2)}, u32[]{:S(2)}) collective-permute-start(bf16[16,896]{1,0:T(8,128)(2,1)S(1)} %subtract_convert_fusion), channel_id=1, source_target_pairs={{0,6},{1,7},{2,4},{3,5},{4,2},{5,3},{6,0},{7,1},{8,14},{9,15},{10,... | collective-permute-start | bytes 86024 | tf_op jit(solution)/shard_map/ppermute | solution.py:11
  42.2 0.0 collective-permute-start.22
  42.2 2.2 %collective-permute-start.21 = (bf16[16,896]{1,0:T(8,128)(2,1)S(1)}, bf16[16,896]{1,0:T(8,128)(2,1)S(1)}, u32[]{:S(2)}, u32[]{:S(2)}) collective-permute-start(bf16[16,896]{1,0:T(8,128)(2,1)S(1)} %subtract_convert_fusion), channel_id=1, source_target_pairs={{0,2},{1,3},{2,0},{3,1},{4,6},{5,7},{6,4},{7,5},{8,10},{9,11},{10,... | collective-permute-start | bytes 86024 | tf_op jit(solution)/shard_map/ppermute | solution.py:11
  44.5 2.2 %collective-permute-start.20 = (bf16[32,896]{1,0:T(8,128)(2,1)S(1)}, bf16[32,896]{1,0:T(8,128)(2,1)S(1)}, u32[]{:S(2)}, u32[]{:S(2)}) collective-permute-start(bf16[32,896]{1,0:T(8,128)(2,1)S(1)} %fusion.24), channel_id=1, source_target_pairs={{0,6},{1,7},{2,4},{3,5},{4,2},{5,3},{6,0},{7,1},{8,14},{9,15},{10,... | collective-permute-start | bytes 172040 | tf_op jit(solution)/shard_map/ppermute | solution.py:11
  46.7 2.2 %collective-permute-start.18 = (bf16[32,896]{1,0:T(8,128)(2,1)S(1)}, bf16[32,896]{1,0:T(8,128)(2,1)S(1)}, u32[]{:S(2)}, u32[]{:S(2)}) collective-permute-start(bf16[32,896]{1,0:T(8,128)(2,1)S(1)} %fusion.24), channel_id=1, source_target_pairs={{0,2},{1,3},{2,0},{3,1},{4,6},{5,7},{6,4},{7,5},{8,10},{9,11},{10,... | collective-permute-start | bytes 172040 | tf_op jit(solution)/shard_map/ppermute | solution.py:11
  49.0 1.7 %collective-permute-start.24 = (bf16[64,896]{1,0:T(8,128)(2,1)S(1)}, bf16[64,896]{1,0:T(8,128)(2,1)S(1)}, u32[]{:S(2)}, u32[]{:S(2)}) collective-permute-start(bf16[64,896]{1,0:T(8,128)(2,1)S(1)} %pad_maximum_fusion.5), channel_id=1, source_target_pairs={{0,1},{1,0},{2,3},{3,2},{4,5},{5,4},{6,7},{7,6},{8,9},{9,8},{10,11... | collective-permute-start | bytes 344072 | tf_op jit(solution)/shard_map/ppermute | solution.py:11
  50.7 1.2 %collective-permute-start.26 = (bf16[16,896]{1,0:T(8,128)(2,1)S(1)}, bf16[16,896]{1,0:T(8,128)(2,1)S(1)}, u32[]{:S(2)}, u32[]{:S(2)}) collective-permute-start(bf16[16,896]{1,0:T(8,128)(2,1)S(1)} %subtract_convert_fusion), channel_id=1, source_target_pairs={{0,16},{8,24},{16,0},{24,8},{1,17},{9,25},{17,1},{25,9},{2,18},{10... | collective-permute-start | bytes 86024 | tf_op jit(solution)/shard_map/ppermute | solution.py:11
  51.9 0.3 fusion.25
  52.2 0.3 fusion.13
  52.6 1.2 %collective-permute-done.24 = bf16[64,896]{1,0:T(8,128)(2,1)S(1)} collective-permute-done((bf16[64,896]{1,0:T(8,128)(2,1)S(1)}, bf16[64,896]{1,0:T(8,128)(2,1)S(1)}, u32[]{:S(2)}, u32[]{:S(2)}) %collective-permute-start.24) | collective-permute-done | bytes 114720 | tf_op jit(solution)/shard_map/ppermute | solution.py:11
  53.8 0.3 fusion.52
  54.1 0.3 convolution_add_fusion.3
  54.5 0.1 collective-permute-start.25
  54.6 1.7 %collective-permute-start.29 = (bf16[16,896]{1,0:T(8,128)(2,1)S(1)}, bf16[16,896]{1,0:T(8,128)(2,1)S(1)}, u32[]{:S(2)}, u32[]{:S(2)}) collective-permute-start(bf16[16,896]{1,0:T(8,128)(2,1)S(1)} %slice_bitcast_fusion), channel_id=1, source_target_pairs={{0,1},{1,0},{2,3},{3,2},{4,5},{5,4},{6,7},{7,6},{8,9},{9,8},{10,11... | collective-permute-start | bytes 86024 | tf_op jit(solution)/shard_map/ppermute | solution.py:11
  56.4 1.4 %collective-permute-start.30 = (bf16[128,128]{1,0:T(8,128)(2,1)S(1)}, bf16[128,128]{1,0:T(8,128)(2,1)S(1)}, u32[]{:S(2)}, u32[]{:S(2)}) collective-permute-start(bf16[128,128]{1,0:T(8,128)(2,1)S(1)} %get-tuple-element.92), channel_id=1, source_target_pairs={{0,1},{1,0},{2,3},{3,2},{4,5},{5,4},{6,7},{7,6},{8,9},{9,8},{10,11... | collective-permute-start | bytes 98312 | tf_op jit(solution)/shard_map/ppermute | solution.py:11
  57.9 1.2 %collective-permute-start.28 = (bf16[128,128]{1,0:T(8,128)(2,1)S(1)}, bf16[128,128]{1,0:T(8,128)(2,1)S(1)}, u32[]{:S(2)}, u32[]{:S(2)}) collective-permute-start(bf16[128,128]{1,0:T(8,128)(2,1)S(1)} %get-tuple-element.93), channel_id=1, source_target_pairs={{0,16},{8,24},{16,0},{24,8},{1,17},{9,25},{17,1},{25,9},{2,18},{10... | collective-permute-start | bytes 98312 | tf_op jit(solution)/shard_map/ppermute | solution.py:11
  59.1 0.1 broadcast_select_fusion.1
  59.2 2.6 %collective-permute-done.28 = bf16[128,128]{1,0:T(8,128)(2,1)S(1)} collective-permute-done((bf16[128,128]{1,0:T(8,128)(2,1)S(1)}, bf16[128,128]{1,0:T(8,128)(2,1)S(1)}, u32[]{:S(2)}, u32[]{:S(2)}) %collective-permute-start.28) | collective-permute-done | bytes 32800 | tf_op jit(solution)/shard_map/ppermute | solution.py:11
  61.8 0.6 %maximum_select_fusion = bf16[1,16,1792]{2,1,0:T(8,128)(2,1)} fusion(bf16[1,16,896]{2,1,0:T(8,128)(2,1)S(1)} %get-tuple-element.95, bf16[1,16,896]{2,1,0:T(8,128)(2,1)S(1)} %get-tuple-element.94, bf16[1,16,896]{2,1,0:T(8,128)(2,1)S(1)} %bitcast.109, bf16[1,16,896]{2,1,0:T(8,128)(2,1)S(1)} %bitcast.122, pred[]{:T(512)S(6)} %eq.46), kind=kLoop, calls=%fused_computation.51 | loop fusion | flops 258048 | bytes 172033 | tf_op jit(solution)/shard_map/jit(_where)/select_n | solution.py:171
  62.4 0.5 fusion.27
  63.0 1.4 %fusion = bf16[1,3584,128]{2,1,0:T(8,128)(2,1)} fusion(bf16[128,1792]{1,0:T(8,128)(2,1)S(1)} %get-tuple-element.78, bf16[128,1792]{1,0:T(8,128)(2,1)S(1)} %get-tuple-element.77, bf16[128,128]{1,0:T(8,128)(2,1)S(1)} %collective-permute-done.28, bf16[128,128]{1,0:T(8,128)(2,1)S(1)} %collective-permute-done.30, f32[384,128]{1,0:T(8,128)S(1)} %select_add_fusion, ...), kind=kOutput, calls=%fused_computation.1 | convolution fusion | flops 119832576 | bytes 1966592 | tf_op jit(solution)/shard_map/dot_general | solution.py:44
  (59 shorter events, 0.5 us)
Async XLA Ops:
  0.6 13.1 %copy-start = (s32[2,1,12]{2,1,0:T(1,128)S(1)}, s32[2,1,12]{2,1,0:T(1,128)}, u32[]{:S(2)}) copy-start(s32[2,1,12]{2,1,0:T(1,128)} %param.11) | copy-start | bytes 292
  0.6 11.9 %copy-start.2 = (bf16[1,3584,128]{2,1,0:T(8,128)(2,1)S(1)}, bf16[1,3584,128]{2,1,0:T(8,128)(2,1)}, u32[]{:S(2)}) copy-start(bf16[1,3584,128]{2,1,0:T(8,128)(2,1)} %param.8) | copy-start | bytes 2752516
  0.7 7.4 %collective-permute-start.3 = (bf16[3584,128]{1,0:T(8,128)(2,1)}, bf16[3584,128]{1,0:T(8,128)(2,1)}, u32[]{:S(2)}, u32[]{:S(2)}) collective-permute-start(bf16[3584,128]{1,0:T(8,128)(2,1)} %bitcast.112), channel_id=1, source_target_pairs={{0,8},{8,0},{16,24},{24,16},{1,9},{9,1},{17,25},{25,17},{2,10},{10... | collective-permute-start | bytes 2752520 | tf_op jit(solution)/shard_map/ppermute | solution.py:11
  2.0 6.0 %collective-permute-start.2 = (bf16[16,1792]{1,0:T(8,128)(2,1)S(1)}, bf16[16,1792]{1,0:T(8,128)(2,1)S(1)}, u32[]{:S(2)}, u32[]{:S(2)}) collective-permute-start(bf16[16,1792]{1,0:T(8,128)(2,1)S(1)} %get-tuple-element.86), channel_id=1, source_target_pairs={{0,1},{1,0},{2,3},{3,2},{4,5},{5,4},{6,7},{7,6},{8,9},{9,8},{10,11... | collective-permute-start | bytes 172040 | tf_op jit(solution)/shard_map/ppermute | solution.py:11
  4.6 9.1 %copy-start.3 = (f32[1,128]{1,0:T(1,128)S(1)}, f32[1,128]{1,0:T(1,128)}, u32[]{:S(2)}) copy-start(f32[1,128]{1,0:T(1,128)} %param.9) | copy-start | bytes 1540
  5.9 12.6 %collective-permute-start.1 = (bf16[256,896]{1,0:T(8,128)(2,1)S(1)}, bf16[256,896]{1,0:T(8,128)(2,1)S(1)}, u32[]{:S(2)}, u32[]{:S(2)}) collective-permute-start(bf16[256,896]{1,0:T(8,128)(2,1)S(1)} %get-tuple-element.75), channel_id=1, source_target_pairs={{0,16},{8,24},{16,0},{24,8},{1,17},{9,25},{17,1},{25,9},{2,18},{10... | collective-permute-start | bytes 1376264 | tf_op jit(solution)/shard_map/ppermute | solution.py:11
  7.5 12.2 %collective-permute-start = (bf16[256,896]{1,0:T(8,128)(2,1)S(1)}, bf16[256,896]{1,0:T(8,128)(2,1)S(1)}, u32[]{:S(2)}, u32[]{:S(2)}) collective-permute-start(bf16[256,896]{1,0:T(8,128)(2,1)S(1)} %get-tuple-element.76), channel_id=1, source_target_pairs={{0,1},{1,0},{2,3},{3,2},{4,5},{5,4},{6,7},{7,6},{8,9},{9,8},{10,11... | collective-permute-start | bytes 1376264 | tf_op jit(solution)/shard_map/ppermute | solution.py:11
  8.0 11.7 %collective-permute-start.6 = (bf16[32,1792]{1,0:T(8,128)(2,1)S(1)}, bf16[32,1792]{1,0:T(8,128)(2,1)S(1)}, u32[]{:S(2)}, u32[]{:S(2)}) collective-permute-start(bf16[32,1792]{1,0:T(8,128)(2,1)S(1)} %bitcast.103), channel_id=1, source_target_pairs={{0,6},{1,7},{2,4},{3,5},{4,2},{5,3},{6,0},{7,1},{8,14},{9,15},{10,... | collective-permute-start | bytes 344072 | tf_op jit(solution)/shard_map/ppermute | solution.py:11
  11.7 9.4 %collective-permute-start.5 = (bf16[32,1792]{1,0:T(8,128)(2,1)S(1)}, bf16[32,1792]{1,0:T(8,128)(2,1)S(1)}, u32[]{:S(2)}, u32[]{:S(2)}) collective-permute-start(bf16[32,1792]{1,0:T(8,128)(2,1)S(1)} %bitcast.104), channel_id=1, source_target_pairs={{0,4},{1,5},{2,6},{3,7},{4,0},{5,1},{6,2},{7,3},{8,12},{9,13},{10,... | collective-permute-start | bytes 344072 | tf_op jit(solution)/shard_map/ppermute | solution.py:11
  11.7 9.4 %collective-permute-start.4 = (bf16[32,1792]{1,0:T(8,128)(2,1)S(1)}, bf16[32,1792]{1,0:T(8,128)(2,1)S(1)}, u32[]{:S(2)}, u32[]{:S(2)}) collective-permute-start(bf16[32,1792]{1,0:T(8,128)(2,1)S(1)} %bitcast.105), channel_id=1, source_target_pairs={{0,2},{1,3},{2,0},{3,1},{4,6},{5,7},{6,4},{7,5},{8,10},{9,11},{10,... | collective-permute-start | bytes 344072 | tf_op jit(solution)/shard_map/ppermute | solution.py:11
  13.9 12.9 %copy-start.1 = (bf16[1,2,2,128,1792]{4,3,2,1,0:T(8,128)(2,1)S(1)}, bf16[1,2,2,128,1792]{4,3,2,1,0:T(8,128)(2,1)}, u32[]{:S(2)}) copy-start(bf16[1,2,2,128,1792]{4,3,2,1,0:T(8,128)(2,1)} %param.10) | copy-start | bytes 5505028
  21.4 1.4 %collective-permute-start.7 = (f32[128,256]{1,0:T(8,128)S(1)}, f32[128,256]{1,0:T(8,128)S(1)}, u32[]{:S(2)}, u32[]{:S(2)}) collective-permute-start(f32[128,256]{1,0:T(8,128)S(1)} %convolution_add_fusion.4), channel_id=1, source_target_pairs={{0,8},{8,0},{16,24},{24,16},{1,9},{9,1},{17,25},{25,17},{2,10},{10... | collective-permute-start | bytes 393224 | tf_op jit(solution)/shard_map/ppermute | solution.py:11
  22.9 4.3 %collective-permute-start.9 = (bf16[128,256]{1,0:T(8,128)(2,1)S(1)}, bf16[128,256]{1,0:T(8,128)(2,1)S(1)}, u32[]{:S(2)}, u32[]{:S(2)}) collective-permute-start(bf16[128,256]{1,0:T(8,128)(2,1)S(1)} %multiply_convert_fusion), channel_id=1, source_target_pairs={{0,16},{8,24},{16,0},{24,8},{1,17},{9,25},{17,1},{25,9},{2,18},{10... | collective-permute-start | bytes 196616 | tf_op jit(solution)/shard_map/ppermute | solution.py:11
  23.8 5.2 %collective-permute-start.8 = (bf16[128,256]{1,0:T(8,128)(2,1)S(1)}, bf16[128,256]{1,0:T(8,128)(2,1)S(1)}, u32[]{:S(2)}, u32[]{:S(2)}) collective-permute-start(bf16[128,256]{1,0:T(8,128)(2,1)S(1)} %bitcast.118), channel_id=1, source_target_pairs={{0,1},{1,0},{2,3},{3,2},{4,5},{5,4},{6,7},{7,6},{8,9},{9,8},{10,11... | collective-permute-start | bytes 196616 | tf_op jit(solution)/shard_map/ppermute | solution.py:11
  26.2 9.6 %collective-permute-start.17 = (bf16[16,896]{1,0:T(8,128)(2,1)S(1)}, bf16[16,896]{1,0:T(8,128)(2,1)S(1)}, u32[]{:S(2)}, u32[]{:S(2)}) collective-permute-start(bf16[16,896]{1,0:T(8,128)(2,1)S(1)} %get-tuple-element.79), channel_id=1, source_target_pairs={{0,1},{1,0},{2,3},{3,2},{4,5},{5,4},{6,7},{7,6},{8,9},{9,8},{10,11... | collective-permute-start | bytes 86024 | tf_op jit(solution)/shard_map/ppermute | solution.py:11
  27.4 4.9 %collective-permute-start.10 = (bf16[64,896]{1,0:T(8,128)(2,1)S(1)}, bf16[64,896]{1,0:T(8,128)(2,1)S(1)}, u32[]{:S(2)}, u32[]{:S(2)}) collective-permute-start(bf16[64,896]{1,0:T(8,128)(2,1)S(1)} %fusion.1), channel_id=1, source_target_pairs={{0,1},{1,0},{2,3},{3,2},{4,5},{5,4},{6,7},{7,6},{8,9},{9,8},{10,11... | collective-permute-start | bytes 344072 | tf_op jit(solution)/shard_map/ppermute | solution.py:11
  29.5 7.3 %collective-permute-start.16 = (bf16[32,896]{1,0:T(8,128)(2,1)S(1)}, bf16[32,896]{1,0:T(8,128)(2,1)S(1)}, u32[]{:S(2)}, u32[]{:S(2)}) collective-permute-start(bf16[32,896]{1,0:T(8,128)(2,1)S(1)} %get-tuple-element.82), channel_id=1, source_target_pairs={{0,6},{1,7},{2,4},{3,5},{4,2},{5,3},{6,0},{7,1},{8,14},{9,15},{10,... | collective-permute-start | bytes 172040 | tf_op jit(solution)/shard_map/ppermute | solution.py:11
  32.0 6.5 %collective-permute-start.15 = (bf16[32,896]{1,0:T(8,128)(2,1)S(1)}, bf16[32,896]{1,0:T(8,128)(2,1)S(1)}, u32[]{:S(2)}, u32[]{:S(2)}) collective-permute-start(bf16[32,896]{1,0:T(8,128)(2,1)S(1)} %get-tuple-element.83), channel_id=1, source_target_pairs={{0,4},{1,5},{2,6},{3,7},{4,0},{5,1},{6,2},{7,3},{8,12},{9,13},{10,... | collective-permute-start | bytes 172040 | tf_op jit(solution)/shard_map/ppermute | solution.py:11
  32.4 6.2 %collective-permute-start.14 = (bf16[16,896]{1,0:T(8,128)(2,1)S(1)}, bf16[16,896]{1,0:T(8,128)(2,1)S(1)}, u32[]{:S(2)}, u32[]{:S(2)}) collective-permute-start(bf16[16,896]{1,0:T(8,128)(2,1)S(1)} %get-tuple-element.89), channel_id=1, source_target_pairs={{0,6},{1,7},{2,4},{3,5},{4,2},{5,3},{6,0},{7,1},{8,14},{9,15},{10,... | collective-permute-start | bytes 86024 | tf_op jit(solution)/shard_map/ppermute | solution.py:11
  34.9 4.9 %collective-permute-start.13 = (bf16[16,896]{1,0:T(8,128)(2,1)S(1)}, bf16[16,896]{1,0:T(8,128)(2,1)S(1)}, u32[]{:S(2)}, u32[]{:S(2)}) collective-permute-start(bf16[16,896]{1,0:T(8,128)(2,1)S(1)} %get-tuple-element.90), channel_id=1, source_target_pairs={{0,4},{1,5},{2,6},{3,7},{4,0},{5,1},{6,2},{7,3},{8,12},{9,13},{10,... | collective-permute-start | bytes 86024 | tf_op jit(solution)/shard_map/ppermute | solution.py:11
  35.8 4.2 %collective-permute-start.12 = (bf16[16,896]{1,0:T(8,128)(2,1)S(1)}, bf16[16,896]{1,0:T(8,128)(2,1)S(1)}, u32[]{:S(2)}, u32[]{:S(2)}) collective-permute-start(bf16[16,896]{1,0:T(8,128)(2,1)S(1)} %get-tuple-element.91), channel_id=1, source_target_pairs={{0,2},{1,3},{2,0},{3,1},{4,6},{5,7},{6,4},{7,5},{8,10},{9,11},{10,... | collective-permute-start | bytes 86024 | tf_op jit(solution)/shard_map/ppermute | solution.py:11
  36.9 7.6 %collective-permute-start.11 = (bf16[32,896]{1,0:T(8,128)(2,1)S(1)}, bf16[32,896]{1,0:T(8,128)(2,1)S(1)}, u32[]{:S(2)}, u32[]{:S(2)}) collective-permute-start(bf16[32,896]{1,0:T(8,128)(2,1)S(1)} %get-tuple-element.48), channel_id=1, source_target_pairs={{0,2},{1,3},{2,0},{3,1},{4,6},{5,7},{6,4},{7,5},{8,10},{9,11},{10,... | collective-permute-start | bytes 172040 | tf_op jit(solution)/shard_map/ppermute | solution.py:11
  40.0 6.7 %collective-permute-start.23 = (bf16[16,896]{1,0:T(8,128)(2,1)S(1)}, bf16[16,896]{1,0:T(8,128)(2,1)S(1)}, u32[]{:S(2)}, u32[]{:S(2)}) collective-permute-start(bf16[16,896]{1,0:T(8,128)(2,1)S(1)} %subtract_convert_fusion), channel_id=1, source_target_pairs={{0,6},{1,7},{2,4},{3,5},{4,2},{5,3},{6,0},{7,1},{8,14},{9,15},{10,... | collective-permute-start | bytes 86024 | tf_op jit(solution)/shard_map/ppermute | solution.py:11
  42.2 6.7 %collective-permute-start.22 = (bf16[16,896]{1,0:T(8,128)(2,1)S(1)}, bf16[16,896]{1,0:T(8,128)(2,1)S(1)}, u32[]{:S(2)}, u32[]{:S(2)}) collective-permute-start(bf16[16,896]{1,0:T(8,128)(2,1)S(1)} %subtract_convert_fusion), channel_id=1, source_target_pairs={{0,4},{1,5},{2,6},{3,7},{4,0},{5,1},{6,2},{7,3},{8,12},{9,13},{10,... | collective-permute-start | bytes 86024 | tf_op jit(solution)/shard_map/ppermute | solution.py:11
  42.2 6.7 %collective-permute-start.21 = (bf16[16,896]{1,0:T(8,128)(2,1)S(1)}, bf16[16,896]{1,0:T(8,128)(2,1)S(1)}, u32[]{:S(2)}, u32[]{:S(2)}) collective-permute-start(bf16[16,896]{1,0:T(8,128)(2,1)S(1)} %subtract_convert_fusion), channel_id=1, source_target_pairs={{0,2},{1,3},{2,0},{3,1},{4,6},{5,7},{6,4},{7,5},{8,10},{9,11},{10,... | collective-permute-start | bytes 86024 | tf_op jit(solution)/shard_map/ppermute | solution.py:11
  44.5 7.4 %collective-permute-start.20 = (bf16[32,896]{1,0:T(8,128)(2,1)S(1)}, bf16[32,896]{1,0:T(8,128)(2,1)S(1)}, u32[]{:S(2)}, u32[]{:S(2)}) collective-permute-start(bf16[32,896]{1,0:T(8,128)(2,1)S(1)} %fusion.24), channel_id=1, source_target_pairs={{0,6},{1,7},{2,4},{3,5},{4,2},{5,3},{6,0},{7,1},{8,14},{9,15},{10,... | collective-permute-start | bytes 172040 | tf_op jit(solution)/shard_map/ppermute | solution.py:11
  46.7 5.2 %collective-permute-start.19 = (bf16[32,896]{1,0:T(8,128)(2,1)S(1)}, bf16[32,896]{1,0:T(8,128)(2,1)S(1)}, u32[]{:S(2)}, u32[]{:S(2)}) collective-permute-start(bf16[32,896]{1,0:T(8,128)(2,1)S(1)} %fusion.24), channel_id=1, source_target_pairs={{0,4},{1,5},{2,6},{3,7},{4,0},{5,1},{6,2},{7,3},{8,12},{9,13},{10,... | collective-permute-start | bytes 172040 | tf_op jit(solution)/shard_map/ppermute | solution.py:11
  46.7 5.2 %collective-permute-start.18 = (bf16[32,896]{1,0:T(8,128)(2,1)S(1)}, bf16[32,896]{1,0:T(8,128)(2,1)S(1)}, u32[]{:S(2)}, u32[]{:S(2)}) collective-permute-start(bf16[32,896]{1,0:T(8,128)(2,1)S(1)} %fusion.24), channel_id=1, source_target_pairs={{0,2},{1,3},{2,0},{3,1},{4,6},{5,7},{6,4},{7,5},{8,10},{9,11},{10,... | collective-permute-start | bytes 172040 | tf_op jit(solution)/shard_map/ppermute | solution.py:11
  49.0 4.9 %collective-permute-start.24 = (bf16[64,896]{1,0:T(8,128)(2,1)S(1)}, bf16[64,896]{1,0:T(8,128)(2,1)S(1)}, u32[]{:S(2)}, u32[]{:S(2)}) collective-permute-start(bf16[64,896]{1,0:T(8,128)(2,1)S(1)} %pad_maximum_fusion.5), channel_id=1, source_target_pairs={{0,1},{1,0},{2,3},{3,2},{4,5},{5,4},{6,7},{7,6},{8,9},{9,8},{10,11... | collective-permute-start | bytes 344072 | tf_op jit(solution)/shard_map/ppermute | solution.py:11
  50.7 5.7 %collective-permute-start.26 = (bf16[16,896]{1,0:T(8,128)(2,1)S(1)}, bf16[16,896]{1,0:T(8,128)(2,1)S(1)}, u32[]{:S(2)}, u32[]{:S(2)}) collective-permute-start(bf16[16,896]{1,0:T(8,128)(2,1)S(1)} %subtract_convert_fusion), channel_id=1, source_target_pairs={{0,16},{8,24},{16,0},{24,8},{1,17},{9,25},{17,1},{25,9},{2,18},{10... | collective-permute-start | bytes 86024 | tf_op jit(solution)/shard_map/ppermute | solution.py:11
  51.9 4.5 %collective-permute-start.27 = (bf16[128,1792]{1,0:T(8,128)(2,1)S(1)}, bf16[128,1792]{1,0:T(8,128)(2,1)S(1)}, u32[]{:S(2)}, u32[]{:S(2)}) collective-permute-start(bf16[128,1792]{1,0:T(8,128)(2,1)S(1)} %constant_dynamic-update-slice_fusion), channel_id=1, source_target_pairs={{0,8},{8,0},{16,24},{24,16},{1,9},{9,1},{17,25},{25,17},{2,10},{10... | collective-permute-start | bytes 1376264 | tf_op jit(solution)/shard_map/ppermute | solution.py:11
  54.5 1.8 %collective-permute-start.25 = (f32[384,128]{1,0:T(8,128)S(1)}, f32[384,128]{1,0:T(8,128)S(1)}, u32[]{:S(2)}, u32[]{:S(2)}) collective-permute-start(f32[384,128]{1,0:T(8,128)S(1)} %slice_select_fusion), channel_id=1, source_target_pairs={{0,8},{8,0},{16,24},{24,16},{1,9},{9,1},{17,25},{25,17},{2,10},{10... | collective-permute-start | bytes 589832 | tf_op jit(solution)/shard_map/ppermute | solution.py:11
  54.6 4.6 %collective-permute-start.29 = (bf16[16,896]{1,0:T(8,128)(2,1)S(1)}, bf16[16,896]{1,0:T(8,128)(2,1)S(1)}, u32[]{:S(2)}, u32[]{:S(2)}) collective-permute-start(bf16[16,896]{1,0:T(8,128)(2,1)S(1)} %slice_bitcast_fusion), channel_id=1, source_target_pairs={{0,1},{1,0},{2,3},{3,2},{4,5},{5,4},{6,7},{7,6},{8,9},{9,8},{10,11... | collective-permute-start | bytes 86024 | tf_op jit(solution)/shard_map/ppermute | solution.py:11
  56.4 6.0 %collective-permute-start.30 = (bf16[128,128]{1,0:T(8,128)(2,1)S(1)}, bf16[128,128]{1,0:T(8,128)(2,1)S(1)}, u32[]{:S(2)}, u32[]{:S(2)}) collective-permute-start(bf16[128,128]{1,0:T(8,128)(2,1)S(1)} %get-tuple-element.92), channel_id=1, source_target_pairs={{0,1},{1,0},{2,3},{3,2},{4,5},{5,4},{6,7},{7,6},{8,9},{9,8},{10,11... | collective-permute-start | bytes 98312 | tf_op jit(solution)/shard_map/ppermute | solution.py:11
  57.9 3.9 %collective-permute-start.28 = (bf16[128,128]{1,0:T(8,128)(2,1)S(1)}, bf16[128,128]{1,0:T(8,128)(2,1)S(1)}, u32[]{:S(2)}, u32[]{:S(2)}) collective-permute-start(bf16[128,128]{1,0:T(8,128)(2,1)S(1)} %get-tuple-element.93), channel_id=1, source_target_pairs={{0,16},{8,24},{16,0},{24,8},{1,17},{9,25},{17,1},{25,9},{2,18},{10... | collective-permute-start | bytes 98312 | tf_op jit(solution)/shard_map/ppermute | solution.py:11

commit v21 on v20

--- a/solution.py
+++ b/solution.py
@@ -114,7 +114,6 @@
     own_mine, shared_mine = decoder_part(decoder, layer, side), decoder_part(decoder, 1 - layer, layer)
     resid_half = jnp.concatenate(column, axis=0)
     firing = gates(blocks, layer, slot, slots, latents, tokens)
-    gate = jnp.where(half == 0, firing[:, :latents], firing[:, latents:])
 
     partial = half_preacts(resid_half, enc_weight[0], weight_other, bias, half)
     acts = ((partial + over_core(partial)) * firing).astype(BF16)
@@ -164,9 +163,11 @@
     grads = jnp.where(half == 0, lower, upper) + over_core(leaving)
     own_there = over_x(rows_at(late_own, 1))
     grads, shared_there, resid_other = hold((grads, shared_there, resid_other))
-    from_x = over_x(grads[tokens:2 * tokens].astype(BF16))
-    from_y = over_y(grads[2 * tokens:].astype(BF16))
-    from_y, own_there = hold((from_y, own_there))
+    to_x, to_y = grads[tokens:2 * tokens].astype(BF16), grads[2 * tokens:].astype(BF16)
+    from_x, from_y = over_x(to_x), over_y(to_y)
+    firing, _, _ = hold((firing, to_x, to_y))
+    gate = jnp.where(half == 0, firing[:, :latents], firing[:, latents:])
+    own_there, gate = hold((own_there, gate))
     from_x, from_y = from_x.astype(F32), from_y.astype(F32)
     errors = jnp.where(
         layer == 0,

time: 64.6 us -> 76.4 us (1.18)
  waiting for transfers between devices: 14.5 us -> 28 us
  starting transfers between devices: 38.7 us -> 37 us
    ppermute x31, waiting for transfers between devices: 14.5 us -> 28 us  [crossed(): lax.ppermute(block, axis, [(i, i ^ mask) for i in range(lax.axis_size(axi...]
    ppermute x31, starting transfers between devices: 38.7 us -> 37 us  [crossed(): lax.ppermute(block, axis, [(i, i ^ mask) for i in range(lax.axis_size(axi...]
  transfers between devices with their start and end apart: 31 -> 31, of which waited for: 9 -> 13; matrix products, arithmetic and copies ran while one was open for 12% -> 10% of each run, Pallas kernels for 0% -> 0%
where the time goes in v21:
time: 76.4 us; the launch traced here: 76.1 us
  starting transfers between devices  37 us (48%)
  waiting for transfers between devices  28 us (37%)
  matrix products  4.15 us (5%)
  local copies, waits for them, and re-layouts  3.02 us (4%)
  other arithmetic  2.95 us (4%)
  between operations  1.05 us (1%)
    ppermute x31, starting transfers between devices, crossed(): lax.ppermute(block, axis, [(i, i ^ mask) for i in range(lax.axis_size(axi...  37 us
    ppermute x31, waiting for transfers between devices, crossed(): lax.ppermute(block, axis, [(i, i ^ mask) for i in range(lax.axis_size(axi...  28 us
    dot_general x7, matrix products, times(): return jnp.dot(left, right, preferred_element_type=F32)  1.6 us
  transfers between devices with their start and end apart: 31, of which 13 were waited for; matrix products, arithmetic and copies ran while one was open for 10% of the time, Pallas kernels for 0%

profile of v21, /device:TPU:0, one launch (start us, length us, event | category | flops | bytes accessed | tf_op | source)
XLA Modules:
  0.0 76.1 jit_solution(6379933021039955226)
XLA Ops:
  0.6 0.0 copy-start
  0.7 0.5 collective-permute-start.3
  1.2 1.2 %dynamic-slice_bitcast_fusion = (bf16[256,896]{1,0:T(8,128)(2,1)S(1)}, bf16[256,896]{1,0:T(8,128)(2,1)S(1)}) fusion(bf16[2,256,1792]{2,1,0:T(8,128)(2,1)} %bitcast.92, s32[]{:T(128)S(6)} %select_n.171, s32[]{:T(128)S(6)} %select_n.172, s32[]{:T(128)S(6)} %select_n.169, s32[]{:T(128)S(6)} %select_n.170), kind=kLoop, calls=%fused_computation.24 | loop fusion | bytes 1835024 | tf_op jit(solution)/shard_map/squeeze | solution.py:91
  2.4 2.7 %collective-permute-start = (bf16[256,896]{1,0:T(8,128)(2,1)S(1)}, bf16[256,896]{1,0:T(8,128)(2,1)S(1)}, u32[]{:S(2)}, u32[]{:S(2)}) collective-permute-start(bf16[256,896]{1,0:T(8,128)(2,1)S(1)} %get-tuple-element.78), channel_id=1, source_target_pairs={{0,1},{1,0},{2,3},{3,2},{4,5},{5,4},{6,7},{7,6},{8,9},{9,8},{10,11... | collective-permute-start | bytes 1376264 | tf_op jit(solution)/shard_map/ppermute | solution.py:11
  5.1 1.5 %collective-permute-start.1 = (bf16[256,896]{1,0:T(8,128)(2,1)S(1)}, bf16[256,896]{1,0:T(8,128)(2,1)S(1)}, u32[]{:S(2)}, u32[]{:S(2)}) collective-permute-start(bf16[256,896]{1,0:T(8,128)(2,1)S(1)} %get-tuple-element.77), channel_id=1, source_target_pairs={{0,16},{8,24},{16,0},{24,8},{1,17},{9,25},{17,1},{25,9},{2,18},{10... | collective-permute-start | bytes 1376264 | tf_op jit(solution)/shard_map/ppermute | solution.py:11
  6.7 0.8 %dynamic-slice_bitcast_fusion.3 = (bf16[1,1,16,1792]{3,2,1,0:T(8,128)(2,1)S(1)}, bf16[16,1792]{1,0:T(8,128)(2,1)S(1)}) fusion(bf16[2,16,3584]{2,1,0:T(8,128)(2,1)} %param.6, s32[]{:T(128)S(6)} %select_n.169, s32[]{:T(128)S(6)} %select_n.174), kind=kLoop, calls=%fused_computation.55 | loop fusion | bytes 172040 | tf_op jit(solution)/shard_map/reshape;squeeze | solution.py:100
  7.5 0.5 collective-permute-start.2
  8.0 9.4 %collective-permute-done.2 = bf16[16,1792]{1,0:T(8,128)(2,1)S(1)} collective-permute-done((bf16[16,1792]{1,0:T(8,128)(2,1)S(1)}, bf16[16,1792]{1,0:T(8,128)(2,1)S(1)}, u32[]{:S(2)}, u32[]{:S(2)}) %collective-permute-start.2) | collective-permute-done | bytes 57376 | tf_op jit(solution)/shard_map/ppermute | solution.py:11
  17.4 1.9 %collective-permute-start.4 = (bf16[32,1792]{1,0:T(8,128)(2,1)S(1)}, bf16[32,1792]{1,0:T(8,128)(2,1)S(1)}, u32[]{:S(2)}, u32[]{:S(2)}) collective-permute-start(bf16[32,1792]{1,0:T(8,128)(2,1)S(1)} %bitcast.103), channel_id=1, source_target_pairs={{0,2},{1,3},{2,0},{3,1},{4,6},{5,7},{6,4},{7,5},{8,10},{9,11},{10,... | collective-permute-start | bytes 344072 | tf_op jit(solution)/shard_map/ppermute | solution.py:11
  19.3 2.6 %collective-permute-start.5 = (bf16[32,1792]{1,0:T(8,128)(2,1)S(1)}, bf16[32,1792]{1,0:T(8,128)(2,1)S(1)}, u32[]{:S(2)}, u32[]{:S(2)}) collective-permute-start(bf16[32,1792]{1,0:T(8,128)(2,1)S(1)} %bitcast.104), channel_id=1, source_target_pairs={{0,4},{1,5},{2,6},{3,7},{4,0},{5,1},{6,2},{7,3},{8,12},{9,13},{10,... | collective-permute-start | bytes 344072 | tf_op jit(solution)/shard_map/ppermute | solution.py:11
  21.9 1.2 %bitcast_select_fusion.1 = (bf16[1792,128]{1,0:T(8,128)(2,1)S(1)}, bf16[1792,128]{1,0:T(8,128)(2,1)S(1)}) fusion(pred[]{:T(512)S(6)} %eq.48, bf16[3584,128]{1,0:T(8,128)(2,1)} %collective-permute-done.3, s32[]{:T(128)S(6)} %select_n.174, bf16[1,3584,128]{2,1,0:T(8,128)(2,1)S(1)} %copy-done.2), kind=kLoop, calls=%fused_computation.23 | loop fusion | flops 458752 | bytes 1835013 | tf_op jit(solution)/shard_map/jit(_where)/select_n | solution.py:23
  23.1 0.0 copy-start.1
  23.2 0.3 collective-permute-done.4
  23.4 7.3 %collective-permute-done.5 = bf16[32,1792]{1,0:T(8,128)(2,1)S(1)} collective-permute-done((bf16[32,1792]{1,0:T(8,128)(2,1)S(1)}, bf16[32,1792]{1,0:T(8,128)(2,1)S(1)}, u32[]{:S(2)}, u32[]{:S(2)}) %collective-permute-start.5) | collective-permute-done | bytes 114720 | tf_op jit(solution)/shard_map/ppermute | solution.py:11
  30.8 0.3 convolution_add_fusion.4
  31.1 0.1 collective-permute-start.7
  31.2 0.1 compare_reduce_fusion
  31.3 1.2 %collective-permute-done.7 = f32[128,256]{1,0:T(8,128)S(1)} collective-permute-done((f32[128,256]{1,0:T(8,128)S(1)}, f32[128,256]{1,0:T(8,128)S(1)}, u32[]{:S(2)}, u32[]{:S(2)}) %collective-permute-start.7) | collective-permute-done | bytes 131104 | tf_op jit(solution)/shard_map/ppermute | solution.py:11
  32.5 1.6 %collective-permute-start.9 = (bf16[128,256]{1,0:T(8,128)(2,1)S(1)}, bf16[128,256]{1,0:T(8,128)(2,1)S(1)}, u32[]{:S(2)}, u32[]{:S(2)}) collective-permute-start(bf16[128,256]{1,0:T(8,128)(2,1)S(1)} %multiply_convert_fusion), channel_id=1, source_target_pairs={{0,16},{8,24},{16,0},{24,8},{1,17},{9,25},{17,1},{25,9},{2,18},{10... | collective-permute-start | bytes 196616 | tf_op jit(solution)/shard_map/ppermute | solution.py:11
  34.1 1.6 %collective-permute-start.8 = (bf16[128,256]{1,0:T(8,128)(2,1)S(1)}, bf16[128,256]{1,0:T(8,128)(2,1)S(1)}, u32[]{:S(2)}, u32[]{:S(2)}) collective-permute-start(bf16[128,256]{1,0:T(8,128)(2,1)S(1)} %bitcast.118), channel_id=1, source_target_pairs={{0,1},{1,0},{2,3},{3,2},{4,5},{5,4},{6,7},{7,6},{8,9},{9,8},{10,11... | collective-permute-start | bytes 196616 | tf_op jit(solution)/shard_map/ppermute | solution.py:11
  35.7 0.2 fusion.11
  35.9 0.2 fusion.9
  36.1 0.8 %dynamic-slice_bitcast_fusion.4 = (bf16[16,896]{1,0:T(8,128)(2,1)S(1)}, bf16[16,896]{1,0:T(8,128)(2,1)S(1)}, bf16[16,896]{1,0:T(8,128)(2,1)S(1)}) fusion(bf16[3,16,3584]{2,1,0:T(8,128)(2,1)} %param.7, s32[]{:T(128)S(6)} %select_n.186, s32[]{:T(128)S(6)} %select_n.189, s32[]{:T(128)S(6)} %select_n.188, s32[]{:T(128)S(6)} %select_n.187), kind=kLoop, calls=%fused_computation.62 | loop fusion | bytes 172048 | tf_op jit(solution)/shard_map/squeeze | solution.py:126
  36.9 0.6 collective-permute-start.17
  37.5 0.2 fusion.1
  37.7 1.5 %collective-permute-start.10 = (bf16[64,896]{1,0:T(8,128)(2,1)S(1)}, bf16[64,896]{1,0:T(8,128)(2,1)S(1)}, u32[]{:S(2)}, u32[]{:S(2)}) collective-permute-start(bf16[64,896]{1,0:T(8,128)(2,1)S(1)} %fusion.1), channel_id=1, source_target_pairs={{0,1},{1,0},{2,3},{3,2},{4,5},{5,4},{6,7},{7,6},{8,9},{9,8},{10,11... | collective-permute-start | bytes 344072 | tf_op jit(solution)/shard_map/ppermute | solution.py:11
  39.3 0.2 fusion.51
  39.5 0.2 fusion.50
  39.8 2.9 %collective-permute-start.15 = (bf16[32,896]{1,0:T(8,128)(2,1)S(1)}, bf16[32,896]{1,0:T(8,128)(2,1)S(1)}, u32[]{:S(2)}, u32[]{:S(2)}) collective-permute-start(bf16[32,896]{1,0:T(8,128)(2,1)S(1)} %get-tuple-element.85), channel_id=1, source_target_pairs={{0,4},{1,5},{2,6},{3,7},{4,0},{5,1},{6,2},{7,3},{8,12},{9,13},{10,... | collective-permute-start | bytes 172040 | tf_op jit(solution)/shard_map/ppermute | solution.py:11
  42.7 1.3 %collective-permute-start.16 = (bf16[32,896]{1,0:T(8,128)(2,1)S(1)}, bf16[32,896]{1,0:T(8,128)(2,1)S(1)}, u32[]{:S(2)}, u32[]{:S(2)}) collective-permute-start(bf16[32,896]{1,0:T(8,128)(2,1)S(1)} %get-tuple-element.84), channel_id=1, source_target_pairs={{0,6},{1,7},{2,4},{3,5},{4,2},{5,3},{6,0},{7,1},{8,14},{9,15},{10,... | collective-permute-start | bytes 172040 | tf_op jit(solution)/shard_map/ppermute | solution.py:11
  44.0 0.2 convolution_add_fusion.1
  44.3 0.2 collective-permute-start.12
  44.5 2.9 %collective-permute-start.13 = (bf16[16,896]{1,0:T(8,128)(2,1)S(1)}, bf16[16,896]{1,0:T(8,128)(2,1)S(1)}, u32[]{:S(2)}, u32[]{:S(2)}) collective-permute-start(bf16[16,896]{1,0:T(8,128)(2,1)S(1)} %get-tuple-element.92), channel_id=1, source_target_pairs={{0,4},{1,5},{2,6},{3,7},{4,0},{5,1},{6,2},{7,3},{8,12},{9,13},{10,... | collective-permute-start | bytes 86024 | tf_op jit(solution)/shard_map/ppermute | solution.py:11
  47.4 1.3 %collective-permute-start.14 = (bf16[16,896]{1,0:T(8,128)(2,1)S(1)}, bf16[16,896]{1,0:T(8,128)(2,1)S(1)}, u32[]{:S(2)}, u32[]{:S(2)}) collective-permute-start(bf16[16,896]{1,0:T(8,128)(2,1)S(1)} %get-tuple-element.91), channel_id=1, source_target_pairs={{0,6},{1,7},{2,4},{3,5},{4,2},{5,3},{6,0},{7,1},{8,14},{9,15},{10,... | collective-permute-start | bytes 86024 | tf_op jit(solution)/shard_map/ppermute | solution.py:11
  48.8 0.1 collective-permute-start.11
  48.9 0.4 collective-permute-done.13
  49.3 3.9 %collective-permute-done.14 = bf16[16,896]{1,0:T(8,128)(2,1)S(1)} collective-permute-done((bf16[16,896]{1,0:T(8,128)(2,1)S(1)}, bf16[16,896]{1,0:T(8,128)(2,1)S(1)}, u32[]{:S(2)}, u32[]{:S(2)}) %collective-permute-start.14) | collective-permute-done | bytes 28704 | tf_op jit(solution)/shard_map/ppermute | solution.py:11
  53.2 1.3 %collective-permute-start.23 = (bf16[16,896]{1,0:T(8,128)(2,1)S(1)}, bf16[16,896]{1,0:T(8,128)(2,1)S(1)}, u32[]{:S(2)}, u32[]{:S(2)}) collective-permute-start(bf16[16,896]{1,0:T(8,128)(2,1)S(1)} %subtract_convert_fusion), channel_id=1, source_target_pairs={{0,6},{1,7},{2,4},{3,5},{4,2},{5,3},{6,0},{7,1},{8,14},{9,15},{10,... | collective-permute-start | bytes 86024 | tf_op jit(solution)/shard_map/ppermute | solution.py:11
  54.5 3.1 %collective-permute-start.21 = (bf16[16,896]{1,0:T(8,128)(2,1)S(1)}, bf16[16,896]{1,0:T(8,128)(2,1)S(1)}, u32[]{:S(2)}, u32[]{:S(2)}) collective-permute-start(bf16[16,896]{1,0:T(8,128)(2,1)S(1)} %subtract_convert_fusion), channel_id=1, source_target_pairs={{0,2},{1,3},{2,0},{3,1},{4,6},{5,7},{6,4},{7,5},{8,10},{9,11},{10,... | collective-permute-start | bytes 86024 | tf_op jit(solution)/shard_map/ppermute | solution.py:11
  57.7 1.3 %collective-permute-start.20 = (bf16[32,896]{1,0:T(8,128)(2,1)S(1)}, bf16[32,896]{1,0:T(8,128)(2,1)S(1)}, u32[]{:S(2)}, u32[]{:S(2)}) collective-permute-start(bf16[32,896]{1,0:T(8,128)(2,1)S(1)} %fusion.24), channel_id=1, source_target_pairs={{0,6},{1,7},{2,4},{3,5},{4,2},{5,3},{6,0},{7,1},{8,14},{9,15},{10,... | collective-permute-start | bytes 172040 | tf_op jit(solution)/shard_map/ppermute | solution.py:11
  59.0 0.2 collective-permute-start.19
  59.2 0.0 collective-permute-done.23
  59.3 2.9 %collective-permute-start.18 = (bf16[32,896]{1,0:T(8,128)(2,1)S(1)}, bf16[32,896]{1,0:T(8,128)(2,1)S(1)}, u32[]{:S(2)}, u32[]{:S(2)}) collective-permute-start(bf16[32,896]{1,0:T(8,128)(2,1)S(1)} %fusion.24), channel_id=1, source_target_pairs={{0,2},{1,3},{2,0},{3,1},{4,6},{5,7},{6,4},{7,5},{8,10},{9,11},{10,... | collective-permute-start | bytes 172040 | tf_op jit(solution)/shard_map/ppermute | solution.py:11
  62.2 1.0 %collective-permute-start.24 = (bf16[64,896]{1,0:T(8,128)(2,1)S(1)}, bf16[64,896]{1,0:T(8,128)(2,1)S(1)}, u32[]{:S(2)}, u32[]{:S(2)}) collective-permute-start(bf16[64,896]{1,0:T(8,128)(2,1)S(1)} %pad_maximum_fusion.5), channel_id=1, source_target_pairs={{0,1},{1,0},{2,3},{3,2},{4,5},{5,4},{6,7},{7,6},{8,9},{9,8},{10,11... | collective-permute-start | bytes 344072 | tf_op jit(solution)/shard_map/ppermute | solution.py:11
  63.2 0.5 collective-permute-start.27
  63.7 0.1 collective-permute-done.20
  63.8 1.2 %collective-permute-done.19 = bf16[32,896]{1,0:T(8,128)(2,1)S(1)} collective-permute-done((bf16[32,896]{1,0:T(8,128)(2,1)S(1)}, bf16[32,896]{1,0:T(8,128)(2,1)S(1)}, u32[]{:S(2)}, u32[]{:S(2)}) %collective-permute-start.19) | collective-permute-done | bytes 57376 | tf_op jit(solution)/shard_map/ppermute | solution.py:11
  65.0 0.3 fusion.13
  65.3 0.3 fusion.25
  65.6 1.4 %collective-permute-done.24 = bf16[64,896]{1,0:T(8,128)(2,1)S(1)} collective-permute-done((bf16[64,896]{1,0:T(8,128)(2,1)S(1)}, bf16[64,896]{1,0:T(8,128)(2,1)S(1)}, u32[]{:S(2)}, u32[]{:S(2)}) %collective-permute-start.24) | collective-permute-done | bytes 114720 | tf_op jit(solution)/shard_map/ppermute | solution.py:11
  67.1 0.3 fusion.52
  67.4 0.3 convolution_add_fusion.3
  67.8 0.1 collective-permute-start.26
  67.9 1.0 %collective-permute-start.25 = (bf16[16,896]{1,0:T(8,128)(2,1)S(1)}, bf16[16,896]{1,0:T(8,128)(2,1)S(1)}, u32[]{:S(2)}, u32[]{:S(2)}) collective-permute-start(bf16[16,896]{1,0:T(8,128)(2,1)S(1)} %slice_bitcast_fusion), channel_id=1, source_target_pairs={{0,1},{1,0},{2,3},{3,2},{4,5},{5,4},{6,7},{7,6},{8,9},{9,8},{10,11... | collective-permute-start | bytes 86024 | tf_op jit(solution)/shard_map/ppermute | solution.py:11
  68.9 0.4 collective-permute-done.26
  69.4 0.9 %collective-permute-start.30 = (bf16[128,128]{1,0:T(8,128)(2,1)S(1)}, bf16[128,128]{1,0:T(8,128)(2,1)S(1)}, u32[]{:S(2)}, u32[]{:S(2)}) collective-permute-start(bf16[128,128]{1,0:T(8,128)(2,1)S(1)} %get-tuple-element.94), channel_id=1, source_target_pairs={{0,16},{8,24},{16,0},{24,8},{1,17},{9,25},{17,1},{25,9},{2,18},{10... | collective-permute-start | bytes 98312 | tf_op jit(solution)/shard_map/ppermute | solution.py:11
  70.3 0.7 collective-permute-start.29
  71.0 0.8 %collective-permute-done.25 = bf16[16,896]{1,0:T(8,128)(2,1)S(1)} collective-permute-done((bf16[16,896]{1,0:T(8,128)(2,1)S(1)}, bf16[16,896]{1,0:T(8,128)(2,1)S(1)}, u32[]{:S(2)}, u32[]{:S(2)}) %collective-permute-start.25) | collective-permute-done | bytes 28704 | tf_op jit(solution)/shard_map/ppermute | solution.py:11
  71.8 0.1 broadcast_select_fusion.1
  71.9 0.6 maximum_select_fusion
  72.6 0.8 %collective-permute-done.30 = bf16[128,128]{1,0:T(8,128)(2,1)S(1)} collective-permute-done((bf16[128,128]{1,0:T(8,128)(2,1)S(1)}, bf16[128,128]{1,0:T(8,128)(2,1)S(1)}, u32[]{:S(2)}, u32[]{:S(2)}) %collective-permute-start.30) | collective-permute-done | bytes 32800 | tf_op jit(solution)/shard_map/ppermute | solution.py:11
  73.3 0.9 %collective-permute-done.29 = bf16[128,128]{1,0:T(8,128)(2,1)S(1)} collective-permute-done((bf16[128,128]{1,0:T(8,128)(2,1)S(1)}, bf16[128,128]{1,0:T(8,128)(2,1)S(1)}, u32[]{:S(2)}, u32[]{:S(2)}) %collective-permute-start.29) | collective-permute-done | bytes 32800 | tf_op jit(solution)/shard_map/ppermute | solution.py:11
  74.2 0.5 fusion.42
  74.8 1.4 %fusion = bf16[1,3584,128]{2,1,0:T(8,128)(2,1)} fusion(bf16[128,1792]{1,0:T(8,128)(2,1)S(1)} %get-tuple-element.80, bf16[128,1792]{1,0:T(8,128)(2,1)S(1)} %get-tuple-element.79, f32[128,128]{1,0:T(8,128)S(1)} %slice_select_fusion.1, bf16[128,128]{1,0:T(8,128)(2,1)S(1)} %collective-permute-done.30, bf16[128,128]{1,0:T(8,128)(2,1)S(1)} %collective-permute-done.29, ...), kind=kOutput, calls=%fused_computation.1 | convolution fusion | flops 119832576 | bytes 2031616 | tf_op jit(solution)/shard_map/dot_general | solution.py:44
  (60 shorter events, 0.5 us)
Async XLA Ops:
  0.6 30.5 %copy-start = (s32[2,1,12]{2,1,0:T(1,128)S(1)}, s32[2,1,12]{2,1,0:T(1,128)}, u32[]{:S(2)}) copy-start(s32[2,1,12]{2,1,0:T(1,128)} %param.11) | copy-start | bytes 292
  0.6 21.3 %copy-start.2 = (bf16[1,3584,128]{2,1,0:T(8,128)(2,1)S(1)}, bf16[1,3584,128]{2,1,0:T(8,128)(2,1)}, u32[]{:S(2)}) copy-start(bf16[1,3584,128]{2,1,0:T(8,128)(2,1)} %param.8) | copy-start | bytes 2752516
  0.7 16.8 %collective-permute-start.3 = (bf16[3584,128]{1,0:T(8,128)(2,1)}, bf16[3584,128]{1,0:T(8,128)(2,1)}, u32[]{:S(2)}, u32[]{:S(2)}) collective-permute-start(bf16[3584,128]{1,0:T(8,128)(2,1)} %bitcast.112), channel_id=1, source_target_pairs={{0,8},{8,0},{16,24},{24,16},{1,9},{9,1},{17,25},{25,17},{2,10},{10... | collective-permute-start | bytes 2752520 | tf_op jit(solution)/shard_map/ppermute | solution.py:11
  1.2 21.9 %copy-start.3 = (f32[1,128]{1,0:T(1,128)S(1)}, f32[1,128]{1,0:T(1,128)}, u32[]{:S(2)}) copy-start(f32[1,128]{1,0:T(1,128)} %param.9) | copy-start | bytes 1540
  2.4 20.7 %collective-permute-start = (bf16[256,896]{1,0:T(8,128)(2,1)S(1)}, bf16[256,896]{1,0:T(8,128)(2,1)S(1)}, u32[]{:S(2)}, u32[]{:S(2)}) collective-permute-start(bf16[256,896]{1,0:T(8,128)(2,1)S(1)} %get-tuple-element.78), channel_id=1, source_target_pairs={{0,1},{1,0},{2,3},{3,2},{4,5},{5,4},{6,7},{7,6},{8,9},{9,8},{10,11... | collective-permute-start | bytes 1376264 | tf_op jit(solution)/shard_map/ppermute | solution.py:11
  5.1 18.0 %collective-permute-start.1 = (bf16[256,896]{1,0:T(8,128)(2,1)S(1)}, bf16[256,896]{1,0:T(8,128)(2,1)S(1)}, u32[]{:S(2)}, u32[]{:S(2)}) collective-permute-start(bf16[256,896]{1,0:T(8,128)(2,1)S(1)} %get-tuple-element.77), channel_id=1, source_target_pairs={{0,16},{8,24},{16,0},{24,8},{1,17},{9,25},{17,1},{25,9},{2,18},{10... | collective-permute-start | bytes 1376264 | tf_op jit(solution)/shard_map/ppermute | solution.py:11
  7.5 9.9 %collective-permute-start.2 = (bf16[16,1792]{1,0:T(8,128)(2,1)S(1)}, bf16[16,1792]{1,0:T(8,128)(2,1)S(1)}, u32[]{:S(2)}, u32[]{:S(2)}) collective-permute-start(bf16[16,1792]{1,0:T(8,128)(2,1)S(1)} %get-tuple-element.88), channel_id=1, source_target_pairs={{0,1},{1,0},{2,3},{3,2},{4,5},{5,4},{6,7},{7,6},{8,9},{9,8},{10,11... | collective-permute-start | bytes 172040 | tf_op jit(solution)/shard_map/ppermute | solution.py:11
  17.4 6.0 %collective-permute-start.4 = (bf16[32,1792]{1,0:T(8,128)(2,1)S(1)}, bf16[32,1792]{1,0:T(8,128)(2,1)S(1)}, u32[]{:S(2)}, u32[]{:S(2)}) collective-permute-start(bf16[32,1792]{1,0:T(8,128)(2,1)S(1)} %bitcast.103), channel_id=1, source_target_pairs={{0,2},{1,3},{2,0},{3,1},{4,6},{5,7},{6,4},{7,5},{8,10},{9,11},{10,... | collective-permute-start | bytes 344072 | tf_op jit(solution)/shard_map/ppermute | solution.py:11
  19.3 11.4 %collective-permute-start.5 = (bf16[32,1792]{1,0:T(8,128)(2,1)S(1)}, bf16[32,1792]{1,0:T(8,128)(2,1)S(1)}, u32[]{:S(2)}, u32[]{:S(2)}) collective-permute-start(bf16[32,1792]{1,0:T(8,128)(2,1)S(1)} %bitcast.104), channel_id=1, source_target_pairs={{0,4},{1,5},{2,6},{3,7},{4,0},{5,1},{6,2},{7,3},{8,12},{9,13},{10,... | collective-permute-start | bytes 344072 | tf_op jit(solution)/shard_map/ppermute | solution.py:11
  21.9 8.8 %collective-permute-start.6 = (bf16[32,1792]{1,0:T(8,128)(2,1)S(1)}, bf16[32,1792]{1,0:T(8,128)(2,1)S(1)}, u32[]{:S(2)}, u32[]{:S(2)}) collective-permute-start(bf16[32,1792]{1,0:T(8,128)(2,1)S(1)} %bitcast.105), channel_id=1, source_target_pairs={{0,6},{1,7},{2,4},{3,5},{4,2},{5,3},{6,0},{7,1},{8,14},{9,15},{10,... | collective-permute-start | bytes 344072 | tf_op jit(solution)/shard_map/ppermute | solution.py:11
  23.1 12.6 %copy-start.1 = (bf16[1,2,2,128,1792]{4,3,2,1,0:T(8,128)(2,1)S(1)}, bf16[1,2,2,128,1792]{4,3,2,1,0:T(8,128)(2,1)}, u32[]{:S(2)}) copy-start(bf16[1,2,2,128,1792]{4,3,2,1,0:T(8,128)(2,1)} %param.10) | copy-start | bytes 5505028
  31.1 1.4 %collective-permute-start.7 = (f32[128,256]{1,0:T(8,128)S(1)}, f32[128,256]{1,0:T(8,128)S(1)}, u32[]{:S(2)}, u32[]{:S(2)}) collective-permute-start(f32[128,256]{1,0:T(8,128)S(1)} %convolution_add_fusion.4), channel_id=1, source_target_pairs={{0,8},{8,0},{16,24},{24,16},{1,9},{9,1},{17,25},{25,17},{2,10},{10... | collective-permute-start | bytes 393224 | tf_op jit(solution)/shard_map/ppermute | solution.py:11
  32.5 5.0 %collective-permute-start.9 = (bf16[128,256]{1,0:T(8,128)(2,1)S(1)}, bf16[128,256]{1,0:T(8,128)(2,1)S(1)}, u32[]{:S(2)}, u32[]{:S(2)}) collective-permute-start(bf16[128,256]{1,0:T(8,128)(2,1)S(1)} %multiply_convert_fusion), channel_id=1, source_target_pairs={{0,16},{8,24},{16,0},{24,8},{1,17},{9,25},{17,1},{25,9},{2,18},{10... | collective-permute-start | bytes 196616 | tf_op jit(solution)/shard_map/ppermute | solution.py:11
  34.1 5.2 %collective-permute-start.8 = (bf16[128,256]{1,0:T(8,128)(2,1)S(1)}, bf16[128,256]{1,0:T(8,128)(2,1)S(1)}, u32[]{:S(2)}, u32[]{:S(2)}) collective-permute-start(bf16[128,256]{1,0:T(8,128)(2,1)S(1)} %bitcast.118), channel_id=1, source_target_pairs={{0,1},{1,0},{2,3},{3,2},{4,5},{5,4},{6,7},{7,6},{8,9},{9,8},{10,11... | collective-permute-start | bytes 196616 | tf_op jit(solution)/shard_map/ppermute | solution.py:11
  36.9 10.5 %collective-permute-start.17 = (bf16[16,896]{1,0:T(8,128)(2,1)S(1)}, bf16[16,896]{1,0:T(8,128)(2,1)S(1)}, u32[]{:S(2)}, u32[]{:S(2)}) collective-permute-start(bf16[16,896]{1,0:T(8,128)(2,1)S(1)} %get-tuple-element.81), channel_id=1, source_target_pairs={{0,1},{1,0},{2,3},{3,2},{4,5},{5,4},{6,7},{7,6},{8,9},{9,8},{10,11... | collective-permute-start | bytes 86024 | tf_op jit(solution)/shard_map/ppermute | solution.py:11
  37.7 6.5 %collective-permute-start.10 = (bf16[64,896]{1,0:T(8,128)(2,1)S(1)}, bf16[64,896]{1,0:T(8,128)(2,1)S(1)}, u32[]{:S(2)}, u32[]{:S(2)}) collective-permute-start(bf16[64,896]{1,0:T(8,128)(2,1)S(1)} %fusion.1), channel_id=1, source_target_pairs={{0,1},{1,0},{2,3},{3,2},{4,5},{5,4},{6,7},{7,6},{8,9},{9,8},{10,11... | collective-permute-start | bytes 344072 | tf_op jit(solution)/shard_map/ppermute | solution.py:11
  39.8 9.0 %collective-permute-start.15 = (bf16[32,896]{1,0:T(8,128)(2,1)S(1)}, bf16[32,896]{1,0:T(8,128)(2,1)S(1)}, u32[]{:S(2)}, u32[]{:S(2)}) collective-permute-start(bf16[32,896]{1,0:T(8,128)(2,1)S(1)} %get-tuple-element.85), channel_id=1, source_target_pairs={{0,4},{1,5},{2,6},{3,7},{4,0},{5,1},{6,2},{7,3},{8,12},{9,13},{10,... | collective-permute-start | bytes 172040 | tf_op jit(solution)/shard_map/ppermute | solution.py:11
  42.7 6.2 %collective-permute-start.16 = (bf16[32,896]{1,0:T(8,128)(2,1)S(1)}, bf16[32,896]{1,0:T(8,128)(2,1)S(1)}, u32[]{:S(2)}, u32[]{:S(2)}) collective-permute-start(bf16[32,896]{1,0:T(8,128)(2,1)S(1)} %get-tuple-element.84), channel_id=1, source_target_pairs={{0,6},{1,7},{2,4},{3,5},{4,2},{5,3},{6,0},{7,1},{8,14},{9,15},{10,... | collective-permute-start | bytes 172040 | tf_op jit(solution)/shard_map/ppermute | solution.py:11
  44.3 4.6 %collective-permute-start.12 = (bf16[16,896]{1,0:T(8,128)(2,1)S(1)}, bf16[16,896]{1,0:T(8,128)(2,1)S(1)}, u32[]{:S(2)}, u32[]{:S(2)}) collective-permute-start(bf16[16,896]{1,0:T(8,128)(2,1)S(1)} %get-tuple-element.93), channel_id=1, source_target_pairs={{0,2},{1,3},{2,0},{3,1},{4,6},{5,7},{6,4},{7,5},{8,10},{9,11},{10,... | collective-permute-start | bytes 86024 | tf_op jit(solution)/shard_map/ppermute | solution.py:11
  44.5 4.8 %collective-permute-start.13 = (bf16[16,896]{1,0:T(8,128)(2,1)S(1)}, bf16[16,896]{1,0:T(8,128)(2,1)S(1)}, u32[]{:S(2)}, u32[]{:S(2)}) collective-permute-start(bf16[16,896]{1,0:T(8,128)(2,1)S(1)} %get-tuple-element.92), channel_id=1, source_target_pairs={{0,4},{1,5},{2,6},{3,7},{4,0},{5,1},{6,2},{7,3},{8,12},{9,13},{10,... | collective-permute-start | bytes 86024 | tf_op jit(solution)/shard_map/ppermute | solution.py:11
  47.4 5.8 %collective-permute-start.14 = (bf16[16,896]{1,0:T(8,128)(2,1)S(1)}, bf16[16,896]{1,0:T(8,128)(2,1)S(1)}, u32[]{:S(2)}, u32[]{:S(2)}) collective-permute-start(bf16[16,896]{1,0:T(8,128)(2,1)S(1)} %get-tuple-element.91), channel_id=1, source_target_pairs={{0,6},{1,7},{2,4},{3,5},{4,2},{5,3},{6,0},{7,1},{8,14},{9,15},{10,... | collective-permute-start | bytes 86024 | tf_op jit(solution)/shard_map/ppermute | solution.py:11
  48.8 8.9 %collective-permute-start.11 = (bf16[32,896]{1,0:T(8,128)(2,1)S(1)}, bf16[32,896]{1,0:T(8,128)(2,1)S(1)}, u32[]{:S(2)}, u32[]{:S(2)}) collective-permute-start(bf16[32,896]{1,0:T(8,128)(2,1)S(1)} %get-tuple-element.49), channel_id=1, source_target_pairs={{0,2},{1,3},{2,0},{3,1},{4,6},{5,7},{6,4},{7,5},{8,10},{9,11},{10,... | collective-permute-start | bytes 172040 | tf_op jit(solution)/shard_map/ppermute | solution.py:11
  53.2 6.1 %collective-permute-start.23 = (bf16[16,896]{1,0:T(8,128)(2,1)S(1)}, bf16[16,896]{1,0:T(8,128)(2,1)S(1)}, u32[]{:S(2)}, u32[]{:S(2)}) collective-permute-start(bf16[16,896]{1,0:T(8,128)(2,1)S(1)} %subtract_convert_fusion), channel_id=1, source_target_pairs={{0,6},{1,7},{2,4},{3,5},{4,2},{5,3},{6,0},{7,1},{8,14},{9,15},{10,... | collective-permute-start | bytes 86024 | tf_op jit(solution)/shard_map/ppermute | solution.py:11
  54.5 7.7 %collective-permute-start.22 = (bf16[16,896]{1,0:T(8,128)(2,1)S(1)}, bf16[16,896]{1,0:T(8,128)(2,1)S(1)}, u32[]{:S(2)}, u32[]{:S(2)}) collective-permute-start(bf16[16,896]{1,0:T(8,128)(2,1)S(1)} %subtract_convert_fusion), channel_id=1, source_target_pairs={{0,4},{1,5},{2,6},{3,7},{4,0},{5,1},{6,2},{7,3},{8,12},{9,13},{10,... | collective-permute-start | bytes 86024 | tf_op jit(solution)/shard_map/ppermute | solution.py:11
  54.5 7.7 %collective-permute-start.21 = (bf16[16,896]{1,0:T(8,128)(2,1)S(1)}, bf16[16,896]{1,0:T(8,128)(2,1)S(1)}, u32[]{:S(2)}, u32[]{:S(2)}) collective-permute-start(bf16[16,896]{1,0:T(8,128)(2,1)S(1)} %subtract_convert_fusion), channel_id=1, source_target_pairs={{0,2},{1,3},{2,0},{3,1},{4,6},{5,7},{6,4},{7,5},{8,10},{9,11},{10,... | collective-permute-start | bytes 86024 | tf_op jit(solution)/shard_map/ppermute | solution.py:11
  57.7 6.1 %collective-permute-start.20 = (bf16[32,896]{1,0:T(8,128)(2,1)S(1)}, bf16[32,896]{1,0:T(8,128)(2,1)S(1)}, u32[]{:S(2)}, u32[]{:S(2)}) collective-permute-start(bf16[32,896]{1,0:T(8,128)(2,1)S(1)} %fusion.24), channel_id=1, source_target_pairs={{0,6},{1,7},{2,4},{3,5},{4,2},{5,3},{6,0},{7,1},{8,14},{9,15},{10,... | collective-permute-start | bytes 172040 | tf_op jit(solution)/shard_map/ppermute | solution.py:11
  59.0 6.0 %collective-permute-start.19 = (bf16[32,896]{1,0:T(8,128)(2,1)S(1)}, bf16[32,896]{1,0:T(8,128)(2,1)S(1)}, u32[]{:S(2)}, u32[]{:S(2)}) collective-permute-start(bf16[32,896]{1,0:T(8,128)(2,1)S(1)} %fusion.24), channel_id=1, source_target_pairs={{0,4},{1,5},{2,6},{3,7},{4,0},{5,1},{6,2},{7,3},{8,12},{9,13},{10,... | collective-permute-start | bytes 172040 | tf_op jit(solution)/shard_map/ppermute | solution.py:11
  59.3 5.7 %collective-permute-start.18 = (bf16[32,896]{1,0:T(8,128)(2,1)S(1)}, bf16[32,896]{1,0:T(8,128)(2,1)S(1)}, u32[]{:S(2)}, u32[]{:S(2)}) collective-permute-start(bf16[32,896]{1,0:T(8,128)(2,1)S(1)} %fusion.24), channel_id=1, source_target_pairs={{0,2},{1,3},{2,0},{3,1},{4,6},{5,7},{6,4},{7,5},{8,10},{9,11},{10,... | collective-permute-start | bytes 172040 | tf_op jit(solution)/shard_map/ppermute | solution.py:11
  62.2 4.9 %collective-permute-start.24 = (bf16[64,896]{1,0:T(8,128)(2,1)S(1)}, bf16[64,896]{1,0:T(8,128)(2,1)S(1)}, u32[]{:S(2)}, u32[]{:S(2)}) collective-permute-start(bf16[64,896]{1,0:T(8,128)(2,1)S(1)} %pad_maximum_fusion.5), channel_id=1, source_target_pairs={{0,1},{1,0},{2,3},{3,2},{4,5},{5,4},{6,7},{7,6},{8,9},{9,8},{10,11... | collective-permute-start | bytes 344072 | tf_op jit(solution)/shard_map/ppermute | solution.py:11
  63.2 6.1 %collective-permute-start.27 = (bf16[16,896]{1,0:T(8,128)(2,1)S(1)}, bf16[16,896]{1,0:T(8,128)(2,1)S(1)}, u32[]{:S(2)}, u32[]{:S(2)}) collective-permute-start(bf16[16,896]{1,0:T(8,128)(2,1)S(1)} %subtract_convert_fusion), channel_id=1, source_target_pairs={{0,16},{8,24},{16,0},{24,8},{1,17},{9,25},{17,1},{25,9},{2,18},{10... | collective-permute-start | bytes 86024 | tf_op jit(solution)/shard_map/ppermute | solution.py:11
  63.8 5.5 %collective-permute-start.28 = (bf16[128,1792]{1,0:T(8,128)(2,1)S(1)}, bf16[128,1792]{1,0:T(8,128)(2,1)S(1)}, u32[]{:S(2)}, u32[]{:S(2)}) collective-permute-start(bf16[128,1792]{1,0:T(8,128)(2,1)S(1)} %constant_dynamic-update-slice_fusion), channel_id=1, source_target_pairs={{0,8},{8,0},{16,24},{24,16},{1,9},{9,1},{17,25},{25,17},{2,10},{10... | collective-permute-start | bytes 1376264 | tf_op jit(solution)/shard_map/ppermute | solution.py:11
  67.8 1.5 %collective-permute-start.26 = (f32[384,128]{1,0:T(8,128)S(1)}, f32[384,128]{1,0:T(8,128)S(1)}, u32[]{:S(2)}, u32[]{:S(2)}) collective-permute-start(f32[384,128]{1,0:T(8,128)S(1)} %slice_select_fusion), channel_id=1, source_target_pairs={{0,8},{8,0},{16,24},{24,16},{1,9},{9,1},{17,25},{25,17},{2,10},{10... | collective-permute-start | bytes 589832 | tf_op jit(solution)/shard_map/ppermute | solution.py:11
  67.9 3.9 %collective-permute-start.25 = (bf16[16,896]{1,0:T(8,128)(2,1)S(1)}, bf16[16,896]{1,0:T(8,128)(2,1)S(1)}, u32[]{:S(2)}, u32[]{:S(2)}) collective-permute-start(bf16[16,896]{1,0:T(8,128)(2,1)S(1)} %slice_bitcast_fusion), channel_id=1, source_target_pairs={{0,1},{1,0},{2,3},{3,2},{4,5},{5,4},{6,7},{7,6},{8,9},{9,8},{10,11... | collective-permute-start | bytes 86024 | tf_op jit(solution)/shard_map/ppermute | solution.py:11
  69.4 4.0 %collective-permute-start.30 = (bf16[128,128]{1,0:T(8,128)(2,1)S(1)}, bf16[128,128]{1,0:T(8,128)(2,1)S(1)}, u32[]{:S(2)}, u32[]{:S(2)}) collective-permute-start(bf16[128,128]{1,0:T(8,128)(2,1)S(1)} %get-tuple-element.94), channel_id=1, source_target_pairs={{0,16},{8,24},{16,0},{24,8},{1,17},{9,25},{17,1},{25,9},{2,18},{10... | collective-permute-start | bytes 98312 | tf_op jit(solution)/shard_map/ppermute | solution.py:11
  70.3 3.9 %collective-permute-start.29 = (bf16[128,128]{1,0:T(8,128)(2,1)S(1)}, bf16[128,128]{1,0:T(8,128)(2,1)S(1)}, u32[]{:S(2)}, u32[]{:S(2)}) collective-permute-start(bf16[128,128]{1,0:T(8,128)(2,1)S(1)} %get-tuple-element.95), channel_id=1, source_target_pairs={{0,1},{1,0},{2,3},{3,2},{4,5},{5,4},{6,7},{7,6},{8,9},{9,8},{10,11... | collective-permute-start | bytes 98312 | tf_op jit(solution)/shard_map/ppermute | solution.py:11

commit v22 on v21

--- a/solution.py
+++ b/solution.py
@@ -108,8 +108,9 @@
     pair, weight_other, bias, blocks = hold((paired(mine, over_x(mine)), weight_other, enc_bias[0], blocks))
     column = along_z(pair)
 
-    own_other = over_x(decoder_part(decoder, layer, 1 - side))
-    shared_other = over_y(decoder_part(decoder, 1 - layer, 1 - layer))
+    after, _ = hold((decoder, mine))
+    own_other = over_x(decoder_part(after, layer, 1 - side))
+    shared_other = over_y(decoder_part(after, 1 - layer, 1 - layer))
     decoder, own_other, shared_other, *column = hold((decoder, own_other, shared_other, *column))
     own_mine, shared_mine = decoder_part(decoder, layer, side), decoder_part(decoder, 1 - layer, layer)
     resid_half = jnp.concatenate(column, axis=0)

time: 76.4 us -> 66.4 us (0.87)
  waiting for transfers between devices: 28 us -> 17.5 us
    ppermute x31, waiting for transfers between devices: 28 us -> 17.5 us  [crossed(): lax.ppermute(block, axis, [(i, i ^ mask) for i in range(lax.axis_size(axi...]
  transfers between devices with their start and end apart: 31 -> 31, of which waited for: 13 -> 12; matrix products, arithmetic and copies ran while one was open for 10% -> 12% of each run, Pallas kernels for 0% -> 0%
where the time goes in v22:
time: 66.4 us; the launch traced here: 66.1 us
  starting transfers between devices  37.5 us (56%)
  waiting for transfers between devices  17.5 us (26%)
  matrix products  4.15 us (6%)
  local copies, waits for them, and re-layouts  3.02 us (5%)
  other arithmetic  2.95 us (4%)
  between operations  1.04 us (2%)
    ppermute x31, starting transfers between devices, crossed(): lax.ppermute(block, axis, [(i, i ^ mask) for i in range(lax.axis_size(axi...  37.5 us
    ppermute x31, waiting for transfers between devices, crossed(): lax.ppermute(block, axis, [(i, i ^ mask) for i in range(lax.axis_size(axi...  17.5 us
    dot_general x7, matrix products, times(): return jnp.dot(left, right, preferred_element_type=F32)  1.6 us
    dot_general x1, matrix products, encoder_gradient(): lax.dot_general(whole, grad_low, (((0,), (0,)), ((), ())), preferred_elem...  1.36 us
  transfers between devices with their start and end apart: 31, of which 12 were waited for; matrix products, arithmetic and copies ran while one was open for 12% of the time, Pallas kernels for 0%

profile of v22, /device:TPU:0, one launch (start us, length us, event | category | flops | bytes accessed | tf_op | source)
XLA Modules:
  0.0 66.1 jit_solution(5712614683401849983)
XLA Ops:
  0.6 0.0 copy-start
  0.7 0.5 collective-permute-start.3
  1.2 0.8 %dynamic-slice_bitcast_fusion.2 = (bf16[1,1,16,1792]{3,2,1,0:T(8,128)(2,1)S(1)}, bf16[16,1792]{1,0:T(8,128)(2,1)S(1)}) fusion(bf16[2,16,3584]{2,1,0:T(8,128)(2,1)} %param.6, s32[]{:T(128)S(6)} %select_n.169, s32[]{:T(128)S(6)} %select_n.171), kind=kLoop, calls=%fused_computation.54 | loop fusion | bytes 172040 | tf_op jit(solution)/shard_map/reshape;squeeze | solution.py:100
  2.0 2.6 %collective-permute-start.2 = (bf16[16,1792]{1,0:T(8,128)(2,1)S(1)}, bf16[16,1792]{1,0:T(8,128)(2,1)S(1)}, u32[]{:S(2)}, u32[]{:S(2)}) collective-permute-start(bf16[16,1792]{1,0:T(8,128)(2,1)S(1)} %get-tuple-element.90), channel_id=1, source_target_pairs={{0,1},{1,0},{2,3},{3,2},{4,5},{5,4},{6,7},{7,6},{8,9},{9,8},{10,11... | collective-permute-start | bytes 172040 | tf_op jit(solution)/shard_map/ppermute | solution.py:11
  4.6 1.2 %dynamic-slice_bitcast_fusion = (bf16[256,896]{1,0:T(8,128)(2,1)S(1)}, bf16[256,896]{1,0:T(8,128)(2,1)S(1)}) fusion(bf16[2,256,1792]{2,1,0:T(8,128)(2,1)} %bitcast.92, s32[]{:T(128)S(6)} %select_n.173, s32[]{:T(128)S(6)} %select_n.174, s32[]{:T(128)S(6)} %select_n.169, s32[]{:T(128)S(6)} %select_n.172), kind=kLoop, calls=%fused_computation.24 | loop fusion | bytes 1835024 | tf_op jit(solution)/shard_map/squeeze | solution.py:91
  5.9 0.1 collective-permute-start
  6.0 2.0 %collective-permute-start.1 = (bf16[256,896]{1,0:T(8,128)(2,1)S(1)}, bf16[256,896]{1,0:T(8,128)(2,1)S(1)}, u32[]{:S(2)}, u32[]{:S(2)}) collective-permute-start(bf16[256,896]{1,0:T(8,128)(2,1)S(1)} %get-tuple-element.79), channel_id=1, source_target_pairs={{0,16},{8,24},{16,0},{24,8},{1,17},{9,25},{17,1},{25,9},{2,18},{10... | collective-permute-start | bytes 1376264 | tf_op jit(solution)/shard_map/ppermute | solution.py:11
  8.0 1.6 %collective-permute-start.4 = (bf16[32,1792]{1,0:T(8,128)(2,1)S(1)}, bf16[32,1792]{1,0:T(8,128)(2,1)S(1)}, u32[]{:S(2)}, u32[]{:S(2)}) collective-permute-start(bf16[32,1792]{1,0:T(8,128)(2,1)S(1)} %bitcast.103), channel_id=1, source_target_pairs={{0,2},{1,3},{2,0},{3,1},{4,6},{5,7},{6,4},{7,5},{8,10},{9,11},{10,... | collective-permute-start | bytes 344072 | tf_op jit(solution)/shard_map/ppermute | solution.py:11
  9.7 2.6 %collective-permute-start.5 = (bf16[32,1792]{1,0:T(8,128)(2,1)S(1)}, bf16[32,1792]{1,0:T(8,128)(2,1)S(1)}, u32[]{:S(2)}, u32[]{:S(2)}) collective-permute-start(bf16[32,1792]{1,0:T(8,128)(2,1)S(1)} %bitcast.104), channel_id=1, source_target_pairs={{0,4},{1,5},{2,6},{3,7},{4,0},{5,1},{6,2},{7,3},{8,12},{9,13},{10,... | collective-permute-start | bytes 344072 | tf_op jit(solution)/shard_map/ppermute | solution.py:11
  12.3 0.2 collective-permute-start.6
  12.5 1.2 %bitcast_select_fusion.1 = (bf16[1792,128]{1,0:T(8,128)(2,1)S(1)}, bf16[1792,128]{1,0:T(8,128)(2,1)S(1)}) fusion(pred[]{:T(512)S(6)} %eq.48, bf16[3584,128]{1,0:T(8,128)(2,1)} %collective-permute-done.3, s32[]{:T(128)S(6)} %select_n.171, bf16[1,3584,128]{2,1,0:T(8,128)(2,1)S(1)} %copy-done.2), kind=kLoop, calls=%fused_computation.23 | loop fusion | flops 458752 | bytes 1835013 | tf_op jit(solution)/shard_map/jit(_where)/select_n | solution.py:23
  13.7 0.0 copy-start.1
  13.8 4.7 %collective-permute-done = bf16[256,896]{1,0:T(8,128)(2,1)S(1)} collective-permute-done((bf16[256,896]{1,0:T(8,128)(2,1)S(1)}, bf16[256,896]{1,0:T(8,128)(2,1)S(1)}, u32[]{:S(2)}, u32[]{:S(2)}) %collective-permute-start) | collective-permute-done | bytes 458784 | tf_op jit(solution)/shard_map/ppermute | solution.py:11
  18.5 0.1 collective-permute-done.1
  18.5 2.5 %collective-permute-done.5 = bf16[32,1792]{1,0:T(8,128)(2,1)S(1)} collective-permute-done((bf16[32,1792]{1,0:T(8,128)(2,1)S(1)}, bf16[32,1792]{1,0:T(8,128)(2,1)S(1)}, u32[]{:S(2)}, u32[]{:S(2)}) %collective-permute-start.5) | collective-permute-done | bytes 114720 | tf_op jit(solution)/shard_map/ppermute | solution.py:11
  21.1 0.3 convolution_add_fusion.4
  21.4 0.1 collective-permute-start.7
  21.5 0.1 compare_reduce_fusion
  21.6 1.2 %collective-permute-done.7 = f32[128,256]{1,0:T(8,128)S(1)} collective-permute-done((f32[128,256]{1,0:T(8,128)S(1)}, f32[128,256]{1,0:T(8,128)S(1)}, u32[]{:S(2)}, u32[]{:S(2)}) %collective-permute-start.7) | collective-permute-done | bytes 131104 | tf_op jit(solution)/shard_map/ppermute | solution.py:11
  22.9 0.9 %collective-permute-start.9 = (bf16[128,256]{1,0:T(8,128)(2,1)S(1)}, bf16[128,256]{1,0:T(8,128)(2,1)S(1)}, u32[]{:S(2)}, u32[]{:S(2)}) collective-permute-start(bf16[128,256]{1,0:T(8,128)(2,1)S(1)} %multiply_convert_fusion), channel_id=1, source_target_pairs={{0,16},{8,24},{16,0},{24,8},{1,17},{9,25},{17,1},{25,9},{2,18},{10... | collective-permute-start | bytes 196616 | tf_op jit(solution)/shard_map/ppermute | solution.py:11
  23.8 1.6 %collective-permute-start.8 = (bf16[128,256]{1,0:T(8,128)(2,1)S(1)}, bf16[128,256]{1,0:T(8,128)(2,1)S(1)}, u32[]{:S(2)}, u32[]{:S(2)}) collective-permute-start(bf16[128,256]{1,0:T(8,128)(2,1)S(1)} %bitcast.118), channel_id=1, source_target_pairs={{0,1},{1,0},{2,3},{3,2},{4,5},{5,4},{6,7},{7,6},{8,9},{9,8},{10,11... | collective-permute-start | bytes 196616 | tf_op jit(solution)/shard_map/ppermute | solution.py:11
  25.4 0.2 fusion.11
  25.6 0.2 fusion.9
  25.8 0.8 %dynamic-slice_bitcast_fusion.4 = (bf16[16,896]{1,0:T(8,128)(2,1)S(1)}, bf16[16,896]{1,0:T(8,128)(2,1)S(1)}, bf16[16,896]{1,0:T(8,128)(2,1)S(1)}) fusion(bf16[3,16,3584]{2,1,0:T(8,128)(2,1)} %param.7, s32[]{:T(128)S(6)} %select_n.186, s32[]{:T(128)S(6)} %select_n.189, s32[]{:T(128)S(6)} %select_n.188, s32[]{:T(128)S(6)} %select_n.187), kind=kLoop, calls=%fused_computation.62 | loop fusion | bytes 172048 | tf_op jit(solution)/shard_map/squeeze | solution.py:127
  26.6 0.6 collective-permute-start.17
  27.2 0.2 fusion.1
  27.4 1.5 %collective-permute-start.10 = (bf16[64,896]{1,0:T(8,128)(2,1)S(1)}, bf16[64,896]{1,0:T(8,128)(2,1)S(1)}, u32[]{:S(2)}, u32[]{:S(2)}) collective-permute-start(bf16[64,896]{1,0:T(8,128)(2,1)S(1)} %fusion.1), channel_id=1, source_target_pairs={{0,1},{1,0},{2,3},{3,2},{4,5},{5,4},{6,7},{7,6},{8,9},{9,8},{10,11... | collective-permute-start | bytes 344072 | tf_op jit(solution)/shard_map/ppermute | solution.py:11
  29.0 0.2 fusion.51
  29.2 0.2 fusion.50
  29.5 2.9 %collective-permute-start.15 = (bf16[32,896]{1,0:T(8,128)(2,1)S(1)}, bf16[32,896]{1,0:T(8,128)(2,1)S(1)}, u32[]{:S(2)}, u32[]{:S(2)}) collective-permute-start(bf16[32,896]{1,0:T(8,128)(2,1)S(1)} %get-tuple-element.87), channel_id=1, source_target_pairs={{0,4},{1,5},{2,6},{3,7},{4,0},{5,1},{6,2},{7,3},{8,12},{9,13},{10,... | collective-permute-start | bytes 172040 | tf_op jit(solution)/shard_map/ppermute | solution.py:11
  32.4 1.4 %collective-permute-start.16 = (bf16[32,896]{1,0:T(8,128)(2,1)S(1)}, bf16[32,896]{1,0:T(8,128)(2,1)S(1)}, u32[]{:S(2)}, u32[]{:S(2)}) collective-permute-start(bf16[32,896]{1,0:T(8,128)(2,1)S(1)} %get-tuple-element.86), channel_id=1, source_target_pairs={{0,6},{1,7},{2,4},{3,5},{4,2},{5,3},{6,0},{7,1},{8,14},{9,15},{10,... | collective-permute-start | bytes 172040 | tf_op jit(solution)/shard_map/ppermute | solution.py:11
  33.7 0.2 convolution_add_fusion.1
  34.0 0.2 collective-permute-start.12
  34.2 2.9 %collective-permute-start.13 = (bf16[16,896]{1,0:T(8,128)(2,1)S(1)}, bf16[16,896]{1,0:T(8,128)(2,1)S(1)}, u32[]{:S(2)}, u32[]{:S(2)}) collective-permute-start(bf16[16,896]{1,0:T(8,128)(2,1)S(1)} %get-tuple-element.94), channel_id=1, source_target_pairs={{0,4},{1,5},{2,6},{3,7},{4,0},{5,1},{6,2},{7,3},{8,12},{9,13},{10,... | collective-permute-start | bytes 86024 | tf_op jit(solution)/shard_map/ppermute | solution.py:11
  37.1 1.4 %collective-permute-start.14 = (bf16[16,896]{1,0:T(8,128)(2,1)S(1)}, bf16[16,896]{1,0:T(8,128)(2,1)S(1)}, u32[]{:S(2)}, u32[]{:S(2)}) collective-permute-start(bf16[16,896]{1,0:T(8,128)(2,1)S(1)} %get-tuple-element.93), channel_id=1, source_target_pairs={{0,6},{1,7},{2,4},{3,5},{4,2},{5,3},{6,0},{7,1},{8,14},{9,15},{10,... | collective-permute-start | bytes 86024 | tf_op jit(solution)/shard_map/ppermute | solution.py:11
  38.5 0.1 collective-permute-start.11
  38.6 0.4 collective-permute-done.13
  39.0 3.9 %collective-permute-done.14 = bf16[16,896]{1,0:T(8,128)(2,1)S(1)} collective-permute-done((bf16[16,896]{1,0:T(8,128)(2,1)S(1)}, bf16[16,896]{1,0:T(8,128)(2,1)S(1)}, u32[]{:S(2)}, u32[]{:S(2)}) %collective-permute-start.14) | collective-permute-done | bytes 28704 | tf_op jit(solution)/shard_map/ppermute | solution.py:11
  42.9 1.3 %collective-permute-start.23 = (bf16[16,896]{1,0:T(8,128)(2,1)S(1)}, bf16[16,896]{1,0:T(8,128)(2,1)S(1)}, u32[]{:S(2)}, u32[]{:S(2)}) collective-permute-start(bf16[16,896]{1,0:T(8,128)(2,1)S(1)} %subtract_convert_fusion), channel_id=1, source_target_pairs={{0,6},{1,7},{2,4},{3,5},{4,2},{5,3},{6,0},{7,1},{8,14},{9,15},{10,... | collective-permute-start | bytes 86024 | tf_op jit(solution)/shard_map/ppermute | solution.py:11
  44.2 3.1 %collective-permute-start.21 = (bf16[16,896]{1,0:T(8,128)(2,1)S(1)}, bf16[16,896]{1,0:T(8,128)(2,1)S(1)}, u32[]{:S(2)}, u32[]{:S(2)}) collective-permute-start(bf16[16,896]{1,0:T(8,128)(2,1)S(1)} %subtract_convert_fusion), channel_id=1, source_target_pairs={{0,2},{1,3},{2,0},{3,1},{4,6},{5,7},{6,4},{7,5},{8,10},{9,11},{10,... | collective-permute-start | bytes 86024 | tf_op jit(solution)/shard_map/ppermute | solution.py:11
  47.4 1.3 %collective-permute-start.20 = (bf16[32,896]{1,0:T(8,128)(2,1)S(1)}, bf16[32,896]{1,0:T(8,128)(2,1)S(1)}, u32[]{:S(2)}, u32[]{:S(2)}) collective-permute-start(bf16[32,896]{1,0:T(8,128)(2,1)S(1)} %fusion.24), channel_id=1, source_target_pairs={{0,6},{1,7},{2,4},{3,5},{4,2},{5,3},{6,0},{7,1},{8,14},{9,15},{10,... | collective-permute-start | bytes 172040 | tf_op jit(solution)/shard_map/ppermute | solution.py:11
  48.7 0.2 collective-permute-start.19
  49.0 0.0 collective-permute-done.23
  49.0 2.9 %collective-permute-start.18 = (bf16[32,896]{1,0:T(8,128)(2,1)S(1)}, bf16[32,896]{1,0:T(8,128)(2,1)S(1)}, u32[]{:S(2)}, u32[]{:S(2)}) collective-permute-start(bf16[32,896]{1,0:T(8,128)(2,1)S(1)} %fusion.24), channel_id=1, source_target_pairs={{0,2},{1,3},{2,0},{3,1},{4,6},{5,7},{6,4},{7,5},{8,10},{9,11},{10,... | collective-permute-start | bytes 172040 | tf_op jit(solution)/shard_map/ppermute | solution.py:11
  51.9 1.0 %collective-permute-start.24 = (bf16[64,896]{1,0:T(8,128)(2,1)S(1)}, bf16[64,896]{1,0:T(8,128)(2,1)S(1)}, u32[]{:S(2)}, u32[]{:S(2)}) collective-permute-start(bf16[64,896]{1,0:T(8,128)(2,1)S(1)} %pad_maximum_fusion.5), channel_id=1, source_target_pairs={{0,1},{1,0},{2,3},{3,2},{4,5},{5,4},{6,7},{7,6},{8,9},{9,8},{10,11... | collective-permute-start | bytes 344072 | tf_op jit(solution)/shard_map/ppermute | solution.py:11
  52.9 1.2 %collective-permute-start.27 = (bf16[16,896]{1,0:T(8,128)(2,1)S(1)}, bf16[16,896]{1,0:T(8,128)(2,1)S(1)}, u32[]{:S(2)}, u32[]{:S(2)}) collective-permute-start(bf16[16,896]{1,0:T(8,128)(2,1)S(1)} %subtract_convert_fusion), channel_id=1, source_target_pairs={{0,16},{8,24},{16,0},{24,8},{1,17},{9,25},{17,1},{25,9},{2,18},{10... | collective-permute-start | bytes 86024 | tf_op jit(solution)/shard_map/ppermute | solution.py:11
  54.1 0.6 collective-permute-done.19
  54.7 0.3 fusion.13
  55.0 0.3 fusion.25
  55.3 1.4 %collective-permute-done.24 = bf16[64,896]{1,0:T(8,128)(2,1)S(1)} collective-permute-done((bf16[64,896]{1,0:T(8,128)(2,1)S(1)}, bf16[64,896]{1,0:T(8,128)(2,1)S(1)}, u32[]{:S(2)}, u32[]{:S(2)}) %collective-permute-start.24) | collective-permute-done | bytes 114720 | tf_op jit(solution)/shard_map/ppermute | solution.py:11
  56.8 0.3 fusion.52
  57.1 0.3 convolution_add_fusion.3
  57.5 0.1 collective-permute-start.26
  57.6 1.0 %collective-permute-start.25 = (bf16[16,896]{1,0:T(8,128)(2,1)S(1)}, bf16[16,896]{1,0:T(8,128)(2,1)S(1)}, u32[]{:S(2)}, u32[]{:S(2)}) collective-permute-start(bf16[16,896]{1,0:T(8,128)(2,1)S(1)} %slice_bitcast_fusion), channel_id=1, source_target_pairs={{0,1},{1,0},{2,3},{3,2},{4,5},{5,4},{6,7},{7,6},{8,9},{9,8},{10,11... | collective-permute-start | bytes 86024 | tf_op jit(solution)/shard_map/ppermute | solution.py:11
  58.6 0.4 collective-permute-done.26
  59.1 1.3 %collective-permute-start.30 = (bf16[128,128]{1,0:T(8,128)(2,1)S(1)}, bf16[128,128]{1,0:T(8,128)(2,1)S(1)}, u32[]{:S(2)}, u32[]{:S(2)}) collective-permute-start(bf16[128,128]{1,0:T(8,128)(2,1)S(1)} %get-tuple-element.96), channel_id=1, source_target_pairs={{0,16},{8,24},{16,0},{24,8},{1,17},{9,25},{17,1},{25,9},{2,18},{10... | collective-permute-start | bytes 98312 | tf_op jit(solution)/shard_map/ppermute | solution.py:11
  60.3 0.9 %collective-permute-start.29 = (bf16[128,128]{1,0:T(8,128)(2,1)S(1)}, bf16[128,128]{1,0:T(8,128)(2,1)S(1)}, u32[]{:S(2)}, u32[]{:S(2)}) collective-permute-start(bf16[128,128]{1,0:T(8,128)(2,1)S(1)} %get-tuple-element.97), channel_id=1, source_target_pairs={{0,1},{1,0},{2,3},{3,2},{4,5},{5,4},{6,7},{7,6},{8,9},{9,8},{10,11... | collective-permute-start | bytes 98312 | tf_op jit(solution)/shard_map/ppermute | solution.py:11
  61.3 0.2 collective-permute-done.25
  61.5 0.1 broadcast_select_fusion.1
  61.6 0.6 maximum_select_fusion
  62.3 0.8 %collective-permute-done.30 = bf16[128,128]{1,0:T(8,128)(2,1)S(1)} collective-permute-done((bf16[128,128]{1,0:T(8,128)(2,1)S(1)}, bf16[128,128]{1,0:T(8,128)(2,1)S(1)}, u32[]{:S(2)}, u32[]{:S(2)}) %collective-permute-start.30) | collective-permute-done | bytes 32800 | tf_op jit(solution)/shard_map/ppermute | solution.py:11
  63.1 1.2 %collective-permute-done.29 = bf16[128,128]{1,0:T(8,128)(2,1)S(1)} collective-permute-done((bf16[128,128]{1,0:T(8,128)(2,1)S(1)}, bf16[128,128]{1,0:T(8,128)(2,1)S(1)}, u32[]{:S(2)}, u32[]{:S(2)}) %collective-permute-start.29) | collective-permute-done | bytes 32800 | tf_op jit(solution)/shard_map/ppermute | solution.py:11
  64.2 0.5 fusion.42
  64.8 1.4 %fusion = bf16[1,3584,128]{2,1,0:T(8,128)(2,1)} fusion(bf16[128,1792]{1,0:T(8,128)(2,1)S(1)} %get-tuple-element.82, bf16[128,1792]{1,0:T(8,128)(2,1)S(1)} %get-tuple-element.81, f32[128,128]{1,0:T(8,128)S(1)} %slice_select_fusion.1, bf16[128,128]{1,0:T(8,128)(2,1)S(1)} %collective-permute-done.30, bf16[128,128]{1,0:T(8,128)(2,1)S(1)} %collective-permute-done.29, ...), kind=kOutput, calls=%fused_computation.1 | convolution fusion | flops 119832576 | bytes 2031616 | tf_op jit(solution)/shard_map/dot_general | solution.py:44
  (60 shorter events, 0.5 us)
Async XLA Ops:
  0.6 20.9 %copy-start = (s32[2,1,12]{2,1,0:T(1,128)S(1)}, s32[2,1,12]{2,1,0:T(1,128)}, u32[]{:S(2)}) copy-start(s32[2,1,12]{2,1,0:T(1,128)} %param.11) | copy-start | bytes 292
  0.6 11.9 %copy-start.2 = (bf16[1,3584,128]{2,1,0:T(8,128)(2,1)S(1)}, bf16[1,3584,128]{2,1,0:T(8,128)(2,1)}, u32[]{:S(2)}) copy-start(bf16[1,3584,128]{2,1,0:T(8,128)(2,1)} %param.8) | copy-start | bytes 2752516
  0.7 7.4 %collective-permute-start.3 = (bf16[3584,128]{1,0:T(8,128)(2,1)}, bf16[3584,128]{1,0:T(8,128)(2,1)}, u32[]{:S(2)}, u32[]{:S(2)}) collective-permute-start(bf16[3584,128]{1,0:T(8,128)(2,1)} %bitcast.112), channel_id=1, source_target_pairs={{0,8},{8,0},{16,24},{24,16},{1,9},{9,1},{17,25},{25,17},{2,10},{10... | collective-permute-start | bytes 2752520 | tf_op jit(solution)/shard_map/ppermute | solution.py:11
  2.0 6.0 %collective-permute-start.2 = (bf16[16,1792]{1,0:T(8,128)(2,1)S(1)}, bf16[16,1792]{1,0:T(8,128)(2,1)S(1)}, u32[]{:S(2)}, u32[]{:S(2)}) collective-permute-start(bf16[16,1792]{1,0:T(8,128)(2,1)S(1)} %get-tuple-element.90), channel_id=1, source_target_pairs={{0,1},{1,0},{2,3},{3,2},{4,5},{5,4},{6,7},{7,6},{8,9},{9,8},{10,11... | collective-permute-start | bytes 172040 | tf_op jit(solution)/shard_map/ppermute | solution.py:11
  4.6 9.1 %copy-start.3 = (f32[1,128]{1,0:T(1,128)S(1)}, f32[1,128]{1,0:T(1,128)}, u32[]{:S(2)}) copy-start(f32[1,128]{1,0:T(1,128)} %param.9) | copy-start | bytes 1540
  5.9 12.6 %collective-permute-start = (bf16[256,896]{1,0:T(8,128)(2,1)S(1)}, bf16[256,896]{1,0:T(8,128)(2,1)S(1)}, u32[]{:S(2)}, u32[]{:S(2)}) collective-permute-start(bf16[256,896]{1,0:T(8,128)(2,1)S(1)} %get-tuple-element.80), channel_id=1, source_target_pairs={{0,1},{1,0},{2,3},{3,2},{4,5},{5,4},{6,7},{7,6},{8,9},{9,8},{10,11... | collective-permute-start | bytes 1376264 | tf_op jit(solution)/shard_map/ppermute | solution.py:11
  6.0 12.5 %collective-permute-start.1 = (bf16[256,896]{1,0:T(8,128)(2,1)S(1)}, bf16[256,896]{1,0:T(8,128)(2,1)S(1)}, u32[]{:S(2)}, u32[]{:S(2)}) collective-permute-start(bf16[256,896]{1,0:T(8,128)(2,1)S(1)} %get-tuple-element.79), channel_id=1, source_target_pairs={{0,16},{8,24},{16,0},{24,8},{1,17},{9,25},{17,1},{25,9},{2,18},{10... | collective-permute-start | bytes 1376264 | tf_op jit(solution)/shard_map/ppermute | solution.py:11
  8.0 10.5 %collective-permute-start.4 = (bf16[32,1792]{1,0:T(8,128)(2,1)S(1)}, bf16[32,1792]{1,0:T(8,128)(2,1)S(1)}, u32[]{:S(2)}, u32[]{:S(2)}) collective-permute-start(bf16[32,1792]{1,0:T(8,128)(2,1)S(1)} %bitcast.103), channel_id=1, source_target_pairs={{0,2},{1,3},{2,0},{3,1},{4,6},{5,7},{6,4},{7,5},{8,10},{9,11},{10,... | collective-permute-start | bytes 344072 | tf_op jit(solution)/shard_map/ppermute | solution.py:11
  9.7 11.4 %collective-permute-start.5 = (bf16[32,1792]{1,0:T(8,128)(2,1)S(1)}, bf16[32,1792]{1,0:T(8,128)(2,1)S(1)}, u32[]{:S(2)}, u32[]{:S(2)}) collective-permute-start(bf16[32,1792]{1,0:T(8,128)(2,1)S(1)} %bitcast.104), channel_id=1, source_target_pairs={{0,4},{1,5},{2,6},{3,7},{4,0},{5,1},{6,2},{7,3},{8,12},{9,13},{10,... | collective-permute-start | bytes 344072 | tf_op jit(solution)/shard_map/ppermute | solution.py:11
  12.3 8.8 %collective-permute-start.6 = (bf16[32,1792]{1,0:T(8,128)(2,1)S(1)}, bf16[32,1792]{1,0:T(8,128)(2,1)S(1)}, u32[]{:S(2)}, u32[]{:S(2)}) collective-permute-start(bf16[32,1792]{1,0:T(8,128)(2,1)S(1)} %bitcast.105), channel_id=1, source_target_pairs={{0,6},{1,7},{2,4},{3,5},{4,2},{5,3},{6,0},{7,1},{8,14},{9,15},{10,... | collective-permute-start | bytes 344072 | tf_op jit(solution)/shard_map/ppermute | solution.py:11
  13.7 11.7 %copy-start.1 = (bf16[1,2,2,128,1792]{4,3,2,1,0:T(8,128)(2,1)S(1)}, bf16[1,2,2,128,1792]{4,3,2,1,0:T(8,128)(2,1)}, u32[]{:S(2)}) copy-start(bf16[1,2,2,128,1792]{4,3,2,1,0:T(8,128)(2,1)} %param.10) | copy-start | bytes 5505028
  21.4 1.4 %collective-permute-start.7 = (f32[128,256]{1,0:T(8,128)S(1)}, f32[128,256]{1,0:T(8,128)S(1)}, u32[]{:S(2)}, u32[]{:S(2)}) collective-permute-start(f32[128,256]{1,0:T(8,128)S(1)} %convolution_add_fusion.4), channel_id=1, source_target_pairs={{0,8},{8,0},{16,24},{24,16},{1,9},{9,1},{17,25},{25,17},{2,10},{10... | collective-permute-start | bytes 393224 | tf_op jit(solution)/shard_map/ppermute | solution.py:11
  22.9 4.3 %collective-permute-start.9 = (bf16[128,256]{1,0:T(8,128)(2,1)S(1)}, bf16[128,256]{1,0:T(8,128)(2,1)S(1)}, u32[]{:S(2)}, u32[]{:S(2)}) collective-permute-start(bf16[128,256]{1,0:T(8,128)(2,1)S(1)} %multiply_convert_fusion), channel_id=1, source_target_pairs={{0,16},{8,24},{16,0},{24,8},{1,17},{9,25},{17,1},{25,9},{2,18},{10... | collective-permute-start | bytes 196616 | tf_op jit(solution)/shard_map/ppermute | solution.py:11
  23.8 5.2 %collective-permute-start.8 = (bf16[128,256]{1,0:T(8,128)(2,1)S(1)}, bf16[128,256]{1,0:T(8,128)(2,1)S(1)}, u32[]{:S(2)}, u32[]{:S(2)}) collective-permute-start(bf16[128,256]{1,0:T(8,128)(2,1)S(1)} %bitcast.118), channel_id=1, source_target_pairs={{0,1},{1,0},{2,3},{3,2},{4,5},{5,4},{6,7},{7,6},{8,9},{9,8},{10,11... | collective-permute-start | bytes 196616 | tf_op jit(solution)/shard_map/ppermute | solution.py:11
  26.6 10.5 %collective-permute-start.17 = (bf16[16,896]{1,0:T(8,128)(2,1)S(1)}, bf16[16,896]{1,0:T(8,128)(2,1)S(1)}, u32[]{:S(2)}, u32[]{:S(2)}) collective-permute-start(bf16[16,896]{1,0:T(8,128)(2,1)S(1)} %get-tuple-element.83), channel_id=1, source_target_pairs={{0,1},{1,0},{2,3},{3,2},{4,5},{5,4},{6,7},{7,6},{8,9},{9,8},{10,11... | collective-permute-start | bytes 86024 | tf_op jit(solution)/shard_map/ppermute | solution.py:11
  27.4 6.5 %collective-permute-start.10 = (bf16[64,896]{1,0:T(8,128)(2,1)S(1)}, bf16[64,896]{1,0:T(8,128)(2,1)S(1)}, u32[]{:S(2)}, u32[]{:S(2)}) collective-permute-start(bf16[64,896]{1,0:T(8,128)(2,1)S(1)} %fusion.1), channel_id=1, source_target_pairs={{0,1},{1,0},{2,3},{3,2},{4,5},{5,4},{6,7},{7,6},{8,9},{9,8},{10,11... | collective-permute-start | bytes 344072 | tf_op jit(solution)/shard_map/ppermute | solution.py:11
  29.5 9.0 %collective-permute-start.15 = (bf16[32,896]{1,0:T(8,128)(2,1)S(1)}, bf16[32,896]{1,0:T(8,128)(2,1)S(1)}, u32[]{:S(2)}, u32[]{:S(2)}) collective-permute-start(bf16[32,896]{1,0:T(8,128)(2,1)S(1)} %get-tuple-element.87), channel_id=1, source_target_pairs={{0,4},{1,5},{2,6},{3,7},{4,0},{5,1},{6,2},{7,3},{8,12},{9,13},{10,... | collective-permute-start | bytes 172040 | tf_op jit(solution)/shard_map/ppermute | solution.py:11
  32.4 6.2 %collective-permute-start.16 = (bf16[32,896]{1,0:T(8,128)(2,1)S(1)}, bf16[32,896]{1,0:T(8,128)(2,1)S(1)}, u32[]{:S(2)}, u32[]{:S(2)}) collective-permute-start(bf16[32,896]{1,0:T(8,128)(2,1)S(1)} %get-tuple-element.86), channel_id=1, source_target_pairs={{0,6},{1,7},{2,4},{3,5},{4,2},{5,3},{6,0},{7,1},{8,14},{9,15},{10,... | collective-permute-start | bytes 172040 | tf_op jit(solution)/shard_map/ppermute | solution.py:11
  34.0 4.6 %collective-permute-start.12 = (bf16[16,896]{1,0:T(8,128)(2,1)S(1)}, bf16[16,896]{1,0:T(8,128)(2,1)S(1)}, u32[]{:S(2)}, u32[]{:S(2)}) collective-permute-start(bf16[16,896]{1,0:T(8,128)(2,1)S(1)} %get-tuple-element.95), channel_id=1, source_target_pairs={{0,2},{1,3},{2,0},{3,1},{4,6},{5,7},{6,4},{7,5},{8,10},{9,11},{10,... | collective-permute-start | bytes 86024 | tf_op jit(solution)/shard_map/ppermute | solution.py:11
  34.2 4.8 %collective-permute-start.13 = (bf16[16,896]{1,0:T(8,128)(2,1)S(1)}, bf16[16,896]{1,0:T(8,128)(2,1)S(1)}, u32[]{:S(2)}, u32[]{:S(2)}) collective-permute-start(bf16[16,896]{1,0:T(8,128)(2,1)S(1)} %get-tuple-element.94), channel_id=1, source_target_pairs={{0,4},{1,5},{2,6},{3,7},{4,0},{5,1},{6,2},{7,3},{8,12},{9,13},{10,... | collective-permute-start | bytes 86024 | tf_op jit(solution)/shard_map/ppermute | solution.py:11
  37.1 5.8 %collective-permute-start.14 = (bf16[16,896]{1,0:T(8,128)(2,1)S(1)}, bf16[16,896]{1,0:T(8,128)(2,1)S(1)}, u32[]{:S(2)}, u32[]{:S(2)}) collective-permute-start(bf16[16,896]{1,0:T(8,128)(2,1)S(1)} %get-tuple-element.93), channel_id=1, source_target_pairs={{0,6},{1,7},{2,4},{3,5},{4,2},{5,3},{6,0},{7,1},{8,14},{9,15},{10,... | collective-permute-start | bytes 86024 | tf_op jit(solution)/shard_map/ppermute | solution.py:11
  38.5 8.9 %collective-permute-start.11 = (bf16[32,896]{1,0:T(8,128)(2,1)S(1)}, bf16[32,896]{1,0:T(8,128)(2,1)S(1)}, u32[]{:S(2)}, u32[]{:S(2)}) collective-permute-start(bf16[32,896]{1,0:T(8,128)(2,1)S(1)} %get-tuple-element.51), channel_id=1, source_target_pairs={{0,2},{1,3},{2,0},{3,1},{4,6},{5,7},{6,4},{7,5},{8,10},{9,11},{10,... | collective-permute-start | bytes 172040 | tf_op jit(solution)/shard_map/ppermute | solution.py:11
  42.9 6.1 %collective-permute-start.23 = (bf16[16,896]{1,0:T(8,128)(2,1)S(1)}, bf16[16,896]{1,0:T(8,128)(2,1)S(1)}, u32[]{:S(2)}, u32[]{:S(2)}) collective-permute-start(bf16[16,896]{1,0:T(8,128)(2,1)S(1)} %subtract_convert_fusion), channel_id=1, source_target_pairs={{0,6},{1,7},{2,4},{3,5},{4,2},{5,3},{6,0},{7,1},{8,14},{9,15},{10,... | collective-permute-start | bytes 86024 | tf_op jit(solution)/shard_map/ppermute | solution.py:11
  44.2 7.7 %collective-permute-start.22 = (bf16[16,896]{1,0:T(8,128)(2,1)S(1)}, bf16[16,896]{1,0:T(8,128)(2,1)S(1)}, u32[]{:S(2)}, u32[]{:S(2)}) collective-permute-start(bf16[16,896]{1,0:T(8,128)(2,1)S(1)} %subtract_convert_fusion), channel_id=1, source_target_pairs={{0,4},{1,5},{2,6},{3,7},{4,0},{5,1},{6,2},{7,3},{8,12},{9,13},{10,... | collective-permute-start | bytes 86024 | tf_op jit(solution)/shard_map/ppermute | solution.py:11
  44.2 7.7 %collective-permute-start.21 = (bf16[16,896]{1,0:T(8,128)(2,1)S(1)}, bf16[16,896]{1,0:T(8,128)(2,1)S(1)}, u32[]{:S(2)}, u32[]{:S(2)}) collective-permute-start(bf16[16,896]{1,0:T(8,128)(2,1)S(1)} %subtract_convert_fusion), channel_id=1, source_target_pairs={{0,2},{1,3},{2,0},{3,1},{4,6},{5,7},{6,4},{7,5},{8,10},{9,11},{10,... | collective-permute-start | bytes 86024 | tf_op jit(solution)/shard_map/ppermute | solution.py:11
  47.4 6.7 %collective-permute-start.20 = (bf16[32,896]{1,0:T(8,128)(2,1)S(1)}, bf16[32,896]{1,0:T(8,128)(2,1)S(1)}, u32[]{:S(2)}, u32[]{:S(2)}) collective-permute-start(bf16[32,896]{1,0:T(8,128)(2,1)S(1)} %fusion.24), channel_id=1, source_target_pairs={{0,6},{1,7},{2,4},{3,5},{4,2},{5,3},{6,0},{7,1},{8,14},{9,15},{10,... | collective-permute-start | bytes 172040 | tf_op jit(solution)/shard_map/ppermute | solution.py:11
  48.7 6.0 %collective-permute-start.19 = (bf16[32,896]{1,0:T(8,128)(2,1)S(1)}, bf16[32,896]{1,0:T(8,128)(2,1)S(1)}, u32[]{:S(2)}, u32[]{:S(2)}) collective-permute-start(bf16[32,896]{1,0:T(8,128)(2,1)S(1)} %fusion.24), channel_id=1, source_target_pairs={{0,4},{1,5},{2,6},{3,7},{4,0},{5,1},{6,2},{7,3},{8,12},{9,13},{10,... | collective-permute-start | bytes 172040 | tf_op jit(solution)/shard_map/ppermute | solution.py:11
  49.0 5.7 %collective-permute-start.18 = (bf16[32,896]{1,0:T(8,128)(2,1)S(1)}, bf16[32,896]{1,0:T(8,128)(2,1)S(1)}, u32[]{:S(2)}, u32[]{:S(2)}) collective-permute-start(bf16[32,896]{1,0:T(8,128)(2,1)S(1)} %fusion.24), channel_id=1, source_target_pairs={{0,2},{1,3},{2,0},{3,1},{4,6},{5,7},{6,4},{7,5},{8,10},{9,11},{10,... | collective-permute-start | bytes 172040 | tf_op jit(solution)/shard_map/ppermute | solution.py:11
  51.9 4.9 %collective-permute-start.24 = (bf16[64,896]{1,0:T(8,128)(2,1)S(1)}, bf16[64,896]{1,0:T(8,128)(2,1)S(1)}, u32[]{:S(2)}, u32[]{:S(2)}) collective-permute-start(bf16[64,896]{1,0:T(8,128)(2,1)S(1)} %pad_maximum_fusion.5), channel_id=1, source_target_pairs={{0,1},{1,0},{2,3},{3,2},{4,5},{5,4},{6,7},{7,6},{8,9},{9,8},{10,11... | collective-permute-start | bytes 344072 | tf_op jit(solution)/shard_map/ppermute | solution.py:11
  52.9 6.1 %collective-permute-start.27 = (bf16[16,896]{1,0:T(8,128)(2,1)S(1)}, bf16[16,896]{1,0:T(8,128)(2,1)S(1)}, u32[]{:S(2)}, u32[]{:S(2)}) collective-permute-start(bf16[16,896]{1,0:T(8,128)(2,1)S(1)} %subtract_convert_fusion), channel_id=1, source_target_pairs={{0,16},{8,24},{16,0},{24,8},{1,17},{9,25},{17,1},{25,9},{2,18},{10... | collective-permute-start | bytes 86024 | tf_op jit(solution)/shard_map/ppermute | solution.py:11
  54.1 4.9 %collective-permute-start.28 = (bf16[128,1792]{1,0:T(8,128)(2,1)S(1)}, bf16[128,1792]{1,0:T(8,128)(2,1)S(1)}, u32[]{:S(2)}, u32[]{:S(2)}) collective-permute-start(bf16[128,1792]{1,0:T(8,128)(2,1)S(1)} %constant_dynamic-update-slice_fusion), channel_id=1, source_target_pairs={{0,8},{8,0},{16,24},{24,16},{1,9},{9,1},{17,25},{25,17},{2,10},{10... | collective-permute-start | bytes 1376264 | tf_op jit(solution)/shard_map/ppermute | solution.py:11
  57.5 1.5 %collective-permute-start.26 = (f32[384,128]{1,0:T(8,128)S(1)}, f32[384,128]{1,0:T(8,128)S(1)}, u32[]{:S(2)}, u32[]{:S(2)}) collective-permute-start(f32[384,128]{1,0:T(8,128)S(1)} %slice_select_fusion), channel_id=1, source_target_pairs={{0,8},{8,0},{16,24},{24,16},{1,9},{9,1},{17,25},{25,17},{2,10},{10... | collective-permute-start | bytes 589832 | tf_op jit(solution)/shard_map/ppermute | solution.py:11
  57.6 3.9 %collective-permute-start.25 = (bf16[16,896]{1,0:T(8,128)(2,1)S(1)}, bf16[16,896]{1,0:T(8,128)(2,1)S(1)}, u32[]{:S(2)}, u32[]{:S(2)}) collective-permute-start(bf16[16,896]{1,0:T(8,128)(2,1)S(1)} %slice_bitcast_fusion), channel_id=1, source_target_pairs={{0,1},{1,0},{2,3},{3,2},{4,5},{5,4},{6,7},{7,6},{8,9},{9,8},{10,11... | collective-permute-start | bytes 86024 | tf_op jit(solution)/shard_map/ppermute | solution.py:11
  59.1 4.0 %collective-permute-start.30 = (bf16[128,128]{1,0:T(8,128)(2,1)S(1)}, bf16[128,128]{1,0:T(8,128)(2,1)S(1)}, u32[]{:S(2)}, u32[]{:S(2)}) collective-permute-start(bf16[128,128]{1,0:T(8,128)(2,1)S(1)} %get-tuple-element.96), channel_id=1, source_target_pairs={{0,16},{8,24},{16,0},{24,8},{1,17},{9,25},{17,1},{25,9},{2,18},{10... | collective-permute-start | bytes 98312 | tf_op jit(solution)/shard_map/ppermute | solution.py:11
  60.3 3.9 %collective-permute-start.29 = (bf16[128,128]{1,0:T(8,128)(2,1)S(1)}, bf16[128,128]{1,0:T(8,128)(2,1)S(1)}, u32[]{:S(2)}, u32[]{:S(2)}) collective-permute-start(bf16[128,128]{1,0:T(8,128)(2,1)S(1)} %get-tuple-element.97), channel_id=1, source_target_pairs={{0,1},{1,0},{2,3},{3,2},{4,5},{5,4},{6,7},{7,6},{8,9},{9,8},{10,11... | collective-permute-start | bytes 98312 | tf_op jit(solution)/shard_map/ppermute | solution.py:11

commit v23 on v22

--- a/solution.py
+++ b/solution.py
@@ -111,7 +111,8 @@
     after, _ = hold((decoder, mine))
     own_other = over_x(decoder_part(after, layer, 1 - side))
     shared_other = over_y(decoder_part(after, 1 - layer, 1 - layer))
-    decoder, own_other, shared_other, *column = hold((decoder, own_other, shared_other, *column))
+    decoder, own_other, shared_other, *column = hold((decoder, own_other, shared_other, *column[::-1]))
+    column = column[::-1]
     own_mine, shared_mine = decoder_part(decoder, layer, side), decoder_part(decoder, 1 - layer, layer)
     resid_half = jnp.concatenate(column, axis=0)
     firing = gates(blocks, layer, slot, slots, latents, tokens)

time: 66.4 us -> 64.9 us (0.977)
  waiting for transfers between devices: 17.5 us -> 16.2 us
    ppermute x31, waiting for transfers between devices: 17.5 us -> 16.2 us  [crossed(): lax.ppermute(block, axis, [(i, i ^ mask) for i in range(lax.axis_size(axi...]
  transfers between devices with their start and end apart: 31 -> 31, of which waited for: 12 -> 11; matrix products, arithmetic and copies ran while one was open for 12% -> 12% of each run, Pallas kernels for 0% -> 0%
where the time goes in v23:
time: 64.9 us; the launch traced here: 64.6 us
  starting transfers between devices  37.3 us (57%)
  waiting for transfers between devices  16.2 us (25%)
  matrix products  4.15 us (6%)
  local copies, waits for them, and re-layouts  3.02 us (5%)
  other arithmetic  2.95 us (5%)
  between operations  1.02 us (2%)
    ppermute x31, starting transfers between devices, crossed(): lax.ppermute(block, axis, [(i, i ^ mask) for i in range(lax.axis_size(axi...  37.3 us
    ppermute x31, waiting for transfers between devices, crossed(): lax.ppermute(block, axis, [(i, i ^ mask) for i in range(lax.axis_size(axi...  16.2 us
    dot_general x7, matrix products, times(): return jnp.dot(left, right, preferred_element_type=F32)  1.6 us
    dot_general x1, matrix products, encoder_gradient(): lax.dot_general(whole, grad_low, (((0,), (0,)), ((), ())), preferred_elem...  1.36 us
    select_n x3, other arithmetic, both_halves(): jnp.where(half == 0, mine, other)  1.32 us
  transfers between devices with their start and end apart: 31, of which 11 were waited for; matrix products, arithmetic and copies ran while one was open for 12% of the time, Pallas kernels for 0%

profile of v23, /device:TPU:0, one launch (start us, length us, event | category | flops | bytes accessed | tf_op | source)
XLA Modules:
  0.0 64.6 jit_solution(15595767186693081928)
XLA Ops:
  0.6 0.0 copy-start
  0.7 0.5 collective-permute-start.3
  1.2 0.8 %dynamic-slice_bitcast_fusion.2 = (bf16[1,1,16,1792]{3,2,1,0:T(8,128)(2,1)S(1)}, bf16[16,1792]{1,0:T(8,128)(2,1)S(1)}) fusion(bf16[2,16,3584]{2,1,0:T(8,128)(2,1)} %param.6, s32[]{:T(128)S(6)} %select_n.169, s32[]{:T(128)S(6)} %select_n.171), kind=kLoop, calls=%fused_computation.54 | loop fusion | bytes 172040 | tf_op jit(solution)/shard_map/reshape;squeeze | solution.py:100
  2.0 2.6 %collective-permute-start.2 = (bf16[16,1792]{1,0:T(8,128)(2,1)S(1)}, bf16[16,1792]{1,0:T(8,128)(2,1)S(1)}, u32[]{:S(2)}, u32[]{:S(2)}) collective-permute-start(bf16[16,1792]{1,0:T(8,128)(2,1)S(1)} %get-tuple-element.90), channel_id=1, source_target_pairs={{0,1},{1,0},{2,3},{3,2},{4,5},{5,4},{6,7},{7,6},{8,9},{9,8},{10,11... | collective-permute-start | bytes 172040 | tf_op jit(solution)/shard_map/ppermute | solution.py:11
  4.6 1.2 %dynamic-slice_bitcast_fusion = (bf16[256,896]{1,0:T(8,128)(2,1)S(1)}, bf16[256,896]{1,0:T(8,128)(2,1)S(1)}) fusion(bf16[2,256,1792]{2,1,0:T(8,128)(2,1)} %bitcast.92, s32[]{:T(128)S(6)} %select_n.173, s32[]{:T(128)S(6)} %select_n.174, s32[]{:T(128)S(6)} %select_n.169, s32[]{:T(128)S(6)} %select_n.172), kind=kLoop, calls=%fused_computation.24 | loop fusion | bytes 1835024 | tf_op jit(solution)/shard_map/squeeze | solution.py:91
  5.9 0.1 collective-permute-start
  6.0 2.0 %collective-permute-start.1 = (bf16[256,896]{1,0:T(8,128)(2,1)S(1)}, bf16[256,896]{1,0:T(8,128)(2,1)S(1)}, u32[]{:S(2)}, u32[]{:S(2)}) collective-permute-start(bf16[256,896]{1,0:T(8,128)(2,1)S(1)} %get-tuple-element.79), channel_id=1, source_target_pairs={{0,16},{8,24},{16,0},{24,8},{1,17},{9,25},{17,1},{25,9},{2,18},{10... | collective-permute-start | bytes 1376264 | tf_op jit(solution)/shard_map/ppermute | solution.py:11
  8.0 0.0 collective-permute-done.2
  8.0 0.0 collective-permute-done.3
  8.0 3.7 %collective-permute-start.4 = (bf16[32,1792]{1,0:T(8,128)(2,1)S(1)}, bf16[32,1792]{1,0:T(8,128)(2,1)S(1)}, u32[]{:S(2)}, u32[]{:S(2)}) collective-permute-start(bf16[32,1792]{1,0:T(8,128)(2,1)S(1)} %bitcast.103), channel_id=1, source_target_pairs={{0,6},{1,7},{2,4},{3,5},{4,2},{5,3},{6,0},{7,1},{8,14},{9,15},{10,... | collective-permute-start | bytes 344072 | tf_op jit(solution)/shard_map/ppermute | solution.py:11
  11.7 0.8 %collective-permute-start.6 = (bf16[32,1792]{1,0:T(8,128)(2,1)S(1)}, bf16[32,1792]{1,0:T(8,128)(2,1)S(1)}, u32[]{:S(2)}, u32[]{:S(2)}) collective-permute-start(bf16[32,1792]{1,0:T(8,128)(2,1)S(1)} %bitcast.105), channel_id=1, source_target_pairs={{0,2},{1,3},{2,0},{3,1},{4,6},{5,7},{6,4},{7,5},{8,10},{9,11},{10,... | collective-permute-start | bytes 344072 | tf_op jit(solution)/shard_map/ppermute | solution.py:11
  12.5 1.2 %bitcast_select_fusion.1 = (bf16[1792,128]{1,0:T(8,128)(2,1)S(1)}, bf16[1792,128]{1,0:T(8,128)(2,1)S(1)}) fusion(pred[]{:T(512)S(6)} %eq.48, bf16[3584,128]{1,0:T(8,128)(2,1)} %collective-permute-done.3, s32[]{:T(128)S(6)} %select_n.171, bf16[1,3584,128]{2,1,0:T(8,128)(2,1)S(1)} %copy-done.2), kind=kLoop, calls=%fused_computation.23 | loop fusion | flops 458752 | bytes 1835013 | tf_op jit(solution)/shard_map/jit(_where)/select_n | solution.py:23
  13.7 0.0 copy-start.1
  13.8 4.7 %collective-permute-done = bf16[256,896]{1,0:T(8,128)(2,1)S(1)} collective-permute-done((bf16[256,896]{1,0:T(8,128)(2,1)S(1)}, bf16[256,896]{1,0:T(8,128)(2,1)S(1)}, u32[]{:S(2)}, u32[]{:S(2)}) %collective-permute-start) | collective-permute-done | bytes 458784 | tf_op jit(solution)/shard_map/ppermute | solution.py:11
  18.5 0.1 collective-permute-done.1
  18.5 0.0 collective-permute-done.4
  18.5 2.5 %collective-permute-done.5 = bf16[32,1792]{1,0:T(8,128)(2,1)S(1)} collective-permute-done((bf16[32,1792]{1,0:T(8,128)(2,1)S(1)}, bf16[32,1792]{1,0:T(8,128)(2,1)S(1)}, u32[]{:S(2)}, u32[]{:S(2)}) %collective-permute-start.5) | collective-permute-done | bytes 114720 | tf_op jit(solution)/shard_map/ppermute | solution.py:11
  21.1 0.3 convolution_add_fusion.4
  21.4 0.1 collective-permute-start.7
  21.5 0.1 compare_reduce_fusion
  21.6 1.2 %collective-permute-done.7 = f32[128,256]{1,0:T(8,128)S(1)} collective-permute-done((f32[128,256]{1,0:T(8,128)S(1)}, f32[128,256]{1,0:T(8,128)S(1)}, u32[]{:S(2)}, u32[]{:S(2)}) %collective-permute-start.7) | collective-permute-done | bytes 131104 | tf_op jit(solution)/shard_map/ppermute | solution.py:11
  22.9 0.9 %collective-permute-start.9 = (bf16[128,256]{1,0:T(8,128)(2,1)S(1)}, bf16[128,256]{1,0:T(8,128)(2,1)S(1)}, u32[]{:S(2)}, u32[]{:S(2)}) collective-permute-start(bf16[128,256]{1,0:T(8,128)(2,1)S(1)} %multiply_convert_fusion), channel_id=1, source_target_pairs={{0,16},{8,24},{16,0},{24,8},{1,17},{9,25},{17,1},{25,9},{2,18},{10... | collective-permute-start | bytes 196616 | tf_op jit(solution)/shard_map/ppermute | solution.py:11
  23.8 1.6 %collective-permute-start.8 = (bf16[128,256]{1,0:T(8,128)(2,1)S(1)}, bf16[128,256]{1,0:T(8,128)(2,1)S(1)}, u32[]{:S(2)}, u32[]{:S(2)}) collective-permute-start(bf16[128,256]{1,0:T(8,128)(2,1)S(1)} %bitcast.118), channel_id=1, source_target_pairs={{0,1},{1,0},{2,3},{3,2},{4,5},{5,4},{6,7},{7,6},{8,9},{9,8},{10,11... | collective-permute-start | bytes 196616 | tf_op jit(solution)/shard_map/ppermute | solution.py:11
  25.4 0.2 fusion.11
  25.6 0.2 fusion.9
  25.8 0.8 %dynamic-slice_bitcast_fusion.4 = (bf16[16,896]{1,0:T(8,128)(2,1)S(1)}, bf16[16,896]{1,0:T(8,128)(2,1)S(1)}, bf16[16,896]{1,0:T(8,128)(2,1)S(1)}) fusion(bf16[3,16,3584]{2,1,0:T(8,128)(2,1)} %param.7, s32[]{:T(128)S(6)} %select_n.186, s32[]{:T(128)S(6)} %select_n.189, s32[]{:T(128)S(6)} %select_n.188, s32[]{:T(128)S(6)} %select_n.187), kind=kLoop, calls=%fused_computation.62 | loop fusion | bytes 172048 | tf_op jit(solution)/shard_map/squeeze | solution.py:128
  26.6 0.6 collective-permute-start.17
  27.2 0.2 fusion.1
  27.4 1.5 %collective-permute-start.10 = (bf16[64,896]{1,0:T(8,128)(2,1)S(1)}, bf16[64,896]{1,0:T(8,128)(2,1)S(1)}, u32[]{:S(2)}, u32[]{:S(2)}) collective-permute-start(bf16[64,896]{1,0:T(8,128)(2,1)S(1)} %fusion.1), channel_id=1, source_target_pairs={{0,1},{1,0},{2,3},{3,2},{4,5},{5,4},{6,7},{7,6},{8,9},{9,8},{10,11... | collective-permute-start | bytes 344072 | tf_op jit(solution)/shard_map/ppermute | solution.py:11
  29.0 0.2 fusion.51
  29.2 0.2 fusion.50
  29.5 1.0 %collective-permute-start.15 = (bf16[32,896]{1,0:T(8,128)(2,1)S(1)}, bf16[32,896]{1,0:T(8,128)(2,1)S(1)}, u32[]{:S(2)}, u32[]{:S(2)}) collective-permute-start(bf16[32,896]{1,0:T(8,128)(2,1)S(1)} %get-tuple-element.87), channel_id=1, source_target_pairs={{0,4},{1,5},{2,6},{3,7},{4,0},{5,1},{6,2},{7,3},{8,12},{9,13},{10,... | collective-permute-start | bytes 172040 | tf_op jit(solution)/shard_map/ppermute | solution.py:11
  30.5 1.7 %collective-permute-start.16 = (bf16[32,896]{1,0:T(8,128)(2,1)S(1)}, bf16[32,896]{1,0:T(8,128)(2,1)S(1)}, u32[]{:S(2)}, u32[]{:S(2)}) collective-permute-start(bf16[32,896]{1,0:T(8,128)(2,1)S(1)} %get-tuple-element.86), channel_id=1, source_target_pairs={{0,6},{1,7},{2,4},{3,5},{4,2},{5,3},{6,0},{7,1},{8,14},{9,15},{10,... | collective-permute-start | bytes 172040 | tf_op jit(solution)/shard_map/ppermute | solution.py:11
  32.1 0.2 convolution_add_fusion.1
  32.4 1.0 %collective-permute-start.12 = (bf16[16,896]{1,0:T(8,128)(2,1)S(1)}, bf16[16,896]{1,0:T(8,128)(2,1)S(1)}, u32[]{:S(2)}, u32[]{:S(2)}) collective-permute-start(bf16[16,896]{1,0:T(8,128)(2,1)S(1)} %get-tuple-element.95), channel_id=1, source_target_pairs={{0,2},{1,3},{2,0},{3,1},{4,6},{5,7},{6,4},{7,5},{8,10},{9,11},{10,... | collective-permute-start | bytes 86024 | tf_op jit(solution)/shard_map/ppermute | solution.py:11
  33.4 2.1 %collective-permute-start.13 = (bf16[16,896]{1,0:T(8,128)(2,1)S(1)}, bf16[16,896]{1,0:T(8,128)(2,1)S(1)}, u32[]{:S(2)}, u32[]{:S(2)}) collective-permute-start(bf16[16,896]{1,0:T(8,128)(2,1)S(1)} %get-tuple-element.94), channel_id=1, source_target_pairs={{0,4},{1,5},{2,6},{3,7},{4,0},{5,1},{6,2},{7,3},{8,12},{9,13},{10,... | collective-permute-start | bytes 86024 | tf_op jit(solution)/shard_map/ppermute | solution.py:11
  35.5 1.4 %collective-permute-start.14 = (bf16[16,896]{1,0:T(8,128)(2,1)S(1)}, bf16[16,896]{1,0:T(8,128)(2,1)S(1)}, u32[]{:S(2)}, u32[]{:S(2)}) collective-permute-start(bf16[16,896]{1,0:T(8,128)(2,1)S(1)} %get-tuple-element.93), channel_id=1, source_target_pairs={{0,6},{1,7},{2,4},{3,5},{4,2},{5,3},{6,0},{7,1},{8,14},{9,15},{10,... | collective-permute-start | bytes 86024 | tf_op jit(solution)/shard_map/ppermute | solution.py:11
  36.9 0.2 collective-permute-done.15
  37.1 1.8 %collective-permute-done.13 = bf16[16,896]{1,0:T(8,128)(2,1)S(1)} collective-permute-done((bf16[16,896]{1,0:T(8,128)(2,1)S(1)}, bf16[16,896]{1,0:T(8,128)(2,1)S(1)}, u32[]{:S(2)}, u32[]{:S(2)}) %collective-permute-start.13) | collective-permute-done | bytes 28704 | tf_op jit(solution)/shard_map/ppermute | solution.py:11
  38.9 2.4 %collective-permute-done.14 = bf16[16,896]{1,0:T(8,128)(2,1)S(1)} collective-permute-done((bf16[16,896]{1,0:T(8,128)(2,1)S(1)}, bf16[16,896]{1,0:T(8,128)(2,1)S(1)}, u32[]{:S(2)}, u32[]{:S(2)}) %collective-permute-start.14) | collective-permute-done | bytes 28704 | tf_op jit(solution)/shard_map/ppermute | solution.py:11
  41.3 1.3 %collective-permute-start.23 = (bf16[16,896]{1,0:T(8,128)(2,1)S(1)}, bf16[16,896]{1,0:T(8,128)(2,1)S(1)}, u32[]{:S(2)}, u32[]{:S(2)}) collective-permute-start(bf16[16,896]{1,0:T(8,128)(2,1)S(1)} %subtract_convert_fusion), channel_id=1, source_target_pairs={{0,6},{1,7},{2,4},{3,5},{4,2},{5,3},{6,0},{7,1},{8,14},{9,15},{10,... | collective-permute-start | bytes 86024 | tf_op jit(solution)/shard_map/ppermute | solution.py:11
  42.6 3.1 %collective-permute-start.21 = (bf16[16,896]{1,0:T(8,128)(2,1)S(1)}, bf16[16,896]{1,0:T(8,128)(2,1)S(1)}, u32[]{:S(2)}, u32[]{:S(2)}) collective-permute-start(bf16[16,896]{1,0:T(8,128)(2,1)S(1)} %subtract_convert_fusion), channel_id=1, source_target_pairs={{0,2},{1,3},{2,0},{3,1},{4,6},{5,7},{6,4},{7,5},{8,10},{9,11},{10,... | collective-permute-start | bytes 86024 | tf_op jit(solution)/shard_map/ppermute | solution.py:11
  45.8 1.3 %collective-permute-start.20 = (bf16[32,896]{1,0:T(8,128)(2,1)S(1)}, bf16[32,896]{1,0:T(8,128)(2,1)S(1)}, u32[]{:S(2)}, u32[]{:S(2)}) collective-permute-start(bf16[32,896]{1,0:T(8,128)(2,1)S(1)} %fusion.24), channel_id=1, source_target_pairs={{0,6},{1,7},{2,4},{3,5},{4,2},{5,3},{6,0},{7,1},{8,14},{9,15},{10,... | collective-permute-start | bytes 172040 | tf_op jit(solution)/shard_map/ppermute | solution.py:11
  47.1 0.2 collective-permute-start.19
  47.3 0.1 collective-permute-done.23
  47.4 2.8 %collective-permute-start.18 = (bf16[32,896]{1,0:T(8,128)(2,1)S(1)}, bf16[32,896]{1,0:T(8,128)(2,1)S(1)}, u32[]{:S(2)}, u32[]{:S(2)}) collective-permute-start(bf16[32,896]{1,0:T(8,128)(2,1)S(1)} %fusion.24), channel_id=1, source_target_pairs={{0,2},{1,3},{2,0},{3,1},{4,6},{5,7},{6,4},{7,5},{8,10},{9,11},{10,... | collective-permute-start | bytes 172040 | tf_op jit(solution)/shard_map/ppermute | solution.py:11
  50.3 1.5 %collective-permute-start.24 = (bf16[64,896]{1,0:T(8,128)(2,1)S(1)}, bf16[64,896]{1,0:T(8,128)(2,1)S(1)}, u32[]{:S(2)}, u32[]{:S(2)}) collective-permute-start(bf16[64,896]{1,0:T(8,128)(2,1)S(1)} %pad_maximum_fusion.5), channel_id=1, source_target_pairs={{0,1},{1,0},{2,3},{3,2},{4,5},{5,4},{6,7},{7,6},{8,9},{9,8},{10,11... | collective-permute-start | bytes 344072 | tf_op jit(solution)/shard_map/ppermute | solution.py:11
  51.8 1.2 %collective-permute-start.27 = (bf16[16,896]{1,0:T(8,128)(2,1)S(1)}, bf16[16,896]{1,0:T(8,128)(2,1)S(1)}, u32[]{:S(2)}, u32[]{:S(2)}) collective-permute-start(bf16[16,896]{1,0:T(8,128)(2,1)S(1)} %subtract_convert_fusion), channel_id=1, source_target_pairs={{0,16},{8,24},{16,0},{24,8},{1,17},{9,25},{17,1},{25,9},{2,18},{10... | collective-permute-start | bytes 86024 | tf_op jit(solution)/shard_map/ppermute | solution.py:11
  53.0 0.0 collective-permute-done.19
  53.0 0.3 fusion.13
  53.3 0.3 fusion.25
  53.7 1.4 %collective-permute-done.24 = bf16[64,896]{1,0:T(8,128)(2,1)S(1)} collective-permute-done((bf16[64,896]{1,0:T(8,128)(2,1)S(1)}, bf16[64,896]{1,0:T(8,128)(2,1)S(1)}, u32[]{:S(2)}, u32[]{:S(2)}) %collective-permute-start.24) | collective-permute-done | bytes 114720 | tf_op jit(solution)/shard_map/ppermute | solution.py:11
  55.1 0.3 fusion.52
  55.4 0.3 convolution_add_fusion.3
  55.8 0.1 collective-permute-start.26
  55.9 1.5 %collective-permute-start.25 = (bf16[16,896]{1,0:T(8,128)(2,1)S(1)}, bf16[16,896]{1,0:T(8,128)(2,1)S(1)}, u32[]{:S(2)}, u32[]{:S(2)}) collective-permute-start(bf16[16,896]{1,0:T(8,128)(2,1)S(1)} %slice_bitcast_fusion), channel_id=1, source_target_pairs={{0,1},{1,0},{2,3},{3,2},{4,5},{5,4},{6,7},{7,6},{8,9},{9,8},{10,11... | collective-permute-start | bytes 86024 | tf_op jit(solution)/shard_map/ppermute | solution.py:11
  57.6 1.3 %collective-permute-start.30 = (bf16[128,128]{1,0:T(8,128)(2,1)S(1)}, bf16[128,128]{1,0:T(8,128)(2,1)S(1)}, u32[]{:S(2)}, u32[]{:S(2)}) collective-permute-start(bf16[128,128]{1,0:T(8,128)(2,1)S(1)} %get-tuple-element.96), channel_id=1, source_target_pairs={{0,16},{8,24},{16,0},{24,8},{1,17},{9,25},{17,1},{25,9},{2,18},{10... | collective-permute-start | bytes 98312 | tf_op jit(solution)/shard_map/ppermute | solution.py:11
  58.8 1.3 %collective-permute-start.29 = (bf16[128,128]{1,0:T(8,128)(2,1)S(1)}, bf16[128,128]{1,0:T(8,128)(2,1)S(1)}, u32[]{:S(2)}, u32[]{:S(2)}) collective-permute-start(bf16[128,128]{1,0:T(8,128)(2,1)S(1)} %get-tuple-element.97), channel_id=1, source_target_pairs={{0,1},{1,0},{2,3},{3,2},{4,5},{5,4},{6,7},{7,6},{8,9},{9,8},{10,11... | collective-permute-start | bytes 98312 | tf_op jit(solution)/shard_map/ppermute | solution.py:11
  60.2 0.1 broadcast_select_fusion.1
  60.3 0.6 maximum_select_fusion
  61.0 0.5 collective-permute-done.30
  61.5 1.2 %collective-permute-done.29 = bf16[128,128]{1,0:T(8,128)(2,1)S(1)} collective-permute-done((bf16[128,128]{1,0:T(8,128)(2,1)S(1)}, bf16[128,128]{1,0:T(8,128)(2,1)S(1)}, u32[]{:S(2)}, u32[]{:S(2)}) %collective-permute-start.29) | collective-permute-done | bytes 32800 | tf_op jit(solution)/shard_map/ppermute | solution.py:11
  62.7 0.5 fusion.42
  63.3 1.4 %fusion = bf16[1,3584,128]{2,1,0:T(8,128)(2,1)} fusion(bf16[128,1792]{1,0:T(8,128)(2,1)S(1)} %get-tuple-element.82, bf16[128,1792]{1,0:T(8,128)(2,1)S(1)} %get-tuple-element.81, f32[128,128]{1,0:T(8,128)S(1)} %slice_select_fusion.1, bf16[128,128]{1,0:T(8,128)(2,1)S(1)} %collective-permute-done.30, bf16[128,128]{1,0:T(8,128)(2,1)S(1)} %collective-permute-done.29, ...), kind=kOutput, calls=%fused_computation.1 | convolution fusion | flops 119832576 | bytes 2031616 | tf_op jit(solution)/shard_map/dot_general | solution.py:44
  (60 shorter events, 0.5 us)
Async XLA Ops:
  0.6 20.9 %copy-start = (s32[2,1,12]{2,1,0:T(1,128)S(1)}, s32[2,1,12]{2,1,0:T(1,128)}, u32[]{:S(2)}) copy-start(s32[2,1,12]{2,1,0:T(1,128)} %param.11) | copy-start | bytes 292
  0.6 11.9 %copy-start.2 = (bf16[1,3584,128]{2,1,0:T(8,128)(2,1)S(1)}, bf16[1,3584,128]{2,1,0:T(8,128)(2,1)}, u32[]{:S(2)}) copy-start(bf16[1,3584,128]{2,1,0:T(8,128)(2,1)} %param.8) | copy-start | bytes 2752516
  0.7 7.4 %collective-permute-start.3 = (bf16[3584,128]{1,0:T(8,128)(2,1)}, bf16[3584,128]{1,0:T(8,128)(2,1)}, u32[]{:S(2)}, u32[]{:S(2)}) collective-permute-start(bf16[3584,128]{1,0:T(8,128)(2,1)} %bitcast.112), channel_id=1, source_target_pairs={{0,8},{8,0},{16,24},{24,16},{1,9},{9,1},{17,25},{25,17},{2,10},{10... | collective-permute-start | bytes 2752520 | tf_op jit(solution)/shard_map/ppermute | solution.py:11
  2.0 6.0 %collective-permute-start.2 = (bf16[16,1792]{1,0:T(8,128)(2,1)S(1)}, bf16[16,1792]{1,0:T(8,128)(2,1)S(1)}, u32[]{:S(2)}, u32[]{:S(2)}) collective-permute-start(bf16[16,1792]{1,0:T(8,128)(2,1)S(1)} %get-tuple-element.90), channel_id=1, source_target_pairs={{0,1},{1,0},{2,3},{3,2},{4,5},{5,4},{6,7},{7,6},{8,9},{9,8},{10,11... | collective-permute-start | bytes 172040 | tf_op jit(solution)/shard_map/ppermute | solution.py:11
  4.6 9.1 %copy-start.3 = (f32[1,128]{1,0:T(1,128)S(1)}, f32[1,128]{1,0:T(1,128)}, u32[]{:S(2)}) copy-start(f32[1,128]{1,0:T(1,128)} %param.9) | copy-start | bytes 1540
  5.9 12.6 %collective-permute-start = (bf16[256,896]{1,0:T(8,128)(2,1)S(1)}, bf16[256,896]{1,0:T(8,128)(2,1)S(1)}, u32[]{:S(2)}, u32[]{:S(2)}) collective-permute-start(bf16[256,896]{1,0:T(8,128)(2,1)S(1)} %get-tuple-element.80), channel_id=1, source_target_pairs={{0,1},{1,0},{2,3},{3,2},{4,5},{5,4},{6,7},{7,6},{8,9},{9,8},{10,11... | collective-permute-start | bytes 1376264 | tf_op jit(solution)/shard_map/ppermute | solution.py:11
  6.0 12.5 %collective-permute-start.1 = (bf16[256,896]{1,0:T(8,128)(2,1)S(1)}, bf16[256,896]{1,0:T(8,128)(2,1)S(1)}, u32[]{:S(2)}, u32[]{:S(2)}) collective-permute-start(bf16[256,896]{1,0:T(8,128)(2,1)S(1)} %get-tuple-element.79), channel_id=1, source_target_pairs={{0,16},{8,24},{16,0},{24,8},{1,17},{9,25},{17,1},{25,9},{2,18},{10... | collective-permute-start | bytes 1376264 | tf_op jit(solution)/shard_map/ppermute | solution.py:11
  8.0 10.5 %collective-permute-start.4 = (bf16[32,1792]{1,0:T(8,128)(2,1)S(1)}, bf16[32,1792]{1,0:T(8,128)(2,1)S(1)}, u32[]{:S(2)}, u32[]{:S(2)}) collective-permute-start(bf16[32,1792]{1,0:T(8,128)(2,1)S(1)} %bitcast.103), channel_id=1, source_target_pairs={{0,6},{1,7},{2,4},{3,5},{4,2},{5,3},{6,0},{7,1},{8,14},{9,15},{10,... | collective-permute-start | bytes 344072 | tf_op jit(solution)/shard_map/ppermute | solution.py:11
  11.7 9.4 %collective-permute-start.5 = (bf16[32,1792]{1,0:T(8,128)(2,1)S(1)}, bf16[32,1792]{1,0:T(8,128)(2,1)S(1)}, u32[]{:S(2)}, u32[]{:S(2)}) collective-permute-start(bf16[32,1792]{1,0:T(8,128)(2,1)S(1)} %bitcast.104), channel_id=1, source_target_pairs={{0,4},{1,5},{2,6},{3,7},{4,0},{5,1},{6,2},{7,3},{8,12},{9,13},{10,... | collective-permute-start | bytes 344072 | tf_op jit(solution)/shard_map/ppermute | solution.py:11
  11.7 9.4 %collective-permute-start.6 = (bf16[32,1792]{1,0:T(8,128)(2,1)S(1)}, bf16[32,1792]{1,0:T(8,128)(2,1)S(1)}, u32[]{:S(2)}, u32[]{:S(2)}) collective-permute-start(bf16[32,1792]{1,0:T(8,128)(2,1)S(1)} %bitcast.105), channel_id=1, source_target_pairs={{0,2},{1,3},{2,0},{3,1},{4,6},{5,7},{6,4},{7,5},{8,10},{9,11},{10,... | collective-permute-start | bytes 344072 | tf_op jit(solution)/shard_map/ppermute | solution.py:11
  13.7 11.7 %copy-start.1 = (bf16[1,2,2,128,1792]{4,3,2,1,0:T(8,128)(2,1)S(1)}, bf16[1,2,2,128,1792]{4,3,2,1,0:T(8,128)(2,1)}, u32[]{:S(2)}) copy-start(bf16[1,2,2,128,1792]{4,3,2,1,0:T(8,128)(2,1)} %param.10) | copy-start | bytes 5505028
  21.4 1.4 %collective-permute-start.7 = (f32[128,256]{1,0:T(8,128)S(1)}, f32[128,256]{1,0:T(8,128)S(1)}, u32[]{:S(2)}, u32[]{:S(2)}) collective-permute-start(f32[128,256]{1,0:T(8,128)S(1)} %convolution_add_fusion.4), channel_id=1, source_target_pairs={{0,8},{8,0},{16,24},{24,16},{1,9},{9,1},{17,25},{25,17},{2,10},{10... | collective-permute-start | bytes 393224 | tf_op jit(solution)/shard_map/ppermute | solution.py:11
  22.9 4.3 %collective-permute-start.9 = (bf16[128,256]{1,0:T(8,128)(2,1)S(1)}, bf16[128,256]{1,0:T(8,128)(2,1)S(1)}, u32[]{:S(2)}, u32[]{:S(2)}) collective-permute-start(bf16[128,256]{1,0:T(8,128)(2,1)S(1)} %multiply_convert_fusion), channel_id=1, source_target_pairs={{0,16},{8,24},{16,0},{24,8},{1,17},{9,25},{17,1},{25,9},{2,18},{10... | collective-permute-start | bytes 196616 | tf_op jit(solution)/shard_map/ppermute | solution.py:11
  23.8 5.2 %collective-permute-start.8 = (bf16[128,256]{1,0:T(8,128)(2,1)S(1)}, bf16[128,256]{1,0:T(8,128)(2,1)S(1)}, u32[]{:S(2)}, u32[]{:S(2)}) collective-permute-start(bf16[128,256]{1,0:T(8,128)(2,1)S(1)} %bitcast.118), channel_id=1, source_target_pairs={{0,1},{1,0},{2,3},{3,2},{4,5},{5,4},{6,7},{7,6},{8,9},{9,8},{10,11... | collective-permute-start | bytes 196616 | tf_op jit(solution)/shard_map/ppermute | solution.py:11
  26.6 8.8 %collective-permute-start.17 = (bf16[16,896]{1,0:T(8,128)(2,1)S(1)}, bf16[16,896]{1,0:T(8,128)(2,1)S(1)}, u32[]{:S(2)}, u32[]{:S(2)}) collective-permute-start(bf16[16,896]{1,0:T(8,128)(2,1)S(1)} %get-tuple-element.83), channel_id=1, source_target_pairs={{0,1},{1,0},{2,3},{3,2},{4,5},{5,4},{6,7},{7,6},{8,9},{9,8},{10,11... | collective-permute-start | bytes 86024 | tf_op jit(solution)/shard_map/ppermute | solution.py:11
  27.4 4.9 %collective-permute-start.10 = (bf16[64,896]{1,0:T(8,128)(2,1)S(1)}, bf16[64,896]{1,0:T(8,128)(2,1)S(1)}, u32[]{:S(2)}, u32[]{:S(2)}) collective-permute-start(bf16[64,896]{1,0:T(8,128)(2,1)S(1)} %fusion.1), channel_id=1, source_target_pairs={{0,1},{1,0},{2,3},{3,2},{4,5},{5,4},{6,7},{7,6},{8,9},{9,8},{10,11... | collective-permute-start | bytes 344072 | tf_op jit(solution)/shard_map/ppermute | solution.py:11
  29.5 7.6 %collective-permute-start.15 = (bf16[32,896]{1,0:T(8,128)(2,1)S(1)}, bf16[32,896]{1,0:T(8,128)(2,1)S(1)}, u32[]{:S(2)}, u32[]{:S(2)}) collective-permute-start(bf16[32,896]{1,0:T(8,128)(2,1)S(1)} %get-tuple-element.87), channel_id=1, source_target_pairs={{0,4},{1,5},{2,6},{3,7},{4,0},{5,1},{6,2},{7,3},{8,12},{9,13},{10,... | collective-permute-start | bytes 172040 | tf_op jit(solution)/shard_map/ppermute | solution.py:11
  30.5 6.6 %collective-permute-start.16 = (bf16[32,896]{1,0:T(8,128)(2,1)S(1)}, bf16[32,896]{1,0:T(8,128)(2,1)S(1)}, u32[]{:S(2)}, u32[]{:S(2)}) collective-permute-start(bf16[32,896]{1,0:T(8,128)(2,1)S(1)} %get-tuple-element.86), channel_id=1, source_target_pairs={{0,6},{1,7},{2,4},{3,5},{4,2},{5,3},{6,0},{7,1},{8,14},{9,15},{10,... | collective-permute-start | bytes 172040 | tf_op jit(solution)/shard_map/ppermute | solution.py:11
  32.4 4.7 %collective-permute-start.12 = (bf16[16,896]{1,0:T(8,128)(2,1)S(1)}, bf16[16,896]{1,0:T(8,128)(2,1)S(1)}, u32[]{:S(2)}, u32[]{:S(2)}) collective-permute-start(bf16[16,896]{1,0:T(8,128)(2,1)S(1)} %get-tuple-element.95), channel_id=1, source_target_pairs={{0,2},{1,3},{2,0},{3,1},{4,6},{5,7},{6,4},{7,5},{8,10},{9,11},{10,... | collective-permute-start | bytes 86024 | tf_op jit(solution)/shard_map/ppermute | solution.py:11
  33.4 5.5 %collective-permute-start.13 = (bf16[16,896]{1,0:T(8,128)(2,1)S(1)}, bf16[16,896]{1,0:T(8,128)(2,1)S(1)}, u32[]{:S(2)}, u32[]{:S(2)}) collective-permute-start(bf16[16,896]{1,0:T(8,128)(2,1)S(1)} %get-tuple-element.94), channel_id=1, source_target_pairs={{0,4},{1,5},{2,6},{3,7},{4,0},{5,1},{6,2},{7,3},{8,12},{9,13},{10,... | collective-permute-start | bytes 86024 | tf_op jit(solution)/shard_map/ppermute | solution.py:11
  35.5 5.8 %collective-permute-start.14 = (bf16[16,896]{1,0:T(8,128)(2,1)S(1)}, bf16[16,896]{1,0:T(8,128)(2,1)S(1)}, u32[]{:S(2)}, u32[]{:S(2)}) collective-permute-start(bf16[16,896]{1,0:T(8,128)(2,1)S(1)} %get-tuple-element.93), channel_id=1, source_target_pairs={{0,6},{1,7},{2,4},{3,5},{4,2},{5,3},{6,0},{7,1},{8,14},{9,15},{10,... | collective-permute-start | bytes 86024 | tf_op jit(solution)/shard_map/ppermute | solution.py:11
  37.1 8.6 %collective-permute-start.11 = (bf16[32,896]{1,0:T(8,128)(2,1)S(1)}, bf16[32,896]{1,0:T(8,128)(2,1)S(1)}, u32[]{:S(2)}, u32[]{:S(2)}) collective-permute-start(bf16[32,896]{1,0:T(8,128)(2,1)S(1)} %get-tuple-element.51), channel_id=1, source_target_pairs={{0,2},{1,3},{2,0},{3,1},{4,6},{5,7},{6,4},{7,5},{8,10},{9,11},{10,... | collective-permute-start | bytes 172040 | tf_op jit(solution)/shard_map/ppermute | solution.py:11
  41.3 6.2 %collective-permute-start.23 = (bf16[16,896]{1,0:T(8,128)(2,1)S(1)}, bf16[16,896]{1,0:T(8,128)(2,1)S(1)}, u32[]{:S(2)}, u32[]{:S(2)}) collective-permute-start(bf16[16,896]{1,0:T(8,128)(2,1)S(1)} %subtract_convert_fusion), channel_id=1, source_target_pairs={{0,6},{1,7},{2,4},{3,5},{4,2},{5,3},{6,0},{7,1},{8,14},{9,15},{10,... | collective-permute-start | bytes 86024 | tf_op jit(solution)/shard_map/ppermute | solution.py:11
  42.6 7.6 %collective-permute-start.22 = (bf16[16,896]{1,0:T(8,128)(2,1)S(1)}, bf16[16,896]{1,0:T(8,128)(2,1)S(1)}, u32[]{:S(2)}, u32[]{:S(2)}) collective-permute-start(bf16[16,896]{1,0:T(8,128)(2,1)S(1)} %subtract_convert_fusion), channel_id=1, source_target_pairs={{0,4},{1,5},{2,6},{3,7},{4,0},{5,1},{6,2},{7,3},{8,12},{9,13},{10,... | collective-permute-start | bytes 86024 | tf_op jit(solution)/shard_map/ppermute | solution.py:11
  42.6 7.6 %collective-permute-start.21 = (bf16[16,896]{1,0:T(8,128)(2,1)S(1)}, bf16[16,896]{1,0:T(8,128)(2,1)S(1)}, u32[]{:S(2)}, u32[]{:S(2)}) collective-permute-start(bf16[16,896]{1,0:T(8,128)(2,1)S(1)} %subtract_convert_fusion), channel_id=1, source_target_pairs={{0,2},{1,3},{2,0},{3,1},{4,6},{5,7},{6,4},{7,5},{8,10},{9,11},{10,... | collective-permute-start | bytes 86024 | tf_op jit(solution)/shard_map/ppermute | solution.py:11
  45.8 7.2 %collective-permute-start.20 = (bf16[32,896]{1,0:T(8,128)(2,1)S(1)}, bf16[32,896]{1,0:T(8,128)(2,1)S(1)}, u32[]{:S(2)}, u32[]{:S(2)}) collective-permute-start(bf16[32,896]{1,0:T(8,128)(2,1)S(1)} %fusion.24), channel_id=1, source_target_pairs={{0,6},{1,7},{2,4},{3,5},{4,2},{5,3},{6,0},{7,1},{8,14},{9,15},{10,... | collective-permute-start | bytes 172040 | tf_op jit(solution)/shard_map/ppermute | solution.py:11
  47.1 5.9 %collective-permute-start.19 = (bf16[32,896]{1,0:T(8,128)(2,1)S(1)}, bf16[32,896]{1,0:T(8,128)(2,1)S(1)}, u32[]{:S(2)}, u32[]{:S(2)}) collective-permute-start(bf16[32,896]{1,0:T(8,128)(2,1)S(1)} %fusion.24), channel_id=1, source_target_pairs={{0,4},{1,5},{2,6},{3,7},{4,0},{5,1},{6,2},{7,3},{8,12},{9,13},{10,... | collective-permute-start | bytes 172040 | tf_op jit(solution)/shard_map/ppermute | solution.py:11
  47.4 5.6 %collective-permute-start.18 = (bf16[32,896]{1,0:T(8,128)(2,1)S(1)}, bf16[32,896]{1,0:T(8,128)(2,1)S(1)}, u32[]{:S(2)}, u32[]{:S(2)}) collective-permute-start(bf16[32,896]{1,0:T(8,128)(2,1)S(1)} %fusion.24), channel_id=1, source_target_pairs={{0,2},{1,3},{2,0},{3,1},{4,6},{5,7},{6,4},{7,5},{8,10},{9,11},{10,... | collective-permute-start | bytes 172040 | tf_op jit(solution)/shard_map/ppermute | solution.py:11
  50.3 4.9 %collective-permute-start.24 = (bf16[64,896]{1,0:T(8,128)(2,1)S(1)}, bf16[64,896]{1,0:T(8,128)(2,1)S(1)}, u32[]{:S(2)}, u32[]{:S(2)}) collective-permute-start(bf16[64,896]{1,0:T(8,128)(2,1)S(1)} %pad_maximum_fusion.5), channel_id=1, source_target_pairs={{0,1},{1,0},{2,3},{3,2},{4,5},{5,4},{6,7},{7,6},{8,9},{9,8},{10,11... | collective-permute-start | bytes 344072 | tf_op jit(solution)/shard_map/ppermute | solution.py:11
  51.8 5.7 %collective-permute-start.27 = (bf16[16,896]{1,0:T(8,128)(2,1)S(1)}, bf16[16,896]{1,0:T(8,128)(2,1)S(1)}, u32[]{:S(2)}, u32[]{:S(2)}) collective-permute-start(bf16[16,896]{1,0:T(8,128)(2,1)S(1)} %subtract_convert_fusion), channel_id=1, source_target_pairs={{0,16},{8,24},{16,0},{24,8},{1,17},{9,25},{17,1},{25,9},{2,18},{10... | collective-permute-start | bytes 86024 | tf_op jit(solution)/shard_map/ppermute | solution.py:11
  53.0 4.5 %collective-permute-start.28 = (bf16[128,1792]{1,0:T(8,128)(2,1)S(1)}, bf16[128,1792]{1,0:T(8,128)(2,1)S(1)}, u32[]{:S(2)}, u32[]{:S(2)}) collective-permute-start(bf16[128,1792]{1,0:T(8,128)(2,1)S(1)} %constant_dynamic-update-slice_fusion), channel_id=1, source_target_pairs={{0,8},{8,0},{16,24},{24,16},{1,9},{9,1},{17,25},{25,17},{2,10},{10... | collective-permute-start | bytes 1376264 | tf_op jit(solution)/shard_map/ppermute | solution.py:11
  55.8 1.6 %collective-permute-start.26 = (f32[384,128]{1,0:T(8,128)S(1)}, f32[384,128]{1,0:T(8,128)S(1)}, u32[]{:S(2)}, u32[]{:S(2)}) collective-permute-start(f32[384,128]{1,0:T(8,128)S(1)} %slice_select_fusion), channel_id=1, source_target_pairs={{0,8},{8,0},{16,24},{24,16},{1,9},{9,1},{17,25},{25,17},{2,10},{10... | collective-permute-start | bytes 589832 | tf_op jit(solution)/shard_map/ppermute | solution.py:11
  55.9 4.3 %collective-permute-start.25 = (bf16[16,896]{1,0:T(8,128)(2,1)S(1)}, bf16[16,896]{1,0:T(8,128)(2,1)S(1)}, u32[]{:S(2)}, u32[]{:S(2)}) collective-permute-start(bf16[16,896]{1,0:T(8,128)(2,1)S(1)} %slice_bitcast_fusion), channel_id=1, source_target_pairs={{0,1},{1,0},{2,3},{3,2},{4,5},{5,4},{6,7},{7,6},{8,9},{9,8},{10,11... | collective-permute-start | bytes 86024 | tf_op jit(solution)/shard_map/ppermute | solution.py:11
  57.6 4.0 %collective-permute-start.30 = (bf16[128,128]{1,0:T(8,128)(2,1)S(1)}, bf16[128,128]{1,0:T(8,128)(2,1)S(1)}, u32[]{:S(2)}, u32[]{:S(2)}) collective-permute-start(bf16[128,128]{1,0:T(8,128)(2,1)S(1)} %get-tuple-element.96), channel_id=1, source_target_pairs={{0,16},{8,24},{16,0},{24,8},{1,17},{9,25},{17,1},{25,9},{2,18},{10... | collective-permute-start | bytes 98312 | tf_op jit(solution)/shard_map/ppermute | solution.py:11
  58.8 3.9 %collective-permute-start.29 = (bf16[128,128]{1,0:T(8,128)(2,1)S(1)}, bf16[128,128]{1,0:T(8,128)(2,1)S(1)}, u32[]{:S(2)}, u32[]{:S(2)}) collective-permute-start(bf16[128,128]{1,0:T(8,128)(2,1)S(1)} %get-tuple-element.97), channel_id=1, source_target_pairs={{0,1},{1,0},{2,3},{3,2},{4,5},{5,4},{6,7},{7,6},{8,9},{9,8},{10,11... | collective-permute-start | bytes 98312 | tf_op jit(solution)/shard_map/ppermute | solution.py:11
